TPU v7x, 32 devices: a whole 2x2x4 slice. The times are simulated.
32 devices in a mesh: groups: 2 (over y), row: 4 (over z), col: 4 (over x, core).
Axes of the slice: x: 2, y: 2, z: 4, core: 2. Of those that a mesh axis runs over, the one named last changes fastest.
Arguments:
- factor_blocks: bfloat16 [20, 4096, 4096], P('groups', 'row', 'col'), parts along dimension 0, may hold values from -0.0390625 to 0.0390625
- inverse_blocks: bfloat16 [10, 4096, 4096], P('groups', 'col', 'row'), parts along dimension 0, as said below
- right_sides: bfloat16 [10, 4096, 256], P('groups', 'row'), parts along dimension 0, may hold values from -6 to 6
Outputs:
- solution: bfloat16 [10, 4096, 256], P('groups', 'col', 'row'), parts along dimension 0
There are 2 independent parts, one for each index of `groups`. A program takes and returns all parts, laid end to end along the dimension named above; each array names one. Nothing has to cross between parts.
Inputs may be any that keep to these rules, and one draw needn't show every extreme that they name: `inverse_blocks`: each block is lower triangular with a diagonal of 0.5 to 2, hence invertible.
All inputs are finite; a program needn't handle non-finite values.
Results may differ from a plain program's by a relative error of at most 0.0095.
Values may be sent and summed in bfloat16 or wider, within the bound.
No kernel may reach another device: no remote copies, remote signals or barrier semaphores. Data moves between devices by JAX's collectives and lax.ppermute only.
A program may use at most 64 MiB of HBM per device.

v0:
```python
import jax
import jax.numpy as jnp
from jax import lax
from jax.sharding import PartitionSpec as P


def pair_index(block_row, column_index):
    return block_row * (block_row - 1) // 2 + column_index


def per_device(factor_blocks, inverse_blocks, right_sides):
    steps_total = right_sides.shape[0]
    angles = right_sides.shape[2]
    col_rows = inverse_blocks.shape[1]
    solved = []
    outputs = []
    for block_row in range(steps_total):
        residual = right_sides[block_row].astype(jnp.float32)
        if block_row > 0:
            partial_value = jnp.zeros((right_sides.shape[1], angles), jnp.float32)
            for column_index in range(block_row):
                partial_value = partial_value + jnp.dot(
                    factor_blocks[pair_index(block_row, column_index)],
                    solved[column_index],
                    preferred_element_type=jnp.float32,
                )
            residual = residual - lax.psum(partial_value, "col")
        residual_bf = residual.astype(jnp.bfloat16)
        term = jnp.dot(inverse_blocks[block_row], residual_bf, preferred_element_type=jnp.float32)
        share = lax.psum_scatter(term, "row", scatter_dimension=1, tiled=True).astype(jnp.bfloat16)
        outputs.append(share)
        if block_row + 1 < steps_total:
            current = lax.all_gather(share, "row", axis=1, tiled=True)
        else:
            current = jnp.zeros((col_rows, angles), jnp.bfloat16)
        solved.append(current)
    return jnp.stack(outputs, axis=0)


def solution(mesh):
    placed = (P("groups", "row", "col"), P("groups", "col", "row"), P("groups", "row", None))
    return jax.shard_map(
        per_device, mesh=mesh, in_specs=placed, out_specs=P("groups", "col", "row"), check_vma=False
    )
```

profile of v0, /device:TPU:0, one launch (start us, length us, event | category | flops | bytes accessed | tf_op | source)
XLA Modules:
  0.0 405.0 jit_solution(15479284260959443623)
XLA Ops:
  6.5 0.0 reduce-scatter.6.cloned.1.call-start
  6.5 3.4 fusion.28
  9.9 0.0 reduce-scatter.6.cloned.1.call-update
  10.0 0.0 all-reduce.5.cloned.1.call-start
  10.0 29.9 %reduce-scatter.6.cloned.1.call-done = f32[1024,64]{0,1:T(8,128)} async-done(((f32[1024,256]{0,1:T(8,128)}), f32[1024,64]{0,1:T(8,128)}) %reduce-scatter.6.cloned.1.call-update) | async-done | bytes 262160 | tf_op jit(solution)/shard_map/reduce_scatter | solution.py:30
  39.9 1.6 bitcast_dynamic-update-slice_fusion.4
  41.6 16.0 %all_gather.12 = bf16[1024,256]{0,1:T(8,128)(2,1)S(1)} all-gather(bf16[1024,64]{0,1:T(8,128)(2,1)S(1)} %get-tuple-element.12), channel_id=1, replica_groups=mesh['groups'=2,'row'=4,'col'=4] {'row'}, dimensions={1}, use_global_device_ids=true | all-gather | bytes 655360 | tf_op jit(solution)/shard_map/all_gather | solution.py:33
  57.6 0.0 copy-start
  57.6 3.5 fusion.45
  61.1 0.0 all-reduce.5.cloned.1.call-update
  61.1 0.0 reduce-scatter.8.cloned.1.call-start
  61.1 34.6 %all-reduce.5.cloned.1.call-done = f32[1024,256]{1,0:T(8,128)} async-done(((f32[1024,256]{1,0:T(8,128)}), f32[1024,256]{1,0:T(8,128)}) %all-reduce.5.cloned.1.call-update) | async-done | bytes 1048592 | tf_op jit(solution)/shard_map/psum | solution.py:27
  95.7 0.0 copy-done
  95.7 3.7 fusion.48
  99.4 0.0 reduce-scatter.8.cloned.1.call-update
  99.4 0.0 all-reduce.7.cloned.1.call-start
  99.5 27.6 %reduce-scatter.8.cloned.1.call-done = f32[1024,64]{0,1:T(8,128)} async-done(((f32[1024,256]{0,1:T(8,128)}), f32[1024,64]{0,1:T(8,128)}) %reduce-scatter.8.cloned.1.call-update) | async-done | bytes 262160 | tf_op jit(solution)/shard_map/reduce_scatter | solution.py:30
  127.1 1.6 bitcast_dynamic-update-slice_fusion.3
  128.7 16.0 %all_gather.13 = bf16[1024,256]{0,1:T(8,128)(2,1)S(1)} all-gather(bf16[1024,64]{0,1:T(8,128)(2,1)S(1)} %get-tuple-element.10), channel_id=1, replica_groups=mesh['groups'=2,'row'=4,'col'=4] {'row'}, dimensions={1}, use_global_device_ids=true | all-gather | bytes 655360 | tf_op jit(solution)/shard_map/all_gather | solution.py:33
  144.7 0.0 copy-start.4
  144.7 0.8 copy-done.4
  145.5 2.3 fusion.20
  147.8 3.3 fusion.63
  151.2 0.0 all-reduce.7.cloned.1.call-update
  151.2 0.0 reduce-scatter.10.cloned.1.call-start
  151.2 34.6 %all-reduce.7.cloned.1.call-done = f32[1024,256]{1,0:T(8,128)} async-done(((f32[1024,256]{1,0:T(8,128)}), f32[1024,256]{1,0:T(8,128)}) %all-reduce.7.cloned.1.call-update) | async-done | bytes 1048592 | tf_op jit(solution)/shard_map/psum | solution.py:27
  185.8 3.6 fusion.51
  189.5 0.0 reduce-scatter.10.cloned.1.call-update
  189.5 0.0 all-reduce.9.cloned.1.call-start
  189.6 3.5 fusion.14
  193.1 24.1 %reduce-scatter.10.cloned.1.call-done = f32[1024,64]{0,1:T(8,128)} async-done(((f32[1024,256]{0,1:T(8,128)}), f32[1024,64]{0,1:T(8,128)}) %reduce-scatter.10.cloned.1.call-update) | async-done | bytes 262160 | tf_op jit(solution)/shard_map/reduce_scatter | solution.py:30
  217.2 0.0 copy-start.3
  217.2 1.7 bitcast_dynamic-update-slice_fusion.2
  218.9 15.8 %all_gather.14 = bf16[1024,256]{0,1:T(8,128)(2,1)S(1)} all-gather(bf16[1024,64]{0,1:T(8,128)(2,1)S(1)} %get-tuple-element.8), channel_id=1, replica_groups=mesh['groups'=2,'row'=4,'col'=4] {'row'}, dimensions={1}, use_global_device_ids=true | all-gather | bytes 655360 | tf_op jit(solution)/shard_map/all_gather | solution.py:33
  234.7 0.0 copy-start.5
  234.7 0.8 copy-done.5
  235.5 2.3 fusion.12
  237.8 0.0 copy-done.3
  237.8 3.3 fusion.72
  241.1 0.0 all-reduce.9.cloned.1.call-update
  241.2 0.0 reduce-scatter.12.cloned.1.call-start
  241.2 34.8 %all-reduce.9.cloned.1.call-done = f32[1024,256]{1,0:T(8,128)} async-done(((f32[1024,256]{1,0:T(8,128)}), f32[1024,256]{1,0:T(8,128)}) %all-reduce.9.cloned.1.call-update) | async-done | bytes 1048592 | tf_op jit(solution)/shard_map/psum | solution.py:27
  276.0 3.6 fusion.54
  279.6 0.0 reduce-scatter.12.cloned.1.call-update
  279.6 0.0 all-reduce.11.cloned.1.call-start
  279.7 0.0 copy-start.6
  279.7 3.6 fusion.6
  283.3 0.0 copy-done.6
  283.3 3.3 fusion.4
  286.6 20.7 %reduce-scatter.12.cloned.1.call-done = f32[1024,64]{0,1:T(8,128)} async-done(((f32[1024,256]{0,1:T(8,128)}), f32[1024,64]{0,1:T(8,128)}) %reduce-scatter.12.cloned.1.call-update) | async-done | bytes 262160 | tf_op jit(solution)/shard_map/reduce_scatter | solution.py:30
  307.3 0.0 copy-start.1
  307.3 1.8 bitcast_dynamic-update-slice_fusion.1
  309.1 15.8 %all_gather.15 = bf16[1024,256]{0,1:T(8,128)(2,1)S(1)} all-gather(bf16[1024,64]{0,1:T(8,128)(2,1)S(1)} %get-tuple-element.6), channel_id=1, replica_groups=mesh['groups'=2,'row'=4,'col'=4] {'row'}, dimensions={1}, use_global_device_ids=true | all-gather | bytes 655360 | tf_op jit(solution)/shard_map/all_gather | solution.py:33
  324.9 2.3 fusion.2
  327.2 0.0 copy-done.1
  327.2 0.0 copy-done.2
  327.2 3.4 fusion.84
  330.6 0.0 all-reduce.11.cloned.1.call-update
  330.6 0.0 reduce-scatter.14.cloned.1.call-start
  330.7 34.8 %all-reduce.11.cloned.1.call-done = f32[1024,256]{1,0:T(8,128)} async-done(((f32[1024,256]{1,0:T(8,128)}), f32[1024,256]{1,0:T(8,128)}) %all-reduce.11.cloned.1.call-update) | async-done | bytes 1048592 | tf_op jit(solution)/shard_map/psum | solution.py:27
  365.5 3.7 fusion.57
  369.2 0.0 reduce-scatter.14.cloned.1.call-update
  369.2 27.7 %reduce-scatter.14.cloned.1.call-done = f32[1024,64]{0,1:T(8,128)} async-done(((f32[1024,256]{0,1:T(8,128)}), f32[1024,64]{0,1:T(8,128)}) %reduce-scatter.14.cloned.1.call-update) | async-done | bytes 262160 | tf_op jit(solution)/shard_map/reduce_scatter | solution.py:30
  396.9 1.6 bitcast_dynamic-update-slice_fusion
  (1 shorter events, 0.0 us)
Async XLA Ops:
  6.5 33.4 %reduce-scatter.6.cloned.1.call-start = ((), (), s32[]{:S(2)}) async-start(), calls=%async_computation.5 | async-start | bytes 1310720 | tf_op jit(solution)/shard_map/reduce_scatter | solution.py:30
  10.0 85.7 %all-reduce.5.cloned.1.call-start = ((), (), s32[]{:S(2)}) async-start(), calls=%async_computation.6 | async-start | bytes 2097152 | tf_op jit(solution)/shard_map/psum | solution.py:27
  57.6 38.1 %copy-start = (bf16[5,1024,256]{2,1,0:T(8,128)(2,1)S(1)}, bf16[5,1024,256]{2,1,0:T(8,128)(2,1)}, u32[]{:S(2)}) copy-start(bf16[5,1024,256]{2,1,0:T(8,128)(2,1)} %param.5) | copy-start | bytes 7864324
  61.1 66.0 %reduce-scatter.8.cloned.1.call-start = ((), (), s32[]{:S(2)}) async-start(), calls=%async_computation.7 | async-start | bytes 1310720 | tf_op jit(solution)/shard_map/reduce_scatter | solution.py:30
  99.4 86.4 %all-reduce.7.cloned.1.call-start = ((), (), s32[]{:S(2)}) async-start(), calls=%async_computation.8 | async-start | bytes 2097152 | tf_op jit(solution)/shard_map/psum | solution.py:27
  144.7 0.8 copy-start.4
  151.2 66.0 %reduce-scatter.10.cloned.1.call-start = ((), (), s32[]{:S(2)}) async-start(), calls=%async_computation.9 | async-start | bytes 1310720 | tf_op jit(solution)/shard_map/reduce_scatter | solution.py:30
  189.5 86.5 %all-reduce.9.cloned.1.call-start = ((), (), s32[]{:S(2)}) async-start(), calls=%async_computation.10 | async-start | bytes 2097152 | tf_op jit(solution)/shard_map/psum | solution.py:27
  217.2 20.6 %copy-start.3 = (f32[256,1024]{0,1:T(8,128)S(1)}, f32[256,1024]{0,1:T(8,128)}, u32[]{:S(2)}) copy-start(f32[256,1024]{0,1:T(8,128)} %fusion.14) | copy-start | bytes 3145732
  234.7 0.8 copy-start.5
  241.2 66.2 %reduce-scatter.12.cloned.1.call-start = ((), (), s32[]{:S(2)}) async-start(), calls=%async_computation.11 | async-start | bytes 1310720 | tf_op jit(solution)/shard_map/reduce_scatter | solution.py:30
  279.6 85.9 %all-reduce.11.cloned.1.call-start = ((), (), s32[]{:S(2)}) async-start(), calls=%async_computation.12 | async-start | bytes 2097152 | tf_op jit(solution)/shard_map/psum | solution.py:27
  279.7 3.6 copy-start.6
  307.3 19.9 %copy-start.1 = (f32[256,1024]{0,1:T(8,128)S(1)}, f32[256,1024]{0,1:T(8,128)}, u32[]{:S(2)}) copy-start(f32[256,1024]{0,1:T(8,128)} %fusion.6) | copy-start | bytes 3145732
  307.3 19.9 %copy-start.2 = (f32[256,1024]{0,1:T(8,128)S(1)}, f32[256,1024]{0,1:T(8,128)}, u32[]{:S(2)}) copy-start(f32[256,1024]{0,1:T(8,128)} %fusion.4) | copy-start | bytes 3145732
  330.6 66.2 %reduce-scatter.14.cloned.1.call-start = ((), (), s32[]{:S(2)}) async-start(), calls=%async_computation.13 | async-start | bytes 1310720 | tf_op jit(solution)/shard_map/reduce_scatter | solution.py:30
Sparse Core Ops, SparseCore 0:
  10.1 29.8 reduce-scatter.5
  61.2 34.4 all-reduce.4
  99.5 27.5 reduce-scatter.7
  151.3 34.4 all-reduce.6
  189.6 27.5 reduce-scatter.9
  241.3 34.6 all-reduce.8
  279.8 27.5 reduce-scatter.11
  330.7 34.7 all-reduce.10
  369.3 27.4 reduce-scatter.13
where the time goes:
time: 406 us; the launch traced here: 405 us
  waiting for transfers between devices  269 us (66%)
  blocking collectives  63.5 us (16%)
  matrix products  49 us (12%)
  between operations  13.3 us (3%)
  other arithmetic  8.36 us (2%)
    psum x4, waiting for transfers between devices, per_device(): residual = residual - lax.psum(partial_value, 'col')  139 us
    reduce_scatter x5, waiting for transfers between devices, per_device(): lax.psum_scatter(term, 'row', scatter_dimension=1, tiled=True)  130 us
    all_gather x4, blocking collectives, per_device(): current = lax.all_gather(share, 'row', axis=1, tiled=True)  63.5 us
    dot_general x10, matrix products, per_device(): jnp.dot(factor_blocks[pair_index(block_row, column_index)], solved[column...  30.9 us
    dot_general x5, matrix products, per_device(): jnp.dot(inverse_blocks[block_row], residual_bf, preferred_element_type=jn...  18.1 us
  transfers between devices with their start and end apart: 9, of which 9 were waited for; matrix products, arithmetic and copies ran while one was open for 3% of the time, Pallas kernels for 0%

commit v1 on v0

v1 whole, which is shorter than its diff:
```python
import jax
import jax.numpy as jnp
from jax import lax
from jax.sharding import PartitionSpec as P

STREAMS = 2


def pair_index(block_row, column_index):
    return block_row * (block_row - 1) // 2 + column_index


def times_transposed(left, right):
    return lax.dot_general(left, right, (((1,), (1,)), ((), ())), preferred_element_type=jnp.float32)


def make_per_device(n_row, n_col):
    def trade(value, axis, step):
        size = n_row if axis == "row" else n_col
        return lax.ppermute(value.astype(jnp.bfloat16), axis, [(i, i ^ step) for i in range(size)])

    def far_sum(value, axis):
        step = 2
        size = n_row if axis == "row" else n_col
        while step < size:
            value = value + trade(value, axis, step).astype(jnp.float32)
            step *= 2
        return value

    def per_device(factor_blocks, inverse_blocks, right_sides):
        steps_total, group_rows, angles = right_sides.shape
        place = lax.axis_index("row")
        core = lax.axis_index("col")
        side = (place ^ core) & 1
        units = 2 * STREAMS
        wide = angles // units

        def ordered(step):
            cut = right_sides[step].T.reshape(STREAMS, 2, wide, group_rows)
            return jnp.where(side == 0, cut, cut[:, ::-1])

        solved = []
        outputs = []
        for step in range(steps_total):
            base = ordered(step)
            current = []
            for s in range(STREAMS):
                if step == 0:
                    own, other = base[s, 0], base[s, 1]
                else:
                    before = [solved[j][s] for j in range(step)]
                    shares = []
                    for unit in (1, 0):
                        share = times_transposed(before[-1][unit], factor_blocks[pair_index(step, step - 1)])
                        for j in range(step - 1):
                            share = share + times_transposed(before[j][unit], factor_blocks[pair_index(step, j)])
                        shares.append(share)
                    share = shares[1] + trade(shares[0], "col", 1).astype(jnp.float32)
                    share = far_sum(share, "col")
                    own = (base[s, 0].astype(jnp.float32) - share).astype(jnp.bfloat16)
                    other = trade(own, "col", 1)
                term_other = times_transposed(other, inverse_blocks[step])
                term_own = times_transposed(own, inverse_blocks[step])
                total = term_own + trade(term_other, "row", 1).astype(jnp.float32)
                mine = far_sum(total, "row").astype(jnp.bfloat16)
                current.append((mine, trade(mine, "row", 1)))
            solved.append(current)
            slot = angles // n_row
            unit = place * units // n_row
            found = current[0][0]
            for s in range(STREAMS):
                for u in range(2):
                    found = jnp.where(unit == 2 * s + (u ^ side), current[s][u], found)
            within = (place % (n_row // units)) * slot if n_row > units else 0
            outputs.append(lax.dynamic_slice_in_dim(found, within, slot, 0).T)
        return jnp.stack(outputs, axis=0)

    return per_device


def solution(mesh):
    placed = (P("groups", "row", "col"), P("groups", "col", "row"), P("groups", "row", None))
    return jax.shard_map(
        make_per_device(mesh.shape["row"], mesh.shape["col"]),
        mesh=mesh,
        in_specs=placed,
        out_specs=P("groups", "col", "row"),
        check_vma=False,
    )
```

time: 406 us -> 208 us (0.51)
  waiting for transfers between devices: 269 us -> 88.7 us
  blocking collectives: 63.5 us -> 0 us
  starting transfers between devices: 0.34 us -> 49.8 us
  matrix products: 49 us -> 63.6 us
  between operations: 13.3 us -> 0.56 us
  other arithmetic: 8.36 us -> 2.31 us
    psum x4 -> x0, waiting for transfers between devices: 139 us -> none  [per_device(): residual = residual - lax.psum(partial_value, 'col')]
    reduce_scatter x5 -> x0, waiting for transfers between devices: 130 us -> none  [per_device(): lax.psum_scatter(term, 'row', scatter_dimension=1, tiled=True)]
    ppermute x0 -> x54, waiting for transfers between devices: none -> 88.7 us  [trade(): lax.ppermute(value.astype(jnp.bfloat16), axis, [(i, i ^ step) for i in ra...]
    all_gather x4 -> x0, blocking collectives: 63.5 us -> none  [per_device(): current = lax.all_gather(share, 'row', axis=1, tiled=True)]
    ppermute x0 -> x54, starting transfers between devices: none -> 49.8 us  [trade(): lax.ppermute(value.astype(jnp.bfloat16), axis, [(i, i ^ step) for i in ra...]
    dot_general x15 -> x60, matrix products: 49 us -> 63.6 us  [times_transposed(): lax.dot_general(left, right, (((1,), (1,)), ((), ())), preferred_element_...]
    unnamed x4 -> x5, other arithmetic: 6.74 us -> 0.29 us
  transfers between devices with their start and end apart: 9 -> 54, of which waited for: 9 -> 34; matrix products, arithmetic and copies ran while one was open for 3% -> 30% of each run, Pallas kernels for 0% -> 0%
where the time goes in v1:
time: 208 us
  waiting for transfers between devices  88.7 us (43%)
  matrix products  63.6 us (31%)
  starting transfers between devices  49.8 us (24%)
  local copies, waits for them, and re-layouts  2.91 us (1%)
  other arithmetic  2.31 us (1%)
    ppermute x54, waiting for transfers between devices, trade(): lax.ppermute(value.astype(jnp.bfloat16), axis, [(i, i ^ step) for i in ra...  88.7 us
    dot_general x60, matrix products, times_transposed(): lax.dot_general(left, right, (((1,), (1,)), ((), ())), preferred_element_...  63.6 us
    ppermute x54, starting transfers between devices, trade(): lax.ppermute(value.astype(jnp.bfloat16), axis, [(i, i ^ step) for i in ra...  49.8 us
  transfers between devices with their start and end apart: 54, of which 34 were waited for; matrix products, arithmetic and copies ran while one was open for 30% of the time, Pallas kernels for 0%

profile of v1, /device:TPU:0, one launch (start us, length us, event | category | flops | bytes accessed | tf_op | source)
XLA Modules:
  0.0 207.8 jit_solution(474619969163840739)
XLA Ops:
  0.0 1.8 slice_bitcast_fusion
  2.2 3.2 %fusion.318 = bf16[64,1024]{1,0:T(8,128)(2,1)} fusion(bf16[5,1024,1024]{2,1,0:T(8,128)(2,1)} %param.4, bf16[2,2,64,1024]{3,2,1,0:T(8,128)(2,1)S(1)} %reverse_select_fusion.4), kind=kOutput, calls=%fused_computation.226 | convolution fusion | flops 134283264 | bytes 2359296 | tf_op jit(solution)/shard_map/dot_general | solution.py:14
  5.4 3.0 %collective-permute-start = (bf16[64,1024]{1,0:T(8,128)(2,1)}, bf16[64,1024]{1,0:T(8,128)(2,1)S(1)}, u32[]{:S(2)}, u32[]{:S(2)}) collective-permute-start(bf16[64,1024]{1,0:T(8,128)(2,1)} %fusion.318), channel_id=1, source_target_pairs={{0,4},{4,0},{8,12},{12,8},{1,5},{5,1},{9,13},{13,9},{2,6},{6,2},{1... | collective-permute-start | bytes 393224 | tf_op jit(solution)/shard_map/ppermute | solution.py:20
  8.4 2.3 %fusion.321 = bf16[64,1024]{1,0:T(8,128)(2,1)S(1)} fusion(bf16[5,1024,1024]{2,1,0:T(8,128)(2,1)} %param.4, bf16[2,2,64,1024]{3,2,1,0:T(8,128)(2,1)S(1)} %reverse_select_fusion.4), kind=kOutput, calls=%fused_computation.227 | convolution fusion | flops 134283264 | bytes 2359296 | tf_op jit(solution)/shard_map/dot_general | solution.py:14
  12.3 2.6 %fusion.362 = (bf16[64,1024]{1,0:T(8,128)(2,1)S(1)}, f32[64,1024]{1,0:T(8,128)S(1)}) fusion(bf16[64,1024]{1,0:T(8,128)(2,1)S(1)} %collective-permute-done, bf16[5,1024,1024]{2,1,0:T(8,128)(2,1)} %param.4, bf16[2,2,64,1024]{3,2,1,0:T(8,128)(2,1)} %copy-done.1), kind=kOutput, calls=%fused_computation.276 | convolution fusion | flops 134414336 | bytes 2752512 | tf_op jit(solution)/shard_map/dot_general | solution.py:14
  14.8 3.1 %collective-permute-start.1 = (bf16[64,1024]{1,0:T(8,128)(2,1)S(1)}, bf16[64,1024]{1,0:T(8,128)(2,1)S(1)}, u32[]{:S(2)}, u32[]{:S(2)}) collective-permute-start(bf16[64,1024]{1,0:T(8,128)(2,1)S(1)} %get-tuple-element.18), channel_id=1, source_target_pairs={{0,8},{4,12},{8,0},{12,4},{1,9},{5,13},{9,1},{13,5},{2,10},{6,14},... | collective-permute-start | bytes 393224 | tf_op jit(solution)/shard_map/ppermute | solution.py:20
  17.9 3.2 %fusion.363 = (bf16[64,1024]{1,0:T(8,128)(2,1)S(1)}, f32[64,1024]{1,0:T(8,128)S(1)}) fusion(bf16[64,1024]{1,0:T(8,128)(2,1)S(1)} %collective-permute-done.3, bf16[5,1024,1024]{2,1,0:T(8,128)(2,1)} %param.4, bf16[2,2,64,1024]{3,2,1,0:T(8,128)(2,1)} %copy-done.1), kind=kOutput, calls=%fused_computation.277 | convolution fusion | flops 134414336 | bytes 2752512 | tf_op jit(solution)/shard_map/dot_general | solution.py:14
  21.6 2.0 collective-permute-done.1
  23.7 3.9 %collective-permute-start.2 = (bf16[64,1024]{1,0:T(8,128)(2,1)S(1)}, bf16[64,1024]{1,0:T(8,128)(2,1)S(1)}, u32[]{:S(2)}, u32[]{:S(2)}) collective-permute-start(bf16[64,1024]{1,0:T(8,128)(2,1)S(1)} %add_convert_fusion.9), channel_id=1, source_target_pairs={{0,4},{4,0},{8,12},{12,8},{1,5},{5,1},{9,13},{13,9},{2,6},{6,2},{1... | collective-permute-start | bytes 393224 | tf_op jit(solution)/shard_map/ppermute | solution.py:20
  27.6 1.8 collective-permute-done.4
  30.1 2.3 %fusion.86 = f32[64,1024]{1,0:T(8,128)S(1)} fusion(bf16[64,1024]{1,0:T(8,128)(2,1)S(1)} %add_convert_fusion.9, bf16[10,1024,1024]{2,1,0:T(8,128)(2,1)} %param.3), kind=kOutput, calls=%fused_computation.86 | convolution fusion | flops 134217728 | bytes 2490368 | tf_op jit(solution)/shard_map/dot_general | solution.py:14
  32.4 2.4 %fusion.82 = f32[64,1024]{1,0:T(8,128)S(1)} fusion(bf16[64,1024]{1,0:T(8,128)(2,1)S(1)} %add_convert_fusion.8, bf16[10,1024,1024]{2,1,0:T(8,128)(2,1)} %param.3), kind=kOutput, calls=%fused_computation.82 | convolution fusion | flops 134217728 | bytes 2490368 | tf_op jit(solution)/shard_map/dot_general | solution.py:14
  34.8 2.4 %fusion.62 = f32[64,1024]{1,0:T(8,128)S(1)} fusion(bf16[64,1024]{1,0:T(8,128)(2,1)S(1)} %add_convert_fusion.9, bf16[10,1024,1024]{2,1,0:T(8,128)(2,1)} %param.3), kind=kOutput, calls=%fused_computation.62 | convolution fusion | flops 134217728 | bytes 2490368 | tf_op jit(solution)/shard_map/dot_general | solution.py:14
  37.2 2.4 %fusion.58 = f32[64,1024]{1,0:T(8,128)S(1)} fusion(bf16[64,1024]{1,0:T(8,128)(2,1)S(1)} %add_convert_fusion.8, bf16[10,1024,1024]{2,1,0:T(8,128)(2,1)} %param.3), kind=kOutput, calls=%fused_computation.58 | convolution fusion | flops 134217728 | bytes 2490368 | tf_op jit(solution)/shard_map/dot_general | solution.py:14
  39.5 2.4 %fusion.30 = f32[64,1024]{1,0:T(8,128)S(1)} fusion(bf16[64,1024]{1,0:T(8,128)(2,1)S(1)} %add_convert_fusion.9, bf16[10,1024,1024]{2,1,0:T(8,128)(2,1)} %param.3), kind=kOutput, calls=%fused_computation.30 | convolution fusion | flops 134217728 | bytes 2490368 | tf_op jit(solution)/shard_map/dot_general | solution.py:14
  41.9 2.4 %fusion.26 = f32[64,1024]{1,0:T(8,128)S(1)} fusion(bf16[64,1024]{1,0:T(8,128)(2,1)S(1)} %add_convert_fusion.8, bf16[10,1024,1024]{2,1,0:T(8,128)(2,1)} %param.3), kind=kOutput, calls=%fused_computation.26 | convolution fusion | flops 134217728 | bytes 2490368 | tf_op jit(solution)/shard_map/dot_general | solution.py:14
  51.0 1.6 collective-permute-start.7
  53.9 0.9 fusion.24
  54.8 2.4 %collective-permute-done.7 = bf16[64,1024]{1,0:T(8,128)(2,1)S(1)} collective-permute-done((bf16[64,1024]{1,0:T(8,128)(2,1)S(1)}, bf16[64,1024]{1,0:T(8,128)(2,1)S(1)}, u32[]{:S(2)}, u32[]{:S(2)}) %collective-permute-start.7) | collective-permute-done | bytes 131104 | tf_op jit(solution)/shard_map/ppermute | solution.py:20
  57.2 2.1 collective-permute-done.13
  61.6 1.5 collective-permute-start.9
  64.5 3.5 %collective-permute-done.9 = bf16[64,1024]{1,0:T(8,128)(2,1)S(1)} collective-permute-done((bf16[64,1024]{1,0:T(8,128)(2,1)S(1)}, bf16[64,1024]{1,0:T(8,128)(2,1)S(1)}, u32[]{:S(2)}, u32[]{:S(2)}) %collective-permute-start.9) | collective-permute-done | bytes 131104 | tf_op jit(solution)/shard_map/ppermute | solution.py:20
  68.8 3.5 %collective-permute-start.10 = (bf16[64,1024]{1,0:T(8,128)(2,1)S(1)}, bf16[64,1024]{1,0:T(8,128)(2,1)S(1)}, u32[]{:S(2)}, u32[]{:S(2)}) collective-permute-start(bf16[64,1024]{1,0:T(8,128)(2,1)S(1)} %get-tuple-element.26), channel_id=1, source_target_pairs={{0,8},{4,12},{8,0},{12,4},{1,9},{5,13},{9,1},{13,5},{2,10},{6,14},... | collective-permute-start | bytes 393224 | tf_op jit(solution)/shard_map/ppermute | solution.py:20
  73.0 2.0 collective-permute-start.16
  75.0 6.4 %collective-permute-done.10 = bf16[64,1024]{1,0:T(8,128)(2,1)S(1)} collective-permute-done((bf16[64,1024]{1,0:T(8,128)(2,1)S(1)}, bf16[64,1024]{1,0:T(8,128)(2,1)S(1)}, u32[]{:S(2)}, u32[]{:S(2)}) %collective-permute-start.10) | collective-permute-done | bytes 131104 | tf_op jit(solution)/shard_map/ppermute | solution.py:20
  83.0 1.5 collective-permute-start.17
  91.6 1.6 collective-permute-start.19
  95.3 2.7 %collective-permute-done.19 = bf16[64,1024]{1,0:T(8,128)(2,1)S(1)} collective-permute-done((bf16[64,1024]{1,0:T(8,128)(2,1)S(1)}, bf16[64,1024]{1,0:T(8,128)(2,1)S(1)}, u32[]{:S(2)}, u32[]{:S(2)}) %collective-permute-start.19) | collective-permute-done | bytes 131104 | tf_op jit(solution)/shard_map/ppermute | solution.py:20
  97.9 2.4 %collective-permute-done.25 = bf16[64,1024]{1,0:T(8,128)(2,1)S(1)} collective-permute-done((bf16[64,1024]{1,0:T(8,128)(2,1)S(1)}, bf16[64,1024]{1,0:T(8,128)(2,1)S(1)}, u32[]{:S(2)}, u32[]{:S(2)}) %collective-permute-start.25) | collective-permute-done | bytes 131104 | tf_op jit(solution)/shard_map/ppermute | solution.py:20
  102.6 1.0 collective-permute-start.21
  104.4 1.1 collective-permute-start.27
  105.5 3.5 %collective-permute-done.21 = bf16[64,1024]{1,0:T(8,128)(2,1)S(1)} collective-permute-done((bf16[64,1024]{1,0:T(8,128)(2,1)S(1)}, bf16[64,1024]{1,0:T(8,128)(2,1)S(1)}, u32[]{:S(2)}, u32[]{:S(2)}) %collective-permute-start.21) | collective-permute-done | bytes 131104 | tf_op jit(solution)/shard_map/ppermute | solution.py:20
  109.8 1.6 collective-permute-start.22
  112.1 1.6 collective-permute-start.28
  113.7 7.8 %collective-permute-done.22 = bf16[64,1024]{1,0:T(8,128)(2,1)S(1)} collective-permute-done((bf16[64,1024]{1,0:T(8,128)(2,1)S(1)}, bf16[64,1024]{1,0:T(8,128)(2,1)S(1)}, u32[]{:S(2)}, u32[]{:S(2)}) %collective-permute-start.22) | collective-permute-done | bytes 131104 | tf_op jit(solution)/shard_map/ppermute | solution.py:20
  122.4 0.9 collective-permute-done.28
  123.3 1.4 collective-permute-start.29
  125.5 2.4 %collective-permute-done.23 = bf16[64,1024]{1,0:T(8,128)(2,1)S(1)} collective-permute-done((bf16[64,1024]{1,0:T(8,128)(2,1)S(1)}, bf16[64,1024]{1,0:T(8,128)(2,1)S(1)}, u32[]{:S(2)}, u32[]{:S(2)}) %collective-permute-start.23) | collective-permute-done | bytes 131104 | tf_op jit(solution)/shard_map/ppermute | solution.py:20
  130.1 0.8 fusion.373
  130.9 1.6 collective-permute-start.31
  132.4 0.8 fusion.372
  134.6 2.7 %collective-permute-done.31 = bf16[64,1024]{1,0:T(8,128)(2,1)S(1)} collective-permute-done((bf16[64,1024]{1,0:T(8,128)(2,1)S(1)}, bf16[64,1024]{1,0:T(8,128)(2,1)S(1)}, u32[]{:S(2)}, u32[]{:S(2)}) %collective-permute-start.31) | collective-permute-done | bytes 131104 | tf_op jit(solution)/shard_map/ppermute | solution.py:20
  137.2 2.4 %collective-permute-done.37 = bf16[64,1024]{1,0:T(8,128)(2,1)S(1)} collective-permute-done((bf16[64,1024]{1,0:T(8,128)(2,1)S(1)}, bf16[64,1024]{1,0:T(8,128)(2,1)S(1)}, u32[]{:S(2)}, u32[]{:S(2)}) %collective-permute-start.37) | collective-permute-done | bytes 131104 | tf_op jit(solution)/shard_map/ppermute | solution.py:20
  143.2 1.7 collective-permute-start.39
  144.8 3.5 %collective-permute-done.33 = bf16[64,1024]{1,0:T(8,128)(2,1)S(1)} collective-permute-done((bf16[64,1024]{1,0:T(8,128)(2,1)S(1)}, bf16[64,1024]{1,0:T(8,128)(2,1)S(1)}, u32[]{:S(2)}, u32[]{:S(2)}) %collective-permute-start.33) | collective-permute-done | bytes 131104 | tf_op jit(solution)/shard_map/ppermute | solution.py:20
  149.1 1.1 collective-permute-start.34
  151.1 1.8 collective-permute-start.40
  152.9 7.6 %collective-permute-done.34 = bf16[64,1024]{1,0:T(8,128)(2,1)S(1)} collective-permute-done((bf16[64,1024]{1,0:T(8,128)(2,1)S(1)}, bf16[64,1024]{1,0:T(8,128)(2,1)S(1)}, u32[]{:S(2)}, u32[]{:S(2)}) %collective-permute-start.34) | collective-permute-done | bytes 131104 | tf_op jit(solution)/shard_map/ppermute | solution.py:20
  160.6 1.9 collective-permute-done.40
  162.7 4.0 %collective-permute-done.35 = bf16[64,1024]{1,0:T(8,128)(2,1)S(1)} collective-permute-done((bf16[64,1024]{1,0:T(8,128)(2,1)S(1)}, bf16[64,1024]{1,0:T(8,128)(2,1)S(1)}, u32[]{:S(2)}, u32[]{:S(2)}) %collective-permute-start.35) | collective-permute-done | bytes 131104 | tf_op jit(solution)/shard_map/ppermute | solution.py:20
  167.6 0.8 collective-permute-done.41
  169.2 0.8 fusion.377
  170.0 1.6 collective-permute-start.43
  171.5 0.8 fusion.376
  173.0 3.3 %collective-permute-done.43 = bf16[64,1024]{1,0:T(8,128)(2,1)S(1)} collective-permute-done((bf16[64,1024]{1,0:T(8,128)(2,1)S(1)}, bf16[64,1024]{1,0:T(8,128)(2,1)S(1)}, u32[]{:S(2)}, u32[]{:S(2)}) %collective-permute-start.43) | collective-permute-done | bytes 131104 | tf_op jit(solution)/shard_map/ppermute | solution.py:20
  176.3 2.4 %collective-permute-done.49 = bf16[64,1024]{1,0:T(8,128)(2,1)S(1)} collective-permute-done((bf16[64,1024]{1,0:T(8,128)(2,1)S(1)}, bf16[64,1024]{1,0:T(8,128)(2,1)S(1)}, u32[]{:S(2)}, u32[]{:S(2)}) %collective-permute-start.49) | collective-permute-done | bytes 131104 | tf_op jit(solution)/shard_map/ppermute | solution.py:20
  181.9 2.1 collective-permute-start.45
  183.9 3.5 %collective-permute-done.51 = bf16[64,1024]{1,0:T(8,128)(2,1)S(1)} collective-permute-done((bf16[64,1024]{1,0:T(8,128)(2,1)S(1)}, bf16[64,1024]{1,0:T(8,128)(2,1)S(1)}, u32[]{:S(2)}, u32[]{:S(2)}) %collective-permute-start.51) | collective-permute-done | bytes 131104 | tf_op jit(solution)/shard_map/ppermute | solution.py:20
  188.2 0.9 collective-permute-start.52
  190.2 1.8 collective-permute-start.46
  192.0 7.2 %collective-permute-done.52 = bf16[64,1024]{1,0:T(8,128)(2,1)S(1)} collective-permute-done((bf16[64,1024]{1,0:T(8,128)(2,1)S(1)}, bf16[64,1024]{1,0:T(8,128)(2,1)S(1)}, u32[]{:S(2)}, u32[]{:S(2)}) %collective-permute-start.52) | collective-permute-done | bytes 131104 | tf_op jit(solution)/shard_map/ppermute | solution.py:20
  199.3 2.2 %collective-permute-done.46 = bf16[64,1024]{1,0:T(8,128)(2,1)S(1)} collective-permute-done((bf16[64,1024]{1,0:T(8,128)(2,1)S(1)}, bf16[64,1024]{1,0:T(8,128)(2,1)S(1)}, u32[]{:S(2)}, u32[]{:S(2)}) %collective-permute-start.46) | collective-permute-done | bytes 131104 | tf_op jit(solution)/shard_map/ppermute | solution.py:20
  201.7 3.1 %collective-permute-done.53 = bf16[64,1024]{1,0:T(8,128)(2,1)S(1)} collective-permute-done((bf16[64,1024]{1,0:T(8,128)(2,1)S(1)}, bf16[64,1024]{1,0:T(8,128)(2,1)S(1)}, u32[]{:S(2)}, u32[]{:S(2)}) %collective-permute-start.53) | collective-permute-done | bytes 131104 | tf_op jit(solution)/shard_map/ppermute | solution.py:20
  204.8 2.3 %collective-permute-done.47 = bf16[64,1024]{1,0:T(8,128)(2,1)S(1)} collective-permute-done((bf16[64,1024]{1,0:T(8,128)(2,1)S(1)}, bf16[64,1024]{1,0:T(8,128)(2,1)S(1)}, u32[]{:S(2)}, u32[]{:S(2)}) %collective-permute-start.47) | collective-permute-done | bytes 131104 | tf_op jit(solution)/shard_map/ppermute | solution.py:20
  (147 shorter events, 50.6 us)
Async XLA Ops:
  2.2 8.7 %copy-start.1 = (bf16[2,2,64,1024]{3,2,1,0:T(8,128)(2,1)}, bf16[2,2,64,1024]{3,2,1,0:T(8,128)(2,1)S(1)}, u32[]{:S(2)}) copy-start(bf16[2,2,64,1024]{3,2,1,0:T(8,128)(2,1)S(1)} %reverse_select_fusion.4) | copy-start | bytes 1572868
  5.4 6.9 %collective-permute-start = (bf16[64,1024]{1,0:T(8,128)(2,1)}, bf16[64,1024]{1,0:T(8,128)(2,1)S(1)}, u32[]{:S(2)}, u32[]{:S(2)}) collective-permute-start(bf16[64,1024]{1,0:T(8,128)(2,1)} %fusion.318), channel_id=1, source_target_pairs={{0,4},{4,0},{8,12},{12,8},{1,5},{5,1},{9,13},{13,9},{2,6},{6,2},{1... | collective-permute-start | bytes 393224 | tf_op jit(solution)/shard_map/ppermute | solution.py:20
  10.8 7.1 %collective-permute-start.3 = (bf16[64,1024]{1,0:T(8,128)(2,1)S(1)}, bf16[64,1024]{1,0:T(8,128)(2,1)S(1)}, u32[]{:S(2)}, u32[]{:S(2)}) collective-permute-start(bf16[64,1024]{1,0:T(8,128)(2,1)S(1)} %fusion.321), channel_id=1, source_target_pairs={{0,4},{4,0},{8,12},{12,8},{1,5},{5,1},{9,13},{13,9},{2,6},{6,2},{1... | collective-permute-start | bytes 393224 | tf_op jit(solution)/shard_map/ppermute | solution.py:20
  12.2 32.0 %copy-start = (bf16[10,1024,1024]{2,1,0:T(8,128)(2,1)S(1)}, bf16[10,1024,1024]{2,1,0:T(8,128)(2,1)}, u32[]{:S(2)}) copy-start(bf16[10,1024,1024]{2,1,0:T(8,128)(2,1)} %param.3) | copy-start | bytes 62914564
  14.8 8.8 %collective-permute-start.1 = (bf16[64,1024]{1,0:T(8,128)(2,1)S(1)}, bf16[64,1024]{1,0:T(8,128)(2,1)S(1)}, u32[]{:S(2)}, u32[]{:S(2)}) collective-permute-start(bf16[64,1024]{1,0:T(8,128)(2,1)S(1)} %get-tuple-element.18), channel_id=1, source_target_pairs={{0,8},{4,12},{8,0},{12,4},{1,9},{5,13},{9,1},{13,5},{2,10},{6,14},... | collective-permute-start | bytes 393224 | tf_op jit(solution)/shard_map/ppermute | solution.py:20
  21.1 8.3 %collective-permute-start.4 = (bf16[64,1024]{1,0:T(8,128)(2,1)S(1)}, bf16[64,1024]{1,0:T(8,128)(2,1)S(1)}, u32[]{:S(2)}, u32[]{:S(2)}) collective-permute-start(bf16[64,1024]{1,0:T(8,128)(2,1)S(1)} %get-tuple-element.20), channel_id=1, source_target_pairs={{0,8},{4,12},{8,0},{12,4},{1,9},{5,13},{9,1},{13,5},{2,10},{6,14},... | collective-permute-start | bytes 393224 | tf_op jit(solution)/shard_map/ppermute | solution.py:20
  23.7 20.5 %collective-permute-start.2 = (bf16[64,1024]{1,0:T(8,128)(2,1)S(1)}, bf16[64,1024]{1,0:T(8,128)(2,1)S(1)}, u32[]{:S(2)}, u32[]{:S(2)}) collective-permute-start(bf16[64,1024]{1,0:T(8,128)(2,1)S(1)} %add_convert_fusion.9), channel_id=1, source_target_pairs={{0,4},{4,0},{8,12},{12,8},{1,5},{5,1},{9,13},{13,9},{2,6},{6,2},{1... | collective-permute-start | bytes 393224 | tf_op jit(solution)/shard_map/ppermute | solution.py:20
  29.4 15.7 %collective-permute-start.5 = (bf16[64,1024]{1,0:T(8,128)(2,1)S(1)}, bf16[64,1024]{1,0:T(8,128)(2,1)S(1)}, u32[]{:S(2)}, u32[]{:S(2)}) collective-permute-start(bf16[64,1024]{1,0:T(8,128)(2,1)S(1)} %add_convert_fusion.8), channel_id=1, source_target_pairs={{0,4},{4,0},{8,12},{12,8},{1,5},{5,1},{9,13},{13,9},{2,6},{6,2},{1... | collective-permute-start | bytes 393224 | tf_op jit(solution)/shard_map/ppermute | solution.py:20
  45.0 5.2 %collective-permute-start.6 = (bf16[64,1024]{1,0:T(8,128)(2,1)S(1)}, bf16[64,1024]{1,0:T(8,128)(2,1)S(1)}, u32[]{:S(2)}, u32[]{:S(2)}) collective-permute-start(bf16[64,1024]{1,0:T(8,128)(2,1)S(1)} %fusion.324), channel_id=1, source_target_pairs={{0,1},{1,0},{2,3},{3,2},{4,5},{5,4},{6,7},{7,6},{8,9},{9,8},{10,11... | collective-permute-start | bytes 393224 | tf_op jit(solution)/shard_map/ppermute | solution.py:20
  45.8 6.7 %collective-permute-start.12 = (bf16[64,1024]{1,0:T(8,128)(2,1)S(1)}, bf16[64,1024]{1,0:T(8,128)(2,1)S(1)}, u32[]{:S(2)}, u32[]{:S(2)}) collective-permute-start(bf16[64,1024]{1,0:T(8,128)(2,1)S(1)} %fusion.327), channel_id=1, source_target_pairs={{0,1},{1,0},{2,3},{3,2},{4,5},{5,4},{6,7},{7,6},{8,9},{9,8},{10,11... | collective-permute-start | bytes 393224 | tf_op jit(solution)/shard_map/ppermute | solution.py:20
  46.4 14.4 %slice-start = ((s8[10485760]{0:T(1024)(128)(4,1)}), s8[4194304]{0:T(1024)(128)(4,1)S(1)}, s32[]{:S(2)}) async-start(s8[10485760]{0:T(1024)(128)(4,1)} %bitcast.444), calls=%async_computation | async-start | bytes 8388608
  47.9 12.9 %slice-start.1 = ((s8[10485760]{0:T(1024)(128)(4,1)}), s8[4194304]{0:T(1024)(128)(4,1)S(1)}, s32[]{:S(2)}) async-start(s8[10485760]{0:T(1024)(128)(4,1)} %bitcast.444), calls=%async_computation.1 | async-start | bytes 8388608
  50.2 10.6 %slice-start.2 = ((s8[10485760]{0:T(1024)(128)(4,1)}), s8[2097152]{0:T(1024)(128)(4,1)S(1)}, s32[]{:S(2)}) async-start(s8[10485760]{0:T(1024)(128)(4,1)} %bitcast.444), calls=%async_computation.2 | async-start | bytes 4194304
  51.0 6.2 %collective-permute-start.7 = (bf16[64,1024]{1,0:T(8,128)(2,1)S(1)}, bf16[64,1024]{1,0:T(8,128)(2,1)S(1)}, u32[]{:S(2)}, u32[]{:S(2)}) collective-permute-start(bf16[64,1024]{1,0:T(8,128)(2,1)S(1)} %get-tuple-element.24), channel_id=1, source_target_pairs={{0,2},{1,3},{2,0},{3,1},{4,6},{5,7},{6,4},{7,5},{8,10},{9,11},{10,... | collective-permute-start | bytes 393224 | tf_op jit(solution)/shard_map/ppermute | solution.py:20
  53.3 6.0 %collective-permute-start.13 = (bf16[64,1024]{1,0:T(8,128)(2,1)S(1)}, bf16[64,1024]{1,0:T(8,128)(2,1)S(1)}, u32[]{:S(2)}, u32[]{:S(2)}) collective-permute-start(bf16[64,1024]{1,0:T(8,128)(2,1)S(1)} %get-tuple-element.22), channel_id=1, source_target_pairs={{0,2},{1,3},{2,0},{3,1},{4,6},{5,7},{6,4},{7,5},{8,10},{9,11},{10,... | collective-permute-start | bytes 393224 | tf_op jit(solution)/shard_map/ppermute | solution.py:20
  59.4 1.4 collective-permute-start.8
  59.6 3.5 %collective-permute-start.14 = (bf16[64,1024]{1,0:T(8,128)(2,1)S(1)}, bf16[64,1024]{1,0:T(8,128)(2,1)S(1)}, u32[]{:S(2)}, u32[]{:S(2)}) collective-permute-start(bf16[64,1024]{1,0:T(8,128)(2,1)S(1)} %get-tuple-element.16), channel_id=1, source_target_pairs={{0,1},{1,0},{2,3},{3,2},{4,5},{5,4},{6,7},{7,6},{8,9},{9,8},{10,11... | collective-permute-start | bytes 393224 | tf_op jit(solution)/shard_map/ppermute | solution.py:20
  61.6 6.4 %collective-permute-start.9 = (bf16[64,1024]{1,0:T(8,128)(2,1)S(1)}, bf16[64,1024]{1,0:T(8,128)(2,1)S(1)}, u32[]{:S(2)}, u32[]{:S(2)}) collective-permute-start(bf16[64,1024]{1,0:T(8,128)(2,1)S(1)} %fusion.330), channel_id=1, source_target_pairs={{0,4},{4,0},{8,12},{12,8},{1,5},{5,1},{9,13},{13,9},{2,6},{6,2},{1... | collective-permute-start | bytes 393224 | tf_op jit(solution)/shard_map/ppermute | solution.py:20
  63.8 8.4 %collective-permute-start.15 = (bf16[64,1024]{1,0:T(8,128)(2,1)S(1)}, bf16[64,1024]{1,0:T(8,128)(2,1)S(1)}, u32[]{:S(2)}, u32[]{:S(2)}) collective-permute-start(bf16[64,1024]{1,0:T(8,128)(2,1)S(1)} %fusion.333), channel_id=1, source_target_pairs={{0,4},{4,0},{8,12},{12,8},{1,5},{5,1},{9,13},{13,9},{2,6},{6,2},{1... | collective-permute-start | bytes 393224 | tf_op jit(solution)/shard_map/ppermute | solution.py:20
  68.8 12.7 %collective-permute-start.10 = (bf16[64,1024]{1,0:T(8,128)(2,1)S(1)}, bf16[64,1024]{1,0:T(8,128)(2,1)S(1)}, u32[]{:S(2)}, u32[]{:S(2)}) collective-permute-start(bf16[64,1024]{1,0:T(8,128)(2,1)S(1)} %get-tuple-element.26), channel_id=1, source_target_pairs={{0,8},{4,12},{8,0},{12,4},{1,9},{5,13},{9,1},{13,5},{2,10},{6,14},... | collective-permute-start | bytes 393224 | tf_op jit(solution)/shard_map/ppermute | solution.py:20
  73.0 9.9 %collective-permute-start.16 = (bf16[64,1024]{1,0:T(8,128)(2,1)S(1)}, bf16[64,1024]{1,0:T(8,128)(2,1)S(1)}, u32[]{:S(2)}, u32[]{:S(2)}) collective-permute-start(bf16[64,1024]{1,0:T(8,128)(2,1)S(1)} %get-tuple-element.28), channel_id=1, source_target_pairs={{0,8},{4,12},{8,0},{12,4},{1,9},{5,13},{9,1},{13,5},{2,10},{6,14},... | collective-permute-start | bytes 393224 | tf_op jit(solution)/shard_map/ppermute | solution.py:20
  81.5 5.6 %collective-permute-start.11 = (bf16[64,1024]{1,0:T(8,128)(2,1)S(1)}, bf16[64,1024]{1,0:T(8,128)(2,1)S(1)}, u32[]{:S(2)}, u32[]{:S(2)}) collective-permute-start(bf16[64,1024]{1,0:T(8,128)(2,1)S(1)} %add_convert_fusion.7), channel_id=1, source_target_pairs={{0,4},{4,0},{8,12},{12,8},{1,5},{5,1},{9,13},{13,9},{2,6},{6,2},{1... | collective-permute-start | bytes 393224 | tf_op jit(solution)/shard_map/ppermute | solution.py:20
  83.0 5.5 %collective-permute-start.17 = (bf16[64,1024]{1,0:T(8,128)(2,1)S(1)}, bf16[64,1024]{1,0:T(8,128)(2,1)S(1)}, u32[]{:S(2)}, u32[]{:S(2)}) collective-permute-start(bf16[64,1024]{1,0:T(8,128)(2,1)S(1)} %add_convert_fusion.6), channel_id=1, source_target_pairs={{0,4},{4,0},{8,12},{12,8},{1,5},{5,1},{9,13},{13,9},{2,6},{6,2},{1... | collective-permute-start | bytes 393224 | tf_op jit(solution)/shard_map/ppermute | solution.py:20
  87.8 3.0 %collective-permute-start.18 = (bf16[64,1024]{1,0:T(8,128)(2,1)S(1)}, bf16[64,1024]{1,0:T(8,128)(2,1)S(1)}, u32[]{:S(2)}, u32[]{:S(2)}) collective-permute-start(bf16[64,1024]{1,0:T(8,128)(2,1)S(1)} %fusion.315), channel_id=1, source_target_pairs={{0,1},{1,0},{2,3},{3,2},{4,5},{5,4},{6,7},{7,6},{8,9},{9,8},{10,11... | collective-permute-start | bytes 393224 | tf_op jit(solution)/shard_map/ppermute | solution.py:20
  89.2 3.9 %collective-permute-start.24 = (bf16[64,1024]{1,0:T(8,128)(2,1)S(1)}, bf16[64,1024]{1,0:T(8,128)(2,1)S(1)}, u32[]{:S(2)}, u32[]{:S(2)}) collective-permute-start(bf16[64,1024]{1,0:T(8,128)(2,1)S(1)} %fusion.312), channel_id=1, source_target_pairs={{0,1},{1,0},{2,3},{3,2},{4,5},{5,4},{6,7},{7,6},{8,9},{9,8},{10,11... | collective-permute-start | bytes 393224 | tf_op jit(solution)/shard_map/ppermute | solution.py:20
  91.6 6.4 %collective-permute-start.19 = (bf16[64,1024]{1,0:T(8,128)(2,1)S(1)}, bf16[64,1024]{1,0:T(8,128)(2,1)S(1)}, u32[]{:S(2)}, u32[]{:S(2)}) collective-permute-start(bf16[64,1024]{1,0:T(8,128)(2,1)S(1)} %get-tuple-element.32), channel_id=1, source_target_pairs={{0,2},{1,3},{2,0},{3,1},{4,6},{5,7},{6,4},{7,5},{8,10},{9,11},{10,... | collective-permute-start | bytes 393224 | tf_op jit(solution)/shard_map/ppermute | solution.py:20
  93.9 6.4 %collective-permute-start.25 = (bf16[64,1024]{1,0:T(8,128)(2,1)S(1)}, bf16[64,1024]{1,0:T(8,128)(2,1)S(1)}, u32[]{:S(2)}, u32[]{:S(2)}) collective-permute-start(bf16[64,1024]{1,0:T(8,128)(2,1)S(1)} %get-tuple-element.30), channel_id=1, source_target_pairs={{0,2},{1,3},{2,0},{3,1},{4,6},{5,7},{6,4},{7,5},{8,10},{9,11},{10,... | collective-permute-start | bytes 393224 | tf_op jit(solution)/shard_map/ppermute | solution.py:20
  100.5 1.4 collective-permute-start.20
  101.3 2.4 %collective-permute-start.26 = (bf16[64,1024]{1,0:T(8,128)(2,1)S(1)}, bf16[64,1024]{1,0:T(8,128)(2,1)S(1)}, u32[]{:S(2)}, u32[]{:S(2)}) collective-permute-start(bf16[64,1024]{1,0:T(8,128)(2,1)S(1)} %get-tuple-element.14), channel_id=1, source_target_pairs={{0,1},{1,0},{2,3},{3,2},{4,5},{5,4},{6,7},{7,6},{8,9},{9,8},{10,11... | collective-permute-start | bytes 393224 | tf_op jit(solution)/shard_map/ppermute | solution.py:20
  102.6 6.4 %collective-permute-start.21 = (bf16[64,1024]{1,0:T(8,128)(2,1)S(1)}, bf16[64,1024]{1,0:T(8,128)(2,1)S(1)}, u32[]{:S(2)}, u32[]{:S(2)}) collective-permute-start(bf16[64,1024]{1,0:T(8,128)(2,1)S(1)} %fusion.336), channel_id=1, source_target_pairs={{0,4},{4,0},{8,12},{12,8},{1,5},{5,1},{9,13},{13,9},{2,6},{6,2},{1... | collective-permute-start | bytes 393224 | tf_op jit(solution)/shard_map/ppermute | solution.py:20
  104.4 7.0 %collective-permute-start.27 = (bf16[64,1024]{1,0:T(8,128)(2,1)S(1)}, bf16[64,1024]{1,0:T(8,128)(2,1)S(1)}, u32[]{:S(2)}, u32[]{:S(2)}) collective-permute-start(bf16[64,1024]{1,0:T(8,128)(2,1)S(1)} %fusion.339), channel_id=1, source_target_pairs={{0,4},{4,0},{8,12},{12,8},{1,5},{5,1},{9,13},{13,9},{2,6},{6,2},{1... | collective-permute-start | bytes 393224 | tf_op jit(solution)/shard_map/ppermute | solution.py:20
  109.8 11.7 %collective-permute-start.22 = (bf16[64,1024]{1,0:T(8,128)(2,1)S(1)}, bf16[64,1024]{1,0:T(8,128)(2,1)S(1)}, u32[]{:S(2)}, u32[]{:S(2)}) collective-permute-start(bf16[64,1024]{1,0:T(8,128)(2,1)S(1)} %get-tuple-element.34), channel_id=1, source_target_pairs={{0,8},{4,12},{8,0},{12,4},{1,9},{5,13},{9,1},{13,5},{2,10},{6,14},... | collective-permute-start | bytes 393224 | tf_op jit(solution)/shard_map/ppermute | solution.py:20
  112.1 11.1 %collective-permute-start.28 = (bf16[64,1024]{1,0:T(8,128)(2,1)S(1)}, bf16[64,1024]{1,0:T(8,128)(2,1)S(1)}, u32[]{:S(2)}, u32[]{:S(2)}) collective-permute-start(bf16[64,1024]{1,0:T(8,128)(2,1)S(1)} %get-tuple-element.36), channel_id=1, source_target_pairs={{0,8},{4,12},{8,0},{12,4},{1,9},{5,13},{9,1},{13,5},{2,10},{6,14},... | collective-permute-start | bytes 393224 | tf_op jit(solution)/shard_map/ppermute | solution.py:20
  121.5 6.3 %collective-permute-start.23 = (bf16[64,1024]{1,0:T(8,128)(2,1)S(1)}, bf16[64,1024]{1,0:T(8,128)(2,1)S(1)}, u32[]{:S(2)}, u32[]{:S(2)}) collective-permute-start(bf16[64,1024]{1,0:T(8,128)(2,1)S(1)} %add_convert_fusion.5), channel_id=1, source_target_pairs={{0,4},{4,0},{8,12},{12,8},{1,5},{5,1},{9,13},{13,9},{2,6},{6,2},{1... | collective-permute-start | bytes 393224 | tf_op jit(solution)/shard_map/ppermute | solution.py:20
  123.3 6.0 %collective-permute-start.29 = (bf16[64,1024]{1,0:T(8,128)(2,1)S(1)}, bf16[64,1024]{1,0:T(8,128)(2,1)S(1)}, u32[]{:S(2)}, u32[]{:S(2)}) collective-permute-start(bf16[64,1024]{1,0:T(8,128)(2,1)S(1)} %add_convert_fusion.4), channel_id=1, source_target_pairs={{0,4},{4,0},{8,12},{12,8},{1,5},{5,1},{9,13},{13,9},{2,6},{6,2},{1... | collective-permute-start | bytes 393224 | tf_op jit(solution)/shard_map/ppermute | solution.py:20
  128.6 1.5 collective-permute-start.30
  130.0 2.4 %collective-permute-start.36 = (bf16[64,1024]{1,0:T(8,128)(2,1)S(1)}, bf16[64,1024]{1,0:T(8,128)(2,1)S(1)}, u32[]{:S(2)}, u32[]{:S(2)}) collective-permute-start(bf16[64,1024]{1,0:T(8,128)(2,1)S(1)} %fusion.306), channel_id=1, source_target_pairs={{0,1},{1,0},{2,3},{3,2},{4,5},{5,4},{6,7},{7,6},{8,9},{9,8},{10,11... | collective-permute-start | bytes 393224 | tf_op jit(solution)/shard_map/ppermute | solution.py:20
  130.9 6.4 %collective-permute-start.31 = (bf16[64,1024]{1,0:T(8,128)(2,1)S(1)}, bf16[64,1024]{1,0:T(8,128)(2,1)S(1)}, u32[]{:S(2)}, u32[]{:S(2)}) collective-permute-start(bf16[64,1024]{1,0:T(8,128)(2,1)S(1)} %get-tuple-element.40), channel_id=1, source_target_pairs={{0,2},{1,3},{2,0},{3,1},{4,6},{5,7},{6,4},{7,5},{8,10},{9,11},{10,... | collective-permute-start | bytes 393224 | tf_op jit(solution)/shard_map/ppermute | solution.py:20
  133.2 6.4 %collective-permute-start.37 = (bf16[64,1024]{1,0:T(8,128)(2,1)S(1)}, bf16[64,1024]{1,0:T(8,128)(2,1)S(1)}, u32[]{:S(2)}, u32[]{:S(2)}) collective-permute-start(bf16[64,1024]{1,0:T(8,128)(2,1)S(1)} %get-tuple-element.38), channel_id=1, source_target_pairs={{0,2},{1,3},{2,0},{3,1},{4,6},{5,7},{6,4},{7,5},{8,10},{9,11},{10,... | collective-permute-start | bytes 393224 | tf_op jit(solution)/shard_map/ppermute | solution.py:20
  139.7 1.4 collective-permute-start.32
  140.6 1.8 collective-permute-start.38
  141.9 6.4 %collective-permute-start.33 = (bf16[64,1024]{1,0:T(8,128)(2,1)S(1)}, bf16[64,1024]{1,0:T(8,128)(2,1)S(1)}, u32[]{:S(2)}, u32[]{:S(2)}) collective-permute-start(bf16[64,1024]{1,0:T(8,128)(2,1)S(1)} %fusion.342), channel_id=1, source_target_pairs={{0,4},{4,0},{8,12},{12,8},{1,5},{5,1},{9,13},{13,9},{2,6},{6,2},{1... | collective-permute-start | bytes 393224 | tf_op jit(solution)/shard_map/ppermute | solution.py:20
  143.2 7.2 %collective-permute-start.39 = (bf16[64,1024]{1,0:T(8,128)(2,1)S(1)}, bf16[64,1024]{1,0:T(8,128)(2,1)S(1)}, u32[]{:S(2)}, u32[]{:S(2)}) collective-permute-start(bf16[64,1024]{1,0:T(8,128)(2,1)S(1)} %fusion.345), channel_id=1, source_target_pairs={{0,4},{4,0},{8,12},{12,8},{1,5},{5,1},{9,13},{13,9},{2,6},{6,2},{1... | collective-permute-start | bytes 393224 | tf_op jit(solution)/shard_map/ppermute | solution.py:20
  149.1 11.4 %collective-permute-start.34 = (bf16[64,1024]{1,0:T(8,128)(2,1)S(1)}, bf16[64,1024]{1,0:T(8,128)(2,1)S(1)}, u32[]{:S(2)}, u32[]{:S(2)}) collective-permute-start(bf16[64,1024]{1,0:T(8,128)(2,1)S(1)} %get-tuple-element.42), channel_id=1, source_target_pairs={{0,8},{4,12},{8,0},{12,4},{1,9},{5,13},{9,1},{13,5},{2,10},{6,14},... | collective-permute-start | bytes 393224 | tf_op jit(solution)/shard_map/ppermute | solution.py:20
  151.1 11.4 %collective-permute-start.40 = (bf16[64,1024]{1,0:T(8,128)(2,1)S(1)}, bf16[64,1024]{1,0:T(8,128)(2,1)S(1)}, u32[]{:S(2)}, u32[]{:S(2)}) collective-permute-start(bf16[64,1024]{1,0:T(8,128)(2,1)S(1)} %get-tuple-element.44), channel_id=1, source_target_pairs={{0,8},{4,12},{8,0},{12,4},{1,9},{5,13},{9,1},{13,5},{2,10},{6,14},... | collective-permute-start | bytes 393224 | tf_op jit(solution)/shard_map/ppermute | solution.py:20
  160.5 6.2 %collective-permute-start.35 = (bf16[64,1024]{1,0:T(8,128)(2,1)S(1)}, bf16[64,1024]{1,0:T(8,128)(2,1)S(1)}, u32[]{:S(2)}, u32[]{:S(2)}) collective-permute-start(bf16[64,1024]{1,0:T(8,128)(2,1)S(1)} %add_convert_fusion.3), channel_id=1, source_target_pairs={{0,4},{4,0},{8,12},{12,8},{1,5},{5,1},{9,13},{13,9},{2,6},{6,2},{1... | collective-permute-start | bytes 393224 | tf_op jit(solution)/shard_map/ppermute | solution.py:20
  162.5 5.8 %collective-permute-start.41 = (bf16[64,1024]{1,0:T(8,128)(2,1)S(1)}, bf16[64,1024]{1,0:T(8,128)(2,1)S(1)}, u32[]{:S(2)}, u32[]{:S(2)}) collective-permute-start(bf16[64,1024]{1,0:T(8,128)(2,1)S(1)} %add_convert_fusion.2), channel_id=1, source_target_pairs={{0,4},{4,0},{8,12},{12,8},{1,5},{5,1},{9,13},{13,9},{2,6},{6,2},{1... | collective-permute-start | bytes 393224 | tf_op jit(solution)/shard_map/ppermute | solution.py:20
  167.5 1.7 collective-permute-start.42
  169.1 2.4 %collective-permute-start.48 = (bf16[64,1024]{1,0:T(8,128)(2,1)S(1)}, bf16[64,1024]{1,0:T(8,128)(2,1)S(1)}, u32[]{:S(2)}, u32[]{:S(2)}) collective-permute-start(bf16[64,1024]{1,0:T(8,128)(2,1)S(1)} %fusion.300), channel_id=1, source_target_pairs={{0,1},{1,0},{2,3},{3,2},{4,5},{5,4},{6,7},{7,6},{8,9},{9,8},{10,11... | collective-permute-start | bytes 393224 | tf_op jit(solution)/shard_map/ppermute | solution.py:20
  170.0 6.4 %collective-permute-start.43 = (bf16[64,1024]{1,0:T(8,128)(2,1)S(1)}, bf16[64,1024]{1,0:T(8,128)(2,1)S(1)}, u32[]{:S(2)}, u32[]{:S(2)}) collective-permute-start(bf16[64,1024]{1,0:T(8,128)(2,1)S(1)} %get-tuple-element.48), channel_id=1, source_target_pairs={{0,2},{1,3},{2,0},{3,1},{4,6},{5,7},{6,4},{7,5},{8,10},{9,11},{10,... | collective-permute-start | bytes 393224 | tf_op jit(solution)/shard_map/ppermute | solution.py:20
  172.3 6.4 %collective-permute-start.49 = (bf16[64,1024]{1,0:T(8,128)(2,1)S(1)}, bf16[64,1024]{1,0:T(8,128)(2,1)S(1)}, u32[]{:S(2)}, u32[]{:S(2)}) collective-permute-start(bf16[64,1024]{1,0:T(8,128)(2,1)S(1)} %get-tuple-element.46), channel_id=1, source_target_pairs={{0,2},{1,3},{2,0},{3,1},{4,6},{5,7},{6,4},{7,5},{8,10},{9,11},{10,... | collective-permute-start | bytes 393224 | tf_op jit(solution)/shard_map/ppermute | solution.py:20
  178.8 1.4 collective-permute-start.50
  179.0 2.1 %collective-permute-start.44 = (bf16[64,1024]{1,0:T(8,128)(2,1)S(1)}, bf16[64,1024]{1,0:T(8,128)(2,1)S(1)}, u32[]{:S(2)}, u32[]{:S(2)}) collective-permute-start(bf16[64,1024]{1,0:T(8,128)(2,1)S(1)} %get-tuple-element.11), channel_id=1, source_target_pairs={{0,1},{1,0},{2,3},{3,2},{4,5},{5,4},{6,7},{7,6},{8,9},{9,8},{10,11... | collective-permute-start | bytes 393224 | tf_op jit(solution)/shard_map/ppermute | solution.py:20
  181.0 6.4 %collective-permute-start.51 = (bf16[64,1024]{1,0:T(8,128)(2,1)S(1)}, bf16[64,1024]{1,0:T(8,128)(2,1)S(1)}, u32[]{:S(2)}, u32[]{:S(2)}) collective-permute-start(bf16[64,1024]{1,0:T(8,128)(2,1)S(1)} %fusion.351), channel_id=1, source_target_pairs={{0,4},{4,0},{8,12},{12,8},{1,5},{5,1},{9,13},{13,9},{2,6},{6,2},{1... | collective-permute-start | bytes 393224 | tf_op jit(solution)/shard_map/ppermute | solution.py:20
  181.9 7.6 %collective-permute-start.45 = (bf16[64,1024]{1,0:T(8,128)(2,1)S(1)}, bf16[64,1024]{1,0:T(8,128)(2,1)S(1)}, u32[]{:S(2)}, u32[]{:S(2)}) collective-permute-start(bf16[64,1024]{1,0:T(8,128)(2,1)S(1)} %fusion.348), channel_id=1, source_target_pairs={{0,4},{4,0},{8,12},{12,8},{1,5},{5,1},{9,13},{13,9},{2,6},{6,2},{1... | collective-permute-start | bytes 393224 | tf_op jit(solution)/shard_map/ppermute | solution.py:20
  188.2 11.0 %collective-permute-start.52 = (bf16[64,1024]{1,0:T(8,128)(2,1)S(1)}, bf16[64,1024]{1,0:T(8,128)(2,1)S(1)}, u32[]{:S(2)}, u32[]{:S(2)}) collective-permute-start(bf16[64,1024]{1,0:T(8,128)(2,1)S(1)} %get-tuple-element.52), channel_id=1, source_target_pairs={{0,8},{4,12},{8,0},{12,4},{1,9},{5,13},{9,1},{13,5},{2,10},{6,14},... | collective-permute-start | bytes 393224 | tf_op jit(solution)/shard_map/ppermute | solution.py:20
  190.2 11.4 %collective-permute-start.46 = (bf16[64,1024]{1,0:T(8,128)(2,1)S(1)}, bf16[64,1024]{1,0:T(8,128)(2,1)S(1)}, u32[]{:S(2)}, u32[]{:S(2)}) collective-permute-start(bf16[64,1024]{1,0:T(8,128)(2,1)S(1)} %get-tuple-element.50), channel_id=1, source_target_pairs={{0,8},{4,12},{8,0},{12,4},{1,9},{5,13},{9,1},{13,5},{2,10},{6,14},... | collective-permute-start | bytes 393224 | tf_op jit(solution)/shard_map/ppermute | solution.py:20
  199.2 5.6 %collective-permute-start.53 = (bf16[64,1024]{1,0:T(8,128)(2,1)S(1)}, bf16[64,1024]{1,0:T(8,128)(2,1)S(1)}, u32[]{:S(2)}, u32[]{:S(2)}) collective-permute-start(bf16[64,1024]{1,0:T(8,128)(2,1)S(1)} %add_convert_fusion), channel_id=1, source_target_pairs={{0,4},{4,0},{8,12},{12,8},{1,5},{5,1},{9,13},{13,9},{2,6},{6,2},{1... | collective-permute-start | bytes 393224 | tf_op jit(solution)/shard_map/ppermute | solution.py:20
  201.6 5.5 %collective-permute-start.47 = (bf16[64,1024]{1,0:T(8,128)(2,1)S(1)}, bf16[64,1024]{1,0:T(8,128)(2,1)S(1)}, u32[]{:S(2)}, u32[]{:S(2)}) collective-permute-start(bf16[64,1024]{1,0:T(8,128)(2,1)S(1)} %add_convert_fusion.1), channel_id=1, source_target_pairs={{0,4},{4,0},{8,12},{12,8},{1,5},{5,1},{9,13},{13,9},{2,6},{6,2},{1... | collective-permute-start | bytes 393224 | tf_op jit(solution)/shard_map/ppermute | solution.py:20
  201.7 5.4 %copy-start.2 = (bf16[5,1024,64]{1,2,0:T(8,128)(2,1)}, bf16[5,1024,64]{1,2,0:T(8,128)(2,1)S(1)}, u32[]{:S(2)}) copy-start(bf16[5,1024,64]{1,2,0:T(8,128)(2,1)S(1)} %bitcast_dynamic-update-slice_fusion.1) | copy-start | bytes 1966084

commit v2 on v1

v2 whole, which is shorter than its diff:
```python
import jax
import jax.numpy as jnp
from jax import lax
from jax.sharding import PartitionSpec as P

STREAMS = 2
UNITS = 2 * STREAMS


def pair_index(block_row, column_index):
    return block_row * (block_row - 1) // 2 + column_index


def times_transposed(left, right):
    return lax.dot_general(left, right, (((1,), (1,)), ((), ())), preferred_element_type=jnp.float32)


def wide(value):
    return value.astype(jnp.float32)


def narrow(value):
    return value.astype(jnp.bfloat16)


class Order:
    def __init__(self):
        self.last = None

    def run(self, work, *values):
        if self.last is not None:
            *values, _ = lax.optimization_barrier((*values, self.last))
        result = work(*values)
        self.last = result[0] if isinstance(result, tuple) else result
        return result


def make_per_device(n_row, n_col):
    def trade(value, axis, step):
        size = n_row if axis == "row" else n_col
        return lax.ppermute(value, axis, [(i, i ^ step) for i in range(size)])

    def more_rounds(value, axis):
        size = n_row if axis == "row" else n_col
        step = 4
        while step < size:
            value = value + wide(trade(narrow(value), axis, step))
            step *= 2
        return value

    def per_device(factor_blocks, inverse_blocks, right_sides):
        steps_total, group_rows, angles = right_sides.shape
        last_step = steps_total - 1
        place = lax.axis_index("row")
        core = lax.axis_index("col") & 1
        side = (place & 1) ^ core
        width = angles // UNITS
        exact = n_row == UNITS
        order = Order()

        def sides_of(step):
            def work(cut):
                cut = cut.T.reshape(STREAMS, 2, width, group_rows)
                return jnp.where(side == 0, cut, cut[:, ::-1])

            return order.run(work, right_sides[step])

        base = [None] * steps_total
        solved = [[None] * STREAMS for _ in range(steps_total)]
        state = [dict() for _ in range(STREAMS)]

        def factor(step, before):
            return factor_blocks[pair_index(step, before)]

        def older(s, step):
            if step >= steps_total or step < 2:
                return
            state[s]["next"] = order.run(
                lambda *known: sum(times_transposed(x, factor(step, j)) for j, x in enumerate(known)),
                *[jnp.concatenate(solved[j][s], axis=0) for j in range(step - 1)],
            )

        def factor_own(s, step):
            st = state[s]
            st["older"] = st.pop("next", None)

            def work(x, *rest):
                value = times_transposed(x, factor(step, step - 1))
                return value + rest[0] if rest else value

            rest = [] if st["older"] is None else [st["older"][:width]]
            st["sum"] = order.run(work, solved[step - 1][s][0], *rest)

        def factor_other(s, step):
            st = state[s]

            def work(x, *rest):
                value = times_transposed(x, factor(step, step - 1))
                return narrow(value + rest[0] if rest else value)

            rest = [] if st["older"] is None else [st["older"][width:]]
            st["flight"] = trade(order.run(work, solved[step - 1][s][1], *rest), "col", 1)

        def chip_sum(s):
            st = state[s]

            def work(value, arrived):
                value = value + wide(arrived)
                return narrow(value), value

            leaving, st["sum"] = order.run(work, st["sum"], st["flight"])
            st["flight"] = trade(leaving, "col", 2) if n_col > 2 else None

        def residual(s, step):
            st = state[s]

            def work(side_values, value, *arrived):
                for a in arrived:
                    value = more_rounds(value + wide(a), "col")
                return narrow(wide(side_values) - value)

            arrived = [] if st["flight"] is None else [st["flight"]]
            st["own"] = order.run(work, base[step][s, 0], st["sum"], *arrived)
            st["flight"] = trade(st["own"], "col", 1)

        def inverse_own(s, step):
            st = state[s]
            st["total"] = order.run(lambda x: times_transposed(x, inverse_blocks[step]), st["own"])

        def inverse_other(s, step):
            st = state[s]
            leaving = order.run(lambda x: narrow(times_transposed(x, inverse_blocks[step])), st["flight"])
            st["flight"] = trade(leaving, "row", 1)

        def pair_sum(s):
            st = state[s]

            def work(value, arrived):
                value = value + wide(arrived)
                return narrow(value), value

            st["leaving"], st["total"] = order.run(work, st["total"], st["flight"])

        def cross(s):
            st = state[s]
            st["flight"] = trade(st["leaving"], "row", 2) if n_row > 2 else None

        def solve(s, step):
            st = state[s]

            def work(value, *arrived):
                for a in arrived:
                    value = more_rounds(value + wide(a), "row")
                return narrow(value)

            arrived = [] if st["flight"] is None else [st["flight"]]
            own = order.run(work, st["total"], *arrived)
            solved[step][s] = (own, trade(own, "row", 1))

        def final_inverse(s):
            st = state[s]

            def leave(own, other):
                return narrow(times_transposed(jnp.where(core == 0, other, own), inverse_blocks[last_step]))

            def keep(own, other):
                return times_transposed(jnp.where(core == 0, own, other), inverse_blocks[last_step])

            leaving = order.run(leave, st["own"], st["flight"])
            st["total"] = order.run(keep, st["own"], st["flight"])
            st["flight"] = trade(leaving, "row", 1)

        base[0] = sides_of(0)
        leaving = order.run(
            lambda x: narrow(times_transposed(x, inverse_blocks[0])),
            base[0][:, 1].reshape(STREAMS * width, group_rows),
        )
        state[0]["flight"] = trade(leaving[:width], "row", 1)
        totals = order.run(
            lambda x: times_transposed(x, inverse_blocks[0]),
            base[0][:, 0].reshape(STREAMS * width, group_rows),
        )
        state[0]["total"], state[1]["total"] = totals[:width], totals[width:]
        pair_sum(0)
        cross(0)
        state[1]["flight"] = trade(order.run(lambda x: x, leaving[width:]), "row", 1)
        if steps_total > 1:
            base[1] = sides_of(1)
        solve(0, 0)
        if steps_total > 1:
            factor_own(0, 1)

        for step in range(1, steps_total):
            final = exact and step == last_step
            factor_other(0, step)
            pair_sum(1)
            cross(1)
            chip_sum(0)
            older(0, step + 1)
            residual(0, step)
            if not final:
                inverse_own(0, step)
            solve(1, step - 1)
            if final:
                final_inverse(0)
            else:
                inverse_other(0, step)
            factor_own(1, step)
            if step < last_step:
                base[step + 1] = sides_of(step + 1)
            factor_other(1, step)
            pair_sum(0)
            if not final:
                cross(0)
            chip_sum(1)
            older(1, step + 1)
            residual(1, step)
            if not final:
                inverse_own(1, step)
                solve(0, step)
                inverse_other(1, step)
            else:
                final_inverse(1)
            if step < last_step:
                factor_own(0, step + 1)

        pair_sum(1)
        outputs = []
        for step in range(steps_total):
            if exact and step == last_step:
                low = place < n_row // 2
                leaving = order.run(
                    lambda a, b: jnp.where(low, b, a), state[0]["leaving"], state[1]["leaving"]
                )
                arrived = trade(leaving, "row", 2)
                found = narrow(jnp.where(low, state[0]["total"], state[1]["total"]) + wide(arrived))
                outputs.append(found.T)
                continue
            if step == last_step:
                cross(1)
                solve(1, step)
            unit = place * UNITS // n_row
            found = solved[step][0][0]
            for s in range(STREAMS):
                for u in range(2):
                    found = jnp.where(unit == 2 * s + (u ^ side), solved[step][s][u], found)
            if not exact:
                slot = angles // n_row
                found = lax.dynamic_slice_in_dim(found, (place * slot) % width, slot, 0)
            outputs.append(found.T)
        return jnp.stack(outputs, axis=0)

    return per_device


def solution(mesh):
    placed = (P("groups", "row", "col"), P("groups", "col", "row"), P("groups", "row", None))
    return jax.shard_map(
        make_per_device(mesh.shape["row"], mesh.shape["col"]),
        mesh=mesh,
        in_specs=placed,
        out_specs=P("groups", "col", "row"),
        check_vma=False,
    )
```

time: 208 us -> 212 us (1.019)
  waiting for transfers between devices: 88.7 us -> 35.4 us
  matrix products: 63.6 us -> 108 us
  other arithmetic: 2.31 us -> 12.2 us
  local copies, waits for them, and re-layouts: 2.91 us -> 6.74 us
  starting transfers between devices: 49.8 us -> 46.9 us
    ppermute x54 -> x51, waiting for transfers between devices: 88.7 us -> 35.4 us  [trade(): return lax.ppermute(value, axis, [(i, i ^ step) for i in range(size)])]
    dot_general x60 -> x46, matrix products: 63.6 us -> 108 us  [times_transposed(): lax.dot_general(left, right, (((1,), (1,)), ((), ())), preferred_element_...]
    convert_element_type x14 -> x34, other arithmetic: 0.72 us -> 7.81 us  [narrow(): return value.astype(jnp.bfloat16)]
    ppermute x54 -> x51, starting transfers between devices: 49.8 us -> 46.9 us  [trade(): return lax.ppermute(value, axis, [(i, i ^ step) for i in range(size)])]
    unnamed x5, other arithmetic: 0.29 us -> 2.92 us
    squeeze x0 -> x5, local copies, waits for them, and re-layouts: none -> 2.58 us  [the longest x1 1.84 us: sides_of(): return order.run(work, right_sides[step])]
    slice x0 -> x9, local copies, waits for them, and re-layouts: none -> 2.43 us  [the longest x4 1.61 us: factor_own(): rest = [] if st['older'] is None else [st['older'][:width]]]
  transfers between devices with their start and end apart: 54 -> 51, of which waited for: 34 -> 15; matrix products, arithmetic and copies ran while one was open for 30% -> 57% of each run, Pallas kernels for 0% -> 0%
where the time goes in v2:
time: 212 us; the launch traced here: 210 us
  matrix products  108 us (51%)
  starting transfers between devices  46.9 us (22%)
  waiting for transfers between devices  35.4 us (17%)
  other arithmetic  12.2 us (6%)
  local copies, waits for them, and re-layouts  6.74 us (3%)
    dot_general x46, matrix products, times_transposed(): lax.dot_general(left, right, (((1,), (1,)), ((), ())), preferred_element_...  108 us
    ppermute x51, starting transfers between devices, trade(): return lax.ppermute(value, axis, [(i, i ^ step) for i in range(size)])  46.9 us
    ppermute x51, waiting for transfers between devices, trade(): return lax.ppermute(value, axis, [(i, i ^ step) for i in range(size)])  35.4 us
    convert_element_type x34, other arithmetic, narrow(): return value.astype(jnp.bfloat16)  7.81 us
  transfers between devices with their start and end apart: 51, of which 15 were waited for; matrix products, arithmetic and copies ran while one was open for 57% of the time, Pallas kernels for 0%

profile of v2, /device:TPU:0, one launch (start us, length us, event | category | flops | bytes accessed | tf_op | source)
XLA Modules:
  0.0 210.0 jit_solution(18257078935950698526)
XLA Ops:
  0.0 1.8 slice_bitcast_fusion
  2.2 2.4 %fusion.156 = bf16[128,1024]{1,0:T(8,128)(2,1)S(1)} fusion(bf16[128,1024]{1,0:T(8,128)(2,1)S(1)} %bitcast.290, bf16[5,1024,1024]{2,1,0:T(8,128)(2,1)} %param.4), kind=kOutput, calls=%fused_computation.144 | convolution fusion | flops 268566528 | bytes 2621440 | tf_op jit(solution)/shard_map/dot_general | solution.py:15
  5.3 3.0 %collective-permute-start = (bf16[64,1024]{1,0:T(8,128)(2,1)S(1)}, bf16[64,1024]{1,0:T(8,128)(2,1)S(1)}, u32[]{:S(2)}, u32[]{:S(2)}) collective-permute-start(bf16[64,1024]{1,0:T(8,128)(2,1)S(1)} %get-tuple-element.356), channel_id=1, source_target_pairs={{0,4},{4,0},{8,12},{12,8},{1,5},{5,1},{9,13},{13,9},{2,6},{6,2},{1... | collective-permute-start | bytes 393224 | tf_op jit(solution)/shard_map/ppermute | solution.py:41
  8.4 2.4 %fusion.88 = f32[128,1024]{1,0:T(8,128)S(1)} fusion(bf16[128,1024]{1,0:T(8,128)(2,1)S(1)} %bitcast.289, bf16[5,1024,1024]{2,1,0:T(8,128)(2,1)} %param.4), kind=kOutput, calls=%fused_computation.88 | convolution fusion | flops 268435456 | bytes 2883584 | tf_op jit(solution)/shard_map/dot_general | solution.py:15
  11.9 2.8 %collective-permute-start.2 = (bf16[64,1024]{1,0:T(8,128)(2,1)S(1)}, bf16[64,1024]{1,0:T(8,128)(2,1)S(1)}, u32[]{:S(2)}, u32[]{:S(2)}) collective-permute-start(bf16[64,1024]{1,0:T(8,128)(2,1)S(1)} %get-tuple-element.325), channel_id=1, source_target_pairs={{0,8},{4,12},{8,0},{12,4},{1,9},{5,13},{9,1},{13,5},{2,10},{6,14},... | collective-permute-start | bytes 393224 | tf_op jit(solution)/shard_map/ppermute | solution.py:41
  14.7 1.6 collective-permute-start.1
  17.3 3.1 %collective-permute-done.2 = bf16[64,1024]{1,0:T(8,128)(2,1)S(1)} collective-permute-done((bf16[64,1024]{1,0:T(8,128)(2,1)S(1)}, bf16[64,1024]{1,0:T(8,128)(2,1)S(1)}, u32[]{:S(2)}, u32[]{:S(2)}) %collective-permute-start.2) | collective-permute-done | bytes 131104 | tf_op jit(solution)/shard_map/ppermute | solution.py:41
  22.5 2.3 %fusion.86 = f32[64,1024]{1,0:T(8,128)S(1)} fusion(bf16[64,1024]{1,0:T(8,128)(2,1)S(1)} %add_convert_fusion.8, bf16[10,1024,1024]{2,1,0:T(8,128)(2,1)} %param.3), kind=kOutput, calls=%fused_computation.86 | convolution fusion | flops 134217728 | bytes 2490368 | tf_op jit(solution)/shard_map/dot_general | solution.py:15
  24.9 2.2 %collective-permute-done.3 = bf16[64,1024]{1,0:T(8,128)(2,1)S(1)} collective-permute-done((bf16[64,1024]{1,0:T(8,128)(2,1)S(1)}, bf16[64,1024]{1,0:T(8,128)(2,1)S(1)}, u32[]{:S(2)}, u32[]{:S(2)}) %collective-permute-start.3) | collective-permute-done | bytes 131104 | tf_op jit(solution)/shard_map/ppermute | solution.py:41
  27.1 2.3 %fusion.213 = bf16[64,1024]{1,0:T(8,128)(2,1)S(1)} fusion(bf16[64,1024]{1,0:T(8,128)(2,1)S(1)} %collective-permute-done.3, bf16[10,1024,1024]{2,1,0:T(8,128)(2,1)} %param.3), kind=kOutput, calls=%fused_computation.163 | convolution fusion | flops 134283264 | bytes 2359296 | tf_op jit(solution)/shard_map/dot_general | solution.py:15
  30.4 1.9 collective-permute-start.4
  32.4 1.6 collective-permute-start.6
  34.0 2.4 %fusion.78 = f32[128,1024]{1,0:T(8,128)S(1)} fusion(bf16[128,1024]{1,0:T(8,128)(2,1)S(1)} %pad_maximum_fusion, bf16[10,1024,1024]{2,1,0:T(8,128)(2,1)} %param.3), kind=kOutput, calls=%fused_computation.78 | convolution fusion | flops 268435456 | bytes 2883584 | tf_op jit(solution)/shard_map/dot_general | solution.py:15
  36.4 1.7 collective-permute-done.6
  38.2 3.1 %fusion.74 = f32[64,1024]{1,0:T(8,128)} fusion(bf16[64,1024]{1,0:T(8,128)(2,1)S(1)} %subtract_convert_fusion.7, bf16[5,1024,1024]{2,1,0:T(8,128)(2,1)} %param.4), kind=kOutput, calls=%fused_computation.74 | convolution fusion | flops 134217728 | bytes 2490368 | tf_op jit(solution)/shard_map/dot_general | solution.py:15
  41.3 2.0 collective-permute-start.7
  43.4 3.0 %fusion.219 = bf16[64,1024]{1,0:T(8,128)(2,1)} fusion(bf16[64,1024]{1,0:T(8,128)(2,1)S(1)} %collective-permute-done.8, bf16[5,1024,1024]{2,1,0:T(8,128)(2,1)} %param.4), kind=kOutput, calls=%fused_computation.165 | convolution fusion | flops 134283264 | bytes 2359296 | tf_op jit(solution)/shard_map/dot_general | solution.py:15
  46.4 3.1 %fusion.82 = f32[64,1024]{1,0:T(8,128)} fusion(bf16[64,1024]{1,0:T(8,128)(2,1)S(1)} %add_convert_fusion.7, bf16[10,1024,1024]{2,1,0:T(8,128)(2,1)} %param.3), kind=kOutput, calls=%fused_computation.82 | convolution fusion | flops 134217728 | bytes 2490368 | tf_op jit(solution)/shard_map/dot_general | solution.py:15
  49.8 2.3 %fusion.216 = bf16[64,1024]{1,0:T(8,128)(2,1)S(1)} fusion(bf16[64,1024]{1,0:T(8,128)(2,1)S(1)} %collective-permute-done.7, bf16[10,1024,1024]{2,1,0:T(8,128)(2,1)} %param.3), kind=kOutput, calls=%fused_computation.164 | convolution fusion | flops 134283264 | bytes 2359296 | tf_op jit(solution)/shard_map/dot_general | solution.py:15
  57.6 2.4 %fusion.76 = f32[128,1024]{1,0:T(8,128)S(1)} fusion(bf16[128,1024]{1,0:T(8,128)(2,1)S(1)} %pad_maximum_fusion.1, bf16[10,1024,1024]{2,1,0:T(8,128)(2,1)} %param.3), kind=kOutput, calls=%fused_computation.76 | convolution fusion | flops 268435456 | bytes 2883584 | tf_op jit(solution)/shard_map/dot_general | solution.py:15
  60.1 1.8 collective-permute-done.11
  62.9 2.4 %fusion.70 = f32[64,1024]{1,0:T(8,128)S(1)} fusion(bf16[64,1024]{1,0:T(8,128)(2,1)S(1)} %subtract_convert_fusion.6, bf16[5,1024,1024]{2,1,0:T(8,128)(2,1)} %param.4), kind=kOutput, calls=%fused_computation.70 | convolution fusion | flops 134217728 | bytes 2490368 | tf_op jit(solution)/shard_map/dot_general | solution.py:15
  66.5 2.3 %fusion.222 = bf16[64,1024]{1,0:T(8,128)(2,1)S(1)} fusion(bf16[64,1024]{1,0:T(8,128)(2,1)S(1)} %collective-permute-done.12, bf16[5,1024,1024]{2,1,0:T(8,128)(2,1)} %param.4), kind=kOutput, calls=%fused_computation.166 | convolution fusion | flops 134283264 | bytes 2359296 | tf_op jit(solution)/shard_map/dot_general | solution.py:15
  69.8 2.3 %fusion.159 = f32[64,1024]{1,0:T(8,128)S(1)} fusion(f32[64,1024]{1,0:T(8,128)S(1)} %get-tuple-element.188, bf16[64,1024]{1,0:T(8,128)(2,1)S(1)} %add_convert_fusion.6, bf16[10,1024,1024]{2,1,0:T(8,128)(2,1)} %param.3), kind=kOutput, calls=%fused_computation.145 | convolution fusion | flops 134283264 | bytes 2752512 | tf_op jit(solution)/shard_map/dot_general | solution.py:15
  72.2 2.4 %fusion.210 = bf16[64,1024]{1,0:T(8,128)(2,1)S(1)} fusion(f32[64,1024]{1,0:T(8,128)S(1)} %get-tuple-element.190, bf16[64,1024]{1,0:T(8,128)(2,1)S(1)} %collective-permute-done.15, bf16[10,1024,1024]{2,1,0:T(8,128)(2,1)} %param.3), kind=kOutput, calls=%fused_computation.162 | convolution fusion | flops 134348800 | bytes 2621440 | tf_op jit(solution)/shard_map/dot_general | solution.py:15
  74.7 2.6 %collective-permute-start.16 = (bf16[64,1024]{1,0:T(8,128)(2,1)S(1)}, bf16[64,1024]{1,0:T(8,128)(2,1)S(1)}, u32[]{:S(2)}, u32[]{:S(2)}) collective-permute-start(bf16[64,1024]{1,0:T(8,128)(2,1)S(1)} %get-tuple-element.315), channel_id=1, source_target_pairs={{0,8},{4,12},{8,0},{12,4},{1,9},{5,13},{9,1},{13,5},{2,10},{6,14},... | collective-permute-start | bytes 393224 | tf_op jit(solution)/shard_map/ppermute | solution.py:41
  77.3 1.6 collective-permute-start.18
  78.9 2.4 %fusion.54 = f32[128,1024]{1,0:T(8,128)S(1)} fusion(bf16[128,1024]{1,0:T(8,128)(2,1)S(1)} %pad_maximum_fusion.2, bf16[10,1024,1024]{2,1,0:T(8,128)(2,1)} %param.3), kind=kOutput, calls=%fused_computation.54 | convolution fusion | flops 268435456 | bytes 2883584 | tf_op jit(solution)/shard_map/dot_general | solution.py:15
  81.3 2.4 %fusion.138 = f32[128,1024]{1,0:T(8,128)S(1)} fusion(f32[128,1024]{1,0:T(8,128)S(1)} %fusion.54, bf16[128,1024]{1,0:T(8,128)(2,1)S(1)} %pad_maximum_fusion, bf16[10,1024,1024]{2,1,0:T(8,128)(2,1)} %param.3), kind=kOutput, calls=%fused_computation.138 | convolution fusion | flops 268566528 | bytes 3407872 | tf_op jit(solution)/shard_map/dot_general | solution.py:15
  84.7 3.2 %fusion.50 = f32[64,1024]{1,0:T(8,128)} fusion(bf16[64,1024]{1,0:T(8,128)(2,1)S(1)} %subtract_convert_fusion.5, bf16[5,1024,1024]{2,1,0:T(8,128)(2,1)} %param.4), kind=kOutput, calls=%fused_computation.50 | convolution fusion | flops 134217728 | bytes 2490368 | tf_op jit(solution)/shard_map/dot_general | solution.py:15
  89.2 3.0 %fusion.225 = bf16[64,1024]{1,0:T(8,128)(2,1)} fusion(bf16[64,1024]{1,0:T(8,128)(2,1)S(1)} %collective-permute-done.20, bf16[5,1024,1024]{2,1,0:T(8,128)(2,1)} %param.4), kind=kOutput, calls=%fused_computation.167 | convolution fusion | flops 134283264 | bytes 2359296 | tf_op jit(solution)/shard_map/dot_general | solution.py:15
  93.0 2.3 %fusion.165 = f32[64,1024]{1,0:T(8,128)S(1)} fusion(f32[64,1024]{1,0:T(8,128)S(1)} %get-tuple-element.205, bf16[64,1024]{1,0:T(8,128)(2,1)S(1)} %add_convert_fusion.5, bf16[10,1024,1024]{2,1,0:T(8,128)(2,1)} %param.3), kind=kOutput, calls=%fused_computation.147 | convolution fusion | flops 134283264 | bytes 2752512 | tf_op jit(solution)/shard_map/dot_general | solution.py:15
  95.7 2.4 %fusion.207 = bf16[64,1024]{1,0:T(8,128)(2,1)S(1)} fusion(f32[64,1024]{1,0:T(8,128)S(1)} %get-tuple-element.208, bf16[64,1024]{1,0:T(8,128)(2,1)S(1)} %collective-permute-done.19, bf16[10,1024,1024]{2,1,0:T(8,128)(2,1)} %param.3), kind=kOutput, calls=%fused_computation.161 | convolution fusion | flops 134348800 | bytes 2621440 | tf_op jit(solution)/shard_map/dot_general | solution.py:15
  101.1 2.4 %fusion.52 = f32[128,1024]{1,0:T(8,128)S(1)} fusion(bf16[128,1024]{1,0:T(8,128)(2,1)S(1)} %pad_maximum_fusion.3, bf16[10,1024,1024]{2,1,0:T(8,128)(2,1)} %param.3), kind=kOutput, calls=%fused_computation.52 | convolution fusion | flops 268435456 | bytes 2883584 | tf_op jit(solution)/shard_map/dot_general | solution.py:15
  103.5 2.4 %fusion.141 = f32[128,1024]{1,0:T(8,128)S(1)} fusion(f32[128,1024]{1,0:T(8,128)S(1)} %fusion.52, bf16[128,1024]{1,0:T(8,128)(2,1)S(1)} %pad_maximum_fusion.1, bf16[10,1024,1024]{2,1,0:T(8,128)(2,1)} %param.3), kind=kOutput, calls=%fused_computation.139 | convolution fusion | flops 268566528 | bytes 3407872 | tf_op jit(solution)/shard_map/dot_general | solution.py:15
  106.2 2.4 %fusion.46 = f32[64,1024]{1,0:T(8,128)S(1)} fusion(bf16[64,1024]{1,0:T(8,128)(2,1)S(1)} %subtract_convert_fusion.4, bf16[5,1024,1024]{2,1,0:T(8,128)(2,1)} %param.4), kind=kOutput, calls=%fused_computation.46 | convolution fusion | flops 134217728 | bytes 2490368 | tf_op jit(solution)/shard_map/dot_general | solution.py:15
  110.2 2.3 %fusion.228 = bf16[64,1024]{1,0:T(8,128)(2,1)S(1)} fusion(bf16[64,1024]{1,0:T(8,128)(2,1)S(1)} %collective-permute-done.24, bf16[5,1024,1024]{2,1,0:T(8,128)(2,1)} %param.4), kind=kOutput, calls=%fused_computation.168 | convolution fusion | flops 134283264 | bytes 2359296 | tf_op jit(solution)/shard_map/dot_general | solution.py:15
  113.6 2.4 %fusion.171 = f32[64,1024]{1,0:T(8,128)S(1)} fusion(f32[64,1024]{1,0:T(8,128)S(1)} %copy-done.1, bf16[64,1024]{1,0:T(8,128)(2,1)S(1)} %add_convert_fusion.4, bf16[10,1024,1024]{2,1,0:T(8,128)(2,1)} %param.3), kind=kOutput, calls=%fused_computation.149 | convolution fusion | flops 134283264 | bytes 2752512 | tf_op jit(solution)/shard_map/dot_general | solution.py:15
  115.9 2.4 %fusion.204 = bf16[64,1024]{1,0:T(8,128)(2,1)S(1)} fusion(f32[64,1024]{1,0:T(8,128)S(1)} %get-tuple-element.225, bf16[64,1024]{1,0:T(8,128)(2,1)S(1)} %collective-permute-done.27, bf16[10,1024,1024]{2,1,0:T(8,128)(2,1)} %param.3), kind=kOutput, calls=%fused_computation.160 | convolution fusion | flops 134348800 | bytes 2621440 | tf_op jit(solution)/shard_map/dot_general | solution.py:15
  118.4 1.6 collective-permute-start.28
  121.5 2.4 %fusion.30 = f32[128,1024]{1,0:T(8,128)S(1)} fusion(bf16[128,1024]{1,0:T(8,128)(2,1)S(1)} %copy-done.4, bf16[10,1024,1024]{2,1,0:T(8,128)(2,1)} %param.3), kind=kOutput, calls=%fused_computation.30 | convolution fusion | flops 268435456 | bytes 2883584 | tf_op jit(solution)/shard_map/dot_general | solution.py:15
  123.9 2.4 %fusion.26 = f32[128,1024]{1,0:T(8,128)S(1)} fusion(bf16[128,1024]{1,0:T(8,128)(2,1)S(1)} %pad_maximum_fusion.4, bf16[10,1024,1024]{2,1,0:T(8,128)(2,1)} %param.3), kind=kOutput, calls=%fused_computation.26 | convolution fusion | flops 268435456 | bytes 2883584 | tf_op jit(solution)/shard_map/dot_general | solution.py:15
  126.4 2.4 %fusion.147 = f32[128,1024]{1,0:T(8,128)S(1)} fusion(f32[128,1024]{1,0:T(8,128)S(1)} %fusion.26, f32[128,1024]{1,0:T(8,128)S(1)} %fusion.30, bf16[128,1024]{1,0:T(8,128)(2,1)S(1)} %pad_maximum_fusion, bf16[10,1024,1024]{2,1,0:T(8,128)(2,1)} %param.3), kind=kOutput, calls=%fused_computation.141 | convolution fusion | flops 268697600 | bytes 3932160 | tf_op jit(solution)/shard_map/dot_general | solution.py:15
  129.7 2.4 %fusion.22 = f32[64,1024]{1,0:T(8,128)S(1)} fusion(bf16[64,1024]{1,0:T(8,128)(2,1)S(1)} %subtract_convert_fusion.3, bf16[5,1024,1024]{2,1,0:T(8,128)(2,1)} %param.4), kind=kOutput, calls=%fused_computation.22 | convolution fusion | flops 134217728 | bytes 2490368 | tf_op jit(solution)/shard_map/dot_general | solution.py:15
  133.4 3.0 %fusion.231 = bf16[64,1024]{1,0:T(8,128)(2,1)} fusion(bf16[64,1024]{1,0:T(8,128)(2,1)S(1)} %collective-permute-done.32, bf16[5,1024,1024]{2,1,0:T(8,128)(2,1)} %param.4), kind=kOutput, calls=%fused_computation.169 | convolution fusion | flops 134283264 | bytes 2359296 | tf_op jit(solution)/shard_map/dot_general | solution.py:15
  137.2 2.4 %fusion.177 = f32[64,1024]{1,0:T(8,128)S(1)} fusion(f32[64,1024]{1,0:T(8,128)S(1)} %get-tuple-element.241, bf16[64,1024]{1,0:T(8,128)(2,1)S(1)} %add_convert_fusion.3, bf16[10,1024,1024]{2,1,0:T(8,128)(2,1)} %param.3), kind=kOutput, calls=%fused_computation.151 | convolution fusion | flops 134283264 | bytes 2752512 | tf_op jit(solution)/shard_map/dot_general | solution.py:15
  139.9 2.4 %fusion.201 = bf16[64,1024]{1,0:T(8,128)(2,1)S(1)} fusion(f32[64,1024]{1,0:T(8,128)S(1)} %get-tuple-element.244, bf16[64,1024]{1,0:T(8,128)(2,1)S(1)} %collective-permute-done.31, bf16[10,1024,1024]{2,1,0:T(8,128)(2,1)} %param.3), kind=kOutput, calls=%fused_computation.159 | convolution fusion | flops 134348800 | bytes 2621440 | tf_op jit(solution)/shard_map/dot_general | solution.py:15
  145.6 2.5 %fusion.28 = f32[128,1024]{1,0:T(8,128)S(1)} fusion(bf16[128,1024]{1,0:T(8,128)(2,1)} %copy-done.2, bf16[10,1024,1024]{2,1,0:T(8,128)(2,1)} %param.3), kind=kOutput, calls=%fused_computation.28 | convolution fusion | flops 268435456 | bytes 2883584 | tf_op jit(solution)/shard_map/dot_general | solution.py:15
  148.2 2.6 %fusion.24 = f32[128,1024]{1,0:T(8,128)S(1)} fusion(bf16[128,1024]{1,0:T(8,128)(2,1)S(1)} %pad_maximum_fusion.5, bf16[10,1024,1024]{2,1,0:T(8,128)(2,1)} %param.3), kind=kOutput, calls=%fused_computation.24 | convolution fusion | flops 268435456 | bytes 2883584 | tf_op jit(solution)/shard_map/dot_general | solution.py:15
  150.7 2.6 %fusion.153 = f32[128,1024]{1,0:T(8,128)S(1)} fusion(f32[128,1024]{1,0:T(8,128)S(1)} %fusion.24, f32[128,1024]{1,0:T(8,128)S(1)} %fusion.28, bf16[128,1024]{1,0:T(8,128)(2,1)S(1)} %pad_maximum_fusion.1, bf16[10,1024,1024]{2,1,0:T(8,128)(2,1)} %param.3), kind=kOutput, calls=%fused_computation.143 | convolution fusion | flops 268697600 | bytes 3932160 | tf_op jit(solution)/shard_map/dot_general | solution.py:15
  153.5 2.5 %fusion.18 = f32[64,1024]{1,0:T(8,128)S(1)} fusion(bf16[64,1024]{1,0:T(8,128)(2,1)S(1)} %subtract_convert_fusion.2, bf16[5,1024,1024]{2,1,0:T(8,128)(2,1)} %param.4), kind=kOutput, calls=%fused_computation.18 | convolution fusion | flops 134217728 | bytes 2490368 | tf_op jit(solution)/shard_map/dot_general | solution.py:15
  157.2 2.3 %fusion.234 = bf16[64,1024]{1,0:T(8,128)(2,1)S(1)} fusion(bf16[64,1024]{1,0:T(8,128)(2,1)S(1)} %collective-permute-done.36, bf16[5,1024,1024]{2,1,0:T(8,128)(2,1)} %param.4), kind=kOutput, calls=%fused_computation.170 | convolution fusion | flops 134283264 | bytes 2359296 | tf_op jit(solution)/shard_map/dot_general | solution.py:15
  160.6 2.5 %fusion.183 = f32[64,1024]{1,0:T(8,128)S(1)} fusion(f32[64,1024]{1,0:T(8,128)S(1)} %copy-done, bf16[64,1024]{1,0:T(8,128)(2,1)S(1)} %add_convert_fusion.2, bf16[10,1024,1024]{2,1,0:T(8,128)(2,1)} %param.3), kind=kOutput, calls=%fused_computation.153 | convolution fusion | flops 134283264 | bytes 2752512 | tf_op jit(solution)/shard_map/dot_general | solution.py:15
  163.1 2.4 %fusion.198 = bf16[64,1024]{1,0:T(8,128)(2,1)S(1)} fusion(f32[64,1024]{1,0:T(8,128)S(1)} %get-tuple-element.262, bf16[64,1024]{1,0:T(8,128)(2,1)S(1)} %collective-permute-done.39, bf16[10,1024,1024]{2,1,0:T(8,128)(2,1)} %param.3), kind=kOutput, calls=%fused_computation.158 | convolution fusion | flops 134348800 | bytes 2621440 | tf_op jit(solution)/shard_map/dot_general | solution.py:15
  168.1 1.8 collective-permute-start.40
  170.0 2.6 %collective-permute-done.42 = bf16[64,1024]{1,0:T(8,128)(2,1)S(1)} collective-permute-done((bf16[64,1024]{1,0:T(8,128)(2,1)S(1)}, bf16[64,1024]{1,0:T(8,128)(2,1)S(1)}, u32[]{:S(2)}, u32[]{:S(2)}) %collective-permute-start.42) | collective-permute-done | bytes 131104 | tf_op jit(solution)/shard_map/ppermute | solution.py:41
  172.7 4.5 %collective-permute-done.40 = bf16[64,1024]{1,0:T(8,128)(2,1)S(1)} collective-permute-done((bf16[64,1024]{1,0:T(8,128)(2,1)S(1)}, bf16[64,1024]{1,0:T(8,128)(2,1)S(1)}, u32[]{:S(2)}, u32[]{:S(2)}) %collective-permute-start.40) | collective-permute-done | bytes 131104 | tf_op jit(solution)/shard_map/ppermute | solution.py:41
  178.1 2.1 collective-permute-start.45
  180.9 2.4 %fusion.189 = f32[64,1024]{1,0:T(8,128)S(1)} fusion(f32[64,1024]{1,0:T(8,128)S(1)} %get-tuple-element.277, bf16[64,1024]{1,0:T(8,128)(2,1)S(1)} %add_convert_fusion.1, bf16[10,1024,1024]{2,1,0:T(8,128)(2,1)} %param.3), kind=kOutput, calls=%fused_computation.155 | convolution fusion | flops 134283264 | bytes 2752512 | tf_op jit(solution)/shard_map/dot_general | solution.py:15
  183.4 2.4 %fusion.195 = bf16[64,1024]{1,0:T(8,128)(2,1)S(1)} fusion(f32[64,1024]{1,0:T(8,128)S(1)} %get-tuple-element.279, bf16[64,1024]{1,0:T(8,128)(2,1)S(1)} %collective-permute-done.43, bf16[10,1024,1024]{2,1,0:T(8,128)(2,1)} %param.3), kind=kOutput, calls=%fused_computation.157 | convolution fusion | flops 134348800 | bytes 2621440 | tf_op jit(solution)/shard_map/dot_general | solution.py:15
  189.1 3.8 %collective-permute-done.47 = bf16[64,1024]{1,0:T(8,128)(2,1)S(1)} collective-permute-done((bf16[64,1024]{1,0:T(8,128)(2,1)S(1)}, bf16[64,1024]{1,0:T(8,128)(2,1)S(1)}, u32[]{:S(2)}, u32[]{:S(2)}) %collective-permute-start.47) | collective-permute-done | bytes 131104 | tf_op jit(solution)/shard_map/ppermute | solution.py:41
  195.9 4.8 %collective-permute-done.49 = bf16[64,1024]{1,0:T(8,128)(2,1)S(1)} collective-permute-done((bf16[64,1024]{1,0:T(8,128)(2,1)S(1)}, bf16[64,1024]{1,0:T(8,128)(2,1)S(1)}, u32[]{:S(2)}, u32[]{:S(2)}) %collective-permute-start.49) | collective-permute-done | bytes 131104 | tf_op jit(solution)/shard_map/ppermute | solution.py:41
  200.7 1.6 collective-permute-start.50
  203.0 6.2 %collective-permute-done.50 = bf16[64,1024]{1,0:T(8,128)(2,1)S(1)} collective-permute-done((bf16[64,1024]{1,0:T(8,128)(2,1)S(1)}, bf16[64,1024]{1,0:T(8,128)(2,1)S(1)}, u32[]{:S(2)}, u32[]{:S(2)}) %collective-permute-start.50) | collective-permute-done | bytes 131104 | tf_op jit(solution)/shard_map/ppermute | solution.py:41
  (173 shorter events, 47.7 us)
Async XLA Ops:
  5.3 6.5 %collective-permute-start = (bf16[64,1024]{1,0:T(8,128)(2,1)S(1)}, bf16[64,1024]{1,0:T(8,128)(2,1)S(1)}, u32[]{:S(2)}, u32[]{:S(2)}) collective-permute-start(bf16[64,1024]{1,0:T(8,128)(2,1)S(1)} %get-tuple-element.356), channel_id=1, source_target_pairs={{0,4},{4,0},{8,12},{12,8},{1,5},{5,1},{9,13},{13,9},{2,6},{6,2},{1... | collective-permute-start | bytes 393224 | tf_op jit(solution)/shard_map/ppermute | solution.py:41
  11.9 8.6 %collective-permute-start.2 = (bf16[64,1024]{1,0:T(8,128)(2,1)S(1)}, bf16[64,1024]{1,0:T(8,128)(2,1)S(1)}, u32[]{:S(2)}, u32[]{:S(2)}) collective-permute-start(bf16[64,1024]{1,0:T(8,128)(2,1)S(1)} %get-tuple-element.325), channel_id=1, source_target_pairs={{0,8},{4,12},{8,0},{12,4},{1,9},{5,13},{9,1},{13,5},{2,10},{6,14},... | collective-permute-start | bytes 393224 | tf_op jit(solution)/shard_map/ppermute | solution.py:41
  14.7 14.8 %collective-permute-start.1 = (bf16[64,1024]{1,0:T(8,128)(2,1)}, bf16[64,1024]{1,0:T(8,128)(2,1)}, u32[]{:S(2)}, u32[]{:S(2)}) collective-permute-start(bf16[64,1024]{1,0:T(8,128)(2,1)} %get-tuple-element.154), channel_id=1, source_target_pairs={{0,4},{4,0},{8,12},{12,8},{1,5},{5,1},{9,13},{13,9},{2,6},{6,2},{1... | collective-permute-start | bytes 393224 | tf_op jit(solution)/shard_map/ppermute | solution.py:41
  20.4 0.7 copy-start.5
  22.0 5.0 %collective-permute-start.3 = (bf16[64,1024]{1,0:T(8,128)(2,1)S(1)}, bf16[64,1024]{1,0:T(8,128)(2,1)S(1)}, u32[]{:S(2)}, u32[]{:S(2)}) collective-permute-start(bf16[64,1024]{1,0:T(8,128)(2,1)S(1)} %add_convert_fusion.8), channel_id=1, source_target_pairs={{0,4},{4,0},{8,12},{12,8},{1,5},{5,1},{9,13},{13,9},{2,6},{6,2},{1... | collective-permute-start | bytes 393224 | tf_op jit(solution)/shard_map/ppermute | solution.py:41
  29.4 3.0 %collective-permute-start.5 = (bf16[64,1024]{1,0:T(8,128)(2,1)S(1)}, bf16[64,1024]{1,0:T(8,128)(2,1)S(1)}, u32[]{:S(2)}, u32[]{:S(2)}) collective-permute-start(bf16[64,1024]{1,0:T(8,128)(2,1)S(1)} %fusion.213), channel_id=1, source_target_pairs={{0,1},{1,0},{2,3},{3,2},{4,5},{5,4},{6,7},{7,6},{8,9},{9,8},{10,11... | collective-permute-start | bytes 393224 | tf_op jit(solution)/shard_map/ppermute | solution.py:41
  30.4 10.8 %collective-permute-start.4 = (bf16[64,1024]{1,0:T(8,128)(2,1)S(1)}, bf16[64,1024]{1,0:T(8,128)(2,1)S(1)}, u32[]{:S(2)}, u32[]{:S(2)}) collective-permute-start(bf16[64,1024]{1,0:T(8,128)(2,1)S(1)} %get-tuple-element.323), channel_id=1, source_target_pairs={{0,8},{4,12},{8,0},{12,4},{1,9},{5,13},{9,1},{13,5},{2,10},{6,14},... | collective-permute-start | bytes 393224 | tf_op jit(solution)/shard_map/ppermute | solution.py:41
  32.4 5.7 %collective-permute-start.6 = (bf16[64,1024]{1,0:T(8,128)(2,1)S(1)}, bf16[64,1024]{1,0:T(8,128)(2,1)S(1)}, u32[]{:S(2)}, u32[]{:S(2)}) collective-permute-start(bf16[64,1024]{1,0:T(8,128)(2,1)S(1)} %get-tuple-element.321), channel_id=1, source_target_pairs={{0,2},{1,3},{2,0},{3,1},{4,6},{5,7},{6,4},{7,5},{8,10},{9,11},{10,... | collective-permute-start | bytes 393224 | tf_op jit(solution)/shard_map/ppermute | solution.py:41
  38.1 5.2 %collective-permute-start.8 = (bf16[64,1024]{1,0:T(8,128)(2,1)S(1)}, bf16[64,1024]{1,0:T(8,128)(2,1)S(1)}, u32[]{:S(2)}, u32[]{:S(2)}) collective-permute-start(bf16[64,1024]{1,0:T(8,128)(2,1)S(1)} %subtract_convert_fusion.7), channel_id=1, source_target_pairs={{0,1},{1,0},{2,3},{3,2},{4,5},{5,4},{6,7},{7,6},{8,9},{9,8},{10,11... | collective-permute-start | bytes 393224 | tf_op jit(solution)/shard_map/ppermute | solution.py:41
  41.3 8.5 %collective-permute-start.7 = (bf16[64,1024]{1,0:T(8,128)(2,1)S(1)}, bf16[64,1024]{1,0:T(8,128)(2,1)S(1)}, u32[]{:S(2)}, u32[]{:S(2)}) collective-permute-start(bf16[64,1024]{1,0:T(8,128)(2,1)S(1)} %add_convert_fusion.7), channel_id=1, source_target_pairs={{0,4},{4,0},{8,12},{12,8},{1,5},{5,1},{9,13},{13,9},{2,6},{6,2},{1... | collective-permute-start | bytes 393224 | tf_op jit(solution)/shard_map/ppermute | solution.py:41
  46.4 6.8 %collective-permute-start.10 = (bf16[64,1024]{1,0:T(8,128)(2,1)}, bf16[64,1024]{1,0:T(8,128)(2,1)S(1)}, u32[]{:S(2)}, u32[]{:S(2)}) collective-permute-start(bf16[64,1024]{1,0:T(8,128)(2,1)} %fusion.219), channel_id=1, source_target_pairs={{0,4},{4,0},{8,12},{12,8},{1,5},{5,1},{9,13},{13,9},{2,6},{6,2},{1... | collective-permute-start | bytes 393224 | tf_op jit(solution)/shard_map/ppermute | solution.py:41
  52.9 2.3 %collective-permute-start.9 = (bf16[64,1024]{1,0:T(8,128)(2,1)S(1)}, bf16[64,1024]{1,0:T(8,128)(2,1)S(1)}, u32[]{:S(2)}, u32[]{:S(2)}) collective-permute-start(bf16[64,1024]{1,0:T(8,128)(2,1)S(1)} %fusion.216), channel_id=1, source_target_pairs={{0,1},{1,0},{2,3},{3,2},{4,5},{5,4},{6,7},{7,6},{8,9},{9,8},{10,11... | collective-permute-start | bytes 393224 | tf_op jit(solution)/shard_map/ppermute | solution.py:41
  54.2 11.1 %collective-permute-start.13 = (bf16[64,1024]{1,0:T(8,128)(2,1)S(1)}, bf16[64,1024]{1,0:T(8,128)(2,1)S(1)}, u32[]{:S(2)}, u32[]{:S(2)}) collective-permute-start(bf16[64,1024]{1,0:T(8,128)(2,1)S(1)} %get-tuple-element.319), channel_id=1, source_target_pairs={{0,8},{4,12},{8,0},{12,4},{1,9},{5,13},{9,1},{13,5},{2,10},{6,14},... | collective-permute-start | bytes 393224 | tf_op jit(solution)/shard_map/ppermute | solution.py:41
  56.2 5.7 %collective-permute-start.11 = (bf16[64,1024]{1,0:T(8,128)(2,1)S(1)}, bf16[64,1024]{1,0:T(8,128)(2,1)S(1)}, u32[]{:S(2)}, u32[]{:S(2)}) collective-permute-start(bf16[64,1024]{1,0:T(8,128)(2,1)S(1)} %get-tuple-element.317), channel_id=1, source_target_pairs={{0,2},{1,3},{2,0},{3,1},{4,6},{5,7},{6,4},{7,5},{8,10},{9,11},{10,... | collective-permute-start | bytes 393224 | tf_op jit(solution)/shard_map/ppermute | solution.py:41
  62.8 3.7 %collective-permute-start.12 = (bf16[64,1024]{1,0:T(8,128)(2,1)S(1)}, bf16[64,1024]{1,0:T(8,128)(2,1)S(1)}, u32[]{:S(2)}, u32[]{:S(2)}) collective-permute-start(bf16[64,1024]{1,0:T(8,128)(2,1)S(1)} %subtract_convert_fusion.6), channel_id=1, source_target_pairs={{0,1},{1,0},{2,3},{3,2},{4,5},{5,4},{6,7},{7,6},{8,9},{9,8},{10,11... | collective-permute-start | bytes 393224 | tf_op jit(solution)/shard_map/ppermute | solution.py:41
  65.3 6.9 %collective-permute-start.15 = (bf16[64,1024]{1,0:T(8,128)(2,1)S(1)}, bf16[64,1024]{1,0:T(8,128)(2,1)S(1)}, u32[]{:S(2)}, u32[]{:S(2)}) collective-permute-start(bf16[64,1024]{1,0:T(8,128)(2,1)S(1)} %add_convert_fusion.6), channel_id=1, source_target_pairs={{0,4},{4,0},{8,12},{12,8},{1,5},{5,1},{9,13},{13,9},{2,6},{6,2},{1... | collective-permute-start | bytes 393224 | tf_op jit(solution)/shard_map/ppermute | solution.py:41
  68.9 5.7 %collective-permute-start.14 = (bf16[64,1024]{1,0:T(8,128)(2,1)S(1)}, bf16[64,1024]{1,0:T(8,128)(2,1)S(1)}, u32[]{:S(2)}, u32[]{:S(2)}) collective-permute-start(bf16[64,1024]{1,0:T(8,128)(2,1)S(1)} %fusion.222), channel_id=1, source_target_pairs={{0,4},{4,0},{8,12},{12,8},{1,5},{5,1},{9,13},{13,9},{2,6},{6,2},{1... | collective-permute-start | bytes 393224 | tf_op jit(solution)/shard_map/ppermute | solution.py:41
  74.5 2.8 %collective-permute-start.17 = (bf16[64,1024]{1,0:T(8,128)(2,1)S(1)}, bf16[64,1024]{1,0:T(8,128)(2,1)S(1)}, u32[]{:S(2)}, u32[]{:S(2)}) collective-permute-start(bf16[64,1024]{1,0:T(8,128)(2,1)S(1)} %fusion.210), channel_id=1, source_target_pairs={{0,1},{1,0},{2,3},{3,2},{4,5},{5,4},{6,7},{7,6},{8,9},{9,8},{10,11... | collective-permute-start | bytes 393224 | tf_op jit(solution)/shard_map/ppermute | solution.py:41
  74.6 6.7 %copy-start.3 = (bf16[128,1024]{1,0:T(8,128)(2,1)}, bf16[128,1024]{1,0:T(8,128)(2,1)S(1)}, u32[]{:S(2)}) copy-start(bf16[128,1024]{1,0:T(8,128)(2,1)S(1)} %pad_maximum_fusion.2) | copy-start | bytes 786436
  74.7 13.2 %collective-permute-start.16 = (bf16[64,1024]{1,0:T(8,128)(2,1)S(1)}, bf16[64,1024]{1,0:T(8,128)(2,1)S(1)}, u32[]{:S(2)}, u32[]{:S(2)}) collective-permute-start(bf16[64,1024]{1,0:T(8,128)(2,1)S(1)} %get-tuple-element.315), channel_id=1, source_target_pairs={{0,8},{4,12},{8,0},{12,4},{1,9},{5,13},{9,1},{13,5},{2,10},{6,14},... | collective-permute-start | bytes 393224 | tf_op jit(solution)/shard_map/ppermute | solution.py:41
  77.3 7.2 %collective-permute-start.18 = (bf16[64,1024]{1,0:T(8,128)(2,1)S(1)}, bf16[64,1024]{1,0:T(8,128)(2,1)S(1)}, u32[]{:S(2)}, u32[]{:S(2)}) collective-permute-start(bf16[64,1024]{1,0:T(8,128)(2,1)S(1)} %get-tuple-element.313), channel_id=1, source_target_pairs={{0,2},{1,3},{2,0},{3,1},{4,6},{5,7},{6,4},{7,5},{8,10},{9,11},{10,... | collective-permute-start | bytes 393224 | tf_op jit(solution)/shard_map/ppermute | solution.py:41
  84.6 4.7 %collective-permute-start.20 = (bf16[64,1024]{1,0:T(8,128)(2,1)S(1)}, bf16[64,1024]{1,0:T(8,128)(2,1)S(1)}, u32[]{:S(2)}, u32[]{:S(2)}) collective-permute-start(bf16[64,1024]{1,0:T(8,128)(2,1)S(1)} %subtract_convert_fusion.5), channel_id=1, source_target_pairs={{0,1},{1,0},{2,3},{3,2},{4,5},{5,4},{6,7},{7,6},{8,9},{9,8},{10,11... | collective-permute-start | bytes 393224 | tf_op jit(solution)/shard_map/ppermute | solution.py:41
  87.9 7.8 %collective-permute-start.19 = (bf16[64,1024]{1,0:T(8,128)(2,1)S(1)}, bf16[64,1024]{1,0:T(8,128)(2,1)S(1)}, u32[]{:S(2)}, u32[]{:S(2)}) collective-permute-start(bf16[64,1024]{1,0:T(8,128)(2,1)S(1)} %add_convert_fusion.5), channel_id=1, source_target_pairs={{0,4},{4,0},{8,12},{12,8},{1,5},{5,1},{9,13},{13,9},{2,6},{6,2},{1... | collective-permute-start | bytes 393224 | tf_op jit(solution)/shard_map/ppermute | solution.py:41
  92.3 6.0 %collective-permute-start.22 = (bf16[64,1024]{1,0:T(8,128)(2,1)}, bf16[64,1024]{1,0:T(8,128)(2,1)}, u32[]{:S(2)}, u32[]{:S(2)}) collective-permute-start(bf16[64,1024]{1,0:T(8,128)(2,1)} %fusion.225), channel_id=1, source_target_pairs={{0,4},{4,0},{8,12},{12,8},{1,5},{5,1},{9,13},{13,9},{2,6},{6,2},{1... | collective-permute-start | bytes 393224 | tf_op jit(solution)/shard_map/ppermute | solution.py:41
  95.6 18.0 %copy-start.1 = (f32[64,1024]{1,0:T(8,128)S(1)}, f32[64,1024]{1,0:T(8,128)}, u32[]{:S(2)}) copy-start(f32[64,1024]{1,0:T(8,128)} %get-tuple-element.223) | copy-start | bytes 786436
  98.1 2.3 %collective-permute-start.21 = (bf16[64,1024]{1,0:T(8,128)(2,1)S(1)}, bf16[64,1024]{1,0:T(8,128)(2,1)S(1)}, u32[]{:S(2)}, u32[]{:S(2)}) collective-permute-start(bf16[64,1024]{1,0:T(8,128)(2,1)S(1)} %fusion.207), channel_id=1, source_target_pairs={{0,1},{1,0},{2,3},{3,2},{4,5},{5,4},{6,7},{7,6},{8,9},{9,8},{10,11... | collective-permute-start | bytes 393224 | tf_op jit(solution)/shard_map/ppermute | solution.py:41
  98.2 5.3 %copy-start.2 = (bf16[128,1024]{1,0:T(8,128)(2,1)}, bf16[128,1024]{1,0:T(8,128)(2,1)S(1)}, u32[]{:S(2)}) copy-start(bf16[128,1024]{1,0:T(8,128)(2,1)S(1)} %pad_maximum_fusion.3) | copy-start | bytes 786436
  99.4 9.7 %collective-permute-start.25 = (bf16[64,1024]{1,0:T(8,128)(2,1)S(1)}, bf16[64,1024]{1,0:T(8,128)(2,1)S(1)}, u32[]{:S(2)}, u32[]{:S(2)}) collective-permute-start(bf16[64,1024]{1,0:T(8,128)(2,1)S(1)} %get-tuple-element.311), channel_id=1, source_target_pairs={{0,8},{4,12},{8,0},{12,4},{1,9},{5,13},{9,1},{13,5},{2,10},{6,14},... | collective-permute-start | bytes 393224 | tf_op jit(solution)/shard_map/ppermute | solution.py:41
  100.5 21.0 %copy-start.4 = (bf16[128,1024]{1,0:T(8,128)(2,1)S(1)}, bf16[128,1024]{1,0:T(8,128)(2,1)}, u32[]{:S(2)}) copy-start(bf16[128,1024]{1,0:T(8,128)(2,1)} %copy-done.3) | copy-start | bytes 786436
  100.5 5.5 %collective-permute-start.23 = (bf16[64,1024]{1,0:T(8,128)(2,1)S(1)}, bf16[64,1024]{1,0:T(8,128)(2,1)S(1)}, u32[]{:S(2)}, u32[]{:S(2)}) collective-permute-start(bf16[64,1024]{1,0:T(8,128)(2,1)S(1)} %get-tuple-element.309), channel_id=1, source_target_pairs={{0,2},{1,3},{2,0},{3,1},{4,6},{5,7},{6,4},{7,5},{8,10},{9,11},{10,... | collective-permute-start | bytes 393224 | tf_op jit(solution)/shard_map/ppermute | solution.py:41
  106.1 4.1 %collective-permute-start.24 = (bf16[64,1024]{1,0:T(8,128)(2,1)S(1)}, bf16[64,1024]{1,0:T(8,128)(2,1)S(1)}, u32[]{:S(2)}, u32[]{:S(2)}) collective-permute-start(bf16[64,1024]{1,0:T(8,128)(2,1)S(1)} %subtract_convert_fusion.4), channel_id=1, source_target_pairs={{0,1},{1,0},{2,3},{3,2},{4,5},{5,4},{6,7},{7,6},{8,9},{9,8},{10,11... | collective-permute-start | bytes 393224 | tf_op jit(solution)/shard_map/ppermute | solution.py:41
  109.1 6.9 %collective-permute-start.27 = (bf16[64,1024]{1,0:T(8,128)(2,1)S(1)}, bf16[64,1024]{1,0:T(8,128)(2,1)S(1)}, u32[]{:S(2)}, u32[]{:S(2)}) collective-permute-start(bf16[64,1024]{1,0:T(8,128)(2,1)S(1)} %add_convert_fusion.4), channel_id=1, source_target_pairs={{0,4},{4,0},{8,12},{12,8},{1,5},{5,1},{9,13},{13,9},{2,6},{6,2},{1... | collective-permute-start | bytes 393224 | tf_op jit(solution)/shard_map/ppermute | solution.py:41
  112.5 5.9 %collective-permute-start.26 = (bf16[64,1024]{1,0:T(8,128)(2,1)S(1)}, bf16[64,1024]{1,0:T(8,128)(2,1)S(1)}, u32[]{:S(2)}, u32[]{:S(2)}) collective-permute-start(bf16[64,1024]{1,0:T(8,128)(2,1)S(1)} %fusion.228), channel_id=1, source_target_pairs={{0,4},{4,0},{8,12},{12,8},{1,5},{5,1},{9,13},{13,9},{2,6},{6,2},{1... | collective-permute-start | bytes 393224 | tf_op jit(solution)/shard_map/ppermute | solution.py:41
  118.3 1.8 collective-permute-start.29
  118.4 13.6 %collective-permute-start.28 = (bf16[64,1024]{1,0:T(8,128)(2,1)S(1)}, bf16[64,1024]{1,0:T(8,128)(2,1)S(1)}, u32[]{:S(2)}, u32[]{:S(2)}) collective-permute-start(bf16[64,1024]{1,0:T(8,128)(2,1)S(1)} %get-tuple-element.307), channel_id=1, source_target_pairs={{0,8},{4,12},{8,0},{12,4},{1,9},{5,13},{9,1},{13,5},{2,10},{6,14},... | collective-permute-start | bytes 393224 | tf_op jit(solution)/shard_map/ppermute | solution.py:41
  120.1 9.5 %collective-permute-start.30 = (bf16[64,1024]{1,0:T(8,128)(2,1)S(1)}, bf16[64,1024]{1,0:T(8,128)(2,1)S(1)}, u32[]{:S(2)}, u32[]{:S(2)}) collective-permute-start(bf16[64,1024]{1,0:T(8,128)(2,1)S(1)} %get-tuple-element.305), channel_id=1, source_target_pairs={{0,2},{1,3},{2,0},{3,1},{4,6},{5,7},{6,4},{7,5},{8,10},{9,11},{10,... | collective-permute-start | bytes 393224 | tf_op jit(solution)/shard_map/ppermute | solution.py:41
  129.6 3.8 %collective-permute-start.32 = (bf16[64,1024]{1,0:T(8,128)(2,1)S(1)}, bf16[64,1024]{1,0:T(8,128)(2,1)S(1)}, u32[]{:S(2)}, u32[]{:S(2)}) collective-permute-start(bf16[64,1024]{1,0:T(8,128)(2,1)S(1)} %subtract_convert_fusion.3), channel_id=1, source_target_pairs={{0,1},{1,0},{2,3},{3,2},{4,5},{5,4},{6,7},{7,6},{8,9},{9,8},{10,11... | collective-permute-start | bytes 393224 | tf_op jit(solution)/shard_map/ppermute | solution.py:41
  132.1 7.8 %collective-permute-start.31 = (bf16[64,1024]{1,0:T(8,128)(2,1)S(1)}, bf16[64,1024]{1,0:T(8,128)(2,1)S(1)}, u32[]{:S(2)}, u32[]{:S(2)}) collective-permute-start(bf16[64,1024]{1,0:T(8,128)(2,1)S(1)} %add_convert_fusion.3), channel_id=1, source_target_pairs={{0,4},{4,0},{8,12},{12,8},{1,5},{5,1},{9,13},{13,9},{2,6},{6,2},{1... | collective-permute-start | bytes 393224 | tf_op jit(solution)/shard_map/ppermute | solution.py:41
  136.4 6.0 %collective-permute-start.34 = (bf16[64,1024]{1,0:T(8,128)(2,1)}, bf16[64,1024]{1,0:T(8,128)(2,1)}, u32[]{:S(2)}, u32[]{:S(2)}) collective-permute-start(bf16[64,1024]{1,0:T(8,128)(2,1)} %fusion.231), channel_id=1, source_target_pairs={{0,4},{4,0},{8,12},{12,8},{1,5},{5,1},{9,13},{13,9},{2,6},{6,2},{1... | collective-permute-start | bytes 393224 | tf_op jit(solution)/shard_map/ppermute | solution.py:41
  139.9 20.7 %copy-start = (f32[64,1024]{1,0:T(8,128)S(1)}, f32[64,1024]{1,0:T(8,128)}, u32[]{:S(2)}) copy-start(f32[64,1024]{1,0:T(8,128)} %get-tuple-element.260) | copy-start | bytes 786436
  142.3 2.3 %collective-permute-start.33 = (bf16[64,1024]{1,0:T(8,128)(2,1)S(1)}, bf16[64,1024]{1,0:T(8,128)(2,1)S(1)}, u32[]{:S(2)}, u32[]{:S(2)}) collective-permute-start(bf16[64,1024]{1,0:T(8,128)(2,1)S(1)} %fusion.201), channel_id=1, source_target_pairs={{0,1},{1,0},{2,3},{3,2},{4,5},{5,4},{6,7},{7,6},{8,9},{9,8},{10,11... | collective-permute-start | bytes 393224 | tf_op jit(solution)/shard_map/ppermute | solution.py:41
  143.4 12.7 %collective-permute-start.37 = (bf16[64,1024]{1,0:T(8,128)(2,1)S(1)}, bf16[64,1024]{1,0:T(8,128)(2,1)S(1)}, u32[]{:S(2)}, u32[]{:S(2)}) collective-permute-start(bf16[64,1024]{1,0:T(8,128)(2,1)S(1)} %get-tuple-element.303), channel_id=1, source_target_pairs={{0,8},{4,12},{8,0},{12,4},{1,9},{5,13},{9,1},{13,5},{2,10},{6,14},... | collective-permute-start | bytes 393224 | tf_op jit(solution)/shard_map/ppermute | solution.py:41
  144.7 8.7 %collective-permute-start.35 = (bf16[64,1024]{1,0:T(8,128)(2,1)S(1)}, bf16[64,1024]{1,0:T(8,128)(2,1)S(1)}, u32[]{:S(2)}, u32[]{:S(2)}) collective-permute-start(bf16[64,1024]{1,0:T(8,128)(2,1)S(1)} %get-tuple-element.301), channel_id=1, source_target_pairs={{0,2},{1,3},{2,0},{3,1},{4,6},{5,7},{6,4},{7,5},{8,10},{9,11},{10,... | collective-permute-start | bytes 393224 | tf_op jit(solution)/shard_map/ppermute | solution.py:41
  148.1 29.2 %slice-start = ((s8[10485760]{0:T(1024)(128)(4,1)}), s8[2097152]{0:T(1024)(128)(4,1)S(1)}, s32[]{:S(2)}) async-start(s8[10485760]{0:T(1024)(128)(4,1)} %bitcast.291), calls=%async_computation | async-start | bytes 4194304
  153.4 23.9 %slice-start.1 = ((s8[10485760]{0:T(1024)(128)(4,1)}), s8[4194304]{0:T(1024)(128)(4,1)S(1)}, s32[]{:S(2)}) async-start(s8[10485760]{0:T(1024)(128)(4,1)} %bitcast.291), calls=%async_computation.1 | async-start | bytes 8388608
  153.5 3.7 %collective-permute-start.36 = (bf16[64,1024]{1,0:T(8,128)(2,1)S(1)}, bf16[64,1024]{1,0:T(8,128)(2,1)S(1)}, u32[]{:S(2)}, u32[]{:S(2)}) collective-permute-start(bf16[64,1024]{1,0:T(8,128)(2,1)S(1)} %subtract_convert_fusion.2), channel_id=1, source_target_pairs={{0,1},{1,0},{2,3},{3,2},{4,5},{5,4},{6,7},{7,6},{8,9},{9,8},{10,11... | collective-permute-start | bytes 393224 | tf_op jit(solution)/shard_map/ppermute | solution.py:41
  156.1 7.0 %collective-permute-start.39 = (bf16[64,1024]{1,0:T(8,128)(2,1)S(1)}, bf16[64,1024]{1,0:T(8,128)(2,1)S(1)}, u32[]{:S(2)}, u32[]{:S(2)}) collective-permute-start(bf16[64,1024]{1,0:T(8,128)(2,1)S(1)} %add_convert_fusion.2), channel_id=1, source_target_pairs={{0,4},{4,0},{8,12},{12,8},{1,5},{5,1},{9,13},{13,9},{2,6},{6,2},{1... | collective-permute-start | bytes 393224 | tf_op jit(solution)/shard_map/ppermute | solution.py:41
  159.6 6.1 %collective-permute-start.38 = (bf16[64,1024]{1,0:T(8,128)(2,1)S(1)}, bf16[64,1024]{1,0:T(8,128)(2,1)S(1)}, u32[]{:S(2)}, u32[]{:S(2)}) collective-permute-start(bf16[64,1024]{1,0:T(8,128)(2,1)S(1)} %fusion.234), channel_id=1, source_target_pairs={{0,4},{4,0},{8,12},{12,8},{1,5},{5,1},{9,13},{13,9},{2,6},{6,2},{1... | collective-permute-start | bytes 393224 | tf_op jit(solution)/shard_map/ppermute | solution.py:41
  160.6 16.7 %slice-start.2 = ((s8[10485760]{0:T(1024)(128)(4,1)}), s8[4194304]{0:T(1024)(128)(4,1)S(1)}, s32[]{:S(2)}) async-start(s8[10485760]{0:T(1024)(128)(4,1)} %bitcast.291), calls=%async_computation.2 | async-start | bytes 8388608
  165.5 1.4 collective-permute-start.41
  166.9 5.6 %collective-permute-start.42 = (bf16[64,1024]{1,0:T(8,128)(2,1)S(1)}, bf16[64,1024]{1,0:T(8,128)(2,1)S(1)}, u32[]{:S(2)}, u32[]{:S(2)}) collective-permute-start(bf16[64,1024]{1,0:T(8,128)(2,1)S(1)} %get-tuple-element.297), channel_id=1, source_target_pairs={{0,2},{1,3},{2,0},{3,1},{4,6},{5,7},{6,4},{7,5},{8,10},{9,11},{10,... | collective-permute-start | bytes 393224 | tf_op jit(solution)/shard_map/ppermute | solution.py:41
  168.1 9.0 %collective-permute-start.40 = (bf16[64,1024]{1,0:T(8,128)(2,1)S(1)}, bf16[64,1024]{1,0:T(8,128)(2,1)S(1)}, u32[]{:S(2)}, u32[]{:S(2)}) collective-permute-start(bf16[64,1024]{1,0:T(8,128)(2,1)S(1)} %get-tuple-element.299), channel_id=1, source_target_pairs={{0,8},{4,12},{8,0},{12,4},{1,9},{5,13},{9,1},{13,5},{2,10},{6,14},... | collective-permute-start | bytes 393224 | tf_op jit(solution)/shard_map/ppermute | solution.py:41
  172.6 4.7 %collective-permute-start.44 = (bf16[64,1024]{1,0:T(8,128)(2,1)S(1)}, bf16[64,1024]{1,0:T(8,128)(2,1)S(1)}, u32[]{:S(2)}, u32[]{:S(2)}) collective-permute-start(bf16[64,1024]{1,0:T(8,128)(2,1)S(1)} %subtract_convert_fusion.1), channel_id=1, source_target_pairs={{0,1},{1,0},{2,3},{3,2},{4,5},{5,4},{6,7},{7,6},{8,9},{9,8},{10,11... | collective-permute-start | bytes 393224 | tf_op jit(solution)/shard_map/ppermute | solution.py:41
  177.2 6.2 %collective-permute-start.43 = (bf16[64,1024]{1,0:T(8,128)(2,1)S(1)}, bf16[64,1024]{1,0:T(8,128)(2,1)S(1)}, u32[]{:S(2)}, u32[]{:S(2)}) collective-permute-start(bf16[64,1024]{1,0:T(8,128)(2,1)S(1)} %add_convert_fusion.1), channel_id=1, source_target_pairs={{0,4},{4,0},{8,12},{12,8},{1,5},{5,1},{9,13},{13,9},{2,6},{6,2},{1... | collective-permute-start | bytes 393224 | tf_op jit(solution)/shard_map/ppermute | solution.py:41
  178.1 7.7 %collective-permute-start.45 = (bf16[64,1024]{1,0:T(8,128)(2,1)S(1)}, bf16[64,1024]{1,0:T(8,128)(2,1)S(1)}, u32[]{:S(2)}, u32[]{:S(2)}) collective-permute-start(bf16[64,1024]{1,0:T(8,128)(2,1)S(1)} %fusion.237), channel_id=1, source_target_pairs={{0,4},{4,0},{8,12},{12,8},{1,5},{5,1},{9,13},{13,9},{2,6},{6,2},{1... | collective-permute-start | bytes 393224 | tf_op jit(solution)/shard_map/ppermute | solution.py:41
  185.8 1.4 collective-permute-start.46
  187.2 5.6 %collective-permute-start.47 = (bf16[64,1024]{1,0:T(8,128)(2,1)S(1)}, bf16[64,1024]{1,0:T(8,128)(2,1)S(1)}, u32[]{:S(2)}, u32[]{:S(2)}) collective-permute-start(bf16[64,1024]{1,0:T(8,128)(2,1)S(1)} %get-tuple-element.295), channel_id=1, source_target_pairs={{0,2},{1,3},{2,0},{3,1},{4,6},{5,7},{6,4},{7,5},{8,10},{9,11},{10,... | collective-permute-start | bytes 393224 | tf_op jit(solution)/shard_map/ppermute | solution.py:41
  192.9 1.4 collective-permute-start.48
  195.1 5.6 %collective-permute-start.49 = (bf16[64,1024]{1,0:T(8,128)(2,1)S(1)}, bf16[64,1024]{1,0:T(8,128)(2,1)S(1)}, u32[]{:S(2)}, u32[]{:S(2)}) collective-permute-start(bf16[64,1024]{1,0:T(8,128)(2,1)S(1)} %fusion.240), channel_id=1, source_target_pairs={{0,4},{4,0},{8,12},{12,8},{1,5},{5,1},{9,13},{13,9},{2,6},{6,2},{1... | collective-permute-start | bytes 393224 | tf_op jit(solution)/shard_map/ppermute | solution.py:41
  200.7 8.5 %collective-permute-start.50 = (bf16[64,1024]{1,0:T(8,128)(2,1)S(1)}, bf16[64,1024]{1,0:T(8,128)(2,1)S(1)}, u32[]{:S(2)}, u32[]{:S(2)}) collective-permute-start(bf16[64,1024]{1,0:T(8,128)(2,1)S(1)} %broadcast_select_fusion), channel_id=1, source_target_pairs={{0,8},{4,12},{8,0},{12,4},{1,9},{5,13},{9,1},{13,5},{2,10},{6,14},... | collective-permute-start | bytes 393224 | tf_op jit(solution)/shard_map/ppermute | solution.py:41

commit v3 on v2

v3 whole, which is shorter than its diff:
```python
import functools

import jax
import jax.numpy as jnp
from jax import lax
from jax.experimental import pallas as pl
from jax.experimental.pallas import tpu as pltpu
from jax.sharding import PartitionSpec as P

STREAMS = 2
UNITS = 2 * STREAMS


def pair_index(block_row, column_index):
    return block_row * (block_row - 1) // 2 + column_index


HBM = pl.BlockSpec(memory_space=pltpu.HBM)
VMEM = pl.BlockSpec(memory_space=pltpu.VMEM)
SMEM = pl.BlockSpec(memory_space=pltpu.SMEM)
TILE = 256


def params():
    return pltpu.CompilerParams(vmem_limit_bytes=16 * 2**20)


COST = pl.CostEstimate(flops=1, bytes_accessed=1, transcendentals=0)


def fetch(source, indices, held, sems):
    rows = held.shape[1]
    tile = min(rows, TILE)
    copies = []
    for slot, index in enumerate(indices):
        tiles = []
        for t in range(rows // tile):
            cut = pl.ds(t * tile, tile)
            copy = pltpu.make_async_copy(source.at[index, cut], held.at[slot, cut], sems.at[slot, t])
            copy.start()
            tiles.append((cut, copy))
        copies.append(tiles)
    return copies


def times_transposed(left, right):
    return lax.dot_general(left, right, (((1,), (1,)), ((), ())), preferred_element_type=jnp.float32)


def fetch_scratch(blocks, rows, depth):
    return [
        pltpu.VMEM((blocks, rows, depth), jnp.bfloat16),
        pltpu.SemaphoreType.DMA((blocks, rows // min(rows, TILE))),
    ]


def pair_kernel(index, source, own, other, *refs):
    *older, keep, leave, held, sems = refs
    width = own.shape[0]
    (tiles,) = fetch(source, [index], held, sems)
    x = jnp.concatenate([own[...], other[...]], axis=0)
    for cut, copy in tiles:
        copy.wait()
        value = times_transposed(x, held[0, cut])
        if older:
            value = value + older[0][:, cut]
        keep[:, cut] = value[:width]
        leave[:, cut] = value[width:].astype(jnp.bfloat16)


def pair_product(source, index, own, other, older=None):
    rows, depth = source.shape[1:]
    width = own.shape[0]
    extra = [] if older is None else [older]
    return pl.pallas_call(
        functools.partial(pair_kernel, index),
        out_shape=(
            jax.ShapeDtypeStruct((width, rows), jnp.float32),
            jax.ShapeDtypeStruct((width, rows), jnp.bfloat16),
        ),
        in_specs=[HBM] + [VMEM] * (2 + len(extra)),
        out_specs=(VMEM, VMEM),
        scratch_shapes=fetch_scratch(1, rows, depth),
        compiler_params=params(),
        cost_estimate=COST,
    )(source, own, other, *extra)


def older_kernel(indices, streams, source, *refs):
    out, held, sems = refs[-3:]
    known = refs[: 2 * streams * len(indices)]
    before = refs[2 * streams * len(indices) : -3]
    copies = fetch(source, indices, held, sems)
    for slot, tiles in enumerate(copies):
        units = known[2 * streams * slot : 2 * streams * (slot + 1)]
        x = jnp.concatenate([u[...] for u in units], axis=0)
        for cut, copy in tiles:
            copy.wait()
            value = times_transposed(x, held[slot, cut])
            if slot:
                value = value + out[:, cut]
            elif before:
                value = value + before[0][:, cut]
            out[:, cut] = value


def older_products(source, indices, known, before=None):
    rows, depth = source.shape[1:]
    angles = len(known[0]) * known[0][0].shape[0]
    extra = [] if before is None else [before]
    flat = [u for units in known for u in units]
    return pl.pallas_call(
        functools.partial(older_kernel, indices, STREAMS),
        out_shape=jax.ShapeDtypeStruct((angles, rows), jnp.float32),
        in_specs=[HBM] + [VMEM] * (len(flat) + len(extra)),
        out_specs=VMEM,
        scratch_shapes=fetch_scratch(len(indices), rows, depth),
        compiler_params=params(),
        cost_estimate=COST,
    )(source, *flat, *extra)


def first_kernel(s, side, sides, source, keep, leave, product, right, held, sems, right_sem):
    width = keep.shape[0]
    (tiles,) = fetch(source, [0], held, sems)
    copy = pltpu.make_async_copy(sides.at[0, :, pl.ds(2 * s * width, 2 * width)], right, right_sem)
    copy.start()
    copy.wait()
    x = right[...].T
    for cut, tile in tiles:
        tile.wait()
        product[:, cut] = times_transposed(x, held[0, cut])
    own = pl.multiple_of(side[0] * width, width)
    other = pl.multiple_of((1 - side[0]) * width, width)
    keep[...] = product[pl.ds(own, width)]
    leave[...] = product[pl.ds(other, width)].astype(jnp.bfloat16)


def first_products(s, side, sides, source):
    rows, depth = source.shape[1:]
    width = sides.shape[2] // UNITS
    return pl.pallas_call(
        functools.partial(first_kernel, s),
        out_shape=(
            jax.ShapeDtypeStruct((width, rows), jnp.float32),
            jax.ShapeDtypeStruct((width, rows), jnp.bfloat16),
        ),
        in_specs=[SMEM, HBM, HBM],
        out_specs=(VMEM, VMEM),
        scratch_shapes=[
            pltpu.VMEM((2 * width, rows), jnp.float32),
            pltpu.VMEM((depth, 2 * width), jnp.bfloat16),
            *fetch_scratch(1, rows, depth),
            pltpu.SemaphoreType.DMA,
        ],
        compiler_params=params(),
        cost_estimate=COST,
    )(side, sides, source)


def turn_kernel(width, side, sides, out, turned):
    turned[...] = sides[0].T
    for s in range(STREAMS):
        own = pl.multiple_of((2 * s + side[0]) * width, width)
        out[0, s] = turned[pl.ds(own, width)]


def turned_sides(side, sides):
    steps, rows, angles = sides.shape
    width = angles // UNITS
    return pl.pallas_call(
        functools.partial(turn_kernel, width),
        grid=(steps - 1,),
        out_shape=jax.ShapeDtypeStruct((steps - 1, STREAMS, width, rows), jnp.bfloat16),
        in_specs=[SMEM, pl.BlockSpec((1, rows, angles), lambda i: (i + 1, 0, 0))],
        out_specs=pl.BlockSpec((1, STREAMS, width, rows), lambda i: (i, 0, 0, 0)),
        scratch_shapes=[pltpu.VMEM((angles, rows), jnp.bfloat16)],
        compiler_params=params(),
        cost_estimate=COST,
    )(side, sides)


def wide(value):
    return value.astype(jnp.float32)


def narrow(value):
    return value.astype(jnp.bfloat16)


class Order:
    def __init__(self):
        self.last = None

    def run(self, work, *values):
        if self.last is not None:
            *values, _ = lax.optimization_barrier((*values, self.last))
        result = work(*values)
        self.last = result[0] if isinstance(result, (tuple, list)) else result
        return result


def make_per_device(n_row, n_col):
    def trade(value, axis, step):
        size = n_row if axis == "row" else n_col
        return lax.ppermute(value, axis, [(i, i ^ step) for i in range(size)])

    def more_rounds(value, axis):
        size = n_row if axis == "row" else n_col
        step = 4
        while step < size:
            value = value + wide(trade(narrow(value), axis, step))
            step *= 2
        return value

    def per_device(factor_blocks, inverse_blocks, right_sides):
        steps_total, group_rows, angles = right_sides.shape
        last_step = steps_total - 1
        place = lax.axis_index("row")
        core = lax.axis_index("col") & 1
        side = (place & 1) ^ core
        width = angles // UNITS
        exact = n_row == UNITS
        order = Order()

        side_ref = side.astype(jnp.int32).reshape(1)
        solved = [[None] * STREAMS for _ in range(steps_total)]
        state = [dict() for _ in range(STREAMS)]
        sums = [None] * (steps_total + 1)

        def older(step, blocks):
            if step >= steps_total or not blocks:
                return
            units = [[u for s in range(STREAMS) for u in solved[j][s]] for j in blocks]
            flat = [u for known in units for u in known]
            extra = [] if sums[step] is None else [sums[step]]

            def work(*values):
                known = [values[2 * STREAMS * i : 2 * STREAMS * (i + 1)] for i in range(len(blocks))]
                return older_products(
                    factor_blocks, [pair_index(step, j) for j in blocks], known, *values[len(flat) :]
                )

            sums[step] = order.run(work, *flat, *extra)

        def factor(s, step):
            st = state[s]
            rest = [] if sums[step] is None else [sums[step][2 * s * width : 2 * (s + 1) * width]]
            st["sum"], leaving = order.run(
                lambda *v: pair_product(factor_blocks, pair_index(step, step - 1), *v),
                *solved[step - 1][s],
                *rest,
            )
            st["flight"] = trade(leaving, "col", 1)

        def chip_sum(s):
            st = state[s]

            def work(value, arrived):
                value = value + wide(arrived)
                return narrow(value), value

            leaving, st["sum"] = order.run(work, st["sum"], st["flight"])
            st["flight"] = trade(leaving, "col", 2) if n_col > 2 else None

        def residual(s, step):
            st = state[s]

            def work(side_values, value, *arrived):
                for a in arrived:
                    value = more_rounds(value + wide(a), "col")
                return narrow(wide(side_values) - value)

            arrived = [] if st["flight"] is None else [st["flight"]]
            st["own"] = order.run(work, base[step - 1, s], st["sum"], *arrived)
            st["flight"] = trade(st["own"], "col", 1)

        def inverse(s, step):
            st = state[s]
            st["total"], leaving = order.run(
                lambda *v: pair_product(inverse_blocks, step, *v), st["own"], st["flight"]
            )
            st["flight"] = trade(leaving, "row", 1)

        def final_inverse(s):
            st = state[s]
            own, other = st["own"], st["flight"]
            st["own"] = jnp.where(core == 0, own, other)
            st["flight"] = jnp.where(core == 0, other, own)
            inverse(s, last_step)

        def pair_sum(s):
            st = state[s]

            def work(value, arrived):
                value = value + wide(arrived)
                return narrow(value), value

            st["leaving"], st["total"] = order.run(work, st["total"], st["flight"])

        def cross(s):
            st = state[s]
            st["flight"] = trade(st["leaving"], "row", 2) if n_row > 2 else None

        def solve(s, step):
            st = state[s]

            def work(value, *arrived):
                for a in arrived:
                    value = more_rounds(value + wide(a), "row")
                return narrow(value)

            arrived = [] if st["flight"] is None else [st["flight"]]
            own = order.run(work, st["total"], *arrived)
            solved[step][s] = (own, trade(own, "row", 1))

        for s in range(STREAMS):
            state[s]["total"], leaving = order.run(
                lambda v: first_products(s, side_ref, v, inverse_blocks), right_sides
            )
            state[s]["flight"] = trade(leaving, "row", 1)
        if steps_total > 1:
            base = order.run(lambda v: turned_sides(side_ref, v), right_sides)
        for s in range(STREAMS):
            pair_sum(s)
            cross(s)
        solve(0, 0)

        for step in range(1, steps_total):
            final = exact and step == last_step
            factor(0, step)
            if step > 1:
                pair_sum(1)
                cross(1)
            chip_sum(0)
            if step == 1:
                solve(1, 0)
            older(step + 1, range(step - 1))
            residual(0, step)
            if step > 1:
                solve(1, step - 1)
            if final:
                final_inverse(0)
            else:
                inverse(0, step)
            factor(1, step)
            pair_sum(0)
            if not final:
                cross(0)
            chip_sum(1)
            older(step + 1, [step - 1])
            residual(1, step)
            if final:
                final_inverse(1)
            else:
                solve(0, step)
                inverse(1, step)

        pair_sum(1)
        outputs = []
        for step in range(steps_total):
            if exact and step == last_step:
                low = place < n_row // 2
                leaving = order.run(
                    lambda a, b: jnp.where(low, b, a), state[0]["leaving"], state[1]["leaving"]
                )
                arrived = trade(leaving, "row", 2)
                found = narrow(jnp.where(low, state[0]["total"], state[1]["total"]) + wide(arrived))
                outputs.append(found.T)
                continue
            if step == last_step:
                cross(1)
                solve(1, step)
            unit = place * UNITS // n_row
            found = solved[step][0][0]
            for s in range(STREAMS):
                for u in range(2):
                    found = jnp.where(unit == 2 * s + (u ^ side), solved[step][s][u], found)
            if not exact:
                slot = angles // n_row
                found = lax.dynamic_slice_in_dim(found, (place * slot) % width, slot, 0)
            outputs.append(found.T)
        return jnp.stack(outputs, axis=0)

    return per_device


def solution(mesh):
    placed = (P("groups", "row", "col"), P("groups", "col", "row"), P("groups", "row", None))
    return jax.shard_map(
        make_per_device(mesh.shape["row"], mesh.shape["col"]),
        mesh=mesh,
        in_specs=placed,
        out_specs=P("groups", "col", "row"),
        check_vma=False,
    )
```

time: 212 us -> 203 us (0.958)
  matrix products: 108 us -> 0 us
  waiting for transfers between devices: 35.4 us -> 87.8 us
  Pallas kernels: 0 us -> 49.5 us
  local copies, waits for them, and re-layouts: 6.74 us -> 20.3 us
  other arithmetic: 12.2 us -> 4.68 us
  starting transfers between devices: 46.9 us -> 39.9 us
    dot_general x46 -> x0, matrix products: 108 us -> none  [times_transposed(): lax.dot_general(left, right, (((1,), (1,)), ((), ())), preferred_element_...]
    ppermute x51, waiting for transfers between devices: 35.4 us -> 87.8 us  [trade(): return lax.ppermute(value, axis, [(i, i ^ step) for i in range(size)])]
    pallas_call x0 -> x24, Pallas kernels: none -> 49.5 us  [the longest x16 32.5 us: pair_product(): pl.pallas_call(functools.partial(pair_kernel, index), out_shape=(jax.Shap...]
    unnamed x18 -> x44, local copies, waits for them, and re-layouts: 0.69 us -> 18.5 us
    ppermute x51, starting transfers between devices: 46.9 us -> 39.9 us  [trade(): return lax.ppermute(value, axis, [(i, i ^ step) for i in range(size)])]
    convert_element_type x34, other arithmetic: 7.81 us -> 2.68 us  [narrow(): return value.astype(jnp.bfloat16)]
    unnamed x5 -> x6, other arithmetic: 2.92 us -> 0.3 us
  transfers between devices with their start and end apart: 51 -> 51, of which waited for: 15 -> 36; matrix products, arithmetic and copies ran while one was open for 57% -> 2% of each run, Pallas kernels for 0% -> 21%
where the time goes in v3:
time: 203 us
  waiting for transfers between devices  87.8 us (43%)
  Pallas kernels  49.5 us (24%)
  starting transfers between devices  39.9 us (20%)
  local copies, waits for them, and re-layouts  20.3 us (10%)
  other arithmetic  4.68 us (2%)
    ppermute x51, waiting for transfers between devices, trade(): return lax.ppermute(value, axis, [(i, i ^ step) for i in range(size)])  87.8 us
    ppermute x51, starting transfers between devices, trade(): return lax.ppermute(value, axis, [(i, i ^ step) for i in range(size)])  39.9 us
    pallas_call x16, Pallas kernels, pair_product(): pl.pallas_call(functools.partial(pair_kernel, index), out_shape=(jax.Shap...  32.5 us
    unnamed x44, local copies, waits for them, and re-layouts  18.5 us
    pallas_call x5, Pallas kernels, older_products(): pl.pallas_call(functools.partial(older_kernel, indices, STREAMS), out_sha...  11.9 us
    pallas_call x2, Pallas kernels, first_products(): pl.pallas_call(functools.partial(first_kernel, s), out_shape=(jax.ShapeDt...  4.19 us
  transfers between devices with their start and end apart: 51, of which 36 were waited for; matrix products, arithmetic and copies ran while one was open for 2% of the time, Pallas kernels for 21%

profile of v3, /device:TPU:0, one launch (start us, length us, event | category | flops | bytes accessed | tf_op | source)
XLA Modules:
  0.0 203.1 jit_solution(13504069857153154793)
XLA Ops:
  0.0 4.0 %copy-done.2 = bf16[5,1024,1024]{2,1,0:T(8,128)(2,1)S(1)} copy-done((bf16[5,1024,1024]{2,1,0:T(8,128)(2,1)S(1)}, bf16[5,1024,1024]{2,1,0:T(8,128)(2,1)}, u32[]{:S(2)}) %copy-start.2) | copy-done | bytes 10485784
  4.0 1.7 copy-done.4
  5.7 2.1 %shard_map.37 = (f32[64,1024]{1,0:T(8,128)S(1)}, bf16[64,1024]{1,0:T(8,128)(2,1)S(1)}) custom-call(s32[1]{0:T(128)} %bitcast.side, bf16[5,1024,256]{2,1,0:T(8,128)(2,1)S(1)} %copy-done.4, bf16[5,1024,1024]{2,1,0:T(8,128)(2,1)S(1)} %copy-done.2), custom_call_target="tpu_custom_call" | custom-call | flops 1 | bytes 1 | tf_op jit(solution)/shard_map/pallas_call | solution.py:142
  7.8 3.1 %collective-permute-start.1 = (bf16[64,1024]{1,0:T(8,128)(2,1)S(1)}, bf16[64,1024]{1,0:T(8,128)(2,1)S(1)}, u32[]{:S(2)}, u32[]{:S(2)}) collective-permute-start(bf16[64,1024]{1,0:T(8,128)(2,1)S(1)} %get-tuple-element.189), channel_id=1, source_target_pairs={{0,4},{4,0},{8,12},{12,8},{1,5},{5,1},{9,13},{13,9},{2,6},{6,2},{1... | collective-permute-start | bytes 393224 | tf_op jit(solution)/shard_map/ppermute | solution.py:206
  10.9 2.1 %shard_map.38 = (f32[64,1024]{1,0:T(8,128)S(1)}, bf16[64,1024]{1,0:T(8,128)(2,1)S(1)}) custom-call(s32[1]{0:T(128)} %bitcast.side, bf16[5,1024,256]{2,1,0:T(8,128)(2,1)S(1)} %copy-done.4, bf16[5,1024,1024]{2,1,0:T(8,128)(2,1)S(1)} %copy-done.2), custom_call_target="tpu_custom_call" | custom-call | flops 1 | bytes 1 | tf_op jit(solution)/shard_map/pallas_call | solution.py:142
  14.4 2.8 %collective-permute-start.3 = (bf16[64,1024]{1,0:T(8,128)(2,1)S(1)}, bf16[64,1024]{1,0:T(8,128)(2,1)S(1)}, u32[]{:S(2)}, u32[]{:S(2)}) collective-permute-start(bf16[64,1024]{1,0:T(8,128)(2,1)S(1)} %get-tuple-element.395), channel_id=1, source_target_pairs={{0,8},{4,12},{8,0},{12,4},{1,9},{5,13},{9,1},{13,5},{2,10},{6,14},... | collective-permute-start | bytes 393224 | tf_op jit(solution)/shard_map/ppermute | solution.py:206
  17.3 2.7 %collective-permute-done = bf16[64,1024]{1,0:T(8,128)(2,1)S(1)} collective-permute-done((bf16[64,1024]{1,0:T(8,128)(2,1)S(1)}, bf16[64,1024]{1,0:T(8,128)(2,1)S(1)}, u32[]{:S(2)}, u32[]{:S(2)}) %collective-permute-start) | collective-permute-done | bytes 131104 | tf_op jit(solution)/shard_map/ppermute | solution.py:206
  20.0 3.0 %collective-permute-done.3 = bf16[64,1024]{1,0:T(8,128)(2,1)S(1)} collective-permute-done((bf16[64,1024]{1,0:T(8,128)(2,1)S(1)}, bf16[64,1024]{1,0:T(8,128)(2,1)S(1)}, u32[]{:S(2)}, u32[]{:S(2)}) %collective-permute-start.3) | collective-permute-done | bytes 131104 | tf_op jit(solution)/shard_map/ppermute | solution.py:206
  23.7 4.4 %collective-permute-done.4.other.refs_1_ = bf16[64,1024]{1,0:T(8,128)(2,1)S(1)} collective-permute-done((bf16[64,1024]{1,0:T(8,128)(2,1)S(1)}, bf16[64,1024]{1,0:T(8,128)(2,1)S(1)}, u32[]{:S(2)}, u32[]{:S(2)}) %collective-permute-start.4) | collective-permute-done | bytes 131104 | tf_op jit(solution)/shard_map/ppermute | solution.py:206
  28.1 1.9 shard_map.40
  30.8 2.3 %collective-permute-start.2 = (bf16[64,1024]{1,0:T(8,128)(2,1)S(1)}, bf16[64,1024]{1,0:T(8,128)(2,1)S(1)}, u32[]{:S(2)}, u32[]{:S(2)}) collective-permute-start(bf16[64,1024]{1,0:T(8,128)(2,1)S(1)} %get-tuple-element.393), channel_id=1, source_target_pairs={{0,8},{4,12},{8,0},{12,4},{1,9},{5,13},{9,1},{13,5},{2,10},{6,14},... | collective-permute-start | bytes 393224 | tf_op jit(solution)/shard_map/ppermute | solution.py:206
  33.2 1.6 collective-permute-start.7
  34.7 5.7 %collective-permute-done.2 = bf16[64,1024]{1,0:T(8,128)(2,1)S(1)} collective-permute-done((bf16[64,1024]{1,0:T(8,128)(2,1)S(1)}, bf16[64,1024]{1,0:T(8,128)(2,1)S(1)}, u32[]{:S(2)}, u32[]{:S(2)}) %collective-permute-start.2) | collective-permute-done | bytes 131104 | tf_op jit(solution)/shard_map/ppermute | solution.py:206
  41.9 1.9 shard_map.41
  44.7 1.8 collective-permute-done.6.other.refs_3_
  46.5 1.9 shard_map.42
  49.9 1.6 collective-permute-start.11
  51.5 2.2 %collective-permute-start.13 = (bf16[64,1024]{1,0:T(8,128)(2,1)S(1)}, bf16[64,1024]{1,0:T(8,128)(2,1)S(1)}, u32[]{:S(2)}, u32[]{:S(2)}) collective-permute-start(bf16[64,1024]{1,0:T(8,128)(2,1)S(1)} %get-tuple-element.389), channel_id=1, source_target_pairs={{0,8},{4,12},{8,0},{12,4},{1,9},{5,13},{9,1},{13,5},{2,10},{6,14},... | collective-permute-start | bytes 393224 | tf_op jit(solution)/shard_map/ppermute | solution.py:206
  53.7 2.0 shard_map.43
  55.8 4.6 %collective-permute-done.13 = bf16[64,1024]{1,0:T(8,128)(2,1)S(1)} collective-permute-done((bf16[64,1024]{1,0:T(8,128)(2,1)S(1)}, bf16[64,1024]{1,0:T(8,128)(2,1)S(1)}, u32[]{:S(2)}, u32[]{:S(2)}) %collective-permute-start.13) | collective-permute-done | bytes 131104 | tf_op jit(solution)/shard_map/ppermute | solution.py:206
  60.6 1.9 shard_map.44
  62.5 2.1 %collective-permute-start.14 = (bf16[64,1024]{1,0:T(8,128)(2,1)S(1)}, bf16[64,1024]{1,0:T(8,128)(2,1)S(1)}, u32[]{:S(2)}, u32[]{:S(2)}) collective-permute-start(bf16[64,1024]{1,0:T(8,128)(2,1)S(1)} %get-tuple-element.232), channel_id=1, source_target_pairs={{0,4},{4,0},{8,12},{12,8},{1,5},{5,1},{9,13},{13,9},{2,6},{6,2},{1... | collective-permute-start | bytes 393224 | tf_op jit(solution)/shard_map/ppermute | solution.py:206
  66.2 1.9 shard_map.45
  70.0 1.8 collective-permute-start.16
  71.8 2.0 shard_map.46.refs_4_
  75.3 3.7 %collective-permute-done.16 = bf16[64,1024]{1,0:T(8,128)(2,1)S(1)} collective-permute-done((bf16[64,1024]{1,0:T(8,128)(2,1)S(1)}, bf16[64,1024]{1,0:T(8,128)(2,1)S(1)}, u32[]{:S(2)}, u32[]{:S(2)}) %collective-permute-start.16) | collective-permute-done | bytes 131104 | tf_op jit(solution)/shard_map/ppermute | solution.py:206
  79.1 1.9 shard_map.47
  81.0 2.1 %collective-permute-start.22 = (bf16[64,1024]{1,0:T(8,128)(2,1)S(1)}, bf16[64,1024]{1,0:T(8,128)(2,1)S(1)}, u32[]{:S(2)}, u32[]{:S(2)}) collective-permute-start(bf16[64,1024]{1,0:T(8,128)(2,1)S(1)} %get-tuple-element.259), channel_id=1, source_target_pairs={{0,4},{4,0},{8,12},{12,8},{1,5},{5,1},{9,13},{13,9},{2,6},{6,2},{1... | collective-permute-start | bytes 393224 | tf_op jit(solution)/shard_map/ppermute | solution.py:206
  83.1 1.9 collective-permute-done.19.other.refs_3_.refs_7_
  85.0 1.9 shard_map.48
  88.3 1.9 collective-permute-start.23
  91.0 2.2 %shard_map.49 = f32[256,1024]{1,0:T(8,128)S(1)} custom-call(bf16[10,1024,1024]{2,1,0:T(8,128)(2,1)S(1)} %copy-done, bf16[64,1024]{1,0:T(8,128)(2,1)S(1)} %add_convert_fusion.6.own.refs_0_.refs_4_, bf16[64,1024]{1,0:T(8,128)(2,1)S(1)} %collective-permute-done.15.other.refs_1_.refs_5_, bf16[64,1024]{1,0:T(8,128)(2,1)S(1)} %add_convert_fusion.5.own.refs_2_.refs_6_, ...), custom_call_target="tpu_custom_call" | custom-call | flops 1 | bytes 1 | tf_op jit(solution)/shard_map/pallas_call | solution.py:112
  94.2 4.9 %collective-permute-done.25 = bf16[64,1024]{1,0:T(8,128)(2,1)S(1)} collective-permute-done((bf16[64,1024]{1,0:T(8,128)(2,1)S(1)}, bf16[64,1024]{1,0:T(8,128)(2,1)S(1)}, u32[]{:S(2)}, u32[]{:S(2)}) %collective-permute-start.25) | collective-permute-done | bytes 131104 | tf_op jit(solution)/shard_map/ppermute | solution.py:206
  99.3 1.9 shard_map.50
  101.2 2.1 %collective-permute-start.26 = (bf16[64,1024]{1,0:T(8,128)(2,1)S(1)}, bf16[64,1024]{1,0:T(8,128)(2,1)S(1)}, u32[]{:S(2)}, u32[]{:S(2)}) collective-permute-start(bf16[64,1024]{1,0:T(8,128)(2,1)S(1)} %get-tuple-element.277), channel_id=1, source_target_pairs={{0,4},{4,0},{8,12},{12,8},{1,5},{5,1},{9,13},{13,9},{2,6},{6,2},{1... | collective-permute-start | bytes 393224 | tf_op jit(solution)/shard_map/ppermute | solution.py:206
  103.3 2.1 %collective-permute-done.27.other.refs_1_ = bf16[64,1024]{1,0:T(8,128)(2,1)S(1)} collective-permute-done((bf16[64,1024]{1,0:T(8,128)(2,1)S(1)}, bf16[64,1024]{1,0:T(8,128)(2,1)S(1)}, u32[]{:S(2)}, u32[]{:S(2)}) %collective-permute-start.27) | collective-permute-done | bytes 131104 | tf_op jit(solution)/shard_map/ppermute | solution.py:206
  105.4 1.9 shard_map.51
  109.3 3.6 %shard_map.52.refs_4_ = f32[256,1024]{1,0:T(8,128)S(1)} custom-call(bf16[10,1024,1024]{2,1,0:T(8,128)(2,1)S(1)} %copy-done, bf16[64,1024]{1,0:T(8,128)(2,1)S(1)} %add_convert_fusion.8.own.refs_0_, bf16[64,1024]{1,0:T(8,128)(2,1)S(1)} %collective-permute-done.4.other.refs_1_, bf16[64,1024]{1,0:T(8,128)(2,1)S(1)} %add_convert_fusion.7.own.refs_2_, ...), custom_call_target="tpu_custom_call" | custom-call | flops 1 | bytes 1 | tf_op jit(solution)/shard_map/pallas_call | solution.py:112
  112.9 1.5 collective-permute-done.30
  114.6 2.8 %collective-permute-done.28 = bf16[64,1024]{1,0:T(8,128)(2,1)S(1)} collective-permute-done((bf16[64,1024]{1,0:T(8,128)(2,1)S(1)}, bf16[64,1024]{1,0:T(8,128)(2,1)S(1)}, u32[]{:S(2)}, u32[]{:S(2)}) %collective-permute-start.28) | collective-permute-done | bytes 131104 | tf_op jit(solution)/shard_map/ppermute | solution.py:206
  117.5 1.9 shard_map.53
  119.4 2.1 %collective-permute-start.34 = (bf16[64,1024]{1,0:T(8,128)(2,1)S(1)}, bf16[64,1024]{1,0:T(8,128)(2,1)S(1)}, u32[]{:S(2)}, u32[]{:S(2)}) collective-permute-start(bf16[64,1024]{1,0:T(8,128)(2,1)S(1)} %get-tuple-element.308), channel_id=1, source_target_pairs={{0,4},{4,0},{8,12},{12,8},{1,5},{5,1},{9,13},{13,9},{2,6},{6,2},{1... | collective-permute-start | bytes 393224 | tf_op jit(solution)/shard_map/ppermute | solution.py:206
  121.5 2.2 %collective-permute-done.31.other.refs_3_ = bf16[64,1024]{1,0:T(8,128)(2,1)S(1)} collective-permute-done((bf16[64,1024]{1,0:T(8,128)(2,1)S(1)}, bf16[64,1024]{1,0:T(8,128)(2,1)S(1)}, u32[]{:S(2)}, u32[]{:S(2)}) %collective-permute-start.31) | collective-permute-done | bytes 131104 | tf_op jit(solution)/shard_map/ppermute | solution.py:206
  123.7 1.9 shard_map.54
  127.1 1.5 collective-permute-start.35
  129.0 2.0 shard_map.55
  131.0 1.6 collective-permute-done.35
  132.8 4.3 %collective-permute-done.37 = bf16[64,1024]{1,0:T(8,128)(2,1)S(1)} collective-permute-done((bf16[64,1024]{1,0:T(8,128)(2,1)S(1)}, bf16[64,1024]{1,0:T(8,128)(2,1)S(1)}, u32[]{:S(2)}, u32[]{:S(2)}) %collective-permute-start.37) | collective-permute-done | bytes 131104 | tf_op jit(solution)/shard_map/ppermute | solution.py:206
  137.3 1.9 shard_map.56
  139.2 2.1 %collective-permute-start.38 = (bf16[64,1024]{1,0:T(8,128)(2,1)S(1)}, bf16[64,1024]{1,0:T(8,128)(2,1)S(1)}, u32[]{:S(2)}, u32[]{:S(2)}) collective-permute-start(bf16[64,1024]{1,0:T(8,128)(2,1)S(1)} %get-tuple-element.326), channel_id=1, source_target_pairs={{0,4},{4,0},{8,12},{12,8},{1,5},{5,1},{9,13},{13,9},{2,6},{6,2},{1... | collective-permute-start | bytes 393224 | tf_op jit(solution)/shard_map/ppermute | solution.py:206
  143.5 1.9 shard_map.57
  147.3 5.1 %collective-permute-done.42 = bf16[64,1024]{1,0:T(8,128)(2,1)S(1)} collective-permute-done((bf16[64,1024]{1,0:T(8,128)(2,1)S(1)}, bf16[64,1024]{1,0:T(8,128)(2,1)S(1)}, u32[]{:S(2)}, u32[]{:S(2)}) %collective-permute-start.42) | collective-permute-done | bytes 131104 | tf_op jit(solution)/shard_map/ppermute | solution.py:206
  152.6 2.8 %collective-permute-done.40 = bf16[64,1024]{1,0:T(8,128)(2,1)S(1)} collective-permute-done((bf16[64,1024]{1,0:T(8,128)(2,1)S(1)}, bf16[64,1024]{1,0:T(8,128)(2,1)S(1)}, u32[]{:S(2)}, u32[]{:S(2)}) %collective-permute-start.40) | collective-permute-done | bytes 131104 | tf_op jit(solution)/shard_map/ppermute | solution.py:206
  156.1 4.0 %copy-done.3 = bf16[5,1024,1024]{2,1,0:T(8,128)(2,1)S(1)} copy-done((bf16[5,1024,1024]{2,1,0:T(8,128)(2,1)S(1)}, bf16[5,1024,1024]{2,1,0:T(8,128)(2,1)}, u32[]{:S(2)}) %copy-start.3) | copy-done | bytes 10485784
  160.1 2.6 %shard_map.58 = (f32[64,1024]{1,0:T(8,128)S(1)}, bf16[64,1024]{1,0:T(8,128)(2,1)}) custom-call(bf16[5,1024,1024]{2,1,0:T(8,128)(2,1)S(1)} %copy-done.3, bf16[64,1024]{1,0:T(8,128)(2,1)S(1)} %get-tuple-element.341.own, bf16[64,1024]{1,0:T(8,128)(2,1)S(1)} %get-tuple-element.342.other), custom_call_target="tpu_custom_call" | custom-call | flops 1 | bytes 1 | tf_op jit(solution)/shard_map/pallas_call | solution.py:75
  163.4 2.0 collective-permute-start.45
  165.4 7.0 %copy-done.1 = bf16[10,1024,1024]{2,1,0:T(8,128)(2,1)S(1)} copy-done((bf16[10,1024,1024]{2,1,0:T(8,128)(2,1)S(1)}, bf16[10,1024,1024]{2,1,0:T(8,128)(2,1)}, u32[]{:S(2)}) %copy-start.1) | copy-done | bytes 20971544
  173.4 3.2 %shard_map.59 = (f32[64,1024]{1,0:T(8,128)S(1)}, bf16[64,1024]{1,0:T(8,128)(2,1)S(1)}) custom-call(bf16[10,1024,1024]{2,1,0:T(8,128)(2,1)S(1)} %copy-done.1, bf16[64,1024]{1,0:T(8,128)(2,1)} %add_convert_fusion.1.own, bf16[64,1024]{1,0:T(8,128)(2,1)} %collective-permute-done.43.other, f32[128,1024]{1,0:T(8,128)S(1)} %copy-done.5), custom_call_target="tpu_custom_call" | custom-call | flops 1 | bytes 1 | tf_op jit(solution)/shard_map/pallas_call | solution.py:75
  178.2 1.5 collective-permute-start.47
  179.8 4.0 %collective-permute-done.47 = bf16[64,1024]{1,0:T(8,128)(2,1)S(1)} collective-permute-done((bf16[64,1024]{1,0:T(8,128)(2,1)S(1)}, bf16[64,1024]{1,0:T(8,128)(2,1)S(1)}, u32[]{:S(2)}, u32[]{:S(2)}) %collective-permute-start.47) | collective-permute-done | bytes 131104 | tf_op jit(solution)/shard_map/ppermute | solution.py:206
  185.3 1.9 shard_map.60
  187.4 5.4 %collective-permute-done.49 = bf16[64,1024]{1,0:T(8,128)(2,1)S(1)} collective-permute-done((bf16[64,1024]{1,0:T(8,128)(2,1)S(1)}, bf16[64,1024]{1,0:T(8,128)(2,1)S(1)}, u32[]{:S(2)}, u32[]{:S(2)}) %collective-permute-start.49) | collective-permute-done | bytes 131104 | tf_op jit(solution)/shard_map/ppermute | solution.py:206
  194.0 7.4 %collective-permute-done.50 = bf16[64,1024]{1,0:T(8,128)(2,1)S(1)} collective-permute-done((bf16[64,1024]{1,0:T(8,128)(2,1)S(1)}, bf16[64,1024]{1,0:T(8,128)(2,1)S(1)}, u32[]{:S(2)}, u32[]{:S(2)}) %collective-permute-start.50) | collective-permute-done | bytes 131104 | tf_op jit(solution)/shard_map/ppermute | solution.py:206
  201.4 1.6 fusion.3
  (154 shorter events, 30.4 us)
Async XLA Ops:
  5.7 22.4 %copy-start = (bf16[10,1024,1024]{2,1,0:T(8,128)(2,1)S(1)}, bf16[10,1024,1024]{2,1,0:T(8,128)(2,1)}, u32[]{:S(2)}) copy-start(bf16[10,1024,1024]{2,1,0:T(8,128)(2,1)} %source.44) | copy-start | bytes 62914564
  7.8 6.6 %collective-permute-start.1 = (bf16[64,1024]{1,0:T(8,128)(2,1)S(1)}, bf16[64,1024]{1,0:T(8,128)(2,1)S(1)}, u32[]{:S(2)}, u32[]{:S(2)}) collective-permute-start(bf16[64,1024]{1,0:T(8,128)(2,1)S(1)} %get-tuple-element.189), channel_id=1, source_target_pairs={{0,4},{4,0},{8,12},{12,8},{1,5},{5,1},{9,13},{13,9},{2,6},{6,2},{1... | collective-permute-start | bytes 393224 | tf_op jit(solution)/shard_map/ppermute | solution.py:206
  13.0 6.9 %collective-permute-start = (bf16[64,1024]{1,0:T(8,128)(2,1)S(1)}, bf16[64,1024]{1,0:T(8,128)(2,1)S(1)}, u32[]{:S(2)}, u32[]{:S(2)}) collective-permute-start(bf16[64,1024]{1,0:T(8,128)(2,1)S(1)} %get-tuple-element.188), channel_id=1, source_target_pairs={{0,4},{4,0},{8,12},{12,8},{1,5},{5,1},{9,13},{13,9},{2,6},{6,2},{1... | collective-permute-start | bytes 393224 | tf_op jit(solution)/shard_map/ppermute | solution.py:206
  14.4 8.5 %collective-permute-start.3 = (bf16[64,1024]{1,0:T(8,128)(2,1)S(1)}, bf16[64,1024]{1,0:T(8,128)(2,1)S(1)}, u32[]{:S(2)}, u32[]{:S(2)}) collective-permute-start(bf16[64,1024]{1,0:T(8,128)(2,1)S(1)} %get-tuple-element.395), channel_id=1, source_target_pairs={{0,8},{4,12},{8,0},{12,4},{1,9},{5,13},{9,1},{13,5},{2,10},{6,14},... | collective-permute-start | bytes 393224 | tf_op jit(solution)/shard_map/ppermute | solution.py:206
  23.0 18.9 %slice-start = ((s8[10485760]{0:T(1024)(128)(4,1)}), s8[4194304]{0:T(1024)(128)(4,1)S(1)}, s32[]{:S(2)}) async-start(s8[10485760]{0:T(1024)(128)(4,1)} %bitcast.39), calls=%async_computation | async-start | bytes 8388608
  23.0 18.9 %slice-start.1 = ((s8[10485760]{0:T(1024)(128)(4,1)}), s8[4194304]{0:T(1024)(128)(4,1)S(1)}, s32[]{:S(2)}) async-start(s8[10485760]{0:T(1024)(128)(4,1)} %bitcast.39), calls=%async_computation.1 | async-start | bytes 8388608
  23.0 18.9 %slice-start.2 = ((s8[10485760]{0:T(1024)(128)(4,1)}), s8[2097152]{0:T(1024)(128)(4,1)S(1)}, s32[]{:S(2)}) async-start(s8[10485760]{0:T(1024)(128)(4,1)} %bitcast.39), calls=%async_computation.2 | async-start | bytes 4194304
  23.1 5.0 %collective-permute-start.4 = (bf16[64,1024]{1,0:T(8,128)(2,1)S(1)}, bf16[64,1024]{1,0:T(8,128)(2,1)S(1)}, u32[]{:S(2)}, u32[]{:S(2)}) collective-permute-start(bf16[64,1024]{1,0:T(8,128)(2,1)S(1)} %add_convert_fusion.8.own.refs_0_), channel_id=1, source_target_pairs={{0,4},{4,0},{8,12},{12,8},{1,5},{5,1},{9,13},{13,9},{2,6},{6,2},{1... | collective-permute-start | bytes 393224 | tf_op jit(solution)/shard_map/ppermute | solution.py:206
  30.0 3.1 %collective-permute-start.5 = (bf16[64,1024]{1,0:T(8,128)(2,1)S(1)}, bf16[64,1024]{1,0:T(8,128)(2,1)S(1)}, u32[]{:S(2)}, u32[]{:S(2)}) collective-permute-start(bf16[64,1024]{1,0:T(8,128)(2,1)S(1)} %get-tuple-element.200), channel_id=1, source_target_pairs={{0,1},{1,0},{2,3},{3,2},{4,5},{5,4},{6,7},{7,6},{8,9},{9,8},{10,11... | collective-permute-start | bytes 393224 | tf_op jit(solution)/shard_map/ppermute | solution.py:206
  30.8 9.6 %collective-permute-start.2 = (bf16[64,1024]{1,0:T(8,128)(2,1)S(1)}, bf16[64,1024]{1,0:T(8,128)(2,1)S(1)}, u32[]{:S(2)}, u32[]{:S(2)}) collective-permute-start(bf16[64,1024]{1,0:T(8,128)(2,1)S(1)} %get-tuple-element.393), channel_id=1, source_target_pairs={{0,8},{4,12},{8,0},{12,4},{1,9},{5,13},{9,1},{13,5},{2,10},{6,14},... | collective-permute-start | bytes 393224 | tf_op jit(solution)/shard_map/ppermute | solution.py:206
  33.2 7.3 %collective-permute-start.7 = (bf16[64,1024]{1,0:T(8,128)(2,1)S(1)}, bf16[64,1024]{1,0:T(8,128)(2,1)S(1)}, u32[]{:S(2)}, u32[]{:S(2)}) collective-permute-start(bf16[64,1024]{1,0:T(8,128)(2,1)S(1)} %get-tuple-element.391), channel_id=1, source_target_pairs={{0,2},{1,3},{2,0},{3,1},{4,6},{5,7},{6,4},{7,5},{8,10},{9,11},{10,... | collective-permute-start | bytes 393224 | tf_op jit(solution)/shard_map/ppermute | solution.py:206
  40.5 1.4 collective-permute-start.8
  40.6 5.9 %collective-permute-start.6 = (bf16[64,1024]{1,0:T(8,128)(2,1)S(1)}, bf16[64,1024]{1,0:T(8,128)(2,1)S(1)}, u32[]{:S(2)}, u32[]{:S(2)}) collective-permute-start(bf16[64,1024]{1,0:T(8,128)(2,1)S(1)} %add_convert_fusion.7.own.refs_2_), channel_id=1, source_target_pairs={{0,4},{4,0},{8,12},{12,8},{1,5},{5,1},{9,13},{13,9},{2,6},{6,2},{1... | collective-permute-start | bytes 393224 | tf_op jit(solution)/shard_map/ppermute | solution.py:206
  43.9 5.6 %collective-permute-start.10 = (bf16[64,1024]{1,0:T(8,128)(2,1)S(1)}, bf16[64,1024]{1,0:T(8,128)(2,1)S(1)}, u32[]{:S(2)}, u32[]{:S(2)}) collective-permute-start(bf16[64,1024]{1,0:T(8,128)(2,1)S(1)} %get-tuple-element.215), channel_id=1, source_target_pairs={{0,4},{4,0},{8,12},{12,8},{1,5},{5,1},{9,13},{13,9},{2,6},{6,2},{1... | collective-permute-start | bytes 393224 | tf_op jit(solution)/shard_map/ppermute | solution.py:206
  48.4 1.4 collective-permute-start.9
  49.9 5.8 %collective-permute-start.11 = (bf16[64,1024]{1,0:T(8,128)(2,1)S(1)}, bf16[64,1024]{1,0:T(8,128)(2,1)S(1)}, u32[]{:S(2)}, u32[]{:S(2)}) collective-permute-start(bf16[64,1024]{1,0:T(8,128)(2,1)S(1)} %get-tuple-element.387), channel_id=1, source_target_pairs={{0,2},{1,3},{2,0},{3,1},{4,6},{5,7},{6,4},{7,5},{8,10},{9,11},{10,... | collective-permute-start | bytes 393224 | tf_op jit(solution)/shard_map/ppermute | solution.py:206
  51.5 9.0 %collective-permute-start.13 = (bf16[64,1024]{1,0:T(8,128)(2,1)S(1)}, bf16[64,1024]{1,0:T(8,128)(2,1)S(1)}, u32[]{:S(2)}, u32[]{:S(2)}) collective-permute-start(bf16[64,1024]{1,0:T(8,128)(2,1)S(1)} %get-tuple-element.389), channel_id=1, source_target_pairs={{0,8},{4,12},{8,0},{12,4},{1,9},{5,13},{9,1},{13,5},{2,10},{6,14},... | collective-permute-start | bytes 393224 | tf_op jit(solution)/shard_map/ppermute | solution.py:206
  55.8 4.8 %collective-permute-start.12 = (bf16[64,1024]{1,0:T(8,128)(2,1)S(1)}, bf16[64,1024]{1,0:T(8,128)(2,1)S(1)}, u32[]{:S(2)}, u32[]{:S(2)}) collective-permute-start(bf16[64,1024]{1,0:T(8,128)(2,1)S(1)} %subtract_convert_fusion.6.own), channel_id=1, source_target_pairs={{0,1},{1,0},{2,3},{3,2},{4,5},{5,4},{6,7},{7,6},{8,9},{9,8},{10,11... | collective-permute-start | bytes 393224 | tf_op jit(solution)/shard_map/ppermute | solution.py:206
  60.5 5.7 %collective-permute-start.15 = (bf16[64,1024]{1,0:T(8,128)(2,1)S(1)}, bf16[64,1024]{1,0:T(8,128)(2,1)S(1)}, u32[]{:S(2)}, u32[]{:S(2)}) collective-permute-start(bf16[64,1024]{1,0:T(8,128)(2,1)S(1)} %add_convert_fusion.6.own.refs_0_.refs_4_), channel_id=1, source_target_pairs={{0,4},{4,0},{8,12},{12,8},{1,5},{5,1},{9,13},{13,9},{2,6},{6,2},{1... | collective-permute-start | bytes 393224 | tf_op jit(solution)/shard_map/ppermute | solution.py:206
  62.5 5.8 %collective-permute-start.14 = (bf16[64,1024]{1,0:T(8,128)(2,1)S(1)}, bf16[64,1024]{1,0:T(8,128)(2,1)S(1)}, u32[]{:S(2)}, u32[]{:S(2)}) collective-permute-start(bf16[64,1024]{1,0:T(8,128)(2,1)S(1)} %get-tuple-element.232), channel_id=1, source_target_pairs={{0,4},{4,0},{8,12},{12,8},{1,5},{5,1},{9,13},{13,9},{2,6},{6,2},{1... | collective-permute-start | bytes 393224 | tf_op jit(solution)/shard_map/ppermute | solution.py:206
  68.1 1.4 collective-permute-start.17
  69.6 5.6 %collective-permute-start.18 = (bf16[64,1024]{1,0:T(8,128)(2,1)S(1)}, bf16[64,1024]{1,0:T(8,128)(2,1)S(1)}, u32[]{:S(2)}, u32[]{:S(2)}) collective-permute-start(bf16[64,1024]{1,0:T(8,128)(2,1)S(1)} %get-tuple-element.383), channel_id=1, source_target_pairs={{0,2},{1,3},{2,0},{3,1},{4,6},{5,7},{6,4},{7,5},{8,10},{9,11},{10,... | collective-permute-start | bytes 393224 | tf_op jit(solution)/shard_map/ppermute | solution.py:206
  70.0 9.0 %collective-permute-start.16 = (bf16[64,1024]{1,0:T(8,128)(2,1)S(1)}, bf16[64,1024]{1,0:T(8,128)(2,1)S(1)}, u32[]{:S(2)}, u32[]{:S(2)}) collective-permute-start(bf16[64,1024]{1,0:T(8,128)(2,1)S(1)} %get-tuple-element.385), channel_id=1, source_target_pairs={{0,8},{4,12},{8,0},{12,4},{1,9},{5,13},{9,1},{13,5},{2,10},{6,14},... | collective-permute-start | bytes 393224 | tf_op jit(solution)/shard_map/ppermute | solution.py:206
  75.2 3.9 %collective-permute-start.20 = (bf16[64,1024]{1,0:T(8,128)(2,1)S(1)}, bf16[64,1024]{1,0:T(8,128)(2,1)S(1)}, u32[]{:S(2)}, u32[]{:S(2)}) collective-permute-start(bf16[64,1024]{1,0:T(8,128)(2,1)S(1)} %subtract_convert_fusion.5.own), channel_id=1, source_target_pairs={{0,1},{1,0},{2,3},{3,2},{4,5},{5,4},{6,7},{7,6},{8,9},{9,8},{10,11... | collective-permute-start | bytes 393224 | tf_op jit(solution)/shard_map/ppermute | solution.py:206
  79.0 6.0 %collective-permute-start.19 = (bf16[64,1024]{1,0:T(8,128)(2,1)S(1)}, bf16[64,1024]{1,0:T(8,128)(2,1)S(1)}, u32[]{:S(2)}, u32[]{:S(2)}) collective-permute-start(bf16[64,1024]{1,0:T(8,128)(2,1)S(1)} %add_convert_fusion.5.own.refs_2_.refs_6_), channel_id=1, source_target_pairs={{0,4},{4,0},{8,12},{12,8},{1,5},{5,1},{9,13},{13,9},{2,6},{6,2},{1... | collective-permute-start | bytes 393224 | tf_op jit(solution)/shard_map/ppermute | solution.py:206
  81.0 6.0 %collective-permute-start.22 = (bf16[64,1024]{1,0:T(8,128)(2,1)S(1)}, bf16[64,1024]{1,0:T(8,128)(2,1)S(1)}, u32[]{:S(2)}, u32[]{:S(2)}) collective-permute-start(bf16[64,1024]{1,0:T(8,128)(2,1)S(1)} %get-tuple-element.259), channel_id=1, source_target_pairs={{0,4},{4,0},{8,12},{12,8},{1,5},{5,1},{9,13},{13,9},{2,6},{6,2},{1... | collective-permute-start | bytes 393224 | tf_op jit(solution)/shard_map/ppermute | solution.py:206
  86.9 1.4 collective-permute-start.21
  88.3 5.8 %collective-permute-start.23 = (bf16[64,1024]{1,0:T(8,128)(2,1)S(1)}, bf16[64,1024]{1,0:T(8,128)(2,1)S(1)}, u32[]{:S(2)}, u32[]{:S(2)}) collective-permute-start(bf16[64,1024]{1,0:T(8,128)(2,1)S(1)} %get-tuple-element.379), channel_id=1, source_target_pairs={{0,2},{1,3},{2,0},{3,1},{4,6},{5,7},{6,4},{7,5},{8,10},{9,11},{10,... | collective-permute-start | bytes 393224 | tf_op jit(solution)/shard_map/ppermute | solution.py:206
  90.3 8.9 %collective-permute-start.25 = (bf16[64,1024]{1,0:T(8,128)(2,1)S(1)}, bf16[64,1024]{1,0:T(8,128)(2,1)S(1)}, u32[]{:S(2)}, u32[]{:S(2)}) collective-permute-start(bf16[64,1024]{1,0:T(8,128)(2,1)S(1)} %get-tuple-element.381), channel_id=1, source_target_pairs={{0,8},{4,12},{8,0},{12,4},{1,9},{5,13},{9,1},{13,5},{2,10},{6,14},... | collective-permute-start | bytes 393224 | tf_op jit(solution)/shard_map/ppermute | solution.py:206
  94.1 5.1 %collective-permute-start.24 = (bf16[64,1024]{1,0:T(8,128)(2,1)S(1)}, bf16[64,1024]{1,0:T(8,128)(2,1)S(1)}, u32[]{:S(2)}, u32[]{:S(2)}) collective-permute-start(bf16[64,1024]{1,0:T(8,128)(2,1)S(1)} %subtract_convert_fusion.4.own), channel_id=1, source_target_pairs={{0,1},{1,0},{2,3},{3,2},{4,5},{5,4},{6,7},{7,6},{8,9},{9,8},{10,11... | collective-permute-start | bytes 393224 | tf_op jit(solution)/shard_map/ppermute | solution.py:206
  99.2 6.3 %collective-permute-start.27 = (bf16[64,1024]{1,0:T(8,128)(2,1)S(1)}, bf16[64,1024]{1,0:T(8,128)(2,1)S(1)}, u32[]{:S(2)}, u32[]{:S(2)}) collective-permute-start(bf16[64,1024]{1,0:T(8,128)(2,1)S(1)} %add_convert_fusion.4.own.refs_0_), channel_id=1, source_target_pairs={{0,4},{4,0},{8,12},{12,8},{1,5},{5,1},{9,13},{13,9},{2,6},{6,2},{1... | collective-permute-start | bytes 393224 | tf_op jit(solution)/shard_map/ppermute | solution.py:206
  101.2 6.3 %collective-permute-start.26 = (bf16[64,1024]{1,0:T(8,128)(2,1)S(1)}, bf16[64,1024]{1,0:T(8,128)(2,1)S(1)}, u32[]{:S(2)}, u32[]{:S(2)}) collective-permute-start(bf16[64,1024]{1,0:T(8,128)(2,1)S(1)} %get-tuple-element.277), channel_id=1, source_target_pairs={{0,4},{4,0},{8,12},{12,8},{1,5},{5,1},{9,13},{13,9},{2,6},{6,2},{1... | collective-permute-start | bytes 393224 | tf_op jit(solution)/shard_map/ppermute | solution.py:206
  107.4 1.4 collective-permute-start.29
  108.8 5.6 %collective-permute-start.30 = (bf16[64,1024]{1,0:T(8,128)(2,1)S(1)}, bf16[64,1024]{1,0:T(8,128)(2,1)S(1)}, u32[]{:S(2)}, u32[]{:S(2)}) collective-permute-start(bf16[64,1024]{1,0:T(8,128)(2,1)S(1)} %get-tuple-element.375), channel_id=1, source_target_pairs={{0,2},{1,3},{2,0},{3,1},{4,6},{5,7},{6,4},{7,5},{8,10},{9,11},{10,... | collective-permute-start | bytes 393224 | tf_op jit(solution)/shard_map/ppermute | solution.py:206
  109.3 8.1 %collective-permute-start.28 = (bf16[64,1024]{1,0:T(8,128)(2,1)S(1)}, bf16[64,1024]{1,0:T(8,128)(2,1)S(1)}, u32[]{:S(2)}, u32[]{:S(2)}) collective-permute-start(bf16[64,1024]{1,0:T(8,128)(2,1)S(1)} %get-tuple-element.377), channel_id=1, source_target_pairs={{0,8},{4,12},{8,0},{12,4},{1,9},{5,13},{9,1},{13,5},{2,10},{6,14},... | collective-permute-start | bytes 393224 | tf_op jit(solution)/shard_map/ppermute | solution.py:206
  114.5 3.0 %collective-permute-start.32 = (bf16[64,1024]{1,0:T(8,128)(2,1)S(1)}, bf16[64,1024]{1,0:T(8,128)(2,1)S(1)}, u32[]{:S(2)}, u32[]{:S(2)}) collective-permute-start(bf16[64,1024]{1,0:T(8,128)(2,1)S(1)} %subtract_convert_fusion.3.own), channel_id=1, source_target_pairs={{0,1},{1,0},{2,3},{3,2},{4,5},{5,4},{6,7},{7,6},{8,9},{9,8},{10,11... | collective-permute-start | bytes 393224 | tf_op jit(solution)/shard_map/ppermute | solution.py:206
  117.4 6.3 %collective-permute-start.31 = (bf16[64,1024]{1,0:T(8,128)(2,1)S(1)}, bf16[64,1024]{1,0:T(8,128)(2,1)S(1)}, u32[]{:S(2)}, u32[]{:S(2)}) collective-permute-start(bf16[64,1024]{1,0:T(8,128)(2,1)S(1)} %add_convert_fusion.3.own.refs_2_), channel_id=1, source_target_pairs={{0,4},{4,0},{8,12},{12,8},{1,5},{5,1},{9,13},{13,9},{2,6},{6,2},{1... | collective-permute-start | bytes 393224 | tf_op jit(solution)/shard_map/ppermute | solution.py:206
  119.4 6.3 %collective-permute-start.34 = (bf16[64,1024]{1,0:T(8,128)(2,1)S(1)}, bf16[64,1024]{1,0:T(8,128)(2,1)S(1)}, u32[]{:S(2)}, u32[]{:S(2)}) collective-permute-start(bf16[64,1024]{1,0:T(8,128)(2,1)S(1)} %get-tuple-element.308), channel_id=1, source_target_pairs={{0,4},{4,0},{8,12},{12,8},{1,5},{5,1},{9,13},{13,9},{2,6},{6,2},{1... | collective-permute-start | bytes 393224 | tf_op jit(solution)/shard_map/ppermute | solution.py:206
  125.6 1.4 collective-permute-start.33
  127.1 5.6 %collective-permute-start.35 = (bf16[64,1024]{1,0:T(8,128)(2,1)S(1)}, bf16[64,1024]{1,0:T(8,128)(2,1)S(1)}, u32[]{:S(2)}, u32[]{:S(2)}) collective-permute-start(bf16[64,1024]{1,0:T(8,128)(2,1)S(1)} %get-tuple-element.371), channel_id=1, source_target_pairs={{0,2},{1,3},{2,0},{3,1},{4,6},{5,7},{6,4},{7,5},{8,10},{9,11},{10,... | collective-permute-start | bytes 393224 | tf_op jit(solution)/shard_map/ppermute | solution.py:206
  128.6 8.5 %collective-permute-start.37 = (bf16[64,1024]{1,0:T(8,128)(2,1)S(1)}, bf16[64,1024]{1,0:T(8,128)(2,1)S(1)}, u32[]{:S(2)}, u32[]{:S(2)}) collective-permute-start(bf16[64,1024]{1,0:T(8,128)(2,1)S(1)} %get-tuple-element.373), channel_id=1, source_target_pairs={{0,8},{4,12},{8,0},{12,4},{1,9},{5,13},{9,1},{13,5},{2,10},{6,14},... | collective-permute-start | bytes 393224 | tf_op jit(solution)/shard_map/ppermute | solution.py:206
  132.7 4.5 %collective-permute-start.36 = (bf16[64,1024]{1,0:T(8,128)(2,1)S(1)}, bf16[64,1024]{1,0:T(8,128)(2,1)S(1)}, u32[]{:S(2)}, u32[]{:S(2)}) collective-permute-start(bf16[64,1024]{1,0:T(8,128)(2,1)S(1)} %subtract_convert_fusion.2.own), channel_id=1, source_target_pairs={{0,1},{1,0},{2,3},{3,2},{4,5},{5,4},{6,7},{7,6},{8,9},{9,8},{10,11... | collective-permute-start | bytes 393224 | tf_op jit(solution)/shard_map/ppermute | solution.py:206
  137.2 8.2 %copy-start.8 = (bf16[64,1024]{1,0:T(8,128)(2,1)}, bf16[64,1024]{1,0:T(8,128)(2,1)S(1)}, u32[]{:S(2)}) copy-start(bf16[64,1024]{1,0:T(8,128)(2,1)S(1)} %add_convert_fusion.2.own) | copy-start | bytes 393220
  137.2 6.3 %collective-permute-start.39 = (bf16[64,1024]{1,0:T(8,128)(2,1)S(1)}, bf16[64,1024]{1,0:T(8,128)(2,1)S(1)}, u32[]{:S(2)}, u32[]{:S(2)}) collective-permute-start(bf16[64,1024]{1,0:T(8,128)(2,1)S(1)} %add_convert_fusion.2.own), channel_id=1, source_target_pairs={{0,4},{4,0},{8,12},{12,8},{1,5},{5,1},{9,13},{13,9},{2,6},{6,2},{1... | collective-permute-start | bytes 393224 | tf_op jit(solution)/shard_map/ppermute | solution.py:206
  139.2 6.3 %collective-permute-start.38 = (bf16[64,1024]{1,0:T(8,128)(2,1)S(1)}, bf16[64,1024]{1,0:T(8,128)(2,1)S(1)}, u32[]{:S(2)}, u32[]{:S(2)}) collective-permute-start(bf16[64,1024]{1,0:T(8,128)(2,1)S(1)} %get-tuple-element.326), channel_id=1, source_target_pairs={{0,4},{4,0},{8,12},{12,8},{1,5},{5,1},{9,13},{13,9},{2,6},{6,2},{1... | collective-permute-start | bytes 393224 | tf_op jit(solution)/shard_map/ppermute | solution.py:206
  145.4 1.4 collective-permute-start.41
  146.8 5.6 %collective-permute-start.42 = (bf16[64,1024]{1,0:T(8,128)(2,1)S(1)}, bf16[64,1024]{1,0:T(8,128)(2,1)S(1)}, u32[]{:S(2)}, u32[]{:S(2)}) collective-permute-start(bf16[64,1024]{1,0:T(8,128)(2,1)S(1)} %get-tuple-element.367), channel_id=1, source_target_pairs={{0,2},{1,3},{2,0},{3,1},{4,6},{5,7},{6,4},{7,5},{8,10},{9,11},{10,... | collective-permute-start | bytes 393224 | tf_op jit(solution)/shard_map/ppermute | solution.py:206
  147.3 8.1 %collective-permute-start.40 = (bf16[64,1024]{1,0:T(8,128)(2,1)S(1)}, bf16[64,1024]{1,0:T(8,128)(2,1)S(1)}, u32[]{:S(2)}, u32[]{:S(2)}) collective-permute-start(bf16[64,1024]{1,0:T(8,128)(2,1)S(1)} %get-tuple-element.369), channel_id=1, source_target_pairs={{0,8},{4,12},{8,0},{12,4},{1,9},{5,13},{9,1},{13,5},{2,10},{6,14},... | collective-permute-start | bytes 393224 | tf_op jit(solution)/shard_map/ppermute | solution.py:206
  152.5 3.6 %collective-permute-start.44 = (bf16[64,1024]{1,0:T(8,128)(2,1)S(1)}, bf16[64,1024]{1,0:T(8,128)(2,1)S(1)}, u32[]{:S(2)}, u32[]{:S(2)}) collective-permute-start(bf16[64,1024]{1,0:T(8,128)(2,1)S(1)} %subtract_convert_fusion.1), channel_id=1, source_target_pairs={{0,1},{1,0},{2,3},{3,2},{4,5},{5,4},{6,7},{7,6},{8,9},{9,8},{10,11... | collective-permute-start | bytes 393224 | tf_op jit(solution)/shard_map/ppermute | solution.py:206
  156.1 9.3 %collective-permute-start.43 = (bf16[64,1024]{1,0:T(8,128)(2,1)}, bf16[64,1024]{1,0:T(8,128)(2,1)}, u32[]{:S(2)}, u32[]{:S(2)}) collective-permute-start(bf16[64,1024]{1,0:T(8,128)(2,1)} %add_convert_fusion.1.own), channel_id=1, source_target_pairs={{0,4},{4,0},{8,12},{12,8},{1,5},{5,1},{9,13},{13,9},{2,6},{6,2},{1... | collective-permute-start | bytes 393224 | tf_op jit(solution)/shard_map/ppermute | solution.py:206
  160.1 25.2 %slice-start.3 = ((s8[10485760]{0:T(1024)(128)(4,1)}), s8[2097152]{0:T(1024)(128)(4,1)S(1)}, s32[]{:S(2)}) async-start(s8[10485760]{0:T(1024)(128)(4,1)} %bitcast.41), calls=%async_computation.3 | async-start | bytes 4194304
  163.4 13.4 %collective-permute-start.45 = (bf16[64,1024]{1,0:T(8,128)(2,1)}, bf16[64,1024]{1,0:T(8,128)(2,1)}, u32[]{:S(2)}, u32[]{:S(2)}) collective-permute-start(bf16[64,1024]{1,0:T(8,128)(2,1)} %get-tuple-element.344), channel_id=1, source_target_pairs={{0,4},{4,0},{8,12},{12,8},{1,5},{5,1},{9,13},{13,9},{2,6},{6,2},{1... | collective-permute-start | bytes 393224 | tf_op jit(solution)/shard_map/ppermute | solution.py:206
  173.4 10.4 %copy-start.14 = (bf16[64,1024]{1,0:T(8,128)(2,1)S(1)}, bf16[64,1024]{1,0:T(8,128)(2,1)}, u32[]{:S(2)}) copy-start(bf16[64,1024]{1,0:T(8,128)(2,1)} %get-tuple-element.354) | copy-start | bytes 393220
  173.4 11.9 %slice-start.4 = ((s8[10485760]{0:T(1024)(128)(4,1)}), s8[4194304]{0:T(1024)(128)(4,1)S(1)}, s32[]{:S(2)}) async-start(s8[10485760]{0:T(1024)(128)(4,1)} %bitcast.41), calls=%async_computation.4 | async-start | bytes 8388608
  173.4 11.9 %slice-start.5 = ((s8[10485760]{0:T(1024)(128)(4,1)}), s8[4194304]{0:T(1024)(128)(4,1)S(1)}, s32[]{:S(2)}) async-start(s8[10485760]{0:T(1024)(128)(4,1)} %bitcast.41), calls=%async_computation.5 | async-start | bytes 8388608
  176.7 10.6 %copy-start.7 = (bf16[64,1024]{1,0:T(8,128)(2,1)S(1)}, bf16[64,1024]{1,0:T(8,128)(2,1)}, u32[]{:S(2)}) copy-start(bf16[64,1024]{1,0:T(8,128)(2,1)} %copy-done.6) | copy-start | bytes 393220
  176.7 17.2 %copy-start.9 = (bf16[64,1024]{1,0:T(8,128)(2,1)S(1)}, bf16[64,1024]{1,0:T(8,128)(2,1)}, u32[]{:S(2)}) copy-start(bf16[64,1024]{1,0:T(8,128)(2,1)} %copy-done.8) | copy-start | bytes 393220
  176.7 17.2 %copy-start.13 = (bf16[64,1024]{1,0:T(8,128)(2,1)S(1)}, bf16[64,1024]{1,0:T(8,128)(2,1)}, u32[]{:S(2)}) copy-start(bf16[64,1024]{1,0:T(8,128)(2,1)} %copy-done.12) | copy-start | bytes 393220
  176.7 1.4 collective-permute-start.46
  178.2 5.6 %collective-permute-start.47 = (bf16[64,1024]{1,0:T(8,128)(2,1)S(1)}, bf16[64,1024]{1,0:T(8,128)(2,1)S(1)}, u32[]{:S(2)}, u32[]{:S(2)}) collective-permute-start(bf16[64,1024]{1,0:T(8,128)(2,1)S(1)} %get-tuple-element.365), channel_id=1, source_target_pairs={{0,2},{1,3},{2,0},{3,1},{4,6},{5,7},{6,4},{7,5},{8,10},{9,11},{10,... | collective-permute-start | bytes 393224 | tf_op jit(solution)/shard_map/ppermute | solution.py:206
  183.9 1.4 collective-permute-start.48
  187.3 5.6 %collective-permute-start.49 = (bf16[64,1024]{1,0:T(8,128)(2,1)S(1)}, bf16[64,1024]{1,0:T(8,128)(2,1)S(1)}, u32[]{:S(2)}, u32[]{:S(2)}) collective-permute-start(bf16[64,1024]{1,0:T(8,128)(2,1)S(1)} %get-tuple-element.360), channel_id=1, source_target_pairs={{0,4},{4,0},{8,12},{12,8},{1,5},{5,1},{9,13},{13,9},{2,6},{6,2},{1... | collective-permute-start | bytes 393224 | tf_op jit(solution)/shard_map/ppermute | solution.py:206
  192.9 8.5 %collective-permute-start.50 = (bf16[64,1024]{1,0:T(8,128)(2,1)S(1)}, bf16[64,1024]{1,0:T(8,128)(2,1)S(1)}, u32[]{:S(2)}, u32[]{:S(2)}) collective-permute-start(bf16[64,1024]{1,0:T(8,128)(2,1)S(1)} %broadcast_select_fusion.4), channel_id=1, source_target_pairs={{0,8},{4,12},{8,0},{12,4},{1,9},{5,13},{9,1},{13,5},{2,10},{6,14},... | collective-permute-start | bytes 393224 | tf_op jit(solution)/shard_map/ppermute | solution.py:206
  194.0 7.4 %copy-start.15 = (bf16[5,1024,64]{1,2,0:T(8,128)(2,1)}, bf16[5,1024,64]{1,2,0:T(8,128)(2,1)S(1)}, u32[]{:S(2)}) copy-start(bf16[5,1024,64]{1,2,0:T(8,128)(2,1)S(1)} %bitcast_dynamic-update-slice_fusion) | copy-start | bytes 1966084
  (9 other events, 29.0 us)

commit v4 on v2

v4 whole, which is shorter than its diff:
```python
import functools

import jax
import jax.numpy as jnp
from jax import lax
from jax.experimental import pallas as pl
from jax.experimental.pallas import tpu as pltpu
from jax.sharding import PartitionSpec as P

STREAMS = 2
UNITS = 2 * STREAMS


def pair_index(block_row, column_index):
    return block_row * (block_row - 1) // 2 + column_index


VMEM = pl.BlockSpec(memory_space=pltpu.VMEM)
SMEM = pl.BlockSpec(memory_space=pltpu.SMEM)
COST = pl.CostEstimate(flops=1, bytes_accessed=1, transcendentals=0)


def params():
    return pltpu.CompilerParams(vmem_limit_bytes=16 * 2**20)


def times_transposed(left, right):
    return lax.dot_general(left, right, (((1,), (1,)), ((), ())), preferred_element_type=jnp.float32)


TILE = 256


def product_kernel(count, block, *refs):
    units, rest, out = refs[:count], refs[count:-1], refs[-1]
    x = units[0][...] if count == 1 else jnp.concatenate([u[...] for u in units], axis=0)
    rows = block.shape[0]
    tile = min(rows, TILE)
    for t in range(rows // tile):
        cut = pl.ds(t * tile, tile)
        value = times_transposed(block[cut], x).T
        for r in rest:
            value = value + r[:, cut]
        out[:, cut] = value.astype(out.dtype)


def product(block, units, rest=(), kind=jnp.float32):
    angles = sum(u.shape[0] for u in units)
    return pl.pallas_call(
        functools.partial(product_kernel, len(units)),
        out_shape=jax.ShapeDtypeStruct((angles, block.shape[0]), kind),
        in_specs=[VMEM] * (1 + len(units) + len(rest)),
        out_specs=VMEM,
        compiler_params=params(),
        cost_estimate=COST,
    )(block, *units, *rest)


def first_kernel(s, side, right, block, keep, leave, product):
    width = keep.shape[0]
    x = right[:, pl.ds(2 * s * width, 2 * width)].T
    product[...] = times_transposed(x, block[...])
    own = pl.multiple_of(side[0] * width, width)
    other = pl.multiple_of((1 - side[0]) * width, width)
    leave[...] = product[pl.ds(own, width)].astype(jnp.bfloat16)
    keep[...] = product[pl.ds(other, width)]


def first_products(s, side, right, block):
    rows = block.shape[0]
    width = right.shape[1] // UNITS
    return pl.pallas_call(
        functools.partial(first_kernel, s),
        out_shape=(
            jax.ShapeDtypeStruct((width, rows), jnp.float32),
            jax.ShapeDtypeStruct((width, rows), jnp.bfloat16),
        ),
        in_specs=[SMEM, VMEM, VMEM],
        out_specs=(VMEM, VMEM),
        scratch_shapes=[pltpu.VMEM((2 * width, rows), jnp.float32)],
        compiler_params=params(),
        cost_estimate=COST,
    )(side, right, block)


def turn_kernel(width, side, sides, out, turned):
    turned[...] = sides[0].T
    for s in range(STREAMS):
        own = pl.multiple_of((2 * s + side[0]) * width, width)
        out[0, s] = turned[pl.ds(own, width)]


def turned_sides(side, sides):
    steps, rows, angles = sides.shape
    width = angles // UNITS
    return pl.pallas_call(
        functools.partial(turn_kernel, width),
        grid=(steps - 1,),
        out_shape=jax.ShapeDtypeStruct((steps - 1, STREAMS, width, rows), jnp.bfloat16),
        in_specs=[SMEM, pl.BlockSpec((1, rows, angles), lambda i: (i + 1, 0, 0))],
        out_specs=pl.BlockSpec((1, STREAMS, width, rows), lambda i: (i, 0, 0, 0)),
        scratch_shapes=[pltpu.VMEM((angles, rows), jnp.bfloat16)],
        compiler_params=params(),
        cost_estimate=COST,
    )(side, sides)


def wide(value):
    return value.astype(jnp.float32)


def narrow(value):
    return value.astype(jnp.bfloat16)


class Order:
    def __init__(self):
        self.last = None

    def run(self, work, *values):
        if self.last is not None:
            *values, _ = lax.optimization_barrier((*values, self.last))
        result = work(*values)
        self.last = result[0] if isinstance(result, (tuple, list)) else result
        return result

    def block(self, blocks, index):
        self.last = lax.optimization_barrier(self.run(lambda v: v[index], blocks))
        return self.last


def make_per_device(n_row, n_col):
    def trade(value, axis, step):
        size = n_row if axis == "row" else n_col
        return lax.ppermute(value, axis, [(i, i ^ step) for i in range(size)])

    def more_rounds(value, axis):
        size = n_row if axis == "row" else n_col
        step = 4
        while step < size:
            value = value + wide(trade(narrow(value), axis, step))
            step *= 2
        return value

    def per_device(factor_blocks, inverse_blocks, right_sides):
        steps_total, group_rows, angles = right_sides.shape
        last_step = steps_total - 1
        place = lax.axis_index("row")
        core = lax.axis_index("col") & 1
        side = (place & 1) ^ core
        side_ref = side.astype(jnp.int32).reshape(1)
        width = angles // UNITS
        exact = n_row == UNITS
        order = Order()
        solved = [[None] * STREAMS for _ in range(steps_total)]
        state = [dict() for _ in range(STREAMS)]
        sums = [None] * (steps_total + 1)
        factors = [None] * steps_total
        inverses = [None] * steps_total

        def load_factor(step):
            if step < steps_total:
                factors[step] = order.block(factor_blocks, pair_index(step, step - 1))

        def load_inverse(step):
            if step < steps_total:
                inverses[step] = order.block(inverse_blocks, step)

        def older(step, blocks):
            if step >= steps_total:
                return
            for j in blocks:
                block = order.block(factor_blocks, pair_index(step, j))
                units = [u for s in range(STREAMS) for u in solved[j][s]]

                rest = [] if sums[step] is None else [sums[step]]
                sums[step] = order.run(
                    lambda block, *v: product(block, v[: len(units)], v[len(units) :]), block, *units, *rest
                )

        def older_part(s, step, u):
            first = (2 * s + u) * width
            return [] if sums[step] is None else [sums[step][first : first + width]]

        def factor_other(s, step):
            st = state[s]
            leaving = order.run(
                lambda block, x, *rest: product(block, [x], rest, jnp.bfloat16),
                factors[step],
                solved[step - 1][s][1],
                *older_part(s, step, 1),
            )
            st["swap"] = trade(leaving, "col", 1)

        def factor_own(s, step):
            state[s]["sum"] = order.run(
                lambda block, x, *rest: product(block, [x], rest),
                factors[step],
                solved[step - 1][s][0],
                *older_part(s, step, 0),
            )

        def chip_sum(s):
            def work(value, arrived):
                value = value + wide(arrived)
                return narrow(value), value

            st = state[s]
            leaving, st["sum"] = order.run(work, st["sum"], st["swap"])
            st["flight"] = trade(leaving, "col", 2) if n_col > 2 else None

        def residual(s, step):
            def work(side_values, value, *arrived):
                for a in arrived:
                    value = more_rounds(value + wide(a), "col")
                return narrow(wide(side_values) - value)

            st = state[s]
            arrived = [] if st["flight"] is None else [st["flight"]]
            st["own"] = order.run(work, base[step - 1, s], st["sum"], *arrived)
            st["swap"] = trade(st["own"], "col", 1)

        def inverse_own(s, step):
            st = state[s]
            if exact and step == last_step:
                own, other = st["own"], st["swap"]
                st["own"], st["swap"] = jnp.where(core == 0, other, own), jnp.where(core == 0, own, other)
            leaving = order.run(
                lambda block, x: product(block, [x], kind=jnp.bfloat16), inverses[step], st["own"]
            )
            st["flight"] = trade(leaving, "row", 1)

        def inverse_other(s, step):
            st = state[s]
            st["total"] = order.run(lambda block, x: product(block, [x]), inverses[step], st["swap"])

        def pair_sum(s):
            def work(value, arrived):
                value = value + wide(arrived)
                return narrow(value), value

            st = state[s]
            st["leaving"], st["total"] = order.run(work, st["total"], st["flight"])

        def cross(s):
            st = state[s]
            st["flight"] = trade(st["leaving"], "row", 2) if n_row > 2 else None

        def solve(s, step):
            def work(value, *arrived):
                for a in arrived:
                    value = more_rounds(value + wide(a), "row")
                return narrow(value)

            st = state[s]
            arrived = [] if st["flight"] is None else [st["flight"]]
            other = order.run(work, st["total"], *arrived)
            solved[step][s] = (trade(other, "row", 1), other)

        inverses[0] = order.block(inverse_blocks, 0)
        right = order.block(right_sides, 0)
        for s in range(STREAMS):
            state[s]["total"], leaving = order.run(
                lambda v, w: first_products(s, side_ref, v, w), right, inverses[0]
            )
            state[s]["flight"] = trade(leaving, "row", 1)
        if steps_total > 1:
            base = order.run(lambda v: turned_sides(side_ref, v), right_sides)
        for s in range(STREAMS):
            pair_sum(s)
            cross(s)
        load_factor(1)
        load_inverse(1)

        for step in range(1, steps_total):
            for s in range(STREAMS):
                solve(s, step - 1)
                factor_other(s, step)
            factor_own(0, step)
            chip_sum(0)
            older(step + 1, range(step - 1))
            factor_own(1, step)
            chip_sum(1)
            for s in range(STREAMS):
                residual(s, step)
                inverse_own(s, step)
            for s in range(STREAMS):
                inverse_other(s, step)
                if s == STREAMS - 1:
                    load_inverse(step + 1)
                pair_sum(s)
                if not (exact and step == last_step):
                    cross(s)
            older(step + 1, [step - 1])
            load_factor(step + 1)

        outputs = []
        for step in range(steps_total):
            if exact and step == last_step:
                low = place < n_row // 2
                leaving = order.run(
                    lambda a, b: jnp.where(low, b, a), state[0]["leaving"], state[1]["leaving"]
                )
                arrived = trade(leaving, "row", 2)
                found = narrow(jnp.where(low, state[0]["total"], state[1]["total"]) + wide(arrived))
                outputs.append(found.T)
                continue
            if step == last_step:
                for s in range(STREAMS):
                    solve(s, step)
            unit = place * UNITS // n_row
            found = solved[step][0][0]
            for s in range(STREAMS):
                for u in range(2):
                    found = jnp.where(unit == 2 * s + (u ^ side), solved[step][s][u], found)
            if not exact:
                slot = angles // n_row
                found = lax.dynamic_slice_in_dim(found, (place * slot) % width, slot, 0)
            outputs.append(found.T)
        return jnp.stack(outputs, axis=0)

    return per_device


def solution(mesh):
    placed = (P("groups", "row", "col"), P("groups", "col", "row"), P("groups", "row", None))
    return jax.shard_map(
        make_per_device(mesh.shape["row"], mesh.shape["col"]),
        mesh=mesh,
        in_specs=placed,
        out_specs=P("groups", "col", "row"),
        check_vma=False,
    )
```

time: 212 us -> 154 us (0.73)
  matrix products: 108 us -> 0 us
  waiting for transfers between devices: 35.4 us -> 69.3 us
  Pallas kernels: 0 us -> 32.4 us
  other arithmetic: 12.2 us -> 2.29 us
  starting transfers between devices: 46.9 us -> 37.5 us
  local copies, waits for them, and re-layouts: 6.74 us -> 10.9 us
    dot_general x46 -> x0, matrix products: 108 us -> none  [times_transposed(): lax.dot_general(left, right, (((1,), (1,)), ((), ())), preferred_element_...]
    ppermute x51, waiting for transfers between devices: 35.4 us -> 69.3 us  [trade(): return lax.ppermute(value, axis, [(i, i ^ step) for i in range(size)])]
    pallas_call x0 -> x41, Pallas kernels: none -> 32.4 us  [the longest x38 29.8 us: product(): pl.pallas_call(functools.partial(product_kernel, len(units)), out_shape=j...]
    ppermute x51, starting transfers between devices: 46.9 us -> 37.5 us  [trade(): return lax.ppermute(value, axis, [(i, i ^ step) for i in range(size)])]
    convert_element_type x34, other arithmetic: 7.81 us -> 1.19 us  [narrow(): return value.astype(jnp.bfloat16)]
    squeeze x5 -> x17, local copies, waits for them, and re-layouts: 2.58 us -> 8.83 us  [the longest x16 8.76 us: block(): self.last = lax.optimization_barrier(self.run(lambda v: v[index], blocks))]
    unnamed x5 -> x6, other arithmetic: 2.92 us -> 0.29 us
    slice x9 -> x3, local copies, waits for them, and re-layouts: 2.43 us -> 0.28 us  [older_part(): return [] if sums[step] is None else [sums[step][first:first + width]]]
  transfers between devices with their start and end apart: 51 -> 51, of which waited for: 15 -> 32; matrix products, arithmetic and copies ran while one was open for 57% -> 5% of each run, Pallas kernels for 0% -> 21%
where the time goes in v4:
time: 154 us; the launch traced here: 153 us
  waiting for transfers between devices  69.3 us (45%)
  starting transfers between devices  37.5 us (24%)
  Pallas kernels  32.4 us (21%)
  local copies, waits for them, and re-layouts  10.9 us (7%)
  other arithmetic  2.29 us (1%)
    ppermute x51, waiting for transfers between devices, trade(): return lax.ppermute(value, axis, [(i, i ^ step) for i in range(size)])  69.3 us
    ppermute x51, starting transfers between devices, trade(): return lax.ppermute(value, axis, [(i, i ^ step) for i in range(size)])  37.5 us
    pallas_call x38, Pallas kernels, product(): pl.pallas_call(functools.partial(product_kernel, len(units)), out_shape=j...  29.8 us
    squeeze x16, local copies, waits for them, and re-layouts, block(): self.last = lax.optimization_barrier(self.run(lambda v: v[index], blocks))  8.76 us
  transfers between devices with their start and end apart: 51, of which 32 were waited for; matrix products, arithmetic and copies ran while one was open for 5% of the time, Pallas kernels for 21%

profile of v4, /device:TPU:0, one launch (start us, length us, event | category | flops | bytes accessed | tf_op | source)
XLA Modules:
  0.0 153.4 jit_solution(3764191130280024084)
XLA Ops:
  0.0 1.8 %slice_bitcast_fusion.14.block = bf16[1024,1024]{1,0:T(8,128)(2,1)S(1)} fusion(bf16[5,1024,1024]{2,1,0:T(8,128)(2,1)} %param.4), kind=kLoop, calls=%fused_computation.14 | loop fusion | bytes 4194304 | tf_op jit(solution)/shard_map/squeeze | solution.py:128
  1.8 1.1 slice_bitcast_fusion.15.right
  2.9 0.9 shard_map.37
  3.7 3.1 %collective-permute-start.1 = (bf16[64,1024]{1,0:T(8,128)(2,1)S(1)}, bf16[64,1024]{1,0:T(8,128)(2,1)S(1)}, u32[]{:S(2)}, u32[]{:S(2)}) collective-permute-start(bf16[64,1024]{1,0:T(8,128)(2,1)S(1)} %get-tuple-element.224), channel_id=1, source_target_pairs={{0,4},{4,0},{8,12},{12,8},{1,5},{5,1},{9,13},{13,9},{2,6},{6,2},{1... | collective-permute-start | bytes 393224 | tf_op jit(solution)/shard_map/ppermute | solution.py:135
  6.8 0.8 shard_map.38
  7.8 1.7 %copy-done = bf16[5,1024,256]{2,1,0:T(8,128)(2,1)S(1)} copy-done((bf16[5,1024,256]{2,1,0:T(8,128)(2,1)S(1)}, bf16[5,1024,256]{2,1,0:T(8,128)(2,1)}, u32[]{:S(2)}) %copy-start) | copy-done | bytes 2621464
  9.5 0.9 shard_map.39
  10.7 3.0 %collective-permute-start.3 = (bf16[64,1024]{1,0:T(8,128)(2,1)S(1)}, bf16[64,1024]{1,0:T(8,128)(2,1)S(1)}, u32[]{:S(2)}, u32[]{:S(2)}) collective-permute-start(bf16[64,1024]{1,0:T(8,128)(2,1)S(1)} %get-tuple-element.457), channel_id=1, source_target_pairs={{0,8},{4,12},{8,0},{12,4},{1,9},{5,13},{9,1},{13,5},{2,10},{6,14},... | collective-permute-start | bytes 393224 | tf_op jit(solution)/shard_map/ppermute | solution.py:135
  13.8 2.6 %collective-permute-start.2 = (bf16[64,1024]{1,0:T(8,128)(2,1)S(1)}, bf16[64,1024]{1,0:T(8,128)(2,1)S(1)}, u32[]{:S(2)}, u32[]{:S(2)}) collective-permute-start(bf16[64,1024]{1,0:T(8,128)(2,1)S(1)} %get-tuple-element.455), channel_id=1, source_target_pairs={{0,8},{4,12},{8,0},{12,4},{1,9},{5,13},{9,1},{13,5},{2,10},{6,14},... | collective-permute-start | bytes 393224 | tf_op jit(solution)/shard_map/ppermute | solution.py:135
  16.4 1.9 %slice_bitcast_fusion.13.block = bf16[1024,1024]{1,0:T(8,128)(2,1)S(1)} fusion(bf16[10,1024,1024]{2,1,0:T(8,128)(2,1)} %param.3), kind=kLoop, calls=%fused_computation.13 | loop fusion | bytes 4194304 | tf_op jit(solution)/shard_map/squeeze | solution.py:128
  18.3 1.9 %slice_bitcast_fusion.12.block = bf16[1024,1024]{1,0:T(8,128)(2,1)S(1)} fusion(bf16[5,1024,1024]{2,1,0:T(8,128)(2,1)} %param.4), kind=kLoop, calls=%fused_computation.12 | loop fusion | bytes 4194304 | tf_op jit(solution)/shard_map/squeeze | solution.py:128
  20.2 3.2 %collective-permute-done.3 = bf16[64,1024]{1,0:T(8,128)(2,1)S(1)} collective-permute-done((bf16[64,1024]{1,0:T(8,128)(2,1)S(1)}, bf16[64,1024]{1,0:T(8,128)(2,1)S(1)}, u32[]{:S(2)}, u32[]{:S(2)}) %collective-permute-start.3) | collective-permute-done | bytes 131104 | tf_op jit(solution)/shard_map/ppermute | solution.py:135
  24.3 0.8 collective-permute-done.2
  25.1 1.3 collective-permute-start.4
  27.5 1.7 %collective-permute-done.5.refs_0_ = bf16[64,1024]{1,0:T(8,128)(2,1)S(1)} collective-permute-done((bf16[64,1024]{1,0:T(8,128)(2,1)S(1)}, bf16[64,1024]{1,0:T(8,128)(2,1)S(1)}, u32[]{:S(2)}, u32[]{:S(2)}) %collective-permute-start.5) | collective-permute-done | bytes 131104 | tf_op jit(solution)/shard_map/ppermute | solution.py:135
  30.0 1.7 %collective-permute-start.9 = (bf16[64,1024]{1,0:T(8,128)(2,1)S(1)}, bf16[64,1024]{1,0:T(8,128)(2,1)S(1)}, u32[]{:S(2)}, u32[]{:S(2)}) collective-permute-start(bf16[64,1024]{1,0:T(8,128)(2,1)S(1)} %get-tuple-element.453), channel_id=1, source_target_pairs={{0,2},{1,3},{2,0},{3,1},{4,6},{5,7},{6,4},{7,5},{8,10},{9,11},{10,... | collective-permute-start | bytes 393224 | tf_op jit(solution)/shard_map/ppermute | solution.py:135
  32.5 1.3 collective-permute-start.8
  33.9 2.0 %collective-permute-done.9 = bf16[64,1024]{1,0:T(8,128)(2,1)S(1)} collective-permute-done((bf16[64,1024]{1,0:T(8,128)(2,1)S(1)}, bf16[64,1024]{1,0:T(8,128)(2,1)S(1)}, u32[]{:S(2)}, u32[]{:S(2)}) %collective-permute-start.9) | collective-permute-done | bytes 131104 | tf_op jit(solution)/shard_map/ppermute | solution.py:135
  36.9 0.9 collective-permute-done.8
  38.7 1.4 collective-permute-start.13
  40.8 2.3 %collective-permute-done.12 = bf16[64,1024]{1,0:T(8,128)(2,1)S(1)} collective-permute-done((bf16[64,1024]{1,0:T(8,128)(2,1)S(1)}, bf16[64,1024]{1,0:T(8,128)(2,1)S(1)}, u32[]{:S(2)}, u32[]{:S(2)}) %collective-permute-start.12) | collective-permute-done | bytes 131104 | tf_op jit(solution)/shard_map/ppermute | solution.py:135
  43.2 1.1 collective-permute-start.15
  45.6 1.7 %collective-permute-start.14 = (bf16[64,1024]{1,0:T(8,128)(2,1)S(1)}, bf16[64,1024]{1,0:T(8,128)(2,1)S(1)}, u32[]{:S(2)}, u32[]{:S(2)}) collective-permute-start(bf16[64,1024]{1,0:T(8,128)(2,1)S(1)} %get-tuple-element.447), channel_id=1, source_target_pairs={{0,8},{4,12},{8,0},{12,4},{1,9},{5,13},{9,1},{13,5},{2,10},{6,14},... | collective-permute-start | bytes 393224 | tf_op jit(solution)/shard_map/ppermute | solution.py:135
  47.5 0.9 shard_map.48
  48.7 6.3 %collective-permute-done.15 = bf16[64,1024]{1,0:T(8,128)(2,1)S(1)} collective-permute-done((bf16[64,1024]{1,0:T(8,128)(2,1)S(1)}, bf16[64,1024]{1,0:T(8,128)(2,1)S(1)}, u32[]{:S(2)}, u32[]{:S(2)}) %collective-permute-start.15) | collective-permute-done | bytes 131104 | tf_op jit(solution)/shard_map/ppermute | solution.py:135
  55.9 1.4 collective-permute-done.14
  59.1 1.5 collective-permute-done.17.refs_0_
  61.4 1.5 collective-permute-start.21
  63.0 0.9 shard_map.52.refs_4_
  65.5 1.4 collective-permute-done.21
  68.1 1.7 %collective-permute-done.20 = bf16[64,1024]{1,0:T(8,128)(2,1)S(1)} collective-permute-done((bf16[64,1024]{1,0:T(8,128)(2,1)S(1)}, bf16[64,1024]{1,0:T(8,128)(2,1)S(1)}, u32[]{:S(2)}, u32[]{:S(2)}) %collective-permute-start.20) | collective-permute-done | bytes 131104 | tf_op jit(solution)/shard_map/ppermute | solution.py:135
  72.2 1.5 collective-permute-done.24
  73.7 1.3 collective-permute-start.27
  75.0 0.9 shard_map.57
  76.7 2.0 %collective-permute-start.26 = (bf16[64,1024]{1,0:T(8,128)(2,1)S(1)}, bf16[64,1024]{1,0:T(8,128)(2,1)S(1)}, u32[]{:S(2)}, u32[]{:S(2)}) collective-permute-start(bf16[64,1024]{1,0:T(8,128)(2,1)S(1)} %get-tuple-element.439), channel_id=1, source_target_pairs={{0,8},{4,12},{8,0},{12,4},{1,9},{5,13},{9,1},{13,5},{2,10},{6,14},... | collective-permute-start | bytes 393224 | tf_op jit(solution)/shard_map/ppermute | solution.py:135
  78.8 0.9 shard_map.58
  80.0 6.1 %collective-permute-done.27 = bf16[64,1024]{1,0:T(8,128)(2,1)S(1)} collective-permute-done((bf16[64,1024]{1,0:T(8,128)(2,1)S(1)}, bf16[64,1024]{1,0:T(8,128)(2,1)S(1)}, u32[]{:S(2)}, u32[]{:S(2)}) %collective-permute-start.27) | collective-permute-done | bytes 131104 | tf_op jit(solution)/shard_map/ppermute | solution.py:135
  87.1 1.2 collective-permute-done.26
  88.3 0.9 collective-permute-start.28
  89.2 0.8 shard_map.60
  90.2 1.6 %collective-permute-done.29.refs_0_ = bf16[64,1024]{1,0:T(8,128)(2,1)S(1)} collective-permute-done((bf16[64,1024]{1,0:T(8,128)(2,1)S(1)}, bf16[64,1024]{1,0:T(8,128)(2,1)S(1)}, u32[]{:S(2)}, u32[]{:S(2)}) %collective-permute-start.29) | collective-permute-done | bytes 131104 | tf_op jit(solution)/shard_map/ppermute | solution.py:135
  92.7 1.4 collective-permute-start.33
  94.3 0.9 shard_map.62.refs_4_
  95.4 0.9 shard_map.63.refs_4_
  99.0 3.1 %collective-permute-done.32 = bf16[64,1024]{1,0:T(8,128)(2,1)S(1)} collective-permute-done((bf16[64,1024]{1,0:T(8,128)(2,1)S(1)}, bf16[64,1024]{1,0:T(8,128)(2,1)S(1)}, u32[]{:S(2)}, u32[]{:S(2)}) %collective-permute-start.32) | collective-permute-done | bytes 131104 | tf_op jit(solution)/shard_map/ppermute | solution.py:135
  104.7 1.8 %collective-permute-start.39 = (bf16[64,1024]{1,0:T(8,128)(2,1)S(1)}, bf16[64,1024]{1,0:T(8,128)(2,1)S(1)}, u32[]{:S(2)}, u32[]{:S(2)}) collective-permute-start(bf16[64,1024]{1,0:T(8,128)(2,1)S(1)} %get-tuple-element.433), channel_id=1, source_target_pairs={{0,8},{4,12},{8,0},{12,4},{1,9},{5,13},{9,1},{13,5},{2,10},{6,14},... | collective-permute-start | bytes 393224 | tf_op jit(solution)/shard_map/ppermute | solution.py:135
  107.5 2.8 %collective-permute-done.37 = bf16[64,1024]{1,0:T(8,128)(2,1)S(1)} collective-permute-done((bf16[64,1024]{1,0:T(8,128)(2,1)S(1)}, bf16[64,1024]{1,0:T(8,128)(2,1)S(1)}, u32[]{:S(2)}, u32[]{:S(2)}) %collective-permute-start.37) | collective-permute-done | bytes 131104 | tf_op jit(solution)/shard_map/ppermute | solution.py:135
  110.6 0.9 shard_map.69
  111.7 5.5 %collective-permute-done.39 = bf16[64,1024]{1,0:T(8,128)(2,1)S(1)} collective-permute-done((bf16[64,1024]{1,0:T(8,128)(2,1)S(1)}, bf16[64,1024]{1,0:T(8,128)(2,1)S(1)}, u32[]{:S(2)}, u32[]{:S(2)}) %collective-permute-start.39) | collective-permute-done | bytes 131104 | tf_op jit(solution)/shard_map/ppermute | solution.py:135
  117.3 0.8 shard_map.70
  118.2 1.2 collective-permute-done.38
  119.4 0.9 collective-permute-start.40
  121.3 1.6 %collective-permute-done.41.refs_0_ = bf16[64,1024]{1,0:T(8,128)(2,1)S(1)} collective-permute-done((bf16[64,1024]{1,0:T(8,128)(2,1)S(1)}, bf16[64,1024]{1,0:T(8,128)(2,1)S(1)}, u32[]{:S(2)}, u32[]{:S(2)}) %collective-permute-start.41) | collective-permute-done | bytes 131104 | tf_op jit(solution)/shard_map/ppermute | solution.py:135
  123.7 1.1 collective-permute-start.43
  125.1 1.0 shard_map.73
  126.1 2.7 %collective-permute-done.43 = bf16[64,1024]{1,0:T(8,128)(2,1)S(1)} collective-permute-done((bf16[64,1024]{1,0:T(8,128)(2,1)S(1)}, bf16[64,1024]{1,0:T(8,128)(2,1)S(1)}, u32[]{:S(2)}, u32[]{:S(2)}) %collective-permute-start.43) | collective-permute-done | bytes 131104 | tf_op jit(solution)/shard_map/ppermute | solution.py:135
  129.0 1.1 collective-permute-start.46
  131.0 3.9 %collective-permute-done.46 = bf16[64,1024]{1,0:T(8,128)(2,1)S(1)} collective-permute-done((bf16[64,1024]{1,0:T(8,128)(2,1)S(1)}, bf16[64,1024]{1,0:T(8,128)(2,1)S(1)}, u32[]{:S(2)}, u32[]{:S(2)}) %collective-permute-start.46) | collective-permute-done | bytes 131104 | tf_op jit(solution)/shard_map/ppermute | solution.py:135
  135.6 0.8 collective-permute-done.47
  137.2 0.9 collective-permute-start.49
  138.9 2.7 %collective-permute-done.48 = bf16[64,1024]{1,0:T(8,128)(2,1)S(1)} collective-permute-done((bf16[64,1024]{1,0:T(8,128)(2,1)S(1)}, bf16[64,1024]{1,0:T(8,128)(2,1)S(1)}, u32[]{:S(2)}, u32[]{:S(2)}) %collective-permute-start.48) | collective-permute-done | bytes 131104 | tf_op jit(solution)/shard_map/ppermute | solution.py:135
  142.3 1.6 %collective-permute-done.49 = bf16[64,1024]{1,0:T(8,128)(2,1)S(1)} collective-permute-done((bf16[64,1024]{1,0:T(8,128)(2,1)S(1)}, bf16[64,1024]{1,0:T(8,128)(2,1)S(1)}, u32[]{:S(2)}, u32[]{:S(2)}) %collective-permute-start.49) | collective-permute-done | bytes 131104 | tf_op jit(solution)/shard_map/ppermute | solution.py:135
  144.0 1.0 collective-permute-start.50
  145.1 7.6 %collective-permute-done.50 = bf16[64,1024]{1,0:T(8,128)(2,1)S(1)} collective-permute-done((bf16[64,1024]{1,0:T(8,128)(2,1)S(1)}, bf16[64,1024]{1,0:T(8,128)(2,1)S(1)}, u32[]{:S(2)}, u32[]{:S(2)}) %collective-permute-start.50) | collective-permute-done | bytes 131104 | tf_op jit(solution)/shard_map/ppermute | solution.py:135
  (163 shorter events, 34.5 us)
Async XLA Ops:
  3.7 7.0 %collective-permute-start.1 = (bf16[64,1024]{1,0:T(8,128)(2,1)S(1)}, bf16[64,1024]{1,0:T(8,128)(2,1)S(1)}, u32[]{:S(2)}, u32[]{:S(2)}) collective-permute-start(bf16[64,1024]{1,0:T(8,128)(2,1)S(1)} %get-tuple-element.224), channel_id=1, source_target_pairs={{0,4},{4,0},{8,12},{12,8},{1,5},{5,1},{9,13},{13,9},{2,6},{6,2},{1... | collective-permute-start | bytes 393224 | tf_op jit(solution)/shard_map/ppermute | solution.py:135
  7.7 6.1 %collective-permute-start = (bf16[64,1024]{1,0:T(8,128)(2,1)S(1)}, bf16[64,1024]{1,0:T(8,128)(2,1)S(1)}, u32[]{:S(2)}, u32[]{:S(2)}) collective-permute-start(bf16[64,1024]{1,0:T(8,128)(2,1)S(1)} %get-tuple-element.223), channel_id=1, source_target_pairs={{0,4},{4,0},{8,12},{12,8},{1,5},{5,1},{9,13},{13,9},{2,6},{6,2},{1... | collective-permute-start | bytes 393224 | tf_op jit(solution)/shard_map/ppermute | solution.py:135
  7.7 1.7 %copy-start = (bf16[5,1024,256]{2,1,0:T(8,128)(2,1)S(1)}, bf16[5,1024,256]{2,1,0:T(8,128)(2,1)}, u32[]{:S(2)}) copy-start(bf16[5,1024,256]{2,1,0:T(8,128)(2,1)} %sides) | copy-start | bytes 7864324
  10.4 34.6 %slice-start.5 = ((s8[10485760]{0:T(1024)(128)(4,1)}), s8[4194304]{0:T(1024)(128)(4,1)S(1)}, s32[]{:S(2)}) async-start(s8[10485760]{0:T(1024)(128)(4,1)} %bitcast.73), calls=%async_computation.5 | async-start | bytes 8388608
  10.7 12.6 %collective-permute-start.3 = (bf16[64,1024]{1,0:T(8,128)(2,1)S(1)}, bf16[64,1024]{1,0:T(8,128)(2,1)S(1)}, u32[]{:S(2)}, u32[]{:S(2)}) collective-permute-start(bf16[64,1024]{1,0:T(8,128)(2,1)S(1)} %get-tuple-element.457), channel_id=1, source_target_pairs={{0,8},{4,12},{8,0},{12,4},{1,9},{5,13},{9,1},{13,5},{2,10},{6,14},... | collective-permute-start | bytes 393224 | tf_op jit(solution)/shard_map/ppermute | solution.py:135
  13.8 11.4 %collective-permute-start.2 = (bf16[64,1024]{1,0:T(8,128)(2,1)S(1)}, bf16[64,1024]{1,0:T(8,128)(2,1)S(1)}, u32[]{:S(2)}, u32[]{:S(2)}) collective-permute-start(bf16[64,1024]{1,0:T(8,128)(2,1)S(1)} %get-tuple-element.455), channel_id=1, source_target_pairs={{0,8},{4,12},{8,0},{12,4},{1,9},{5,13},{9,1},{13,5},{2,10},{6,14},... | collective-permute-start | bytes 393224 | tf_op jit(solution)/shard_map/ppermute | solution.py:135
  16.4 31.0 %slice-start = ((s8[20971520]{0:T(1024)(128)(4,1)}), s8[4194304]{0:T(1024)(128)(4,1)S(1)}, s32[]{:S(2)}) async-start(s8[20971520]{0:T(1024)(128)(4,1)} %bitcast.71), calls=%async_computation | async-start | bytes 8388608
  18.3 29.1 %slice-start.1 = ((s8[20971520]{0:T(1024)(128)(4,1)}), s8[4194304]{0:T(1024)(128)(4,1)S(1)}, s32[]{:S(2)}) async-start(s8[20971520]{0:T(1024)(128)(4,1)} %bitcast.71), calls=%async_computation.1 | async-start | bytes 8388608
  23.4 21.7 %slice-start.6 = ((s8[10485760]{0:T(1024)(128)(4,1)}), s8[4194304]{0:T(1024)(128)(4,1)S(1)}, s32[]{:S(2)}) async-start(s8[10485760]{0:T(1024)(128)(4,1)} %bitcast.73), calls=%async_computation.6 | async-start | bytes 8388608
  23.4 5.7 %collective-permute-start.5 = (bf16[64,1024]{1,0:T(8,128)(2,1)S(1)}, bf16[64,1024]{1,0:T(8,128)(2,1)S(1)}, u32[]{:S(2)}, u32[]{:S(2)}) collective-permute-start(bf16[64,1024]{1,0:T(8,128)(2,1)S(1)} %add_convert_fusion.8.refs_0_.refs_1_), channel_id=1, source_target_pairs={{0,4},{4,0},{8,12},{12,8},{1,5},{5,1},{9,13},{13,9},{2,6},{6,2},{1... | collective-permute-start | bytes 393224 | tf_op jit(solution)/shard_map/ppermute | solution.py:135
  24.2 5.7 %collective-permute-start.6 = (bf16[64,1024]{1,0:T(8,128)(2,1)S(1)}, bf16[64,1024]{1,0:T(8,128)(2,1)S(1)}, u32[]{:S(2)}, u32[]{:S(2)}) collective-permute-start(bf16[64,1024]{1,0:T(8,128)(2,1)S(1)} %shard_map.40), channel_id=1, source_target_pairs={{0,1},{1,0},{2,3},{3,2},{4,5},{5,4},{6,7},{7,6},{8,9},{9,8},{10,11... | collective-permute-start | bytes 393224 | tf_op jit(solution)/shard_map/ppermute | solution.py:135
  25.1 6.6 %collective-permute-start.4 = (bf16[64,1024]{1,0:T(8,128)(2,1)S(1)}, bf16[64,1024]{1,0:T(8,128)(2,1)S(1)}, u32[]{:S(2)}, u32[]{:S(2)}) collective-permute-start(bf16[64,1024]{1,0:T(8,128)(2,1)S(1)} %add_convert_fusion.7.refs_0_.refs_3_), channel_id=1, source_target_pairs={{0,4},{4,0},{8,12},{12,8},{1,5},{5,1},{9,13},{13,9},{2,6},{6,2},{1... | collective-permute-start | bytes 393224 | tf_op jit(solution)/shard_map/ppermute | solution.py:135
  27.2 20.2 %slice-start.2 = ((s8[20971520]{0:T(1024)(128)(4,1)}), s8[4194304]{0:T(1024)(128)(4,1)S(1)}, s32[]{:S(2)}) async-start(s8[20971520]{0:T(1024)(128)(4,1)} %bitcast.71), calls=%async_computation.2 | async-start | bytes 8388608
  27.2 5.3 %collective-permute-start.7 = (bf16[64,1024]{1,0:T(8,128)(2,1)S(1)}, bf16[64,1024]{1,0:T(8,128)(2,1)S(1)}, u32[]{:S(2)}, u32[]{:S(2)}) collective-permute-start(bf16[64,1024]{1,0:T(8,128)(2,1)S(1)} %shard_map.41), channel_id=1, source_target_pairs={{0,1},{1,0},{2,3},{3,2},{4,5},{5,4},{6,7},{7,6},{8,9},{9,8},{10,11... | collective-permute-start | bytes 393224 | tf_op jit(solution)/shard_map/ppermute | solution.py:135
  30.0 5.9 %collective-permute-start.9 = (bf16[64,1024]{1,0:T(8,128)(2,1)S(1)}, bf16[64,1024]{1,0:T(8,128)(2,1)S(1)}, u32[]{:S(2)}, u32[]{:S(2)}) collective-permute-start(bf16[64,1024]{1,0:T(8,128)(2,1)S(1)} %get-tuple-element.453), channel_id=1, source_target_pairs={{0,2},{1,3},{2,0},{3,1},{4,6},{5,7},{6,4},{7,5},{8,10},{9,11},{10,... | collective-permute-start | bytes 393224 | tf_op jit(solution)/shard_map/ppermute | solution.py:135
  32.5 12.6 %slice-start.7 = ((s8[10485760]{0:T(1024)(128)(4,1)}), s8[2097152]{0:T(1024)(128)(4,1)S(1)}, s32[]{:S(2)}) async-start(s8[10485760]{0:T(1024)(128)(4,1)} %bitcast.73), calls=%async_computation.7 | async-start | bytes 4194304
  32.5 5.3 %collective-permute-start.8 = (bf16[64,1024]{1,0:T(8,128)(2,1)S(1)}, bf16[64,1024]{1,0:T(8,128)(2,1)S(1)}, u32[]{:S(2)}, u32[]{:S(2)}) collective-permute-start(bf16[64,1024]{1,0:T(8,128)(2,1)S(1)} %get-tuple-element.451), channel_id=1, source_target_pairs={{0,2},{1,3},{2,0},{3,1},{4,6},{5,7},{6,4},{7,5},{8,10},{9,11},{10,... | collective-permute-start | bytes 393224 | tf_op jit(solution)/shard_map/ppermute | solution.py:135
  36.0 11.4 %slice-start.3 = ((s8[20971520]{0:T(1024)(128)(4,1)}), s8[4194304]{0:T(1024)(128)(4,1)S(1)}, s32[]{:S(2)}) async-start(s8[20971520]{0:T(1024)(128)(4,1)} %bitcast.71), calls=%async_computation.3 | async-start | bytes 8388608
  36.0 4.1 %collective-permute-start.11 = (bf16[64,1024]{1,0:T(8,128)(2,1)S(1)}, bf16[64,1024]{1,0:T(8,128)(2,1)S(1)}, u32[]{:S(2)}, u32[]{:S(2)}) collective-permute-start(bf16[64,1024]{1,0:T(8,128)(2,1)S(1)} %subtract_convert_fusion.7.refs_0_), channel_id=1, source_target_pairs={{0,1},{1,0},{2,3},{3,2},{4,5},{5,4},{6,7},{7,6},{8,9},{9,8},{10,11... | collective-permute-start | bytes 393224 | tf_op jit(solution)/shard_map/ppermute | solution.py:135
  36.8 6.4 %collective-permute-start.12 = (bf16[64,1024]{1,0:T(8,128)(2,1)S(1)}, bf16[64,1024]{1,0:T(8,128)(2,1)S(1)}, u32[]{:S(2)}, u32[]{:S(2)}) collective-permute-start(bf16[64,1024]{1,0:T(8,128)(2,1)S(1)} %shard_map.44), channel_id=1, source_target_pairs={{0,4},{4,0},{8,12},{12,8},{1,5},{5,1},{9,13},{13,9},{2,6},{6,2},{1... | collective-permute-start | bytes 393224 | tf_op jit(solution)/shard_map/ppermute | solution.py:135
  37.9 6.4 %collective-permute-start.10 = (bf16[64,1024]{1,0:T(8,128)(2,1)S(1)}, bf16[64,1024]{1,0:T(8,128)(2,1)S(1)}, u32[]{:S(2)}, u32[]{:S(2)}) collective-permute-start(bf16[64,1024]{1,0:T(8,128)(2,1)S(1)} %subtract_convert_fusion.6.refs_0_), channel_id=1, source_target_pairs={{0,1},{1,0},{2,3},{3,2},{4,5},{5,4},{6,7},{7,6},{8,9},{9,8},{10,11... | collective-permute-start | bytes 393224 | tf_op jit(solution)/shard_map/ppermute | solution.py:135
  38.7 6.9 %collective-permute-start.13 = (bf16[64,1024]{1,0:T(8,128)(2,1)S(1)}, bf16[64,1024]{1,0:T(8,128)(2,1)S(1)}, u32[]{:S(2)}, u32[]{:S(2)}) collective-permute-start(bf16[64,1024]{1,0:T(8,128)(2,1)S(1)} %shard_map.45), channel_id=1, source_target_pairs={{0,4},{4,0},{8,12},{12,8},{1,5},{5,1},{9,13},{13,9},{2,6},{6,2},{1... | collective-permute-start | bytes 393224 | tf_op jit(solution)/shard_map/ppermute | solution.py:135
  40.8 6.5 %slice-start.4 = ((s8[20971520]{0:T(1024)(128)(4,1)}), s8[4194304]{0:T(1024)(128)(4,1)S(1)}, s32[]{:S(2)}) async-start(s8[20971520]{0:T(1024)(128)(4,1)} %bitcast.71), calls=%async_computation.4 | async-start | bytes 8388608
  43.2 11.8 %collective-permute-start.15 = (bf16[64,1024]{1,0:T(8,128)(2,1)S(1)}, bf16[64,1024]{1,0:T(8,128)(2,1)S(1)}, u32[]{:S(2)}, u32[]{:S(2)}) collective-permute-start(bf16[64,1024]{1,0:T(8,128)(2,1)S(1)} %get-tuple-element.449), channel_id=1, source_target_pairs={{0,8},{4,12},{8,0},{12,4},{1,9},{5,13},{9,1},{13,5},{2,10},{6,14},... | collective-permute-start | bytes 393224 | tf_op jit(solution)/shard_map/ppermute | solution.py:135
  45.6 11.8 %collective-permute-start.14 = (bf16[64,1024]{1,0:T(8,128)(2,1)S(1)}, bf16[64,1024]{1,0:T(8,128)(2,1)S(1)}, u32[]{:S(2)}, u32[]{:S(2)}) collective-permute-start(bf16[64,1024]{1,0:T(8,128)(2,1)S(1)} %get-tuple-element.447), channel_id=1, source_target_pairs={{0,8},{4,12},{8,0},{12,4},{1,9},{5,13},{9,1},{13,5},{2,10},{6,14},... | collective-permute-start | bytes 393224 | tf_op jit(solution)/shard_map/ppermute | solution.py:135
  55.0 5.6 %collective-permute-start.17 = (bf16[64,1024]{1,0:T(8,128)(2,1)S(1)}, bf16[64,1024]{1,0:T(8,128)(2,1)S(1)}, u32[]{:S(2)}, u32[]{:S(2)}) collective-permute-start(bf16[64,1024]{1,0:T(8,128)(2,1)S(1)} %add_convert_fusion.6.refs_0_.refs_1_), channel_id=1, source_target_pairs={{0,4},{4,0},{8,12},{12,8},{1,5},{5,1},{9,13},{13,9},{2,6},{6,2},{1... | collective-permute-start | bytes 393224 | tf_op jit(solution)/shard_map/ppermute | solution.py:135
  55.9 5.5 %collective-permute-start.18 = (bf16[64,1024]{1,0:T(8,128)(2,1)S(1)}, bf16[64,1024]{1,0:T(8,128)(2,1)S(1)}, u32[]{:S(2)}, u32[]{:S(2)}) collective-permute-start(bf16[64,1024]{1,0:T(8,128)(2,1)S(1)} %shard_map.49), channel_id=1, source_target_pairs={{0,1},{1,0},{2,3},{3,2},{4,5},{5,4},{6,7},{7,6},{8,9},{9,8},{10,11... | collective-permute-start | bytes 393224 | tf_op jit(solution)/shard_map/ppermute | solution.py:135
  57.4 6.5 %collective-permute-start.16 = (bf16[64,1024]{1,0:T(8,128)(2,1)S(1)}, bf16[64,1024]{1,0:T(8,128)(2,1)S(1)}, u32[]{:S(2)}, u32[]{:S(2)}) collective-permute-start(bf16[64,1024]{1,0:T(8,128)(2,1)S(1)} %add_convert_fusion.5.refs_0_.refs_3_), channel_id=1, source_target_pairs={{0,4},{4,0},{8,12},{12,8},{1,5},{5,1},{9,13},{13,9},{2,6},{6,2},{1... | collective-permute-start | bytes 393224 | tf_op jit(solution)/shard_map/ppermute | solution.py:135
  58.8 5.9 %collective-permute-start.19 = (bf16[64,1024]{1,0:T(8,128)(2,1)S(1)}, bf16[64,1024]{1,0:T(8,128)(2,1)S(1)}, u32[]{:S(2)}, u32[]{:S(2)}) collective-permute-start(bf16[64,1024]{1,0:T(8,128)(2,1)S(1)} %shard_map.50), channel_id=1, source_target_pairs={{0,1},{1,0},{2,3},{3,2},{4,5},{5,4},{6,7},{7,6},{8,9},{9,8},{10,11... | collective-permute-start | bytes 393224 | tf_op jit(solution)/shard_map/ppermute | solution.py:135
  61.4 5.5 %collective-permute-start.21 = (bf16[64,1024]{1,0:T(8,128)(2,1)S(1)}, bf16[64,1024]{1,0:T(8,128)(2,1)S(1)}, u32[]{:S(2)}, u32[]{:S(2)}) collective-permute-start(bf16[64,1024]{1,0:T(8,128)(2,1)S(1)} %get-tuple-element.445), channel_id=1, source_target_pairs={{0,2},{1,3},{2,0},{3,1},{4,6},{5,7},{6,4},{7,5},{8,10},{9,11},{10,... | collective-permute-start | bytes 393224 | tf_op jit(solution)/shard_map/ppermute | solution.py:135
  64.8 5.0 %collective-permute-start.20 = (bf16[64,1024]{1,0:T(8,128)(2,1)S(1)}, bf16[64,1024]{1,0:T(8,128)(2,1)S(1)}, u32[]{:S(2)}, u32[]{:S(2)}) collective-permute-start(bf16[64,1024]{1,0:T(8,128)(2,1)S(1)} %get-tuple-element.443), channel_id=1, source_target_pairs={{0,2},{1,3},{2,0},{3,1},{4,6},{5,7},{6,4},{7,5},{8,10},{9,11},{10,... | collective-permute-start | bytes 393224 | tf_op jit(solution)/shard_map/ppermute | solution.py:135
  66.9 4.5 %collective-permute-start.23 = (bf16[64,1024]{1,0:T(8,128)(2,1)S(1)}, bf16[64,1024]{1,0:T(8,128)(2,1)S(1)}, u32[]{:S(2)}, u32[]{:S(2)}) collective-permute-start(bf16[64,1024]{1,0:T(8,128)(2,1)S(1)} %subtract_convert_fusion.5.refs_0_), channel_id=1, source_target_pairs={{0,1},{1,0},{2,3},{3,2},{4,5},{5,4},{6,7},{7,6},{8,9},{9,8},{10,11... | collective-permute-start | bytes 393224 | tf_op jit(solution)/shard_map/ppermute | solution.py:135
  67.7 6.0 %collective-permute-start.24 = (bf16[64,1024]{1,0:T(8,128)(2,1)S(1)}, bf16[64,1024]{1,0:T(8,128)(2,1)S(1)}, u32[]{:S(2)}, u32[]{:S(2)}) collective-permute-start(bf16[64,1024]{1,0:T(8,128)(2,1)S(1)} %shard_map.54), channel_id=1, source_target_pairs={{0,4},{4,0},{8,12},{12,8},{1,5},{5,1},{9,13},{13,9},{2,6},{6,2},{1... | collective-permute-start | bytes 393224 | tf_op jit(solution)/shard_map/ppermute | solution.py:135
  69.9 5.2 %collective-permute-start.22 = (bf16[64,1024]{1,0:T(8,128)(2,1)S(1)}, bf16[64,1024]{1,0:T(8,128)(2,1)S(1)}, u32[]{:S(2)}, u32[]{:S(2)}) collective-permute-start(bf16[64,1024]{1,0:T(8,128)(2,1)S(1)} %subtract_convert_fusion.4.refs_0_), channel_id=1, source_target_pairs={{0,1},{1,0},{2,3},{3,2},{4,5},{5,4},{6,7},{7,6},{8,9},{9,8},{10,11... | collective-permute-start | bytes 393224 | tf_op jit(solution)/shard_map/ppermute | solution.py:135
  70.7 6.0 %collective-permute-start.25 = (bf16[64,1024]{1,0:T(8,128)(2,1)S(1)}, bf16[64,1024]{1,0:T(8,128)(2,1)S(1)}, u32[]{:S(2)}, u32[]{:S(2)}) collective-permute-start(bf16[64,1024]{1,0:T(8,128)(2,1)S(1)} %shard_map.55), channel_id=1, source_target_pairs={{0,4},{4,0},{8,12},{12,8},{1,5},{5,1},{9,13},{13,9},{2,6},{6,2},{1... | collective-permute-start | bytes 393224 | tf_op jit(solution)/shard_map/ppermute | solution.py:135
  73.7 12.4 %collective-permute-start.27 = (bf16[64,1024]{1,0:T(8,128)(2,1)S(1)}, bf16[64,1024]{1,0:T(8,128)(2,1)S(1)}, u32[]{:S(2)}, u32[]{:S(2)}) collective-permute-start(bf16[64,1024]{1,0:T(8,128)(2,1)S(1)} %get-tuple-element.441), channel_id=1, source_target_pairs={{0,8},{4,12},{8,0},{12,4},{1,9},{5,13},{9,1},{13,5},{2,10},{6,14},... | collective-permute-start | bytes 393224 | tf_op jit(solution)/shard_map/ppermute | solution.py:135
  76.7 11.6 %collective-permute-start.26 = (bf16[64,1024]{1,0:T(8,128)(2,1)S(1)}, bf16[64,1024]{1,0:T(8,128)(2,1)S(1)}, u32[]{:S(2)}, u32[]{:S(2)}) collective-permute-start(bf16[64,1024]{1,0:T(8,128)(2,1)S(1)} %get-tuple-element.439), channel_id=1, source_target_pairs={{0,8},{4,12},{8,0},{12,4},{1,9},{5,13},{9,1},{13,5},{2,10},{6,14},... | collective-permute-start | bytes 393224 | tf_op jit(solution)/shard_map/ppermute | solution.py:135
  86.2 5.7 %collective-permute-start.29 = (bf16[64,1024]{1,0:T(8,128)(2,1)S(1)}, bf16[64,1024]{1,0:T(8,128)(2,1)S(1)}, u32[]{:S(2)}, u32[]{:S(2)}) collective-permute-start(bf16[64,1024]{1,0:T(8,128)(2,1)S(1)} %add_convert_fusion.4.refs_0_.refs_1_), channel_id=1, source_target_pairs={{0,4},{4,0},{8,12},{12,8},{1,5},{5,1},{9,13},{13,9},{2,6},{6,2},{1... | collective-permute-start | bytes 393224 | tf_op jit(solution)/shard_map/ppermute | solution.py:135
  87.0 5.6 %collective-permute-start.30 = (bf16[64,1024]{1,0:T(8,128)(2,1)S(1)}, bf16[64,1024]{1,0:T(8,128)(2,1)S(1)}, u32[]{:S(2)}, u32[]{:S(2)}) collective-permute-start(bf16[64,1024]{1,0:T(8,128)(2,1)S(1)} %shard_map.59), channel_id=1, source_target_pairs={{0,1},{1,0},{2,3},{3,2},{4,5},{5,4},{6,7},{7,6},{8,9},{9,8},{10,11... | collective-permute-start | bytes 393224 | tf_op jit(solution)/shard_map/ppermute | solution.py:135
  88.3 7.9 %collective-permute-start.28 = (bf16[64,1024]{1,0:T(8,128)(2,1)S(1)}, bf16[64,1024]{1,0:T(8,128)(2,1)S(1)}, u32[]{:S(2)}, u32[]{:S(2)}) collective-permute-start(bf16[64,1024]{1,0:T(8,128)(2,1)S(1)} %add_convert_fusion.3.refs_0_.refs_3_), channel_id=1, source_target_pairs={{0,4},{4,0},{8,12},{12,8},{1,5},{5,1},{9,13},{13,9},{2,6},{6,2},{1... | collective-permute-start | bytes 393224 | tf_op jit(solution)/shard_map/ppermute | solution.py:135
  90.0 7.1 %collective-permute-start.31 = (bf16[64,1024]{1,0:T(8,128)(2,1)S(1)}, bf16[64,1024]{1,0:T(8,128)(2,1)S(1)}, u32[]{:S(2)}, u32[]{:S(2)}) collective-permute-start(bf16[64,1024]{1,0:T(8,128)(2,1)S(1)} %shard_map.60), channel_id=1, source_target_pairs={{0,1},{1,0},{2,3},{3,2},{4,5},{5,4},{6,7},{7,6},{8,9},{9,8},{10,11... | collective-permute-start | bytes 393224 | tf_op jit(solution)/shard_map/ppermute | solution.py:135
  92.7 5.1 %collective-permute-start.33 = (bf16[64,1024]{1,0:T(8,128)(2,1)S(1)}, bf16[64,1024]{1,0:T(8,128)(2,1)S(1)}, u32[]{:S(2)}, u32[]{:S(2)}) collective-permute-start(bf16[64,1024]{1,0:T(8,128)(2,1)S(1)} %get-tuple-element.437), channel_id=1, source_target_pairs={{0,2},{1,3},{2,0},{3,1},{4,6},{5,7},{6,4},{7,5},{8,10},{9,11},{10,... | collective-permute-start | bytes 393224 | tf_op jit(solution)/shard_map/ppermute | solution.py:135
  97.1 5.0 %collective-permute-start.32 = (bf16[64,1024]{1,0:T(8,128)(2,1)S(1)}, bf16[64,1024]{1,0:T(8,128)(2,1)S(1)}, u32[]{:S(2)}, u32[]{:S(2)}) collective-permute-start(bf16[64,1024]{1,0:T(8,128)(2,1)S(1)} %get-tuple-element.435), channel_id=1, source_target_pairs={{0,2},{1,3},{2,0},{3,1},{4,6},{5,7},{6,4},{7,5},{8,10},{9,11},{10,... | collective-permute-start | bytes 393224 | tf_op jit(solution)/shard_map/ppermute | solution.py:135
  97.9 5.4 %collective-permute-start.35 = (bf16[64,1024]{1,0:T(8,128)(2,1)S(1)}, bf16[64,1024]{1,0:T(8,128)(2,1)S(1)}, u32[]{:S(2)}, u32[]{:S(2)}) collective-permute-start(bf16[64,1024]{1,0:T(8,128)(2,1)S(1)} %subtract_convert_fusion.3.refs_0_), channel_id=1, source_target_pairs={{0,1},{1,0},{2,3},{3,2},{4,5},{5,4},{6,7},{7,6},{8,9},{9,8},{10,11... | collective-permute-start | bytes 393224 | tf_op jit(solution)/shard_map/ppermute | solution.py:135
  98.7 6.0 %collective-permute-start.36 = (bf16[64,1024]{1,0:T(8,128)(2,1)S(1)}, bf16[64,1024]{1,0:T(8,128)(2,1)S(1)}, u32[]{:S(2)}, u32[]{:S(2)}) collective-permute-start(bf16[64,1024]{1,0:T(8,128)(2,1)S(1)} %shard_map.65), channel_id=1, source_target_pairs={{0,4},{4,0},{8,12},{12,8},{1,5},{5,1},{9,13},{13,9},{2,6},{6,2},{1... | collective-permute-start | bytes 393224 | tf_op jit(solution)/shard_map/ppermute | solution.py:135
  102.2 4.4 %collective-permute-start.34 = (bf16[64,1024]{1,0:T(8,128)(2,1)S(1)}, bf16[64,1024]{1,0:T(8,128)(2,1)S(1)}, u32[]{:S(2)}, u32[]{:S(2)}) collective-permute-start(bf16[64,1024]{1,0:T(8,128)(2,1)S(1)} %subtract_convert_fusion.2.refs_0_), channel_id=1, source_target_pairs={{0,1},{1,0},{2,3},{3,2},{4,5},{5,4},{6,7},{7,6},{8,9},{9,8},{10,11... | collective-permute-start | bytes 393224 | tf_op jit(solution)/shard_map/ppermute | solution.py:135
  103.0 7.3 %collective-permute-start.37 = (bf16[64,1024]{1,0:T(8,128)(2,1)S(1)}, bf16[64,1024]{1,0:T(8,128)(2,1)S(1)}, u32[]{:S(2)}, u32[]{:S(2)}) collective-permute-start(bf16[64,1024]{1,0:T(8,128)(2,1)S(1)} %shard_map.66), channel_id=1, source_target_pairs={{0,4},{4,0},{8,12},{12,8},{1,5},{5,1},{9,13},{13,9},{2,6},{6,2},{1... | collective-permute-start | bytes 393224 | tf_op jit(solution)/shard_map/ppermute | solution.py:135
  104.7 12.5 %collective-permute-start.39 = (bf16[64,1024]{1,0:T(8,128)(2,1)S(1)}, bf16[64,1024]{1,0:T(8,128)(2,1)S(1)}, u32[]{:S(2)}, u32[]{:S(2)}) collective-permute-start(bf16[64,1024]{1,0:T(8,128)(2,1)S(1)} %get-tuple-element.433), channel_id=1, source_target_pairs={{0,8},{4,12},{8,0},{12,4},{1,9},{5,13},{9,1},{13,5},{2,10},{6,14},... | collective-permute-start | bytes 393224 | tf_op jit(solution)/shard_map/ppermute | solution.py:135
  110.3 9.1 %collective-permute-start.38 = (bf16[64,1024]{1,0:T(8,128)(2,1)S(1)}, bf16[64,1024]{1,0:T(8,128)(2,1)S(1)}, u32[]{:S(2)}, u32[]{:S(2)}) collective-permute-start(bf16[64,1024]{1,0:T(8,128)(2,1)S(1)} %get-tuple-element.431), channel_id=1, source_target_pairs={{0,8},{4,12},{8,0},{12,4},{1,9},{5,13},{9,1},{13,5},{2,10},{6,14},... | collective-permute-start | bytes 393224 | tf_op jit(solution)/shard_map/ppermute | solution.py:135
  117.2 5.7 %collective-permute-start.41 = (bf16[64,1024]{1,0:T(8,128)(2,1)S(1)}, bf16[64,1024]{1,0:T(8,128)(2,1)S(1)}, u32[]{:S(2)}, u32[]{:S(2)}) collective-permute-start(bf16[64,1024]{1,0:T(8,128)(2,1)S(1)} %add_convert_fusion.2.refs_0_), channel_id=1, source_target_pairs={{0,4},{4,0},{8,12},{12,8},{1,5},{5,1},{9,13},{13,9},{2,6},{6,2},{1... | collective-permute-start | bytes 393224 | tf_op jit(solution)/shard_map/ppermute | solution.py:135
  118.1 5.6 %collective-permute-start.42 = (bf16[64,1024]{1,0:T(8,128)(2,1)S(1)}, bf16[64,1024]{1,0:T(8,128)(2,1)S(1)}, u32[]{:S(2)}, u32[]{:S(2)}) collective-permute-start(bf16[64,1024]{1,0:T(8,128)(2,1)S(1)} %shard_map.70), channel_id=1, source_target_pairs={{0,1},{1,0},{2,3},{3,2},{4,5},{5,4},{6,7},{7,6},{8,9},{9,8},{10,11... | collective-permute-start | bytes 393224 | tf_op jit(solution)/shard_map/ppermute | solution.py:135
  119.4 5.7 %collective-permute-start.40 = (bf16[64,1024]{1,0:T(8,128)(2,1)S(1)}, bf16[64,1024]{1,0:T(8,128)(2,1)S(1)}, u32[]{:S(2)}, u32[]{:S(2)}) collective-permute-start(bf16[64,1024]{1,0:T(8,128)(2,1)S(1)} %add_convert_fusion.1.refs_0_), channel_id=1, source_target_pairs={{0,4},{4,0},{8,12},{12,8},{1,5},{5,1},{9,13},{13,9},{2,6},{6,2},{1... | collective-permute-start | bytes 393224 | tf_op jit(solution)/shard_map/ppermute | solution.py:135
  121.1 5.0 %collective-permute-start.44 = (bf16[64,1024]{1,0:T(8,128)(2,1)S(1)}, bf16[64,1024]{1,0:T(8,128)(2,1)S(1)}, u32[]{:S(2)}, u32[]{:S(2)}) collective-permute-start(bf16[64,1024]{1,0:T(8,128)(2,1)S(1)} %shard_map.71), channel_id=1, source_target_pairs={{0,1},{1,0},{2,3},{3,2},{4,5},{5,4},{6,7},{7,6},{8,9},{9,8},{10,11... | collective-permute-start | bytes 393224 | tf_op jit(solution)/shard_map/ppermute | solution.py:135
  123.7 5.0 %collective-permute-start.43 = (bf16[64,1024]{1,0:T(8,128)(2,1)S(1)}, bf16[64,1024]{1,0:T(8,128)(2,1)S(1)}, u32[]{:S(2)}, u32[]{:S(2)}) collective-permute-start(bf16[64,1024]{1,0:T(8,128)(2,1)S(1)} %get-tuple-element.429), channel_id=1, source_target_pairs={{0,2},{1,3},{2,0},{3,1},{4,6},{5,7},{6,4},{7,5},{8,10},{9,11},{10,... | collective-permute-start | bytes 393224 | tf_op jit(solution)/shard_map/ppermute | solution.py:135
  128.8 1.4 collective-permute-start.45
  129.0 6.0 %collective-permute-start.46 = (bf16[64,1024]{1,0:T(8,128)(2,1)S(1)}, bf16[64,1024]{1,0:T(8,128)(2,1)S(1)}, u32[]{:S(2)}, u32[]{:S(2)}) collective-permute-start(bf16[64,1024]{1,0:T(8,128)(2,1)S(1)} %get-tuple-element.427), channel_id=1, source_target_pairs={{0,2},{1,3},{2,0},{3,1},{4,6},{5,7},{6,4},{7,5},{8,10},{9,11},{10,... | collective-permute-start | bytes 393224 | tf_op jit(solution)/shard_map/ppermute | solution.py:135
  135.0 1.4 collective-permute-start.47
  135.2 6.4 %collective-permute-start.48 = (bf16[64,1024]{1,0:T(8,128)(2,1)S(1)}, bf16[64,1024]{1,0:T(8,128)(2,1)S(1)}, u32[]{:S(2)}, u32[]{:S(2)}) collective-permute-start(bf16[64,1024]{1,0:T(8,128)(2,1)S(1)} %shard_map.74), channel_id=1, source_target_pairs={{0,4},{4,0},{8,12},{12,8},{1,5},{5,1},{9,13},{13,9},{2,6},{6,2},{1... | collective-permute-start | bytes 393224 | tf_op jit(solution)/shard_map/ppermute | solution.py:135
  137.2 6.7 %collective-permute-start.49 = (bf16[64,1024]{1,0:T(8,128)(2,1)S(1)}, bf16[64,1024]{1,0:T(8,128)(2,1)S(1)}, u32[]{:S(2)}, u32[]{:S(2)}) collective-permute-start(bf16[64,1024]{1,0:T(8,128)(2,1)S(1)} %shard_map.75), channel_id=1, source_target_pairs={{0,4},{4,0},{8,12},{12,8},{1,5},{5,1},{9,13},{13,9},{2,6},{6,2},{1... | collective-permute-start | bytes 393224 | tf_op jit(solution)/shard_map/ppermute | solution.py:135
  144.0 8.7 %collective-permute-start.50 = (bf16[64,1024]{1,0:T(8,128)(2,1)S(1)}, bf16[64,1024]{1,0:T(8,128)(2,1)S(1)}, u32[]{:S(2)}, u32[]{:S(2)}) collective-permute-start(bf16[64,1024]{1,0:T(8,128)(2,1)S(1)} %broadcast_select_fusion.4), channel_id=1, source_target_pairs={{0,8},{4,12},{8,0},{12,4},{1,9},{5,13},{9,1},{13,5},{2,10},{6,14},... | collective-permute-start | bytes 393224 | tf_op jit(solution)/shard_map/ppermute | solution.py:135
  145.0 7.6 %copy-start.1 = (bf16[5,1024,64]{1,2,0:T(8,128)(2,1)}, bf16[5,1024,64]{1,2,0:T(8,128)(2,1)S(1)}, u32[]{:S(2)}) copy-start(bf16[5,1024,64]{1,2,0:T(8,128)(2,1)S(1)} %bitcast_dynamic-update-slice_fusion) | copy-start | bytes 1966084

commit v5 on v4

--- a/solution.py
+++ b/solution.py
@@ -15,6 +15,7 @@
     return block_row * (block_row - 1) // 2 + column_index
 
 
+HBM = pl.BlockSpec(memory_space=pl.ANY)
 VMEM = pl.BlockSpec(memory_space=pltpu.VMEM)
 SMEM = pl.BlockSpec(memory_space=pltpu.SMEM)
 COST = pl.CostEstimate(flops=1, bytes_accessed=1, transcendentals=0)
@@ -56,31 +57,49 @@
     )(block, *units, *rest)
 
 
-def first_kernel(s, side, right, block, keep, leave, product):
-    width = keep.shape[0]
-    x = right[:, pl.ds(2 * s * width, 2 * width)].T
-    product[...] = times_transposed(x, block[...])
+def first_kernel(s, side, sides, blocks, keep, leave, product, right, held, sems, right_sem):
+    width, rows = keep.shape
+    tile = min(rows, TILE)
+    bring = pltpu.make_async_copy(sides.at[0, :, pl.ds(2 * s * width, 2 * width)], right, right_sem)
+    bring.start()
+    copies = []
+    for t in range(rows // tile):
+        cut = pl.ds(t * tile, tile)
+        copy = pltpu.make_async_copy(blocks.at[0, cut], held.at[cut], sems.at[t])
+        copy.start()
+        copies.append((cut, copy))
+    bring.wait()
+    x = right[...].T
+    for cut, copy in copies:
+        copy.wait()
+        product[:, cut] = times_transposed(held[cut], x).T
     own = pl.multiple_of(side[0] * width, width)
     other = pl.multiple_of((1 - side[0]) * width, width)
     leave[...] = product[pl.ds(own, width)].astype(jnp.bfloat16)
     keep[...] = product[pl.ds(other, width)]
 
 
-def first_products(s, side, right, block):
-    rows = block.shape[0]
-    width = right.shape[1] // UNITS
+def first_products(s, side, sides, blocks):
+    rows, depth = blocks.shape[1:]
+    width = sides.shape[2] // UNITS
     return pl.pallas_call(
         functools.partial(first_kernel, s),
         out_shape=(
             jax.ShapeDtypeStruct((width, rows), jnp.float32),
             jax.ShapeDtypeStruct((width, rows), jnp.bfloat16),
         ),
-        in_specs=[SMEM, VMEM, VMEM],
+        in_specs=[SMEM, HBM, HBM],
         out_specs=(VMEM, VMEM),
-        scratch_shapes=[pltpu.VMEM((2 * width, rows), jnp.float32)],
-        compiler_params=params(),
+        scratch_shapes=[
+            pltpu.VMEM((2 * width, rows), jnp.float32),
+            pltpu.VMEM((depth, 2 * width), jnp.bfloat16),
+            pltpu.VMEM((rows, depth), jnp.bfloat16),
+            pltpu.SemaphoreType.DMA((rows // min(rows, TILE),)),
+            pltpu.SemaphoreType.DMA,
+        ],
+        compiler_params=pltpu.CompilerParams(vmem_limit_bytes=56 * 2**20),
         cost_estimate=COST,
-    )(side, right, block)
+    )(side, sides, blocks)
 
 
 def turn_kernel(width, side, sides, out, turned):
@@ -257,42 +276,47 @@
             other = order.run(work, st["total"], *arrived)
             solved[step][s] = (trade(other, "row", 1), other)
 
-        inverses[0] = order.block(inverse_blocks, 0)
-        right = order.block(right_sides, 0)
         for s in range(STREAMS):
             state[s]["total"], leaving = order.run(
-                lambda v, w: first_products(s, side_ref, v, w), right, inverses[0]
+                lambda v, w: first_products(s, side_ref, v, w), right_sides, inverse_blocks
             )
             state[s]["flight"] = trade(leaving, "row", 1)
         if steps_total > 1:
             base = order.run(lambda v: turned_sides(side_ref, v), right_sides)
-        for s in range(STREAMS):
-            pair_sum(s)
-            cross(s)
+        pair_sum(0)
+        cross(0)
         load_factor(1)
         load_inverse(1)
 
         for step in range(1, steps_total):
-            for s in range(STREAMS):
-                solve(s, step - 1)
-                factor_other(s, step)
+            final = exact and step == last_step
+            solve(0, step - 1)
+            factor_other(0, step)
+            pair_sum(1)
+            cross(1)
             factor_own(0, step)
             chip_sum(0)
             older(step + 1, range(step - 1))
+            if step == 1:
+                load_factor(2)
+            residual(0, step)
+            inverse_own(0, step)
+            solve(1, step - 1)
+            factor_other(1, step)
+            inverse_other(0, step)
+            pair_sum(0)
+            if not final:
+                cross(0)
             factor_own(1, step)
             chip_sum(1)
-            for s in range(STREAMS):
-                residual(s, step)
-                inverse_own(s, step)
-            for s in range(STREAMS):
-                inverse_other(s, step)
-                if s == STREAMS - 1:
-                    load_inverse(step + 1)
-                pair_sum(s)
-                if not (exact and step == last_step):
-                    cross(s)
             older(step + 1, [step - 1])
-            load_factor(step + 1)
+            if step > 1:
+                load_factor(step + 1)
+            residual(1, step)
+            inverse_own(1, step)
+            inverse_other(1, step)
+            load_inverse(step + 1)
+        pair_sum(1)
 
         outputs = []
         for step in range(steps_total):
@@ -306,8 +330,9 @@
                 outputs.append(found.T)
                 continue
             if step == last_step:
-                for s in range(STREAMS):
-                    solve(s, step)
+                solve(0, step)
+                cross(1)
+                solve(1, step)
             unit = place * UNITS // n_row
             found = solved[step][0][0]
             for s in range(STREAMS):

time: 154 us -> 174 us (1.13)
  starting transfers between devices: 37.5 us -> 50.2 us
  waiting for transfers between devices: 69.3 us -> 57.4 us
  local copies, waits for them, and re-layouts: 10.9 us -> 22 us
  Pallas kernels: 32.4 us -> 38.3 us
  other arithmetic: 2.29 us -> 4.61 us
    ppermute x51, starting transfers between devices: 37.5 us -> 50.2 us  [trade(): return lax.ppermute(value, axis, [(i, i ^ step) for i in range(size)])]
    ppermute x51, waiting for transfers between devices: 69.3 us -> 57.4 us  [trade(): return lax.ppermute(value, axis, [(i, i ^ step) for i in range(size)])]
    squeeze x16 -> x14, local copies, waits for them, and re-layouts: 8.76 us -> 19.9 us  [block(): self.last = lax.optimization_barrier(self.run(lambda v: v[index], blocks))]
    pallas_call x2, Pallas kernels: 1.7 us -> 7.5 us  [first_products(): pl.pallas_call(functools.partial(first_kernel, s), out_shape=(jax.ShapeDt...]
  transfers between devices with their start and end apart: 51 -> 51, of which waited for: 32 -> 22; matrix products, arithmetic and copies ran while one was open for 5% -> 14% of each run, Pallas kernels for 21% -> 20%
where the time goes in v5:
time: 174 us; the launch traced here: 173 us
  waiting for transfers between devices  57.4 us (33%)
  starting transfers between devices  50.2 us (29%)
  Pallas kernels  38.3 us (22%)
  local copies, waits for them, and re-layouts  22 us (13%)
  other arithmetic  4.61 us (3%)
    ppermute x51, waiting for transfers between devices, trade(): return lax.ppermute(value, axis, [(i, i ^ step) for i in range(size)])  57.4 us
    ppermute x51, starting transfers between devices, trade(): return lax.ppermute(value, axis, [(i, i ^ step) for i in range(size)])  50.2 us
    pallas_call x38, Pallas kernels, product(): pl.pallas_call(functools.partial(product_kernel, len(units)), out_shape=j...  29.8 us
    squeeze x14, local copies, waits for them, and re-layouts, block(): self.last = lax.optimization_barrier(self.run(lambda v: v[index], blocks))  19.9 us
    pallas_call x2, Pallas kernels, first_products(): pl.pallas_call(functools.partial(first_kernel, s), out_shape=(jax.ShapeDt...  7.5 us
  transfers between devices with their start and end apart: 51, of which 22 were waited for; matrix products, arithmetic and copies ran while one was open for 14% of the time, Pallas kernels for 20%

profile of v5, /device:TPU:0, one launch (start us, length us, event | category | flops | bytes accessed | tf_op | source)
XLA Modules:
  0.0 173.5 jit_solution(8863991168971931959)
XLA Ops:
  0.0 3.7 %shard_map.37 = (f32[64,1024]{1,0:T(8,128)}, bf16[64,1024]{1,0:T(8,128)(2,1)}) custom-call(s32[1]{0:T(128)} %bitcast.side, bf16[5,1024,256]{2,1,0:T(8,128)(2,1)} %sides.3, bf16[5,1024,1024]{2,1,0:T(8,128)(2,1)} %blocks.2), custom_call_target="tpu_custom_call" | custom-call | flops 1 | bytes 1 | tf_op jit(solution)/shard_map/pallas_call | solution.py:85
  3.7 3.1 %collective-permute-start.1 = (bf16[64,1024]{1,0:T(8,128)(2,1)}, bf16[64,1024]{1,0:T(8,128)(2,1)S(1)}, u32[]{:S(2)}, u32[]{:S(2)}) collective-permute-start(bf16[64,1024]{1,0:T(8,128)(2,1)} %get-tuple-element.218), channel_id=1, source_target_pairs={{0,4},{4,0},{8,12},{12,8},{1,5},{5,1},{9,13},{13,9},{2,6},{6,2},{1... | collective-permute-start | bytes 393224 | tf_op jit(solution)/shard_map/ppermute | solution.py:154
  6.8 3.8 %shard_map.38 = (f32[64,1024]{1,0:T(8,128)}, bf16[64,1024]{1,0:T(8,128)(2,1)}) custom-call(s32[1]{0:T(128)} %bitcast.side, bf16[5,1024,256]{2,1,0:T(8,128)(2,1)} %sides.3, bf16[5,1024,1024]{2,1,0:T(8,128)(2,1)} %blocks.2), custom_call_target="tpu_custom_call" | custom-call | flops 1 | bytes 1 | tf_op jit(solution)/shard_map/pallas_call | solution.py:85
  10.7 0.9 shard_map.39
  12.4 3.1 %collective-permute-start.2 = (bf16[64,1024]{1,0:T(8,128)(2,1)S(1)}, bf16[64,1024]{1,0:T(8,128)(2,1)S(1)}, u32[]{:S(2)}, u32[]{:S(2)}) collective-permute-start(bf16[64,1024]{1,0:T(8,128)(2,1)S(1)} %get-tuple-element.451), channel_id=1, source_target_pairs={{0,8},{4,12},{8,0},{12,4},{1,9},{5,13},{9,1},{13,5},{2,10},{6,14},... | collective-permute-start | bytes 393224 | tf_op jit(solution)/shard_map/ppermute | solution.py:154
  15.5 1.8 %slice_bitcast_fusion.13.block = bf16[1024,1024]{1,0:T(8,128)(2,1)S(1)} fusion(bf16[10,1024,1024]{2,1,0:T(8,128)(2,1)} %param.3), kind=kLoop, calls=%fused_computation.13 | loop fusion | bytes 4194304 | tf_op jit(solution)/shard_map/squeeze | solution.py:147
  17.2 1.8 %slice_bitcast_fusion.12.block = bf16[1024,1024]{1,0:T(8,128)(2,1)S(1)} fusion(bf16[5,1024,1024]{2,1,0:T(8,128)(2,1)} %blocks.2), kind=kLoop, calls=%fused_computation.12 | loop fusion | bytes 4194304 | tf_op jit(solution)/shard_map/squeeze | solution.py:147
  19.0 2.3 %collective-permute-done.2 = bf16[64,1024]{1,0:T(8,128)(2,1)S(1)} collective-permute-done((bf16[64,1024]{1,0:T(8,128)(2,1)S(1)}, bf16[64,1024]{1,0:T(8,128)(2,1)S(1)}, u32[]{:S(2)}, u32[]{:S(2)}) %collective-permute-start.2) | collective-permute-done | bytes 131104 | tf_op jit(solution)/shard_map/ppermute | solution.py:154
  22.9 3.4 %collective-permute-start.3 = (bf16[64,1024]{1,0:T(8,128)(2,1)S(1)}, bf16[64,1024]{1,0:T(8,128)(2,1)S(1)}, u32[]{:S(2)}, u32[]{:S(2)}) collective-permute-start(bf16[64,1024]{1,0:T(8,128)(2,1)S(1)} %get-tuple-element.449), channel_id=1, source_target_pairs={{0,8},{4,12},{8,0},{12,4},{1,9},{5,13},{9,1},{13,5},{2,10},{6,14},... | collective-permute-start | bytes 393224 | tf_op jit(solution)/shard_map/ppermute | solution.py:154
  27.2 1.6 collective-permute-start.6
  28.7 1.8 %slice_bitcast_fusion.11.block = bf16[1024,1024]{1,0:T(8,128)(2,1)S(1)} fusion(bf16[10,1024,1024]{2,1,0:T(8,128)(2,1)} %param.3), kind=kLoop, calls=%fused_computation.11 | loop fusion | bytes 4194304 | tf_op jit(solution)/shard_map/squeeze | solution.py:147
  30.5 2.3 %collective-permute-done.6 = bf16[64,1024]{1,0:T(8,128)(2,1)S(1)} collective-permute-done((bf16[64,1024]{1,0:T(8,128)(2,1)S(1)}, bf16[64,1024]{1,0:T(8,128)(2,1)S(1)}, u32[]{:S(2)}, u32[]{:S(2)}) %collective-permute-start.6) | collective-permute-done | bytes 131104 | tf_op jit(solution)/shard_map/ppermute | solution.py:154
  34.1 1.8 %collective-permute-start.7 = (bf16[64,1024]{1,0:T(8,128)(2,1)S(1)}, bf16[64,1024]{1,0:T(8,128)(2,1)S(1)}, u32[]{:S(2)}, u32[]{:S(2)}) collective-permute-start(bf16[64,1024]{1,0:T(8,128)(2,1)S(1)} %add_convert_fusion.7.refs_0_.refs_3_), channel_id=1, source_target_pairs={{0,4},{4,0},{8,12},{12,8},{1,5},{5,1},{9,13},{13,9},{2,6},{6,2},{1... | collective-permute-start | bytes 393224 | tf_op jit(solution)/shard_map/ppermute | solution.py:154
  37.5 2.6 %collective-permute-done.9 = bf16[64,1024]{1,0:T(8,128)(2,1)S(1)} collective-permute-done((bf16[64,1024]{1,0:T(8,128)(2,1)S(1)}, bf16[64,1024]{1,0:T(8,128)(2,1)S(1)}, u32[]{:S(2)}, u32[]{:S(2)}) %collective-permute-start.9) | collective-permute-done | bytes 131104 | tf_op jit(solution)/shard_map/ppermute | solution.py:154
  40.1 2.4 %collective-permute-done.7.refs_0_.refs_2_ = bf16[64,1024]{1,0:T(8,128)(2,1)S(1)} collective-permute-done((bf16[64,1024]{1,0:T(8,128)(2,1)S(1)}, bf16[64,1024]{1,0:T(8,128)(2,1)S(1)}, u32[]{:S(2)}, u32[]{:S(2)}) %collective-permute-start.7) | collective-permute-done | bytes 131104 | tf_op jit(solution)/shard_map/ppermute | solution.py:154
  43.3 1.6 collective-permute-start.11
  44.9 3.4 %collective-permute-start.14 = (bf16[64,1024]{1,0:T(8,128)(2,1)S(1)}, bf16[64,1024]{1,0:T(8,128)(2,1)S(1)}, u32[]{:S(2)}, u32[]{:S(2)}) collective-permute-start(bf16[64,1024]{1,0:T(8,128)(2,1)S(1)} %get-tuple-element.445), channel_id=1, source_target_pairs={{0,8},{4,12},{8,0},{12,4},{1,9},{5,13},{9,1},{13,5},{2,10},{6,14},... | collective-permute-start | bytes 393224 | tf_op jit(solution)/shard_map/ppermute | solution.py:154
  48.3 1.8 %slice_bitcast_fusion.10.block = bf16[1024,1024]{1,0:T(8,128)(2,1)S(1)} fusion(bf16[10,1024,1024]{2,1,0:T(8,128)(2,1)} %param.3), kind=kLoop, calls=%fused_computation.10 | loop fusion | bytes 4194304 | tf_op jit(solution)/shard_map/squeeze | solution.py:147
  50.0 0.9 shard_map.46
  51.9 1.8 %collective-permute-start.13 = (bf16[64,1024]{1,0:T(8,128)(2,1)S(1)}, bf16[64,1024]{1,0:T(8,128)(2,1)S(1)}, u32[]{:S(2)}, u32[]{:S(2)}) collective-permute-start(bf16[64,1024]{1,0:T(8,128)(2,1)S(1)} %shard_map.47), channel_id=1, source_target_pairs={{0,4},{4,0},{8,12},{12,8},{1,5},{5,1},{9,13},{13,9},{2,6},{6,2},{1... | collective-permute-start | bytes 393224 | tf_op jit(solution)/shard_map/ppermute | solution.py:154
  56.1 2.0 %collective-permute-done.13 = bf16[64,1024]{1,0:T(8,128)(2,1)S(1)} collective-permute-done((bf16[64,1024]{1,0:T(8,128)(2,1)S(1)}, bf16[64,1024]{1,0:T(8,128)(2,1)S(1)}, u32[]{:S(2)}, u32[]{:S(2)}) %collective-permute-start.13) | collective-permute-done | bytes 131104 | tf_op jit(solution)/shard_map/ppermute | solution.py:154
  58.1 1.5 collective-permute-start.15
  59.6 1.1 collective-permute-done.16.refs_0_
  62.1 1.8 %slice_bitcast_fusion.8.block = bf16[1024,1024]{1,0:T(8,128)(2,1)S(1)} fusion(bf16[10,1024,1024]{2,1,0:T(8,128)(2,1)} %param.3), kind=kLoop, calls=%fused_computation.8 | loop fusion | bytes 4194304 | tf_op jit(solution)/shard_map/squeeze | solution.py:147
  64.8 1.8 %collective-permute-done.18 = bf16[64,1024]{1,0:T(8,128)(2,1)S(1)} collective-permute-done((bf16[64,1024]{1,0:T(8,128)(2,1)S(1)}, bf16[64,1024]{1,0:T(8,128)(2,1)S(1)}, u32[]{:S(2)}, u32[]{:S(2)}) %collective-permute-start.18) | collective-permute-done | bytes 131104 | tf_op jit(solution)/shard_map/ppermute | solution.py:154
  67.5 1.9 %collective-permute-start.21 = (bf16[64,1024]{1,0:T(8,128)(2,1)S(1)}, bf16[64,1024]{1,0:T(8,128)(2,1)S(1)}, u32[]{:S(2)}, u32[]{:S(2)}) collective-permute-start(bf16[64,1024]{1,0:T(8,128)(2,1)S(1)} %shard_map.52), channel_id=1, source_target_pairs={{0,4},{4,0},{8,12},{12,8},{1,5},{5,1},{9,13},{13,9},{2,6},{6,2},{1... | collective-permute-start | bytes 393224 | tf_op jit(solution)/shard_map/ppermute | solution.py:154
  71.3 2.5 %collective-permute-done.21 = bf16[64,1024]{1,0:T(8,128)(2,1)S(1)} collective-permute-done((bf16[64,1024]{1,0:T(8,128)(2,1)S(1)}, bf16[64,1024]{1,0:T(8,128)(2,1)S(1)}, u32[]{:S(2)}, u32[]{:S(2)}) %collective-permute-start.21) | collective-permute-done | bytes 131104 | tf_op jit(solution)/shard_map/ppermute | solution.py:154
  73.9 2.4 %collective-permute-done.19.refs_0_.refs_2_ = bf16[64,1024]{1,0:T(8,128)(2,1)S(1)} collective-permute-done((bf16[64,1024]{1,0:T(8,128)(2,1)S(1)}, bf16[64,1024]{1,0:T(8,128)(2,1)S(1)}, u32[]{:S(2)}, u32[]{:S(2)}) %collective-permute-start.19) | collective-permute-done | bytes 131104 | tf_op jit(solution)/shard_map/ppermute | solution.py:154
  77.7 2.1 %collective-permute-start.26 = (bf16[64,1024]{1,0:T(8,128)(2,1)S(1)}, bf16[64,1024]{1,0:T(8,128)(2,1)S(1)}, u32[]{:S(2)}, u32[]{:S(2)}) collective-permute-start(bf16[64,1024]{1,0:T(8,128)(2,1)S(1)} %get-tuple-element.437), channel_id=1, source_target_pairs={{0,8},{4,12},{8,0},{12,4},{1,9},{5,13},{9,1},{13,5},{2,10},{6,14},... | collective-permute-start | bytes 393224 | tf_op jit(solution)/shard_map/ppermute | solution.py:154
  79.8 1.8 %slice_bitcast_fusion.7.block = bf16[1024,1024]{1,0:T(8,128)(2,1)S(1)} fusion(bf16[10,1024,1024]{2,1,0:T(8,128)(2,1)} %param.3), kind=kLoop, calls=%fused_computation.7 | loop fusion | bytes 4194304 | tf_op jit(solution)/shard_map/squeeze | solution.py:147
  81.6 1.1 shard_map.56
  82.7 1.8 %slice_bitcast_fusion.6.block = bf16[1024,1024]{1,0:T(8,128)(2,1)S(1)} fusion(bf16[10,1024,1024]{2,1,0:T(8,128)(2,1)} %param.3), kind=kLoop, calls=%fused_computation.6 | loop fusion | bytes 4194304 | tf_op jit(solution)/shard_map/squeeze | solution.py:147
  85.4 1.5 collective-permute-start.25
  89.5 2.4 %collective-permute-done.25 = bf16[64,1024]{1,0:T(8,128)(2,1)S(1)} collective-permute-done((bf16[64,1024]{1,0:T(8,128)(2,1)S(1)}, bf16[64,1024]{1,0:T(8,128)(2,1)S(1)}, u32[]{:S(2)}, u32[]{:S(2)}) %collective-permute-start.25) | collective-permute-done | bytes 131104 | tf_op jit(solution)/shard_map/ppermute | solution.py:154
  92.6 1.7 collective-permute-done.28.refs_0_
  95.1 1.0 collective-permute-start.30
  96.0 1.8 %slice_bitcast_fusion.4.block = bf16[1024,1024]{1,0:T(8,128)(2,1)S(1)} fusion(bf16[10,1024,1024]{2,1,0:T(8,128)(2,1)} %param.3), kind=kLoop, calls=%fused_computation.4 | loop fusion | bytes 4194304 | tf_op jit(solution)/shard_map/squeeze | solution.py:147
  97.8 0.9 shard_map.61.refs_4_
  98.7 1.8 %slice_bitcast_fusion.3.block = bf16[1024,1024]{1,0:T(8,128)(2,1)S(1)} fusion(bf16[10,1024,1024]{2,1,0:T(8,128)(2,1)} %param.3), kind=kLoop, calls=%fused_computation.3 | loop fusion | bytes 4194304 | tf_op jit(solution)/shard_map/squeeze | solution.py:147
  100.5 0.9 shard_map.62.refs_4_
  102.2 2.2 %collective-permute-start.33 = (bf16[64,1024]{1,0:T(8,128)(2,1)S(1)}, bf16[64,1024]{1,0:T(8,128)(2,1)S(1)}, u32[]{:S(2)}, u32[]{:S(2)}) collective-permute-start(bf16[64,1024]{1,0:T(8,128)(2,1)S(1)} %shard_map.63), channel_id=1, source_target_pairs={{0,4},{4,0},{8,12},{12,8},{1,5},{5,1},{9,13},{13,9},{2,6},{6,2},{1... | collective-permute-start | bytes 393224 | tf_op jit(solution)/shard_map/ppermute | solution.py:154
  106.4 2.4 %collective-permute-done.33 = bf16[64,1024]{1,0:T(8,128)(2,1)S(1)} collective-permute-done((bf16[64,1024]{1,0:T(8,128)(2,1)S(1)}, bf16[64,1024]{1,0:T(8,128)(2,1)S(1)}, u32[]{:S(2)}, u32[]{:S(2)}) %collective-permute-start.33) | collective-permute-done | bytes 131104 | tf_op jit(solution)/shard_map/ppermute | solution.py:154
  108.8 2.6 %collective-permute-done.31.refs_0_.refs_2_ = bf16[64,1024]{1,0:T(8,128)(2,1)S(1)} collective-permute-done((bf16[64,1024]{1,0:T(8,128)(2,1)S(1)}, bf16[64,1024]{1,0:T(8,128)(2,1)S(1)}, u32[]{:S(2)}, u32[]{:S(2)}) %collective-permute-start.31) | collective-permute-done | bytes 131104 | tf_op jit(solution)/shard_map/ppermute | solution.py:154
  113.9 1.8 %slice_bitcast_fusion.2.block = bf16[1024,1024]{1,0:T(8,128)(2,1)S(1)} fusion(bf16[10,1024,1024]{2,1,0:T(8,128)(2,1)} %param.3), kind=kLoop, calls=%fused_computation.2 | loop fusion | bytes 4194304 | tf_op jit(solution)/shard_map/squeeze | solution.py:147
  115.6 0.9 shard_map.67
  116.5 1.8 %slice_bitcast_fusion.1.block = bf16[1024,1024]{1,0:T(8,128)(2,1)S(1)} fusion(bf16[10,1024,1024]{2,1,0:T(8,128)(2,1)} %param.3), kind=kLoop, calls=%fused_computation.1 | loop fusion | bytes 4194304 | tf_op jit(solution)/shard_map/squeeze | solution.py:147
  118.5 1.1 fusion.20
  120.3 1.8 %collective-permute-start.37 = (bf16[64,1024]{1,0:T(8,128)(2,1)S(1)}, bf16[64,1024]{1,0:T(8,128)(2,1)S(1)}, u32[]{:S(2)}, u32[]{:S(2)}) collective-permute-start(bf16[64,1024]{1,0:T(8,128)(2,1)S(1)} %shard_map.68), channel_id=1, source_target_pairs={{0,4},{4,0},{8,12},{12,8},{1,5},{5,1},{9,13},{13,9},{2,6},{6,2},{1... | collective-permute-start | bytes 393224 | tf_op jit(solution)/shard_map/ppermute | solution.py:154
  124.3 2.0 %collective-permute-done.37 = bf16[64,1024]{1,0:T(8,128)(2,1)S(1)} collective-permute-done((bf16[64,1024]{1,0:T(8,128)(2,1)S(1)}, bf16[64,1024]{1,0:T(8,128)(2,1)S(1)}, u32[]{:S(2)}, u32[]{:S(2)}) %collective-permute-start.37) | collective-permute-done | bytes 131104 | tf_op jit(solution)/shard_map/ppermute | solution.py:154
  127.1 1.8 %collective-permute-done.40.refs_0_ = bf16[64,1024]{1,0:T(8,128)(2,1)S(1)} collective-permute-done((bf16[64,1024]{1,0:T(8,128)(2,1)S(1)}, bf16[64,1024]{1,0:T(8,128)(2,1)S(1)}, u32[]{:S(2)}, u32[]{:S(2)}) %collective-permute-start.40) | collective-permute-done | bytes 131104 | tf_op jit(solution)/shard_map/ppermute | solution.py:154
  129.7 1.5 collective-permute-start.42
  131.2 3.5 %collective-permute-done.42 = bf16[64,1024]{1,0:T(8,128)(2,1)S(1)} collective-permute-done((bf16[64,1024]{1,0:T(8,128)(2,1)S(1)}, bf16[64,1024]{1,0:T(8,128)(2,1)S(1)}, u32[]{:S(2)}, u32[]{:S(2)}) %collective-permute-start.42) | collective-permute-done | bytes 131104 | tf_op jit(solution)/shard_map/ppermute | solution.py:154
  135.5 2.2 %collective-permute-start.39 = (bf16[64,1024]{1,0:T(8,128)(2,1)}, bf16[64,1024]{1,0:T(8,128)(2,1)S(1)}, u32[]{:S(2)}, u32[]{:S(2)}) collective-permute-start(bf16[64,1024]{1,0:T(8,128)(2,1)} %get-tuple-element.425), channel_id=1, source_target_pairs={{0,8},{4,12},{8,0},{12,4},{1,9},{5,13},{9,1},{13,5},{2,10},{6,14},... | collective-permute-start | bytes 393224 | tf_op jit(solution)/shard_map/ppermute | solution.py:154
  137.6 1.0 broadcast_select_fusion.3
  139.4 1.8 %collective-permute-start.45 = (bf16[64,1024]{1,0:T(8,128)(2,1)S(1)}, bf16[64,1024]{1,0:T(8,128)(2,1)S(1)}, u32[]{:S(2)}, u32[]{:S(2)}) collective-permute-start(bf16[64,1024]{1,0:T(8,128)(2,1)S(1)} %shard_map.72), channel_id=1, source_target_pairs={{0,4},{4,0},{8,12},{12,8},{1,5},{5,1},{9,13},{13,9},{2,6},{6,2},{1... | collective-permute-start | bytes 393224 | tf_op jit(solution)/shard_map/ppermute | solution.py:154
  141.2 4.2 %collective-permute-done.39 = bf16[64,1024]{1,0:T(8,128)(2,1)S(1)} collective-permute-done((bf16[64,1024]{1,0:T(8,128)(2,1)}, bf16[64,1024]{1,0:T(8,128)(2,1)S(1)}, u32[]{:S(2)}, u32[]{:S(2)}) %collective-permute-start.39) | collective-permute-done | bytes 131104 | tf_op jit(solution)/shard_map/ppermute | solution.py:154
  145.7 1.0 shard_map.73
  147.7 2.8 %collective-permute-done.44.refs_0_ = bf16[64,1024]{1,0:T(8,128)(2,1)S(1)} collective-permute-done((bf16[64,1024]{1,0:T(8,128)(2,1)S(1)}, bf16[64,1024]{1,0:T(8,128)(2,1)S(1)}, u32[]{:S(2)}, u32[]{:S(2)}) %collective-permute-start.44) | collective-permute-done | bytes 131104 | tf_op jit(solution)/shard_map/ppermute | solution.py:154
  151.3 1.5 collective-permute-start.47
  152.9 3.4 %collective-permute-done.47 = bf16[64,1024]{1,0:T(8,128)(2,1)S(1)} collective-permute-done((bf16[64,1024]{1,0:T(8,128)(2,1)S(1)}, bf16[64,1024]{1,0:T(8,128)(2,1)S(1)}, u32[]{:S(2)}, u32[]{:S(2)}) %collective-permute-start.47) | collective-permute-done | bytes 131104 | tf_op jit(solution)/shard_map/ppermute | solution.py:154
  156.5 1.3 collective-permute-done.48
  160.2 3.9 %collective-permute-done.49 = bf16[64,1024]{1,0:T(8,128)(2,1)S(1)} collective-permute-done((bf16[64,1024]{1,0:T(8,128)(2,1)S(1)}, bf16[64,1024]{1,0:T(8,128)(2,1)S(1)}, u32[]{:S(2)}, u32[]{:S(2)}) %collective-permute-start.49) | collective-permute-done | bytes 131104 | tf_op jit(solution)/shard_map/ppermute | solution.py:154
  164.2 2.4 %collective-permute-start.50 = (bf16[64,1024]{1,0:T(8,128)(2,1)S(1)}, bf16[64,1024]{1,0:T(8,128)(2,1)S(1)}, u32[]{:S(2)}, u32[]{:S(2)}) collective-permute-start(bf16[64,1024]{1,0:T(8,128)(2,1)S(1)} %broadcast_select_fusion), channel_id=1, source_target_pairs={{0,8},{4,12},{8,0},{12,4},{1,9},{5,13},{9,1},{13,5},{2,10},{6,14},... | collective-permute-start | bytes 393224 | tf_op jit(solution)/shard_map/ppermute | solution.py:154
  166.7 6.0 %collective-permute-done.50 = bf16[64,1024]{1,0:T(8,128)(2,1)S(1)} collective-permute-done((bf16[64,1024]{1,0:T(8,128)(2,1)S(1)}, bf16[64,1024]{1,0:T(8,128)(2,1)S(1)}, u32[]{:S(2)}, u32[]{:S(2)}) %collective-permute-start.50) | collective-permute-done | bytes 131104 | tf_op jit(solution)/shard_map/ppermute | solution.py:154
  (178 shorter events, 38.6 us)
Async XLA Ops:
  3.7 8.7 %collective-permute-start.1 = (bf16[64,1024]{1,0:T(8,128)(2,1)}, bf16[64,1024]{1,0:T(8,128)(2,1)S(1)}, u32[]{:S(2)}, u32[]{:S(2)}) collective-permute-start(bf16[64,1024]{1,0:T(8,128)(2,1)} %get-tuple-element.218), channel_id=1, source_target_pairs={{0,4},{4,0},{8,12},{12,8},{1,5},{5,1},{9,13},{13,9},{2,6},{6,2},{1... | collective-permute-start | bytes 393224 | tf_op jit(solution)/shard_map/ppermute | solution.py:154
  6.8 3.9 %copy-start.2 = (bf16[5,1024,256]{2,1,0:T(8,128)(2,1)S(1)}, bf16[5,1024,256]{2,1,0:T(8,128)(2,1)}, u32[]{:S(2)}) copy-start(bf16[5,1024,256]{2,1,0:T(8,128)(2,1)} %sides.3) | copy-start | bytes 7864324
  10.6 12.2 %collective-permute-start = (bf16[64,1024]{1,0:T(8,128)(2,1)}, bf16[64,1024]{1,0:T(8,128)(2,1)S(1)}, u32[]{:S(2)}, u32[]{:S(2)}) collective-permute-start(bf16[64,1024]{1,0:T(8,128)(2,1)} %get-tuple-element.217), channel_id=1, source_target_pairs={{0,4},{4,0},{8,12},{12,8},{1,5},{5,1},{9,13},{13,9},{2,6},{6,2},{1... | collective-permute-start | bytes 393224 | tf_op jit(solution)/shard_map/ppermute | solution.py:154
  12.4 8.9 %collective-permute-start.2 = (bf16[64,1024]{1,0:T(8,128)(2,1)S(1)}, bf16[64,1024]{1,0:T(8,128)(2,1)S(1)}, u32[]{:S(2)}, u32[]{:S(2)}) collective-permute-start(bf16[64,1024]{1,0:T(8,128)(2,1)S(1)} %get-tuple-element.451), channel_id=1, source_target_pairs={{0,8},{4,12},{8,0},{12,4},{1,9},{5,13},{9,1},{13,5},{2,10},{6,14},... | collective-permute-start | bytes 393224 | tf_op jit(solution)/shard_map/ppermute | solution.py:154
  21.3 5.1 %collective-permute-start.4 = (bf16[64,1024]{1,0:T(8,128)(2,1)S(1)}, bf16[64,1024]{1,0:T(8,128)(2,1)S(1)}, u32[]{:S(2)}, u32[]{:S(2)}) collective-permute-start(bf16[64,1024]{1,0:T(8,128)(2,1)S(1)} %add_convert_fusion.8.refs_0_.refs_1_), channel_id=1, source_target_pairs={{0,4},{4,0},{8,12},{12,8},{1,5},{5,1},{9,13},{13,9},{2,6},{6,2},{1... | collective-permute-start | bytes 393224 | tf_op jit(solution)/shard_map/ppermute | solution.py:154
  22.8 4.4 %collective-permute-start.5 = (bf16[64,1024]{1,0:T(8,128)(2,1)S(1)}, bf16[64,1024]{1,0:T(8,128)(2,1)S(1)}, u32[]{:S(2)}, u32[]{:S(2)}) collective-permute-start(bf16[64,1024]{1,0:T(8,128)(2,1)S(1)} %shard_map.40), channel_id=1, source_target_pairs={{0,1},{1,0},{2,3},{3,2},{4,5},{5,4},{6,7},{7,6},{8,9},{9,8},{10,11... | collective-permute-start | bytes 393224 | tf_op jit(solution)/shard_map/ppermute | solution.py:154
  22.9 11.1 %collective-permute-start.3 = (bf16[64,1024]{1,0:T(8,128)(2,1)S(1)}, bf16[64,1024]{1,0:T(8,128)(2,1)S(1)}, u32[]{:S(2)}, u32[]{:S(2)}) collective-permute-start(bf16[64,1024]{1,0:T(8,128)(2,1)S(1)} %get-tuple-element.449), channel_id=1, source_target_pairs={{0,8},{4,12},{8,0},{12,4},{1,9},{5,13},{9,1},{13,5},{2,10},{6,14},... | collective-permute-start | bytes 393224 | tf_op jit(solution)/shard_map/ppermute | solution.py:154
  27.2 5.7 %collective-permute-start.6 = (bf16[64,1024]{1,0:T(8,128)(2,1)S(1)}, bf16[64,1024]{1,0:T(8,128)(2,1)S(1)}, u32[]{:S(2)}, u32[]{:S(2)}) collective-permute-start(bf16[64,1024]{1,0:T(8,128)(2,1)S(1)} %get-tuple-element.447), channel_id=1, source_target_pairs={{0,2},{1,3},{2,0},{3,1},{4,6},{5,7},{6,4},{7,5},{8,10},{9,11},{10,... | collective-permute-start | bytes 393224 | tf_op jit(solution)/shard_map/ppermute | solution.py:154
  32.9 3.8 %collective-permute-start.8 = (bf16[64,1024]{1,0:T(8,128)(2,1)S(1)}, bf16[64,1024]{1,0:T(8,128)(2,1)S(1)}, u32[]{:S(2)}, u32[]{:S(2)}) collective-permute-start(bf16[64,1024]{1,0:T(8,128)(2,1)S(1)} %subtract_convert_fusion.7.refs_0_), channel_id=1, source_target_pairs={{0,1},{1,0},{2,3},{3,2},{4,5},{5,4},{6,7},{7,6},{8,9},{9,8},{10,11... | collective-permute-start | bytes 393224 | tf_op jit(solution)/shard_map/ppermute | solution.py:154
  33.7 6.4 %collective-permute-start.9 = (bf16[64,1024]{1,0:T(8,128)(2,1)S(1)}, bf16[64,1024]{1,0:T(8,128)(2,1)S(1)}, u32[]{:S(2)}, u32[]{:S(2)}) collective-permute-start(bf16[64,1024]{1,0:T(8,128)(2,1)S(1)} %shard_map.42), channel_id=1, source_target_pairs={{0,4},{4,0},{8,12},{12,8},{1,5},{5,1},{9,13},{13,9},{2,6},{6,2},{1... | collective-permute-start | bytes 393224 | tf_op jit(solution)/shard_map/ppermute | solution.py:154
  34.1 8.4 %collective-permute-start.7 = (bf16[64,1024]{1,0:T(8,128)(2,1)S(1)}, bf16[64,1024]{1,0:T(8,128)(2,1)S(1)}, u32[]{:S(2)}, u32[]{:S(2)}) collective-permute-start(bf16[64,1024]{1,0:T(8,128)(2,1)S(1)} %add_convert_fusion.7.refs_0_.refs_3_), channel_id=1, source_target_pairs={{0,4},{4,0},{8,12},{12,8},{1,5},{5,1},{9,13},{13,9},{2,6},{6,2},{1... | collective-permute-start | bytes 393224 | tf_op jit(solution)/shard_map/ppermute | solution.py:154
  36.6 6.6 %collective-permute-start.10 = (bf16[64,1024]{1,0:T(8,128)(2,1)S(1)}, bf16[64,1024]{1,0:T(8,128)(2,1)S(1)}, u32[]{:S(2)}, u32[]{:S(2)}) collective-permute-start(bf16[64,1024]{1,0:T(8,128)(2,1)S(1)} %shard_map.43), channel_id=1, source_target_pairs={{0,1},{1,0},{2,3},{3,2},{4,5},{5,4},{6,7},{7,6},{8,9},{9,8},{10,11... | collective-permute-start | bytes 393224 | tf_op jit(solution)/shard_map/ppermute | solution.py:154
  36.7 17.7 %slice-start = ((s8[10485760]{0:T(1024)(128)(4,1)}), s8[4194304]{0:T(1024)(128)(4,1)S(1)}, s32[]{:S(2)}) async-start(s8[10485760]{0:T(1024)(128)(4,1)} %bitcast.67), calls=%async_computation | async-start | bytes 8388608
  43.3 11.2 %slice-start.1 = ((s8[10485760]{0:T(1024)(128)(4,1)}), s8[4194304]{0:T(1024)(128)(4,1)S(1)}, s32[]{:S(2)}) async-start(s8[10485760]{0:T(1024)(128)(4,1)} %bitcast.67), calls=%async_computation.1 | async-start | bytes 8388608
  43.3 7.6 %collective-permute-start.11 = (bf16[64,1024]{1,0:T(8,128)(2,1)S(1)}, bf16[64,1024]{1,0:T(8,128)(2,1)S(1)}, u32[]{:S(2)}, u32[]{:S(2)}) collective-permute-start(bf16[64,1024]{1,0:T(8,128)(2,1)S(1)} %get-tuple-element.443), channel_id=1, source_target_pairs={{0,2},{1,3},{2,0},{3,1},{4,6},{5,7},{6,4},{7,5},{8,10},{9,11},{10,... | collective-permute-start | bytes 393224 | tf_op jit(solution)/shard_map/ppermute | solution.py:154
  44.9 9.8 %collective-permute-start.14 = (bf16[64,1024]{1,0:T(8,128)(2,1)S(1)}, bf16[64,1024]{1,0:T(8,128)(2,1)S(1)}, u32[]{:S(2)}, u32[]{:S(2)}) collective-permute-start(bf16[64,1024]{1,0:T(8,128)(2,1)S(1)} %get-tuple-element.445), channel_id=1, source_target_pairs={{0,8},{4,12},{8,0},{12,4},{1,9},{5,13},{9,1},{13,5},{2,10},{6,14},... | collective-permute-start | bytes 393224 | tf_op jit(solution)/shard_map/ppermute | solution.py:154
  51.0 2.7 %collective-permute-start.12 = (bf16[64,1024]{1,0:T(8,128)(2,1)S(1)}, bf16[64,1024]{1,0:T(8,128)(2,1)S(1)}, u32[]{:S(2)}, u32[]{:S(2)}) collective-permute-start(bf16[64,1024]{1,0:T(8,128)(2,1)S(1)} %subtract_convert_fusion.6.refs_0_), channel_id=1, source_target_pairs={{0,1},{1,0},{2,3},{3,2},{4,5},{5,4},{6,7},{7,6},{8,9},{9,8},{10,11... | collective-permute-start | bytes 393224 | tf_op jit(solution)/shard_map/ppermute | solution.py:154
  51.9 6.2 %collective-permute-start.13 = (bf16[64,1024]{1,0:T(8,128)(2,1)S(1)}, bf16[64,1024]{1,0:T(8,128)(2,1)S(1)}, u32[]{:S(2)}, u32[]{:S(2)}) collective-permute-start(bf16[64,1024]{1,0:T(8,128)(2,1)S(1)} %shard_map.47), channel_id=1, source_target_pairs={{0,4},{4,0},{8,12},{12,8},{1,5},{5,1},{9,13},{13,9},{2,6},{6,2},{1... | collective-permute-start | bytes 393224 | tf_op jit(solution)/shard_map/ppermute | solution.py:154
  54.7 5.9 %collective-permute-start.16 = (bf16[64,1024]{1,0:T(8,128)(2,1)S(1)}, bf16[64,1024]{1,0:T(8,128)(2,1)S(1)}, u32[]{:S(2)}, u32[]{:S(2)}) collective-permute-start(bf16[64,1024]{1,0:T(8,128)(2,1)S(1)} %add_convert_fusion.6.refs_0_.refs_1_), channel_id=1, source_target_pairs={{0,4},{4,0},{8,12},{12,8},{1,5},{5,1},{9,13},{13,9},{2,6},{6,2},{1... | collective-permute-start | bytes 393224 | tf_op jit(solution)/shard_map/ppermute | solution.py:154
  56.0 5.4 %collective-permute-start.17 = (bf16[64,1024]{1,0:T(8,128)(2,1)S(1)}, bf16[64,1024]{1,0:T(8,128)(2,1)S(1)}, u32[]{:S(2)}, u32[]{:S(2)}) collective-permute-start(bf16[64,1024]{1,0:T(8,128)(2,1)S(1)} %shard_map.49), channel_id=1, source_target_pairs={{0,1},{1,0},{2,3},{3,2},{4,5},{5,4},{6,7},{7,6},{8,9},{9,8},{10,11... | collective-permute-start | bytes 393224 | tf_op jit(solution)/shard_map/ppermute | solution.py:154
  58.1 11.3 %collective-permute-start.15 = (bf16[64,1024]{1,0:T(8,128)(2,1)S(1)}, bf16[64,1024]{1,0:T(8,128)(2,1)S(1)}, u32[]{:S(2)}, u32[]{:S(2)}) collective-permute-start(bf16[64,1024]{1,0:T(8,128)(2,1)S(1)} %get-tuple-element.441), channel_id=1, source_target_pairs={{0,8},{4,12},{8,0},{12,4},{1,9},{5,13},{9,1},{13,5},{2,10},{6,14},... | collective-permute-start | bytes 393224 | tf_op jit(solution)/shard_map/ppermute | solution.py:154
  61.5 5.1 %collective-permute-start.18 = (bf16[64,1024]{1,0:T(8,128)(2,1)S(1)}, bf16[64,1024]{1,0:T(8,128)(2,1)S(1)}, u32[]{:S(2)}, u32[]{:S(2)}) collective-permute-start(bf16[64,1024]{1,0:T(8,128)(2,1)S(1)} %get-tuple-element.439), channel_id=1, source_target_pairs={{0,2},{1,3},{2,0},{3,1},{4,6},{5,7},{6,4},{7,5},{8,10},{9,11},{10,... | collective-permute-start | bytes 393224 | tf_op jit(solution)/shard_map/ppermute | solution.py:154
  66.7 3.9 %collective-permute-start.20 = (bf16[64,1024]{1,0:T(8,128)(2,1)S(1)}, bf16[64,1024]{1,0:T(8,128)(2,1)S(1)}, u32[]{:S(2)}, u32[]{:S(2)}) collective-permute-start(bf16[64,1024]{1,0:T(8,128)(2,1)S(1)} %subtract_convert_fusion.5.refs_0_), channel_id=1, source_target_pairs={{0,1},{1,0},{2,3},{3,2},{4,5},{5,4},{6,7},{7,6},{8,9},{9,8},{10,11... | collective-permute-start | bytes 393224 | tf_op jit(solution)/shard_map/ppermute | solution.py:154
  67.5 6.4 %collective-permute-start.21 = (bf16[64,1024]{1,0:T(8,128)(2,1)S(1)}, bf16[64,1024]{1,0:T(8,128)(2,1)S(1)}, u32[]{:S(2)}, u32[]{:S(2)}) collective-permute-start(bf16[64,1024]{1,0:T(8,128)(2,1)S(1)} %shard_map.52), channel_id=1, source_target_pairs={{0,4},{4,0},{8,12},{12,8},{1,5},{5,1},{9,13},{13,9},{2,6},{6,2},{1... | collective-permute-start | bytes 393224 | tf_op jit(solution)/shard_map/ppermute | solution.py:154
  69.4 6.9 %collective-permute-start.19 = (bf16[64,1024]{1,0:T(8,128)(2,1)S(1)}, bf16[64,1024]{1,0:T(8,128)(2,1)S(1)}, u32[]{:S(2)}, u32[]{:S(2)}) collective-permute-start(bf16[64,1024]{1,0:T(8,128)(2,1)S(1)} %add_convert_fusion.5.refs_0_.refs_3_), channel_id=1, source_target_pairs={{0,4},{4,0},{8,12},{12,8},{1,5},{5,1},{9,13},{13,9},{2,6},{6,2},{1... | collective-permute-start | bytes 393224 | tf_op jit(solution)/shard_map/ppermute | solution.py:154
  70.4 6.6 %collective-permute-start.22 = (bf16[64,1024]{1,0:T(8,128)(2,1)S(1)}, bf16[64,1024]{1,0:T(8,128)(2,1)S(1)}, u32[]{:S(2)}, u32[]{:S(2)}) collective-permute-start(bf16[64,1024]{1,0:T(8,128)(2,1)S(1)} %shard_map.53), channel_id=1, source_target_pairs={{0,1},{1,0},{2,3},{3,2},{4,5},{5,4},{6,7},{7,6},{8,9},{9,8},{10,11... | collective-permute-start | bytes 393224 | tf_op jit(solution)/shard_map/ppermute | solution.py:154
  77.1 7.3 %collective-permute-start.23 = (bf16[64,1024]{1,0:T(8,128)(2,1)S(1)}, bf16[64,1024]{1,0:T(8,128)(2,1)S(1)}, u32[]{:S(2)}, u32[]{:S(2)}) collective-permute-start(bf16[64,1024]{1,0:T(8,128)(2,1)S(1)} %get-tuple-element.435), channel_id=1, source_target_pairs={{0,2},{1,3},{2,0},{3,1},{4,6},{5,7},{6,4},{7,5},{8,10},{9,11},{10,... | collective-permute-start | bytes 393224 | tf_op jit(solution)/shard_map/ppermute | solution.py:154
  77.7 10.1 %collective-permute-start.26 = (bf16[64,1024]{1,0:T(8,128)(2,1)S(1)}, bf16[64,1024]{1,0:T(8,128)(2,1)S(1)}, u32[]{:S(2)}, u32[]{:S(2)}) collective-permute-start(bf16[64,1024]{1,0:T(8,128)(2,1)S(1)} %get-tuple-element.437), channel_id=1, source_target_pairs={{0,8},{4,12},{8,0},{12,4},{1,9},{5,13},{9,1},{13,5},{2,10},{6,14},... | collective-permute-start | bytes 393224 | tf_op jit(solution)/shard_map/ppermute | solution.py:154
  84.5 2.4 %collective-permute-start.24 = (bf16[64,1024]{1,0:T(8,128)(2,1)S(1)}, bf16[64,1024]{1,0:T(8,128)(2,1)S(1)}, u32[]{:S(2)}, u32[]{:S(2)}) collective-permute-start(bf16[64,1024]{1,0:T(8,128)(2,1)S(1)} %subtract_convert_fusion.4.refs_0_), channel_id=1, source_target_pairs={{0,1},{1,0},{2,3},{3,2},{4,5},{5,4},{6,7},{7,6},{8,9},{9,8},{10,11... | collective-permute-start | bytes 393224 | tf_op jit(solution)/shard_map/ppermute | solution.py:154
  85.4 6.4 %collective-permute-start.25 = (bf16[64,1024]{1,0:T(8,128)(2,1)S(1)}, bf16[64,1024]{1,0:T(8,128)(2,1)S(1)}, u32[]{:S(2)}, u32[]{:S(2)}) collective-permute-start(bf16[64,1024]{1,0:T(8,128)(2,1)S(1)} %shard_map.57), channel_id=1, source_target_pairs={{0,4},{4,0},{8,12},{12,8},{1,5},{5,1},{9,13},{13,9},{2,6},{6,2},{1... | collective-permute-start | bytes 393224 | tf_op jit(solution)/shard_map/ppermute | solution.py:154
  87.9 6.3 %collective-permute-start.28 = (bf16[64,1024]{1,0:T(8,128)(2,1)S(1)}, bf16[64,1024]{1,0:T(8,128)(2,1)S(1)}, u32[]{:S(2)}, u32[]{:S(2)}) collective-permute-start(bf16[64,1024]{1,0:T(8,128)(2,1)S(1)} %add_convert_fusion.4.refs_0_.refs_1_), channel_id=1, source_target_pairs={{0,4},{4,0},{8,12},{12,8},{1,5},{5,1},{9,13},{13,9},{2,6},{6,2},{1... | collective-permute-start | bytes 393224 | tf_op jit(solution)/shard_map/ppermute | solution.py:154
  89.4 5.6 %collective-permute-start.29 = (bf16[64,1024]{1,0:T(8,128)(2,1)S(1)}, bf16[64,1024]{1,0:T(8,128)(2,1)S(1)}, u32[]{:S(2)}, u32[]{:S(2)}) collective-permute-start(bf16[64,1024]{1,0:T(8,128)(2,1)S(1)} %shard_map.59), channel_id=1, source_target_pairs={{0,1},{1,0},{2,3},{3,2},{4,5},{5,4},{6,7},{7,6},{8,9},{9,8},{10,11... | collective-permute-start | bytes 393224 | tf_op jit(solution)/shard_map/ppermute | solution.py:154
  91.8 12.6 %collective-permute-start.27 = (bf16[64,1024]{1,0:T(8,128)(2,1)S(1)}, bf16[64,1024]{1,0:T(8,128)(2,1)S(1)}, u32[]{:S(2)}, u32[]{:S(2)}) collective-permute-start(bf16[64,1024]{1,0:T(8,128)(2,1)S(1)} %get-tuple-element.433), channel_id=1, source_target_pairs={{0,8},{4,12},{8,0},{12,4},{1,9},{5,13},{9,1},{13,5},{2,10},{6,14},... | collective-permute-start | bytes 393224 | tf_op jit(solution)/shard_map/ppermute | solution.py:154
  94.2 21.4 %copy-start.3 = (bf16[64,1024]{1,0:T(8,128)(2,1)}, bf16[64,1024]{1,0:T(8,128)(2,1)S(1)}, u32[]{:S(2)}) copy-start(bf16[64,1024]{1,0:T(8,128)(2,1)S(1)} %collective-permute-done.28.refs_0_) | copy-start | bytes 393220
  95.1 6.3 %collective-permute-start.30 = (bf16[64,1024]{1,0:T(8,128)(2,1)S(1)}, bf16[64,1024]{1,0:T(8,128)(2,1)S(1)}, u32[]{:S(2)}, u32[]{:S(2)}) collective-permute-start(bf16[64,1024]{1,0:T(8,128)(2,1)S(1)} %get-tuple-element.431), channel_id=1, source_target_pairs={{0,2},{1,3},{2,0},{3,1},{4,6},{5,7},{6,4},{7,5},{8,10},{9,11},{10,... | collective-permute-start | bytes 393224 | tf_op jit(solution)/shard_map/ppermute | solution.py:154
  101.4 4.2 %collective-permute-start.32 = (bf16[64,1024]{1,0:T(8,128)(2,1)S(1)}, bf16[64,1024]{1,0:T(8,128)(2,1)S(1)}, u32[]{:S(2)}, u32[]{:S(2)}) collective-permute-start(bf16[64,1024]{1,0:T(8,128)(2,1)S(1)} %subtract_convert_fusion.3.refs_0_), channel_id=1, source_target_pairs={{0,1},{1,0},{2,3},{3,2},{4,5},{5,4},{6,7},{7,6},{8,9},{9,8},{10,11... | collective-permute-start | bytes 393224 | tf_op jit(solution)/shard_map/ppermute | solution.py:154
  102.2 6.5 %collective-permute-start.33 = (bf16[64,1024]{1,0:T(8,128)(2,1)S(1)}, bf16[64,1024]{1,0:T(8,128)(2,1)S(1)}, u32[]{:S(2)}, u32[]{:S(2)}) collective-permute-start(bf16[64,1024]{1,0:T(8,128)(2,1)S(1)} %shard_map.63), channel_id=1, source_target_pairs={{0,4},{4,0},{8,12},{12,8},{1,5},{5,1},{9,13},{13,9},{2,6},{6,2},{1... | collective-permute-start | bytes 393224 | tf_op jit(solution)/shard_map/ppermute | solution.py:154
  104.5 6.9 %collective-permute-start.31 = (bf16[64,1024]{1,0:T(8,128)(2,1)S(1)}, bf16[64,1024]{1,0:T(8,128)(2,1)S(1)}, u32[]{:S(2)}, u32[]{:S(2)}) collective-permute-start(bf16[64,1024]{1,0:T(8,128)(2,1)S(1)} %add_convert_fusion.3.refs_0_.refs_3_), channel_id=1, source_target_pairs={{0,4},{4,0},{8,12},{12,8},{1,5},{5,1},{9,13},{13,9},{2,6},{6,2},{1... | collective-permute-start | bytes 393224 | tf_op jit(solution)/shard_map/ppermute | solution.py:154
  105.4 6.8 %collective-permute-start.34 = (bf16[64,1024]{1,0:T(8,128)(2,1)S(1)}, bf16[64,1024]{1,0:T(8,128)(2,1)S(1)}, u32[]{:S(2)}, u32[]{:S(2)}) collective-permute-start(bf16[64,1024]{1,0:T(8,128)(2,1)S(1)} %shard_map.64), channel_id=1, source_target_pairs={{0,1},{1,0},{2,3},{3,2},{4,5},{5,4},{6,7},{7,6},{8,9},{9,8},{10,11... | collective-permute-start | bytes 393224 | tf_op jit(solution)/shard_map/ppermute | solution.py:154
  111.4 4.2 %copy-start.5 = (bf16[64,1024]{1,0:T(8,128)(2,1)}, bf16[64,1024]{1,0:T(8,128)(2,1)S(1)}, u32[]{:S(2)}) copy-start(bf16[64,1024]{1,0:T(8,128)(2,1)S(1)} %collective-permute-done.31.refs_0_.refs_2_) | copy-start | bytes 393220
  112.2 6.1 %collective-permute-start.35 = (bf16[64,1024]{1,0:T(8,128)(2,1)S(1)}, bf16[64,1024]{1,0:T(8,128)(2,1)S(1)}, u32[]{:S(2)}, u32[]{:S(2)}) collective-permute-start(bf16[64,1024]{1,0:T(8,128)(2,1)S(1)} %get-tuple-element.427), channel_id=1, source_target_pairs={{0,2},{1,3},{2,0},{3,1},{4,6},{5,7},{6,4},{7,5},{8,10},{9,11},{10,... | collective-permute-start | bytes 393224 | tf_op jit(solution)/shard_map/ppermute | solution.py:154
  113.0 10.0 %collective-permute-start.38 = (bf16[64,1024]{1,0:T(8,128)(2,1)S(1)}, bf16[64,1024]{1,0:T(8,128)(2,1)S(1)}, u32[]{:S(2)}, u32[]{:S(2)}) collective-permute-start(bf16[64,1024]{1,0:T(8,128)(2,1)S(1)} %get-tuple-element.429), channel_id=1, source_target_pairs={{0,8},{4,12},{8,0},{12,4},{1,9},{5,13},{9,1},{13,5},{2,10},{6,14},... | collective-permute-start | bytes 393224 | tf_op jit(solution)/shard_map/ppermute | solution.py:154
  118.3 10.6 %copy-start = (bf16[1024,1024]{1,0:T(8,128)(2,1)}, bf16[1024,1024]{1,0:T(8,128)(2,1)S(1)}, u32[]{:S(2)}) copy-start(bf16[1024,1024]{1,0:T(8,128)(2,1)S(1)} %slice_bitcast_fusion.1.block) | copy-start | bytes 6291460
  118.4 3.7 %collective-permute-start.36 = (bf16[64,1024]{1,0:T(8,128)(2,1)S(1)}, bf16[64,1024]{1,0:T(8,128)(2,1)S(1)}, u32[]{:S(2)}, u32[]{:S(2)}) collective-permute-start(bf16[64,1024]{1,0:T(8,128)(2,1)S(1)} %subtract_convert_fusion.2.refs_0_), channel_id=1, source_target_pairs={{0,1},{1,0},{2,3},{3,2},{4,5},{5,4},{6,7},{7,6},{8,9},{9,8},{10,11... | collective-permute-start | bytes 393224 | tf_op jit(solution)/shard_map/ppermute | solution.py:154
  120.3 6.0 %collective-permute-start.37 = (bf16[64,1024]{1,0:T(8,128)(2,1)S(1)}, bf16[64,1024]{1,0:T(8,128)(2,1)S(1)}, u32[]{:S(2)}, u32[]{:S(2)}) collective-permute-start(bf16[64,1024]{1,0:T(8,128)(2,1)S(1)} %shard_map.68), channel_id=1, source_target_pairs={{0,4},{4,0},{8,12},{12,8},{1,5},{5,1},{9,13},{13,9},{2,6},{6,2},{1... | collective-permute-start | bytes 393224 | tf_op jit(solution)/shard_map/ppermute | solution.py:154
  123.1 5.8 %collective-permute-start.40 = (bf16[64,1024]{1,0:T(8,128)(2,1)S(1)}, bf16[64,1024]{1,0:T(8,128)(2,1)S(1)}, u32[]{:S(2)}, u32[]{:S(2)}) collective-permute-start(bf16[64,1024]{1,0:T(8,128)(2,1)S(1)} %add_convert_fusion.2.refs_0_), channel_id=1, source_target_pairs={{0,4},{4,0},{8,12},{12,8},{1,5},{5,1},{9,13},{13,9},{2,6},{6,2},{1... | collective-permute-start | bytes 393224 | tf_op jit(solution)/shard_map/ppermute | solution.py:154
  124.2 5.5 %collective-permute-start.41 = (bf16[64,1024]{1,0:T(8,128)(2,1)S(1)}, bf16[64,1024]{1,0:T(8,128)(2,1)S(1)}, u32[]{:S(2)}, u32[]{:S(2)}) collective-permute-start(bf16[64,1024]{1,0:T(8,128)(2,1)S(1)} %shard_map.70), channel_id=1, source_target_pairs={{0,1},{1,0},{2,3},{3,2},{4,5},{5,4},{6,7},{7,6},{8,9},{9,8},{10,11... | collective-permute-start | bytes 393224 | tf_op jit(solution)/shard_map/ppermute | solution.py:154
  128.9 6.6 %copy-start.9 = (bf16[64,1024]{1,0:T(8,128)(2,1)}, bf16[64,1024]{1,0:T(8,128)(2,1)S(1)}, u32[]{:S(2)}) copy-start(bf16[64,1024]{1,0:T(8,128)(2,1)S(1)} %collective-permute-done.40.refs_0_) | copy-start | bytes 393220
  129.7 5.0 %collective-permute-start.42 = (bf16[64,1024]{1,0:T(8,128)(2,1)S(1)}, bf16[64,1024]{1,0:T(8,128)(2,1)S(1)}, u32[]{:S(2)}, u32[]{:S(2)}) collective-permute-start(bf16[64,1024]{1,0:T(8,128)(2,1)S(1)} %get-tuple-element.423), channel_id=1, source_target_pairs={{0,2},{1,3},{2,0},{3,1},{4,6},{5,7},{6,4},{7,5},{8,10},{9,11},{10,... | collective-permute-start | bytes 393224 | tf_op jit(solution)/shard_map/ppermute | solution.py:154
  135.4 2.2 %collective-permute-start.43 = (bf16[64,1024]{1,0:T(8,128)(2,1)}, bf16[64,1024]{1,0:T(8,128)(2,1)}, u32[]{:S(2)}, u32[]{:S(2)}) collective-permute-start(bf16[64,1024]{1,0:T(8,128)(2,1)} %subtract_convert_fusion.1), channel_id=1, source_target_pairs={{0,1},{1,0},{2,3},{3,2},{4,5},{5,4},{6,7},{7,6},{8,9},{9,8},{10,11... | collective-permute-start | bytes 393224 | tf_op jit(solution)/shard_map/ppermute | solution.py:154
  135.4 10.0 %copy-start.11 = (f32[64,1024]{1,0:T(8,128)S(1)}, f32[64,1024]{1,0:T(8,128)}, u32[]{:S(2)}) copy-start(f32[64,1024]{1,0:T(8,128)} %get-tuple-element.396) | copy-start | bytes 786436
  135.4 10.3 %copy-start.1 = (bf16[1024,1024]{1,0:T(8,128)(2,1)S(1)}, bf16[1024,1024]{1,0:T(8,128)(2,1)}, u32[]{:S(2)}) copy-start(bf16[1024,1024]{1,0:T(8,128)(2,1)} %copy-done) | copy-start | bytes 6291460
  135.4 10.3 %copy-start.7 = (f32[64,1024]{1,0:T(8,128)S(1)}, f32[64,1024]{1,0:T(8,128)}, u32[]{:S(2)}) copy-start(f32[64,1024]{1,0:T(8,128)} %get-tuple-element.400.refs_1_) | copy-start | bytes 786436
  135.5 9.9 %collective-permute-start.39 = (bf16[64,1024]{1,0:T(8,128)(2,1)}, bf16[64,1024]{1,0:T(8,128)(2,1)S(1)}, u32[]{:S(2)}, u32[]{:S(2)}) collective-permute-start(bf16[64,1024]{1,0:T(8,128)(2,1)} %get-tuple-element.425), channel_id=1, source_target_pairs={{0,8},{4,12},{8,0},{12,4},{1,9},{5,13},{9,1},{13,5},{2,10},{6,14},... | collective-permute-start | bytes 393224 | tf_op jit(solution)/shard_map/ppermute | solution.py:154
  139.4 8.2 %collective-permute-start.45 = (bf16[64,1024]{1,0:T(8,128)(2,1)S(1)}, bf16[64,1024]{1,0:T(8,128)(2,1)S(1)}, u32[]{:S(2)}, u32[]{:S(2)}) collective-permute-start(bf16[64,1024]{1,0:T(8,128)(2,1)S(1)} %shard_map.72), channel_id=1, source_target_pairs={{0,4},{4,0},{8,12},{12,8},{1,5},{5,1},{9,13},{13,9},{2,6},{6,2},{1... | collective-permute-start | bytes 393224 | tf_op jit(solution)/shard_map/ppermute | solution.py:154
  145.4 5.0 %collective-permute-start.44 = (bf16[64,1024]{1,0:T(8,128)(2,1)S(1)}, bf16[64,1024]{1,0:T(8,128)(2,1)S(1)}, u32[]{:S(2)}, u32[]{:S(2)}) collective-permute-start(bf16[64,1024]{1,0:T(8,128)(2,1)S(1)} %add_convert_fusion.1.refs_0_), channel_id=1, source_target_pairs={{0,4},{4,0},{8,12},{12,8},{1,5},{5,1},{9,13},{13,9},{2,6},{6,2},{1... | collective-permute-start | bytes 393224 | tf_op jit(solution)/shard_map/ppermute | solution.py:154
  146.8 4.5 %collective-permute-start.46 = (bf16[64,1024]{1,0:T(8,128)(2,1)S(1)}, bf16[64,1024]{1,0:T(8,128)(2,1)S(1)}, u32[]{:S(2)}, u32[]{:S(2)}) collective-permute-start(bf16[64,1024]{1,0:T(8,128)(2,1)S(1)} %shard_map.73), channel_id=1, source_target_pairs={{0,1},{1,0},{2,3},{3,2},{4,5},{5,4},{6,7},{7,6},{8,9},{9,8},{10,11... | collective-permute-start | bytes 393224 | tf_op jit(solution)/shard_map/ppermute | solution.py:154
  150.5 5.9 %copy-start.12 = (bf16[64,1024]{1,0:T(8,128)(2,1)S(1)}, bf16[64,1024]{1,0:T(8,128)(2,1)}, u32[]{:S(2)}) copy-start(bf16[64,1024]{1,0:T(8,128)(2,1)} %get-tuple-element.410) | copy-start | bytes 393220
  151.3 5.0 %collective-permute-start.47 = (bf16[64,1024]{1,0:T(8,128)(2,1)S(1)}, bf16[64,1024]{1,0:T(8,128)(2,1)S(1)}, u32[]{:S(2)}, u32[]{:S(2)}) collective-permute-start(bf16[64,1024]{1,0:T(8,128)(2,1)S(1)} %get-tuple-element.421), channel_id=1, source_target_pairs={{0,2},{1,3},{2,0},{3,1},{4,6},{5,7},{6,4},{7,5},{8,10},{9,11},{10,... | collective-permute-start | bytes 393224 | tf_op jit(solution)/shard_map/ppermute | solution.py:154
  156.4 1.4 collective-permute-start.48
  158.5 8.0 %copy-start.10 = (bf16[64,1024]{1,0:T(8,128)(2,1)S(1)}, bf16[64,1024]{1,0:T(8,128)(2,1)}, u32[]{:S(2)}) copy-start(bf16[64,1024]{1,0:T(8,128)(2,1)} %copy-done.9) | copy-start | bytes 393220
  158.6 5.6 %collective-permute-start.49 = (bf16[64,1024]{1,0:T(8,128)(2,1)S(1)}, bf16[64,1024]{1,0:T(8,128)(2,1)S(1)}, u32[]{:S(2)}, u32[]{:S(2)}) collective-permute-start(bf16[64,1024]{1,0:T(8,128)(2,1)S(1)} %shard_map.76), channel_id=1, source_target_pairs={{0,4},{4,0},{8,12},{12,8},{1,5},{5,1},{9,13},{13,9},{2,6},{6,2},{1... | collective-permute-start | bytes 393224 | tf_op jit(solution)/shard_map/ppermute | solution.py:154
  164.2 8.5 %collective-permute-start.50 = (bf16[64,1024]{1,0:T(8,128)(2,1)S(1)}, bf16[64,1024]{1,0:T(8,128)(2,1)S(1)}, u32[]{:S(2)}, u32[]{:S(2)}) collective-permute-start(bf16[64,1024]{1,0:T(8,128)(2,1)S(1)} %broadcast_select_fusion), channel_id=1, source_target_pairs={{0,8},{4,12},{8,0},{12,4},{1,9},{5,13},{9,1},{13,5},{2,10},{6,14},... | collective-permute-start | bytes 393224 | tf_op jit(solution)/shard_map/ppermute | solution.py:154
  166.7 6.1 %copy-start.15 = (bf16[5,1024,64]{1,2,0:T(8,128)(2,1)}, bf16[5,1024,64]{1,2,0:T(8,128)(2,1)S(1)}, u32[]{:S(2)}) copy-start(bf16[5,1024,64]{1,2,0:T(8,128)(2,1)S(1)} %bitcast_dynamic-update-slice_fusion) | copy-start | bytes 1966084
  (6 other events, 19.0 us)

commit v6 on v4

--- a/solution.py
+++ b/solution.py
@@ -21,7 +21,7 @@
 
 
 def params():
-    return pltpu.CompilerParams(vmem_limit_bytes=16 * 2**20)
+    return pltpu.CompilerParams(vmem_limit_bytes=8 * 2**20)
 
 
 def times_transposed(left, right):
@@ -266,33 +266,37 @@
             state[s]["flight"] = trade(leaving, "row", 1)
         if steps_total > 1:
             base = order.run(lambda v: turned_sides(side_ref, v), right_sides)
-        for s in range(STREAMS):
-            pair_sum(s)
-            cross(s)
+        pair_sum(0)
+        cross(0)
         load_factor(1)
         load_inverse(1)
 
         for step in range(1, steps_total):
-            for s in range(STREAMS):
-                solve(s, step - 1)
-                factor_other(s, step)
+            final = exact and step == last_step
+            solve(0, step - 1)
+            factor_other(0, step)
+            pair_sum(1)
+            cross(1)
             factor_own(0, step)
             chip_sum(0)
+            solve(1, step - 1)
+            factor_other(1, step)
             older(step + 1, range(step - 1))
+            load_factor(step + 1)
+            load_inverse(step + 1)
+            residual(0, step)
+            inverse_own(0, step)
             factor_own(1, step)
             chip_sum(1)
-            for s in range(STREAMS):
-                residual(s, step)
-                inverse_own(s, step)
-            for s in range(STREAMS):
-                inverse_other(s, step)
-                if s == STREAMS - 1:
-                    load_inverse(step + 1)
-                pair_sum(s)
-                if not (exact and step == last_step):
-                    cross(s)
             older(step + 1, [step - 1])
-            load_factor(step + 1)
+            inverse_other(0, step)
+            pair_sum(0)
+            if not final:
+                cross(0)
+            residual(1, step)
+            inverse_own(1, step)
+            inverse_other(1, step)
+        pair_sum(1)
 
         outputs = []
         for step in range(steps_total):
@@ -306,8 +310,9 @@
                 outputs.append(found.T)
                 continue
             if step == last_step:
-                for s in range(STREAMS):
-                    solve(s, step)
+                solve(0, step)
+                cross(1)
+                solve(1, step)
             unit = place * UNITS // n_row
             found = solved[step][0][0]
             for s in range(STREAMS):

time: 154 us -> 156 us (1.013)
  waiting for transfers between devices: 69.3 us -> 58.9 us
  starting transfers between devices: 37.5 us -> 44.2 us
  local copies, waits for them, and re-layouts: 10.9 us -> 16.6 us
    ppermute x51, waiting for transfers between devices: 69.3 us -> 58.9 us  [trade(): return lax.ppermute(value, axis, [(i, i ^ step) for i in range(size)])]
    ppermute x51, starting transfers between devices: 37.5 us -> 44.2 us  [trade(): return lax.ppermute(value, axis, [(i, i ^ step) for i in range(size)])]
    squeeze x16, local copies, waits for them, and re-layouts: 8.76 us -> 14.4 us  [block(): self.last = lax.optimization_barrier(self.run(lambda v: v[index], blocks))]
  transfers between devices with their start and end apart: 51 -> 51, of which waited for: 32 -> 22; matrix products, arithmetic and copies ran while one was open for 5% -> 9% of each run, Pallas kernels for 21% -> 20%
where the time goes in v6:
time: 156 us; the launch traced here: 155 us
  waiting for transfers between devices  58.9 us (38%)
  starting transfers between devices  44.2 us (28%)
  Pallas kernels  32.5 us (21%)
  local copies, waits for them, and re-layouts  16.6 us (11%)
  other arithmetic  2.24 us (1%)
    ppermute x51, waiting for transfers between devices, trade(): return lax.ppermute(value, axis, [(i, i ^ step) for i in range(size)])  58.9 us
    ppermute x51, starting transfers between devices, trade(): return lax.ppermute(value, axis, [(i, i ^ step) for i in range(size)])  44.2 us
    pallas_call x38, Pallas kernels, product(): pl.pallas_call(functools.partial(product_kernel, len(units)), out_shape=j...  29.9 us
    squeeze x16, local copies, waits for them, and re-layouts, block(): self.last = lax.optimization_barrier(self.run(lambda v: v[index], blocks))  14.4 us
  transfers between devices with their start and end apart: 51, of which 22 were waited for; matrix products, arithmetic and copies ran while one was open for 9% of the time, Pallas kernels for 20%

profile of v6, /device:TPU:0, one launch (start us, length us, event | category | flops | bytes accessed | tf_op | source)
XLA Modules:
  0.0 155.4 jit_solution(5270848654919934147)
XLA Ops:
  0.0 1.8 %slice_bitcast_fusion.14.block = bf16[1024,1024]{1,0:T(8,128)(2,1)S(1)} fusion(bf16[5,1024,1024]{2,1,0:T(8,128)(2,1)} %param.4), kind=kLoop, calls=%fused_computation.14 | loop fusion | bytes 4194304 | tf_op jit(solution)/shard_map/squeeze | solution.py:128
  1.8 1.1 slice_bitcast_fusion.15.right
  2.9 0.9 shard_map.37
  3.7 3.1 %collective-permute-start.1 = (bf16[64,1024]{1,0:T(8,128)(2,1)S(1)}, bf16[64,1024]{1,0:T(8,128)(2,1)S(1)}, u32[]{:S(2)}, u32[]{:S(2)}) collective-permute-start(bf16[64,1024]{1,0:T(8,128)(2,1)S(1)} %get-tuple-element.224), channel_id=1, source_target_pairs={{0,4},{4,0},{8,12},{12,8},{1,5},{5,1},{9,13},{13,9},{2,6},{6,2},{1... | collective-permute-start | bytes 393224 | tf_op jit(solution)/shard_map/ppermute | solution.py:135
  6.8 0.8 shard_map.38
  7.8 1.7 %copy-done = bf16[5,1024,256]{2,1,0:T(8,128)(2,1)S(1)} copy-done((bf16[5,1024,256]{2,1,0:T(8,128)(2,1)S(1)}, bf16[5,1024,256]{2,1,0:T(8,128)(2,1)}, u32[]{:S(2)}) %copy-start) | copy-done | bytes 2621464
  9.5 0.9 shard_map.39
  10.7 3.0 %collective-permute-start.2 = (bf16[64,1024]{1,0:T(8,128)(2,1)S(1)}, bf16[64,1024]{1,0:T(8,128)(2,1)S(1)}, u32[]{:S(2)}, u32[]{:S(2)}) collective-permute-start(bf16[64,1024]{1,0:T(8,128)(2,1)S(1)} %get-tuple-element.457), channel_id=1, source_target_pairs={{0,8},{4,12},{8,0},{12,4},{1,9},{5,13},{9,1},{13,5},{2,10},{6,14},... | collective-permute-start | bytes 393224 | tf_op jit(solution)/shard_map/ppermute | solution.py:135
  13.7 2.5 %slice_bitcast_fusion.13.block = bf16[1024,1024]{1,0:T(8,128)(2,1)S(1)} fusion(bf16[10,1024,1024]{2,1,0:T(8,128)(2,1)} %param.3), kind=kLoop, calls=%fused_computation.13 | loop fusion | bytes 4194304 | tf_op jit(solution)/shard_map/squeeze | solution.py:128
  16.2 2.2 %slice_bitcast_fusion.12.block = bf16[1024,1024]{1,0:T(8,128)(2,1)S(1)} fusion(bf16[5,1024,1024]{2,1,0:T(8,128)(2,1)} %param.4), kind=kLoop, calls=%fused_computation.12 | loop fusion | bytes 4194304 | tf_op jit(solution)/shard_map/squeeze | solution.py:128
  18.5 0.9 collective-permute-done.2
  19.4 1.3 collective-permute-start.4
  21.6 2.9 %collective-permute-start.3 = (bf16[64,1024]{1,0:T(8,128)(2,1)S(1)}, bf16[64,1024]{1,0:T(8,128)(2,1)S(1)}, u32[]{:S(2)}, u32[]{:S(2)}) collective-permute-start(bf16[64,1024]{1,0:T(8,128)(2,1)S(1)} %get-tuple-element.455), channel_id=1, source_target_pairs={{0,8},{4,12},{8,0},{12,4},{1,9},{5,13},{9,1},{13,5},{2,10},{6,14},... | collective-permute-start | bytes 393224 | tf_op jit(solution)/shard_map/ppermute | solution.py:135
  25.3 1.6 %collective-permute-start.7 = (bf16[64,1024]{1,0:T(8,128)(2,1)S(1)}, bf16[64,1024]{1,0:T(8,128)(2,1)S(1)}, u32[]{:S(2)}, u32[]{:S(2)}) collective-permute-start(bf16[64,1024]{1,0:T(8,128)(2,1)S(1)} %get-tuple-element.453), channel_id=1, source_target_pairs={{0,2},{1,3},{2,0},{3,1},{4,6},{5,7},{6,4},{7,5},{8,10},{9,11},{10,... | collective-permute-start | bytes 393224 | tf_op jit(solution)/shard_map/ppermute | solution.py:135
  26.9 4.6 %collective-permute-done.3 = bf16[64,1024]{1,0:T(8,128)(2,1)S(1)} collective-permute-done((bf16[64,1024]{1,0:T(8,128)(2,1)S(1)}, bf16[64,1024]{1,0:T(8,128)(2,1)S(1)}, u32[]{:S(2)}, u32[]{:S(2)}) %collective-permute-start.3) | collective-permute-done | bytes 131104 | tf_op jit(solution)/shard_map/ppermute | solution.py:135
  32.6 1.8 %slice_bitcast_fusion.10.block = bf16[1024,1024]{1,0:T(8,128)(2,1)S(1)} fusion(bf16[5,1024,1024]{2,1,0:T(8,128)(2,1)} %param.4), kind=kLoop, calls=%fused_computation.10 | loop fusion | bytes 4194304 | tf_op jit(solution)/shard_map/squeeze | solution.py:128
  35.7 2.1 %collective-permute-start.11 = (bf16[64,1024]{1,0:T(8,128)(2,1)S(1)}, bf16[64,1024]{1,0:T(8,128)(2,1)S(1)}, u32[]{:S(2)}, u32[]{:S(2)}) collective-permute-start(bf16[64,1024]{1,0:T(8,128)(2,1)S(1)} %shard_map.43), channel_id=1, source_target_pairs={{0,4},{4,0},{8,12},{12,8},{1,5},{5,1},{9,13},{13,9},{2,6},{6,2},{1... | collective-permute-start | bytes 393224 | tf_op jit(solution)/shard_map/ppermute | solution.py:135
  38.6 1.6 %collective-permute-start.9 = (bf16[64,1024]{1,0:T(8,128)(2,1)S(1)}, bf16[64,1024]{1,0:T(8,128)(2,1)S(1)}, u32[]{:S(2)}, u32[]{:S(2)}) collective-permute-start(bf16[64,1024]{1,0:T(8,128)(2,1)S(1)} %get-tuple-element.451), channel_id=1, source_target_pairs={{0,2},{1,3},{2,0},{3,1},{4,6},{5,7},{6,4},{7,5},{8,10},{9,11},{10,... | collective-permute-start | bytes 393224 | tf_op jit(solution)/shard_map/ppermute | solution.py:135
  40.4 0.9 shard_map.45
  42.1 1.9 %collective-permute-start.14 = (bf16[64,1024]{1,0:T(8,128)(2,1)S(1)}, bf16[64,1024]{1,0:T(8,128)(2,1)S(1)}, u32[]{:S(2)}, u32[]{:S(2)}) collective-permute-start(bf16[64,1024]{1,0:T(8,128)(2,1)S(1)} %get-tuple-element.449), channel_id=1, source_target_pairs={{0,8},{4,12},{8,0},{12,4},{1,9},{5,13},{9,1},{13,5},{2,10},{6,14},... | collective-permute-start | bytes 393224 | tf_op jit(solution)/shard_map/ppermute | solution.py:135
  45.0 0.9 collective-permute-start.13
  46.7 4.2 %collective-permute-done.14 = bf16[64,1024]{1,0:T(8,128)(2,1)S(1)} collective-permute-done((bf16[64,1024]{1,0:T(8,128)(2,1)S(1)}, bf16[64,1024]{1,0:T(8,128)(2,1)S(1)}, u32[]{:S(2)}, u32[]{:S(2)}) %collective-permute-start.14) | collective-permute-done | bytes 131104 | tf_op jit(solution)/shard_map/ppermute | solution.py:135
  51.8 1.3 collective-permute-done.13
  53.1 1.5 collective-permute-start.15
  54.6 1.3 collective-permute-done.16.refs_0_
  56.7 1.1 collective-permute-start.19
  57.8 4.2 %collective-permute-done.15 = bf16[64,1024]{1,0:T(8,128)(2,1)S(1)} collective-permute-done((bf16[64,1024]{1,0:T(8,128)(2,1)S(1)}, bf16[64,1024]{1,0:T(8,128)(2,1)S(1)}, u32[]{:S(2)}, u32[]{:S(2)}) %collective-permute-start.15) | collective-permute-done | bytes 131104 | tf_op jit(solution)/shard_map/ppermute | solution.py:135
  63.1 0.9 shard_map.52.refs_4_
  64.2 1.8 %slice_bitcast_fusion.6.block = bf16[1024,1024]{1,0:T(8,128)(2,1)S(1)} fusion(bf16[5,1024,1024]{2,1,0:T(8,128)(2,1)} %param.4), kind=kLoop, calls=%fused_computation.6 | loop fusion | bytes 4194304 | tf_op jit(solution)/shard_map/squeeze | solution.py:128
  67.3 2.1 %collective-permute-start.23 = (bf16[64,1024]{1,0:T(8,128)(2,1)S(1)}, bf16[64,1024]{1,0:T(8,128)(2,1)S(1)}, u32[]{:S(2)}, u32[]{:S(2)}) collective-permute-start(bf16[64,1024]{1,0:T(8,128)(2,1)S(1)} %shard_map.53), channel_id=1, source_target_pairs={{0,4},{4,0},{8,12},{12,8},{1,5},{5,1},{9,13},{13,9},{2,6},{6,2},{1... | collective-permute-start | bytes 393224 | tf_op jit(solution)/shard_map/ppermute | solution.py:135
  69.4 0.8 shard_map.54
  70.2 1.1 collective-permute-start.21
  71.5 0.9 shard_map.55
  72.4 1.0 shard_map.56
  73.4 1.9 %collective-permute-start.26 = (bf16[64,1024]{1,0:T(8,128)(2,1)S(1)}, bf16[64,1024]{1,0:T(8,128)(2,1)S(1)}, u32[]{:S(2)}, u32[]{:S(2)}) collective-permute-start(bf16[64,1024]{1,0:T(8,128)(2,1)S(1)} %get-tuple-element.441), channel_id=1, source_target_pairs={{0,8},{4,12},{8,0},{12,4},{1,9},{5,13},{9,1},{13,5},{2,10},{6,14},... | collective-permute-start | bytes 393224 | tf_op jit(solution)/shard_map/ppermute | solution.py:135
  77.8 4.4 %collective-permute-done.26 = bf16[64,1024]{1,0:T(8,128)(2,1)S(1)} collective-permute-done((bf16[64,1024]{1,0:T(8,128)(2,1)S(1)}, bf16[64,1024]{1,0:T(8,128)(2,1)S(1)}, u32[]{:S(2)}, u32[]{:S(2)}) %collective-permute-start.26) | collective-permute-done | bytes 131104 | tf_op jit(solution)/shard_map/ppermute | solution.py:135
  83.1 1.1 collective-permute-done.25
  84.3 1.5 collective-permute-start.27
  85.7 1.5 collective-permute-done.28.refs_0_
  88.1 1.0 collective-permute-start.31
  89.1 4.1 %collective-permute-done.27 = bf16[64,1024]{1,0:T(8,128)(2,1)S(1)} collective-permute-done((bf16[64,1024]{1,0:T(8,128)(2,1)S(1)}, bf16[64,1024]{1,0:T(8,128)(2,1)S(1)}, u32[]{:S(2)}, u32[]{:S(2)}) %collective-permute-start.27) | collective-permute-done | bytes 131104 | tf_op jit(solution)/shard_map/ppermute | solution.py:135
  94.3 0.9 shard_map.62.refs_4_
  95.4 0.9 shard_map.63.refs_4_
  96.4 1.8 %slice_bitcast_fusion.1.block = bf16[1024,1024]{1,0:T(8,128)(2,1)S(1)} fusion(bf16[5,1024,1024]{2,1,0:T(8,128)(2,1)} %param.4), kind=kLoop, calls=%fused_computation.1 | loop fusion | bytes 4194304 | tf_op jit(solution)/shard_map/squeeze | solution.py:128
  99.6 2.1 %collective-permute-start.35 = (bf16[64,1024]{1,0:T(8,128)(2,1)S(1)}, bf16[64,1024]{1,0:T(8,128)(2,1)S(1)}, u32[]{:S(2)}, u32[]{:S(2)}) collective-permute-start(bf16[64,1024]{1,0:T(8,128)(2,1)S(1)} %shard_map.64), channel_id=1, source_target_pairs={{0,4},{4,0},{8,12},{12,8},{1,5},{5,1},{9,13},{13,9},{2,6},{6,2},{1... | collective-permute-start | bytes 393224 | tf_op jit(solution)/shard_map/ppermute | solution.py:135
  102.5 1.1 collective-permute-start.33
  103.7 0.9 shard_map.66
  105.4 2.2 %collective-permute-start.38 = (bf16[64,1024]{1,0:T(8,128)(2,1)S(1)}, bf16[64,1024]{1,0:T(8,128)(2,1)S(1)}, u32[]{:S(2)}, u32[]{:S(2)}) collective-permute-start(bf16[64,1024]{1,0:T(8,128)(2,1)S(1)} %get-tuple-element.433), channel_id=1, source_target_pairs={{0,8},{4,12},{8,0},{12,4},{1,9},{5,13},{9,1},{13,5},{2,10},{6,14},... | collective-permute-start | bytes 393224 | tf_op jit(solution)/shard_map/ppermute | solution.py:135
  109.9 4.2 %collective-permute-done.38 = bf16[64,1024]{1,0:T(8,128)(2,1)S(1)} collective-permute-done((bf16[64,1024]{1,0:T(8,128)(2,1)S(1)}, bf16[64,1024]{1,0:T(8,128)(2,1)S(1)}, u32[]{:S(2)}, u32[]{:S(2)}) %collective-permute-start.38) | collective-permute-done | bytes 131104 | tf_op jit(solution)/shard_map/ppermute | solution.py:135
  114.2 0.8 shard_map.70
  115.1 1.4 collective-permute-done.37
  116.5 1.2 collective-permute-start.39
  117.7 1.5 collective-permute-done.40.refs_0_
  120.0 1.1 collective-permute-start.43
  121.1 4.1 %collective-permute-done.39 = bf16[64,1024]{1,0:T(8,128)(2,1)S(1)} collective-permute-done((bf16[64,1024]{1,0:T(8,128)(2,1)S(1)}, bf16[64,1024]{1,0:T(8,128)(2,1)S(1)}, u32[]{:S(2)}, u32[]{:S(2)}) %collective-permute-start.39) | collective-permute-done | bytes 131104 | tf_op jit(solution)/shard_map/ppermute | solution.py:135
  127.5 1.0 shard_map.73
  128.5 1.1 collective-permute-start.46
  129.6 3.0 %collective-permute-done.42.refs_0_ = bf16[64,1024]{1,0:T(8,128)(2,1)S(1)} collective-permute-done((bf16[64,1024]{1,0:T(8,128)(2,1)S(1)}, bf16[64,1024]{1,0:T(8,128)(2,1)S(1)}, u32[]{:S(2)}, u32[]{:S(2)}) %collective-permute-start.42) | collective-permute-done | bytes 131104 | tf_op jit(solution)/shard_map/ppermute | solution.py:135
  133.4 1.2 collective-permute-start.47
  135.4 3.1 %collective-permute-done.47 = bf16[64,1024]{1,0:T(8,128)(2,1)S(1)} collective-permute-done((bf16[64,1024]{1,0:T(8,128)(2,1)S(1)}, bf16[64,1024]{1,0:T(8,128)(2,1)S(1)}, u32[]{:S(2)}, u32[]{:S(2)}) %collective-permute-start.47) | collective-permute-done | bytes 131104 | tf_op jit(solution)/shard_map/ppermute | solution.py:135
  138.7 1.3 collective-permute-done.48
  141.8 4.5 %collective-permute-done.49 = bf16[64,1024]{1,0:T(8,128)(2,1)S(1)} collective-permute-done((bf16[64,1024]{1,0:T(8,128)(2,1)S(1)}, bf16[64,1024]{1,0:T(8,128)(2,1)S(1)}, u32[]{:S(2)}, u32[]{:S(2)}) %collective-permute-start.49) | collective-permute-done | bytes 131104 | tf_op jit(solution)/shard_map/ppermute | solution.py:135
  146.4 0.8 collective-permute-start.50
  147.3 7.4 %collective-permute-done.50 = bf16[64,1024]{1,0:T(8,128)(2,1)S(1)} collective-permute-done((bf16[64,1024]{1,0:T(8,128)(2,1)S(1)}, bf16[64,1024]{1,0:T(8,128)(2,1)S(1)}, u32[]{:S(2)}, u32[]{:S(2)}) %collective-permute-start.50) | collective-permute-done | bytes 131104 | tf_op jit(solution)/shard_map/ppermute | solution.py:135
  (147 shorter events, 31.3 us)
Async XLA Ops:
  3.7 7.0 %collective-permute-start.1 = (bf16[64,1024]{1,0:T(8,128)(2,1)S(1)}, bf16[64,1024]{1,0:T(8,128)(2,1)S(1)}, u32[]{:S(2)}, u32[]{:S(2)}) collective-permute-start(bf16[64,1024]{1,0:T(8,128)(2,1)S(1)} %get-tuple-element.224), channel_id=1, source_target_pairs={{0,4},{4,0},{8,12},{12,8},{1,5},{5,1},{9,13},{13,9},{2,6},{6,2},{1... | collective-permute-start | bytes 393224 | tf_op jit(solution)/shard_map/ppermute | solution.py:135
  7.7 13.9 %collective-permute-start = (bf16[64,1024]{1,0:T(8,128)(2,1)S(1)}, bf16[64,1024]{1,0:T(8,128)(2,1)S(1)}, u32[]{:S(2)}, u32[]{:S(2)}) collective-permute-start(bf16[64,1024]{1,0:T(8,128)(2,1)S(1)} %get-tuple-element.223), channel_id=1, source_target_pairs={{0,4},{4,0},{8,12},{12,8},{1,5},{5,1},{9,13},{13,9},{2,6},{6,2},{1... | collective-permute-start | bytes 393224 | tf_op jit(solution)/shard_map/ppermute | solution.py:135
  7.7 1.7 %copy-start = (bf16[5,1024,256]{2,1,0:T(8,128)(2,1)S(1)}, bf16[5,1024,256]{2,1,0:T(8,128)(2,1)}, u32[]{:S(2)}) copy-start(bf16[5,1024,256]{2,1,0:T(8,128)(2,1)} %sides) | copy-start | bytes 7864324
  10.4 22.0 %copy-start.1 = (bf16[10,1024,1024]{2,1,0:T(8,128)(2,1)S(1)}, bf16[10,1024,1024]{2,1,0:T(8,128)(2,1)}, u32[]{:S(2)}) copy-start(bf16[10,1024,1024]{2,1,0:T(8,128)(2,1)} %param.3) | copy-start | bytes 62914564
  10.7 8.7 %collective-permute-start.2 = (bf16[64,1024]{1,0:T(8,128)(2,1)S(1)}, bf16[64,1024]{1,0:T(8,128)(2,1)S(1)}, u32[]{:S(2)}, u32[]{:S(2)}) collective-permute-start(bf16[64,1024]{1,0:T(8,128)(2,1)S(1)} %get-tuple-element.457), channel_id=1, source_target_pairs={{0,8},{4,12},{8,0},{12,4},{1,9},{5,13},{9,1},{13,5},{2,10},{6,14},... | collective-permute-start | bytes 393224 | tf_op jit(solution)/shard_map/ppermute | solution.py:135
  19.4 5.1 %collective-permute-start.4 = (bf16[64,1024]{1,0:T(8,128)(2,1)S(1)}, bf16[64,1024]{1,0:T(8,128)(2,1)S(1)}, u32[]{:S(2)}, u32[]{:S(2)}) collective-permute-start(bf16[64,1024]{1,0:T(8,128)(2,1)S(1)} %add_convert_fusion.8.refs_0_.refs_1_), channel_id=1, source_target_pairs={{0,4},{4,0},{8,12},{12,8},{1,5},{5,1},{9,13},{13,9},{2,6},{6,2},{1... | collective-permute-start | bytes 393224 | tf_op jit(solution)/shard_map/ppermute | solution.py:135
  21.5 3.8 %collective-permute-start.5 = (bf16[64,1024]{1,0:T(8,128)(2,1)S(1)}, bf16[64,1024]{1,0:T(8,128)(2,1)S(1)}, u32[]{:S(2)}, u32[]{:S(2)}) collective-permute-start(bf16[64,1024]{1,0:T(8,128)(2,1)S(1)} %shard_map.40), channel_id=1, source_target_pairs={{0,1},{1,0},{2,3},{3,2},{4,5},{5,4},{6,7},{7,6},{8,9},{9,8},{10,11... | collective-permute-start | bytes 393224 | tf_op jit(solution)/shard_map/ppermute | solution.py:135
  21.6 9.9 %collective-permute-start.3 = (bf16[64,1024]{1,0:T(8,128)(2,1)S(1)}, bf16[64,1024]{1,0:T(8,128)(2,1)S(1)}, u32[]{:S(2)}, u32[]{:S(2)}) collective-permute-start(bf16[64,1024]{1,0:T(8,128)(2,1)S(1)} %get-tuple-element.455), channel_id=1, source_target_pairs={{0,8},{4,12},{8,0},{12,4},{1,9},{5,13},{9,1},{13,5},{2,10},{6,14},... | collective-permute-start | bytes 393224 | tf_op jit(solution)/shard_map/ppermute | solution.py:135
  25.3 9.0 %collective-permute-start.7 = (bf16[64,1024]{1,0:T(8,128)(2,1)S(1)}, bf16[64,1024]{1,0:T(8,128)(2,1)S(1)}, u32[]{:S(2)}, u32[]{:S(2)}) collective-permute-start(bf16[64,1024]{1,0:T(8,128)(2,1)S(1)} %get-tuple-element.453), channel_id=1, source_target_pairs={{0,2},{1,3},{2,0},{3,1},{4,6},{5,7},{6,4},{7,5},{8,10},{9,11},{10,... | collective-permute-start | bytes 393224 | tf_op jit(solution)/shard_map/ppermute | solution.py:135
  31.5 6.3 %collective-permute-start.6 = (bf16[64,1024]{1,0:T(8,128)(2,1)S(1)}, bf16[64,1024]{1,0:T(8,128)(2,1)S(1)}, u32[]{:S(2)}, u32[]{:S(2)}) collective-permute-start(bf16[64,1024]{1,0:T(8,128)(2,1)S(1)} %add_convert_fusion.7.refs_0_.refs_3_), channel_id=1, source_target_pairs={{0,4},{4,0},{8,12},{12,8},{1,5},{5,1},{9,13},{13,9},{2,6},{6,2},{1... | collective-permute-start | bytes 393224 | tf_op jit(solution)/shard_map/ppermute | solution.py:135
  32.3 6.2 %collective-permute-start.8 = (bf16[64,1024]{1,0:T(8,128)(2,1)S(1)}, bf16[64,1024]{1,0:T(8,128)(2,1)S(1)}, u32[]{:S(2)}, u32[]{:S(2)}) collective-permute-start(bf16[64,1024]{1,0:T(8,128)(2,1)S(1)} %shard_map.42), channel_id=1, source_target_pairs={{0,1},{1,0},{2,3},{3,2},{4,5},{5,4},{6,7},{7,6},{8,9},{9,8},{10,11... | collective-permute-start | bytes 393224 | tf_op jit(solution)/shard_map/ppermute | solution.py:135
  34.4 6.8 %collective-permute-start.10 = (bf16[64,1024]{1,0:T(8,128)(2,1)S(1)}, bf16[64,1024]{1,0:T(8,128)(2,1)S(1)}, u32[]{:S(2)}, u32[]{:S(2)}) collective-permute-start(bf16[64,1024]{1,0:T(8,128)(2,1)S(1)} %subtract_convert_fusion.7.refs_0_), channel_id=1, source_target_pairs={{0,1},{1,0},{2,3},{3,2},{4,5},{5,4},{6,7},{7,6},{8,9},{9,8},{10,11... | collective-permute-start | bytes 393224 | tf_op jit(solution)/shard_map/ppermute | solution.py:135
  35.7 6.3 %collective-permute-start.11 = (bf16[64,1024]{1,0:T(8,128)(2,1)S(1)}, bf16[64,1024]{1,0:T(8,128)(2,1)S(1)}, u32[]{:S(2)}, u32[]{:S(2)}) collective-permute-start(bf16[64,1024]{1,0:T(8,128)(2,1)S(1)} %shard_map.43), channel_id=1, source_target_pairs={{0,4},{4,0},{8,12},{12,8},{1,5},{5,1},{9,13},{13,9},{2,6},{6,2},{1... | collective-permute-start | bytes 393224 | tf_op jit(solution)/shard_map/ppermute | solution.py:135
  38.6 5.4 %collective-permute-start.9 = (bf16[64,1024]{1,0:T(8,128)(2,1)S(1)}, bf16[64,1024]{1,0:T(8,128)(2,1)S(1)}, u32[]{:S(2)}, u32[]{:S(2)}) collective-permute-start(bf16[64,1024]{1,0:T(8,128)(2,1)S(1)} %get-tuple-element.451), channel_id=1, source_target_pairs={{0,2},{1,3},{2,0},{3,1},{4,6},{5,7},{6,4},{7,5},{8,10},{9,11},{10,... | collective-permute-start | bytes 393224 | tf_op jit(solution)/shard_map/ppermute | solution.py:135
  42.1 8.7 %collective-permute-start.14 = (bf16[64,1024]{1,0:T(8,128)(2,1)S(1)}, bf16[64,1024]{1,0:T(8,128)(2,1)S(1)}, u32[]{:S(2)}, u32[]{:S(2)}) collective-permute-start(bf16[64,1024]{1,0:T(8,128)(2,1)S(1)} %get-tuple-element.449), channel_id=1, source_target_pairs={{0,8},{4,12},{8,0},{12,4},{1,9},{5,13},{9,1},{13,5},{2,10},{6,14},... | collective-permute-start | bytes 393224 | tf_op jit(solution)/shard_map/ppermute | solution.py:135
  44.1 1.8 %collective-permute-start.12 = (bf16[64,1024]{1,0:T(8,128)(2,1)S(1)}, bf16[64,1024]{1,0:T(8,128)(2,1)S(1)}, u32[]{:S(2)}, u32[]{:S(2)}) collective-permute-start(bf16[64,1024]{1,0:T(8,128)(2,1)S(1)} %subtract_convert_fusion.6.refs_0_), channel_id=1, source_target_pairs={{0,1},{1,0},{2,3},{3,2},{4,5},{5,4},{6,7},{7,6},{8,9},{9,8},{10,11... | collective-permute-start | bytes 393224 | tf_op jit(solution)/shard_map/ppermute | solution.py:135
  45.0 8.0 %collective-permute-start.13 = (bf16[64,1024]{1,0:T(8,128)(2,1)S(1)}, bf16[64,1024]{1,0:T(8,128)(2,1)S(1)}, u32[]{:S(2)}, u32[]{:S(2)}) collective-permute-start(bf16[64,1024]{1,0:T(8,128)(2,1)S(1)} %shard_map.47), channel_id=1, source_target_pairs={{0,4},{4,0},{8,12},{12,8},{1,5},{5,1},{9,13},{13,9},{2,6},{6,2},{1... | collective-permute-start | bytes 393224 | tf_op jit(solution)/shard_map/ppermute | solution.py:135
  50.8 5.0 %collective-permute-start.16 = (bf16[64,1024]{1,0:T(8,128)(2,1)S(1)}, bf16[64,1024]{1,0:T(8,128)(2,1)S(1)}, u32[]{:S(2)}, u32[]{:S(2)}) collective-permute-start(bf16[64,1024]{1,0:T(8,128)(2,1)S(1)} %add_convert_fusion.6.refs_0_.refs_1_), channel_id=1, source_target_pairs={{0,4},{4,0},{8,12},{12,8},{1,5},{5,1},{9,13},{13,9},{2,6},{6,2},{1... | collective-permute-start | bytes 393224 | tf_op jit(solution)/shard_map/ppermute | solution.py:135
  51.7 5.0 %collective-permute-start.17 = (bf16[64,1024]{1,0:T(8,128)(2,1)S(1)}, bf16[64,1024]{1,0:T(8,128)(2,1)S(1)}, u32[]{:S(2)}, u32[]{:S(2)}) collective-permute-start(bf16[64,1024]{1,0:T(8,128)(2,1)S(1)} %shard_map.49), channel_id=1, source_target_pairs={{0,1},{1,0},{2,3},{3,2},{4,5},{5,4},{6,7},{7,6},{8,9},{9,8},{10,11... | collective-permute-start | bytes 393224 | tf_op jit(solution)/shard_map/ppermute | solution.py:135
  53.1 8.9 %collective-permute-start.15 = (bf16[64,1024]{1,0:T(8,128)(2,1)S(1)}, bf16[64,1024]{1,0:T(8,128)(2,1)S(1)}, u32[]{:S(2)}, u32[]{:S(2)}) collective-permute-start(bf16[64,1024]{1,0:T(8,128)(2,1)S(1)} %get-tuple-element.447), channel_id=1, source_target_pairs={{0,8},{4,12},{8,0},{12,4},{1,9},{5,13},{9,1},{13,5},{2,10},{6,14},... | collective-permute-start | bytes 393224 | tf_op jit(solution)/shard_map/ppermute | solution.py:135
  56.7 9.2 %collective-permute-start.19 = (bf16[64,1024]{1,0:T(8,128)(2,1)S(1)}, bf16[64,1024]{1,0:T(8,128)(2,1)S(1)}, u32[]{:S(2)}, u32[]{:S(2)}) collective-permute-start(bf16[64,1024]{1,0:T(8,128)(2,1)S(1)} %get-tuple-element.445), channel_id=1, source_target_pairs={{0,2},{1,3},{2,0},{3,1},{4,6},{5,7},{6,4},{7,5},{8,10},{9,11},{10,... | collective-permute-start | bytes 393224 | tf_op jit(solution)/shard_map/ppermute | solution.py:135
  62.0 7.4 %collective-permute-start.18 = (bf16[64,1024]{1,0:T(8,128)(2,1)S(1)}, bf16[64,1024]{1,0:T(8,128)(2,1)S(1)}, u32[]{:S(2)}, u32[]{:S(2)}) collective-permute-start(bf16[64,1024]{1,0:T(8,128)(2,1)S(1)} %add_convert_fusion.5.refs_0_.refs_3_), channel_id=1, source_target_pairs={{0,4},{4,0},{8,12},{12,8},{1,5},{5,1},{9,13},{13,9},{2,6},{6,2},{1... | collective-permute-start | bytes 393224 | tf_op jit(solution)/shard_map/ppermute | solution.py:135
  62.8 7.3 %collective-permute-start.20 = (bf16[64,1024]{1,0:T(8,128)(2,1)S(1)}, bf16[64,1024]{1,0:T(8,128)(2,1)S(1)}, u32[]{:S(2)}, u32[]{:S(2)}) collective-permute-start(bf16[64,1024]{1,0:T(8,128)(2,1)S(1)} %shard_map.51), channel_id=1, source_target_pairs={{0,1},{1,0},{2,3},{3,2},{4,5},{5,4},{6,7},{7,6},{8,9},{9,8},{10,11... | collective-permute-start | bytes 393224 | tf_op jit(solution)/shard_map/ppermute | solution.py:135
  66.0 6.4 %collective-permute-start.22 = (bf16[64,1024]{1,0:T(8,128)(2,1)S(1)}, bf16[64,1024]{1,0:T(8,128)(2,1)S(1)}, u32[]{:S(2)}, u32[]{:S(2)}) collective-permute-start(bf16[64,1024]{1,0:T(8,128)(2,1)S(1)} %subtract_convert_fusion.5.refs_0_), channel_id=1, source_target_pairs={{0,1},{1,0},{2,3},{3,2},{4,5},{5,4},{6,7},{7,6},{8,9},{9,8},{10,11... | collective-permute-start | bytes 393224 | tf_op jit(solution)/shard_map/ppermute | solution.py:135
  67.3 6.1 %collective-permute-start.23 = (bf16[64,1024]{1,0:T(8,128)(2,1)S(1)}, bf16[64,1024]{1,0:T(8,128)(2,1)S(1)}, u32[]{:S(2)}, u32[]{:S(2)}) collective-permute-start(bf16[64,1024]{1,0:T(8,128)(2,1)S(1)} %shard_map.53), channel_id=1, source_target_pairs={{0,4},{4,0},{8,12},{12,8},{1,5},{5,1},{9,13},{13,9},{2,6},{6,2},{1... | collective-permute-start | bytes 393224 | tf_op jit(solution)/shard_map/ppermute | solution.py:135
  70.2 5.2 %collective-permute-start.21 = (bf16[64,1024]{1,0:T(8,128)(2,1)S(1)}, bf16[64,1024]{1,0:T(8,128)(2,1)S(1)}, u32[]{:S(2)}, u32[]{:S(2)}) collective-permute-start(bf16[64,1024]{1,0:T(8,128)(2,1)S(1)} %get-tuple-element.443), channel_id=1, source_target_pairs={{0,2},{1,3},{2,0},{3,1},{4,6},{5,7},{6,4},{7,5},{8,10},{9,11},{10,... | collective-permute-start | bytes 393224 | tf_op jit(solution)/shard_map/ppermute | solution.py:135
  73.4 8.7 %collective-permute-start.26 = (bf16[64,1024]{1,0:T(8,128)(2,1)S(1)}, bf16[64,1024]{1,0:T(8,128)(2,1)S(1)}, u32[]{:S(2)}, u32[]{:S(2)}) collective-permute-start(bf16[64,1024]{1,0:T(8,128)(2,1)S(1)} %get-tuple-element.441), channel_id=1, source_target_pairs={{0,8},{4,12},{8,0},{12,4},{1,9},{5,13},{9,1},{13,5},{2,10},{6,14},... | collective-permute-start | bytes 393224 | tf_op jit(solution)/shard_map/ppermute | solution.py:135
  75.4 1.6 %collective-permute-start.24 = (bf16[64,1024]{1,0:T(8,128)(2,1)S(1)}, bf16[64,1024]{1,0:T(8,128)(2,1)S(1)}, u32[]{:S(2)}, u32[]{:S(2)}) collective-permute-start(bf16[64,1024]{1,0:T(8,128)(2,1)S(1)} %subtract_convert_fusion.4.refs_0_), channel_id=1, source_target_pairs={{0,1},{1,0},{2,3},{3,2},{4,5},{5,4},{6,7},{7,6},{8,9},{9,8},{10,11... | collective-permute-start | bytes 393224 | tf_op jit(solution)/shard_map/ppermute | solution.py:135
  76.4 7.8 %collective-permute-start.25 = (bf16[64,1024]{1,0:T(8,128)(2,1)S(1)}, bf16[64,1024]{1,0:T(8,128)(2,1)S(1)}, u32[]{:S(2)}, u32[]{:S(2)}) collective-permute-start(bf16[64,1024]{1,0:T(8,128)(2,1)S(1)} %shard_map.57), channel_id=1, source_target_pairs={{0,4},{4,0},{8,12},{12,8},{1,5},{5,1},{9,13},{13,9},{2,6},{6,2},{1... | collective-permute-start | bytes 393224 | tf_op jit(solution)/shard_map/ppermute | solution.py:135
  82.2 5.0 %collective-permute-start.28 = (bf16[64,1024]{1,0:T(8,128)(2,1)S(1)}, bf16[64,1024]{1,0:T(8,128)(2,1)S(1)}, u32[]{:S(2)}, u32[]{:S(2)}) collective-permute-start(bf16[64,1024]{1,0:T(8,128)(2,1)S(1)} %add_convert_fusion.4.refs_0_.refs_1_), channel_id=1, source_target_pairs={{0,4},{4,0},{8,12},{12,8},{1,5},{5,1},{9,13},{13,9},{2,6},{6,2},{1... | collective-permute-start | bytes 393224 | tf_op jit(solution)/shard_map/ppermute | solution.py:135
  83.1 5.0 %collective-permute-start.29 = (bf16[64,1024]{1,0:T(8,128)(2,1)S(1)}, bf16[64,1024]{1,0:T(8,128)(2,1)S(1)}, u32[]{:S(2)}, u32[]{:S(2)}) collective-permute-start(bf16[64,1024]{1,0:T(8,128)(2,1)S(1)} %shard_map.59), channel_id=1, source_target_pairs={{0,1},{1,0},{2,3},{3,2},{4,5},{5,4},{6,7},{7,6},{8,9},{9,8},{10,11... | collective-permute-start | bytes 393224 | tf_op jit(solution)/shard_map/ppermute | solution.py:135
  84.3 8.9 %collective-permute-start.27 = (bf16[64,1024]{1,0:T(8,128)(2,1)S(1)}, bf16[64,1024]{1,0:T(8,128)(2,1)S(1)}, u32[]{:S(2)}, u32[]{:S(2)}) collective-permute-start(bf16[64,1024]{1,0:T(8,128)(2,1)S(1)} %get-tuple-element.439), channel_id=1, source_target_pairs={{0,8},{4,12},{8,0},{12,4},{1,9},{5,13},{9,1},{13,5},{2,10},{6,14},... | collective-permute-start | bytes 393224 | tf_op jit(solution)/shard_map/ppermute | solution.py:135
  88.1 10.1 %collective-permute-start.31 = (bf16[64,1024]{1,0:T(8,128)(2,1)S(1)}, bf16[64,1024]{1,0:T(8,128)(2,1)S(1)}, u32[]{:S(2)}, u32[]{:S(2)}) collective-permute-start(bf16[64,1024]{1,0:T(8,128)(2,1)S(1)} %get-tuple-element.437), channel_id=1, source_target_pairs={{0,2},{1,3},{2,0},{3,1},{4,6},{5,7},{6,4},{7,5},{8,10},{9,11},{10,... | collective-permute-start | bytes 393224 | tf_op jit(solution)/shard_map/ppermute | solution.py:135
  93.2 8.5 %collective-permute-start.30 = (bf16[64,1024]{1,0:T(8,128)(2,1)S(1)}, bf16[64,1024]{1,0:T(8,128)(2,1)S(1)}, u32[]{:S(2)}, u32[]{:S(2)}) collective-permute-start(bf16[64,1024]{1,0:T(8,128)(2,1)S(1)} %add_convert_fusion.3.refs_0_.refs_3_), channel_id=1, source_target_pairs={{0,4},{4,0},{8,12},{12,8},{1,5},{5,1},{9,13},{13,9},{2,6},{6,2},{1... | collective-permute-start | bytes 393224 | tf_op jit(solution)/shard_map/ppermute | solution.py:135
  94.0 8.4 %collective-permute-start.32 = (bf16[64,1024]{1,0:T(8,128)(2,1)S(1)}, bf16[64,1024]{1,0:T(8,128)(2,1)S(1)}, u32[]{:S(2)}, u32[]{:S(2)}) collective-permute-start(bf16[64,1024]{1,0:T(8,128)(2,1)S(1)} %shard_map.61), channel_id=1, source_target_pairs={{0,1},{1,0},{2,3},{3,2},{4,5},{5,4},{6,7},{7,6},{8,9},{9,8},{10,11... | collective-permute-start | bytes 393224 | tf_op jit(solution)/shard_map/ppermute | solution.py:135
  98.3 6.3 %collective-permute-start.34 = (bf16[64,1024]{1,0:T(8,128)(2,1)S(1)}, bf16[64,1024]{1,0:T(8,128)(2,1)S(1)}, u32[]{:S(2)}, u32[]{:S(2)}) collective-permute-start(bf16[64,1024]{1,0:T(8,128)(2,1)S(1)} %subtract_convert_fusion.3.refs_0_), channel_id=1, source_target_pairs={{0,1},{1,0},{2,3},{3,2},{4,5},{5,4},{6,7},{7,6},{8,9},{9,8},{10,11... | collective-permute-start | bytes 393224 | tf_op jit(solution)/shard_map/ppermute | solution.py:135
  99.6 5.8 %collective-permute-start.35 = (bf16[64,1024]{1,0:T(8,128)(2,1)S(1)}, bf16[64,1024]{1,0:T(8,128)(2,1)S(1)}, u32[]{:S(2)}, u32[]{:S(2)}) collective-permute-start(bf16[64,1024]{1,0:T(8,128)(2,1)S(1)} %shard_map.64), channel_id=1, source_target_pairs={{0,4},{4,0},{8,12},{12,8},{1,5},{5,1},{9,13},{13,9},{2,6},{6,2},{1... | collective-permute-start | bytes 393224 | tf_op jit(solution)/shard_map/ppermute | solution.py:135
  102.5 5.2 %collective-permute-start.33 = (bf16[64,1024]{1,0:T(8,128)(2,1)S(1)}, bf16[64,1024]{1,0:T(8,128)(2,1)S(1)}, u32[]{:S(2)}, u32[]{:S(2)}) collective-permute-start(bf16[64,1024]{1,0:T(8,128)(2,1)S(1)} %get-tuple-element.435), channel_id=1, source_target_pairs={{0,2},{1,3},{2,0},{3,1},{4,6},{5,7},{6,4},{7,5},{8,10},{9,11},{10,... | collective-permute-start | bytes 393224 | tf_op jit(solution)/shard_map/ppermute | solution.py:135
  105.4 8.7 %collective-permute-start.38 = (bf16[64,1024]{1,0:T(8,128)(2,1)S(1)}, bf16[64,1024]{1,0:T(8,128)(2,1)S(1)}, u32[]{:S(2)}, u32[]{:S(2)}) collective-permute-start(bf16[64,1024]{1,0:T(8,128)(2,1)S(1)} %get-tuple-element.433), channel_id=1, source_target_pairs={{0,8},{4,12},{8,0},{12,4},{1,9},{5,13},{9,1},{13,5},{2,10},{6,14},... | collective-permute-start | bytes 393224 | tf_op jit(solution)/shard_map/ppermute | solution.py:135
  107.7 1.4 collective-permute-start.36
  108.7 7.8 %collective-permute-start.37 = (bf16[64,1024]{1,0:T(8,128)(2,1)S(1)}, bf16[64,1024]{1,0:T(8,128)(2,1)S(1)}, u32[]{:S(2)}, u32[]{:S(2)}) collective-permute-start(bf16[64,1024]{1,0:T(8,128)(2,1)S(1)} %shard_map.68), channel_id=1, source_target_pairs={{0,4},{4,0},{8,12},{12,8},{1,5},{5,1},{9,13},{13,9},{2,6},{6,2},{1... | collective-permute-start | bytes 393224 | tf_op jit(solution)/shard_map/ppermute | solution.py:135
  114.2 5.0 %collective-permute-start.40 = (bf16[64,1024]{1,0:T(8,128)(2,1)S(1)}, bf16[64,1024]{1,0:T(8,128)(2,1)S(1)}, u32[]{:S(2)}, u32[]{:S(2)}) collective-permute-start(bf16[64,1024]{1,0:T(8,128)(2,1)S(1)} %add_convert_fusion.2.refs_0_), channel_id=1, source_target_pairs={{0,4},{4,0},{8,12},{12,8},{1,5},{5,1},{9,13},{13,9},{2,6},{6,2},{1... | collective-permute-start | bytes 393224 | tf_op jit(solution)/shard_map/ppermute | solution.py:135
  115.0 5.0 %collective-permute-start.41 = (bf16[64,1024]{1,0:T(8,128)(2,1)S(1)}, bf16[64,1024]{1,0:T(8,128)(2,1)S(1)}, u32[]{:S(2)}, u32[]{:S(2)}) collective-permute-start(bf16[64,1024]{1,0:T(8,128)(2,1)S(1)} %shard_map.70), channel_id=1, source_target_pairs={{0,1},{1,0},{2,3},{3,2},{4,5},{5,4},{6,7},{7,6},{8,9},{9,8},{10,11... | collective-permute-start | bytes 393224 | tf_op jit(solution)/shard_map/ppermute | solution.py:135
  116.5 8.7 %collective-permute-start.39 = (bf16[64,1024]{1,0:T(8,128)(2,1)S(1)}, bf16[64,1024]{1,0:T(8,128)(2,1)S(1)}, u32[]{:S(2)}, u32[]{:S(2)}) collective-permute-start(bf16[64,1024]{1,0:T(8,128)(2,1)S(1)} %get-tuple-element.431), channel_id=1, source_target_pairs={{0,8},{4,12},{8,0},{12,4},{1,9},{5,13},{9,1},{13,5},{2,10},{6,14},... | collective-permute-start | bytes 393224 | tf_op jit(solution)/shard_map/ppermute | solution.py:135
  120.0 6.0 %collective-permute-start.43 = (bf16[64,1024]{1,0:T(8,128)(2,1)S(1)}, bf16[64,1024]{1,0:T(8,128)(2,1)S(1)}, u32[]{:S(2)}, u32[]{:S(2)}) collective-permute-start(bf16[64,1024]{1,0:T(8,128)(2,1)S(1)} %get-tuple-element.429), channel_id=1, source_target_pairs={{0,2},{1,3},{2,0},{3,1},{4,6},{5,7},{6,4},{7,5},{8,10},{9,11},{10,... | collective-permute-start | bytes 393224 | tf_op jit(solution)/shard_map/ppermute | solution.py:135
  126.1 1.4 collective-permute-start.44
  126.2 6.4 %collective-permute-start.42 = (bf16[64,1024]{1,0:T(8,128)(2,1)S(1)}, bf16[64,1024]{1,0:T(8,128)(2,1)S(1)}, u32[]{:S(2)}, u32[]{:S(2)}) collective-permute-start(bf16[64,1024]{1,0:T(8,128)(2,1)S(1)} %add_convert_fusion.1.refs_0_), channel_id=1, source_target_pairs={{0,4},{4,0},{8,12},{12,8},{1,5},{5,1},{9,13},{13,9},{2,6},{6,2},{1... | collective-permute-start | bytes 393224 | tf_op jit(solution)/shard_map/ppermute | solution.py:135
  126.3 7.1 %collective-permute-start.45 = (bf16[64,1024]{1,0:T(8,128)(2,1)S(1)}, bf16[64,1024]{1,0:T(8,128)(2,1)S(1)}, u32[]{:S(2)}, u32[]{:S(2)}) collective-permute-start(bf16[64,1024]{1,0:T(8,128)(2,1)S(1)} %shard_map.72), channel_id=1, source_target_pairs={{0,1},{1,0},{2,3},{3,2},{4,5},{5,4},{6,7},{7,6},{8,9},{9,8},{10,11... | collective-permute-start | bytes 393224 | tf_op jit(solution)/shard_map/ppermute | solution.py:135
  128.5 6.9 %collective-permute-start.46 = (bf16[64,1024]{1,0:T(8,128)(2,1)S(1)}, bf16[64,1024]{1,0:T(8,128)(2,1)S(1)}, u32[]{:S(2)}, u32[]{:S(2)}) collective-permute-start(bf16[64,1024]{1,0:T(8,128)(2,1)S(1)} %shard_map.73), channel_id=1, source_target_pairs={{0,4},{4,0},{8,12},{12,8},{1,5},{5,1},{9,13},{13,9},{2,6},{6,2},{1... | collective-permute-start | bytes 393224 | tf_op jit(solution)/shard_map/ppermute | solution.py:135
  133.4 5.0 %collective-permute-start.47 = (bf16[64,1024]{1,0:T(8,128)(2,1)S(1)}, bf16[64,1024]{1,0:T(8,128)(2,1)S(1)}, u32[]{:S(2)}, u32[]{:S(2)}) collective-permute-start(bf16[64,1024]{1,0:T(8,128)(2,1)S(1)} %get-tuple-element.427), channel_id=1, source_target_pairs={{0,2},{1,3},{2,0},{3,1},{4,6},{5,7},{6,4},{7,5},{8,10},{9,11},{10,... | collective-permute-start | bytes 393224 | tf_op jit(solution)/shard_map/ppermute | solution.py:135
  138.5 1.4 collective-permute-start.48
  140.7 5.6 %collective-permute-start.49 = (bf16[64,1024]{1,0:T(8,128)(2,1)S(1)}, bf16[64,1024]{1,0:T(8,128)(2,1)S(1)}, u32[]{:S(2)}, u32[]{:S(2)}) collective-permute-start(bf16[64,1024]{1,0:T(8,128)(2,1)S(1)} %shard_map.76), channel_id=1, source_target_pairs={{0,4},{4,0},{8,12},{12,8},{1,5},{5,1},{9,13},{13,9},{2,6},{6,2},{1... | collective-permute-start | bytes 393224 | tf_op jit(solution)/shard_map/ppermute | solution.py:135
  146.4 8.3 %collective-permute-start.50 = (bf16[64,1024]{1,0:T(8,128)(2,1)S(1)}, bf16[64,1024]{1,0:T(8,128)(2,1)S(1)}, u32[]{:S(2)}, u32[]{:S(2)}) collective-permute-start(bf16[64,1024]{1,0:T(8,128)(2,1)S(1)} %broadcast_select_fusion.4), channel_id=1, source_target_pairs={{0,8},{4,12},{8,0},{12,4},{1,9},{5,13},{9,1},{13,5},{2,10},{6,14},... | collective-permute-start | bytes 393224 | tf_op jit(solution)/shard_map/ppermute | solution.py:135
  147.3 7.4 %copy-start.2 = (bf16[5,1024,64]{1,2,0:T(8,128)(2,1)}, bf16[5,1024,64]{1,2,0:T(8,128)(2,1)S(1)}, u32[]{:S(2)}) copy-start(bf16[5,1024,64]{1,2,0:T(8,128)(2,1)S(1)} %bitcast_dynamic-update-slice_fusion) | copy-start | bytes 1966084

commit v7 on v6

--- a/solution.py
+++ b/solution.py
@@ -259,16 +259,19 @@
 
         inverses[0] = order.block(inverse_blocks, 0)
         right = order.block(right_sides, 0)
-        for s in range(STREAMS):
+        def first(s):
             state[s]["total"], leaving = order.run(
                 lambda v, w: first_products(s, side_ref, v, w), right, inverses[0]
             )
             state[s]["flight"] = trade(leaving, "row", 1)
+
+        first(0)
         if steps_total > 1:
             base = order.run(lambda v: turned_sides(side_ref, v), right_sides)
+            load_factor(1)
         pair_sum(0)
         cross(0)
-        load_factor(1)
+        first(1)
         load_inverse(1)
 
         for step in range(1, steps_total):
@@ -279,11 +282,11 @@
             cross(1)
             factor_own(0, step)
             chip_sum(0)
-            solve(1, step - 1)
-            factor_other(1, step)
             older(step + 1, range(step - 1))
             load_factor(step + 1)
             load_inverse(step + 1)
+            solve(1, step - 1)
+            factor_other(1, step)
             residual(0, step)
             inverse_own(0, step)
             factor_own(1, step)

time: 156 us -> 152 us (0.974)
  waiting for transfers between devices: 58.9 us -> 53 us
  local copies, waits for them, and re-layouts: 16.6 us -> 21.5 us
  starting transfers between devices: 44.2 us -> 41.5 us
    ppermute x51, waiting for transfers between devices: 58.9 us -> 53 us  [trade(): return lax.ppermute(value, axis, [(i, i ^ step) for i in range(size)])]
    ppermute x51, starting transfers between devices: 44.2 us -> 41.5 us  [trade(): return lax.ppermute(value, axis, [(i, i ^ step) for i in range(size)])]
    squeeze x16, local copies, waits for them, and re-layouts: 14.4 us -> 16.9 us  [block(): self.last = lax.optimization_barrier(self.run(lambda v: v[index], blocks))]
  transfers between devices with their start and end apart: 51 -> 51, of which waited for: 22 -> 25; matrix products, arithmetic and copies ran while one was open for 9% -> 11% of each run, Pallas kernels for 20% -> 20%
where the time goes in v7:
time: 152 us
  waiting for transfers between devices  53 us (35%)
  starting transfers between devices  41.5 us (27%)
  Pallas kernels  32.2 us (21%)
  local copies, waits for them, and re-layouts  21.5 us (14%)
  other arithmetic  2.46 us (2%)
    ppermute x51, waiting for transfers between devices, trade(): return lax.ppermute(value, axis, [(i, i ^ step) for i in range(size)])  53 us
    ppermute x51, starting transfers between devices, trade(): return lax.ppermute(value, axis, [(i, i ^ step) for i in range(size)])  41.5 us
    pallas_call x38, Pallas kernels, product(): pl.pallas_call(functools.partial(product_kernel, len(units)), out_shape=j...  29.6 us
    squeeze x16, local copies, waits for them, and re-layouts, block(): self.last = lax.optimization_barrier(self.run(lambda v: v[index], blocks))  16.9 us
  transfers between devices with their start and end apart: 51, of which 25 were waited for; matrix products, arithmetic and copies ran while one was open for 11% of the time, Pallas kernels for 20%

profile of v7, /device:TPU:0, one launch (start us, length us, event | category | flops | bytes accessed | tf_op | source)
XLA Modules:
  0.0 151.7 jit_solution(2032526808108796706)
XLA Ops:
  0.0 1.8 %slice_bitcast_fusion.14.block = bf16[1024,1024]{1,0:T(8,128)(2,1)S(1)} fusion(bf16[5,1024,1024]{2,1,0:T(8,128)(2,1)} %param.4), kind=kLoop, calls=%fused_computation.14 | loop fusion | bytes 4194304 | tf_op jit(solution)/shard_map/squeeze | solution.py:128
  1.8 1.5 slice_bitcast_fusion.15.right
  3.2 0.9 shard_map.37
  4.1 3.1 %collective-permute-start = (bf16[64,1024]{1,0:T(8,128)(2,1)S(1)}, bf16[64,1024]{1,0:T(8,128)(2,1)S(1)}, u32[]{:S(2)}, u32[]{:S(2)}) collective-permute-start(bf16[64,1024]{1,0:T(8,128)(2,1)S(1)} %get-tuple-element.220), channel_id=1, source_target_pairs={{0,4},{4,0},{8,12},{12,8},{1,5},{5,1},{9,13},{13,9},{2,6},{6,2},{1... | collective-permute-start | bytes 393224 | tf_op jit(solution)/shard_map/ppermute | solution.py:135
  7.2 1.7 %copy-done.3 = bf16[5,1024,256]{2,1,0:T(8,128)(2,1)S(1)} copy-done((bf16[5,1024,256]{2,1,0:T(8,128)(2,1)S(1)}, bf16[5,1024,256]{2,1,0:T(8,128)(2,1)}, u32[]{:S(2)}) %copy-start.3) | copy-done | bytes 2621464
  8.9 0.9 shard_map.38
  9.9 1.0 copy-done.2
  10.8 1.8 %slice_bitcast_fusion.13.block = bf16[1024,1024]{1,0:T(8,128)(2,1)S(1)} fusion(bf16[10,1024,1024]{2,1,0:T(8,128)(2,1)} %param.3), kind=kLoop, calls=%fused_computation.13 | loop fusion | bytes 4194304 | tf_op jit(solution)/shard_map/squeeze | solution.py:128
  12.6 1.5 slice_bitcast_fusion.16
  14.2 2.6 %collective-permute-start.2 = (bf16[64,1024]{1,0:T(8,128)(2,1)S(1)}, bf16[64,1024]{1,0:T(8,128)(2,1)S(1)}, u32[]{:S(2)}, u32[]{:S(2)}) collective-permute-start(bf16[64,1024]{1,0:T(8,128)(2,1)S(1)} %get-tuple-element.457), channel_id=1, source_target_pairs={{0,8},{4,12},{8,0},{12,4},{1,9},{5,13},{9,1},{13,5},{2,10},{6,14},... | collective-permute-start | bytes 393224 | tf_op jit(solution)/shard_map/ppermute | solution.py:135
  16.8 0.9 shard_map.39
  17.7 1.8 %slice_bitcast_fusion.12.block = bf16[1024,1024]{1,0:T(8,128)(2,1)S(1)} fusion(bf16[5,1024,1024]{2,1,0:T(8,128)(2,1)} %param.4), kind=kLoop, calls=%fused_computation.12 | loop fusion | bytes 4194304 | tf_op jit(solution)/shard_map/squeeze | solution.py:128
  20.0 2.9 %collective-permute-done.2 = bf16[64,1024]{1,0:T(8,128)(2,1)S(1)} collective-permute-done((bf16[64,1024]{1,0:T(8,128)(2,1)S(1)}, bf16[64,1024]{1,0:T(8,128)(2,1)S(1)}, u32[]{:S(2)}, u32[]{:S(2)}) %collective-permute-start.2) | collective-permute-done | bytes 131104 | tf_op jit(solution)/shard_map/ppermute | solution.py:135
  23.8 1.8 %collective-permute-done.1 = bf16[64,1024]{1,0:T(8,128)(2,1)S(1)} collective-permute-done((bf16[64,1024]{1,0:T(8,128)(2,1)S(1)}, bf16[64,1024]{1,0:T(8,128)(2,1)S(1)}, u32[]{:S(2)}, u32[]{:S(2)}) %collective-permute-start.1) | collective-permute-done | bytes 131104 | tf_op jit(solution)/shard_map/ppermute | solution.py:135
  25.6 1.5 collective-permute-start.3
  27.1 1.3 collective-permute-done.4.refs_0_
  29.2 1.6 %collective-permute-start.7 = (bf16[64,1024]{1,0:T(8,128)(2,1)S(1)}, bf16[64,1024]{1,0:T(8,128)(2,1)S(1)}, u32[]{:S(2)}, u32[]{:S(2)}) collective-permute-start(bf16[64,1024]{1,0:T(8,128)(2,1)S(1)} %get-tuple-element.453), channel_id=1, source_target_pairs={{0,2},{1,3},{2,0},{3,1},{4,6},{5,7},{6,4},{7,5},{8,10},{9,11},{10,... | collective-permute-start | bytes 393224 | tf_op jit(solution)/shard_map/ppermute | solution.py:135
  30.8 1.8 %slice_bitcast_fusion.11.block = bf16[1024,1024]{1,0:T(8,128)(2,1)S(1)} fusion(bf16[10,1024,1024]{2,1,0:T(8,128)(2,1)} %param.3), kind=kLoop, calls=%fused_computation.11 | loop fusion | bytes 4194304 | tf_op jit(solution)/shard_map/squeeze | solution.py:128
  32.6 1.9 %slice_bitcast_fusion.10.block = bf16[1024,1024]{1,0:T(8,128)(2,1)S(1)} fusion(bf16[5,1024,1024]{2,1,0:T(8,128)(2,1)} %param.4), kind=kLoop, calls=%fused_computation.10 | loop fusion | bytes 4194304 | tf_op jit(solution)/shard_map/squeeze | solution.py:128
  37.0 1.9 %collective-permute-start.11 = (bf16[64,1024]{1,0:T(8,128)(2,1)S(1)}, bf16[64,1024]{1,0:T(8,128)(2,1)S(1)}, u32[]{:S(2)}, u32[]{:S(2)}) collective-permute-start(bf16[64,1024]{1,0:T(8,128)(2,1)S(1)} %shard_map.43), channel_id=1, source_target_pairs={{0,4},{4,0},{8,12},{12,8},{1,5},{5,1},{9,13},{13,9},{2,6},{6,2},{1... | collective-permute-start | bytes 393224 | tf_op jit(solution)/shard_map/ppermute | solution.py:135
  40.4 1.7 %collective-permute-start.9 = (bf16[64,1024]{1,0:T(8,128)(2,1)S(1)}, bf16[64,1024]{1,0:T(8,128)(2,1)S(1)}, u32[]{:S(2)}, u32[]{:S(2)}) collective-permute-start(bf16[64,1024]{1,0:T(8,128)(2,1)S(1)} %get-tuple-element.451), channel_id=1, source_target_pairs={{0,2},{1,3},{2,0},{3,1},{4,6},{5,7},{6,4},{7,5},{8,10},{9,11},{10,... | collective-permute-start | bytes 393224 | tf_op jit(solution)/shard_map/ppermute | solution.py:135
  42.1 1.8 %slice_bitcast_fusion.9.block = bf16[1024,1024]{1,0:T(8,128)(2,1)S(1)} fusion(bf16[10,1024,1024]{2,1,0:T(8,128)(2,1)} %param.3), kind=kLoop, calls=%fused_computation.9 | loop fusion | bytes 4194304 | tf_op jit(solution)/shard_map/squeeze | solution.py:128
  43.9 0.9 shard_map.45
  47.1 1.9 %collective-permute-start.13 = (bf16[64,1024]{1,0:T(8,128)(2,1)S(1)}, bf16[64,1024]{1,0:T(8,128)(2,1)S(1)}, u32[]{:S(2)}, u32[]{:S(2)}) collective-permute-start(bf16[64,1024]{1,0:T(8,128)(2,1)S(1)} %shard_map.47), channel_id=1, source_target_pairs={{0,4},{4,0},{8,12},{12,8},{1,5},{5,1},{9,13},{13,9},{2,6},{6,2},{1... | collective-permute-start | bytes 393224 | tf_op jit(solution)/shard_map/ppermute | solution.py:135
  49.7 3.6 %collective-permute-done.14 = bf16[64,1024]{1,0:T(8,128)(2,1)S(1)} collective-permute-done((bf16[64,1024]{1,0:T(8,128)(2,1)S(1)}, bf16[64,1024]{1,0:T(8,128)(2,1)S(1)}, u32[]{:S(2)}, u32[]{:S(2)}) %collective-permute-start.14) | collective-permute-done | bytes 131104 | tf_op jit(solution)/shard_map/ppermute | solution.py:135
  53.5 0.8 shard_map.49
  55.1 1.9 %collective-permute-start.15 = (bf16[64,1024]{1,0:T(8,128)(2,1)S(1)}, bf16[64,1024]{1,0:T(8,128)(2,1)S(1)}, u32[]{:S(2)}, u32[]{:S(2)}) collective-permute-start(bf16[64,1024]{1,0:T(8,128)(2,1)S(1)} %get-tuple-element.447), channel_id=1, source_target_pairs={{0,8},{4,12},{8,0},{12,4},{1,9},{5,13},{9,1},{13,5},{2,10},{6,14},... | collective-permute-start | bytes 393224 | tf_op jit(solution)/shard_map/ppermute | solution.py:135
  56.9 1.5 collective-permute-done.16.refs_0_
  58.4 0.8 shard_map.50
  60.1 0.9 shard_map.51.refs_4_
  61.2 1.8 %slice_bitcast_fusion.6.block = bf16[1024,1024]{1,0:T(8,128)(2,1)S(1)} fusion(bf16[5,1024,1024]{2,1,0:T(8,128)(2,1)} %param.4), kind=kLoop, calls=%fused_computation.6 | loop fusion | bytes 4194304 | tf_op jit(solution)/shard_map/squeeze | solution.py:128
  63.0 1.1 collective-permute-done.15
  66.4 2.1 %collective-permute-start.23 = (bf16[64,1024]{1,0:T(8,128)(2,1)S(1)}, bf16[64,1024]{1,0:T(8,128)(2,1)S(1)}, u32[]{:S(2)}, u32[]{:S(2)}) collective-permute-start(bf16[64,1024]{1,0:T(8,128)(2,1)S(1)} %shard_map.53), channel_id=1, source_target_pairs={{0,4},{4,0},{8,12},{12,8},{1,5},{5,1},{9,13},{13,9},{2,6},{6,2},{1... | collective-permute-start | bytes 393224 | tf_op jit(solution)/shard_map/ppermute | solution.py:135
  70.0 1.2 collective-permute-start.21
  71.4 1.1 shard_map.55
  73.3 1.8 %collective-permute-start.26 = (bf16[64,1024]{1,0:T(8,128)(2,1)S(1)}, bf16[64,1024]{1,0:T(8,128)(2,1)S(1)}, u32[]{:S(2)}, u32[]{:S(2)}) collective-permute-start(bf16[64,1024]{1,0:T(8,128)(2,1)S(1)} %get-tuple-element.441), channel_id=1, source_target_pairs={{0,8},{4,12},{8,0},{12,4},{1,9},{5,13},{9,1},{13,5},{2,10},{6,14},... | collective-permute-start | bytes 393224 | tf_op jit(solution)/shard_map/ppermute | solution.py:135
  77.5 3.9 %collective-permute-done.26 = bf16[64,1024]{1,0:T(8,128)(2,1)S(1)} collective-permute-done((bf16[64,1024]{1,0:T(8,128)(2,1)S(1)}, bf16[64,1024]{1,0:T(8,128)(2,1)S(1)}, u32[]{:S(2)}, u32[]{:S(2)}) %collective-permute-start.26) | collective-permute-done | bytes 131104 | tf_op jit(solution)/shard_map/ppermute | solution.py:135
  82.3 1.8 %collective-permute-done.25 = bf16[64,1024]{1,0:T(8,128)(2,1)S(1)} collective-permute-done((bf16[64,1024]{1,0:T(8,128)(2,1)S(1)}, bf16[64,1024]{1,0:T(8,128)(2,1)S(1)}, u32[]{:S(2)}, u32[]{:S(2)}) %collective-permute-start.25) | collective-permute-done | bytes 131104 | tf_op jit(solution)/shard_map/ppermute | solution.py:135
  84.2 0.9 collective-permute-start.27
  85.1 1.6 %collective-permute-done.28.refs_0_ = bf16[64,1024]{1,0:T(8,128)(2,1)S(1)} collective-permute-done((bf16[64,1024]{1,0:T(8,128)(2,1)S(1)}, bf16[64,1024]{1,0:T(8,128)(2,1)S(1)}, u32[]{:S(2)}, u32[]{:S(2)}) %collective-permute-start.28) | collective-permute-done | bytes 131104 | tf_op jit(solution)/shard_map/ppermute | solution.py:135
  87.5 0.9 collective-permute-start.31
  88.6 0.9 shard_map.61.refs_4_
  89.7 0.9 shard_map.62.refs_4_
  90.8 1.8 %slice_bitcast_fusion.1.block = bf16[1024,1024]{1,0:T(8,128)(2,1)S(1)} fusion(bf16[5,1024,1024]{2,1,0:T(8,128)(2,1)} %param.4), kind=kLoop, calls=%fused_computation.1 | loop fusion | bytes 4194304 | tf_op jit(solution)/shard_map/squeeze | solution.py:128
  93.2 0.8 shard_map.63
  95.4 2.0 %collective-permute-start.35 = (bf16[64,1024]{1,0:T(8,128)(2,1)S(1)}, bf16[64,1024]{1,0:T(8,128)(2,1)S(1)}, u32[]{:S(2)}, u32[]{:S(2)}) collective-permute-start(bf16[64,1024]{1,0:T(8,128)(2,1)S(1)} %shard_map.64), channel_id=1, source_target_pairs={{0,4},{4,0},{8,12},{12,8},{1,5},{5,1},{9,13},{13,9},{2,6},{6,2},{1... | collective-permute-start | bytes 393224 | tf_op jit(solution)/shard_map/ppermute | solution.py:135
  98.9 0.9 collective-permute-start.33
  100.0 0.9 shard_map.66
  101.7 1.8 %collective-permute-start.38 = (bf16[64,1024]{1,0:T(8,128)(2,1)S(1)}, bf16[64,1024]{1,0:T(8,128)(2,1)S(1)}, u32[]{:S(2)}, u32[]{:S(2)}) collective-permute-start(bf16[64,1024]{1,0:T(8,128)(2,1)S(1)} %get-tuple-element.433), channel_id=1, source_target_pairs={{0,8},{4,12},{8,0},{12,4},{1,9},{5,13},{9,1},{13,5},{2,10},{6,14},... | collective-permute-start | bytes 393224 | tf_op jit(solution)/shard_map/ppermute | solution.py:135
  104.9 0.9 collective-permute-start.37
  106.6 3.2 %collective-permute-done.38 = bf16[64,1024]{1,0:T(8,128)(2,1)S(1)} collective-permute-done((bf16[64,1024]{1,0:T(8,128)(2,1)S(1)}, bf16[64,1024]{1,0:T(8,128)(2,1)S(1)}, u32[]{:S(2)}, u32[]{:S(2)}) %collective-permute-start.38) | collective-permute-done | bytes 131104 | tf_op jit(solution)/shard_map/ppermute | solution.py:135
  110.8 1.8 %collective-permute-done.37 = bf16[64,1024]{1,0:T(8,128)(2,1)S(1)} collective-permute-done((bf16[64,1024]{1,0:T(8,128)(2,1)S(1)}, bf16[64,1024]{1,0:T(8,128)(2,1)S(1)}, u32[]{:S(2)}, u32[]{:S(2)}) %collective-permute-start.37) | collective-permute-done | bytes 131104 | tf_op jit(solution)/shard_map/ppermute | solution.py:135
  112.6 1.2 collective-permute-start.39
  113.9 1.3 collective-permute-done.40.refs_0_
  115.9 1.3 collective-permute-start.43
  117.2 4.2 %collective-permute-done.39 = bf16[64,1024]{1,0:T(8,128)(2,1)S(1)} collective-permute-done((bf16[64,1024]{1,0:T(8,128)(2,1)S(1)}, bf16[64,1024]{1,0:T(8,128)(2,1)S(1)}, u32[]{:S(2)}, u32[]{:S(2)}) %collective-permute-start.39) | collective-permute-done | bytes 131104 | tf_op jit(solution)/shard_map/ppermute | solution.py:135
  124.6 1.1 collective-permute-start.46
  125.8 3.2 %collective-permute-done.42.refs_0_ = bf16[64,1024]{1,0:T(8,128)(2,1)S(1)} collective-permute-done((bf16[64,1024]{1,0:T(8,128)(2,1)S(1)}, bf16[64,1024]{1,0:T(8,128)(2,1)S(1)}, u32[]{:S(2)}, u32[]{:S(2)}) %collective-permute-start.42) | collective-permute-done | bytes 131104 | tf_op jit(solution)/shard_map/ppermute | solution.py:135
  129.8 1.3 collective-permute-start.47
  131.9 3.0 %collective-permute-done.47 = bf16[64,1024]{1,0:T(8,128)(2,1)S(1)} collective-permute-done((bf16[64,1024]{1,0:T(8,128)(2,1)S(1)}, bf16[64,1024]{1,0:T(8,128)(2,1)S(1)}, u32[]{:S(2)}, u32[]{:S(2)}) %collective-permute-start.47) | collective-permute-done | bytes 131104 | tf_op jit(solution)/shard_map/ppermute | solution.py:135
  135.0 1.3 collective-permute-done.48
  138.2 4.5 %collective-permute-done.49 = bf16[64,1024]{1,0:T(8,128)(2,1)S(1)} collective-permute-done((bf16[64,1024]{1,0:T(8,128)(2,1)S(1)}, bf16[64,1024]{1,0:T(8,128)(2,1)S(1)}, u32[]{:S(2)}, u32[]{:S(2)}) %collective-permute-start.49) | collective-permute-done | bytes 131104 | tf_op jit(solution)/shard_map/ppermute | solution.py:135
  142.7 1.3 collective-permute-start.50
  144.1 6.9 %collective-permute-done.50 = bf16[64,1024]{1,0:T(8,128)(2,1)S(1)} collective-permute-done((bf16[64,1024]{1,0:T(8,128)(2,1)S(1)}, bf16[64,1024]{1,0:T(8,128)(2,1)S(1)}, u32[]{:S(2)}, u32[]{:S(2)}) %collective-permute-start.50) | collective-permute-done | bytes 131104 | tf_op jit(solution)/shard_map/ppermute | solution.py:135
  (162 shorter events, 36.6 us)
Async XLA Ops:
  1.8 5.4 %copy-start = (bf16[1024,1024]{1,0:T(8,128)(2,1)}, bf16[1024,1024]{1,0:T(8,128)(2,1)S(1)}, u32[]{:S(2)}) copy-start(bf16[1024,1024]{1,0:T(8,128)(2,1)S(1)} %slice_bitcast_fusion.14.block) | copy-start | bytes 6291460
  4.1 10.0 %collective-permute-start = (bf16[64,1024]{1,0:T(8,128)(2,1)S(1)}, bf16[64,1024]{1,0:T(8,128)(2,1)S(1)}, u32[]{:S(2)}, u32[]{:S(2)}) collective-permute-start(bf16[64,1024]{1,0:T(8,128)(2,1)S(1)} %get-tuple-element.220), channel_id=1, source_target_pairs={{0,4},{4,0},{8,12},{12,8},{1,5},{5,1},{9,13},{13,9},{2,6},{6,2},{1... | collective-permute-start | bytes 393224 | tf_op jit(solution)/shard_map/ppermute | solution.py:135
  7.2 1.7 %copy-start.3 = (bf16[5,1024,256]{2,1,0:T(8,128)(2,1)S(1)}, bf16[5,1024,256]{2,1,0:T(8,128)(2,1)}, u32[]{:S(2)}) copy-start(bf16[5,1024,256]{2,1,0:T(8,128)(2,1)} %sides) | copy-start | bytes 7864324
  9.8 1.0 copy-start.2
  12.6 4.2 %copy-start.1 = (bf16[1024,1024]{1,0:T(8,128)(2,1)S(1)}, bf16[1024,1024]{1,0:T(8,128)(2,1)}, u32[]{:S(2)}) copy-start(bf16[1024,1024]{1,0:T(8,128)(2,1)} %copy-done) | copy-start | bytes 6291460
  14.2 8.7 %collective-permute-start.2 = (bf16[64,1024]{1,0:T(8,128)(2,1)S(1)}, bf16[64,1024]{1,0:T(8,128)(2,1)S(1)}, u32[]{:S(2)}, u32[]{:S(2)}) collective-permute-start(bf16[64,1024]{1,0:T(8,128)(2,1)S(1)} %get-tuple-element.457), channel_id=1, source_target_pairs={{0,8},{4,12},{8,0},{12,4},{1,9},{5,13},{9,1},{13,5},{2,10},{6,14},... | collective-permute-start | bytes 393224 | tf_op jit(solution)/shard_map/ppermute | solution.py:135
  19.5 6.1 %collective-permute-start.1 = (bf16[64,1024]{1,0:T(8,128)(2,1)S(1)}, bf16[64,1024]{1,0:T(8,128)(2,1)S(1)}, u32[]{:S(2)}, u32[]{:S(2)}) collective-permute-start(bf16[64,1024]{1,0:T(8,128)(2,1)S(1)} %get-tuple-element.228), channel_id=1, source_target_pairs={{0,4},{4,0},{8,12},{12,8},{1,5},{5,1},{9,13},{13,9},{2,6},{6,2},{1... | collective-permute-start | bytes 393224 | tf_op jit(solution)/shard_map/ppermute | solution.py:135
  22.9 5.5 %collective-permute-start.4 = (bf16[64,1024]{1,0:T(8,128)(2,1)S(1)}, bf16[64,1024]{1,0:T(8,128)(2,1)S(1)}, u32[]{:S(2)}, u32[]{:S(2)}) collective-permute-start(bf16[64,1024]{1,0:T(8,128)(2,1)S(1)} %add_convert_fusion.8.refs_0_.refs_1_), channel_id=1, source_target_pairs={{0,4},{4,0},{8,12},{12,8},{1,5},{5,1},{9,13},{13,9},{2,6},{6,2},{1... | collective-permute-start | bytes 393224 | tf_op jit(solution)/shard_map/ppermute | solution.py:135
  23.7 5.4 %collective-permute-start.5 = (bf16[64,1024]{1,0:T(8,128)(2,1)S(1)}, bf16[64,1024]{1,0:T(8,128)(2,1)S(1)}, u32[]{:S(2)}, u32[]{:S(2)}) collective-permute-start(bf16[64,1024]{1,0:T(8,128)(2,1)S(1)} %shard_map.40), channel_id=1, source_target_pairs={{0,1},{1,0},{2,3},{3,2},{4,5},{5,4},{6,7},{7,6},{8,9},{9,8},{10,11... | collective-permute-start | bytes 393224 | tf_op jit(solution)/shard_map/ppermute | solution.py:135
  25.6 8.9 %collective-permute-start.3 = (bf16[64,1024]{1,0:T(8,128)(2,1)S(1)}, bf16[64,1024]{1,0:T(8,128)(2,1)S(1)}, u32[]{:S(2)}, u32[]{:S(2)}) collective-permute-start(bf16[64,1024]{1,0:T(8,128)(2,1)S(1)} %get-tuple-element.455), channel_id=1, source_target_pairs={{0,8},{4,12},{8,0},{12,4},{1,9},{5,13},{9,1},{13,5},{2,10},{6,14},... | collective-permute-start | bytes 393224 | tf_op jit(solution)/shard_map/ppermute | solution.py:135
  29.2 6.4 %collective-permute-start.7 = (bf16[64,1024]{1,0:T(8,128)(2,1)S(1)}, bf16[64,1024]{1,0:T(8,128)(2,1)S(1)}, u32[]{:S(2)}, u32[]{:S(2)}) collective-permute-start(bf16[64,1024]{1,0:T(8,128)(2,1)S(1)} %get-tuple-element.453), channel_id=1, source_target_pairs={{0,2},{1,3},{2,0},{3,1},{4,6},{5,7},{6,4},{7,5},{8,10},{9,11},{10,... | collective-permute-start | bytes 393224 | tf_op jit(solution)/shard_map/ppermute | solution.py:135
  32.5 27.4 %slice-start = ((s8[20971520]{0:T(1024)(128)(4,1)}), s8[4194304]{0:T(1024)(128)(4,1)S(1)}, s32[]{:S(2)}) async-start(s8[20971520]{0:T(1024)(128)(4,1)} %bitcast.71), calls=%async_computation | async-start | bytes 8388608
  34.5 5.0 %collective-permute-start.6 = (bf16[64,1024]{1,0:T(8,128)(2,1)S(1)}, bf16[64,1024]{1,0:T(8,128)(2,1)S(1)}, u32[]{:S(2)}, u32[]{:S(2)}) collective-permute-start(bf16[64,1024]{1,0:T(8,128)(2,1)S(1)} %add_convert_fusion.7.refs_0_.refs_3_), channel_id=1, source_target_pairs={{0,4},{4,0},{8,12},{12,8},{1,5},{5,1},{9,13},{13,9},{2,6},{6,2},{1... | collective-permute-start | bytes 393224 | tf_op jit(solution)/shard_map/ppermute | solution.py:135
  35.5 4.8 %collective-permute-start.8 = (bf16[64,1024]{1,0:T(8,128)(2,1)S(1)}, bf16[64,1024]{1,0:T(8,128)(2,1)S(1)}, u32[]{:S(2)}, u32[]{:S(2)}) collective-permute-start(bf16[64,1024]{1,0:T(8,128)(2,1)S(1)} %shard_map.42), channel_id=1, source_target_pairs={{0,1},{1,0},{2,3},{3,2},{4,5},{5,4},{6,7},{7,6},{8,9},{9,8},{10,11... | collective-permute-start | bytes 393224 | tf_op jit(solution)/shard_map/ppermute | solution.py:135
  35.7 24.3 %slice-start.1 = ((s8[20971520]{0:T(1024)(128)(4,1)}), s8[4194304]{0:T(1024)(128)(4,1)S(1)}, s32[]{:S(2)}) async-start(s8[20971520]{0:T(1024)(128)(4,1)} %bitcast.71), calls=%async_computation.1 | async-start | bytes 8388608
  35.7 9.1 %collective-permute-start.10 = (bf16[64,1024]{1,0:T(8,128)(2,1)S(1)}, bf16[64,1024]{1,0:T(8,128)(2,1)S(1)}, u32[]{:S(2)}, u32[]{:S(2)}) collective-permute-start(bf16[64,1024]{1,0:T(8,128)(2,1)S(1)} %subtract_convert_fusion.7.refs_0_), channel_id=1, source_target_pairs={{0,1},{1,0},{2,3},{3,2},{4,5},{5,4},{6,7},{7,6},{8,9},{9,8},{10,11... | collective-permute-start | bytes 393224 | tf_op jit(solution)/shard_map/ppermute | solution.py:135
  37.0 8.6 %collective-permute-start.11 = (bf16[64,1024]{1,0:T(8,128)(2,1)S(1)}, bf16[64,1024]{1,0:T(8,128)(2,1)S(1)}, u32[]{:S(2)}, u32[]{:S(2)}) collective-permute-start(bf16[64,1024]{1,0:T(8,128)(2,1)S(1)} %shard_map.43), channel_id=1, source_target_pairs={{0,4},{4,0},{8,12},{12,8},{1,5},{5,1},{9,13},{13,9},{2,6},{6,2},{1... | collective-permute-start | bytes 393224 | tf_op jit(solution)/shard_map/ppermute | solution.py:135
  40.4 19.6 %slice-start.2 = ((s8[20971520]{0:T(1024)(128)(4,1)}), s8[4194304]{0:T(1024)(128)(4,1)S(1)}, s32[]{:S(2)}) async-start(s8[20971520]{0:T(1024)(128)(4,1)} %bitcast.71), calls=%async_computation.2 | async-start | bytes 8388608
  40.4 5.7 %collective-permute-start.9 = (bf16[64,1024]{1,0:T(8,128)(2,1)S(1)}, bf16[64,1024]{1,0:T(8,128)(2,1)S(1)}, u32[]{:S(2)}, u32[]{:S(2)}) collective-permute-start(bf16[64,1024]{1,0:T(8,128)(2,1)S(1)} %get-tuple-element.451), channel_id=1, source_target_pairs={{0,2},{1,3},{2,0},{3,1},{4,6},{5,7},{6,4},{7,5},{8,10},{9,11},{10,... | collective-permute-start | bytes 393224 | tf_op jit(solution)/shard_map/ppermute | solution.py:135
  45.5 14.4 %slice-start.3 = ((s8[20971520]{0:T(1024)(128)(4,1)}), s8[4194304]{0:T(1024)(128)(4,1)S(1)}, s32[]{:S(2)}) async-start(s8[20971520]{0:T(1024)(128)(4,1)} %bitcast.71), calls=%async_computation.3 | async-start | bytes 8388608
  45.6 7.8 %collective-permute-start.14 = (bf16[64,1024]{1,0:T(8,128)(2,1)S(1)}, bf16[64,1024]{1,0:T(8,128)(2,1)S(1)}, u32[]{:S(2)}, u32[]{:S(2)}) collective-permute-start(bf16[64,1024]{1,0:T(8,128)(2,1)S(1)} %get-tuple-element.449), channel_id=1, source_target_pairs={{0,8},{4,12},{8,0},{12,4},{1,9},{5,13},{9,1},{13,5},{2,10},{6,14},... | collective-permute-start | bytes 393224 | tf_op jit(solution)/shard_map/ppermute | solution.py:135
  46.1 2.9 %collective-permute-start.12 = (bf16[64,1024]{1,0:T(8,128)(2,1)S(1)}, bf16[64,1024]{1,0:T(8,128)(2,1)S(1)}, u32[]{:S(2)}, u32[]{:S(2)}) collective-permute-start(bf16[64,1024]{1,0:T(8,128)(2,1)S(1)} %subtract_convert_fusion.6.refs_0_), channel_id=1, source_target_pairs={{0,1},{1,0},{2,3},{3,2},{4,5},{5,4},{6,7},{7,6},{8,9},{9,8},{10,11... | collective-permute-start | bytes 393224 | tf_op jit(solution)/shard_map/ppermute | solution.py:135
  47.0 12.9 %slice-start.4 = ((s8[20971520]{0:T(1024)(128)(4,1)}), s8[4194304]{0:T(1024)(128)(4,1)S(1)}, s32[]{:S(2)}) async-start(s8[20971520]{0:T(1024)(128)(4,1)} %bitcast.71), calls=%async_computation.4 | async-start | bytes 8388608
  47.1 8.0 %collective-permute-start.13 = (bf16[64,1024]{1,0:T(8,128)(2,1)S(1)}, bf16[64,1024]{1,0:T(8,128)(2,1)S(1)}, u32[]{:S(2)}, u32[]{:S(2)}) collective-permute-start(bf16[64,1024]{1,0:T(8,128)(2,1)S(1)} %shard_map.47), channel_id=1, source_target_pairs={{0,4},{4,0},{8,12},{12,8},{1,5},{5,1},{9,13},{13,9},{2,6},{6,2},{1... | collective-permute-start | bytes 393224 | tf_op jit(solution)/shard_map/ppermute | solution.py:135
  53.4 5.0 %collective-permute-start.16 = (bf16[64,1024]{1,0:T(8,128)(2,1)S(1)}, bf16[64,1024]{1,0:T(8,128)(2,1)S(1)}, u32[]{:S(2)}, u32[]{:S(2)}) collective-permute-start(bf16[64,1024]{1,0:T(8,128)(2,1)S(1)} %add_convert_fusion.6.refs_0_.refs_1_), channel_id=1, source_target_pairs={{0,4},{4,0},{8,12},{12,8},{1,5},{5,1},{9,13},{13,9},{2,6},{6,2},{1... | collective-permute-start | bytes 393224 | tf_op jit(solution)/shard_map/ppermute | solution.py:135
  54.2 5.0 %collective-permute-start.17 = (bf16[64,1024]{1,0:T(8,128)(2,1)S(1)}, bf16[64,1024]{1,0:T(8,128)(2,1)S(1)}, u32[]{:S(2)}, u32[]{:S(2)}) collective-permute-start(bf16[64,1024]{1,0:T(8,128)(2,1)S(1)} %shard_map.49), channel_id=1, source_target_pairs={{0,1},{1,0},{2,3},{3,2},{4,5},{5,4},{6,7},{7,6},{8,9},{9,8},{10,11... | collective-permute-start | bytes 393224 | tf_op jit(solution)/shard_map/ppermute | solution.py:135
  55.1 9.0 %collective-permute-start.15 = (bf16[64,1024]{1,0:T(8,128)(2,1)S(1)}, bf16[64,1024]{1,0:T(8,128)(2,1)S(1)}, u32[]{:S(2)}, u32[]{:S(2)}) collective-permute-start(bf16[64,1024]{1,0:T(8,128)(2,1)S(1)} %get-tuple-element.447), channel_id=1, source_target_pairs={{0,8},{4,12},{8,0},{12,4},{1,9},{5,13},{9,1},{13,5},{2,10},{6,14},... | collective-permute-start | bytes 393224 | tf_op jit(solution)/shard_map/ppermute | solution.py:135
  59.2 5.8 %collective-permute-start.19 = (bf16[64,1024]{1,0:T(8,128)(2,1)S(1)}, bf16[64,1024]{1,0:T(8,128)(2,1)S(1)}, u32[]{:S(2)}, u32[]{:S(2)}) collective-permute-start(bf16[64,1024]{1,0:T(8,128)(2,1)S(1)} %get-tuple-element.445), channel_id=1, source_target_pairs={{0,2},{1,3},{2,0},{3,1},{4,6},{5,7},{6,4},{7,5},{8,10},{9,11},{10,... | collective-permute-start | bytes 393224 | tf_op jit(solution)/shard_map/ppermute | solution.py:135
  64.1 5.0 %collective-permute-start.18 = (bf16[64,1024]{1,0:T(8,128)(2,1)S(1)}, bf16[64,1024]{1,0:T(8,128)(2,1)S(1)}, u32[]{:S(2)}, u32[]{:S(2)}) collective-permute-start(bf16[64,1024]{1,0:T(8,128)(2,1)S(1)} %add_convert_fusion.5.refs_0_.refs_3_), channel_id=1, source_target_pairs={{0,4},{4,0},{8,12},{12,8},{1,5},{5,1},{9,13},{13,9},{2,6},{6,2},{1... | collective-permute-start | bytes 393224 | tf_op jit(solution)/shard_map/ppermute | solution.py:135
  65.0 5.0 %collective-permute-start.20 = (bf16[64,1024]{1,0:T(8,128)(2,1)S(1)}, bf16[64,1024]{1,0:T(8,128)(2,1)S(1)}, u32[]{:S(2)}, u32[]{:S(2)}) collective-permute-start(bf16[64,1024]{1,0:T(8,128)(2,1)S(1)} %shard_map.52), channel_id=1, source_target_pairs={{0,1},{1,0},{2,3},{3,2},{4,5},{5,4},{6,7},{7,6},{8,9},{9,8},{10,11... | collective-permute-start | bytes 393224 | tf_op jit(solution)/shard_map/ppermute | solution.py:135
  65.1 7.3 %collective-permute-start.22 = (bf16[64,1024]{1,0:T(8,128)(2,1)S(1)}, bf16[64,1024]{1,0:T(8,128)(2,1)S(1)}, u32[]{:S(2)}, u32[]{:S(2)}) collective-permute-start(bf16[64,1024]{1,0:T(8,128)(2,1)S(1)} %subtract_convert_fusion.5.refs_0_), channel_id=1, source_target_pairs={{0,1},{1,0},{2,3},{3,2},{4,5},{5,4},{6,7},{7,6},{8,9},{9,8},{10,11... | collective-permute-start | bytes 393224 | tf_op jit(solution)/shard_map/ppermute | solution.py:135
  66.4 6.8 %collective-permute-start.23 = (bf16[64,1024]{1,0:T(8,128)(2,1)S(1)}, bf16[64,1024]{1,0:T(8,128)(2,1)S(1)}, u32[]{:S(2)}, u32[]{:S(2)}) collective-permute-start(bf16[64,1024]{1,0:T(8,128)(2,1)S(1)} %shard_map.53), channel_id=1, source_target_pairs={{0,4},{4,0},{8,12},{12,8},{1,5},{5,1},{9,13},{13,9},{2,6},{6,2},{1... | collective-permute-start | bytes 393224 | tf_op jit(solution)/shard_map/ppermute | solution.py:135
  70.0 5.1 %collective-permute-start.21 = (bf16[64,1024]{1,0:T(8,128)(2,1)S(1)}, bf16[64,1024]{1,0:T(8,128)(2,1)S(1)}, u32[]{:S(2)}, u32[]{:S(2)}) collective-permute-start(bf16[64,1024]{1,0:T(8,128)(2,1)S(1)} %get-tuple-element.443), channel_id=1, source_target_pairs={{0,2},{1,3},{2,0},{3,1},{4,6},{5,7},{6,4},{7,5},{8,10},{9,11},{10,... | collective-permute-start | bytes 393224 | tf_op jit(solution)/shard_map/ppermute | solution.py:135
  73.3 8.1 %collective-permute-start.26 = (bf16[64,1024]{1,0:T(8,128)(2,1)S(1)}, bf16[64,1024]{1,0:T(8,128)(2,1)S(1)}, u32[]{:S(2)}, u32[]{:S(2)}) collective-permute-start(bf16[64,1024]{1,0:T(8,128)(2,1)S(1)} %get-tuple-element.441), channel_id=1, source_target_pairs={{0,8},{4,12},{8,0},{12,4},{1,9},{5,13},{9,1},{13,5},{2,10},{6,14},... | collective-permute-start | bytes 393224 | tf_op jit(solution)/shard_map/ppermute | solution.py:135
  75.1 1.6 %collective-permute-start.24 = (bf16[64,1024]{1,0:T(8,128)(2,1)S(1)}, bf16[64,1024]{1,0:T(8,128)(2,1)S(1)}, u32[]{:S(2)}, u32[]{:S(2)}) collective-permute-start(bf16[64,1024]{1,0:T(8,128)(2,1)S(1)} %subtract_convert_fusion.4.refs_0_), channel_id=1, source_target_pairs={{0,1},{1,0},{2,3},{3,2},{4,5},{5,4},{6,7},{7,6},{8,9},{9,8},{10,11... | collective-permute-start | bytes 393224 | tf_op jit(solution)/shard_map/ppermute | solution.py:135
  76.0 8.1 %collective-permute-start.25 = (bf16[64,1024]{1,0:T(8,128)(2,1)S(1)}, bf16[64,1024]{1,0:T(8,128)(2,1)S(1)}, u32[]{:S(2)}, u32[]{:S(2)}) collective-permute-start(bf16[64,1024]{1,0:T(8,128)(2,1)S(1)} %shard_map.57), channel_id=1, source_target_pairs={{0,4},{4,0},{8,12},{12,8},{1,5},{5,1},{9,13},{13,9},{2,6},{6,2},{1... | collective-permute-start | bytes 393224 | tf_op jit(solution)/shard_map/ppermute | solution.py:135
  81.4 5.3 %collective-permute-start.28 = (bf16[64,1024]{1,0:T(8,128)(2,1)S(1)}, bf16[64,1024]{1,0:T(8,128)(2,1)S(1)}, u32[]{:S(2)}, u32[]{:S(2)}) collective-permute-start(bf16[64,1024]{1,0:T(8,128)(2,1)S(1)} %add_convert_fusion.4.refs_0_.refs_1_), channel_id=1, source_target_pairs={{0,4},{4,0},{8,12},{12,8},{1,5},{5,1},{9,13},{13,9},{2,6},{6,2},{1... | collective-permute-start | bytes 393224 | tf_op jit(solution)/shard_map/ppermute | solution.py:135
  82.2 5.3 %collective-permute-start.29 = (bf16[64,1024]{1,0:T(8,128)(2,1)S(1)}, bf16[64,1024]{1,0:T(8,128)(2,1)S(1)}, u32[]{:S(2)}, u32[]{:S(2)}) collective-permute-start(bf16[64,1024]{1,0:T(8,128)(2,1)S(1)} %shard_map.59), channel_id=1, source_target_pairs={{0,1},{1,0},{2,3},{3,2},{4,5},{5,4},{6,7},{7,6},{8,9},{9,8},{10,11... | collective-permute-start | bytes 393224 | tf_op jit(solution)/shard_map/ppermute | solution.py:135
  84.2 8.8 %collective-permute-start.27 = (bf16[64,1024]{1,0:T(8,128)(2,1)S(1)}, bf16[64,1024]{1,0:T(8,128)(2,1)S(1)}, u32[]{:S(2)}, u32[]{:S(2)}) collective-permute-start(bf16[64,1024]{1,0:T(8,128)(2,1)S(1)} %get-tuple-element.439), channel_id=1, source_target_pairs={{0,8},{4,12},{8,0},{12,4},{1,9},{5,13},{9,1},{13,5},{2,10},{6,14},... | collective-permute-start | bytes 393224 | tf_op jit(solution)/shard_map/ppermute | solution.py:135
  87.5 6.5 %collective-permute-start.31 = (bf16[64,1024]{1,0:T(8,128)(2,1)S(1)}, bf16[64,1024]{1,0:T(8,128)(2,1)S(1)}, u32[]{:S(2)}, u32[]{:S(2)}) collective-permute-start(bf16[64,1024]{1,0:T(8,128)(2,1)S(1)} %get-tuple-element.437), channel_id=1, source_target_pairs={{0,2},{1,3},{2,0},{3,1},{4,6},{5,7},{6,4},{7,5},{8,10},{9,11},{10,... | collective-permute-start | bytes 393224 | tf_op jit(solution)/shard_map/ppermute | solution.py:135
  93.0 5.0 %collective-permute-start.30 = (bf16[64,1024]{1,0:T(8,128)(2,1)S(1)}, bf16[64,1024]{1,0:T(8,128)(2,1)S(1)}, u32[]{:S(2)}, u32[]{:S(2)}) collective-permute-start(bf16[64,1024]{1,0:T(8,128)(2,1)S(1)} %add_convert_fusion.3.refs_0_.refs_3_), channel_id=1, source_target_pairs={{0,4},{4,0},{8,12},{12,8},{1,5},{5,1},{9,13},{13,9},{2,6},{6,2},{1... | collective-permute-start | bytes 393224 | tf_op jit(solution)/shard_map/ppermute | solution.py:135
  94.0 4.9 %collective-permute-start.32 = (bf16[64,1024]{1,0:T(8,128)(2,1)S(1)}, bf16[64,1024]{1,0:T(8,128)(2,1)S(1)}, u32[]{:S(2)}, u32[]{:S(2)}) collective-permute-start(bf16[64,1024]{1,0:T(8,128)(2,1)S(1)} %shard_map.63), channel_id=1, source_target_pairs={{0,1},{1,0},{2,3},{3,2},{4,5},{5,4},{6,7},{7,6},{8,9},{9,8},{10,11... | collective-permute-start | bytes 393224 | tf_op jit(solution)/shard_map/ppermute | solution.py:135
  94.1 6.8 %collective-permute-start.34 = (bf16[64,1024]{1,0:T(8,128)(2,1)S(1)}, bf16[64,1024]{1,0:T(8,128)(2,1)S(1)}, u32[]{:S(2)}, u32[]{:S(2)}) collective-permute-start(bf16[64,1024]{1,0:T(8,128)(2,1)S(1)} %subtract_convert_fusion.3.refs_0_), channel_id=1, source_target_pairs={{0,1},{1,0},{2,3},{3,2},{4,5},{5,4},{6,7},{7,6},{8,9},{9,8},{10,11... | collective-permute-start | bytes 393224 | tf_op jit(solution)/shard_map/ppermute | solution.py:135
  95.4 6.2 %collective-permute-start.35 = (bf16[64,1024]{1,0:T(8,128)(2,1)S(1)}, bf16[64,1024]{1,0:T(8,128)(2,1)S(1)}, u32[]{:S(2)}, u32[]{:S(2)}) collective-permute-start(bf16[64,1024]{1,0:T(8,128)(2,1)S(1)} %shard_map.64), channel_id=1, source_target_pairs={{0,4},{4,0},{8,12},{12,8},{1,5},{5,1},{9,13},{13,9},{2,6},{6,2},{1... | collective-permute-start | bytes 393224 | tf_op jit(solution)/shard_map/ppermute | solution.py:135
  98.9 5.0 %collective-permute-start.33 = (bf16[64,1024]{1,0:T(8,128)(2,1)S(1)}, bf16[64,1024]{1,0:T(8,128)(2,1)S(1)}, u32[]{:S(2)}, u32[]{:S(2)}) collective-permute-start(bf16[64,1024]{1,0:T(8,128)(2,1)S(1)} %get-tuple-element.435), channel_id=1, source_target_pairs={{0,2},{1,3},{2,0},{3,1},{4,6},{5,7},{6,4},{7,5},{8,10},{9,11},{10,... | collective-permute-start | bytes 393224 | tf_op jit(solution)/shard_map/ppermute | solution.py:135
  101.7 8.1 %collective-permute-start.38 = (bf16[64,1024]{1,0:T(8,128)(2,1)S(1)}, bf16[64,1024]{1,0:T(8,128)(2,1)S(1)}, u32[]{:S(2)}, u32[]{:S(2)}) collective-permute-start(bf16[64,1024]{1,0:T(8,128)(2,1)S(1)} %get-tuple-element.433), channel_id=1, source_target_pairs={{0,8},{4,12},{8,0},{12,4},{1,9},{5,13},{9,1},{13,5},{2,10},{6,14},... | collective-permute-start | bytes 393224 | tf_op jit(solution)/shard_map/ppermute | solution.py:135
  104.0 1.9 %collective-permute-start.36 = (bf16[64,1024]{1,0:T(8,128)(2,1)S(1)}, bf16[64,1024]{1,0:T(8,128)(2,1)S(1)}, u32[]{:S(2)}, u32[]{:S(2)}) collective-permute-start(bf16[64,1024]{1,0:T(8,128)(2,1)S(1)} %subtract_convert_fusion.2.refs_0_), channel_id=1, source_target_pairs={{0,1},{1,0},{2,3},{3,2},{4,5},{5,4},{6,7},{7,6},{8,9},{9,8},{10,11... | collective-permute-start | bytes 393224 | tf_op jit(solution)/shard_map/ppermute | solution.py:135
  104.9 7.7 %collective-permute-start.37 = (bf16[64,1024]{1,0:T(8,128)(2,1)S(1)}, bf16[64,1024]{1,0:T(8,128)(2,1)S(1)}, u32[]{:S(2)}, u32[]{:S(2)}) collective-permute-start(bf16[64,1024]{1,0:T(8,128)(2,1)S(1)} %shard_map.68), channel_id=1, source_target_pairs={{0,4},{4,0},{8,12},{12,8},{1,5},{5,1},{9,13},{13,9},{2,6},{6,2},{1... | collective-permute-start | bytes 393224 | tf_op jit(solution)/shard_map/ppermute | solution.py:135
  109.8 5.3 %collective-permute-start.40 = (bf16[64,1024]{1,0:T(8,128)(2,1)S(1)}, bf16[64,1024]{1,0:T(8,128)(2,1)S(1)}, u32[]{:S(2)}, u32[]{:S(2)}) collective-permute-start(bf16[64,1024]{1,0:T(8,128)(2,1)S(1)} %add_convert_fusion.2.refs_0_), channel_id=1, source_target_pairs={{0,4},{4,0},{8,12},{12,8},{1,5},{5,1},{9,13},{13,9},{2,6},{6,2},{1... | collective-permute-start | bytes 393224 | tf_op jit(solution)/shard_map/ppermute | solution.py:135
  110.7 5.2 %collective-permute-start.41 = (bf16[64,1024]{1,0:T(8,128)(2,1)S(1)}, bf16[64,1024]{1,0:T(8,128)(2,1)S(1)}, u32[]{:S(2)}, u32[]{:S(2)}) collective-permute-start(bf16[64,1024]{1,0:T(8,128)(2,1)S(1)} %shard_map.70), channel_id=1, source_target_pairs={{0,1},{1,0},{2,3},{3,2},{4,5},{5,4},{6,7},{7,6},{8,9},{9,8},{10,11... | collective-permute-start | bytes 393224 | tf_op jit(solution)/shard_map/ppermute | solution.py:135
  112.6 8.7 %collective-permute-start.39 = (bf16[64,1024]{1,0:T(8,128)(2,1)S(1)}, bf16[64,1024]{1,0:T(8,128)(2,1)S(1)}, u32[]{:S(2)}, u32[]{:S(2)}) collective-permute-start(bf16[64,1024]{1,0:T(8,128)(2,1)S(1)} %get-tuple-element.431), channel_id=1, source_target_pairs={{0,8},{4,12},{8,0},{12,4},{1,9},{5,13},{9,1},{13,5},{2,10},{6,14},... | collective-permute-start | bytes 393224 | tf_op jit(solution)/shard_map/ppermute | solution.py:135
  115.9 6.2 %collective-permute-start.43 = (bf16[64,1024]{1,0:T(8,128)(2,1)S(1)}, bf16[64,1024]{1,0:T(8,128)(2,1)S(1)}, u32[]{:S(2)}, u32[]{:S(2)}) collective-permute-start(bf16[64,1024]{1,0:T(8,128)(2,1)S(1)} %get-tuple-element.429), channel_id=1, source_target_pairs={{0,2},{1,3},{2,0},{3,1},{4,6},{5,7},{6,4},{7,5},{8,10},{9,11},{10,... | collective-permute-start | bytes 393224 | tf_op jit(solution)/shard_map/ppermute | solution.py:135
  122.4 1.4 collective-permute-start.44
  122.6 6.4 %collective-permute-start.42 = (bf16[64,1024]{1,0:T(8,128)(2,1)S(1)}, bf16[64,1024]{1,0:T(8,128)(2,1)S(1)}, u32[]{:S(2)}, u32[]{:S(2)}) collective-permute-start(bf16[64,1024]{1,0:T(8,128)(2,1)S(1)} %add_convert_fusion.1.refs_0_), channel_id=1, source_target_pairs={{0,4},{4,0},{8,12},{12,8},{1,5},{5,1},{9,13},{13,9},{2,6},{6,2},{1... | collective-permute-start | bytes 393224 | tf_op jit(solution)/shard_map/ppermute | solution.py:135
  122.7 7.1 %collective-permute-start.45 = (bf16[64,1024]{1,0:T(8,128)(2,1)S(1)}, bf16[64,1024]{1,0:T(8,128)(2,1)S(1)}, u32[]{:S(2)}, u32[]{:S(2)}) collective-permute-start(bf16[64,1024]{1,0:T(8,128)(2,1)S(1)} %shard_map.72), channel_id=1, source_target_pairs={{0,1},{1,0},{2,3},{3,2},{4,5},{5,4},{6,7},{7,6},{8,9},{9,8},{10,11... | collective-permute-start | bytes 393224 | tf_op jit(solution)/shard_map/ppermute | solution.py:135
  124.6 7.2 %collective-permute-start.46 = (bf16[64,1024]{1,0:T(8,128)(2,1)S(1)}, bf16[64,1024]{1,0:T(8,128)(2,1)S(1)}, u32[]{:S(2)}, u32[]{:S(2)}) collective-permute-start(bf16[64,1024]{1,0:T(8,128)(2,1)S(1)} %shard_map.73), channel_id=1, source_target_pairs={{0,4},{4,0},{8,12},{12,8},{1,5},{5,1},{9,13},{13,9},{2,6},{6,2},{1... | collective-permute-start | bytes 393224 | tf_op jit(solution)/shard_map/ppermute | solution.py:135
  129.8 5.0 %collective-permute-start.47 = (bf16[64,1024]{1,0:T(8,128)(2,1)S(1)}, bf16[64,1024]{1,0:T(8,128)(2,1)S(1)}, u32[]{:S(2)}, u32[]{:S(2)}) collective-permute-start(bf16[64,1024]{1,0:T(8,128)(2,1)S(1)} %get-tuple-element.427), channel_id=1, source_target_pairs={{0,2},{1,3},{2,0},{3,1},{4,6},{5,7},{6,4},{7,5},{8,10},{9,11},{10,... | collective-permute-start | bytes 393224 | tf_op jit(solution)/shard_map/ppermute | solution.py:135
  134.9 1.4 collective-permute-start.48
  137.1 5.6 %collective-permute-start.49 = (bf16[64,1024]{1,0:T(8,128)(2,1)S(1)}, bf16[64,1024]{1,0:T(8,128)(2,1)S(1)}, u32[]{:S(2)}, u32[]{:S(2)}) collective-permute-start(bf16[64,1024]{1,0:T(8,128)(2,1)S(1)} %shard_map.76), channel_id=1, source_target_pairs={{0,4},{4,0},{8,12},{12,8},{1,5},{5,1},{9,13},{13,9},{2,6},{6,2},{1... | collective-permute-start | bytes 393224 | tf_op jit(solution)/shard_map/ppermute | solution.py:135
  142.7 8.3 %collective-permute-start.50 = (bf16[64,1024]{1,0:T(8,128)(2,1)S(1)}, bf16[64,1024]{1,0:T(8,128)(2,1)S(1)}, u32[]{:S(2)}, u32[]{:S(2)}) collective-permute-start(bf16[64,1024]{1,0:T(8,128)(2,1)S(1)} %broadcast_select_fusion.4), channel_id=1, source_target_pairs={{0,8},{4,12},{8,0},{12,4},{1,9},{5,13},{9,1},{13,5},{2,10},{6,14},... | collective-permute-start | bytes 393224 | tf_op jit(solution)/shard_map/ppermute | solution.py:135
  144.1 6.9 %copy-start.4 = (bf16[5,1024,64]{1,2,0:T(8,128)(2,1)}, bf16[5,1024,64]{1,2,0:T(8,128)(2,1)S(1)}, u32[]{:S(2)}) copy-start(bf16[5,1024,64]{1,2,0:T(8,128)(2,1)S(1)} %bitcast_dynamic-update-slice_fusion) | copy-start | bytes 1966084

commit v8 on v7

--- a/solution.py
+++ b/solution.py
@@ -154,7 +154,7 @@
         order = Order()
         solved = [[None] * STREAMS for _ in range(steps_total)]
         state = [dict() for _ in range(STREAMS)]
-        sums = [None] * (steps_total + 1)
+        sums = [[None] * STREAMS for _ in range(steps_total)]
         factors = [None] * steps_total
         inverses = [None] * steps_total
 
@@ -166,21 +166,21 @@
             if step < steps_total:
                 inverses[step] = order.block(inverse_blocks, step)
 
-        def older(step, blocks):
+        def older(s, step, blocks):
             if step >= steps_total:
                 return
             for j in blocks:
                 block = order.block(factor_blocks, pair_index(step, j))
-                units = [u for s in range(STREAMS) for u in solved[j][s]]
-
-                rest = [] if sums[step] is None else [sums[step]]
-                sums[step] = order.run(
-                    lambda block, *v: product(block, v[: len(units)], v[len(units) :]), block, *units, *rest
+                rest = [] if sums[step][s] is None else [sums[step][s]]
+                sums[step][s] = order.run(
+                    lambda block, own, other, *rest: product(block, [own, other], rest),
+                    block,
+                    *solved[j][s],
+                    *rest,
                 )
 
         def older_part(s, step, u):
-            first = (2 * s + u) * width
-            return [] if sums[step] is None else [sums[step][first : first + width]]
+            return [] if sums[step][s] is None else [sums[step][s][u * width : (u + 1) * width]]
 
         def factor_other(s, step):
             st = state[s]
@@ -268,30 +268,33 @@
         first(0)
         if steps_total > 1:
             base = order.run(lambda v: turned_sides(side_ref, v), right_sides)
-            load_factor(1)
         pair_sum(0)
         cross(0)
         first(1)
+        load_factor(1)
         load_inverse(1)
 
         for step in range(1, steps_total):
             final = exact and step == last_step
             solve(0, step - 1)
             factor_other(0, step)
+            load_inverse(step + 1)
             pair_sum(1)
             cross(1)
+            older(1, step, range(step - 1))
             factor_own(0, step)
             chip_sum(0)
-            older(step + 1, range(step - 1))
+            older(0, step + 1, range(step))
             load_factor(step + 1)
-            load_inverse(step + 1)
+            if step == last_step:
+                residual(0, step)
             solve(1, step - 1)
             factor_other(1, step)
-            residual(0, step)
+            if step < last_step:
+                residual(0, step)
             inverse_own(0, step)
             factor_own(1, step)
             chip_sum(1)
-            older(step + 1, [step - 1])
             inverse_other(0, step)
             pair_sum(0)
             if not final:

time: 152 us -> 154 us (1.013)
  waiting for transfers between devices: 53 us -> 47.5 us
  starting transfers between devices: 41.5 us -> 46.5 us
  Pallas kernels: 32.2 us -> 36.5 us
  local copies, waits for them, and re-layouts: 21.5 us -> 19.4 us
    ppermute x51, waiting for transfers between devices: 53 us -> 47.5 us  [trade(): return lax.ppermute(value, axis, [(i, i ^ step) for i in range(size)])]
    ppermute x51, starting transfers between devices: 41.5 us -> 46.5 us  [trade(): return lax.ppermute(value, axis, [(i, i ^ step) for i in range(size)])]
    pallas_call x38 -> x44, Pallas kernels: 29.6 us -> 33.9 us  [product(): pl.pallas_call(functools.partial(product_kernel, len(units)), out_shape=j...]
    squeeze x16 -> x22, local copies, waits for them, and re-layouts: 16.9 us -> 15.1 us  [block(): self.last = lax.optimization_barrier(self.run(lambda v: v[index], blocks))]
  transfers between devices with their start and end apart: 51 -> 51, of which waited for: 25 -> 27; matrix products, arithmetic and copies ran while one was open for 11% -> 10% of each run, Pallas kernels for 20% -> 23%
where the time goes in v8:
time: 154 us; the launch traced here: 153 us
  waiting for transfers between devices  47.5 us (31%)
  starting transfers between devices  46.5 us (30%)
  Pallas kernels  36.5 us (24%)
  local copies, waits for them, and re-layouts  19.4 us (13%)
  other arithmetic  2.24 us (1%)
    ppermute x51, waiting for transfers between devices, trade(): return lax.ppermute(value, axis, [(i, i ^ step) for i in range(size)])  47.5 us
    ppermute x51, starting transfers between devices, trade(): return lax.ppermute(value, axis, [(i, i ^ step) for i in range(size)])  46.5 us
    pallas_call x44, Pallas kernels, product(): pl.pallas_call(functools.partial(product_kernel, len(units)), out_shape=j...  33.9 us
    squeeze x22, local copies, waits for them, and re-layouts, block(): self.last = lax.optimization_barrier(self.run(lambda v: v[index], blocks))  15.1 us
  transfers between devices with their start and end apart: 51, of which 27 were waited for; matrix products, arithmetic and copies ran while one was open for 10% of the time, Pallas kernels for 23%

profile of v8, /device:TPU:0, one launch (start us, length us, event | category | flops | bytes accessed | tf_op | source)
XLA Modules:
  0.0 153.2 jit_solution(31110842362229934)
XLA Ops:
  0.0 1.8 %slice_bitcast_fusion.20.block = bf16[1024,1024]{1,0:T(8,128)(2,1)S(1)} fusion(bf16[5,1024,1024]{2,1,0:T(8,128)(2,1)} %param.4), kind=kLoop, calls=%fused_computation.20 | loop fusion | bytes 4194304 | tf_op jit(solution)/shard_map/squeeze | solution.py:128
  1.8 1.1 slice_bitcast_fusion.21.right
  2.9 0.9 shard_map.37
  3.7 3.1 %collective-permute-start = (bf16[64,1024]{1,0:T(8,128)(2,1)S(1)}, bf16[64,1024]{1,0:T(8,128)(2,1)S(1)}, u32[]{:S(2)}, u32[]{:S(2)}) collective-permute-start(bf16[64,1024]{1,0:T(8,128)(2,1)S(1)} %get-tuple-element.235), channel_id=1, source_target_pairs={{0,4},{4,0},{8,12},{12,8},{1,5},{5,1},{9,13},{13,9},{2,6},{6,2},{1... | collective-permute-start | bytes 393224 | tf_op jit(solution)/shard_map/ppermute | solution.py:135
  6.8 1.7 %copy-done.1 = bf16[5,1024,256]{2,1,0:T(8,128)(2,1)S(1)} copy-done((bf16[5,1024,256]{2,1,0:T(8,128)(2,1)S(1)}, bf16[5,1024,256]{2,1,0:T(8,128)(2,1)}, u32[]{:S(2)}) %copy-start.1) | copy-done | bytes 2621464
  8.5 0.9 shard_map.38
  9.5 1.0 copy-done
  10.4 1.4 slice_bitcast_fusion.22
  11.9 2.7 %collective-permute-start.2 = (bf16[64,1024]{1,0:T(8,128)(2,1)S(1)}, bf16[64,1024]{1,0:T(8,128)(2,1)S(1)}, u32[]{:S(2)}, u32[]{:S(2)}) collective-permute-start(bf16[64,1024]{1,0:T(8,128)(2,1)S(1)} %get-tuple-element.487), channel_id=1, source_target_pairs={{0,8},{4,12},{8,0},{12,4},{1,9},{5,13},{9,1},{13,5},{2,10},{6,14},... | collective-permute-start | bytes 393224 | tf_op jit(solution)/shard_map/ppermute | solution.py:135
  14.5 0.8 shard_map.39
  15.4 2.1 %slice_bitcast_fusion.19.block = bf16[1024,1024]{1,0:T(8,128)(2,1)S(1)} fusion(bf16[10,1024,1024]{2,1,0:T(8,128)(2,1)} %param.3), kind=kLoop, calls=%fused_computation.19 | loop fusion | bytes 4194304 | tf_op jit(solution)/shard_map/squeeze | solution.py:128
  17.5 2.2 %slice_bitcast_fusion.18.block = bf16[1024,1024]{1,0:T(8,128)(2,1)S(1)} fusion(bf16[5,1024,1024]{2,1,0:T(8,128)(2,1)} %param.4), kind=kLoop, calls=%fused_computation.18 | loop fusion | bytes 4194304 | tf_op jit(solution)/shard_map/squeeze | solution.py:128
  20.5 1.5 collective-permute-start.4
  22.7 1.8 %slice_bitcast_fusion.17.block = bf16[1024,1024]{1,0:T(8,128)(2,1)S(1)} fusion(bf16[5,1024,1024]{2,1,0:T(8,128)(2,1)} %param.4), kind=kLoop, calls=%fused_computation.17 | loop fusion | bytes 4194304 | tf_op jit(solution)/shard_map/squeeze | solution.py:128
  24.5 1.4 collective-permute-done.1
  26.5 0.8 collective-permute-done.4.refs_0_
  28.2 1.6 %collective-permute-start.7 = (bf16[64,1024]{1,0:T(8,128)(2,1)S(1)}, bf16[64,1024]{1,0:T(8,128)(2,1)S(1)}, u32[]{:S(2)}, u32[]{:S(2)}) collective-permute-start(bf16[64,1024]{1,0:T(8,128)(2,1)S(1)} %get-tuple-element.483), channel_id=1, source_target_pairs={{0,2},{1,3},{2,0},{3,1},{4,6},{5,7},{6,4},{7,5},{8,10},{9,11},{10,... | collective-permute-start | bytes 393224 | tf_op jit(solution)/shard_map/ppermute | solution.py:135
  30.9 3.3 %collective-permute-done.3 = bf16[64,1024]{1,0:T(8,128)(2,1)S(1)} collective-permute-done((bf16[64,1024]{1,0:T(8,128)(2,1)S(1)}, bf16[64,1024]{1,0:T(8,128)(2,1)S(1)}, u32[]{:S(2)}, u32[]{:S(2)}) %collective-permute-start.3) | collective-permute-done | bytes 131104 | tf_op jit(solution)/shard_map/ppermute | solution.py:135
  36.6 2.1 %collective-permute-start.11 = (bf16[64,1024]{1,0:T(8,128)(2,1)S(1)}, bf16[64,1024]{1,0:T(8,128)(2,1)S(1)}, u32[]{:S(2)}, u32[]{:S(2)}) collective-permute-start(bf16[64,1024]{1,0:T(8,128)(2,1)S(1)} %shard_map.44), channel_id=1, source_target_pairs={{0,4},{4,0},{8,12},{12,8},{1,5},{5,1},{9,13},{13,9},{2,6},{6,2},{1... | collective-permute-start | bytes 393224 | tf_op jit(solution)/shard_map/ppermute | solution.py:135
  38.7 0.9 collective-permute-done.6.refs_0_
  40.4 1.5 collective-permute-start.9
  42.7 1.4 collective-permute-start.14
  44.1 1.3 collective-permute-done.9
  47.6 3.5 %collective-permute-done.14 = bf16[64,1024]{1,0:T(8,128)(2,1)S(1)} collective-permute-done((bf16[64,1024]{1,0:T(8,128)(2,1)S(1)}, bf16[64,1024]{1,0:T(8,128)(2,1)S(1)}, u32[]{:S(2)}, u32[]{:S(2)}) %collective-permute-start.14) | collective-permute-done | bytes 131104 | tf_op jit(solution)/shard_map/ppermute | solution.py:135
  52.1 1.8 %slice_bitcast_fusion.14.block = bf16[1024,1024]{1,0:T(8,128)(2,1)S(1)} fusion(bf16[5,1024,1024]{2,1,0:T(8,128)(2,1)} %param.4), kind=kLoop, calls=%fused_computation.14 | loop fusion | bytes 4194304 | tf_op jit(solution)/shard_map/squeeze | solution.py:128
  54.0 1.9 %collective-permute-start.15 = (bf16[64,1024]{1,0:T(8,128)(2,1)S(1)}, bf16[64,1024]{1,0:T(8,128)(2,1)S(1)}, u32[]{:S(2)}, u32[]{:S(2)}) collective-permute-start(bf16[64,1024]{1,0:T(8,128)(2,1)S(1)} %get-tuple-element.477), channel_id=1, source_target_pairs={{0,8},{4,12},{8,0},{12,4},{1,9},{5,13},{9,1},{13,5},{2,10},{6,14},... | collective-permute-start | bytes 393224 | tf_op jit(solution)/shard_map/ppermute | solution.py:135
  56.0 0.8 shard_map.50
  57.7 1.6 %collective-permute-start.19 = (bf16[64,1024]{1,0:T(8,128)(2,1)S(1)}, bf16[64,1024]{1,0:T(8,128)(2,1)S(1)}, u32[]{:S(2)}, u32[]{:S(2)}) collective-permute-start(bf16[64,1024]{1,0:T(8,128)(2,1)S(1)} %get-tuple-element.475), channel_id=1, source_target_pairs={{0,2},{1,3},{2,0},{3,1},{4,6},{5,7},{6,4},{7,5},{8,10},{9,11},{10,... | collective-permute-start | bytes 393224 | tf_op jit(solution)/shard_map/ppermute | solution.py:135
  60.4 0.8 shard_map.53
  61.4 2.1 %collective-permute-done.15 = bf16[64,1024]{1,0:T(8,128)(2,1)S(1)} collective-permute-done((bf16[64,1024]{1,0:T(8,128)(2,1)S(1)}, bf16[64,1024]{1,0:T(8,128)(2,1)S(1)}, u32[]{:S(2)}, u32[]{:S(2)}) %collective-permute-start.15) | collective-permute-done | bytes 131104 | tf_op jit(solution)/shard_map/ppermute | solution.py:135
  65.2 0.9 shard_map.55
  66.1 2.1 %collective-permute-start.23 = (bf16[64,1024]{1,0:T(8,128)(2,1)S(1)}, bf16[64,1024]{1,0:T(8,128)(2,1)S(1)}, u32[]{:S(2)}, u32[]{:S(2)}) collective-permute-start(bf16[64,1024]{1,0:T(8,128)(2,1)S(1)} %shard_map.55), channel_id=1, source_target_pairs={{0,4},{4,0},{8,12},{12,8},{1,5},{5,1},{9,13},{13,9},{2,6},{6,2},{1... | collective-permute-start | bytes 393224 | tf_op jit(solution)/shard_map/ppermute | solution.py:135
  69.5 1.6 %collective-permute-start.21 = (bf16[64,1024]{1,0:T(8,128)(2,1)S(1)}, bf16[64,1024]{1,0:T(8,128)(2,1)S(1)}, u32[]{:S(2)}, u32[]{:S(2)}) collective-permute-start(bf16[64,1024]{1,0:T(8,128)(2,1)S(1)} %get-tuple-element.473), channel_id=1, source_target_pairs={{0,2},{1,3},{2,0},{3,1},{4,6},{5,7},{6,4},{7,5},{8,10},{9,11},{10,... | collective-permute-start | bytes 393224 | tf_op jit(solution)/shard_map/ppermute | solution.py:135
  72.0 2.0 %collective-permute-start.26 = (bf16[64,1024]{1,0:T(8,128)(2,1)S(1)}, bf16[64,1024]{1,0:T(8,128)(2,1)S(1)}, u32[]{:S(2)}, u32[]{:S(2)}) collective-permute-start(bf16[64,1024]{1,0:T(8,128)(2,1)S(1)} %get-tuple-element.471), channel_id=1, source_target_pairs={{0,8},{4,12},{8,0},{12,4},{1,9},{5,13},{9,1},{13,5},{2,10},{6,14},... | collective-permute-start | bytes 393224 | tf_op jit(solution)/shard_map/ppermute | solution.py:135
  76.8 3.9 %collective-permute-done.26 = bf16[64,1024]{1,0:T(8,128)(2,1)S(1)} collective-permute-done((bf16[64,1024]{1,0:T(8,128)(2,1)S(1)}, bf16[64,1024]{1,0:T(8,128)(2,1)S(1)}, u32[]{:S(2)}, u32[]{:S(2)}) %collective-permute-start.26) | collective-permute-done | bytes 131104 | tf_op jit(solution)/shard_map/ppermute | solution.py:135
  81.6 1.8 %slice_bitcast_fusion.9.block = bf16[1024,1024]{1,0:T(8,128)(2,1)S(1)} fusion(bf16[5,1024,1024]{2,1,0:T(8,128)(2,1)} %param.4), kind=kLoop, calls=%fused_computation.9 | loop fusion | bytes 4194304 | tf_op jit(solution)/shard_map/squeeze | solution.py:128
  83.5 2.4 %collective-permute-start.27 = (bf16[64,1024]{1,0:T(8,128)(2,1)S(1)}, bf16[64,1024]{1,0:T(8,128)(2,1)S(1)}, u32[]{:S(2)}, u32[]{:S(2)}) collective-permute-start(bf16[64,1024]{1,0:T(8,128)(2,1)S(1)} %get-tuple-element.469), channel_id=1, source_target_pairs={{0,8},{4,12},{8,0},{12,4},{1,9},{5,13},{9,1},{13,5},{2,10},{6,14},... | collective-permute-start | bytes 393224 | tf_op jit(solution)/shard_map/ppermute | solution.py:135
  86.0 0.8 shard_map.61.refs_2_
  87.0 0.8 shard_map.62
  88.7 1.5 collective-permute-start.31
  91.3 0.8 shard_map.65.refs_2_
  92.3 0.8 shard_map.66
  95.7 2.0 %collective-permute-start.35 = (bf16[64,1024]{1,0:T(8,128)(2,1)S(1)}, bf16[64,1024]{1,0:T(8,128)(2,1)S(1)}, u32[]{:S(2)}, u32[]{:S(2)}) collective-permute-start(bf16[64,1024]{1,0:T(8,128)(2,1)S(1)} %shard_map.68), channel_id=1, source_target_pairs={{0,4},{4,0},{8,12},{12,8},{1,5},{5,1},{9,13},{13,9},{2,6},{6,2},{1... | collective-permute-start | bytes 393224 | tf_op jit(solution)/shard_map/ppermute | solution.py:135
  97.7 1.1 collective-permute-done.30.refs_0_
  99.7 1.0 collective-permute-start.33
  101.6 2.3 %collective-permute-start.38 = (bf16[64,1024]{1,0:T(8,128)(2,1)S(1)}, bf16[64,1024]{1,0:T(8,128)(2,1)S(1)}, u32[]{:S(2)}, u32[]{:S(2)}) collective-permute-start(bf16[64,1024]{1,0:T(8,128)(2,1)S(1)} %get-tuple-element.463), channel_id=1, source_target_pairs={{0,8},{4,12},{8,0},{12,4},{1,9},{5,13},{9,1},{13,5},{2,10},{6,14},... | collective-permute-start | bytes 393224 | tf_op jit(solution)/shard_map/ppermute | solution.py:135
  103.9 0.8 collective-permute-done.33
  106.9 3.5 %collective-permute-done.38 = bf16[64,1024]{1,0:T(8,128)(2,1)S(1)} collective-permute-done((bf16[64,1024]{1,0:T(8,128)(2,1)S(1)}, bf16[64,1024]{1,0:T(8,128)(2,1)S(1)}, u32[]{:S(2)}, u32[]{:S(2)}) %collective-permute-start.38) | collective-permute-done | bytes 131104 | tf_op jit(solution)/shard_map/ppermute | solution.py:135
  111.4 1.8 %collective-permute-done.37 = bf16[64,1024]{1,0:T(8,128)(2,1)S(1)} collective-permute-done((bf16[64,1024]{1,0:T(8,128)(2,1)S(1)}, bf16[64,1024]{1,0:T(8,128)(2,1)S(1)}, u32[]{:S(2)}, u32[]{:S(2)}) %collective-permute-start.37) | collective-permute-done | bytes 131104 | tf_op jit(solution)/shard_map/ppermute | solution.py:135
  113.2 1.2 collective-permute-start.39
  114.7 0.8 shard_map.74.refs_2_
  115.6 0.8 shard_map.75.refs_2_
  116.6 0.8 shard_map.76
  118.3 1.2 collective-permute-start.42
  119.5 4.4 %collective-permute-done.42 = bf16[64,1024]{1,0:T(8,128)(2,1)S(1)} collective-permute-done((bf16[64,1024]{1,0:T(8,128)(2,1)S(1)}, bf16[64,1024]{1,0:T(8,128)(2,1)S(1)}, u32[]{:S(2)}, u32[]{:S(2)}) %collective-permute-start.42) | collective-permute-done | bytes 131104 | tf_op jit(solution)/shard_map/ppermute | solution.py:135
  124.1 1.4 collective-permute-start.43
  128.1 2.0 %collective-permute-done.43.refs_0_ = bf16[64,1024]{1,0:T(8,128)(2,1)S(1)} collective-permute-done((bf16[64,1024]{1,0:T(8,128)(2,1)S(1)}, bf16[64,1024]{1,0:T(8,128)(2,1)S(1)}, u32[]{:S(2)}, u32[]{:S(2)}) %collective-permute-start.43) | collective-permute-done | bytes 131104 | tf_op jit(solution)/shard_map/ppermute | solution.py:135
  130.9 1.2 collective-permute-start.47
  133.1 2.9 %collective-permute-done.47 = bf16[64,1024]{1,0:T(8,128)(2,1)S(1)} collective-permute-done((bf16[64,1024]{1,0:T(8,128)(2,1)S(1)}, bf16[64,1024]{1,0:T(8,128)(2,1)S(1)}, u32[]{:S(2)}, u32[]{:S(2)}) %collective-permute-start.47) | collective-permute-done | bytes 131104 | tf_op jit(solution)/shard_map/ppermute | solution.py:135
  136.3 1.3 collective-permute-done.48
  138.3 1.6 %collective-permute-start.49 = (bf16[64,1024]{1,0:T(8,128)(2,1)S(1)}, bf16[64,1024]{1,0:T(8,128)(2,1)S(1)}, u32[]{:S(2)}, u32[]{:S(2)}) collective-permute-start(bf16[64,1024]{1,0:T(8,128)(2,1)S(1)} %shard_map.82), channel_id=1, source_target_pairs={{0,4},{4,0},{8,12},{12,8},{1,5},{5,1},{9,13},{13,9},{2,6},{6,2},{1... | collective-permute-start | bytes 393224 | tf_op jit(solution)/shard_map/ppermute | solution.py:135
  140.7 3.2 %collective-permute-done.49 = bf16[64,1024]{1,0:T(8,128)(2,1)S(1)} collective-permute-done((bf16[64,1024]{1,0:T(8,128)(2,1)S(1)}, bf16[64,1024]{1,0:T(8,128)(2,1)S(1)}, u32[]{:S(2)}, u32[]{:S(2)}) %collective-permute-start.49) | collective-permute-done | bytes 131104 | tf_op jit(solution)/shard_map/ppermute | solution.py:135
  144.0 1.8 %collective-permute-start.50 = (bf16[64,1024]{1,0:T(8,128)(2,1)S(1)}, bf16[64,1024]{1,0:T(8,128)(2,1)S(1)}, u32[]{:S(2)}, u32[]{:S(2)}) collective-permute-start(bf16[64,1024]{1,0:T(8,128)(2,1)S(1)} %broadcast_select_fusion.4), channel_id=1, source_target_pairs={{0,8},{4,12},{8,0},{12,4},{1,9},{5,13},{9,1},{13,5},{2,10},{6,14},... | collective-permute-start | bytes 393224 | tf_op jit(solution)/shard_map/ppermute | solution.py:135
  145.9 6.6 %collective-permute-done.50 = bf16[64,1024]{1,0:T(8,128)(2,1)S(1)} collective-permute-done((bf16[64,1024]{1,0:T(8,128)(2,1)S(1)}, bf16[64,1024]{1,0:T(8,128)(2,1)S(1)}, u32[]{:S(2)}, u32[]{:S(2)}) %collective-permute-start.50) | collective-permute-done | bytes 131104 | tf_op jit(solution)/shard_map/ppermute | solution.py:135
  (164 shorter events, 39.4 us)
Async XLA Ops:
  3.7 8.1 %collective-permute-start = (bf16[64,1024]{1,0:T(8,128)(2,1)S(1)}, bf16[64,1024]{1,0:T(8,128)(2,1)S(1)}, u32[]{:S(2)}, u32[]{:S(2)}) collective-permute-start(bf16[64,1024]{1,0:T(8,128)(2,1)S(1)} %get-tuple-element.235), channel_id=1, source_target_pairs={{0,4},{4,0},{8,12},{12,8},{1,5},{5,1},{9,13},{13,9},{2,6},{6,2},{1... | collective-permute-start | bytes 393224 | tf_op jit(solution)/shard_map/ppermute | solution.py:135
  6.8 1.7 %copy-start.1 = (bf16[5,1024,256]{2,1,0:T(8,128)(2,1)S(1)}, bf16[5,1024,256]{2,1,0:T(8,128)(2,1)}, u32[]{:S(2)}) copy-start(bf16[5,1024,256]{2,1,0:T(8,128)(2,1)} %sides) | copy-start | bytes 7864324
  9.4 1.0 copy-start
  11.9 8.6 %collective-permute-start.2 = (bf16[64,1024]{1,0:T(8,128)(2,1)S(1)}, bf16[64,1024]{1,0:T(8,128)(2,1)S(1)}, u32[]{:S(2)}, u32[]{:S(2)}) collective-permute-start(bf16[64,1024]{1,0:T(8,128)(2,1)S(1)} %get-tuple-element.487), channel_id=1, source_target_pairs={{0,8},{4,12},{8,0},{12,4},{1,9},{5,13},{9,1},{13,5},{2,10},{6,14},... | collective-permute-start | bytes 393224 | tf_op jit(solution)/shard_map/ppermute | solution.py:135
  14.5 15.3 %copy-start.2 = (bf16[10,1024,1024]{2,1,0:T(8,128)(2,1)S(1)}, bf16[10,1024,1024]{2,1,0:T(8,128)(2,1)}, u32[]{:S(2)}) copy-start(bf16[10,1024,1024]{2,1,0:T(8,128)(2,1)} %param.3) | copy-start | bytes 62914564
  19.7 6.2 %collective-permute-start.1 = (bf16[64,1024]{1,0:T(8,128)(2,1)S(1)}, bf16[64,1024]{1,0:T(8,128)(2,1)S(1)}, u32[]{:S(2)}, u32[]{:S(2)}) collective-permute-start(bf16[64,1024]{1,0:T(8,128)(2,1)S(1)} %get-tuple-element.242), channel_id=1, source_target_pairs={{0,4},{4,0},{8,12},{12,8},{1,5},{5,1},{9,13},{13,9},{2,6},{6,2},{1... | collective-permute-start | bytes 393224 | tf_op jit(solution)/shard_map/ppermute | solution.py:135
  20.5 6.9 %collective-permute-start.4 = (bf16[64,1024]{1,0:T(8,128)(2,1)S(1)}, bf16[64,1024]{1,0:T(8,128)(2,1)S(1)}, u32[]{:S(2)}, u32[]{:S(2)}) collective-permute-start(bf16[64,1024]{1,0:T(8,128)(2,1)S(1)} %add_convert_fusion.8.refs_0_.refs_1_), channel_id=1, source_target_pairs={{0,4},{4,0},{8,12},{12,8},{1,5},{5,1},{9,13},{13,9},{2,6},{6,2},{1... | collective-permute-start | bytes 393224 | tf_op jit(solution)/shard_map/ppermute | solution.py:135
  22.7 5.4 %collective-permute-start.5 = (bf16[64,1024]{1,0:T(8,128)(2,1)S(1)}, bf16[64,1024]{1,0:T(8,128)(2,1)S(1)}, u32[]{:S(2)}, u32[]{:S(2)}) collective-permute-start(bf16[64,1024]{1,0:T(8,128)(2,1)S(1)} %shard_map.40), channel_id=1, source_target_pairs={{0,1},{1,0},{2,3},{3,2},{4,5},{5,4},{6,7},{7,6},{8,9},{9,8},{10,11... | collective-permute-start | bytes 393224 | tf_op jit(solution)/shard_map/ppermute | solution.py:135
  26.0 8.3 %collective-permute-start.3 = (bf16[64,1024]{1,0:T(8,128)(2,1)S(1)}, bf16[64,1024]{1,0:T(8,128)(2,1)S(1)}, u32[]{:S(2)}, u32[]{:S(2)}) collective-permute-start(bf16[64,1024]{1,0:T(8,128)(2,1)S(1)} %get-tuple-element.485), channel_id=1, source_target_pairs={{0,8},{4,12},{8,0},{12,4},{1,9},{5,13},{9,1},{13,5},{2,10},{6,14},... | collective-permute-start | bytes 393224 | tf_op jit(solution)/shard_map/ppermute | solution.py:135
  28.2 7.1 %collective-permute-start.7 = (bf16[64,1024]{1,0:T(8,128)(2,1)S(1)}, bf16[64,1024]{1,0:T(8,128)(2,1)S(1)}, u32[]{:S(2)}, u32[]{:S(2)}) collective-permute-start(bf16[64,1024]{1,0:T(8,128)(2,1)S(1)} %get-tuple-element.483), channel_id=1, source_target_pairs={{0,2},{1,3},{2,0},{3,1},{4,6},{5,7},{6,4},{7,5},{8,10},{9,11},{10,... | collective-permute-start | bytes 393224 | tf_op jit(solution)/shard_map/ppermute | solution.py:135
  34.3 5.3 %collective-permute-start.6 = (bf16[64,1024]{1,0:T(8,128)(2,1)S(1)}, bf16[64,1024]{1,0:T(8,128)(2,1)S(1)}, u32[]{:S(2)}, u32[]{:S(2)}) collective-permute-start(bf16[64,1024]{1,0:T(8,128)(2,1)S(1)} %add_convert_fusion.7.refs_0_.refs_1_), channel_id=1, source_target_pairs={{0,4},{4,0},{8,12},{12,8},{1,5},{5,1},{9,13},{13,9},{2,6},{6,2},{1... | collective-permute-start | bytes 393224 | tf_op jit(solution)/shard_map/ppermute | solution.py:135
  35.1 5.2 %collective-permute-start.8 = (bf16[64,1024]{1,0:T(8,128)(2,1)S(1)}, bf16[64,1024]{1,0:T(8,128)(2,1)S(1)}, u32[]{:S(2)}, u32[]{:S(2)}) collective-permute-start(bf16[64,1024]{1,0:T(8,128)(2,1)S(1)} %shard_map.43), channel_id=1, source_target_pairs={{0,1},{1,0},{2,3},{3,2},{4,5},{5,4},{6,7},{7,6},{8,9},{9,8},{10,11... | collective-permute-start | bytes 393224 | tf_op jit(solution)/shard_map/ppermute | solution.py:135
  35.3 6.6 %collective-permute-start.10 = (bf16[64,1024]{1,0:T(8,128)(2,1)S(1)}, bf16[64,1024]{1,0:T(8,128)(2,1)S(1)}, u32[]{:S(2)}, u32[]{:S(2)}) collective-permute-start(bf16[64,1024]{1,0:T(8,128)(2,1)S(1)} %subtract_convert_fusion.7.refs_0_), channel_id=1, source_target_pairs={{0,1},{1,0},{2,3},{3,2},{4,5},{5,4},{6,7},{7,6},{8,9},{9,8},{10,11... | collective-permute-start | bytes 393224 | tf_op jit(solution)/shard_map/ppermute | solution.py:135
  36.6 6.1 %collective-permute-start.11 = (bf16[64,1024]{1,0:T(8,128)(2,1)S(1)}, bf16[64,1024]{1,0:T(8,128)(2,1)S(1)}, u32[]{:S(2)}, u32[]{:S(2)}) collective-permute-start(bf16[64,1024]{1,0:T(8,128)(2,1)S(1)} %shard_map.44), channel_id=1, source_target_pairs={{0,4},{4,0},{8,12},{12,8},{1,5},{5,1},{9,13},{13,9},{2,6},{6,2},{1... | collective-permute-start | bytes 393224 | tf_op jit(solution)/shard_map/ppermute | solution.py:135
  40.4 5.0 %collective-permute-start.9 = (bf16[64,1024]{1,0:T(8,128)(2,1)S(1)}, bf16[64,1024]{1,0:T(8,128)(2,1)S(1)}, u32[]{:S(2)}, u32[]{:S(2)}) collective-permute-start(bf16[64,1024]{1,0:T(8,128)(2,1)S(1)} %get-tuple-element.481), channel_id=1, source_target_pairs={{0,2},{1,3},{2,0},{3,1},{4,6},{5,7},{6,4},{7,5},{8,10},{9,11},{10,... | collective-permute-start | bytes 393224 | tf_op jit(solution)/shard_map/ppermute | solution.py:135
  42.7 8.4 %collective-permute-start.14 = (bf16[64,1024]{1,0:T(8,128)(2,1)S(1)}, bf16[64,1024]{1,0:T(8,128)(2,1)S(1)}, u32[]{:S(2)}, u32[]{:S(2)}) collective-permute-start(bf16[64,1024]{1,0:T(8,128)(2,1)S(1)} %get-tuple-element.479), channel_id=1, source_target_pairs={{0,8},{4,12},{8,0},{12,4},{1,9},{5,13},{9,1},{13,5},{2,10},{6,14},... | collective-permute-start | bytes 393224 | tf_op jit(solution)/shard_map/ppermute | solution.py:135
  45.4 1.4 collective-permute-start.12
  46.3 7.6 %collective-permute-start.13 = (bf16[64,1024]{1,0:T(8,128)(2,1)S(1)}, bf16[64,1024]{1,0:T(8,128)(2,1)S(1)}, u32[]{:S(2)}, u32[]{:S(2)}) collective-permute-start(bf16[64,1024]{1,0:T(8,128)(2,1)S(1)} %shard_map.47), channel_id=1, source_target_pairs={{0,4},{4,0},{8,12},{12,8},{1,5},{5,1},{9,13},{13,9},{2,6},{6,2},{1... | collective-permute-start | bytes 393224 | tf_op jit(solution)/shard_map/ppermute | solution.py:135
  51.2 5.7 %collective-permute-start.16 = (bf16[64,1024]{1,0:T(8,128)(2,1)S(1)}, bf16[64,1024]{1,0:T(8,128)(2,1)S(1)}, u32[]{:S(2)}, u32[]{:S(2)}) collective-permute-start(bf16[64,1024]{1,0:T(8,128)(2,1)S(1)} %add_convert_fusion.6.refs_0_.refs_1_), channel_id=1, source_target_pairs={{0,4},{4,0},{8,12},{12,8},{1,5},{5,1},{9,13},{13,9},{2,6},{6,2},{1... | collective-permute-start | bytes 393224 | tf_op jit(solution)/shard_map/ppermute | solution.py:135
  52.0 5.7 %collective-permute-start.17 = (bf16[64,1024]{1,0:T(8,128)(2,1)S(1)}, bf16[64,1024]{1,0:T(8,128)(2,1)S(1)}, u32[]{:S(2)}, u32[]{:S(2)}) collective-permute-start(bf16[64,1024]{1,0:T(8,128)(2,1)S(1)} %shard_map.49), channel_id=1, source_target_pairs={{0,1},{1,0},{2,3},{3,2},{4,5},{5,4},{6,7},{7,6},{8,9},{9,8},{10,11... | collective-permute-start | bytes 393224 | tf_op jit(solution)/shard_map/ppermute | solution.py:135
  54.0 9.6 %collective-permute-start.15 = (bf16[64,1024]{1,0:T(8,128)(2,1)S(1)}, bf16[64,1024]{1,0:T(8,128)(2,1)S(1)}, u32[]{:S(2)}, u32[]{:S(2)}) collective-permute-start(bf16[64,1024]{1,0:T(8,128)(2,1)S(1)} %get-tuple-element.477), channel_id=1, source_target_pairs={{0,8},{4,12},{8,0},{12,4},{1,9},{5,13},{9,1},{13,5},{2,10},{6,14},... | collective-permute-start | bytes 393224 | tf_op jit(solution)/shard_map/ppermute | solution.py:135
  57.7 6.8 %collective-permute-start.19 = (bf16[64,1024]{1,0:T(8,128)(2,1)S(1)}, bf16[64,1024]{1,0:T(8,128)(2,1)S(1)}, u32[]{:S(2)}, u32[]{:S(2)}) collective-permute-start(bf16[64,1024]{1,0:T(8,128)(2,1)S(1)} %get-tuple-element.475), channel_id=1, source_target_pairs={{0,2},{1,3},{2,0},{3,1},{4,6},{5,7},{6,4},{7,5},{8,10},{9,11},{10,... | collective-permute-start | bytes 393224 | tf_op jit(solution)/shard_map/ppermute | solution.py:135
  63.6 5.1 %collective-permute-start.18 = (bf16[64,1024]{1,0:T(8,128)(2,1)S(1)}, bf16[64,1024]{1,0:T(8,128)(2,1)S(1)}, u32[]{:S(2)}, u32[]{:S(2)}) collective-permute-start(bf16[64,1024]{1,0:T(8,128)(2,1)S(1)} %add_convert_fusion.5.refs_0_.refs_1_), channel_id=1, source_target_pairs={{0,4},{4,0},{8,12},{12,8},{1,5},{5,1},{9,13},{13,9},{2,6},{6,2},{1... | collective-permute-start | bytes 393224 | tf_op jit(solution)/shard_map/ppermute | solution.py:135
  64.5 5.0 %collective-permute-start.20 = (bf16[64,1024]{1,0:T(8,128)(2,1)S(1)}, bf16[64,1024]{1,0:T(8,128)(2,1)S(1)}, u32[]{:S(2)}, u32[]{:S(2)}) collective-permute-start(bf16[64,1024]{1,0:T(8,128)(2,1)S(1)} %shard_map.54), channel_id=1, source_target_pairs={{0,1},{1,0},{2,3},{3,2},{4,5},{5,4},{6,7},{7,6},{8,9},{9,8},{10,11... | collective-permute-start | bytes 393224 | tf_op jit(solution)/shard_map/ppermute | solution.py:135
  64.6 6.6 %collective-permute-start.22 = (bf16[64,1024]{1,0:T(8,128)(2,1)S(1)}, bf16[64,1024]{1,0:T(8,128)(2,1)S(1)}, u32[]{:S(2)}, u32[]{:S(2)}) collective-permute-start(bf16[64,1024]{1,0:T(8,128)(2,1)S(1)} %subtract_convert_fusion.5.refs_0_), channel_id=1, source_target_pairs={{0,1},{1,0},{2,3},{3,2},{4,5},{5,4},{6,7},{7,6},{8,9},{9,8},{10,11... | collective-permute-start | bytes 393224 | tf_op jit(solution)/shard_map/ppermute | solution.py:135
  66.1 5.8 %collective-permute-start.23 = (bf16[64,1024]{1,0:T(8,128)(2,1)S(1)}, bf16[64,1024]{1,0:T(8,128)(2,1)S(1)}, u32[]{:S(2)}, u32[]{:S(2)}) collective-permute-start(bf16[64,1024]{1,0:T(8,128)(2,1)S(1)} %shard_map.55), channel_id=1, source_target_pairs={{0,4},{4,0},{8,12},{12,8},{1,5},{5,1},{9,13},{13,9},{2,6},{6,2},{1... | collective-permute-start | bytes 393224 | tf_op jit(solution)/shard_map/ppermute | solution.py:135
  69.5 5.0 %collective-permute-start.21 = (bf16[64,1024]{1,0:T(8,128)(2,1)S(1)}, bf16[64,1024]{1,0:T(8,128)(2,1)S(1)}, u32[]{:S(2)}, u32[]{:S(2)}) collective-permute-start(bf16[64,1024]{1,0:T(8,128)(2,1)S(1)} %get-tuple-element.473), channel_id=1, source_target_pairs={{0,2},{1,3},{2,0},{3,1},{4,6},{5,7},{6,4},{7,5},{8,10},{9,11},{10,... | collective-permute-start | bytes 393224 | tf_op jit(solution)/shard_map/ppermute | solution.py:135
  72.0 8.7 %collective-permute-start.26 = (bf16[64,1024]{1,0:T(8,128)(2,1)S(1)}, bf16[64,1024]{1,0:T(8,128)(2,1)S(1)}, u32[]{:S(2)}, u32[]{:S(2)}) collective-permute-start(bf16[64,1024]{1,0:T(8,128)(2,1)S(1)} %get-tuple-element.471), channel_id=1, source_target_pairs={{0,8},{4,12},{8,0},{12,4},{1,9},{5,13},{9,1},{13,5},{2,10},{6,14},... | collective-permute-start | bytes 393224 | tf_op jit(solution)/shard_map/ppermute | solution.py:135
  74.6 1.4 collective-permute-start.24
  75.5 7.9 %collective-permute-start.25 = (bf16[64,1024]{1,0:T(8,128)(2,1)S(1)}, bf16[64,1024]{1,0:T(8,128)(2,1)S(1)}, u32[]{:S(2)}, u32[]{:S(2)}) collective-permute-start(bf16[64,1024]{1,0:T(8,128)(2,1)S(1)} %shard_map.58), channel_id=1, source_target_pairs={{0,4},{4,0},{8,12},{12,8},{1,5},{5,1},{9,13},{13,9},{2,6},{6,2},{1... | collective-permute-start | bytes 393224 | tf_op jit(solution)/shard_map/ppermute | solution.py:135
  80.7 7.1 %collective-permute-start.28 = (bf16[64,1024]{1,0:T(8,128)(2,1)S(1)}, bf16[64,1024]{1,0:T(8,128)(2,1)S(1)}, u32[]{:S(2)}, u32[]{:S(2)}) collective-permute-start(bf16[64,1024]{1,0:T(8,128)(2,1)S(1)} %add_convert_fusion.4.refs_0_.refs_1_), channel_id=1, source_target_pairs={{0,4},{4,0},{8,12},{12,8},{1,5},{5,1},{9,13},{13,9},{2,6},{6,2},{1... | collective-permute-start | bytes 393224 | tf_op jit(solution)/shard_map/ppermute | solution.py:135
  81.6 7.1 %collective-permute-start.29 = (bf16[64,1024]{1,0:T(8,128)(2,1)S(1)}, bf16[64,1024]{1,0:T(8,128)(2,1)S(1)}, u32[]{:S(2)}, u32[]{:S(2)}) collective-permute-start(bf16[64,1024]{1,0:T(8,128)(2,1)S(1)} %shard_map.60), channel_id=1, source_target_pairs={{0,1},{1,0},{2,3},{3,2},{4,5},{5,4},{6,7},{7,6},{8,9},{9,8},{10,11... | collective-permute-start | bytes 393224 | tf_op jit(solution)/shard_map/ppermute | solution.py:135
  83.5 9.9 %collective-permute-start.27 = (bf16[64,1024]{1,0:T(8,128)(2,1)S(1)}, bf16[64,1024]{1,0:T(8,128)(2,1)S(1)}, u32[]{:S(2)}, u32[]{:S(2)}) collective-permute-start(bf16[64,1024]{1,0:T(8,128)(2,1)S(1)} %get-tuple-element.469), channel_id=1, source_target_pairs={{0,8},{4,12},{8,0},{12,4},{1,9},{5,13},{9,1},{13,5},{2,10},{6,14},... | collective-permute-start | bytes 393224 | tf_op jit(solution)/shard_map/ppermute | solution.py:135
  88.7 5.7 %collective-permute-start.31 = (bf16[64,1024]{1,0:T(8,128)(2,1)S(1)}, bf16[64,1024]{1,0:T(8,128)(2,1)S(1)}, u32[]{:S(2)}, u32[]{:S(2)}) collective-permute-start(bf16[64,1024]{1,0:T(8,128)(2,1)S(1)} %get-tuple-element.467), channel_id=1, source_target_pairs={{0,2},{1,3},{2,0},{3,1},{4,6},{5,7},{6,4},{7,5},{8,10},{9,11},{10,... | collective-permute-start | bytes 393224 | tf_op jit(solution)/shard_map/ppermute | solution.py:135
  93.4 5.5 %collective-permute-start.30 = (bf16[64,1024]{1,0:T(8,128)(2,1)S(1)}, bf16[64,1024]{1,0:T(8,128)(2,1)S(1)}, u32[]{:S(2)}, u32[]{:S(2)}) collective-permute-start(bf16[64,1024]{1,0:T(8,128)(2,1)S(1)} %add_convert_fusion.3.refs_0_.refs_1_), channel_id=1, source_target_pairs={{0,4},{4,0},{8,12},{12,8},{1,5},{5,1},{9,13},{13,9},{2,6},{6,2},{1... | collective-permute-start | bytes 393224 | tf_op jit(solution)/shard_map/ppermute | solution.py:135
  94.3 5.4 %collective-permute-start.32 = (bf16[64,1024]{1,0:T(8,128)(2,1)S(1)}, bf16[64,1024]{1,0:T(8,128)(2,1)S(1)}, u32[]{:S(2)}, u32[]{:S(2)}) collective-permute-start(bf16[64,1024]{1,0:T(8,128)(2,1)S(1)} %shard_map.67), channel_id=1, source_target_pairs={{0,1},{1,0},{2,3},{3,2},{4,5},{5,4},{6,7},{7,6},{8,9},{9,8},{10,11... | collective-permute-start | bytes 393224 | tf_op jit(solution)/shard_map/ppermute | solution.py:135
  94.4 6.3 %collective-permute-start.34 = (bf16[64,1024]{1,0:T(8,128)(2,1)S(1)}, bf16[64,1024]{1,0:T(8,128)(2,1)S(1)}, u32[]{:S(2)}, u32[]{:S(2)}) collective-permute-start(bf16[64,1024]{1,0:T(8,128)(2,1)S(1)} %subtract_convert_fusion.3.refs_0_), channel_id=1, source_target_pairs={{0,1},{1,0},{2,3},{3,2},{4,5},{5,4},{6,7},{7,6},{8,9},{9,8},{10,11... | collective-permute-start | bytes 393224 | tf_op jit(solution)/shard_map/ppermute | solution.py:135
  95.7 5.9 %collective-permute-start.35 = (bf16[64,1024]{1,0:T(8,128)(2,1)S(1)}, bf16[64,1024]{1,0:T(8,128)(2,1)S(1)}, u32[]{:S(2)}, u32[]{:S(2)}) collective-permute-start(bf16[64,1024]{1,0:T(8,128)(2,1)S(1)} %shard_map.68), channel_id=1, source_target_pairs={{0,4},{4,0},{8,12},{12,8},{1,5},{5,1},{9,13},{13,9},{2,6},{6,2},{1... | collective-permute-start | bytes 393224 | tf_op jit(solution)/shard_map/ppermute | solution.py:135
  99.7 5.0 %collective-permute-start.33 = (bf16[64,1024]{1,0:T(8,128)(2,1)S(1)}, bf16[64,1024]{1,0:T(8,128)(2,1)S(1)}, u32[]{:S(2)}, u32[]{:S(2)}) collective-permute-start(bf16[64,1024]{1,0:T(8,128)(2,1)S(1)} %get-tuple-element.465), channel_id=1, source_target_pairs={{0,2},{1,3},{2,0},{3,1},{4,6},{5,7},{6,4},{7,5},{8,10},{9,11},{10,... | collective-permute-start | bytes 393224 | tf_op jit(solution)/shard_map/ppermute | solution.py:135
  101.6 8.9 %collective-permute-start.38 = (bf16[64,1024]{1,0:T(8,128)(2,1)S(1)}, bf16[64,1024]{1,0:T(8,128)(2,1)S(1)}, u32[]{:S(2)}, u32[]{:S(2)}) collective-permute-start(bf16[64,1024]{1,0:T(8,128)(2,1)S(1)} %get-tuple-element.463), channel_id=1, source_target_pairs={{0,8},{4,12},{8,0},{12,4},{1,9},{5,13},{9,1},{13,5},{2,10},{6,14},... | collective-permute-start | bytes 393224 | tf_op jit(solution)/shard_map/ppermute | solution.py:135
  104.8 1.4 collective-permute-start.36
  105.6 7.6 %collective-permute-start.37 = (bf16[64,1024]{1,0:T(8,128)(2,1)S(1)}, bf16[64,1024]{1,0:T(8,128)(2,1)S(1)}, u32[]{:S(2)}, u32[]{:S(2)}) collective-permute-start(bf16[64,1024]{1,0:T(8,128)(2,1)S(1)} %shard_map.71), channel_id=1, source_target_pairs={{0,4},{4,0},{8,12},{12,8},{1,5},{5,1},{9,13},{13,9},{2,6},{6,2},{1... | collective-permute-start | bytes 393224 | tf_op jit(solution)/shard_map/ppermute | solution.py:135
  110.5 7.0 %collective-permute-start.40 = (bf16[64,1024]{1,0:T(8,128)(2,1)S(1)}, bf16[64,1024]{1,0:T(8,128)(2,1)S(1)}, u32[]{:S(2)}, u32[]{:S(2)}) collective-permute-start(bf16[64,1024]{1,0:T(8,128)(2,1)S(1)} %add_convert_fusion.2.refs_0_), channel_id=1, source_target_pairs={{0,4},{4,0},{8,12},{12,8},{1,5},{5,1},{9,13},{13,9},{2,6},{6,2},{1... | collective-permute-start | bytes 393224 | tf_op jit(solution)/shard_map/ppermute | solution.py:135
  111.3 6.9 %collective-permute-start.41 = (bf16[64,1024]{1,0:T(8,128)(2,1)S(1)}, bf16[64,1024]{1,0:T(8,128)(2,1)S(1)}, u32[]{:S(2)}, u32[]{:S(2)}) collective-permute-start(bf16[64,1024]{1,0:T(8,128)(2,1)S(1)} %shard_map.73), channel_id=1, source_target_pairs={{0,1},{1,0},{2,3},{3,2},{4,5},{5,4},{6,7},{7,6},{8,9},{9,8},{10,11... | collective-permute-start | bytes 393224 | tf_op jit(solution)/shard_map/ppermute | solution.py:135
  113.2 10.8 %collective-permute-start.39 = (bf16[64,1024]{1,0:T(8,128)(2,1)S(1)}, bf16[64,1024]{1,0:T(8,128)(2,1)S(1)}, u32[]{:S(2)}, u32[]{:S(2)}) collective-permute-start(bf16[64,1024]{1,0:T(8,128)(2,1)S(1)} %get-tuple-element.461), channel_id=1, source_target_pairs={{0,8},{4,12},{8,0},{12,4},{1,9},{5,13},{9,1},{13,5},{2,10},{6,14},... | collective-permute-start | bytes 393224 | tf_op jit(solution)/shard_map/ppermute | solution.py:135
  118.3 5.7 %collective-permute-start.42 = (bf16[64,1024]{1,0:T(8,128)(2,1)S(1)}, bf16[64,1024]{1,0:T(8,128)(2,1)S(1)}, u32[]{:S(2)}, u32[]{:S(2)}) collective-permute-start(bf16[64,1024]{1,0:T(8,128)(2,1)S(1)} %get-tuple-element.459), channel_id=1, source_target_pairs={{0,2},{1,3},{2,0},{3,1},{4,6},{5,7},{6,4},{7,5},{8,10},{9,11},{10,... | collective-permute-start | bytes 393224 | tf_op jit(solution)/shard_map/ppermute | solution.py:135
  124.0 2.5 %collective-permute-start.44 = (bf16[64,1024]{1,0:T(8,128)(2,1)S(1)}, bf16[64,1024]{1,0:T(8,128)(2,1)S(1)}, u32[]{:S(2)}, u32[]{:S(2)}) collective-permute-start(bf16[64,1024]{1,0:T(8,128)(2,1)S(1)} %subtract_convert_fusion.1), channel_id=1, source_target_pairs={{0,1},{1,0},{2,3},{3,2},{4,5},{5,4},{6,7},{7,6},{8,9},{9,8},{10,11... | collective-permute-start | bytes 393224 | tf_op jit(solution)/shard_map/ppermute | solution.py:135
  124.1 6.0 %collective-permute-start.43 = (bf16[64,1024]{1,0:T(8,128)(2,1)S(1)}, bf16[64,1024]{1,0:T(8,128)(2,1)S(1)}, u32[]{:S(2)}, u32[]{:S(2)}) collective-permute-start(bf16[64,1024]{1,0:T(8,128)(2,1)S(1)} %add_convert_fusion.1.refs_0_), channel_id=1, source_target_pairs={{0,4},{4,0},{8,12},{12,8},{1,5},{5,1},{9,13},{13,9},{2,6},{6,2},{1... | collective-permute-start | bytes 393224 | tf_op jit(solution)/shard_map/ppermute | solution.py:135
  126.3 4.6 %collective-permute-start.45 = (bf16[64,1024]{1,0:T(8,128)(2,1)S(1)}, bf16[64,1024]{1,0:T(8,128)(2,1)S(1)}, u32[]{:S(2)}, u32[]{:S(2)}) collective-permute-start(bf16[64,1024]{1,0:T(8,128)(2,1)S(1)} %shard_map.78), channel_id=1, source_target_pairs={{0,1},{1,0},{2,3},{3,2},{4,5},{5,4},{6,7},{7,6},{8,9},{9,8},{10,11... | collective-permute-start | bytes 393224 | tf_op jit(solution)/shard_map/ppermute | solution.py:135
  127.3 5.8 %collective-permute-start.46 = (bf16[64,1024]{1,0:T(8,128)(2,1)S(1)}, bf16[64,1024]{1,0:T(8,128)(2,1)S(1)}, u32[]{:S(2)}, u32[]{:S(2)}) collective-permute-start(bf16[64,1024]{1,0:T(8,128)(2,1)S(1)} %shard_map.79), channel_id=1, source_target_pairs={{0,4},{4,0},{8,12},{12,8},{1,5},{5,1},{9,13},{13,9},{2,6},{6,2},{1... | collective-permute-start | bytes 393224 | tf_op jit(solution)/shard_map/ppermute | solution.py:135
  130.9 5.2 %collective-permute-start.47 = (bf16[64,1024]{1,0:T(8,128)(2,1)S(1)}, bf16[64,1024]{1,0:T(8,128)(2,1)S(1)}, u32[]{:S(2)}, u32[]{:S(2)}) collective-permute-start(bf16[64,1024]{1,0:T(8,128)(2,1)S(1)} %get-tuple-element.457), channel_id=1, source_target_pairs={{0,2},{1,3},{2,0},{3,1},{4,6},{5,7},{6,4},{7,5},{8,10},{9,11},{10,... | collective-permute-start | bytes 393224 | tf_op jit(solution)/shard_map/ppermute | solution.py:135
  136.1 1.4 collective-permute-start.48
  138.3 5.6 %collective-permute-start.49 = (bf16[64,1024]{1,0:T(8,128)(2,1)S(1)}, bf16[64,1024]{1,0:T(8,128)(2,1)S(1)}, u32[]{:S(2)}, u32[]{:S(2)}) collective-permute-start(bf16[64,1024]{1,0:T(8,128)(2,1)S(1)} %shard_map.82), channel_id=1, source_target_pairs={{0,4},{4,0},{8,12},{12,8},{1,5},{5,1},{9,13},{13,9},{2,6},{6,2},{1... | collective-permute-start | bytes 393224 | tf_op jit(solution)/shard_map/ppermute | solution.py:135
  144.0 8.5 %collective-permute-start.50 = (bf16[64,1024]{1,0:T(8,128)(2,1)S(1)}, bf16[64,1024]{1,0:T(8,128)(2,1)S(1)}, u32[]{:S(2)}, u32[]{:S(2)}) collective-permute-start(bf16[64,1024]{1,0:T(8,128)(2,1)S(1)} %broadcast_select_fusion.4), channel_id=1, source_target_pairs={{0,8},{4,12},{8,0},{12,4},{1,9},{5,13},{9,1},{13,5},{2,10},{6,14},... | collective-permute-start | bytes 393224 | tf_op jit(solution)/shard_map/ppermute | solution.py:135
  145.9 6.6 %copy-start.3 = (bf16[5,1024,64]{1,2,0:T(8,128)(2,1)}, bf16[5,1024,64]{1,2,0:T(8,128)(2,1)S(1)}, u32[]{:S(2)}) copy-start(bf16[5,1024,64]{1,2,0:T(8,128)(2,1)S(1)} %bitcast_dynamic-update-slice_fusion) | copy-start | bytes 1966084

commit v9 on v8

--- a/solution.py
+++ b/solution.py
@@ -83,22 +83,24 @@
     )(side, right, block)
 
 
-def turn_kernel(width, side, sides, out, turned):
+def turn_kernel(side, sides, *refs):
+    outs, turned = refs[:STREAMS], refs[STREAMS]
+    width = outs[0].shape[0]
     turned[...] = sides[0].T
     for s in range(STREAMS):
         own = pl.multiple_of((2 * s + side[0]) * width, width)
-        out[0, s] = turned[pl.ds(own, width)]
-
-
-def turned_sides(side, sides):
-    steps, rows, angles = sides.shape
+        outs[s][...] = turned[pl.ds(own, width)]
+
+
+def turned_sides(step, side, sides):
+    rows, angles = sides.shape[1:]
     width = angles // UNITS
     return pl.pallas_call(
-        functools.partial(turn_kernel, width),
-        grid=(steps - 1,),
-        out_shape=jax.ShapeDtypeStruct((steps - 1, STREAMS, width, rows), jnp.bfloat16),
-        in_specs=[SMEM, pl.BlockSpec((1, rows, angles), lambda i: (i + 1, 0, 0))],
-        out_specs=pl.BlockSpec((1, STREAMS, width, rows), lambda i: (i, 0, 0, 0)),
+        turn_kernel,
+        grid=(1,),
+        out_shape=[jax.ShapeDtypeStruct((width, rows), jnp.bfloat16)] * STREAMS,
+        in_specs=[SMEM, pl.BlockSpec((1, rows, angles), lambda i: (step, 0, 0))],
+        out_specs=[pl.BlockSpec((width, rows), lambda i: (0, 0))] * STREAMS,
         scratch_shapes=[pltpu.VMEM((angles, rows), jnp.bfloat16)],
         compiler_params=params(),
         cost_estimate=COST,
@@ -217,7 +219,7 @@
 
             st = state[s]
             arrived = [] if st["flight"] is None else [st["flight"]]
-            st["own"] = order.run(work, base[step - 1, s], st["sum"], *arrived)
+            st["own"] = order.run(work, base[s], st["sum"], *arrived)
             st["swap"] = trade(st["own"], "col", 1)
 
         def inverse_own(s, step):
@@ -266,24 +268,22 @@
             state[s]["flight"] = trade(leaving, "row", 1)
 
         first(0)
-        if steps_total > 1:
-            base = order.run(lambda v: turned_sides(side_ref, v), right_sides)
+        first(1)
         pair_sum(0)
         cross(0)
-        first(1)
         load_factor(1)
-        load_inverse(1)
 
         for step in range(1, steps_total):
             final = exact and step == last_step
             solve(0, step - 1)
             factor_other(0, step)
-            load_inverse(step + 1)
+            load_inverse(step)
             pair_sum(1)
             cross(1)
-            older(1, step, range(step - 1))
             factor_own(0, step)
             chip_sum(0)
+            base = order.run(lambda v: turned_sides(step, side_ref, v), right_sides)
+            older(1, step, range(step - 1))
             older(0, step + 1, range(step))
             load_factor(step + 1)
             if step == last_step:

time: 154 us -> 153 us (level)
  local copies, waits for them, and re-layouts: 19.4 us -> 13.8 us
  waiting for transfers between devices: 47.5 us -> 51.7 us
  other arithmetic: 2.24 us -> 5.88 us
  starting transfers between devices: 46.5 us -> 43 us
    ppermute x51, waiting for transfers between devices: 47.5 us -> 51.7 us  [trade(): return lax.ppermute(value, axis, [(i, i ^ step) for i in range(size)])]
    ppermute x51, starting transfers between devices: 46.5 us -> 43 us  [trade(): return lax.ppermute(value, axis, [(i, i ^ step) for i in range(size)])]
    squeeze x22, local copies, waits for them, and re-layouts: 15.1 us -> 11.9 us  [block(): self.last = lax.optimization_barrier(self.run(lambda v: v[index], blocks))]
    unnamed x4 -> x5, other arithmetic: 0.29 us -> 2.92 us
  transfers between devices with their start and end apart: 51 -> 51, of which waited for: 27 -> 30; matrix products, arithmetic and copies ran while one was open for 10% -> 9% of each run, Pallas kernels for 23% -> 23%
where the time goes in v9:
time: 153 us
  waiting for transfers between devices  51.7 us (34%)
  starting transfers between devices  43 us (28%)
  Pallas kernels  37.3 us (24%)
  local copies, waits for them, and re-layouts  13.8 us (9%)
  other arithmetic  5.88 us (4%)
    ppermute x51, waiting for transfers between devices, trade(): return lax.ppermute(value, axis, [(i, i ^ step) for i in range(size)])  51.7 us
    ppermute x51, starting transfers between devices, trade(): return lax.ppermute(value, axis, [(i, i ^ step) for i in range(size)])  43 us
    pallas_call x44, Pallas kernels, product(): pl.pallas_call(functools.partial(product_kernel, len(units)), out_shape=j...  34.1 us
    squeeze x22, local copies, waits for them, and re-layouts, block(): self.last = lax.optimization_barrier(self.run(lambda v: v[index], blocks))  11.9 us
  transfers between devices with their start and end apart: 51, of which 30 were waited for; matrix products, arithmetic and copies ran while one was open for 9% of the time, Pallas kernels for 23%

profile of v9, /device:TPU:0, one launch (start us, length us, event | category | flops | bytes accessed | tf_op | source)
XLA Modules:
  0.0 152.8 jit_solution(7113323948706237774)
XLA Ops:
  0.0 3.2 %slice_bitcast_fusion.20.block = bf16[1024,1024]{1,0:T(8,128)(2,1)} fusion(bf16[5,1024,1024]{2,1,0:T(8,128)(2,1)} %param.4), kind=kLoop, calls=%fused_computation.20 | loop fusion | bytes 4194304 | tf_op jit(solution)/shard_map/squeeze | solution.py:130
  3.3 1.6 %copy-done.1 = bf16[1024,1024]{1,0:T(8,128)(2,1)S(1)} copy-done((bf16[1024,1024]{1,0:T(8,128)(2,1)S(1)}, bf16[1024,1024]{1,0:T(8,128)(2,1)}, u32[]{:S(2)}) %copy-start.1) | copy-done | bytes 2097176
  4.9 1.5 shard_map.37
  6.3 3.0 %collective-permute-start.1 = (bf16[64,1024]{1,0:T(8,128)(2,1)}, bf16[64,1024]{1,0:T(8,128)(2,1)}, u32[]{:S(2)}, u32[]{:S(2)}) collective-permute-start(bf16[64,1024]{1,0:T(8,128)(2,1)} %get-tuple-element.250), channel_id=1, source_target_pairs={{0,4},{4,0},{8,12},{12,8},{1,5},{5,1},{9,13},{13,9},{2,6},{6,2},{1... | collective-permute-start | bytes 393224 | tf_op jit(solution)/shard_map/ppermute | solution.py:137
  9.4 0.9 shard_map.38
  10.4 3.4 %collective-permute-done.1 = bf16[64,1024]{1,0:T(8,128)(2,1)} collective-permute-done((bf16[64,1024]{1,0:T(8,128)(2,1)}, bf16[64,1024]{1,0:T(8,128)(2,1)}, u32[]{:S(2)}, u32[]{:S(2)}) %collective-permute-start.1) | collective-permute-done | bytes 131104 | tf_op jit(solution)/shard_map/ppermute | solution.py:137
  13.8 1.0 fusion.19
  14.8 3.0 %collective-permute-start.2 = (bf16[64,1024]{1,0:T(8,128)(2,1)S(1)}, bf16[64,1024]{1,0:T(8,128)(2,1)S(1)}, u32[]{:S(2)}, u32[]{:S(2)}) collective-permute-start(bf16[64,1024]{1,0:T(8,128)(2,1)S(1)} %get-tuple-element.509), channel_id=1, source_target_pairs={{0,8},{4,12},{8,0},{12,4},{1,9},{5,13},{9,1},{13,5},{2,10},{6,14},... | collective-permute-start | bytes 393224 | tf_op jit(solution)/shard_map/ppermute | solution.py:137
  17.8 1.9 %slice_bitcast_fusion.19.block = bf16[1024,1024]{1,0:T(8,128)(2,1)S(1)} fusion(bf16[10,1024,1024]{2,1,0:T(8,128)(2,1)} %param.3), kind=kLoop, calls=%fused_computation.19 | loop fusion | bytes 4194304 | tf_op jit(solution)/shard_map/squeeze | solution.py:130
  19.8 2.9 %collective-permute-done.2 = bf16[64,1024]{1,0:T(8,128)(2,1)S(1)} collective-permute-done((bf16[64,1024]{1,0:T(8,128)(2,1)S(1)}, bf16[64,1024]{1,0:T(8,128)(2,1)S(1)}, u32[]{:S(2)}, u32[]{:S(2)}) %collective-permute-start.2) | collective-permute-done | bytes 131104 | tf_op jit(solution)/shard_map/ppermute | solution.py:137
  24.1 2.1 %slice_bitcast_fusion.18.block = bf16[1024,1024]{1,0:T(8,128)(2,1)S(1)} fusion(bf16[5,1024,1024]{2,1,0:T(8,128)(2,1)} %param.4), kind=kLoop, calls=%fused_computation.18 | loop fusion | bytes 4194304 | tf_op jit(solution)/shard_map/squeeze | solution.py:130
  26.2 3.2 %collective-permute-start.3 = (bf16[64,1024]{1,0:T(8,128)(2,1)S(1)}, bf16[64,1024]{1,0:T(8,128)(2,1)S(1)}, u32[]{:S(2)}, u32[]{:S(2)}) collective-permute-start(bf16[64,1024]{1,0:T(8,128)(2,1)S(1)} %get-tuple-element.507), channel_id=1, source_target_pairs={{0,8},{4,12},{8,0},{12,4},{1,9},{5,13},{9,1},{13,5},{2,10},{6,14},... | collective-permute-start | bytes 393224 | tf_op jit(solution)/shard_map/ppermute | solution.py:137
  30.2 1.6 %collective-permute-start.7 = (bf16[64,1024]{1,0:T(8,128)(2,1)S(1)}, bf16[64,1024]{1,0:T(8,128)(2,1)S(1)}, u32[]{:S(2)}, u32[]{:S(2)}) collective-permute-start(bf16[64,1024]{1,0:T(8,128)(2,1)S(1)} %get-tuple-element.505), channel_id=1, source_target_pairs={{0,2},{1,3},{2,0},{3,1},{4,6},{5,7},{6,4},{7,5},{8,10},{9,11},{10,... | collective-permute-start | bytes 393224 | tf_op jit(solution)/shard_map/ppermute | solution.py:137
  32.0 1.8 %slice_bitcast_fusion.17.block = bf16[1024,1024]{1,0:T(8,128)(2,1)S(1)} fusion(bf16[10,1024,1024]{2,1,0:T(8,128)(2,1)} %param.3), kind=kLoop, calls=%fused_computation.17 | loop fusion | bytes 4194304 | tf_op jit(solution)/shard_map/squeeze | solution.py:130
  33.8 0.8 shard_map.42
  34.7 1.6 %collective-permute-done.3 = bf16[64,1024]{1,0:T(8,128)(2,1)S(1)} collective-permute-done((bf16[64,1024]{1,0:T(8,128)(2,1)S(1)}, bf16[64,1024]{1,0:T(8,128)(2,1)S(1)}, u32[]{:S(2)}, u32[]{:S(2)}) %collective-permute-start.3) | collective-permute-done | bytes 131104 | tf_op jit(solution)/shard_map/ppermute | solution.py:137
  38.7 2.1 %collective-permute-start.11 = (bf16[64,1024]{1,0:T(8,128)(2,1)S(1)}, bf16[64,1024]{1,0:T(8,128)(2,1)S(1)}, u32[]{:S(2)}, u32[]{:S(2)}) collective-permute-start(bf16[64,1024]{1,0:T(8,128)(2,1)S(1)} %shard_map.44), channel_id=1, source_target_pairs={{0,4},{4,0},{8,12},{12,8},{1,5},{5,1},{9,13},{13,9},{2,6},{6,2},{1... | collective-permute-start | bytes 393224 | tf_op jit(solution)/shard_map/ppermute | solution.py:137
  40.8 1.0 collective-permute-done.6.refs_0_
  42.6 1.3 collective-permute-start.9
  44.8 2.1 %collective-permute-start.14 = (bf16[64,1024]{1,0:T(8,128)(2,1)S(1)}, bf16[64,1024]{1,0:T(8,128)(2,1)S(1)}, u32[]{:S(2)}, u32[]{:S(2)}) collective-permute-start(bf16[64,1024]{1,0:T(8,128)(2,1)S(1)} %get-tuple-element.501), channel_id=1, source_target_pairs={{0,8},{4,12},{8,0},{12,4},{1,9},{5,13},{9,1},{13,5},{2,10},{6,14},... | collective-permute-start | bytes 393224 | tf_op jit(solution)/shard_map/ppermute | solution.py:137
  50.4 3.1 %collective-permute-done.14 = bf16[64,1024]{1,0:T(8,128)(2,1)S(1)} collective-permute-done((bf16[64,1024]{1,0:T(8,128)(2,1)S(1)}, bf16[64,1024]{1,0:T(8,128)(2,1)S(1)}, u32[]{:S(2)}, u32[]{:S(2)}) %collective-permute-start.14) | collective-permute-done | bytes 131104 | tf_op jit(solution)/shard_map/ppermute | solution.py:137
  54.7 1.6 %collective-permute-done.13 = bf16[64,1024]{1,0:T(8,128)(2,1)S(1)} collective-permute-done((bf16[64,1024]{1,0:T(8,128)(2,1)S(1)}, bf16[64,1024]{1,0:T(8,128)(2,1)S(1)}, u32[]{:S(2)}, u32[]{:S(2)}) %collective-permute-start.13) | collective-permute-done | bytes 131104 | tf_op jit(solution)/shard_map/ppermute | solution.py:137
  56.3 0.9 collective-permute-start.15
  57.2 1.8 %collective-permute-done.16.refs_0_ = bf16[64,1024]{1,0:T(8,128)(2,1)S(1)} collective-permute-done((bf16[64,1024]{1,0:T(8,128)(2,1)S(1)}, bf16[64,1024]{1,0:T(8,128)(2,1)S(1)}, u32[]{:S(2)}, u32[]{:S(2)}) %collective-permute-start.16) | collective-permute-done | bytes 131104 | tf_op jit(solution)/shard_map/ppermute | solution.py:137
  59.8 1.3 collective-permute-start.19
  61.6 0.8 shard_map.52
  62.6 0.8 shard_map.53.refs_2_
  63.5 0.8 shard_map.54
  64.5 1.0 collective-permute-done.15
  65.7 1.0 shard_map.55
  68.0 2.1 %collective-permute-start.23 = (bf16[64,1024]{1,0:T(8,128)(2,1)S(1)}, bf16[64,1024]{1,0:T(8,128)(2,1)S(1)}, u32[]{:S(2)}, u32[]{:S(2)}) collective-permute-start(bf16[64,1024]{1,0:T(8,128)(2,1)S(1)} %shard_map.56), channel_id=1, source_target_pairs={{0,4},{4,0},{8,12},{12,8},{1,5},{5,1},{9,13},{13,9},{2,6},{6,2},{1... | collective-permute-start | bytes 393224 | tf_op jit(solution)/shard_map/ppermute | solution.py:137
  71.5 1.3 collective-permute-start.21
  73.9 2.2 %collective-permute-start.26 = (bf16[64,1024]{1,0:T(8,128)(2,1)S(1)}, bf16[64,1024]{1,0:T(8,128)(2,1)S(1)}, u32[]{:S(2)}, u32[]{:S(2)}) collective-permute-start(bf16[64,1024]{1,0:T(8,128)(2,1)S(1)} %get-tuple-element.493), channel_id=1, source_target_pairs={{0,8},{4,12},{8,0},{12,4},{1,9},{5,13},{9,1},{13,5},{2,10},{6,14},... | collective-permute-start | bytes 393224 | tf_op jit(solution)/shard_map/ppermute | solution.py:137
  78.8 3.9 %collective-permute-done.26 = bf16[64,1024]{1,0:T(8,128)(2,1)S(1)} collective-permute-done((bf16[64,1024]{1,0:T(8,128)(2,1)S(1)}, bf16[64,1024]{1,0:T(8,128)(2,1)S(1)}, u32[]{:S(2)}, u32[]{:S(2)}) %collective-permute-start.26) | collective-permute-done | bytes 131104 | tf_op jit(solution)/shard_map/ppermute | solution.py:137
  82.7 0.8 shard_map.61
  83.8 1.5 collective-permute-done.25
  85.3 1.0 collective-permute-start.27
  86.3 1.5 collective-permute-done.28.refs_0_
  88.6 1.3 collective-permute-start.31
  90.3 0.8 shard_map.64.refs_2_
  91.3 0.8 shard_map.65
  92.3 0.8 shard_map.66.refs_2_
  93.3 0.8 shard_map.67.refs_2_
  94.3 0.8 shard_map.68
  97.8 1.9 %collective-permute-start.35 = (bf16[64,1024]{1,0:T(8,128)(2,1)S(1)}, bf16[64,1024]{1,0:T(8,128)(2,1)S(1)}, u32[]{:S(2)}, u32[]{:S(2)}) collective-permute-start(bf16[64,1024]{1,0:T(8,128)(2,1)S(1)} %shard_map.70), channel_id=1, source_target_pairs={{0,4},{4,0},{8,12},{12,8},{1,5},{5,1},{9,13},{13,9},{2,6},{6,2},{1... | collective-permute-start | bytes 393224 | tf_op jit(solution)/shard_map/ppermute | solution.py:137
  101.2 0.8 collective-permute-start.33
  103.5 2.4 %collective-permute-start.38 = (bf16[64,1024]{1,0:T(8,128)(2,1)S(1)}, bf16[64,1024]{1,0:T(8,128)(2,1)S(1)}, u32[]{:S(2)}, u32[]{:S(2)}) collective-permute-start(bf16[64,1024]{1,0:T(8,128)(2,1)S(1)} %get-tuple-element.485), channel_id=1, source_target_pairs={{0,8},{4,12},{8,0},{12,4},{1,9},{5,13},{9,1},{13,5},{2,10},{6,14},... | collective-permute-start | bytes 393224 | tf_op jit(solution)/shard_map/ppermute | solution.py:137
  107.7 1.0 shard_map.74
  108.7 3.4 %collective-permute-done.38 = bf16[64,1024]{1,0:T(8,128)(2,1)S(1)} collective-permute-done((bf16[64,1024]{1,0:T(8,128)(2,1)S(1)}, bf16[64,1024]{1,0:T(8,128)(2,1)S(1)}, u32[]{:S(2)}, u32[]{:S(2)}) %collective-permute-start.38) | collective-permute-done | bytes 131104 | tf_op jit(solution)/shard_map/ppermute | solution.py:137
  113.2 1.6 %collective-permute-done.37 = bf16[64,1024]{1,0:T(8,128)(2,1)S(1)} collective-permute-done((bf16[64,1024]{1,0:T(8,128)(2,1)S(1)}, bf16[64,1024]{1,0:T(8,128)(2,1)S(1)}, u32[]{:S(2)}, u32[]{:S(2)}) %collective-permute-start.37) | collective-permute-done | bytes 131104 | tf_op jit(solution)/shard_map/ppermute | solution.py:137
  114.8 1.3 collective-permute-start.39
  116.1 1.2 collective-permute-done.40.refs_0_
  118.1 1.0 collective-permute-start.42
  119.5 0.8 shard_map.78.refs_2_
  120.5 0.8 shard_map.79.refs_2_
  121.5 0.8 shard_map.80
  122.3 0.8 collective-permute-done.42
  125.6 1.8 %collective-permute-start.46 = (bf16[64,1024]{1,0:T(8,128)(2,1)S(1)}, bf16[64,1024]{1,0:T(8,128)(2,1)S(1)}, u32[]{:S(2)}, u32[]{:S(2)}) collective-permute-start(bf16[64,1024]{1,0:T(8,128)(2,1)S(1)} %shard_map.82), channel_id=1, source_target_pairs={{0,4},{4,0},{8,12},{12,8},{1,5},{5,1},{9,13},{13,9},{2,6},{6,2},{1... | collective-permute-start | bytes 393224 | tf_op jit(solution)/shard_map/ppermute | solution.py:137
  127.3 2.5 %collective-permute-done.43.refs_0_ = bf16[64,1024]{1,0:T(8,128)(2,1)S(1)} collective-permute-done((bf16[64,1024]{1,0:T(8,128)(2,1)S(1)}, bf16[64,1024]{1,0:T(8,128)(2,1)S(1)}, u32[]{:S(2)}, u32[]{:S(2)}) %collective-permute-start.43) | collective-permute-done | bytes 131104 | tf_op jit(solution)/shard_map/ppermute | solution.py:137
  130.6 1.0 collective-permute-start.47
  132.5 3.2 %collective-permute-done.47 = bf16[64,1024]{1,0:T(8,128)(2,1)S(1)} collective-permute-done((bf16[64,1024]{1,0:T(8,128)(2,1)S(1)}, bf16[64,1024]{1,0:T(8,128)(2,1)S(1)}, u32[]{:S(2)}, u32[]{:S(2)}) %collective-permute-start.47) | collective-permute-done | bytes 131104 | tf_op jit(solution)/shard_map/ppermute | solution.py:137
  139.5 4.1 %collective-permute-done.49 = bf16[64,1024]{1,0:T(8,128)(2,1)S(1)} collective-permute-done((bf16[64,1024]{1,0:T(8,128)(2,1)S(1)}, bf16[64,1024]{1,0:T(8,128)(2,1)S(1)}, u32[]{:S(2)}, u32[]{:S(2)}) %collective-permute-start.49) | collective-permute-done | bytes 131104 | tf_op jit(solution)/shard_map/ppermute | solution.py:137
  143.6 1.1 collective-permute-start.50
  145.4 6.7 %collective-permute-done.50 = bf16[64,1024]{1,0:T(8,128)(2,1)S(1)} collective-permute-done((bf16[64,1024]{1,0:T(8,128)(2,1)S(1)}, bf16[64,1024]{1,0:T(8,128)(2,1)S(1)}, u32[]{:S(2)}, u32[]{:S(2)}) %collective-permute-start.50) | collective-permute-done | bytes 131104 | tf_op jit(solution)/shard_map/ppermute | solution.py:137
  (173 shorter events, 41.0 us)
Async XLA Ops:
  0.0 3.2 %copy-start = (bf16[5,1024,256]{2,1,0:T(8,128)(2,1)S(1)}, bf16[5,1024,256]{2,1,0:T(8,128)(2,1)}, u32[]{:S(2)}) copy-start(bf16[5,1024,256]{2,1,0:T(8,128)(2,1)} %sides.3) | copy-start | bytes 7864324
  3.3 1.6 %copy-start.1 = (bf16[1024,1024]{1,0:T(8,128)(2,1)S(1)}, bf16[1024,1024]{1,0:T(8,128)(2,1)}, u32[]{:S(2)}) copy-start(bf16[1024,1024]{1,0:T(8,128)(2,1)} %slice_bitcast_fusion.20.block) | copy-start | bytes 6291460
  6.3 3.9 %copy-start.2 = (f32[64,1024]{1,0:T(8,128)}, f32[64,1024]{1,0:T(8,128)S(1)}, u32[]{:S(2)}) copy-start(f32[64,1024]{1,0:T(8,128)S(1)} %get-tuple-element.251) | copy-start | bytes 786436
  6.3 7.4 %collective-permute-start.1 = (bf16[64,1024]{1,0:T(8,128)(2,1)}, bf16[64,1024]{1,0:T(8,128)(2,1)}, u32[]{:S(2)}, u32[]{:S(2)}) collective-permute-start(bf16[64,1024]{1,0:T(8,128)(2,1)} %get-tuple-element.250), channel_id=1, source_target_pairs={{0,4},{4,0},{8,12},{12,8},{1,5},{5,1},{9,13},{13,9},{2,6},{6,2},{1... | collective-permute-start | bytes 393224 | tf_op jit(solution)/shard_map/ppermute | solution.py:137
  10.2 16.0 %collective-permute-start = (bf16[64,1024]{1,0:T(8,128)(2,1)S(1)}, bf16[64,1024]{1,0:T(8,128)(2,1)S(1)}, u32[]{:S(2)}, u32[]{:S(2)}) collective-permute-start(bf16[64,1024]{1,0:T(8,128)(2,1)S(1)} %get-tuple-element.249), channel_id=1, source_target_pairs={{0,4},{4,0},{8,12},{12,8},{1,5},{5,1},{9,13},{13,9},{2,6},{6,2},{1... | collective-permute-start | bytes 393224 | tf_op jit(solution)/shard_map/ppermute | solution.py:137
  14.8 7.9 %collective-permute-start.2 = (bf16[64,1024]{1,0:T(8,128)(2,1)S(1)}, bf16[64,1024]{1,0:T(8,128)(2,1)S(1)}, u32[]{:S(2)}, u32[]{:S(2)}) collective-permute-start(bf16[64,1024]{1,0:T(8,128)(2,1)S(1)} %get-tuple-element.509), channel_id=1, source_target_pairs={{0,8},{4,12},{8,0},{12,4},{1,9},{5,13},{9,1},{13,5},{2,10},{6,14},... | collective-permute-start | bytes 393224 | tf_op jit(solution)/shard_map/ppermute | solution.py:137
  17.8 16.7 %copy-start.3 = (bf16[10,1024,1024]{2,1,0:T(8,128)(2,1)S(1)}, bf16[10,1024,1024]{2,1,0:T(8,128)(2,1)}, u32[]{:S(2)}) copy-start(bf16[10,1024,1024]{2,1,0:T(8,128)(2,1)} %param.3) | copy-start | bytes 62914564
  22.7 6.7 %collective-permute-start.4 = (bf16[64,1024]{1,0:T(8,128)(2,1)S(1)}, bf16[64,1024]{1,0:T(8,128)(2,1)S(1)}, u32[]{:S(2)}, u32[]{:S(2)}) collective-permute-start(bf16[64,1024]{1,0:T(8,128)(2,1)S(1)} %add_convert_fusion.8.refs_0_.refs_1_), channel_id=1, source_target_pairs={{0,4},{4,0},{8,12},{12,8},{1,5},{5,1},{9,13},{13,9},{2,6},{6,2},{1... | collective-permute-start | bytes 393224 | tf_op jit(solution)/shard_map/ppermute | solution.py:137
  24.0 6.1 %collective-permute-start.5 = (bf16[64,1024]{1,0:T(8,128)(2,1)S(1)}, bf16[64,1024]{1,0:T(8,128)(2,1)S(1)}, u32[]{:S(2)}, u32[]{:S(2)}) collective-permute-start(bf16[64,1024]{1,0:T(8,128)(2,1)S(1)} %shard_map.39), channel_id=1, source_target_pairs={{0,1},{1,0},{2,3},{3,2},{4,5},{5,4},{6,7},{7,6},{8,9},{9,8},{10,11... | collective-permute-start | bytes 393224 | tf_op jit(solution)/shard_map/ppermute | solution.py:137
  26.2 10.1 %collective-permute-start.3 = (bf16[64,1024]{1,0:T(8,128)(2,1)S(1)}, bf16[64,1024]{1,0:T(8,128)(2,1)S(1)}, u32[]{:S(2)}, u32[]{:S(2)}) collective-permute-start(bf16[64,1024]{1,0:T(8,128)(2,1)S(1)} %get-tuple-element.507), channel_id=1, source_target_pairs={{0,8},{4,12},{8,0},{12,4},{1,9},{5,13},{9,1},{13,5},{2,10},{6,14},... | collective-permute-start | bytes 393224 | tf_op jit(solution)/shard_map/ppermute | solution.py:137
  30.2 7.1 %collective-permute-start.7 = (bf16[64,1024]{1,0:T(8,128)(2,1)S(1)}, bf16[64,1024]{1,0:T(8,128)(2,1)S(1)}, u32[]{:S(2)}, u32[]{:S(2)}) collective-permute-start(bf16[64,1024]{1,0:T(8,128)(2,1)S(1)} %get-tuple-element.505), channel_id=1, source_target_pairs={{0,2},{1,3},{2,0},{3,1},{4,6},{5,7},{6,4},{7,5},{8,10},{9,11},{10,... | collective-permute-start | bytes 393224 | tf_op jit(solution)/shard_map/ppermute | solution.py:137
  36.4 5.4 %collective-permute-start.6 = (bf16[64,1024]{1,0:T(8,128)(2,1)S(1)}, bf16[64,1024]{1,0:T(8,128)(2,1)S(1)}, u32[]{:S(2)}, u32[]{:S(2)}) collective-permute-start(bf16[64,1024]{1,0:T(8,128)(2,1)S(1)} %add_convert_fusion.7.refs_0_.refs_1_), channel_id=1, source_target_pairs={{0,4},{4,0},{8,12},{12,8},{1,5},{5,1},{9,13},{13,9},{2,6},{6,2},{1... | collective-permute-start | bytes 393224 | tf_op jit(solution)/shard_map/ppermute | solution.py:137
  36.5 18.0 %slice-start = ((s8[10485760]{0:T(1024)(128)(4,1)}), s8[4194304]{0:T(1024)(128)(4,1)S(1)}, s32[]{:S(2)}) async-start(s8[10485760]{0:T(1024)(128)(4,1)} %bitcast.67), calls=%async_computation | async-start | bytes 8388608
  37.2 5.4 %collective-permute-start.8 = (bf16[64,1024]{1,0:T(8,128)(2,1)S(1)}, bf16[64,1024]{1,0:T(8,128)(2,1)S(1)}, u32[]{:S(2)}, u32[]{:S(2)}) collective-permute-start(bf16[64,1024]{1,0:T(8,128)(2,1)S(1)} %shard_map.43), channel_id=1, source_target_pairs={{0,1},{1,0},{2,3},{3,2},{4,5},{5,4},{6,7},{7,6},{8,9},{9,8},{10,11... | collective-permute-start | bytes 393224 | tf_op jit(solution)/shard_map/ppermute | solution.py:137
  37.4 6.6 %collective-permute-start.10 = (bf16[64,1024]{1,0:T(8,128)(2,1)S(1)}, bf16[64,1024]{1,0:T(8,128)(2,1)S(1)}, u32[]{:S(2)}, u32[]{:S(2)}) collective-permute-start(bf16[64,1024]{1,0:T(8,128)(2,1)S(1)} %subtract_convert_fusion.7.refs_0_), channel_id=1, source_target_pairs={{0,1},{1,0},{2,3},{3,2},{4,5},{5,4},{6,7},{7,6},{8,9},{9,8},{10,11... | collective-permute-start | bytes 393224 | tf_op jit(solution)/shard_map/ppermute | solution.py:137
  38.7 15.8 %slice-start.1 = ((s8[10485760]{0:T(1024)(128)(4,1)}), s8[4194304]{0:T(1024)(128)(4,1)S(1)}, s32[]{:S(2)}) async-start(s8[10485760]{0:T(1024)(128)(4,1)} %bitcast.67), calls=%async_computation.1 | async-start | bytes 8388608
  38.7 6.0 %collective-permute-start.11 = (bf16[64,1024]{1,0:T(8,128)(2,1)S(1)}, bf16[64,1024]{1,0:T(8,128)(2,1)S(1)}, u32[]{:S(2)}, u32[]{:S(2)}) collective-permute-start(bf16[64,1024]{1,0:T(8,128)(2,1)S(1)} %shard_map.44), channel_id=1, source_target_pairs={{0,4},{4,0},{8,12},{12,8},{1,5},{5,1},{9,13},{13,9},{2,6},{6,2},{1... | collective-permute-start | bytes 393224 | tf_op jit(solution)/shard_map/ppermute | solution.py:137
  42.6 5.0 %collective-permute-start.9 = (bf16[64,1024]{1,0:T(8,128)(2,1)S(1)}, bf16[64,1024]{1,0:T(8,128)(2,1)S(1)}, u32[]{:S(2)}, u32[]{:S(2)}) collective-permute-start(bf16[64,1024]{1,0:T(8,128)(2,1)S(1)} %get-tuple-element.503), channel_id=1, source_target_pairs={{0,2},{1,3},{2,0},{3,1},{4,6},{5,7},{6,4},{7,5},{8,10},{9,11},{10,... | collective-permute-start | bytes 393224 | tf_op jit(solution)/shard_map/ppermute | solution.py:137
  44.8 8.7 %collective-permute-start.14 = (bf16[64,1024]{1,0:T(8,128)(2,1)S(1)}, bf16[64,1024]{1,0:T(8,128)(2,1)S(1)}, u32[]{:S(2)}, u32[]{:S(2)}) collective-permute-start(bf16[64,1024]{1,0:T(8,128)(2,1)S(1)} %get-tuple-element.501), channel_id=1, source_target_pairs={{0,8},{4,12},{8,0},{12,4},{1,9},{5,13},{9,1},{13,5},{2,10},{6,14},... | collective-permute-start | bytes 393224 | tf_op jit(solution)/shard_map/ppermute | solution.py:137
  47.7 1.9 %collective-permute-start.12 = (bf16[64,1024]{1,0:T(8,128)(2,1)S(1)}, bf16[64,1024]{1,0:T(8,128)(2,1)S(1)}, u32[]{:S(2)}, u32[]{:S(2)}) collective-permute-start(bf16[64,1024]{1,0:T(8,128)(2,1)S(1)} %subtract_convert_fusion.6.refs_0_), channel_id=1, source_target_pairs={{0,1},{1,0},{2,3},{3,2},{4,5},{5,4},{6,7},{7,6},{8,9},{9,8},{10,11... | collective-permute-start | bytes 393224 | tf_op jit(solution)/shard_map/ppermute | solution.py:137
  48.5 6.0 %slice-start.2 = ((s8[10485760]{0:T(1024)(128)(4,1)}), s8[2097152]{0:T(1024)(128)(4,1)S(1)}, s32[]{:S(2)}) async-start(s8[10485760]{0:T(1024)(128)(4,1)} %bitcast.67), calls=%async_computation.2 | async-start | bytes 4194304
  49.3 7.0 %collective-permute-start.13 = (bf16[64,1024]{1,0:T(8,128)(2,1)S(1)}, bf16[64,1024]{1,0:T(8,128)(2,1)S(1)}, u32[]{:S(2)}, u32[]{:S(2)}) collective-permute-start(bf16[64,1024]{1,0:T(8,128)(2,1)S(1)} %shard_map.47), channel_id=1, source_target_pairs={{0,4},{4,0},{8,12},{12,8},{1,5},{5,1},{9,13},{13,9},{2,6},{6,2},{1... | collective-permute-start | bytes 393224 | tf_op jit(solution)/shard_map/ppermute | solution.py:137
  53.5 5.5 %collective-permute-start.16 = (bf16[64,1024]{1,0:T(8,128)(2,1)S(1)}, bf16[64,1024]{1,0:T(8,128)(2,1)S(1)}, u32[]{:S(2)}, u32[]{:S(2)}) collective-permute-start(bf16[64,1024]{1,0:T(8,128)(2,1)S(1)} %add_convert_fusion.6.refs_0_.refs_1_), channel_id=1, source_target_pairs={{0,4},{4,0},{8,12},{12,8},{1,5},{5,1},{9,13},{13,9},{2,6},{6,2},{1... | collective-permute-start | bytes 393224 | tf_op jit(solution)/shard_map/ppermute | solution.py:137
  54.4 5.4 %collective-permute-start.17 = (bf16[64,1024]{1,0:T(8,128)(2,1)S(1)}, bf16[64,1024]{1,0:T(8,128)(2,1)S(1)}, u32[]{:S(2)}, u32[]{:S(2)}) collective-permute-start(bf16[64,1024]{1,0:T(8,128)(2,1)S(1)} %shard_map.49), channel_id=1, source_target_pairs={{0,1},{1,0},{2,3},{3,2},{4,5},{5,4},{6,7},{7,6},{8,9},{9,8},{10,11... | collective-permute-start | bytes 393224 | tf_op jit(solution)/shard_map/ppermute | solution.py:137
  56.3 9.2 %collective-permute-start.15 = (bf16[64,1024]{1,0:T(8,128)(2,1)S(1)}, bf16[64,1024]{1,0:T(8,128)(2,1)S(1)}, u32[]{:S(2)}, u32[]{:S(2)}) collective-permute-start(bf16[64,1024]{1,0:T(8,128)(2,1)S(1)} %get-tuple-element.499), channel_id=1, source_target_pairs={{0,8},{4,12},{8,0},{12,4},{1,9},{5,13},{9,1},{13,5},{2,10},{6,14},... | collective-permute-start | bytes 393224 | tf_op jit(solution)/shard_map/ppermute | solution.py:137
  59.8 6.9 %collective-permute-start.19 = (bf16[64,1024]{1,0:T(8,128)(2,1)S(1)}, bf16[64,1024]{1,0:T(8,128)(2,1)S(1)}, u32[]{:S(2)}, u32[]{:S(2)}) collective-permute-start(bf16[64,1024]{1,0:T(8,128)(2,1)S(1)} %get-tuple-element.497), channel_id=1, source_target_pairs={{0,2},{1,3},{2,0},{3,1},{4,6},{5,7},{6,4},{7,5},{8,10},{9,11},{10,... | collective-permute-start | bytes 393224 | tf_op jit(solution)/shard_map/ppermute | solution.py:137
  65.5 5.2 %collective-permute-start.18 = (bf16[64,1024]{1,0:T(8,128)(2,1)S(1)}, bf16[64,1024]{1,0:T(8,128)(2,1)S(1)}, u32[]{:S(2)}, u32[]{:S(2)}) collective-permute-start(bf16[64,1024]{1,0:T(8,128)(2,1)S(1)} %add_convert_fusion.5.refs_0_.refs_1_), channel_id=1, source_target_pairs={{0,4},{4,0},{8,12},{12,8},{1,5},{5,1},{9,13},{13,9},{2,6},{6,2},{1... | collective-permute-start | bytes 393224 | tf_op jit(solution)/shard_map/ppermute | solution.py:137
  66.6 4.8 %collective-permute-start.20 = (bf16[64,1024]{1,0:T(8,128)(2,1)S(1)}, bf16[64,1024]{1,0:T(8,128)(2,1)S(1)}, u32[]{:S(2)}, u32[]{:S(2)}) collective-permute-start(bf16[64,1024]{1,0:T(8,128)(2,1)S(1)} %shard_map.55), channel_id=1, source_target_pairs={{0,1},{1,0},{2,3},{3,2},{4,5},{5,4},{6,7},{7,6},{8,9},{9,8},{10,11... | collective-permute-start | bytes 393224 | tf_op jit(solution)/shard_map/ppermute | solution.py:137
  66.8 6.1 %collective-permute-start.22 = (bf16[64,1024]{1,0:T(8,128)(2,1)S(1)}, bf16[64,1024]{1,0:T(8,128)(2,1)S(1)}, u32[]{:S(2)}, u32[]{:S(2)}) collective-permute-start(bf16[64,1024]{1,0:T(8,128)(2,1)S(1)} %subtract_convert_fusion.5.refs_0_), channel_id=1, source_target_pairs={{0,1},{1,0},{2,3},{3,2},{4,5},{5,4},{6,7},{7,6},{8,9},{9,8},{10,11... | collective-permute-start | bytes 393224 | tf_op jit(solution)/shard_map/ppermute | solution.py:137
  68.0 5.8 %collective-permute-start.23 = (bf16[64,1024]{1,0:T(8,128)(2,1)S(1)}, bf16[64,1024]{1,0:T(8,128)(2,1)S(1)}, u32[]{:S(2)}, u32[]{:S(2)}) collective-permute-start(bf16[64,1024]{1,0:T(8,128)(2,1)S(1)} %shard_map.56), channel_id=1, source_target_pairs={{0,4},{4,0},{8,12},{12,8},{1,5},{5,1},{9,13},{13,9},{2,6},{6,2},{1... | collective-permute-start | bytes 393224 | tf_op jit(solution)/shard_map/ppermute | solution.py:137
  71.5 5.0 %collective-permute-start.21 = (bf16[64,1024]{1,0:T(8,128)(2,1)S(1)}, bf16[64,1024]{1,0:T(8,128)(2,1)S(1)}, u32[]{:S(2)}, u32[]{:S(2)}) collective-permute-start(bf16[64,1024]{1,0:T(8,128)(2,1)S(1)} %get-tuple-element.495), channel_id=1, source_target_pairs={{0,2},{1,3},{2,0},{3,1},{4,6},{5,7},{6,4},{7,5},{8,10},{9,11},{10,... | collective-permute-start | bytes 393224 | tf_op jit(solution)/shard_map/ppermute | solution.py:137
  73.9 8.8 %collective-permute-start.26 = (bf16[64,1024]{1,0:T(8,128)(2,1)S(1)}, bf16[64,1024]{1,0:T(8,128)(2,1)S(1)}, u32[]{:S(2)}, u32[]{:S(2)}) collective-permute-start(bf16[64,1024]{1,0:T(8,128)(2,1)S(1)} %get-tuple-element.493), channel_id=1, source_target_pairs={{0,8},{4,12},{8,0},{12,4},{1,9},{5,13},{9,1},{13,5},{2,10},{6,14},... | collective-permute-start | bytes 393224 | tf_op jit(solution)/shard_map/ppermute | solution.py:137
  76.6 1.4 collective-permute-start.24
  77.5 7.8 %collective-permute-start.25 = (bf16[64,1024]{1,0:T(8,128)(2,1)S(1)}, bf16[64,1024]{1,0:T(8,128)(2,1)S(1)}, u32[]{:S(2)}, u32[]{:S(2)}) collective-permute-start(bf16[64,1024]{1,0:T(8,128)(2,1)S(1)} %shard_map.59), channel_id=1, source_target_pairs={{0,4},{4,0},{8,12},{12,8},{1,5},{5,1},{9,13},{13,9},{2,6},{6,2},{1... | collective-permute-start | bytes 393224 | tf_op jit(solution)/shard_map/ppermute | solution.py:137
  82.7 5.1 %collective-permute-start.28 = (bf16[64,1024]{1,0:T(8,128)(2,1)S(1)}, bf16[64,1024]{1,0:T(8,128)(2,1)S(1)}, u32[]{:S(2)}, u32[]{:S(2)}) collective-permute-start(bf16[64,1024]{1,0:T(8,128)(2,1)S(1)} %add_convert_fusion.4.refs_0_.refs_1_), channel_id=1, source_target_pairs={{0,4},{4,0},{8,12},{12,8},{1,5},{5,1},{9,13},{13,9},{2,6},{6,2},{1... | collective-permute-start | bytes 393224 | tf_op jit(solution)/shard_map/ppermute | solution.py:137
  83.5 5.1 %collective-permute-start.29 = (bf16[64,1024]{1,0:T(8,128)(2,1)S(1)}, bf16[64,1024]{1,0:T(8,128)(2,1)S(1)}, u32[]{:S(2)}, u32[]{:S(2)}) collective-permute-start(bf16[64,1024]{1,0:T(8,128)(2,1)S(1)} %shard_map.61), channel_id=1, source_target_pairs={{0,1},{1,0},{2,3},{3,2},{4,5},{5,4},{6,7},{7,6},{8,9},{9,8},{10,11... | collective-permute-start | bytes 393224 | tf_op jit(solution)/shard_map/ppermute | solution.py:137
  85.3 10.0 %collective-permute-start.27 = (bf16[64,1024]{1,0:T(8,128)(2,1)S(1)}, bf16[64,1024]{1,0:T(8,128)(2,1)S(1)}, u32[]{:S(2)}, u32[]{:S(2)}) collective-permute-start(bf16[64,1024]{1,0:T(8,128)(2,1)S(1)} %get-tuple-element.491), channel_id=1, source_target_pairs={{0,8},{4,12},{8,0},{12,4},{1,9},{5,13},{9,1},{13,5},{2,10},{6,14},... | collective-permute-start | bytes 393224 | tf_op jit(solution)/shard_map/ppermute | solution.py:137
  88.6 7.9 %collective-permute-start.31 = (bf16[64,1024]{1,0:T(8,128)(2,1)S(1)}, bf16[64,1024]{1,0:T(8,128)(2,1)S(1)}, u32[]{:S(2)}, u32[]{:S(2)}) collective-permute-start(bf16[64,1024]{1,0:T(8,128)(2,1)S(1)} %get-tuple-element.489), channel_id=1, source_target_pairs={{0,2},{1,3},{2,0},{3,1},{4,6},{5,7},{6,4},{7,5},{8,10},{9,11},{10,... | collective-permute-start | bytes 393224 | tf_op jit(solution)/shard_map/ppermute | solution.py:137
  95.3 5.0 %collective-permute-start.30 = (bf16[64,1024]{1,0:T(8,128)(2,1)S(1)}, bf16[64,1024]{1,0:T(8,128)(2,1)S(1)}, u32[]{:S(2)}, u32[]{:S(2)}) collective-permute-start(bf16[64,1024]{1,0:T(8,128)(2,1)S(1)} %add_convert_fusion.3.refs_0_.refs_1_), channel_id=1, source_target_pairs={{0,4},{4,0},{8,12},{12,8},{1,5},{5,1},{9,13},{13,9},{2,6},{6,2},{1... | collective-permute-start | bytes 393224 | tf_op jit(solution)/shard_map/ppermute | solution.py:137
  96.4 4.8 %collective-permute-start.32 = (bf16[64,1024]{1,0:T(8,128)(2,1)S(1)}, bf16[64,1024]{1,0:T(8,128)(2,1)S(1)}, u32[]{:S(2)}, u32[]{:S(2)}) collective-permute-start(bf16[64,1024]{1,0:T(8,128)(2,1)S(1)} %shard_map.69), channel_id=1, source_target_pairs={{0,1},{1,0},{2,3},{3,2},{4,5},{5,4},{6,7},{7,6},{8,9},{9,8},{10,11... | collective-permute-start | bytes 393224 | tf_op jit(solution)/shard_map/ppermute | solution.py:137
  96.5 5.5 %collective-permute-start.34 = (bf16[64,1024]{1,0:T(8,128)(2,1)S(1)}, bf16[64,1024]{1,0:T(8,128)(2,1)S(1)}, u32[]{:S(2)}, u32[]{:S(2)}) collective-permute-start(bf16[64,1024]{1,0:T(8,128)(2,1)S(1)} %subtract_convert_fusion.3.refs_0_), channel_id=1, source_target_pairs={{0,1},{1,0},{2,3},{3,2},{4,5},{5,4},{6,7},{7,6},{8,9},{9,8},{10,11... | collective-permute-start | bytes 393224 | tf_op jit(solution)/shard_map/ppermute | solution.py:137
  97.8 5.6 %collective-permute-start.35 = (bf16[64,1024]{1,0:T(8,128)(2,1)S(1)}, bf16[64,1024]{1,0:T(8,128)(2,1)S(1)}, u32[]{:S(2)}, u32[]{:S(2)}) collective-permute-start(bf16[64,1024]{1,0:T(8,128)(2,1)S(1)} %shard_map.70), channel_id=1, source_target_pairs={{0,4},{4,0},{8,12},{12,8},{1,5},{5,1},{9,13},{13,9},{2,6},{6,2},{1... | collective-permute-start | bytes 393224 | tf_op jit(solution)/shard_map/ppermute | solution.py:137
  101.2 5.0 %collective-permute-start.33 = (bf16[64,1024]{1,0:T(8,128)(2,1)S(1)}, bf16[64,1024]{1,0:T(8,128)(2,1)S(1)}, u32[]{:S(2)}, u32[]{:S(2)}) collective-permute-start(bf16[64,1024]{1,0:T(8,128)(2,1)S(1)} %get-tuple-element.487), channel_id=1, source_target_pairs={{0,2},{1,3},{2,0},{3,1},{4,6},{5,7},{6,4},{7,5},{8,10},{9,11},{10,... | collective-permute-start | bytes 393224 | tf_op jit(solution)/shard_map/ppermute | solution.py:137
  103.5 8.6 %collective-permute-start.38 = (bf16[64,1024]{1,0:T(8,128)(2,1)S(1)}, bf16[64,1024]{1,0:T(8,128)(2,1)S(1)}, u32[]{:S(2)}, u32[]{:S(2)}) collective-permute-start(bf16[64,1024]{1,0:T(8,128)(2,1)S(1)} %get-tuple-element.485), channel_id=1, source_target_pairs={{0,8},{4,12},{8,0},{12,4},{1,9},{5,13},{9,1},{13,5},{2,10},{6,14},... | collective-permute-start | bytes 393224 | tf_op jit(solution)/shard_map/ppermute | solution.py:137
  106.3 1.4 collective-permute-start.36
  107.2 7.6 %collective-permute-start.37 = (bf16[64,1024]{1,0:T(8,128)(2,1)S(1)}, bf16[64,1024]{1,0:T(8,128)(2,1)S(1)}, u32[]{:S(2)}, u32[]{:S(2)}) collective-permute-start(bf16[64,1024]{1,0:T(8,128)(2,1)S(1)} %shard_map.73), channel_id=1, source_target_pairs={{0,4},{4,0},{8,12},{12,8},{1,5},{5,1},{9,13},{13,9},{2,6},{6,2},{1... | collective-permute-start | bytes 393224 | tf_op jit(solution)/shard_map/ppermute | solution.py:137
  112.1 5.2 %collective-permute-start.40 = (bf16[64,1024]{1,0:T(8,128)(2,1)S(1)}, bf16[64,1024]{1,0:T(8,128)(2,1)S(1)}, u32[]{:S(2)}, u32[]{:S(2)}) collective-permute-start(bf16[64,1024]{1,0:T(8,128)(2,1)S(1)} %add_convert_fusion.2.refs_0_), channel_id=1, source_target_pairs={{0,4},{4,0},{8,12},{12,8},{1,5},{5,1},{9,13},{13,9},{2,6},{6,2},{1... | collective-permute-start | bytes 393224 | tf_op jit(solution)/shard_map/ppermute | solution.py:137
  112.9 5.1 %collective-permute-start.41 = (bf16[64,1024]{1,0:T(8,128)(2,1)S(1)}, bf16[64,1024]{1,0:T(8,128)(2,1)S(1)}, u32[]{:S(2)}, u32[]{:S(2)}) collective-permute-start(bf16[64,1024]{1,0:T(8,128)(2,1)S(1)} %shard_map.75), channel_id=1, source_target_pairs={{0,1},{1,0},{2,3},{3,2},{4,5},{5,4},{6,7},{7,6},{8,9},{9,8},{10,11... | collective-permute-start | bytes 393224 | tf_op jit(solution)/shard_map/ppermute | solution.py:137
  114.8 8.7 %collective-permute-start.39 = (bf16[64,1024]{1,0:T(8,128)(2,1)S(1)}, bf16[64,1024]{1,0:T(8,128)(2,1)S(1)}, u32[]{:S(2)}, u32[]{:S(2)}) collective-permute-start(bf16[64,1024]{1,0:T(8,128)(2,1)S(1)} %get-tuple-element.483), channel_id=1, source_target_pairs={{0,8},{4,12},{8,0},{12,4},{1,9},{5,13},{9,1},{13,5},{2,10},{6,14},... | collective-permute-start | bytes 393224 | tf_op jit(solution)/shard_map/ppermute | solution.py:137
  118.1 5.0 %collective-permute-start.42 = (bf16[64,1024]{1,0:T(8,128)(2,1)S(1)}, bf16[64,1024]{1,0:T(8,128)(2,1)S(1)}, u32[]{:S(2)}, u32[]{:S(2)}) collective-permute-start(bf16[64,1024]{1,0:T(8,128)(2,1)S(1)} %get-tuple-element.481), channel_id=1, source_target_pairs={{0,2},{1,3},{2,0},{3,1},{4,6},{5,7},{6,4},{7,5},{8,10},{9,11},{10,... | collective-permute-start | bytes 393224 | tf_op jit(solution)/shard_map/ppermute | solution.py:137
  123.2 1.6 %collective-permute-start.44 = (bf16[64,1024]{1,0:T(8,128)(2,1)S(1)}, bf16[64,1024]{1,0:T(8,128)(2,1)S(1)}, u32[]{:S(2)}, u32[]{:S(2)}) collective-permute-start(bf16[64,1024]{1,0:T(8,128)(2,1)S(1)} %subtract_convert_fusion.1), channel_id=1, source_target_pairs={{0,1},{1,0},{2,3},{3,2},{4,5},{5,4},{6,7},{7,6},{8,9},{9,8},{10,11... | collective-permute-start | bytes 393224 | tf_op jit(solution)/shard_map/ppermute | solution.py:137
  123.5 6.3 %collective-permute-start.43 = (bf16[64,1024]{1,0:T(8,128)(2,1)S(1)}, bf16[64,1024]{1,0:T(8,128)(2,1)S(1)}, u32[]{:S(2)}, u32[]{:S(2)}) collective-permute-start(bf16[64,1024]{1,0:T(8,128)(2,1)S(1)} %add_convert_fusion.1.refs_0_), channel_id=1, source_target_pairs={{0,4},{4,0},{8,12},{12,8},{1,5},{5,1},{9,13},{13,9},{2,6},{6,2},{1... | collective-permute-start | bytes 393224 | tf_op jit(solution)/shard_map/ppermute | solution.py:137
  124.5 6.1 %collective-permute-start.45 = (bf16[64,1024]{1,0:T(8,128)(2,1)S(1)}, bf16[64,1024]{1,0:T(8,128)(2,1)S(1)}, u32[]{:S(2)}, u32[]{:S(2)}) collective-permute-start(bf16[64,1024]{1,0:T(8,128)(2,1)S(1)} %shard_map.81), channel_id=1, source_target_pairs={{0,1},{1,0},{2,3},{3,2},{4,5},{5,4},{6,7},{7,6},{8,9},{9,8},{10,11... | collective-permute-start | bytes 393224 | tf_op jit(solution)/shard_map/ppermute | solution.py:137
  125.6 6.8 %collective-permute-start.46 = (bf16[64,1024]{1,0:T(8,128)(2,1)S(1)}, bf16[64,1024]{1,0:T(8,128)(2,1)S(1)}, u32[]{:S(2)}, u32[]{:S(2)}) collective-permute-start(bf16[64,1024]{1,0:T(8,128)(2,1)S(1)} %shard_map.82), channel_id=1, source_target_pairs={{0,4},{4,0},{8,12},{12,8},{1,5},{5,1},{9,13},{13,9},{2,6},{6,2},{1... | collective-permute-start | bytes 393224 | tf_op jit(solution)/shard_map/ppermute | solution.py:137
  130.6 5.0 %collective-permute-start.47 = (bf16[64,1024]{1,0:T(8,128)(2,1)S(1)}, bf16[64,1024]{1,0:T(8,128)(2,1)S(1)}, u32[]{:S(2)}, u32[]{:S(2)}) collective-permute-start(bf16[64,1024]{1,0:T(8,128)(2,1)S(1)} %get-tuple-element.479), channel_id=1, source_target_pairs={{0,2},{1,3},{2,0},{3,1},{4,6},{5,7},{6,4},{7,5},{8,10},{9,11},{10,... | collective-permute-start | bytes 393224 | tf_op jit(solution)/shard_map/ppermute | solution.py:137
  135.7 1.4 collective-permute-start.48
  137.9 5.6 %collective-permute-start.49 = (bf16[64,1024]{1,0:T(8,128)(2,1)S(1)}, bf16[64,1024]{1,0:T(8,128)(2,1)S(1)}, u32[]{:S(2)}, u32[]{:S(2)}) collective-permute-start(bf16[64,1024]{1,0:T(8,128)(2,1)S(1)} %shard_map.85), channel_id=1, source_target_pairs={{0,4},{4,0},{8,12},{12,8},{1,5},{5,1},{9,13},{13,9},{2,6},{6,2},{1... | collective-permute-start | bytes 393224 | tf_op jit(solution)/shard_map/ppermute | solution.py:137
  143.6 8.5 %collective-permute-start.50 = (bf16[64,1024]{1,0:T(8,128)(2,1)S(1)}, bf16[64,1024]{1,0:T(8,128)(2,1)S(1)}, u32[]{:S(2)}, u32[]{:S(2)}) collective-permute-start(bf16[64,1024]{1,0:T(8,128)(2,1)S(1)} %broadcast_select_fusion.4), channel_id=1, source_target_pairs={{0,8},{4,12},{8,0},{12,4},{1,9},{5,13},{9,1},{13,5},{2,10},{6,14},... | collective-permute-start | bytes 393224 | tf_op jit(solution)/shard_map/ppermute | solution.py:137

commit v10 on v8

--- a/solution.py
+++ b/solution.py
@@ -266,11 +266,11 @@
             state[s]["flight"] = trade(leaving, "row", 1)
 
         first(0)
+        first(1)
         if steps_total > 1:
             base = order.run(lambda v: turned_sides(side_ref, v), right_sides)
         pair_sum(0)
         cross(0)
-        first(1)
         load_factor(1)
         load_inverse(1)
 
@@ -278,19 +278,21 @@
             final = exact and step == last_step
             solve(0, step - 1)
             factor_other(0, step)
-            load_inverse(step + 1)
+            older(1, step, range(step - 1))
             pair_sum(1)
             cross(1)
-            older(1, step, range(step - 1))
             factor_own(0, step)
             chip_sum(0)
             older(0, step + 1, range(step))
             load_factor(step + 1)
+            load_inverse(step + 1)
             if step == last_step:
                 residual(0, step)
-            solve(1, step - 1)
-            factor_other(1, step)
-            if step < last_step:
+                solve(1, step - 1)
+                factor_other(1, step)
+            else:
+                solve(1, step - 1)
+                factor_other(1, step)
                 residual(0, step)
             inverse_own(0, step)
             factor_own(1, step)

time: 154 us -> 153 us (level)
  starting transfers between devices: 46.5 us -> 48.4 us
  waiting for transfers between devices: 47.5 us -> 45.6 us
    ppermute x51, waiting for transfers between devices: 47.5 us -> 45.6 us  [trade(): return lax.ppermute(value, axis, [(i, i ^ step) for i in range(size)])]
    ppermute x51, starting transfers between devices: 46.5 us -> 48.4 us  [trade(): return lax.ppermute(value, axis, [(i, i ^ step) for i in range(size)])]
  transfers between devices with their start and end apart: 51 -> 51, of which waited for: 27 -> 26; matrix products, arithmetic and copies ran while one was open for 10% -> 10% of each run, Pallas kernels for 23% -> 23%
where the time goes in v10:
time: 153 us; the launch traced here: 152 us
  starting transfers between devices  48.4 us (32%)
  waiting for transfers between devices  45.6 us (30%)
  Pallas kernels  36.5 us (24%)
  local copies, waits for them, and re-layouts  18.6 us (12%)
  other arithmetic  2.27 us (1%)
    ppermute x51, starting transfers between devices, trade(): return lax.ppermute(value, axis, [(i, i ^ step) for i in range(size)])  48.4 us
    ppermute x51, waiting for transfers between devices, trade(): return lax.ppermute(value, axis, [(i, i ^ step) for i in range(size)])  45.6 us
    pallas_call x44, Pallas kernels, product(): pl.pallas_call(functools.partial(product_kernel, len(units)), out_shape=j...  33.9 us
    squeeze x22, local copies, waits for them, and re-layouts, block(): self.last = lax.optimization_barrier(self.run(lambda v: v[index], blocks))  16.5 us
  transfers between devices with their start and end apart: 51, of which 26 were waited for; matrix products, arithmetic and copies ran while one was open for 10% of the time, Pallas kernels for 23%

profile of v10, /device:TPU:0, one launch (start us, length us, event | category | flops | bytes accessed | tf_op | source)
XLA Modules:
  0.0 152.4 jit_solution(6064629039985765110)
XLA Ops:
  0.0 1.8 %slice_bitcast_fusion.20.block = bf16[1024,1024]{1,0:T(8,128)(2,1)S(1)} fusion(bf16[5,1024,1024]{2,1,0:T(8,128)(2,1)} %param.4), kind=kLoop, calls=%fused_computation.20 | loop fusion | bytes 4194304 | tf_op jit(solution)/shard_map/squeeze | solution.py:128
  1.8 1.1 slice_bitcast_fusion.21.right
  2.9 0.9 shard_map.37
  3.7 3.1 %collective-permute-start.1 = (bf16[64,1024]{1,0:T(8,128)(2,1)S(1)}, bf16[64,1024]{1,0:T(8,128)(2,1)S(1)}, u32[]{:S(2)}, u32[]{:S(2)}) collective-permute-start(bf16[64,1024]{1,0:T(8,128)(2,1)S(1)} %get-tuple-element.239), channel_id=1, source_target_pairs={{0,4},{4,0},{8,12},{12,8},{1,5},{5,1},{9,13},{13,9},{2,6},{6,2},{1... | collective-permute-start | bytes 393224 | tf_op jit(solution)/shard_map/ppermute | solution.py:135
  6.8 0.8 shard_map.38
  7.8 1.7 %copy-done = bf16[5,1024,256]{2,1,0:T(8,128)(2,1)S(1)} copy-done((bf16[5,1024,256]{2,1,0:T(8,128)(2,1)S(1)}, bf16[5,1024,256]{2,1,0:T(8,128)(2,1)}, u32[]{:S(2)}) %copy-start) | copy-done | bytes 2621464
  9.5 0.9 shard_map.39
  10.7 3.0 %collective-permute-start.2 = (bf16[64,1024]{1,0:T(8,128)(2,1)S(1)}, bf16[64,1024]{1,0:T(8,128)(2,1)S(1)}, u32[]{:S(2)}, u32[]{:S(2)}) collective-permute-start(bf16[64,1024]{1,0:T(8,128)(2,1)S(1)} %get-tuple-element.487), channel_id=1, source_target_pairs={{0,8},{4,12},{8,0},{12,4},{1,9},{5,13},{9,1},{13,5},{2,10},{6,14},... | collective-permute-start | bytes 393224 | tf_op jit(solution)/shard_map/ppermute | solution.py:135
  13.7 1.9 %slice_bitcast_fusion.19.block = bf16[1024,1024]{1,0:T(8,128)(2,1)S(1)} fusion(bf16[10,1024,1024]{2,1,0:T(8,128)(2,1)} %param.3), kind=kLoop, calls=%fused_computation.19 | loop fusion | bytes 4194304 | tf_op jit(solution)/shard_map/squeeze | solution.py:128
  15.6 2.1 %slice_bitcast_fusion.18.block = bf16[1024,1024]{1,0:T(8,128)(2,1)S(1)} fusion(bf16[5,1024,1024]{2,1,0:T(8,128)(2,1)} %param.4), kind=kLoop, calls=%fused_computation.18 | loop fusion | bytes 4194304 | tf_op jit(solution)/shard_map/squeeze | solution.py:128
  17.7 1.6 %collective-permute-done.2 = bf16[64,1024]{1,0:T(8,128)(2,1)S(1)} collective-permute-done((bf16[64,1024]{1,0:T(8,128)(2,1)S(1)}, bf16[64,1024]{1,0:T(8,128)(2,1)S(1)}, u32[]{:S(2)}, u32[]{:S(2)}) %collective-permute-start.2) | collective-permute-done | bytes 131104 | tf_op jit(solution)/shard_map/ppermute | solution.py:135
  19.4 0.8 collective-permute-start.4
  21.1 3.5 %collective-permute-start.3 = (bf16[64,1024]{1,0:T(8,128)(2,1)S(1)}, bf16[64,1024]{1,0:T(8,128)(2,1)S(1)}, u32[]{:S(2)}, u32[]{:S(2)}) collective-permute-start(bf16[64,1024]{1,0:T(8,128)(2,1)S(1)} %get-tuple-element.485), channel_id=1, source_target_pairs={{0,8},{4,12},{8,0},{12,4},{1,9},{5,13},{9,1},{13,5},{2,10},{6,14},... | collective-permute-start | bytes 393224 | tf_op jit(solution)/shard_map/ppermute | solution.py:135
  25.3 1.6 %collective-permute-start.7 = (bf16[64,1024]{1,0:T(8,128)(2,1)S(1)}, bf16[64,1024]{1,0:T(8,128)(2,1)S(1)}, u32[]{:S(2)}, u32[]{:S(2)}) collective-permute-start(bf16[64,1024]{1,0:T(8,128)(2,1)S(1)} %get-tuple-element.483), channel_id=1, source_target_pairs={{0,2},{1,3},{2,0},{3,1},{4,6},{5,7},{6,4},{7,5},{8,10},{9,11},{10,... | collective-permute-start | bytes 393224 | tf_op jit(solution)/shard_map/ppermute | solution.py:135
  26.9 1.8 %slice_bitcast_fusion.17.block = bf16[1024,1024]{1,0:T(8,128)(2,1)S(1)} fusion(bf16[10,1024,1024]{2,1,0:T(8,128)(2,1)} %param.3), kind=kLoop, calls=%fused_computation.17 | loop fusion | bytes 4194304 | tf_op jit(solution)/shard_map/squeeze | solution.py:128
  28.7 0.8 shard_map.42
  29.7 1.8 %slice_bitcast_fusion.15.block = bf16[1024,1024]{1,0:T(8,128)(2,1)S(1)} fusion(bf16[5,1024,1024]{2,1,0:T(8,128)(2,1)} %param.4), kind=kLoop, calls=%fused_computation.15 | loop fusion | bytes 4194304 | tf_op jit(solution)/shard_map/squeeze | solution.py:128
  31.5 0.8 collective-permute-start.6
  34.5 1.4 collective-permute-start.11
  35.9 1.1 collective-permute-done.6.refs_0_
  37.8 1.6 %collective-permute-start.9 = (bf16[64,1024]{1,0:T(8,128)(2,1)S(1)}, bf16[64,1024]{1,0:T(8,128)(2,1)S(1)}, u32[]{:S(2)}, u32[]{:S(2)}) collective-permute-start(bf16[64,1024]{1,0:T(8,128)(2,1)S(1)} %get-tuple-element.481), channel_id=1, source_target_pairs={{0,2},{1,3},{2,0},{3,1},{4,6},{5,7},{6,4},{7,5},{8,10},{9,11},{10,... | collective-permute-start | bytes 393224 | tf_op jit(solution)/shard_map/ppermute | solution.py:135
  40.2 4.8 %collective-permute-start.14 = (bf16[64,1024]{1,0:T(8,128)(2,1)S(1)}, bf16[64,1024]{1,0:T(8,128)(2,1)S(1)}, u32[]{:S(2)}, u32[]{:S(2)}) collective-permute-start(bf16[64,1024]{1,0:T(8,128)(2,1)S(1)} %get-tuple-element.479), channel_id=1, source_target_pairs={{0,8},{4,12},{8,0},{12,4},{1,9},{5,13},{9,1},{13,5},{2,10},{6,14},... | collective-permute-start | bytes 393224 | tf_op jit(solution)/shard_map/ppermute | solution.py:135
  47.2 3.5 %collective-permute-done.14 = bf16[64,1024]{1,0:T(8,128)(2,1)S(1)} collective-permute-done((bf16[64,1024]{1,0:T(8,128)(2,1)S(1)}, bf16[64,1024]{1,0:T(8,128)(2,1)S(1)}, u32[]{:S(2)}, u32[]{:S(2)}) %collective-permute-start.14) | collective-permute-done | bytes 131104 | tf_op jit(solution)/shard_map/ppermute | solution.py:135
  50.8 0.8 shard_map.49
  51.9 0.8 shard_map.50
  52.7 0.8 collective-permute-done.13
  53.5 2.5 %collective-permute-start.15 = (bf16[64,1024]{1,0:T(8,128)(2,1)S(1)}, bf16[64,1024]{1,0:T(8,128)(2,1)S(1)}, u32[]{:S(2)}, u32[]{:S(2)}) collective-permute-start(bf16[64,1024]{1,0:T(8,128)(2,1)S(1)} %get-tuple-element.477), channel_id=1, source_target_pairs={{0,8},{4,12},{8,0},{12,4},{1,9},{5,13},{9,1},{13,5},{2,10},{6,14},... | collective-permute-start | bytes 393224 | tf_op jit(solution)/shard_map/ppermute | solution.py:135
  57.8 0.8 shard_map.52.refs_2_
  58.8 0.8 shard_map.53
  59.8 1.8 %slice_bitcast_fusion.10.block = bf16[1024,1024]{1,0:T(8,128)(2,1)S(1)} fusion(bf16[5,1024,1024]{2,1,0:T(8,128)(2,1)} %param.4), kind=kLoop, calls=%fused_computation.10 | loop fusion | bytes 4194304 | tf_op jit(solution)/shard_map/squeeze | solution.py:128
  61.6 1.4 collective-permute-done.15
  63.1 0.8 shard_map.54
  65.3 2.1 %collective-permute-start.23 = (bf16[64,1024]{1,0:T(8,128)(2,1)S(1)}, bf16[64,1024]{1,0:T(8,128)(2,1)S(1)}, u32[]{:S(2)}, u32[]{:S(2)}) collective-permute-start(bf16[64,1024]{1,0:T(8,128)(2,1)S(1)} %shard_map.55), channel_id=1, source_target_pairs={{0,4},{4,0},{8,12},{12,8},{1,5},{5,1},{9,13},{13,9},{2,6},{6,2},{1... | collective-permute-start | bytes 393224 | tf_op jit(solution)/shard_map/ppermute | solution.py:135
  68.1 0.9 shard_map.56
  71.1 2.4 %collective-permute-start.26 = (bf16[64,1024]{1,0:T(8,128)(2,1)S(1)}, bf16[64,1024]{1,0:T(8,128)(2,1)S(1)}, u32[]{:S(2)}, u32[]{:S(2)}) collective-permute-start(bf16[64,1024]{1,0:T(8,128)(2,1)S(1)} %get-tuple-element.471), channel_id=1, source_target_pairs={{0,8},{4,12},{8,0},{12,4},{1,9},{5,13},{9,1},{13,5},{2,10},{6,14},... | collective-permute-start | bytes 393224 | tf_op jit(solution)/shard_map/ppermute | solution.py:135
  76.3 3.6 %collective-permute-done.26 = bf16[64,1024]{1,0:T(8,128)(2,1)S(1)} collective-permute-done((bf16[64,1024]{1,0:T(8,128)(2,1)S(1)}, bf16[64,1024]{1,0:T(8,128)(2,1)S(1)}, u32[]{:S(2)}, u32[]{:S(2)}) %collective-permute-start.26) | collective-permute-done | bytes 131104 | tf_op jit(solution)/shard_map/ppermute | solution.py:135
  80.0 0.8 shard_map.60
  81.0 0.8 shard_map.61.refs_2_
  82.0 0.8 shard_map.62
  82.9 2.7 %collective-permute-start.27 = (bf16[64,1024]{1,0:T(8,128)(2,1)S(1)}, bf16[64,1024]{1,0:T(8,128)(2,1)S(1)}, u32[]{:S(2)}, u32[]{:S(2)}) collective-permute-start(bf16[64,1024]{1,0:T(8,128)(2,1)S(1)} %get-tuple-element.469), channel_id=1, source_target_pairs={{0,8},{4,12},{8,0},{12,4},{1,9},{5,13},{9,1},{13,5},{2,10},{6,14},... | collective-permute-start | bytes 393224 | tf_op jit(solution)/shard_map/ppermute | solution.py:135
  85.6 0.8 shard_map.63
  87.2 0.8 shard_map.64.refs_2_
  88.2 0.8 shard_map.65.refs_2_
  89.2 0.8 shard_map.66
  90.2 1.8 %slice_bitcast_fusion.3.block = bf16[1024,1024]{1,0:T(8,128)(2,1)S(1)} fusion(bf16[5,1024,1024]{2,1,0:T(8,128)(2,1)} %param.4), kind=kLoop, calls=%fused_computation.3 | loop fusion | bytes 4194304 | tf_op jit(solution)/shard_map/squeeze | solution.py:128
  92.7 0.8 shard_map.67
  94.9 2.1 %collective-permute-start.35 = (bf16[64,1024]{1,0:T(8,128)(2,1)S(1)}, bf16[64,1024]{1,0:T(8,128)(2,1)S(1)}, u32[]{:S(2)}, u32[]{:S(2)}) collective-permute-start(bf16[64,1024]{1,0:T(8,128)(2,1)S(1)} %shard_map.68), channel_id=1, source_target_pairs={{0,4},{4,0},{8,12},{12,8},{1,5},{5,1},{9,13},{13,9},{2,6},{6,2},{1... | collective-permute-start | bytes 393224 | tf_op jit(solution)/shard_map/ppermute | solution.py:135
  97.0 0.8 collective-permute-done.30.refs_0_
  98.6 1.3 collective-permute-start.33
  100.7 2.4 %collective-permute-start.38 = (bf16[64,1024]{1,0:T(8,128)(2,1)S(1)}, bf16[64,1024]{1,0:T(8,128)(2,1)S(1)}, u32[]{:S(2)}, u32[]{:S(2)}) collective-permute-start(bf16[64,1024]{1,0:T(8,128)(2,1)S(1)} %get-tuple-element.463), channel_id=1, source_target_pairs={{0,8},{4,12},{8,0},{12,4},{1,9},{5,13},{9,1},{13,5},{2,10},{6,14},... | collective-permute-start | bytes 393224 | tf_op jit(solution)/shard_map/ppermute | solution.py:135
  105.8 3.6 %collective-permute-done.38 = bf16[64,1024]{1,0:T(8,128)(2,1)S(1)} collective-permute-done((bf16[64,1024]{1,0:T(8,128)(2,1)S(1)}, bf16[64,1024]{1,0:T(8,128)(2,1)S(1)}, u32[]{:S(2)}, u32[]{:S(2)}) %collective-permute-start.38) | collective-permute-done | bytes 131104 | tf_op jit(solution)/shard_map/ppermute | solution.py:135
  109.6 0.8 shard_map.73
  110.6 0.8 shard_map.74.refs_2_
  111.8 0.8 shard_map.75.refs_2_
  112.8 0.8 shard_map.76
  113.7 2.7 %collective-permute-start.39 = (bf16[64,1024]{1,0:T(8,128)(2,1)S(1)}, bf16[64,1024]{1,0:T(8,128)(2,1)S(1)}, u32[]{:S(2)}, u32[]{:S(2)}) collective-permute-start(bf16[64,1024]{1,0:T(8,128)(2,1)S(1)} %get-tuple-element.461), channel_id=1, source_target_pairs={{0,8},{4,12},{8,0},{12,4},{1,9},{5,13},{9,1},{13,5},{2,10},{6,14},... | collective-permute-start | bytes 393224 | tf_op jit(solution)/shard_map/ppermute | solution.py:135
  117.2 0.9 collective-permute-start.42
  118.2 4.7 %collective-permute-done.42 = bf16[64,1024]{1,0:T(8,128)(2,1)S(1)} collective-permute-done((bf16[64,1024]{1,0:T(8,128)(2,1)S(1)}, bf16[64,1024]{1,0:T(8,128)(2,1)S(1)}, u32[]{:S(2)}, u32[]{:S(2)}) %collective-permute-start.42) | collective-permute-done | bytes 131104 | tf_op jit(solution)/shard_map/ppermute | solution.py:135
  125.2 1.9 %collective-permute-start.46 = (bf16[64,1024]{1,0:T(8,128)(2,1)S(1)}, bf16[64,1024]{1,0:T(8,128)(2,1)S(1)}, u32[]{:S(2)}, u32[]{:S(2)}) collective-permute-start(bf16[64,1024]{1,0:T(8,128)(2,1)S(1)} %shard_map.79), channel_id=1, source_target_pairs={{0,4},{4,0},{8,12},{12,8},{1,5},{5,1},{9,13},{13,9},{2,6},{6,2},{1... | collective-permute-start | bytes 393224 | tf_op jit(solution)/shard_map/ppermute | solution.py:135
  127.2 2.3 %collective-permute-done.43.refs_0_ = bf16[64,1024]{1,0:T(8,128)(2,1)S(1)} collective-permute-done((bf16[64,1024]{1,0:T(8,128)(2,1)S(1)}, bf16[64,1024]{1,0:T(8,128)(2,1)S(1)}, u32[]{:S(2)}, u32[]{:S(2)}) %collective-permute-start.43) | collective-permute-done | bytes 131104 | tf_op jit(solution)/shard_map/ppermute | solution.py:135
  131.8 3.4 %collective-permute-done.47 = bf16[64,1024]{1,0:T(8,128)(2,1)S(1)} collective-permute-done((bf16[64,1024]{1,0:T(8,128)(2,1)S(1)}, bf16[64,1024]{1,0:T(8,128)(2,1)S(1)}, u32[]{:S(2)}, u32[]{:S(2)}) %collective-permute-start.47) | collective-permute-done | bytes 131104 | tf_op jit(solution)/shard_map/ppermute | solution.py:135
  135.5 1.3 collective-permute-done.48
  138.4 4.7 %collective-permute-done.49 = bf16[64,1024]{1,0:T(8,128)(2,1)S(1)} collective-permute-done((bf16[64,1024]{1,0:T(8,128)(2,1)S(1)}, bf16[64,1024]{1,0:T(8,128)(2,1)S(1)}, u32[]{:S(2)}, u32[]{:S(2)}) %collective-permute-start.49) | collective-permute-done | bytes 131104 | tf_op jit(solution)/shard_map/ppermute | solution.py:135
  143.5 8.1 %collective-permute-done.50 = bf16[64,1024]{1,0:T(8,128)(2,1)S(1)} collective-permute-done((bf16[64,1024]{1,0:T(8,128)(2,1)S(1)}, bf16[64,1024]{1,0:T(8,128)(2,1)S(1)}, u32[]{:S(2)}, u32[]{:S(2)}) %collective-permute-start.50) | collective-permute-done | bytes 131104 | tf_op jit(solution)/shard_map/ppermute | solution.py:135
  (162 shorter events, 35.5 us)
Async XLA Ops:
  3.7 7.0 %collective-permute-start.1 = (bf16[64,1024]{1,0:T(8,128)(2,1)S(1)}, bf16[64,1024]{1,0:T(8,128)(2,1)S(1)}, u32[]{:S(2)}, u32[]{:S(2)}) collective-permute-start(bf16[64,1024]{1,0:T(8,128)(2,1)S(1)} %get-tuple-element.239), channel_id=1, source_target_pairs={{0,4},{4,0},{8,12},{12,8},{1,5},{5,1},{9,13},{13,9},{2,6},{6,2},{1... | collective-permute-start | bytes 393224 | tf_op jit(solution)/shard_map/ppermute | solution.py:135
  7.7 13.4 %collective-permute-start = (bf16[64,1024]{1,0:T(8,128)(2,1)S(1)}, bf16[64,1024]{1,0:T(8,128)(2,1)S(1)}, u32[]{:S(2)}, u32[]{:S(2)}) collective-permute-start(bf16[64,1024]{1,0:T(8,128)(2,1)S(1)} %get-tuple-element.238), channel_id=1, source_target_pairs={{0,4},{4,0},{8,12},{12,8},{1,5},{5,1},{9,13},{13,9},{2,6},{6,2},{1... | collective-permute-start | bytes 393224 | tf_op jit(solution)/shard_map/ppermute | solution.py:135
  7.7 1.7 %copy-start = (bf16[5,1024,256]{2,1,0:T(8,128)(2,1)S(1)}, bf16[5,1024,256]{2,1,0:T(8,128)(2,1)}, u32[]{:S(2)}) copy-start(bf16[5,1024,256]{2,1,0:T(8,128)(2,1)} %sides) | copy-start | bytes 7864324
  10.7 8.6 %collective-permute-start.2 = (bf16[64,1024]{1,0:T(8,128)(2,1)S(1)}, bf16[64,1024]{1,0:T(8,128)(2,1)S(1)}, u32[]{:S(2)}, u32[]{:S(2)}) collective-permute-start(bf16[64,1024]{1,0:T(8,128)(2,1)S(1)} %get-tuple-element.487), channel_id=1, source_target_pairs={{0,8},{4,12},{8,0},{12,4},{1,9},{5,13},{9,1},{13,5},{2,10},{6,14},... | collective-permute-start | bytes 393224 | tf_op jit(solution)/shard_map/ppermute | solution.py:135
  13.7 15.8 %copy-start.1 = (bf16[10,1024,1024]{2,1,0:T(8,128)(2,1)S(1)}, bf16[10,1024,1024]{2,1,0:T(8,128)(2,1)}, u32[]{:S(2)}) copy-start(bf16[10,1024,1024]{2,1,0:T(8,128)(2,1)} %param.3) | copy-start | bytes 62914564
  19.4 5.1 %collective-permute-start.4 = (bf16[64,1024]{1,0:T(8,128)(2,1)S(1)}, bf16[64,1024]{1,0:T(8,128)(2,1)S(1)}, u32[]{:S(2)}, u32[]{:S(2)}) collective-permute-start(bf16[64,1024]{1,0:T(8,128)(2,1)S(1)} %add_convert_fusion.8.refs_0_.refs_1_), channel_id=1, source_target_pairs={{0,4},{4,0},{8,12},{12,8},{1,5},{5,1},{9,13},{13,9},{2,6},{6,2},{1... | collective-permute-start | bytes 393224 | tf_op jit(solution)/shard_map/ppermute | solution.py:135
  20.9 4.4 %collective-permute-start.5 = (bf16[64,1024]{1,0:T(8,128)(2,1)S(1)}, bf16[64,1024]{1,0:T(8,128)(2,1)S(1)}, u32[]{:S(2)}, u32[]{:S(2)}) collective-permute-start(bf16[64,1024]{1,0:T(8,128)(2,1)S(1)} %shard_map.40), channel_id=1, source_target_pairs={{0,1},{1,0},{2,3},{3,2},{4,5},{5,4},{6,7},{7,6},{8,9},{9,8},{10,11... | collective-permute-start | bytes 393224 | tf_op jit(solution)/shard_map/ppermute | solution.py:135
  21.1 10.4 %collective-permute-start.3 = (bf16[64,1024]{1,0:T(8,128)(2,1)S(1)}, bf16[64,1024]{1,0:T(8,128)(2,1)S(1)}, u32[]{:S(2)}, u32[]{:S(2)}) collective-permute-start(bf16[64,1024]{1,0:T(8,128)(2,1)S(1)} %get-tuple-element.485), channel_id=1, source_target_pairs={{0,8},{4,12},{8,0},{12,4},{1,9},{5,13},{9,1},{13,5},{2,10},{6,14},... | collective-permute-start | bytes 393224 | tf_op jit(solution)/shard_map/ppermute | solution.py:135
  25.3 7.8 %collective-permute-start.7 = (bf16[64,1024]{1,0:T(8,128)(2,1)S(1)}, bf16[64,1024]{1,0:T(8,128)(2,1)S(1)}, u32[]{:S(2)}, u32[]{:S(2)}) collective-permute-start(bf16[64,1024]{1,0:T(8,128)(2,1)S(1)} %get-tuple-element.483), channel_id=1, source_target_pairs={{0,2},{1,3},{2,0},{3,1},{4,6},{5,7},{6,4},{7,5},{8,10},{9,11},{10,... | collective-permute-start | bytes 393224 | tf_op jit(solution)/shard_map/ppermute | solution.py:135
  31.5 5.5 %collective-permute-start.6 = (bf16[64,1024]{1,0:T(8,128)(2,1)S(1)}, bf16[64,1024]{1,0:T(8,128)(2,1)S(1)}, u32[]{:S(2)}, u32[]{:S(2)}) collective-permute-start(bf16[64,1024]{1,0:T(8,128)(2,1)S(1)} %add_convert_fusion.7.refs_0_.refs_1_), channel_id=1, source_target_pairs={{0,4},{4,0},{8,12},{12,8},{1,5},{5,1},{9,13},{13,9},{2,6},{6,2},{1... | collective-permute-start | bytes 393224 | tf_op jit(solution)/shard_map/ppermute | solution.py:135
  33.0 4.7 %collective-permute-start.8 = (bf16[64,1024]{1,0:T(8,128)(2,1)S(1)}, bf16[64,1024]{1,0:T(8,128)(2,1)S(1)}, u32[]{:S(2)}, u32[]{:S(2)}) collective-permute-start(bf16[64,1024]{1,0:T(8,128)(2,1)S(1)} %shard_map.43), channel_id=1, source_target_pairs={{0,1},{1,0},{2,3},{3,2},{4,5},{5,4},{6,7},{7,6},{8,9},{9,8},{10,11... | collective-permute-start | bytes 393224 | tf_op jit(solution)/shard_map/ppermute | solution.py:135
  33.2 6.1 %collective-permute-start.10 = (bf16[64,1024]{1,0:T(8,128)(2,1)S(1)}, bf16[64,1024]{1,0:T(8,128)(2,1)S(1)}, u32[]{:S(2)}, u32[]{:S(2)}) collective-permute-start(bf16[64,1024]{1,0:T(8,128)(2,1)S(1)} %subtract_convert_fusion.7.refs_0_), channel_id=1, source_target_pairs={{0,1},{1,0},{2,3},{3,2},{4,5},{5,4},{6,7},{7,6},{8,9},{9,8},{10,11... | collective-permute-start | bytes 393224 | tf_op jit(solution)/shard_map/ppermute | solution.py:135
  34.5 5.6 %collective-permute-start.11 = (bf16[64,1024]{1,0:T(8,128)(2,1)S(1)}, bf16[64,1024]{1,0:T(8,128)(2,1)S(1)}, u32[]{:S(2)}, u32[]{:S(2)}) collective-permute-start(bf16[64,1024]{1,0:T(8,128)(2,1)S(1)} %shard_map.44), channel_id=1, source_target_pairs={{0,4},{4,0},{8,12},{12,8},{1,5},{5,1},{9,13},{13,9},{2,6},{6,2},{1... | collective-permute-start | bytes 393224 | tf_op jit(solution)/shard_map/ppermute | solution.py:135
  37.8 7.2 %collective-permute-start.9 = (bf16[64,1024]{1,0:T(8,128)(2,1)S(1)}, bf16[64,1024]{1,0:T(8,128)(2,1)S(1)}, u32[]{:S(2)}, u32[]{:S(2)}) collective-permute-start(bf16[64,1024]{1,0:T(8,128)(2,1)S(1)} %get-tuple-element.481), channel_id=1, source_target_pairs={{0,2},{1,3},{2,0},{3,1},{4,6},{5,7},{6,4},{7,5},{8,10},{9,11},{10,... | collective-permute-start | bytes 393224 | tf_op jit(solution)/shard_map/ppermute | solution.py:135
  40.2 10.5 %collective-permute-start.14 = (bf16[64,1024]{1,0:T(8,128)(2,1)S(1)}, bf16[64,1024]{1,0:T(8,128)(2,1)S(1)}, u32[]{:S(2)}, u32[]{:S(2)}) collective-permute-start(bf16[64,1024]{1,0:T(8,128)(2,1)S(1)} %get-tuple-element.479), channel_id=1, source_target_pairs={{0,8},{4,12},{8,0},{12,4},{1,9},{5,13},{9,1},{13,5},{2,10},{6,14},... | collective-permute-start | bytes 393224 | tf_op jit(solution)/shard_map/ppermute | solution.py:135
  45.0 1.4 collective-permute-start.12
  45.9 7.5 %collective-permute-start.13 = (bf16[64,1024]{1,0:T(8,128)(2,1)S(1)}, bf16[64,1024]{1,0:T(8,128)(2,1)S(1)}, u32[]{:S(2)}, u32[]{:S(2)}) collective-permute-start(bf16[64,1024]{1,0:T(8,128)(2,1)S(1)} %shard_map.47), channel_id=1, source_target_pairs={{0,4},{4,0},{8,12},{12,8},{1,5},{5,1},{9,13},{13,9},{2,6},{6,2},{1... | collective-permute-start | bytes 393224 | tf_op jit(solution)/shard_map/ppermute | solution.py:135
  50.8 5.5 %collective-permute-start.16 = (bf16[64,1024]{1,0:T(8,128)(2,1)S(1)}, bf16[64,1024]{1,0:T(8,128)(2,1)S(1)}, u32[]{:S(2)}, u32[]{:S(2)}) collective-permute-start(bf16[64,1024]{1,0:T(8,128)(2,1)S(1)} %add_convert_fusion.6.refs_0_.refs_1_), channel_id=1, source_target_pairs={{0,4},{4,0},{8,12},{12,8},{1,5},{5,1},{9,13},{13,9},{2,6},{6,2},{1... | collective-permute-start | bytes 393224 | tf_op jit(solution)/shard_map/ppermute | solution.py:135
  51.6 5.4 %collective-permute-start.17 = (bf16[64,1024]{1,0:T(8,128)(2,1)S(1)}, bf16[64,1024]{1,0:T(8,128)(2,1)S(1)}, u32[]{:S(2)}, u32[]{:S(2)}) collective-permute-start(bf16[64,1024]{1,0:T(8,128)(2,1)S(1)} %shard_map.49), channel_id=1, source_target_pairs={{0,1},{1,0},{2,3},{3,2},{4,5},{5,4},{6,7},{7,6},{8,9},{9,8},{10,11... | collective-permute-start | bytes 393224 | tf_op jit(solution)/shard_map/ppermute | solution.py:135
  53.5 9.5 %collective-permute-start.15 = (bf16[64,1024]{1,0:T(8,128)(2,1)S(1)}, bf16[64,1024]{1,0:T(8,128)(2,1)S(1)}, u32[]{:S(2)}, u32[]{:S(2)}) collective-permute-start(bf16[64,1024]{1,0:T(8,128)(2,1)S(1)} %get-tuple-element.477), channel_id=1, source_target_pairs={{0,8},{4,12},{8,0},{12,4},{1,9},{5,13},{9,1},{13,5},{2,10},{6,14},... | collective-permute-start | bytes 393224 | tf_op jit(solution)/shard_map/ppermute | solution.py:135
  57.1 6.9 %collective-permute-start.19 = (bf16[64,1024]{1,0:T(8,128)(2,1)S(1)}, bf16[64,1024]{1,0:T(8,128)(2,1)S(1)}, u32[]{:S(2)}, u32[]{:S(2)}) collective-permute-start(bf16[64,1024]{1,0:T(8,128)(2,1)S(1)} %get-tuple-element.475), channel_id=1, source_target_pairs={{0,2},{1,3},{2,0},{3,1},{4,6},{5,7},{6,4},{7,5},{8,10},{9,11},{10,... | collective-permute-start | bytes 393224 | tf_op jit(solution)/shard_map/ppermute | solution.py:135
  63.0 5.0 %collective-permute-start.18 = (bf16[64,1024]{1,0:T(8,128)(2,1)S(1)}, bf16[64,1024]{1,0:T(8,128)(2,1)S(1)}, u32[]{:S(2)}, u32[]{:S(2)}) collective-permute-start(bf16[64,1024]{1,0:T(8,128)(2,1)S(1)} %add_convert_fusion.5.refs_0_.refs_1_), channel_id=1, source_target_pairs={{0,4},{4,0},{8,12},{12,8},{1,5},{5,1},{9,13},{13,9},{2,6},{6,2},{1... | collective-permute-start | bytes 393224 | tf_op jit(solution)/shard_map/ppermute | solution.py:135
  63.9 5.1 %collective-permute-start.20 = (bf16[64,1024]{1,0:T(8,128)(2,1)S(1)}, bf16[64,1024]{1,0:T(8,128)(2,1)S(1)}, u32[]{:S(2)}, u32[]{:S(2)}) collective-permute-start(bf16[64,1024]{1,0:T(8,128)(2,1)S(1)} %shard_map.54), channel_id=1, source_target_pairs={{0,1},{1,0},{2,3},{3,2},{4,5},{5,4},{6,7},{7,6},{8,9},{9,8},{10,11... | collective-permute-start | bytes 393224 | tf_op jit(solution)/shard_map/ppermute | solution.py:135
  64.0 5.6 %collective-permute-start.22 = (bf16[64,1024]{1,0:T(8,128)(2,1)S(1)}, bf16[64,1024]{1,0:T(8,128)(2,1)S(1)}, u32[]{:S(2)}, u32[]{:S(2)}) collective-permute-start(bf16[64,1024]{1,0:T(8,128)(2,1)S(1)} %subtract_convert_fusion.5.refs_0_), channel_id=1, source_target_pairs={{0,1},{1,0},{2,3},{3,2},{4,5},{5,4},{6,7},{7,6},{8,9},{9,8},{10,11... | collective-permute-start | bytes 393224 | tf_op jit(solution)/shard_map/ppermute | solution.py:135
  65.3 5.8 %collective-permute-start.23 = (bf16[64,1024]{1,0:T(8,128)(2,1)S(1)}, bf16[64,1024]{1,0:T(8,128)(2,1)S(1)}, u32[]{:S(2)}, u32[]{:S(2)}) collective-permute-start(bf16[64,1024]{1,0:T(8,128)(2,1)S(1)} %shard_map.55), channel_id=1, source_target_pairs={{0,4},{4,0},{8,12},{12,8},{1,5},{5,1},{9,13},{13,9},{2,6},{6,2},{1... | collective-permute-start | bytes 393224 | tf_op jit(solution)/shard_map/ppermute | solution.py:135
  69.0 5.0 %collective-permute-start.21 = (bf16[64,1024]{1,0:T(8,128)(2,1)S(1)}, bf16[64,1024]{1,0:T(8,128)(2,1)S(1)}, u32[]{:S(2)}, u32[]{:S(2)}) collective-permute-start(bf16[64,1024]{1,0:T(8,128)(2,1)S(1)} %get-tuple-element.473), channel_id=1, source_target_pairs={{0,2},{1,3},{2,0},{3,1},{4,6},{5,7},{6,4},{7,5},{8,10},{9,11},{10,... | collective-permute-start | bytes 393224 | tf_op jit(solution)/shard_map/ppermute | solution.py:135
  71.1 8.8 %collective-permute-start.26 = (bf16[64,1024]{1,0:T(8,128)(2,1)S(1)}, bf16[64,1024]{1,0:T(8,128)(2,1)S(1)}, u32[]{:S(2)}, u32[]{:S(2)}) collective-permute-start(bf16[64,1024]{1,0:T(8,128)(2,1)S(1)} %get-tuple-element.471), channel_id=1, source_target_pairs={{0,8},{4,12},{8,0},{12,4},{1,9},{5,13},{9,1},{13,5},{2,10},{6,14},... | collective-permute-start | bytes 393224 | tf_op jit(solution)/shard_map/ppermute | solution.py:135
  74.1 1.4 collective-permute-start.24
  75.0 7.9 %collective-permute-start.25 = (bf16[64,1024]{1,0:T(8,128)(2,1)S(1)}, bf16[64,1024]{1,0:T(8,128)(2,1)S(1)}, u32[]{:S(2)}, u32[]{:S(2)}) collective-permute-start(bf16[64,1024]{1,0:T(8,128)(2,1)S(1)} %shard_map.58), channel_id=1, source_target_pairs={{0,4},{4,0},{8,12},{12,8},{1,5},{5,1},{9,13},{13,9},{2,6},{6,2},{1... | collective-permute-start | bytes 393224 | tf_op jit(solution)/shard_map/ppermute | solution.py:135
  79.9 5.7 %collective-permute-start.28 = (bf16[64,1024]{1,0:T(8,128)(2,1)S(1)}, bf16[64,1024]{1,0:T(8,128)(2,1)S(1)}, u32[]{:S(2)}, u32[]{:S(2)}) collective-permute-start(bf16[64,1024]{1,0:T(8,128)(2,1)S(1)} %add_convert_fusion.4.refs_0_.refs_1_), channel_id=1, source_target_pairs={{0,4},{4,0},{8,12},{12,8},{1,5},{5,1},{9,13},{13,9},{2,6},{6,2},{1... | collective-permute-start | bytes 393224 | tf_op jit(solution)/shard_map/ppermute | solution.py:135
  80.8 5.6 %collective-permute-start.29 = (bf16[64,1024]{1,0:T(8,128)(2,1)S(1)}, bf16[64,1024]{1,0:T(8,128)(2,1)S(1)}, u32[]{:S(2)}, u32[]{:S(2)}) collective-permute-start(bf16[64,1024]{1,0:T(8,128)(2,1)S(1)} %shard_map.60), channel_id=1, source_target_pairs={{0,1},{1,0},{2,3},{3,2},{4,5},{5,4},{6,7},{7,6},{8,9},{9,8},{10,11... | collective-permute-start | bytes 393224 | tf_op jit(solution)/shard_map/ppermute | solution.py:135
  82.9 9.7 %collective-permute-start.27 = (bf16[64,1024]{1,0:T(8,128)(2,1)S(1)}, bf16[64,1024]{1,0:T(8,128)(2,1)S(1)}, u32[]{:S(2)}, u32[]{:S(2)}) collective-permute-start(bf16[64,1024]{1,0:T(8,128)(2,1)S(1)} %get-tuple-element.469), channel_id=1, source_target_pairs={{0,8},{4,12},{8,0},{12,4},{1,9},{5,13},{9,1},{13,5},{2,10},{6,14},... | collective-permute-start | bytes 393224 | tf_op jit(solution)/shard_map/ppermute | solution.py:135
  86.5 7.1 %collective-permute-start.31 = (bf16[64,1024]{1,0:T(8,128)(2,1)S(1)}, bf16[64,1024]{1,0:T(8,128)(2,1)S(1)}, u32[]{:S(2)}, u32[]{:S(2)}) collective-permute-start(bf16[64,1024]{1,0:T(8,128)(2,1)S(1)} %get-tuple-element.467), channel_id=1, source_target_pairs={{0,2},{1,3},{2,0},{3,1},{4,6},{5,7},{6,4},{7,5},{8,10},{9,11},{10,... | collective-permute-start | bytes 393224 | tf_op jit(solution)/shard_map/ppermute | solution.py:135
  92.6 5.2 %collective-permute-start.30 = (bf16[64,1024]{1,0:T(8,128)(2,1)S(1)}, bf16[64,1024]{1,0:T(8,128)(2,1)S(1)}, u32[]{:S(2)}, u32[]{:S(2)}) collective-permute-start(bf16[64,1024]{1,0:T(8,128)(2,1)S(1)} %add_convert_fusion.3.refs_0_.refs_1_), channel_id=1, source_target_pairs={{0,4},{4,0},{8,12},{12,8},{1,5},{5,1},{9,13},{13,9},{2,6},{6,2},{1... | collective-permute-start | bytes 393224 | tf_op jit(solution)/shard_map/ppermute | solution.py:135
  93.4 5.1 %collective-permute-start.32 = (bf16[64,1024]{1,0:T(8,128)(2,1)S(1)}, bf16[64,1024]{1,0:T(8,128)(2,1)S(1)}, u32[]{:S(2)}, u32[]{:S(2)}) collective-permute-start(bf16[64,1024]{1,0:T(8,128)(2,1)S(1)} %shard_map.67), channel_id=1, source_target_pairs={{0,1},{1,0},{2,3},{3,2},{4,5},{5,4},{6,7},{7,6},{8,9},{9,8},{10,11... | collective-permute-start | bytes 393224 | tf_op jit(solution)/shard_map/ppermute | solution.py:135
  93.6 6.3 %collective-permute-start.34 = (bf16[64,1024]{1,0:T(8,128)(2,1)S(1)}, bf16[64,1024]{1,0:T(8,128)(2,1)S(1)}, u32[]{:S(2)}, u32[]{:S(2)}) collective-permute-start(bf16[64,1024]{1,0:T(8,128)(2,1)S(1)} %subtract_convert_fusion.3.refs_0_), channel_id=1, source_target_pairs={{0,1},{1,0},{2,3},{3,2},{4,5},{5,4},{6,7},{7,6},{8,9},{9,8},{10,11... | collective-permute-start | bytes 393224 | tf_op jit(solution)/shard_map/ppermute | solution.py:135
  94.9 5.8 %collective-permute-start.35 = (bf16[64,1024]{1,0:T(8,128)(2,1)S(1)}, bf16[64,1024]{1,0:T(8,128)(2,1)S(1)}, u32[]{:S(2)}, u32[]{:S(2)}) collective-permute-start(bf16[64,1024]{1,0:T(8,128)(2,1)S(1)} %shard_map.68), channel_id=1, source_target_pairs={{0,4},{4,0},{8,12},{12,8},{1,5},{5,1},{9,13},{13,9},{2,6},{6,2},{1... | collective-permute-start | bytes 393224 | tf_op jit(solution)/shard_map/ppermute | solution.py:135
  98.6 5.0 %collective-permute-start.33 = (bf16[64,1024]{1,0:T(8,128)(2,1)S(1)}, bf16[64,1024]{1,0:T(8,128)(2,1)S(1)}, u32[]{:S(2)}, u32[]{:S(2)}) collective-permute-start(bf16[64,1024]{1,0:T(8,128)(2,1)S(1)} %get-tuple-element.465), channel_id=1, source_target_pairs={{0,2},{1,3},{2,0},{3,1},{4,6},{5,7},{6,4},{7,5},{8,10},{9,11},{10,... | collective-permute-start | bytes 393224 | tf_op jit(solution)/shard_map/ppermute | solution.py:135
  100.7 8.8 %collective-permute-start.38 = (bf16[64,1024]{1,0:T(8,128)(2,1)S(1)}, bf16[64,1024]{1,0:T(8,128)(2,1)S(1)}, u32[]{:S(2)}, u32[]{:S(2)}) collective-permute-start(bf16[64,1024]{1,0:T(8,128)(2,1)S(1)} %get-tuple-element.463), channel_id=1, source_target_pairs={{0,8},{4,12},{8,0},{12,4},{1,9},{5,13},{9,1},{13,5},{2,10},{6,14},... | collective-permute-start | bytes 393224 | tf_op jit(solution)/shard_map/ppermute | solution.py:135
  103.7 1.4 collective-permute-start.36
  104.5 9.1 %collective-permute-start.37 = (bf16[64,1024]{1,0:T(8,128)(2,1)S(1)}, bf16[64,1024]{1,0:T(8,128)(2,1)S(1)}, u32[]{:S(2)}, u32[]{:S(2)}) collective-permute-start(bf16[64,1024]{1,0:T(8,128)(2,1)S(1)} %shard_map.71), channel_id=1, source_target_pairs={{0,4},{4,0},{8,12},{12,8},{1,5},{5,1},{9,13},{13,9},{2,6},{6,2},{1... | collective-permute-start | bytes 393224 | tf_op jit(solution)/shard_map/ppermute | solution.py:135
  109.5 6.9 %collective-permute-start.40 = (bf16[64,1024]{1,0:T(8,128)(2,1)S(1)}, bf16[64,1024]{1,0:T(8,128)(2,1)S(1)}, u32[]{:S(2)}, u32[]{:S(2)}) collective-permute-start(bf16[64,1024]{1,0:T(8,128)(2,1)S(1)} %add_convert_fusion.2.refs_0_), channel_id=1, source_target_pairs={{0,4},{4,0},{8,12},{12,8},{1,5},{5,1},{9,13},{13,9},{2,6},{6,2},{1... | collective-permute-start | bytes 393224 | tf_op jit(solution)/shard_map/ppermute | solution.py:135
  110.3 6.8 %collective-permute-start.41 = (bf16[64,1024]{1,0:T(8,128)(2,1)S(1)}, bf16[64,1024]{1,0:T(8,128)(2,1)S(1)}, u32[]{:S(2)}, u32[]{:S(2)}) collective-permute-start(bf16[64,1024]{1,0:T(8,128)(2,1)S(1)} %shard_map.73), channel_id=1, source_target_pairs={{0,1},{1,0},{2,3},{3,2},{4,5},{5,4},{6,7},{7,6},{8,9},{9,8},{10,11... | collective-permute-start | bytes 393224 | tf_op jit(solution)/shard_map/ppermute | solution.py:135
  113.7 9.7 %collective-permute-start.39 = (bf16[64,1024]{1,0:T(8,128)(2,1)S(1)}, bf16[64,1024]{1,0:T(8,128)(2,1)S(1)}, u32[]{:S(2)}, u32[]{:S(2)}) collective-permute-start(bf16[64,1024]{1,0:T(8,128)(2,1)S(1)} %get-tuple-element.461), channel_id=1, source_target_pairs={{0,8},{4,12},{8,0},{12,4},{1,9},{5,13},{9,1},{13,5},{2,10},{6,14},... | collective-permute-start | bytes 393224 | tf_op jit(solution)/shard_map/ppermute | solution.py:135
  117.2 5.7 %collective-permute-start.42 = (bf16[64,1024]{1,0:T(8,128)(2,1)S(1)}, bf16[64,1024]{1,0:T(8,128)(2,1)S(1)}, u32[]{:S(2)}, u32[]{:S(2)}) collective-permute-start(bf16[64,1024]{1,0:T(8,128)(2,1)S(1)} %get-tuple-element.459), channel_id=1, source_target_pairs={{0,2},{1,3},{2,0},{3,1},{4,6},{5,7},{6,4},{7,5},{8,10},{9,11},{10,... | collective-permute-start | bytes 393224 | tf_op jit(solution)/shard_map/ppermute | solution.py:135
  122.9 1.5 %collective-permute-start.44 = (bf16[64,1024]{1,0:T(8,128)(2,1)S(1)}, bf16[64,1024]{1,0:T(8,128)(2,1)S(1)}, u32[]{:S(2)}, u32[]{:S(2)}) collective-permute-start(bf16[64,1024]{1,0:T(8,128)(2,1)S(1)} %subtract_convert_fusion.1), channel_id=1, source_target_pairs={{0,1},{1,0},{2,3},{3,2},{4,5},{5,4},{6,7},{7,6},{8,9},{9,8},{10,11... | collective-permute-start | bytes 393224 | tf_op jit(solution)/shard_map/ppermute | solution.py:135
  123.4 6.1 %collective-permute-start.43 = (bf16[64,1024]{1,0:T(8,128)(2,1)S(1)}, bf16[64,1024]{1,0:T(8,128)(2,1)S(1)}, u32[]{:S(2)}, u32[]{:S(2)}) collective-permute-start(bf16[64,1024]{1,0:T(8,128)(2,1)S(1)} %add_convert_fusion.1.refs_0_), channel_id=1, source_target_pairs={{0,4},{4,0},{8,12},{12,8},{1,5},{5,1},{9,13},{13,9},{2,6},{6,2},{1... | collective-permute-start | bytes 393224 | tf_op jit(solution)/shard_map/ppermute | solution.py:135
  124.2 6.0 %collective-permute-start.45 = (bf16[64,1024]{1,0:T(8,128)(2,1)S(1)}, bf16[64,1024]{1,0:T(8,128)(2,1)S(1)}, u32[]{:S(2)}, u32[]{:S(2)}) collective-permute-start(bf16[64,1024]{1,0:T(8,128)(2,1)S(1)} %shard_map.78), channel_id=1, source_target_pairs={{0,1},{1,0},{2,3},{3,2},{4,5},{5,4},{6,7},{7,6},{8,9},{9,8},{10,11... | collective-permute-start | bytes 393224 | tf_op jit(solution)/shard_map/ppermute | solution.py:135
  125.2 6.6 %collective-permute-start.46 = (bf16[64,1024]{1,0:T(8,128)(2,1)S(1)}, bf16[64,1024]{1,0:T(8,128)(2,1)S(1)}, u32[]{:S(2)}, u32[]{:S(2)}) collective-permute-start(bf16[64,1024]{1,0:T(8,128)(2,1)S(1)} %shard_map.79), channel_id=1, source_target_pairs={{0,4},{4,0},{8,12},{12,8},{1,5},{5,1},{9,13},{13,9},{2,6},{6,2},{1... | collective-permute-start | bytes 393224 | tf_op jit(solution)/shard_map/ppermute | solution.py:135
  130.3 5.0 %collective-permute-start.47 = (bf16[64,1024]{1,0:T(8,128)(2,1)S(1)}, bf16[64,1024]{1,0:T(8,128)(2,1)S(1)}, u32[]{:S(2)}, u32[]{:S(2)}) collective-permute-start(bf16[64,1024]{1,0:T(8,128)(2,1)S(1)} %get-tuple-element.457), channel_id=1, source_target_pairs={{0,2},{1,3},{2,0},{3,1},{4,6},{5,7},{6,4},{7,5},{8,10},{9,11},{10,... | collective-permute-start | bytes 393224 | tf_op jit(solution)/shard_map/ppermute | solution.py:135
  135.3 1.4 collective-permute-start.48
  137.5 5.6 %collective-permute-start.49 = (bf16[64,1024]{1,0:T(8,128)(2,1)S(1)}, bf16[64,1024]{1,0:T(8,128)(2,1)S(1)}, u32[]{:S(2)}, u32[]{:S(2)}) collective-permute-start(bf16[64,1024]{1,0:T(8,128)(2,1)S(1)} %shard_map.82), channel_id=1, source_target_pairs={{0,4},{4,0},{8,12},{12,8},{1,5},{5,1},{9,13},{13,9},{2,6},{6,2},{1... | collective-permute-start | bytes 393224 | tf_op jit(solution)/shard_map/ppermute | solution.py:135
  143.2 8.5 %collective-permute-start.50 = (bf16[64,1024]{1,0:T(8,128)(2,1)S(1)}, bf16[64,1024]{1,0:T(8,128)(2,1)S(1)}, u32[]{:S(2)}, u32[]{:S(2)}) collective-permute-start(bf16[64,1024]{1,0:T(8,128)(2,1)S(1)} %broadcast_select_fusion.4), channel_id=1, source_target_pairs={{0,8},{4,12},{8,0},{12,4},{1,9},{5,13},{9,1},{13,5},{2,10},{6,14},... | collective-permute-start | bytes 393224 | tf_op jit(solution)/shard_map/ppermute | solution.py:135
  143.5 8.2 %copy-start.2 = (bf16[5,1024,64]{1,2,0:T(8,128)(2,1)}, bf16[5,1024,64]{1,2,0:T(8,128)(2,1)S(1)}, u32[]{:S(2)}) copy-start(bf16[5,1024,64]{1,2,0:T(8,128)(2,1)S(1)} %bitcast_dynamic-update-slice_fusion) | copy-start | bytes 1966084

commit v11 on v7

--- a/solution.py
+++ b/solution.py
@@ -266,13 +266,12 @@
             state[s]["flight"] = trade(leaving, "row", 1)
 
         first(0)
+        first(1)
         if steps_total > 1:
             base = order.run(lambda v: turned_sides(side_ref, v), right_sides)
-            load_factor(1)
         pair_sum(0)
         cross(0)
-        first(1)
-        load_inverse(1)
+        load_factor(1)
 
         for step in range(1, steps_total):
             final = exact and step == last_step
@@ -284,7 +283,20 @@
             chip_sum(0)
             older(step + 1, range(step - 1))
             load_factor(step + 1)
-            load_inverse(step + 1)
+            load_inverse(step)
+            if final:
+                residual(0, step)
+                solve(1, step - 1)
+                factor_other(1, step)
+                factor_own(1, step)
+                chip_sum(1)
+                inverse_own(0, step)
+                inverse_other(0, step)
+                residual(1, step)
+                pair_sum(0)
+                inverse_own(1, step)
+                inverse_other(1, step)
+                continue
             solve(1, step - 1)
             factor_other(1, step)
             residual(0, step)
@@ -294,8 +306,7 @@
             older(step + 1, [step - 1])
             inverse_other(0, step)
             pair_sum(0)
-            if not final:
-                cross(0)
+            cross(0)
             residual(1, step)
             inverse_own(1, step)
             inverse_other(1, step)

time: 152 us -> 149 us (0.980)
  local copies, waits for them, and re-layouts: 21.5 us -> 17 us
  waiting for transfers between devices: 53 us -> 55.4 us
    ppermute x51, waiting for transfers between devices: 53 us -> 55.4 us  [trade(): return lax.ppermute(value, axis, [(i, i ^ step) for i in range(size)])]
    squeeze x16, local copies, waits for them, and re-layouts: 16.9 us -> 14.9 us  [block(): self.last = lax.optimization_barrier(self.run(lambda v: v[index], blocks))]
  transfers between devices with their start and end apart: 51 -> 51, of which waited for: 25 -> 28; matrix products, arithmetic and copies ran while one was open for 11% -> 9% of each run, Pallas kernels for 20% -> 21%
where the time goes in v11:
time: 149 us; the launch traced here: 148 us
  waiting for transfers between devices  55.4 us (37%)
  starting transfers between devices  40.1 us (27%)
  Pallas kernels  32.5 us (22%)
  local copies, waits for them, and re-layouts  17 us (11%)
  other arithmetic  2.24 us (2%)
    ppermute x51, waiting for transfers between devices, trade(): return lax.ppermute(value, axis, [(i, i ^ step) for i in range(size)])  55.4 us
    ppermute x51, starting transfers between devices, trade(): return lax.ppermute(value, axis, [(i, i ^ step) for i in range(size)])  40.1 us
    pallas_call x38, Pallas kernels, product(): pl.pallas_call(functools.partial(product_kernel, len(units)), out_shape=j...  29.9 us
    squeeze x16, local copies, waits for them, and re-layouts, block(): self.last = lax.optimization_barrier(self.run(lambda v: v[index], blocks))  14.9 us
  transfers between devices with their start and end apart: 51, of which 28 were waited for; matrix products, arithmetic and copies ran while one was open for 9% of the time, Pallas kernels for 21%

profile of v11, /device:TPU:0, one launch (start us, length us, event | category | flops | bytes accessed | tf_op | source)
XLA Modules:
  0.0 148.2 jit_solution(2980605649205027214)
XLA Ops:
  0.0 1.8 %slice_bitcast_fusion.14.block = bf16[1024,1024]{1,0:T(8,128)(2,1)S(1)} fusion(bf16[5,1024,1024]{2,1,0:T(8,128)(2,1)} %param.4), kind=kLoop, calls=%fused_computation.14 | loop fusion | bytes 4194304 | tf_op jit(solution)/shard_map/squeeze | solution.py:128
  1.8 1.1 slice_bitcast_fusion.15.right
  2.9 0.9 shard_map.37
  3.7 3.1 %collective-permute-start.1 = (bf16[64,1024]{1,0:T(8,128)(2,1)S(1)}, bf16[64,1024]{1,0:T(8,128)(2,1)S(1)}, u32[]{:S(2)}, u32[]{:S(2)}) collective-permute-start(bf16[64,1024]{1,0:T(8,128)(2,1)S(1)} %get-tuple-element.224), channel_id=1, source_target_pairs={{0,4},{4,0},{8,12},{12,8},{1,5},{5,1},{9,13},{13,9},{2,6},{6,2},{1... | collective-permute-start | bytes 393224 | tf_op jit(solution)/shard_map/ppermute | solution.py:135
  6.8 0.8 shard_map.38
  7.8 1.7 %copy-done = bf16[5,1024,256]{2,1,0:T(8,128)(2,1)S(1)} copy-done((bf16[5,1024,256]{2,1,0:T(8,128)(2,1)S(1)}, bf16[5,1024,256]{2,1,0:T(8,128)(2,1)}, u32[]{:S(2)}) %copy-start) | copy-done | bytes 2621464
  9.5 0.9 shard_map.39
  10.7 3.0 %collective-permute-start.2 = (bf16[64,1024]{1,0:T(8,128)(2,1)S(1)}, bf16[64,1024]{1,0:T(8,128)(2,1)S(1)}, u32[]{:S(2)}, u32[]{:S(2)}) collective-permute-start(bf16[64,1024]{1,0:T(8,128)(2,1)S(1)} %get-tuple-element.457), channel_id=1, source_target_pairs={{0,8},{4,12},{8,0},{12,4},{1,9},{5,13},{9,1},{13,5},{2,10},{6,14},... | collective-permute-start | bytes 393224 | tf_op jit(solution)/shard_map/ppermute | solution.py:135
  13.7 1.8 %slice_bitcast_fusion.13.block = bf16[1024,1024]{1,0:T(8,128)(2,1)S(1)} fusion(bf16[10,1024,1024]{2,1,0:T(8,128)(2,1)} %param.3), kind=kLoop, calls=%fused_computation.13 | loop fusion | bytes 4194304 | tf_op jit(solution)/shard_map/squeeze | solution.py:128
  15.5 3.9 %collective-permute-done.2 = bf16[64,1024]{1,0:T(8,128)(2,1)S(1)} collective-permute-done((bf16[64,1024]{1,0:T(8,128)(2,1)S(1)}, bf16[64,1024]{1,0:T(8,128)(2,1)S(1)}, u32[]{:S(2)}, u32[]{:S(2)}) %collective-permute-start.2) | collective-permute-done | bytes 131104 | tf_op jit(solution)/shard_map/ppermute | solution.py:135
  19.4 0.8 collective-permute-start.4
  21.1 3.5 %collective-permute-start.3 = (bf16[64,1024]{1,0:T(8,128)(2,1)S(1)}, bf16[64,1024]{1,0:T(8,128)(2,1)S(1)}, u32[]{:S(2)}, u32[]{:S(2)}) collective-permute-start(bf16[64,1024]{1,0:T(8,128)(2,1)S(1)} %get-tuple-element.455), channel_id=1, source_target_pairs={{0,8},{4,12},{8,0},{12,4},{1,9},{5,13},{9,1},{13,5},{2,10},{6,14},... | collective-permute-start | bytes 393224 | tf_op jit(solution)/shard_map/ppermute | solution.py:135
  25.3 1.6 %collective-permute-start.7 = (bf16[64,1024]{1,0:T(8,128)(2,1)S(1)}, bf16[64,1024]{1,0:T(8,128)(2,1)S(1)}, u32[]{:S(2)}, u32[]{:S(2)}) collective-permute-start(bf16[64,1024]{1,0:T(8,128)(2,1)S(1)} %get-tuple-element.453), channel_id=1, source_target_pairs={{0,2},{1,3},{2,0},{3,1},{4,6},{5,7},{6,4},{7,5},{8,10},{9,11},{10,... | collective-permute-start | bytes 393224 | tf_op jit(solution)/shard_map/ppermute | solution.py:135
  26.9 1.9 %slice_bitcast_fusion.12.block = bf16[1024,1024]{1,0:T(8,128)(2,1)S(1)} fusion(bf16[10,1024,1024]{2,1,0:T(8,128)(2,1)} %param.3), kind=kLoop, calls=%fused_computation.12 | loop fusion | bytes 4194304 | tf_op jit(solution)/shard_map/squeeze | solution.py:128
  28.8 1.8 %slice_bitcast_fusion.11.block = bf16[1024,1024]{1,0:T(8,128)(2,1)S(1)} fusion(bf16[5,1024,1024]{2,1,0:T(8,128)(2,1)} %param.4), kind=kLoop, calls=%fused_computation.11 | loop fusion | bytes 4194304 | tf_op jit(solution)/shard_map/squeeze | solution.py:128
  30.5 0.9 collective-permute-done.3
  34.1 1.7 %collective-permute-start.11 = (bf16[64,1024]{1,0:T(8,128)(2,1)S(1)}, bf16[64,1024]{1,0:T(8,128)(2,1)S(1)}, u32[]{:S(2)}, u32[]{:S(2)}) collective-permute-start(bf16[64,1024]{1,0:T(8,128)(2,1)S(1)} %shard_map.43), channel_id=1, source_target_pairs={{0,4},{4,0},{8,12},{12,8},{1,5},{5,1},{9,13},{13,9},{2,6},{6,2},{1... | collective-permute-start | bytes 393224 | tf_op jit(solution)/shard_map/ppermute | solution.py:135
  35.8 1.2 collective-permute-done.6.refs_0_.refs_2_
  37.9 1.5 %collective-permute-start.9 = (bf16[64,1024]{1,0:T(8,128)(2,1)S(1)}, bf16[64,1024]{1,0:T(8,128)(2,1)S(1)}, u32[]{:S(2)}, u32[]{:S(2)}) collective-permute-start(bf16[64,1024]{1,0:T(8,128)(2,1)S(1)} %get-tuple-element.451), channel_id=1, source_target_pairs={{0,2},{1,3},{2,0},{3,1},{4,6},{5,7},{6,4},{7,5},{8,10},{9,11},{10,... | collective-permute-start | bytes 393224 | tf_op jit(solution)/shard_map/ppermute | solution.py:135
  39.6 0.9 shard_map.45
  41.4 2.6 %collective-permute-start.14 = (bf16[64,1024]{1,0:T(8,128)(2,1)S(1)}, bf16[64,1024]{1,0:T(8,128)(2,1)S(1)}, u32[]{:S(2)}, u32[]{:S(2)}) collective-permute-start(bf16[64,1024]{1,0:T(8,128)(2,1)S(1)} %get-tuple-element.449), channel_id=1, source_target_pairs={{0,8},{4,12},{8,0},{12,4},{1,9},{5,13},{9,1},{13,5},{2,10},{6,14},... | collective-permute-start | bytes 393224 | tf_op jit(solution)/shard_map/ppermute | solution.py:135
  46.4 3.3 %collective-permute-done.14 = bf16[64,1024]{1,0:T(8,128)(2,1)S(1)} collective-permute-done((bf16[64,1024]{1,0:T(8,128)(2,1)S(1)}, bf16[64,1024]{1,0:T(8,128)(2,1)S(1)}, u32[]{:S(2)}, u32[]{:S(2)}) %collective-permute-start.14) | collective-permute-done | bytes 131104 | tf_op jit(solution)/shard_map/ppermute | solution.py:135
  50.6 1.8 %collective-permute-done.13 = bf16[64,1024]{1,0:T(8,128)(2,1)S(1)} collective-permute-done((bf16[64,1024]{1,0:T(8,128)(2,1)S(1)}, bf16[64,1024]{1,0:T(8,128)(2,1)S(1)}, u32[]{:S(2)}, u32[]{:S(2)}) %collective-permute-start.13) | collective-permute-done | bytes 131104 | tf_op jit(solution)/shard_map/ppermute | solution.py:135
  52.5 1.5 %collective-permute-start.15 = (bf16[64,1024]{1,0:T(8,128)(2,1)S(1)}, bf16[64,1024]{1,0:T(8,128)(2,1)S(1)}, u32[]{:S(2)}, u32[]{:S(2)}) collective-permute-start(bf16[64,1024]{1,0:T(8,128)(2,1)S(1)} %get-tuple-element.447), channel_id=1, source_target_pairs={{0,8},{4,12},{8,0},{12,4},{1,9},{5,13},{9,1},{13,5},{2,10},{6,14},... | collective-permute-start | bytes 393224 | tf_op jit(solution)/shard_map/ppermute | solution.py:135
  54.0 1.2 collective-permute-done.16.refs_0_
  56.8 0.9 shard_map.51.refs_4_
  57.9 1.8 %slice_bitcast_fusion.7.block = bf16[1024,1024]{1,0:T(8,128)(2,1)S(1)} fusion(bf16[5,1024,1024]{2,1,0:T(8,128)(2,1)} %param.4), kind=kLoop, calls=%fused_computation.7 | loop fusion | bytes 4194304 | tf_op jit(solution)/shard_map/squeeze | solution.py:128
  59.6 2.0 %collective-permute-done.15 = bf16[64,1024]{1,0:T(8,128)(2,1)S(1)} collective-permute-done((bf16[64,1024]{1,0:T(8,128)(2,1)S(1)}, bf16[64,1024]{1,0:T(8,128)(2,1)S(1)}, u32[]{:S(2)}, u32[]{:S(2)}) %collective-permute-start.15) | collective-permute-done | bytes 131104 | tf_op jit(solution)/shard_map/ppermute | solution.py:135
  61.8 0.8 shard_map.52
  64.0 2.1 %collective-permute-start.23 = (bf16[64,1024]{1,0:T(8,128)(2,1)S(1)}, bf16[64,1024]{1,0:T(8,128)(2,1)S(1)}, u32[]{:S(2)}, u32[]{:S(2)}) collective-permute-start(bf16[64,1024]{1,0:T(8,128)(2,1)S(1)} %shard_map.53), channel_id=1, source_target_pairs={{0,4},{4,0},{8,12},{12,8},{1,5},{5,1},{9,13},{13,9},{2,6},{6,2},{1... | collective-permute-start | bytes 393224 | tf_op jit(solution)/shard_map/ppermute | solution.py:135
  66.1 1.0 collective-permute-done.18.refs_0_.refs_2_
  68.6 0.9 shard_map.55
  69.5 1.0 shard_map.56
  70.5 1.8 %collective-permute-start.26 = (bf16[64,1024]{1,0:T(8,128)(2,1)S(1)}, bf16[64,1024]{1,0:T(8,128)(2,1)S(1)}, u32[]{:S(2)}, u32[]{:S(2)}) collective-permute-start(bf16[64,1024]{1,0:T(8,128)(2,1)S(1)} %get-tuple-element.441), channel_id=1, source_target_pairs={{0,8},{4,12},{8,0},{12,4},{1,9},{5,13},{9,1},{13,5},{2,10},{6,14},... | collective-permute-start | bytes 393224 | tf_op jit(solution)/shard_map/ppermute | solution.py:135
  73.9 0.9 collective-permute-start.25
  75.6 3.2 %collective-permute-done.26 = bf16[64,1024]{1,0:T(8,128)(2,1)S(1)} collective-permute-done((bf16[64,1024]{1,0:T(8,128)(2,1)S(1)}, bf16[64,1024]{1,0:T(8,128)(2,1)S(1)}, u32[]{:S(2)}, u32[]{:S(2)}) %collective-permute-start.26) | collective-permute-done | bytes 131104 | tf_op jit(solution)/shard_map/ppermute | solution.py:135
  78.9 0.8 shard_map.59
  79.7 1.8 %collective-permute-done.25 = bf16[64,1024]{1,0:T(8,128)(2,1)S(1)} collective-permute-done((bf16[64,1024]{1,0:T(8,128)(2,1)S(1)}, bf16[64,1024]{1,0:T(8,128)(2,1)S(1)}, u32[]{:S(2)}, u32[]{:S(2)}) %collective-permute-start.25) | collective-permute-done | bytes 131104 | tf_op jit(solution)/shard_map/ppermute | solution.py:135
  81.5 1.3 collective-permute-start.27
  82.8 1.5 collective-permute-done.28.refs_0_
  84.3 0.8 shard_map.60
  85.1 1.3 collective-permute-start.31
  86.6 0.9 shard_map.61.refs_4_
  87.6 0.9 shard_map.62.refs_4_
  88.7 1.8 %slice_bitcast_fusion.2.block = bf16[1024,1024]{1,0:T(8,128)(2,1)S(1)} fusion(bf16[5,1024,1024]{2,1,0:T(8,128)(2,1)} %param.4), kind=kLoop, calls=%fused_computation.2 | loop fusion | bytes 4194304 | tf_op jit(solution)/shard_map/squeeze | solution.py:128
  93.1 2.1 %collective-permute-start.35 = (bf16[64,1024]{1,0:T(8,128)(2,1)S(1)}, bf16[64,1024]{1,0:T(8,128)(2,1)S(1)}, u32[]{:S(2)}, u32[]{:S(2)}) collective-permute-start(bf16[64,1024]{1,0:T(8,128)(2,1)S(1)} %shard_map.64), channel_id=1, source_target_pairs={{0,4},{4,0},{8,12},{12,8},{1,5},{5,1},{9,13},{13,9},{2,6},{6,2},{1... | collective-permute-start | bytes 393224 | tf_op jit(solution)/shard_map/ppermute | solution.py:135
  95.1 1.0 collective-permute-done.30.refs_0_.refs_2_
  97.0 0.9 collective-permute-start.33
  98.0 0.9 shard_map.66
  99.8 1.5 collective-permute-start.38
  101.2 0.8 collective-permute-done.33
  104.3 3.6 %collective-permute-done.38 = bf16[64,1024]{1,0:T(8,128)(2,1)S(1)} collective-permute-done((bf16[64,1024]{1,0:T(8,128)(2,1)S(1)}, bf16[64,1024]{1,0:T(8,128)(2,1)S(1)}, u32[]{:S(2)}, u32[]{:S(2)}) %collective-permute-start.38) | collective-permute-done | bytes 131104 | tf_op jit(solution)/shard_map/ppermute | solution.py:135
  108.0 0.8 shard_map.70
  108.8 1.8 %collective-permute-done.37 = bf16[64,1024]{1,0:T(8,128)(2,1)S(1)} collective-permute-done((bf16[64,1024]{1,0:T(8,128)(2,1)S(1)}, bf16[64,1024]{1,0:T(8,128)(2,1)S(1)}, u32[]{:S(2)}, u32[]{:S(2)}) %collective-permute-start.37) | collective-permute-done | bytes 131104 | tf_op jit(solution)/shard_map/ppermute | solution.py:135
  111.3 2.1 %collective-permute-done.40.refs_0_ = bf16[64,1024]{1,0:T(8,128)(2,1)S(1)} collective-permute-done((bf16[64,1024]{1,0:T(8,128)(2,1)S(1)}, bf16[64,1024]{1,0:T(8,128)(2,1)S(1)}, u32[]{:S(2)}, u32[]{:S(2)}) %collective-permute-start.40) | collective-permute-done | bytes 131104 | tf_op jit(solution)/shard_map/ppermute | solution.py:135
  114.2 1.1 collective-permute-start.42
  115.3 1.8 %slice_bitcast_fusion.block = bf16[1024,1024]{1,0:T(8,128)(2,1)S(1)} fusion(bf16[5,1024,1024]{2,1,0:T(8,128)(2,1)} %param.4), kind=kLoop, calls=%fused_computation | loop fusion | bytes 4194304 | tf_op jit(solution)/shard_map/squeeze | solution.py:128
  117.0 2.2 %collective-permute-done.42 = bf16[64,1024]{1,0:T(8,128)(2,1)S(1)} collective-permute-done((bf16[64,1024]{1,0:T(8,128)(2,1)S(1)}, bf16[64,1024]{1,0:T(8,128)(2,1)S(1)}, u32[]{:S(2)}, u32[]{:S(2)}) %collective-permute-start.42) | collective-permute-done | bytes 131104 | tf_op jit(solution)/shard_map/ppermute | solution.py:135
  121.5 3.8 %collective-permute-done.43.refs_0_ = bf16[64,1024]{1,0:T(8,128)(2,1)S(1)} collective-permute-done((bf16[64,1024]{1,0:T(8,128)(2,1)S(1)}, bf16[64,1024]{1,0:T(8,128)(2,1)S(1)}, u32[]{:S(2)}, u32[]{:S(2)}) %collective-permute-start.43) | collective-permute-done | bytes 131104 | tf_op jit(solution)/shard_map/ppermute | solution.py:135
  125.2 1.0 shard_map.73
  128.8 2.6 %collective-permute-done.47 = bf16[64,1024]{1,0:T(8,128)(2,1)S(1)} collective-permute-done((bf16[64,1024]{1,0:T(8,128)(2,1)S(1)}, bf16[64,1024]{1,0:T(8,128)(2,1)S(1)}, u32[]{:S(2)}, u32[]{:S(2)}) %collective-permute-start.47) | collective-permute-done | bytes 131104 | tf_op jit(solution)/shard_map/ppermute | solution.py:135
  131.5 1.2 collective-permute-done.46
  134.8 4.4 %collective-permute-done.49 = bf16[64,1024]{1,0:T(8,128)(2,1)S(1)} collective-permute-done((bf16[64,1024]{1,0:T(8,128)(2,1)S(1)}, bf16[64,1024]{1,0:T(8,128)(2,1)S(1)}, u32[]{:S(2)}, u32[]{:S(2)}) %collective-permute-start.49) | collective-permute-done | bytes 131104 | tf_op jit(solution)/shard_map/ppermute | solution.py:135
  139.4 8.1 %collective-permute-done.50 = bf16[64,1024]{1,0:T(8,128)(2,1)S(1)} collective-permute-done((bf16[64,1024]{1,0:T(8,128)(2,1)S(1)}, bf16[64,1024]{1,0:T(8,128)(2,1)S(1)}, u32[]{:S(2)}, u32[]{:S(2)}) %collective-permute-start.50) | collective-permute-done | bytes 131104 | tf_op jit(solution)/shard_map/ppermute | solution.py:135
  (147 shorter events, 33.6 us)
Async XLA Ops:
  3.7 7.0 %collective-permute-start.1 = (bf16[64,1024]{1,0:T(8,128)(2,1)S(1)}, bf16[64,1024]{1,0:T(8,128)(2,1)S(1)}, u32[]{:S(2)}, u32[]{:S(2)}) collective-permute-start(bf16[64,1024]{1,0:T(8,128)(2,1)S(1)} %get-tuple-element.224), channel_id=1, source_target_pairs={{0,4},{4,0},{8,12},{12,8},{1,5},{5,1},{9,13},{13,9},{2,6},{6,2},{1... | collective-permute-start | bytes 393224 | tf_op jit(solution)/shard_map/ppermute | solution.py:135
  7.7 13.4 %collective-permute-start = (bf16[64,1024]{1,0:T(8,128)(2,1)S(1)}, bf16[64,1024]{1,0:T(8,128)(2,1)S(1)}, u32[]{:S(2)}, u32[]{:S(2)}) collective-permute-start(bf16[64,1024]{1,0:T(8,128)(2,1)S(1)} %get-tuple-element.223), channel_id=1, source_target_pairs={{0,4},{4,0},{8,12},{12,8},{1,5},{5,1},{9,13},{13,9},{2,6},{6,2},{1... | collective-permute-start | bytes 393224 | tf_op jit(solution)/shard_map/ppermute | solution.py:135
  7.7 1.7 %copy-start = (bf16[5,1024,256]{2,1,0:T(8,128)(2,1)S(1)}, bf16[5,1024,256]{2,1,0:T(8,128)(2,1)}, u32[]{:S(2)}) copy-start(bf16[5,1024,256]{2,1,0:T(8,128)(2,1)} %sides) | copy-start | bytes 7864324
  10.7 8.6 %collective-permute-start.2 = (bf16[64,1024]{1,0:T(8,128)(2,1)S(1)}, bf16[64,1024]{1,0:T(8,128)(2,1)S(1)}, u32[]{:S(2)}, u32[]{:S(2)}) collective-permute-start(bf16[64,1024]{1,0:T(8,128)(2,1)S(1)} %get-tuple-element.457), channel_id=1, source_target_pairs={{0,8},{4,12},{8,0},{12,4},{1,9},{5,13},{9,1},{13,5},{2,10},{6,14},... | collective-permute-start | bytes 393224 | tf_op jit(solution)/shard_map/ppermute | solution.py:135
  19.4 5.1 %collective-permute-start.4 = (bf16[64,1024]{1,0:T(8,128)(2,1)S(1)}, bf16[64,1024]{1,0:T(8,128)(2,1)S(1)}, u32[]{:S(2)}, u32[]{:S(2)}) collective-permute-start(bf16[64,1024]{1,0:T(8,128)(2,1)S(1)} %add_convert_fusion.8.refs_0_.refs_1_), channel_id=1, source_target_pairs={{0,4},{4,0},{8,12},{12,8},{1,5},{5,1},{9,13},{13,9},{2,6},{6,2},{1... | collective-permute-start | bytes 393224 | tf_op jit(solution)/shard_map/ppermute | solution.py:135
  20.9 4.4 %collective-permute-start.5 = (bf16[64,1024]{1,0:T(8,128)(2,1)S(1)}, bf16[64,1024]{1,0:T(8,128)(2,1)S(1)}, u32[]{:S(2)}, u32[]{:S(2)}) collective-permute-start(bf16[64,1024]{1,0:T(8,128)(2,1)S(1)} %shard_map.40), channel_id=1, source_target_pairs={{0,1},{1,0},{2,3},{3,2},{4,5},{5,4},{6,7},{7,6},{8,9},{9,8},{10,11... | collective-permute-start | bytes 393224 | tf_op jit(solution)/shard_map/ppermute | solution.py:135
  21.0 18.4 %copy-start.1 = (bf16[10,1024,1024]{2,1,0:T(8,128)(2,1)S(1)}, bf16[10,1024,1024]{2,1,0:T(8,128)(2,1)}, u32[]{:S(2)}) copy-start(bf16[10,1024,1024]{2,1,0:T(8,128)(2,1)} %param.3) | copy-start | bytes 62914564
  21.1 10.4 %collective-permute-start.3 = (bf16[64,1024]{1,0:T(8,128)(2,1)S(1)}, bf16[64,1024]{1,0:T(8,128)(2,1)S(1)}, u32[]{:S(2)}, u32[]{:S(2)}) collective-permute-start(bf16[64,1024]{1,0:T(8,128)(2,1)S(1)} %get-tuple-element.455), channel_id=1, source_target_pairs={{0,8},{4,12},{8,0},{12,4},{1,9},{5,13},{9,1},{13,5},{2,10},{6,14},... | collective-permute-start | bytes 393224 | tf_op jit(solution)/shard_map/ppermute | solution.py:135
  25.3 7.4 %collective-permute-start.7 = (bf16[64,1024]{1,0:T(8,128)(2,1)S(1)}, bf16[64,1024]{1,0:T(8,128)(2,1)S(1)}, u32[]{:S(2)}, u32[]{:S(2)}) collective-permute-start(bf16[64,1024]{1,0:T(8,128)(2,1)S(1)} %get-tuple-element.453), channel_id=1, source_target_pairs={{0,2},{1,3},{2,0},{3,1},{4,6},{5,7},{6,4},{7,5},{8,10},{9,11},{10,... | collective-permute-start | bytes 393224 | tf_op jit(solution)/shard_map/ppermute | solution.py:135
  31.5 5.5 %collective-permute-start.6 = (bf16[64,1024]{1,0:T(8,128)(2,1)S(1)}, bf16[64,1024]{1,0:T(8,128)(2,1)S(1)}, u32[]{:S(2)}, u32[]{:S(2)}) collective-permute-start(bf16[64,1024]{1,0:T(8,128)(2,1)S(1)} %add_convert_fusion.7.refs_0_.refs_3_), channel_id=1, source_target_pairs={{0,4},{4,0},{8,12},{12,8},{1,5},{5,1},{9,13},{13,9},{2,6},{6,2},{1... | collective-permute-start | bytes 393224 | tf_op jit(solution)/shard_map/ppermute | solution.py:135
  32.7 5.1 %collective-permute-start.8 = (bf16[64,1024]{1,0:T(8,128)(2,1)S(1)}, bf16[64,1024]{1,0:T(8,128)(2,1)S(1)}, u32[]{:S(2)}, u32[]{:S(2)}) collective-permute-start(bf16[64,1024]{1,0:T(8,128)(2,1)S(1)} %shard_map.42), channel_id=1, source_target_pairs={{0,1},{1,0},{2,3},{3,2},{4,5},{5,4},{6,7},{7,6},{8,9},{9,8},{10,11... | collective-permute-start | bytes 393224 | tf_op jit(solution)/shard_map/ppermute | solution.py:135
  32.8 7.7 %collective-permute-start.10 = (bf16[64,1024]{1,0:T(8,128)(2,1)S(1)}, bf16[64,1024]{1,0:T(8,128)(2,1)S(1)}, u32[]{:S(2)}, u32[]{:S(2)}) collective-permute-start(bf16[64,1024]{1,0:T(8,128)(2,1)S(1)} %subtract_convert_fusion.7.refs_0_), channel_id=1, source_target_pairs={{0,1},{1,0},{2,3},{3,2},{4,5},{5,4},{6,7},{7,6},{8,9},{9,8},{10,11... | collective-permute-start | bytes 393224 | tf_op jit(solution)/shard_map/ppermute | solution.py:135
  34.1 7.2 %collective-permute-start.11 = (bf16[64,1024]{1,0:T(8,128)(2,1)S(1)}, bf16[64,1024]{1,0:T(8,128)(2,1)S(1)}, u32[]{:S(2)}, u32[]{:S(2)}) collective-permute-start(bf16[64,1024]{1,0:T(8,128)(2,1)S(1)} %shard_map.43), channel_id=1, source_target_pairs={{0,4},{4,0},{8,12},{12,8},{1,5},{5,1},{9,13},{13,9},{2,6},{6,2},{1... | collective-permute-start | bytes 393224 | tf_op jit(solution)/shard_map/ppermute | solution.py:135
  37.9 6.1 %collective-permute-start.9 = (bf16[64,1024]{1,0:T(8,128)(2,1)S(1)}, bf16[64,1024]{1,0:T(8,128)(2,1)S(1)}, u32[]{:S(2)}, u32[]{:S(2)}) collective-permute-start(bf16[64,1024]{1,0:T(8,128)(2,1)S(1)} %get-tuple-element.451), channel_id=1, source_target_pairs={{0,2},{1,3},{2,0},{3,1},{4,6},{5,7},{6,4},{7,5},{8,10},{9,11},{10,... | collective-permute-start | bytes 393224 | tf_op jit(solution)/shard_map/ppermute | solution.py:135
  41.4 8.3 %collective-permute-start.14 = (bf16[64,1024]{1,0:T(8,128)(2,1)S(1)}, bf16[64,1024]{1,0:T(8,128)(2,1)S(1)}, u32[]{:S(2)}, u32[]{:S(2)}) collective-permute-start(bf16[64,1024]{1,0:T(8,128)(2,1)S(1)} %get-tuple-element.449), channel_id=1, source_target_pairs={{0,8},{4,12},{8,0},{12,4},{1,9},{5,13},{9,1},{13,5},{2,10},{6,14},... | collective-permute-start | bytes 393224 | tf_op jit(solution)/shard_map/ppermute | solution.py:135
  44.0 1.6 %collective-permute-start.12 = (bf16[64,1024]{1,0:T(8,128)(2,1)S(1)}, bf16[64,1024]{1,0:T(8,128)(2,1)S(1)}, u32[]{:S(2)}, u32[]{:S(2)}) collective-permute-start(bf16[64,1024]{1,0:T(8,128)(2,1)S(1)} %subtract_convert_fusion.6.refs_0_), channel_id=1, source_target_pairs={{0,1},{1,0},{2,3},{3,2},{4,5},{5,4},{6,7},{7,6},{8,9},{9,8},{10,11... | collective-permute-start | bytes 393224 | tf_op jit(solution)/shard_map/ppermute | solution.py:135
  44.9 7.6 %collective-permute-start.13 = (bf16[64,1024]{1,0:T(8,128)(2,1)S(1)}, bf16[64,1024]{1,0:T(8,128)(2,1)S(1)}, u32[]{:S(2)}, u32[]{:S(2)}) collective-permute-start(bf16[64,1024]{1,0:T(8,128)(2,1)S(1)} %shard_map.47), channel_id=1, source_target_pairs={{0,4},{4,0},{8,12},{12,8},{1,5},{5,1},{9,13},{13,9},{2,6},{6,2},{1... | collective-permute-start | bytes 393224 | tf_op jit(solution)/shard_map/ppermute | solution.py:135
  49.7 5.5 %collective-permute-start.16 = (bf16[64,1024]{1,0:T(8,128)(2,1)S(1)}, bf16[64,1024]{1,0:T(8,128)(2,1)S(1)}, u32[]{:S(2)}, u32[]{:S(2)}) collective-permute-start(bf16[64,1024]{1,0:T(8,128)(2,1)S(1)} %add_convert_fusion.6.refs_0_.refs_1_), channel_id=1, source_target_pairs={{0,4},{4,0},{8,12},{12,8},{1,5},{5,1},{9,13},{13,9},{2,6},{6,2},{1... | collective-permute-start | bytes 393224 | tf_op jit(solution)/shard_map/ppermute | solution.py:135
  50.6 5.4 %collective-permute-start.17 = (bf16[64,1024]{1,0:T(8,128)(2,1)S(1)}, bf16[64,1024]{1,0:T(8,128)(2,1)S(1)}, u32[]{:S(2)}, u32[]{:S(2)}) collective-permute-start(bf16[64,1024]{1,0:T(8,128)(2,1)S(1)} %shard_map.49), channel_id=1, source_target_pairs={{0,1},{1,0},{2,3},{3,2},{4,5},{5,4},{6,7},{7,6},{8,9},{9,8},{10,11... | collective-permute-start | bytes 393224 | tf_op jit(solution)/shard_map/ppermute | solution.py:135
  52.5 9.2 %collective-permute-start.15 = (bf16[64,1024]{1,0:T(8,128)(2,1)S(1)}, bf16[64,1024]{1,0:T(8,128)(2,1)S(1)}, u32[]{:S(2)}, u32[]{:S(2)}) collective-permute-start(bf16[64,1024]{1,0:T(8,128)(2,1)S(1)} %get-tuple-element.447), channel_id=1, source_target_pairs={{0,8},{4,12},{8,0},{12,4},{1,9},{5,13},{9,1},{13,5},{2,10},{6,14},... | collective-permute-start | bytes 393224 | tf_op jit(solution)/shard_map/ppermute | solution.py:135
  56.0 6.6 %collective-permute-start.19 = (bf16[64,1024]{1,0:T(8,128)(2,1)S(1)}, bf16[64,1024]{1,0:T(8,128)(2,1)S(1)}, u32[]{:S(2)}, u32[]{:S(2)}) collective-permute-start(bf16[64,1024]{1,0:T(8,128)(2,1)S(1)} %get-tuple-element.445), channel_id=1, source_target_pairs={{0,2},{1,3},{2,0},{3,1},{4,6},{5,7},{6,4},{7,5},{8,10},{9,11},{10,... | collective-permute-start | bytes 393224 | tf_op jit(solution)/shard_map/ppermute | solution.py:135
  61.7 5.4 %collective-permute-start.18 = (bf16[64,1024]{1,0:T(8,128)(2,1)S(1)}, bf16[64,1024]{1,0:T(8,128)(2,1)S(1)}, u32[]{:S(2)}, u32[]{:S(2)}) collective-permute-start(bf16[64,1024]{1,0:T(8,128)(2,1)S(1)} %add_convert_fusion.5.refs_0_.refs_3_), channel_id=1, source_target_pairs={{0,4},{4,0},{8,12},{12,8},{1,5},{5,1},{9,13},{13,9},{2,6},{6,2},{1... | collective-permute-start | bytes 393224 | tf_op jit(solution)/shard_map/ppermute | solution.py:135
  62.6 5.3 %collective-permute-start.20 = (bf16[64,1024]{1,0:T(8,128)(2,1)S(1)}, bf16[64,1024]{1,0:T(8,128)(2,1)S(1)}, u32[]{:S(2)}, u32[]{:S(2)}) collective-permute-start(bf16[64,1024]{1,0:T(8,128)(2,1)S(1)} %shard_map.52), channel_id=1, source_target_pairs={{0,1},{1,0},{2,3},{3,2},{4,5},{5,4},{6,7},{7,6},{8,9},{9,8},{10,11... | collective-permute-start | bytes 393224 | tf_op jit(solution)/shard_map/ppermute | solution.py:135
  62.7 6.8 %collective-permute-start.22 = (bf16[64,1024]{1,0:T(8,128)(2,1)S(1)}, bf16[64,1024]{1,0:T(8,128)(2,1)S(1)}, u32[]{:S(2)}, u32[]{:S(2)}) collective-permute-start(bf16[64,1024]{1,0:T(8,128)(2,1)S(1)} %subtract_convert_fusion.5.refs_0_), channel_id=1, source_target_pairs={{0,1},{1,0},{2,3},{3,2},{4,5},{5,4},{6,7},{7,6},{8,9},{9,8},{10,11... | collective-permute-start | bytes 393224 | tf_op jit(solution)/shard_map/ppermute | solution.py:135
  64.0 6.5 %collective-permute-start.23 = (bf16[64,1024]{1,0:T(8,128)(2,1)S(1)}, bf16[64,1024]{1,0:T(8,128)(2,1)S(1)}, u32[]{:S(2)}, u32[]{:S(2)}) collective-permute-start(bf16[64,1024]{1,0:T(8,128)(2,1)S(1)} %shard_map.53), channel_id=1, source_target_pairs={{0,4},{4,0},{8,12},{12,8},{1,5},{5,1},{9,13},{13,9},{2,6},{6,2},{1... | collective-permute-start | bytes 393224 | tf_op jit(solution)/shard_map/ppermute | solution.py:135
  67.9 5.0 %collective-permute-start.21 = (bf16[64,1024]{1,0:T(8,128)(2,1)S(1)}, bf16[64,1024]{1,0:T(8,128)(2,1)S(1)}, u32[]{:S(2)}, u32[]{:S(2)}) collective-permute-start(bf16[64,1024]{1,0:T(8,128)(2,1)S(1)} %get-tuple-element.443), channel_id=1, source_target_pairs={{0,2},{1,3},{2,0},{3,1},{4,6},{5,7},{6,4},{7,5},{8,10},{9,11},{10,... | collective-permute-start | bytes 393224 | tf_op jit(solution)/shard_map/ppermute | solution.py:135
  70.5 8.2 %collective-permute-start.26 = (bf16[64,1024]{1,0:T(8,128)(2,1)S(1)}, bf16[64,1024]{1,0:T(8,128)(2,1)S(1)}, u32[]{:S(2)}, u32[]{:S(2)}) collective-permute-start(bf16[64,1024]{1,0:T(8,128)(2,1)S(1)} %get-tuple-element.441), channel_id=1, source_target_pairs={{0,8},{4,12},{8,0},{12,4},{1,9},{5,13},{9,1},{13,5},{2,10},{6,14},... | collective-permute-start | bytes 393224 | tf_op jit(solution)/shard_map/ppermute | solution.py:135
  73.0 1.8 %collective-permute-start.24 = (bf16[64,1024]{1,0:T(8,128)(2,1)S(1)}, bf16[64,1024]{1,0:T(8,128)(2,1)S(1)}, u32[]{:S(2)}, u32[]{:S(2)}) collective-permute-start(bf16[64,1024]{1,0:T(8,128)(2,1)S(1)} %subtract_convert_fusion.4.refs_0_), channel_id=1, source_target_pairs={{0,1},{1,0},{2,3},{3,2},{4,5},{5,4},{6,7},{7,6},{8,9},{9,8},{10,11... | collective-permute-start | bytes 393224 | tf_op jit(solution)/shard_map/ppermute | solution.py:135
  73.9 7.6 %collective-permute-start.25 = (bf16[64,1024]{1,0:T(8,128)(2,1)S(1)}, bf16[64,1024]{1,0:T(8,128)(2,1)S(1)}, u32[]{:S(2)}, u32[]{:S(2)}) collective-permute-start(bf16[64,1024]{1,0:T(8,128)(2,1)S(1)} %shard_map.57), channel_id=1, source_target_pairs={{0,4},{4,0},{8,12},{12,8},{1,5},{5,1},{9,13},{13,9},{2,6},{6,2},{1... | collective-permute-start | bytes 393224 | tf_op jit(solution)/shard_map/ppermute | solution.py:135
  78.8 5.5 %collective-permute-start.28 = (bf16[64,1024]{1,0:T(8,128)(2,1)S(1)}, bf16[64,1024]{1,0:T(8,128)(2,1)S(1)}, u32[]{:S(2)}, u32[]{:S(2)}) collective-permute-start(bf16[64,1024]{1,0:T(8,128)(2,1)S(1)} %add_convert_fusion.4.refs_0_.refs_1_), channel_id=1, source_target_pairs={{0,4},{4,0},{8,12},{12,8},{1,5},{5,1},{9,13},{13,9},{2,6},{6,2},{1... | collective-permute-start | bytes 393224 | tf_op jit(solution)/shard_map/ppermute | solution.py:135
  79.7 5.4 %collective-permute-start.29 = (bf16[64,1024]{1,0:T(8,128)(2,1)S(1)}, bf16[64,1024]{1,0:T(8,128)(2,1)S(1)}, u32[]{:S(2)}, u32[]{:S(2)}) collective-permute-start(bf16[64,1024]{1,0:T(8,128)(2,1)S(1)} %shard_map.59), channel_id=1, source_target_pairs={{0,1},{1,0},{2,3},{3,2},{4,5},{5,4},{6,7},{7,6},{8,9},{9,8},{10,11... | collective-permute-start | bytes 393224 | tf_op jit(solution)/shard_map/ppermute | solution.py:135
  81.5 9.2 %collective-permute-start.27 = (bf16[64,1024]{1,0:T(8,128)(2,1)S(1)}, bf16[64,1024]{1,0:T(8,128)(2,1)S(1)}, u32[]{:S(2)}, u32[]{:S(2)}) collective-permute-start(bf16[64,1024]{1,0:T(8,128)(2,1)S(1)} %get-tuple-element.439), channel_id=1, source_target_pairs={{0,8},{4,12},{8,0},{12,4},{1,9},{5,13},{9,1},{13,5},{2,10},{6,14},... | collective-permute-start | bytes 393224 | tf_op jit(solution)/shard_map/ppermute | solution.py:135
  85.1 6.6 %collective-permute-start.31 = (bf16[64,1024]{1,0:T(8,128)(2,1)S(1)}, bf16[64,1024]{1,0:T(8,128)(2,1)S(1)}, u32[]{:S(2)}, u32[]{:S(2)}) collective-permute-start(bf16[64,1024]{1,0:T(8,128)(2,1)S(1)} %get-tuple-element.437), channel_id=1, source_target_pairs={{0,2},{1,3},{2,0},{3,1},{4,6},{5,7},{6,4},{7,5},{8,10},{9,11},{10,... | collective-permute-start | bytes 393224 | tf_op jit(solution)/shard_map/ppermute | solution.py:135
  90.8 5.4 %collective-permute-start.30 = (bf16[64,1024]{1,0:T(8,128)(2,1)S(1)}, bf16[64,1024]{1,0:T(8,128)(2,1)S(1)}, u32[]{:S(2)}, u32[]{:S(2)}) collective-permute-start(bf16[64,1024]{1,0:T(8,128)(2,1)S(1)} %add_convert_fusion.3.refs_0_.refs_3_), channel_id=1, source_target_pairs={{0,4},{4,0},{8,12},{12,8},{1,5},{5,1},{9,13},{13,9},{2,6},{6,2},{1... | collective-permute-start | bytes 393224 | tf_op jit(solution)/shard_map/ppermute | solution.py:135
  91.6 5.3 %collective-permute-start.32 = (bf16[64,1024]{1,0:T(8,128)(2,1)S(1)}, bf16[64,1024]{1,0:T(8,128)(2,1)S(1)}, u32[]{:S(2)}, u32[]{:S(2)}) collective-permute-start(bf16[64,1024]{1,0:T(8,128)(2,1)S(1)} %shard_map.63), channel_id=1, source_target_pairs={{0,1},{1,0},{2,3},{3,2},{4,5},{5,4},{6,7},{7,6},{8,9},{9,8},{10,11... | collective-permute-start | bytes 393224 | tf_op jit(solution)/shard_map/ppermute | solution.py:135
  91.8 7.2 %collective-permute-start.34 = (bf16[64,1024]{1,0:T(8,128)(2,1)S(1)}, bf16[64,1024]{1,0:T(8,128)(2,1)S(1)}, u32[]{:S(2)}, u32[]{:S(2)}) collective-permute-start(bf16[64,1024]{1,0:T(8,128)(2,1)S(1)} %subtract_convert_fusion.3.refs_0_), channel_id=1, source_target_pairs={{0,1},{1,0},{2,3},{3,2},{4,5},{5,4},{6,7},{7,6},{8,9},{9,8},{10,11... | collective-permute-start | bytes 393224 | tf_op jit(solution)/shard_map/ppermute | solution.py:135
  93.1 6.7 %collective-permute-start.35 = (bf16[64,1024]{1,0:T(8,128)(2,1)S(1)}, bf16[64,1024]{1,0:T(8,128)(2,1)S(1)}, u32[]{:S(2)}, u32[]{:S(2)}) collective-permute-start(bf16[64,1024]{1,0:T(8,128)(2,1)S(1)} %shard_map.64), channel_id=1, source_target_pairs={{0,4},{4,0},{8,12},{12,8},{1,5},{5,1},{9,13},{13,9},{2,6},{6,2},{1... | collective-permute-start | bytes 393224 | tf_op jit(solution)/shard_map/ppermute | solution.py:135
  97.0 5.0 %collective-permute-start.33 = (bf16[64,1024]{1,0:T(8,128)(2,1)S(1)}, bf16[64,1024]{1,0:T(8,128)(2,1)S(1)}, u32[]{:S(2)}, u32[]{:S(2)}) collective-permute-start(bf16[64,1024]{1,0:T(8,128)(2,1)S(1)} %get-tuple-element.435), channel_id=1, source_target_pairs={{0,2},{1,3},{2,0},{3,1},{4,6},{5,7},{6,4},{7,5},{8,10},{9,11},{10,... | collective-permute-start | bytes 393224 | tf_op jit(solution)/shard_map/ppermute | solution.py:135
  99.8 8.1 %collective-permute-start.38 = (bf16[64,1024]{1,0:T(8,128)(2,1)S(1)}, bf16[64,1024]{1,0:T(8,128)(2,1)S(1)}, u32[]{:S(2)}, u32[]{:S(2)}) collective-permute-start(bf16[64,1024]{1,0:T(8,128)(2,1)S(1)} %get-tuple-element.433), channel_id=1, source_target_pairs={{0,8},{4,12},{8,0},{12,4},{1,9},{5,13},{9,1},{13,5},{2,10},{6,14},... | collective-permute-start | bytes 393224 | tf_op jit(solution)/shard_map/ppermute | solution.py:135
  102.1 1.4 collective-permute-start.36
  103.0 7.6 %collective-permute-start.37 = (bf16[64,1024]{1,0:T(8,128)(2,1)S(1)}, bf16[64,1024]{1,0:T(8,128)(2,1)S(1)}, u32[]{:S(2)}, u32[]{:S(2)}) collective-permute-start(bf16[64,1024]{1,0:T(8,128)(2,1)S(1)} %shard_map.68), channel_id=1, source_target_pairs={{0,4},{4,0},{8,12},{12,8},{1,5},{5,1},{9,13},{13,9},{2,6},{6,2},{1... | collective-permute-start | bytes 393224 | tf_op jit(solution)/shard_map/ppermute | solution.py:135
  107.9 5.5 %collective-permute-start.40 = (bf16[64,1024]{1,0:T(8,128)(2,1)S(1)}, bf16[64,1024]{1,0:T(8,128)(2,1)S(1)}, u32[]{:S(2)}, u32[]{:S(2)}) collective-permute-start(bf16[64,1024]{1,0:T(8,128)(2,1)S(1)} %add_convert_fusion.2.refs_0_), channel_id=1, source_target_pairs={{0,4},{4,0},{8,12},{12,8},{1,5},{5,1},{9,13},{13,9},{2,6},{6,2},{1... | collective-permute-start | bytes 393224 | tf_op jit(solution)/shard_map/ppermute | solution.py:135
  108.8 5.4 %collective-permute-start.41 = (bf16[64,1024]{1,0:T(8,128)(2,1)S(1)}, bf16[64,1024]{1,0:T(8,128)(2,1)S(1)}, u32[]{:S(2)}, u32[]{:S(2)}) collective-permute-start(bf16[64,1024]{1,0:T(8,128)(2,1)S(1)} %shard_map.70), channel_id=1, source_target_pairs={{0,1},{1,0},{2,3},{3,2},{4,5},{5,4},{6,7},{7,6},{8,9},{9,8},{10,11... | collective-permute-start | bytes 393224 | tf_op jit(solution)/shard_map/ppermute | solution.py:135
  110.6 9.2 %collective-permute-start.39 = (bf16[64,1024]{1,0:T(8,128)(2,1)S(1)}, bf16[64,1024]{1,0:T(8,128)(2,1)S(1)}, u32[]{:S(2)}, u32[]{:S(2)}) collective-permute-start(bf16[64,1024]{1,0:T(8,128)(2,1)S(1)} %get-tuple-element.431), channel_id=1, source_target_pairs={{0,8},{4,12},{8,0},{12,4},{1,9},{5,13},{9,1},{13,5},{2,10},{6,14},... | collective-permute-start | bytes 393224 | tf_op jit(solution)/shard_map/ppermute | solution.py:135
  114.2 5.0 %collective-permute-start.42 = (bf16[64,1024]{1,0:T(8,128)(2,1)S(1)}, bf16[64,1024]{1,0:T(8,128)(2,1)S(1)}, u32[]{:S(2)}, u32[]{:S(2)}) collective-permute-start(bf16[64,1024]{1,0:T(8,128)(2,1)S(1)} %get-tuple-element.429), channel_id=1, source_target_pairs={{0,2},{1,3},{2,0},{3,1},{4,6},{5,7},{6,4},{7,5},{8,10},{9,11},{10,... | collective-permute-start | bytes 393224 | tf_op jit(solution)/shard_map/ppermute | solution.py:135
  119.9 5.3 %collective-permute-start.43 = (bf16[64,1024]{1,0:T(8,128)(2,1)S(1)}, bf16[64,1024]{1,0:T(8,128)(2,1)S(1)}, u32[]{:S(2)}, u32[]{:S(2)}) collective-permute-start(bf16[64,1024]{1,0:T(8,128)(2,1)S(1)} %add_convert_fusion.1.refs_0_), channel_id=1, source_target_pairs={{0,4},{4,0},{8,12},{12,8},{1,5},{5,1},{9,13},{13,9},{2,6},{6,2},{1... | collective-permute-start | bytes 393224 | tf_op jit(solution)/shard_map/ppermute | solution.py:135
  120.7 5.5 %collective-permute-start.45 = (bf16[64,1024]{1,0:T(8,128)(2,1)S(1)}, bf16[64,1024]{1,0:T(8,128)(2,1)S(1)}, u32[]{:S(2)}, u32[]{:S(2)}) collective-permute-start(bf16[64,1024]{1,0:T(8,128)(2,1)S(1)} %shard_map.72), channel_id=1, source_target_pairs={{0,1},{1,0},{2,3},{3,2},{4,5},{5,4},{6,7},{7,6},{8,9},{9,8},{10,11... | collective-permute-start | bytes 393224 | tf_op jit(solution)/shard_map/ppermute | solution.py:135
  120.9 6.0 %collective-permute-start.44 = (bf16[64,1024]{1,0:T(8,128)(2,1)S(1)}, bf16[64,1024]{1,0:T(8,128)(2,1)S(1)}, u32[]{:S(2)}, u32[]{:S(2)}) collective-permute-start(bf16[64,1024]{1,0:T(8,128)(2,1)S(1)} %subtract_convert_fusion.1), channel_id=1, source_target_pairs={{0,1},{1,0},{2,3},{3,2},{4,5},{5,4},{6,7},{7,6},{8,9},{9,8},{10,11... | collective-permute-start | bytes 393224 | tf_op jit(solution)/shard_map/ppermute | solution.py:135
  126.3 5.0 %collective-permute-start.47 = (bf16[64,1024]{1,0:T(8,128)(2,1)S(1)}, bf16[64,1024]{1,0:T(8,128)(2,1)S(1)}, u32[]{:S(2)}, u32[]{:S(2)}) collective-permute-start(bf16[64,1024]{1,0:T(8,128)(2,1)S(1)} %get-tuple-element.427), channel_id=1, source_target_pairs={{0,2},{1,3},{2,0},{3,1},{4,6},{5,7},{6,4},{7,5},{8,10},{9,11},{10,... | collective-permute-start | bytes 393224 | tf_op jit(solution)/shard_map/ppermute | solution.py:135
  127.7 5.0 %collective-permute-start.46 = (bf16[64,1024]{1,0:T(8,128)(2,1)S(1)}, bf16[64,1024]{1,0:T(8,128)(2,1)S(1)}, u32[]{:S(2)}, u32[]{:S(2)}) collective-permute-start(bf16[64,1024]{1,0:T(8,128)(2,1)S(1)} %shard_map.74), channel_id=1, source_target_pairs={{0,4},{4,0},{8,12},{12,8},{1,5},{5,1},{9,13},{13,9},{2,6},{6,2},{1... | collective-permute-start | bytes 393224 | tf_op jit(solution)/shard_map/ppermute | solution.py:135
  131.4 1.4 collective-permute-start.48
  133.6 5.6 %collective-permute-start.49 = (bf16[64,1024]{1,0:T(8,128)(2,1)S(1)}, bf16[64,1024]{1,0:T(8,128)(2,1)S(1)}, u32[]{:S(2)}, u32[]{:S(2)}) collective-permute-start(bf16[64,1024]{1,0:T(8,128)(2,1)S(1)} %shard_map.76), channel_id=1, source_target_pairs={{0,4},{4,0},{8,12},{12,8},{1,5},{5,1},{9,13},{13,9},{2,6},{6,2},{1... | collective-permute-start | bytes 393224 | tf_op jit(solution)/shard_map/ppermute | solution.py:135
  139.3 8.2 %collective-permute-start.50 = (bf16[64,1024]{1,0:T(8,128)(2,1)S(1)}, bf16[64,1024]{1,0:T(8,128)(2,1)S(1)}, u32[]{:S(2)}, u32[]{:S(2)}) collective-permute-start(bf16[64,1024]{1,0:T(8,128)(2,1)S(1)} %broadcast_select_fusion.4), channel_id=1, source_target_pairs={{0,8},{4,12},{8,0},{12,4},{1,9},{5,13},{9,1},{13,5},{2,10},{6,14},... | collective-permute-start | bytes 393224 | tf_op jit(solution)/shard_map/ppermute | solution.py:135
  139.4 8.1 %copy-start.2 = (bf16[5,1024,64]{1,2,0:T(8,128)(2,1)}, bf16[5,1024,64]{1,2,0:T(8,128)(2,1)S(1)}, u32[]{:S(2)}) copy-start(bf16[5,1024,64]{1,2,0:T(8,128)(2,1)S(1)} %bitcast_dynamic-update-slice_fusion) | copy-start | bytes 1966084

commit v12 on v11

--- a/solution.py
+++ b/solution.py
@@ -58,7 +58,10 @@
 
 def first_kernel(s, side, right, block, keep, leave, product):
     width = keep.shape[0]
-    x = right[:, pl.ds(2 * s * width, 2 * width)].T
+    x = right[...].T
+    x = jnp.concatenate(
+        [x[g * width : (g + 1) * width] for g in (s, STREAMS + s)], axis=0
+    )
     product[...] = times_transposed(x, block[...])
     own = pl.multiple_of(side[0] * width, width)
     other = pl.multiple_of((1 - side[0]) * width, width)
@@ -86,7 +89,7 @@
 def turn_kernel(width, side, sides, out, turned):
     turned[...] = sides[0].T
     for s in range(STREAMS):
-        own = pl.multiple_of((2 * s + side[0]) * width, width)
+        own = pl.multiple_of((STREAMS * side[0] + s) * width, width)
         out[0, s] = turned[pl.ds(own, width)]
 
 
@@ -224,7 +227,8 @@
             st = state[s]
             if exact and step == last_step:
                 own, other = st["own"], st["swap"]
-                st["own"], st["swap"] = jnp.where(core == 0, other, own), jnp.where(core == 0, own, other)
+                stays = core == (s ^ (place >> 1))
+                st["own"], st["swap"] = jnp.where(stays, other, own), jnp.where(stays, own, other)
             leaving = order.run(
                 lambda block, x: product(block, [x], kind=jnp.bfloat16), inverses[step], st["own"]
             )
@@ -245,6 +249,11 @@
         def cross(s):
             st = state[s]
             st["flight"] = trade(st["leaving"], "row", 2) if n_row > 2 else None
+
+        def final_cross(s):
+            st = state[s]
+            pairs = [(r ^ (n_row - 1), r) for r in range(n_row) if r % STREAMS == s]
+            st["flight"] = lax.ppermute(st["leaving"], "row", pairs)
 
         def solve(s, step):
             def work(value, *arrived):
@@ -294,6 +303,7 @@
                 inverse_other(0, step)
                 residual(1, step)
                 pair_sum(0)
+                final_cross(0)
                 inverse_own(1, step)
                 inverse_other(1, step)
                 continue
@@ -315,12 +325,11 @@
         outputs = []
         for step in range(steps_total):
             if exact and step == last_step:
-                low = place < n_row // 2
-                leaving = order.run(
-                    lambda a, b: jnp.where(low, b, a), state[0]["leaving"], state[1]["leaving"]
-                )
-                arrived = trade(leaving, "row", 2)
-                found = narrow(jnp.where(low, state[0]["total"], state[1]["total"]) + wide(arrived))
+                final_cross(1)
+                even = (place & 1) == 0
+                found = jnp.where(even, state[0]["total"], state[1]["total"])
+                found = found + wide(jnp.where(even, state[0]["flight"], state[1]["flight"]))
+                found = narrow(found)
                 outputs.append(found.T)
                 continue
             if step == last_step:
@@ -331,7 +340,7 @@
             found = solved[step][0][0]
             for s in range(STREAMS):
                 for u in range(2):
-                    found = jnp.where(unit == 2 * s + (u ^ side), solved[step][s][u], found)
+                    found = jnp.where(unit == STREAMS * (u ^ side) + s, solved[step][s][u], found)
             if not exact:
                 slot = angles // n_row
                 found = lax.dynamic_slice_in_dim(found, (place * slot) % width, slot, 0)

time: 149 us -> 146 us (0.980)
  waiting for transfers between devices: 55.4 us -> 48.7 us
  starting transfers between devices: 40.1 us -> 44.4 us
    ppermute x51 -> x50, waiting for transfers between devices: 55.4 us -> 46.3 us  [trade(): return lax.ppermute(value, axis, [(i, i ^ step) for i in range(size)])]
    ppermute x0 -> x2, starting transfers between devices: none -> 4.53 us  [final_cross(): st['flight'] = lax.ppermute(st['leaving'], 'row', pairs)]
    ppermute x0 -> x2, waiting for transfers between devices: none -> 2.41 us  [final_cross(): st['flight'] = lax.ppermute(st['leaving'], 'row', pairs)]
    ppermute x51 -> x50, starting transfers between devices: 40.1 us -> 39.9 us  [trade(): return lax.ppermute(value, axis, [(i, i ^ step) for i in range(size)])]
  transfers between devices with their start and end apart: 51 -> 52, of which waited for: 28 -> 29; matrix products, arithmetic and copies ran while one was open for 9% -> 9% of each run, Pallas kernels for 21% -> 21%
where the time goes in v12:
time: 146 us
  waiting for transfers between devices  48.7 us (33%)
  starting transfers between devices  44.4 us (30%)
  Pallas kernels  32.5 us (22%)
  local copies, waits for them, and re-layouts  17 us (12%)
  other arithmetic  2.25 us (2%)
    ppermute x50, waiting for transfers between devices, trade(): return lax.ppermute(value, axis, [(i, i ^ step) for i in range(size)])  46.3 us
    ppermute x50, starting transfers between devices, trade(): return lax.ppermute(value, axis, [(i, i ^ step) for i in range(size)])  39.9 us
    pallas_call x38, Pallas kernels, product(): pl.pallas_call(functools.partial(product_kernel, len(units)), out_shape=j...  29.9 us
    squeeze x16, local copies, waits for them, and re-layouts, block(): self.last = lax.optimization_barrier(self.run(lambda v: v[index], blocks))  14.9 us
    ppermute x2, starting transfers between devices, final_cross(): st['flight'] = lax.ppermute(st['leaving'], 'row', pairs)  4.53 us
  transfers between devices with their start and end apart: 52, of which 29 were waited for; matrix products, arithmetic and copies ran while one was open for 9% of the time, Pallas kernels for 21%

profile of v12, /device:TPU:0, one launch (start us, length us, event | category | flops | bytes accessed | tf_op | source)
XLA Modules:
  0.0 145.8 jit_solution(7521153067758577252)
XLA Ops:
  0.0 1.8 %slice_bitcast_fusion.14.block = bf16[1024,1024]{1,0:T(8,128)(2,1)S(1)} fusion(bf16[5,1024,1024]{2,1,0:T(8,128)(2,1)} %param.4), kind=kLoop, calls=%fused_computation.14 | loop fusion | bytes 4194304 | tf_op jit(solution)/shard_map/squeeze | solution.py:131
  1.8 1.1 slice_bitcast_fusion.15.right
  2.9 0.9 shard_map.37
  3.7 3.1 %collective-permute-start.1 = (bf16[64,1024]{1,0:T(8,128)(2,1)S(1)}, bf16[64,1024]{1,0:T(8,128)(2,1)S(1)}, u32[]{:S(2)}, u32[]{:S(2)}) collective-permute-start(bf16[64,1024]{1,0:T(8,128)(2,1)S(1)} %get-tuple-element.222), channel_id=1, source_target_pairs={{0,4},{4,0},{8,12},{12,8},{1,5},{5,1},{9,13},{13,9},{2,6},{6,2},{1... | collective-permute-start | bytes 393224 | tf_op jit(solution)/shard_map/ppermute | solution.py:138
  6.8 0.8 shard_map.38
  7.8 1.7 %copy-done = bf16[5,1024,256]{2,1,0:T(8,128)(2,1)S(1)} copy-done((bf16[5,1024,256]{2,1,0:T(8,128)(2,1)S(1)}, bf16[5,1024,256]{2,1,0:T(8,128)(2,1)}, u32[]{:S(2)}) %copy-start) | copy-done | bytes 2621464
  9.5 0.9 shard_map.39
  10.7 3.0 %collective-permute-start.2 = (bf16[64,1024]{1,0:T(8,128)(2,1)S(1)}, bf16[64,1024]{1,0:T(8,128)(2,1)S(1)}, u32[]{:S(2)}, u32[]{:S(2)}) collective-permute-start(bf16[64,1024]{1,0:T(8,128)(2,1)S(1)} %get-tuple-element.453), channel_id=1, source_target_pairs={{0,8},{4,12},{8,0},{12,4},{1,9},{5,13},{9,1},{13,5},{2,10},{6,14},... | collective-permute-start | bytes 393224 | tf_op jit(solution)/shard_map/ppermute | solution.py:138
  13.7 1.8 %slice_bitcast_fusion.13.block = bf16[1024,1024]{1,0:T(8,128)(2,1)S(1)} fusion(bf16[10,1024,1024]{2,1,0:T(8,128)(2,1)} %param.3), kind=kLoop, calls=%fused_computation.13 | loop fusion | bytes 4194304 | tf_op jit(solution)/shard_map/squeeze | solution.py:131
  15.5 3.9 %collective-permute-done.2 = bf16[64,1024]{1,0:T(8,128)(2,1)S(1)} collective-permute-done((bf16[64,1024]{1,0:T(8,128)(2,1)S(1)}, bf16[64,1024]{1,0:T(8,128)(2,1)S(1)}, u32[]{:S(2)}, u32[]{:S(2)}) %collective-permute-start.2) | collective-permute-done | bytes 131104 | tf_op jit(solution)/shard_map/ppermute | solution.py:138
  19.4 0.8 collective-permute-start.4
  21.1 3.4 %collective-permute-start.3 = (bf16[64,1024]{1,0:T(8,128)(2,1)S(1)}, bf16[64,1024]{1,0:T(8,128)(2,1)S(1)}, u32[]{:S(2)}, u32[]{:S(2)}) collective-permute-start(bf16[64,1024]{1,0:T(8,128)(2,1)S(1)} %get-tuple-element.451), channel_id=1, source_target_pairs={{0,8},{4,12},{8,0},{12,4},{1,9},{5,13},{9,1},{13,5},{2,10},{6,14},... | collective-permute-start | bytes 393224 | tf_op jit(solution)/shard_map/ppermute | solution.py:138
  25.3 1.6 %collective-permute-start.7 = (bf16[64,1024]{1,0:T(8,128)(2,1)S(1)}, bf16[64,1024]{1,0:T(8,128)(2,1)S(1)}, u32[]{:S(2)}, u32[]{:S(2)}) collective-permute-start(bf16[64,1024]{1,0:T(8,128)(2,1)S(1)} %get-tuple-element.449), channel_id=1, source_target_pairs={{0,2},{1,3},{2,0},{3,1},{4,6},{5,7},{6,4},{7,5},{8,10},{9,11},{10,... | collective-permute-start | bytes 393224 | tf_op jit(solution)/shard_map/ppermute | solution.py:138
  26.9 1.8 %slice_bitcast_fusion.12.block = bf16[1024,1024]{1,0:T(8,128)(2,1)S(1)} fusion(bf16[10,1024,1024]{2,1,0:T(8,128)(2,1)} %param.3), kind=kLoop, calls=%fused_computation.12 | loop fusion | bytes 4194304 | tf_op jit(solution)/shard_map/squeeze | solution.py:131
  28.8 1.8 %slice_bitcast_fusion.11.block = bf16[1024,1024]{1,0:T(8,128)(2,1)S(1)} fusion(bf16[5,1024,1024]{2,1,0:T(8,128)(2,1)} %param.4), kind=kLoop, calls=%fused_computation.11 | loop fusion | bytes 4194304 | tf_op jit(solution)/shard_map/squeeze | solution.py:131
  30.5 0.9 collective-permute-done.3
  34.1 1.7 %collective-permute-start.11 = (bf16[64,1024]{1,0:T(8,128)(2,1)S(1)}, bf16[64,1024]{1,0:T(8,128)(2,1)S(1)}, u32[]{:S(2)}, u32[]{:S(2)}) collective-permute-start(bf16[64,1024]{1,0:T(8,128)(2,1)S(1)} %shard_map.43), channel_id=1, source_target_pairs={{0,4},{4,0},{8,12},{12,8},{1,5},{5,1},{9,13},{13,9},{2,6},{6,2},{1... | collective-permute-start | bytes 393224 | tf_op jit(solution)/shard_map/ppermute | solution.py:138
  35.8 1.2 collective-permute-done.6.refs_0_.refs_2_
  37.8 1.6 %collective-permute-start.9 = (bf16[64,1024]{1,0:T(8,128)(2,1)S(1)}, bf16[64,1024]{1,0:T(8,128)(2,1)S(1)}, u32[]{:S(2)}, u32[]{:S(2)}) collective-permute-start(bf16[64,1024]{1,0:T(8,128)(2,1)S(1)} %get-tuple-element.447), channel_id=1, source_target_pairs={{0,2},{1,3},{2,0},{3,1},{4,6},{5,7},{6,4},{7,5},{8,10},{9,11},{10,... | collective-permute-start | bytes 393224 | tf_op jit(solution)/shard_map/ppermute | solution.py:138
  39.6 0.9 shard_map.45
  41.4 2.6 %collective-permute-start.14 = (bf16[64,1024]{1,0:T(8,128)(2,1)S(1)}, bf16[64,1024]{1,0:T(8,128)(2,1)S(1)}, u32[]{:S(2)}, u32[]{:S(2)}) collective-permute-start(bf16[64,1024]{1,0:T(8,128)(2,1)S(1)} %get-tuple-element.445), channel_id=1, source_target_pairs={{0,8},{4,12},{8,0},{12,4},{1,9},{5,13},{9,1},{13,5},{2,10},{6,14},... | collective-permute-start | bytes 393224 | tf_op jit(solution)/shard_map/ppermute | solution.py:138
  46.4 3.4 %collective-permute-done.14 = bf16[64,1024]{1,0:T(8,128)(2,1)S(1)} collective-permute-done((bf16[64,1024]{1,0:T(8,128)(2,1)S(1)}, bf16[64,1024]{1,0:T(8,128)(2,1)S(1)}, u32[]{:S(2)}, u32[]{:S(2)}) %collective-permute-start.14) | collective-permute-done | bytes 131104 | tf_op jit(solution)/shard_map/ppermute | solution.py:138
  50.7 1.8 %collective-permute-done.13 = bf16[64,1024]{1,0:T(8,128)(2,1)S(1)} collective-permute-done((bf16[64,1024]{1,0:T(8,128)(2,1)S(1)}, bf16[64,1024]{1,0:T(8,128)(2,1)S(1)}, u32[]{:S(2)}, u32[]{:S(2)}) %collective-permute-start.13) | collective-permute-done | bytes 131104 | tf_op jit(solution)/shard_map/ppermute | solution.py:138
  52.5 1.5 %collective-permute-start.15 = (bf16[64,1024]{1,0:T(8,128)(2,1)S(1)}, bf16[64,1024]{1,0:T(8,128)(2,1)S(1)}, u32[]{:S(2)}, u32[]{:S(2)}) collective-permute-start(bf16[64,1024]{1,0:T(8,128)(2,1)S(1)} %get-tuple-element.443), channel_id=1, source_target_pairs={{0,8},{4,12},{8,0},{12,4},{1,9},{5,13},{9,1},{13,5},{2,10},{6,14},... | collective-permute-start | bytes 393224 | tf_op jit(solution)/shard_map/ppermute | solution.py:138
  54.0 1.2 collective-permute-done.16.refs_0_
  56.8 0.9 shard_map.51.refs_4_
  57.9 1.8 %slice_bitcast_fusion.7.block = bf16[1024,1024]{1,0:T(8,128)(2,1)S(1)} fusion(bf16[5,1024,1024]{2,1,0:T(8,128)(2,1)} %param.4), kind=kLoop, calls=%fused_computation.7 | loop fusion | bytes 4194304 | tf_op jit(solution)/shard_map/squeeze | solution.py:131
  59.6 2.1 %collective-permute-done.15 = bf16[64,1024]{1,0:T(8,128)(2,1)S(1)} collective-permute-done((bf16[64,1024]{1,0:T(8,128)(2,1)S(1)}, bf16[64,1024]{1,0:T(8,128)(2,1)S(1)}, u32[]{:S(2)}, u32[]{:S(2)}) %collective-permute-start.15) | collective-permute-done | bytes 131104 | tf_op jit(solution)/shard_map/ppermute | solution.py:138
  61.8 0.8 shard_map.52
  64.0 2.1 %collective-permute-start.23 = (bf16[64,1024]{1,0:T(8,128)(2,1)S(1)}, bf16[64,1024]{1,0:T(8,128)(2,1)S(1)}, u32[]{:S(2)}, u32[]{:S(2)}) collective-permute-start(bf16[64,1024]{1,0:T(8,128)(2,1)S(1)} %shard_map.53), channel_id=1, source_target_pairs={{0,4},{4,0},{8,12},{12,8},{1,5},{5,1},{9,13},{13,9},{2,6},{6,2},{1... | collective-permute-start | bytes 393224 | tf_op jit(solution)/shard_map/ppermute | solution.py:138
  66.1 1.0 collective-permute-done.18.refs_0_.refs_2_
  68.6 0.9 shard_map.55
  69.5 1.0 shard_map.56
  70.5 1.9 %collective-permute-start.26 = (bf16[64,1024]{1,0:T(8,128)(2,1)S(1)}, bf16[64,1024]{1,0:T(8,128)(2,1)S(1)}, u32[]{:S(2)}, u32[]{:S(2)}) collective-permute-start(bf16[64,1024]{1,0:T(8,128)(2,1)S(1)} %get-tuple-element.437), channel_id=1, source_target_pairs={{0,8},{4,12},{8,0},{12,4},{1,9},{5,13},{9,1},{13,5},{2,10},{6,14},... | collective-permute-start | bytes 393224 | tf_op jit(solution)/shard_map/ppermute | solution.py:138
  74.0 0.8 collective-permute-start.25
  75.6 3.2 %collective-permute-done.26 = bf16[64,1024]{1,0:T(8,128)(2,1)S(1)} collective-permute-done((bf16[64,1024]{1,0:T(8,128)(2,1)S(1)}, bf16[64,1024]{1,0:T(8,128)(2,1)S(1)}, u32[]{:S(2)}, u32[]{:S(2)}) %collective-permute-start.26) | collective-permute-done | bytes 131104 | tf_op jit(solution)/shard_map/ppermute | solution.py:138
  79.8 1.8 %collective-permute-done.25 = bf16[64,1024]{1,0:T(8,128)(2,1)S(1)} collective-permute-done((bf16[64,1024]{1,0:T(8,128)(2,1)S(1)}, bf16[64,1024]{1,0:T(8,128)(2,1)S(1)}, u32[]{:S(2)}, u32[]{:S(2)}) %collective-permute-start.25) | collective-permute-done | bytes 131104 | tf_op jit(solution)/shard_map/ppermute | solution.py:138
  81.6 1.3 collective-permute-start.27
  82.8 1.5 %collective-permute-done.28.refs_0_ = bf16[64,1024]{1,0:T(8,128)(2,1)S(1)} collective-permute-done((bf16[64,1024]{1,0:T(8,128)(2,1)S(1)}, bf16[64,1024]{1,0:T(8,128)(2,1)S(1)}, u32[]{:S(2)}, u32[]{:S(2)}) %collective-permute-start.28) | collective-permute-done | bytes 131104 | tf_op jit(solution)/shard_map/ppermute | solution.py:138
  85.1 1.3 collective-permute-start.31
  86.6 0.9 shard_map.61.refs_4_
  87.7 0.9 shard_map.62.refs_4_
  88.7 1.8 %slice_bitcast_fusion.2.block = bf16[1024,1024]{1,0:T(8,128)(2,1)S(1)} fusion(bf16[5,1024,1024]{2,1,0:T(8,128)(2,1)} %param.4), kind=kLoop, calls=%fused_computation.2 | loop fusion | bytes 4194304 | tf_op jit(solution)/shard_map/squeeze | solution.py:131
  93.1 2.1 %collective-permute-start.35 = (bf16[64,1024]{1,0:T(8,128)(2,1)S(1)}, bf16[64,1024]{1,0:T(8,128)(2,1)S(1)}, u32[]{:S(2)}, u32[]{:S(2)}) collective-permute-start(bf16[64,1024]{1,0:T(8,128)(2,1)S(1)} %shard_map.64), channel_id=1, source_target_pairs={{0,4},{4,0},{8,12},{12,8},{1,5},{5,1},{9,13},{13,9},{2,6},{6,2},{1... | collective-permute-start | bytes 393224 | tf_op jit(solution)/shard_map/ppermute | solution.py:138
  95.2 1.0 collective-permute-done.30.refs_0_.refs_2_
  97.0 0.8 collective-permute-start.33
  98.0 0.9 shard_map.66
  99.7 1.5 %collective-permute-start.38 = (bf16[64,1024]{1,0:T(8,128)(2,1)S(1)}, bf16[64,1024]{1,0:T(8,128)(2,1)S(1)}, u32[]{:S(2)}, u32[]{:S(2)}) collective-permute-start(bf16[64,1024]{1,0:T(8,128)(2,1)S(1)} %get-tuple-element.429), channel_id=1, source_target_pairs={{0,8},{4,12},{8,0},{12,4},{1,9},{5,13},{9,1},{13,5},{2,10},{6,14},... | collective-permute-start | bytes 393224 | tf_op jit(solution)/shard_map/ppermute | solution.py:138
  101.2 0.8 collective-permute-done.33
  104.3 3.6 %collective-permute-done.38 = bf16[64,1024]{1,0:T(8,128)(2,1)S(1)} collective-permute-done((bf16[64,1024]{1,0:T(8,128)(2,1)S(1)}, bf16[64,1024]{1,0:T(8,128)(2,1)S(1)}, u32[]{:S(2)}, u32[]{:S(2)}) %collective-permute-start.38) | collective-permute-done | bytes 131104 | tf_op jit(solution)/shard_map/ppermute | solution.py:138
  108.0 0.8 shard_map.70
  108.9 1.8 %collective-permute-done.37 = bf16[64,1024]{1,0:T(8,128)(2,1)S(1)} collective-permute-done((bf16[64,1024]{1,0:T(8,128)(2,1)S(1)}, bf16[64,1024]{1,0:T(8,128)(2,1)S(1)}, u32[]{:S(2)}, u32[]{:S(2)}) %collective-permute-start.37) | collective-permute-done | bytes 131104 | tf_op jit(solution)/shard_map/ppermute | solution.py:138
  111.3 2.1 %collective-permute-done.40.refs_0_ = bf16[64,1024]{1,0:T(8,128)(2,1)S(1)} collective-permute-done((bf16[64,1024]{1,0:T(8,128)(2,1)S(1)}, bf16[64,1024]{1,0:T(8,128)(2,1)S(1)}, u32[]{:S(2)}, u32[]{:S(2)}) %collective-permute-start.40) | collective-permute-done | bytes 131104 | tf_op jit(solution)/shard_map/ppermute | solution.py:138
  114.2 1.0 collective-permute-start.42
  115.3 1.8 %slice_bitcast_fusion.block = bf16[1024,1024]{1,0:T(8,128)(2,1)S(1)} fusion(bf16[5,1024,1024]{2,1,0:T(8,128)(2,1)} %param.4), kind=kLoop, calls=%fused_computation | loop fusion | bytes 4194304 | tf_op jit(solution)/shard_map/squeeze | solution.py:131
  117.0 2.2 %collective-permute-done.42 = bf16[64,1024]{1,0:T(8,128)(2,1)S(1)} collective-permute-done((bf16[64,1024]{1,0:T(8,128)(2,1)S(1)}, bf16[64,1024]{1,0:T(8,128)(2,1)S(1)}, u32[]{:S(2)}, u32[]{:S(2)}) %collective-permute-start.42) | collective-permute-done | bytes 131104 | tf_op jit(solution)/shard_map/ppermute | solution.py:138
  121.5 3.8 %collective-permute-done.43.refs_0_ = bf16[64,1024]{1,0:T(8,128)(2,1)S(1)} collective-permute-done((bf16[64,1024]{1,0:T(8,128)(2,1)S(1)}, bf16[64,1024]{1,0:T(8,128)(2,1)S(1)}, u32[]{:S(2)}, u32[]{:S(2)}) %collective-permute-start.43) | collective-permute-done | bytes 131104 | tf_op jit(solution)/shard_map/ppermute | solution.py:138
  125.3 1.0 shard_map.73
  128.7 2.7 %collective-permute-done.47 = bf16[64,1024]{1,0:T(8,128)(2,1)S(1)} collective-permute-done((bf16[64,1024]{1,0:T(8,128)(2,1)S(1)}, bf16[64,1024]{1,0:T(8,128)(2,1)S(1)}, u32[]{:S(2)}, u32[]{:S(2)}) %collective-permute-start.47) | collective-permute-done | bytes 131104 | tf_op jit(solution)/shard_map/ppermute | solution.py:138
  131.5 1.2 collective-permute-done.46
  134.0 1.3 collective-permute-start.50
  136.1 3.1 %collective-permute-done.49 = bf16[64,1024]{1,0:T(8,128)(2,1)S(1)} collective-permute-done((bf16[64,1024]{1,0:T(8,128)(2,1)S(1)}, bf16[64,1024]{1,0:T(8,128)(2,1)S(1)}, u32[]{:S(2)}, u32[]{:S(2)}) %collective-permute-start.49) | collective-permute-done | bytes 131104 | tf_op jit(solution)/shard_map/ppermute | solution.py:138
  139.2 3.2 %collective-permute-start.51 = (bf16[64,1024]{1,0:T(8,128)(2,1)S(1)}, bf16[64,1024]{1,0:T(8,128)(2,1)S(1)}, u32[]{:S(2)}, u32[]{:S(2)}) collective-permute-start(bf16[64,1024]{1,0:T(8,128)(2,1)S(1)} %fusion.1), channel_id=1, source_target_pairs={{8,4},{0,12},{9,5},{1,13},{10,6},{2,14},{11,7},{3,15},{24,20},{16,... | collective-permute-start | bytes 393224 | tf_op jit(solution)/shard_map/ppermute | solution.py:256
  143.0 2.0 %collective-permute-done.51 = bf16[64,1024]{1,0:T(8,128)(2,1)S(1)} collective-permute-done((bf16[64,1024]{1,0:T(8,128)(2,1)S(1)}, bf16[64,1024]{1,0:T(8,128)(2,1)S(1)}, u32[]{:S(2)}, u32[]{:S(2)}) %collective-permute-start.51) | collective-permute-done | bytes 131104 | tf_op jit(solution)/shard_map/ppermute | solution.py:256
  (148 shorter events, 35.3 us)
Async XLA Ops:
  3.7 7.0 %collective-permute-start.1 = (bf16[64,1024]{1,0:T(8,128)(2,1)S(1)}, bf16[64,1024]{1,0:T(8,128)(2,1)S(1)}, u32[]{:S(2)}, u32[]{:S(2)}) collective-permute-start(bf16[64,1024]{1,0:T(8,128)(2,1)S(1)} %get-tuple-element.222), channel_id=1, source_target_pairs={{0,4},{4,0},{8,12},{12,8},{1,5},{5,1},{9,13},{13,9},{2,6},{6,2},{1... | collective-permute-start | bytes 393224 | tf_op jit(solution)/shard_map/ppermute | solution.py:138
  7.7 13.4 %collective-permute-start = (bf16[64,1024]{1,0:T(8,128)(2,1)S(1)}, bf16[64,1024]{1,0:T(8,128)(2,1)S(1)}, u32[]{:S(2)}, u32[]{:S(2)}) collective-permute-start(bf16[64,1024]{1,0:T(8,128)(2,1)S(1)} %get-tuple-element.221), channel_id=1, source_target_pairs={{0,4},{4,0},{8,12},{12,8},{1,5},{5,1},{9,13},{13,9},{2,6},{6,2},{1... | collective-permute-start | bytes 393224 | tf_op jit(solution)/shard_map/ppermute | solution.py:138
  7.7 1.7 %copy-start = (bf16[5,1024,256]{2,1,0:T(8,128)(2,1)S(1)}, bf16[5,1024,256]{2,1,0:T(8,128)(2,1)}, u32[]{:S(2)}) copy-start(bf16[5,1024,256]{2,1,0:T(8,128)(2,1)} %sides) | copy-start | bytes 7864324
  10.7 8.6 %collective-permute-start.2 = (bf16[64,1024]{1,0:T(8,128)(2,1)S(1)}, bf16[64,1024]{1,0:T(8,128)(2,1)S(1)}, u32[]{:S(2)}, u32[]{:S(2)}) collective-permute-start(bf16[64,1024]{1,0:T(8,128)(2,1)S(1)} %get-tuple-element.453), channel_id=1, source_target_pairs={{0,8},{4,12},{8,0},{12,4},{1,9},{5,13},{9,1},{13,5},{2,10},{6,14},... | collective-permute-start | bytes 393224 | tf_op jit(solution)/shard_map/ppermute | solution.py:138
  19.4 5.1 %collective-permute-start.4 = (bf16[64,1024]{1,0:T(8,128)(2,1)S(1)}, bf16[64,1024]{1,0:T(8,128)(2,1)S(1)}, u32[]{:S(2)}, u32[]{:S(2)}) collective-permute-start(bf16[64,1024]{1,0:T(8,128)(2,1)S(1)} %add_convert_fusion.8.refs_0_.refs_1_), channel_id=1, source_target_pairs={{0,4},{4,0},{8,12},{12,8},{1,5},{5,1},{9,13},{13,9},{2,6},{6,2},{1... | collective-permute-start | bytes 393224 | tf_op jit(solution)/shard_map/ppermute | solution.py:138
  20.9 4.4 %collective-permute-start.5 = (bf16[64,1024]{1,0:T(8,128)(2,1)S(1)}, bf16[64,1024]{1,0:T(8,128)(2,1)S(1)}, u32[]{:S(2)}, u32[]{:S(2)}) collective-permute-start(bf16[64,1024]{1,0:T(8,128)(2,1)S(1)} %shard_map.40), channel_id=1, source_target_pairs={{0,1},{1,0},{2,3},{3,2},{4,5},{5,4},{6,7},{7,6},{8,9},{9,8},{10,11... | collective-permute-start | bytes 393224 | tf_op jit(solution)/shard_map/ppermute | solution.py:138
  21.0 18.4 %copy-start.1 = (bf16[10,1024,1024]{2,1,0:T(8,128)(2,1)S(1)}, bf16[10,1024,1024]{2,1,0:T(8,128)(2,1)}, u32[]{:S(2)}) copy-start(bf16[10,1024,1024]{2,1,0:T(8,128)(2,1)} %param.3) | copy-start | bytes 62914564
  21.1 10.4 %collective-permute-start.3 = (bf16[64,1024]{1,0:T(8,128)(2,1)S(1)}, bf16[64,1024]{1,0:T(8,128)(2,1)S(1)}, u32[]{:S(2)}, u32[]{:S(2)}) collective-permute-start(bf16[64,1024]{1,0:T(8,128)(2,1)S(1)} %get-tuple-element.451), channel_id=1, source_target_pairs={{0,8},{4,12},{8,0},{12,4},{1,9},{5,13},{9,1},{13,5},{2,10},{6,14},... | collective-permute-start | bytes 393224 | tf_op jit(solution)/shard_map/ppermute | solution.py:138
  25.3 7.4 %collective-permute-start.7 = (bf16[64,1024]{1,0:T(8,128)(2,1)S(1)}, bf16[64,1024]{1,0:T(8,128)(2,1)S(1)}, u32[]{:S(2)}, u32[]{:S(2)}) collective-permute-start(bf16[64,1024]{1,0:T(8,128)(2,1)S(1)} %get-tuple-element.449), channel_id=1, source_target_pairs={{0,2},{1,3},{2,0},{3,1},{4,6},{5,7},{6,4},{7,5},{8,10},{9,11},{10,... | collective-permute-start | bytes 393224 | tf_op jit(solution)/shard_map/ppermute | solution.py:138
  31.5 5.5 %collective-permute-start.6 = (bf16[64,1024]{1,0:T(8,128)(2,1)S(1)}, bf16[64,1024]{1,0:T(8,128)(2,1)S(1)}, u32[]{:S(2)}, u32[]{:S(2)}) collective-permute-start(bf16[64,1024]{1,0:T(8,128)(2,1)S(1)} %add_convert_fusion.7.refs_0_.refs_3_), channel_id=1, source_target_pairs={{0,4},{4,0},{8,12},{12,8},{1,5},{5,1},{9,13},{13,9},{2,6},{6,2},{1... | collective-permute-start | bytes 393224 | tf_op jit(solution)/shard_map/ppermute | solution.py:138
  32.7 5.1 %collective-permute-start.8 = (bf16[64,1024]{1,0:T(8,128)(2,1)S(1)}, bf16[64,1024]{1,0:T(8,128)(2,1)S(1)}, u32[]{:S(2)}, u32[]{:S(2)}) collective-permute-start(bf16[64,1024]{1,0:T(8,128)(2,1)S(1)} %shard_map.42), channel_id=1, source_target_pairs={{0,1},{1,0},{2,3},{3,2},{4,5},{5,4},{6,7},{7,6},{8,9},{9,8},{10,11... | collective-permute-start | bytes 393224 | tf_op jit(solution)/shard_map/ppermute | solution.py:138
  32.8 7.7 %collective-permute-start.10 = (bf16[64,1024]{1,0:T(8,128)(2,1)S(1)}, bf16[64,1024]{1,0:T(8,128)(2,1)S(1)}, u32[]{:S(2)}, u32[]{:S(2)}) collective-permute-start(bf16[64,1024]{1,0:T(8,128)(2,1)S(1)} %subtract_convert_fusion.7.refs_0_), channel_id=1, source_target_pairs={{0,1},{1,0},{2,3},{3,2},{4,5},{5,4},{6,7},{7,6},{8,9},{9,8},{10,11... | collective-permute-start | bytes 393224 | tf_op jit(solution)/shard_map/ppermute | solution.py:138
  34.1 7.2 %collective-permute-start.11 = (bf16[64,1024]{1,0:T(8,128)(2,1)S(1)}, bf16[64,1024]{1,0:T(8,128)(2,1)S(1)}, u32[]{:S(2)}, u32[]{:S(2)}) collective-permute-start(bf16[64,1024]{1,0:T(8,128)(2,1)S(1)} %shard_map.43), channel_id=1, source_target_pairs={{0,4},{4,0},{8,12},{12,8},{1,5},{5,1},{9,13},{13,9},{2,6},{6,2},{1... | collective-permute-start | bytes 393224 | tf_op jit(solution)/shard_map/ppermute | solution.py:138
  37.8 6.1 %collective-permute-start.9 = (bf16[64,1024]{1,0:T(8,128)(2,1)S(1)}, bf16[64,1024]{1,0:T(8,128)(2,1)S(1)}, u32[]{:S(2)}, u32[]{:S(2)}) collective-permute-start(bf16[64,1024]{1,0:T(8,128)(2,1)S(1)} %get-tuple-element.447), channel_id=1, source_target_pairs={{0,2},{1,3},{2,0},{3,1},{4,6},{5,7},{6,4},{7,5},{8,10},{9,11},{10,... | collective-permute-start | bytes 393224 | tf_op jit(solution)/shard_map/ppermute | solution.py:138
  41.4 8.3 %collective-permute-start.14 = (bf16[64,1024]{1,0:T(8,128)(2,1)S(1)}, bf16[64,1024]{1,0:T(8,128)(2,1)S(1)}, u32[]{:S(2)}, u32[]{:S(2)}) collective-permute-start(bf16[64,1024]{1,0:T(8,128)(2,1)S(1)} %get-tuple-element.445), channel_id=1, source_target_pairs={{0,8},{4,12},{8,0},{12,4},{1,9},{5,13},{9,1},{13,5},{2,10},{6,14},... | collective-permute-start | bytes 393224 | tf_op jit(solution)/shard_map/ppermute | solution.py:138
  44.0 1.6 %collective-permute-start.12 = (bf16[64,1024]{1,0:T(8,128)(2,1)S(1)}, bf16[64,1024]{1,0:T(8,128)(2,1)S(1)}, u32[]{:S(2)}, u32[]{:S(2)}) collective-permute-start(bf16[64,1024]{1,0:T(8,128)(2,1)S(1)} %subtract_convert_fusion.6.refs_0_), channel_id=1, source_target_pairs={{0,1},{1,0},{2,3},{3,2},{4,5},{5,4},{6,7},{7,6},{8,9},{9,8},{10,11... | collective-permute-start | bytes 393224 | tf_op jit(solution)/shard_map/ppermute | solution.py:138
  44.9 7.6 %collective-permute-start.13 = (bf16[64,1024]{1,0:T(8,128)(2,1)S(1)}, bf16[64,1024]{1,0:T(8,128)(2,1)S(1)}, u32[]{:S(2)}, u32[]{:S(2)}) collective-permute-start(bf16[64,1024]{1,0:T(8,128)(2,1)S(1)} %shard_map.47), channel_id=1, source_target_pairs={{0,4},{4,0},{8,12},{12,8},{1,5},{5,1},{9,13},{13,9},{2,6},{6,2},{1... | collective-permute-start | bytes 393224 | tf_op jit(solution)/shard_map/ppermute | solution.py:138
  49.7 5.5 %collective-permute-start.16 = (bf16[64,1024]{1,0:T(8,128)(2,1)S(1)}, bf16[64,1024]{1,0:T(8,128)(2,1)S(1)}, u32[]{:S(2)}, u32[]{:S(2)}) collective-permute-start(bf16[64,1024]{1,0:T(8,128)(2,1)S(1)} %add_convert_fusion.6.refs_0_.refs_1_), channel_id=1, source_target_pairs={{0,4},{4,0},{8,12},{12,8},{1,5},{5,1},{9,13},{13,9},{2,6},{6,2},{1... | collective-permute-start | bytes 393224 | tf_op jit(solution)/shard_map/ppermute | solution.py:138
  50.6 5.4 %collective-permute-start.17 = (bf16[64,1024]{1,0:T(8,128)(2,1)S(1)}, bf16[64,1024]{1,0:T(8,128)(2,1)S(1)}, u32[]{:S(2)}, u32[]{:S(2)}) collective-permute-start(bf16[64,1024]{1,0:T(8,128)(2,1)S(1)} %shard_map.49), channel_id=1, source_target_pairs={{0,1},{1,0},{2,3},{3,2},{4,5},{5,4},{6,7},{7,6},{8,9},{9,8},{10,11... | collective-permute-start | bytes 393224 | tf_op jit(solution)/shard_map/ppermute | solution.py:138
  52.5 9.2 %collective-permute-start.15 = (bf16[64,1024]{1,0:T(8,128)(2,1)S(1)}, bf16[64,1024]{1,0:T(8,128)(2,1)S(1)}, u32[]{:S(2)}, u32[]{:S(2)}) collective-permute-start(bf16[64,1024]{1,0:T(8,128)(2,1)S(1)} %get-tuple-element.443), channel_id=1, source_target_pairs={{0,8},{4,12},{8,0},{12,4},{1,9},{5,13},{9,1},{13,5},{2,10},{6,14},... | collective-permute-start | bytes 393224 | tf_op jit(solution)/shard_map/ppermute | solution.py:138
  56.0 6.6 %collective-permute-start.19 = (bf16[64,1024]{1,0:T(8,128)(2,1)S(1)}, bf16[64,1024]{1,0:T(8,128)(2,1)S(1)}, u32[]{:S(2)}, u32[]{:S(2)}) collective-permute-start(bf16[64,1024]{1,0:T(8,128)(2,1)S(1)} %get-tuple-element.441), channel_id=1, source_target_pairs={{0,2},{1,3},{2,0},{3,1},{4,6},{5,7},{6,4},{7,5},{8,10},{9,11},{10,... | collective-permute-start | bytes 393224 | tf_op jit(solution)/shard_map/ppermute | solution.py:138
  61.7 5.4 %collective-permute-start.18 = (bf16[64,1024]{1,0:T(8,128)(2,1)S(1)}, bf16[64,1024]{1,0:T(8,128)(2,1)S(1)}, u32[]{:S(2)}, u32[]{:S(2)}) collective-permute-start(bf16[64,1024]{1,0:T(8,128)(2,1)S(1)} %add_convert_fusion.5.refs_0_.refs_3_), channel_id=1, source_target_pairs={{0,4},{4,0},{8,12},{12,8},{1,5},{5,1},{9,13},{13,9},{2,6},{6,2},{1... | collective-permute-start | bytes 393224 | tf_op jit(solution)/shard_map/ppermute | solution.py:138
  62.6 5.3 %collective-permute-start.20 = (bf16[64,1024]{1,0:T(8,128)(2,1)S(1)}, bf16[64,1024]{1,0:T(8,128)(2,1)S(1)}, u32[]{:S(2)}, u32[]{:S(2)}) collective-permute-start(bf16[64,1024]{1,0:T(8,128)(2,1)S(1)} %shard_map.52), channel_id=1, source_target_pairs={{0,1},{1,0},{2,3},{3,2},{4,5},{5,4},{6,7},{7,6},{8,9},{9,8},{10,11... | collective-permute-start | bytes 393224 | tf_op jit(solution)/shard_map/ppermute | solution.py:138
  62.7 6.8 %collective-permute-start.22 = (bf16[64,1024]{1,0:T(8,128)(2,1)S(1)}, bf16[64,1024]{1,0:T(8,128)(2,1)S(1)}, u32[]{:S(2)}, u32[]{:S(2)}) collective-permute-start(bf16[64,1024]{1,0:T(8,128)(2,1)S(1)} %subtract_convert_fusion.5.refs_0_), channel_id=1, source_target_pairs={{0,1},{1,0},{2,3},{3,2},{4,5},{5,4},{6,7},{7,6},{8,9},{9,8},{10,11... | collective-permute-start | bytes 393224 | tf_op jit(solution)/shard_map/ppermute | solution.py:138
  64.0 6.5 %collective-permute-start.23 = (bf16[64,1024]{1,0:T(8,128)(2,1)S(1)}, bf16[64,1024]{1,0:T(8,128)(2,1)S(1)}, u32[]{:S(2)}, u32[]{:S(2)}) collective-permute-start(bf16[64,1024]{1,0:T(8,128)(2,1)S(1)} %shard_map.53), channel_id=1, source_target_pairs={{0,4},{4,0},{8,12},{12,8},{1,5},{5,1},{9,13},{13,9},{2,6},{6,2},{1... | collective-permute-start | bytes 393224 | tf_op jit(solution)/shard_map/ppermute | solution.py:138
  67.9 5.0 %collective-permute-start.21 = (bf16[64,1024]{1,0:T(8,128)(2,1)S(1)}, bf16[64,1024]{1,0:T(8,128)(2,1)S(1)}, u32[]{:S(2)}, u32[]{:S(2)}) collective-permute-start(bf16[64,1024]{1,0:T(8,128)(2,1)S(1)} %get-tuple-element.439), channel_id=1, source_target_pairs={{0,2},{1,3},{2,0},{3,1},{4,6},{5,7},{6,4},{7,5},{8,10},{9,11},{10,... | collective-permute-start | bytes 393224 | tf_op jit(solution)/shard_map/ppermute | solution.py:138
  70.5 8.3 %collective-permute-start.26 = (bf16[64,1024]{1,0:T(8,128)(2,1)S(1)}, bf16[64,1024]{1,0:T(8,128)(2,1)S(1)}, u32[]{:S(2)}, u32[]{:S(2)}) collective-permute-start(bf16[64,1024]{1,0:T(8,128)(2,1)S(1)} %get-tuple-element.437), channel_id=1, source_target_pairs={{0,8},{4,12},{8,0},{12,4},{1,9},{5,13},{9,1},{13,5},{2,10},{6,14},... | collective-permute-start | bytes 393224 | tf_op jit(solution)/shard_map/ppermute | solution.py:138
  73.0 1.8 %collective-permute-start.24 = (bf16[64,1024]{1,0:T(8,128)(2,1)S(1)}, bf16[64,1024]{1,0:T(8,128)(2,1)S(1)}, u32[]{:S(2)}, u32[]{:S(2)}) collective-permute-start(bf16[64,1024]{1,0:T(8,128)(2,1)S(1)} %subtract_convert_fusion.4.refs_0_), channel_id=1, source_target_pairs={{0,1},{1,0},{2,3},{3,2},{4,5},{5,4},{6,7},{7,6},{8,9},{9,8},{10,11... | collective-permute-start | bytes 393224 | tf_op jit(solution)/shard_map/ppermute | solution.py:138
  74.0 7.6 %collective-permute-start.25 = (bf16[64,1024]{1,0:T(8,128)(2,1)S(1)}, bf16[64,1024]{1,0:T(8,128)(2,1)S(1)}, u32[]{:S(2)}, u32[]{:S(2)}) collective-permute-start(bf16[64,1024]{1,0:T(8,128)(2,1)S(1)} %shard_map.57), channel_id=1, source_target_pairs={{0,4},{4,0},{8,12},{12,8},{1,5},{5,1},{9,13},{13,9},{2,6},{6,2},{1... | collective-permute-start | bytes 393224 | tf_op jit(solution)/shard_map/ppermute | solution.py:138
  78.8 5.5 %collective-permute-start.28 = (bf16[64,1024]{1,0:T(8,128)(2,1)S(1)}, bf16[64,1024]{1,0:T(8,128)(2,1)S(1)}, u32[]{:S(2)}, u32[]{:S(2)}) collective-permute-start(bf16[64,1024]{1,0:T(8,128)(2,1)S(1)} %add_convert_fusion.4.refs_0_.refs_1_), channel_id=1, source_target_pairs={{0,4},{4,0},{8,12},{12,8},{1,5},{5,1},{9,13},{13,9},{2,6},{6,2},{1... | collective-permute-start | bytes 393224 | tf_op jit(solution)/shard_map/ppermute | solution.py:138
  79.7 5.4 %collective-permute-start.29 = (bf16[64,1024]{1,0:T(8,128)(2,1)S(1)}, bf16[64,1024]{1,0:T(8,128)(2,1)S(1)}, u32[]{:S(2)}, u32[]{:S(2)}) collective-permute-start(bf16[64,1024]{1,0:T(8,128)(2,1)S(1)} %shard_map.59), channel_id=1, source_target_pairs={{0,1},{1,0},{2,3},{3,2},{4,5},{5,4},{6,7},{7,6},{8,9},{9,8},{10,11... | collective-permute-start | bytes 393224 | tf_op jit(solution)/shard_map/ppermute | solution.py:138
  81.6 9.2 %collective-permute-start.27 = (bf16[64,1024]{1,0:T(8,128)(2,1)S(1)}, bf16[64,1024]{1,0:T(8,128)(2,1)S(1)}, u32[]{:S(2)}, u32[]{:S(2)}) collective-permute-start(bf16[64,1024]{1,0:T(8,128)(2,1)S(1)} %get-tuple-element.435), channel_id=1, source_target_pairs={{0,8},{4,12},{8,0},{12,4},{1,9},{5,13},{9,1},{13,5},{2,10},{6,14},... | collective-permute-start | bytes 393224 | tf_op jit(solution)/shard_map/ppermute | solution.py:138
  85.1 6.6 %collective-permute-start.31 = (bf16[64,1024]{1,0:T(8,128)(2,1)S(1)}, bf16[64,1024]{1,0:T(8,128)(2,1)S(1)}, u32[]{:S(2)}, u32[]{:S(2)}) collective-permute-start(bf16[64,1024]{1,0:T(8,128)(2,1)S(1)} %get-tuple-element.433), channel_id=1, source_target_pairs={{0,2},{1,3},{2,0},{3,1},{4,6},{5,7},{6,4},{7,5},{8,10},{9,11},{10,... | collective-permute-start | bytes 393224 | tf_op jit(solution)/shard_map/ppermute | solution.py:138
  90.8 5.4 %collective-permute-start.30 = (bf16[64,1024]{1,0:T(8,128)(2,1)S(1)}, bf16[64,1024]{1,0:T(8,128)(2,1)S(1)}, u32[]{:S(2)}, u32[]{:S(2)}) collective-permute-start(bf16[64,1024]{1,0:T(8,128)(2,1)S(1)} %add_convert_fusion.3.refs_0_.refs_3_), channel_id=1, source_target_pairs={{0,4},{4,0},{8,12},{12,8},{1,5},{5,1},{9,13},{13,9},{2,6},{6,2},{1... | collective-permute-start | bytes 393224 | tf_op jit(solution)/shard_map/ppermute | solution.py:138
  91.7 5.3 %collective-permute-start.32 = (bf16[64,1024]{1,0:T(8,128)(2,1)S(1)}, bf16[64,1024]{1,0:T(8,128)(2,1)S(1)}, u32[]{:S(2)}, u32[]{:S(2)}) collective-permute-start(bf16[64,1024]{1,0:T(8,128)(2,1)S(1)} %shard_map.63), channel_id=1, source_target_pairs={{0,1},{1,0},{2,3},{3,2},{4,5},{5,4},{6,7},{7,6},{8,9},{9,8},{10,11... | collective-permute-start | bytes 393224 | tf_op jit(solution)/shard_map/ppermute | solution.py:138
  91.8 7.1 %collective-permute-start.34 = (bf16[64,1024]{1,0:T(8,128)(2,1)S(1)}, bf16[64,1024]{1,0:T(8,128)(2,1)S(1)}, u32[]{:S(2)}, u32[]{:S(2)}) collective-permute-start(bf16[64,1024]{1,0:T(8,128)(2,1)S(1)} %subtract_convert_fusion.3.refs_0_), channel_id=1, source_target_pairs={{0,1},{1,0},{2,3},{3,2},{4,5},{5,4},{6,7},{7,6},{8,9},{9,8},{10,11... | collective-permute-start | bytes 393224 | tf_op jit(solution)/shard_map/ppermute | solution.py:138
  93.1 6.6 %collective-permute-start.35 = (bf16[64,1024]{1,0:T(8,128)(2,1)S(1)}, bf16[64,1024]{1,0:T(8,128)(2,1)S(1)}, u32[]{:S(2)}, u32[]{:S(2)}) collective-permute-start(bf16[64,1024]{1,0:T(8,128)(2,1)S(1)} %shard_map.64), channel_id=1, source_target_pairs={{0,4},{4,0},{8,12},{12,8},{1,5},{5,1},{9,13},{13,9},{2,6},{6,2},{1... | collective-permute-start | bytes 393224 | tf_op jit(solution)/shard_map/ppermute | solution.py:138
  97.0 5.0 %collective-permute-start.33 = (bf16[64,1024]{1,0:T(8,128)(2,1)S(1)}, bf16[64,1024]{1,0:T(8,128)(2,1)S(1)}, u32[]{:S(2)}, u32[]{:S(2)}) collective-permute-start(bf16[64,1024]{1,0:T(8,128)(2,1)S(1)} %get-tuple-element.431), channel_id=1, source_target_pairs={{0,2},{1,3},{2,0},{3,1},{4,6},{5,7},{6,4},{7,5},{8,10},{9,11},{10,... | collective-permute-start | bytes 393224 | tf_op jit(solution)/shard_map/ppermute | solution.py:138
  99.7 8.1 %collective-permute-start.38 = (bf16[64,1024]{1,0:T(8,128)(2,1)S(1)}, bf16[64,1024]{1,0:T(8,128)(2,1)S(1)}, u32[]{:S(2)}, u32[]{:S(2)}) collective-permute-start(bf16[64,1024]{1,0:T(8,128)(2,1)S(1)} %get-tuple-element.429), channel_id=1, source_target_pairs={{0,8},{4,12},{8,0},{12,4},{1,9},{5,13},{9,1},{13,5},{2,10},{6,14},... | collective-permute-start | bytes 393224 | tf_op jit(solution)/shard_map/ppermute | solution.py:138
  102.1 1.4 collective-permute-start.36
  103.0 7.6 %collective-permute-start.37 = (bf16[64,1024]{1,0:T(8,128)(2,1)S(1)}, bf16[64,1024]{1,0:T(8,128)(2,1)S(1)}, u32[]{:S(2)}, u32[]{:S(2)}) collective-permute-start(bf16[64,1024]{1,0:T(8,128)(2,1)S(1)} %shard_map.68), channel_id=1, source_target_pairs={{0,4},{4,0},{8,12},{12,8},{1,5},{5,1},{9,13},{13,9},{2,6},{6,2},{1... | collective-permute-start | bytes 393224 | tf_op jit(solution)/shard_map/ppermute | solution.py:138
  107.9 5.5 %collective-permute-start.40 = (bf16[64,1024]{1,0:T(8,128)(2,1)S(1)}, bf16[64,1024]{1,0:T(8,128)(2,1)S(1)}, u32[]{:S(2)}, u32[]{:S(2)}) collective-permute-start(bf16[64,1024]{1,0:T(8,128)(2,1)S(1)} %add_convert_fusion.2.refs_0_), channel_id=1, source_target_pairs={{0,4},{4,0},{8,12},{12,8},{1,5},{5,1},{9,13},{13,9},{2,6},{6,2},{1... | collective-permute-start | bytes 393224 | tf_op jit(solution)/shard_map/ppermute | solution.py:138
  108.8 5.4 %collective-permute-start.41 = (bf16[64,1024]{1,0:T(8,128)(2,1)S(1)}, bf16[64,1024]{1,0:T(8,128)(2,1)S(1)}, u32[]{:S(2)}, u32[]{:S(2)}) collective-permute-start(bf16[64,1024]{1,0:T(8,128)(2,1)S(1)} %shard_map.70), channel_id=1, source_target_pairs={{0,1},{1,0},{2,3},{3,2},{4,5},{5,4},{6,7},{7,6},{8,9},{9,8},{10,11... | collective-permute-start | bytes 393224 | tf_op jit(solution)/shard_map/ppermute | solution.py:138
  110.7 9.2 %collective-permute-start.39 = (bf16[64,1024]{1,0:T(8,128)(2,1)S(1)}, bf16[64,1024]{1,0:T(8,128)(2,1)S(1)}, u32[]{:S(2)}, u32[]{:S(2)}) collective-permute-start(bf16[64,1024]{1,0:T(8,128)(2,1)S(1)} %get-tuple-element.427), channel_id=1, source_target_pairs={{0,8},{4,12},{8,0},{12,4},{1,9},{5,13},{9,1},{13,5},{2,10},{6,14},... | collective-permute-start | bytes 393224 | tf_op jit(solution)/shard_map/ppermute | solution.py:138
  114.2 5.0 %collective-permute-start.42 = (bf16[64,1024]{1,0:T(8,128)(2,1)S(1)}, bf16[64,1024]{1,0:T(8,128)(2,1)S(1)}, u32[]{:S(2)}, u32[]{:S(2)}) collective-permute-start(bf16[64,1024]{1,0:T(8,128)(2,1)S(1)} %get-tuple-element.425), channel_id=1, source_target_pairs={{0,2},{1,3},{2,0},{3,1},{4,6},{5,7},{6,4},{7,5},{8,10},{9,11},{10,... | collective-permute-start | bytes 393224 | tf_op jit(solution)/shard_map/ppermute | solution.py:138
  119.9 5.3 %collective-permute-start.43 = (bf16[64,1024]{1,0:T(8,128)(2,1)S(1)}, bf16[64,1024]{1,0:T(8,128)(2,1)S(1)}, u32[]{:S(2)}, u32[]{:S(2)}) collective-permute-start(bf16[64,1024]{1,0:T(8,128)(2,1)S(1)} %add_convert_fusion.1.refs_0_), channel_id=1, source_target_pairs={{0,4},{4,0},{8,12},{12,8},{1,5},{5,1},{9,13},{13,9},{2,6},{6,2},{1... | collective-permute-start | bytes 393224 | tf_op jit(solution)/shard_map/ppermute | solution.py:138
  120.8 5.5 %collective-permute-start.45 = (bf16[64,1024]{1,0:T(8,128)(2,1)S(1)}, bf16[64,1024]{1,0:T(8,128)(2,1)S(1)}, u32[]{:S(2)}, u32[]{:S(2)}) collective-permute-start(bf16[64,1024]{1,0:T(8,128)(2,1)S(1)} %shard_map.72), channel_id=1, source_target_pairs={{0,1},{1,0},{2,3},{3,2},{4,5},{5,4},{6,7},{7,6},{8,9},{9,8},{10,11... | collective-permute-start | bytes 393224 | tf_op jit(solution)/shard_map/ppermute | solution.py:138
  120.9 5.9 %collective-permute-start.44 = (bf16[64,1024]{1,0:T(8,128)(2,1)S(1)}, bf16[64,1024]{1,0:T(8,128)(2,1)S(1)}, u32[]{:S(2)}, u32[]{:S(2)}) collective-permute-start(bf16[64,1024]{1,0:T(8,128)(2,1)S(1)} %subtract_convert_fusion.1), channel_id=1, source_target_pairs={{0,1},{1,0},{2,3},{3,2},{4,5},{5,4},{6,7},{7,6},{8,9},{9,8},{10,11... | collective-permute-start | bytes 393224 | tf_op jit(solution)/shard_map/ppermute | solution.py:138
  126.3 5.0 %collective-permute-start.47 = (bf16[64,1024]{1,0:T(8,128)(2,1)S(1)}, bf16[64,1024]{1,0:T(8,128)(2,1)S(1)}, u32[]{:S(2)}, u32[]{:S(2)}) collective-permute-start(bf16[64,1024]{1,0:T(8,128)(2,1)S(1)} %get-tuple-element.423), channel_id=1, source_target_pairs={{0,2},{1,3},{2,0},{3,1},{4,6},{5,7},{6,4},{7,5},{8,10},{9,11},{10,... | collective-permute-start | bytes 393224 | tf_op jit(solution)/shard_map/ppermute | solution.py:138
  127.6 5.0 %collective-permute-start.46 = (bf16[64,1024]{1,0:T(8,128)(2,1)S(1)}, bf16[64,1024]{1,0:T(8,128)(2,1)S(1)}, u32[]{:S(2)}, u32[]{:S(2)}) collective-permute-start(bf16[64,1024]{1,0:T(8,128)(2,1)S(1)} %shard_map.74), channel_id=1, source_target_pairs={{0,4},{4,0},{8,12},{12,8},{1,5},{5,1},{9,13},{13,9},{2,6},{6,2},{1... | collective-permute-start | bytes 393224 | tf_op jit(solution)/shard_map/ppermute | solution.py:138
  131.4 1.4 collective-permute-start.48
  133.6 5.6 %collective-permute-start.49 = (bf16[64,1024]{1,0:T(8,128)(2,1)S(1)}, bf16[64,1024]{1,0:T(8,128)(2,1)S(1)}, u32[]{:S(2)}, u32[]{:S(2)}) collective-permute-start(bf16[64,1024]{1,0:T(8,128)(2,1)S(1)} %shard_map.76), channel_id=1, source_target_pairs={{0,4},{4,0},{8,12},{12,8},{1,5},{5,1},{9,13},{13,9},{2,6},{6,2},{1... | collective-permute-start | bytes 393224 | tf_op jit(solution)/shard_map/ppermute | solution.py:138
  134.0 9.0 %collective-permute-start.50 = (bf16[64,1024]{1,0:T(8,128)(2,1)S(1)}, bf16[64,1024]{1,0:T(8,128)(2,1)S(1)}, u32[]{:S(2)}, u32[]{:S(2)}) collective-permute-start(bf16[64,1024]{1,0:T(8,128)(2,1)S(1)} %fusion), channel_id=1, source_target_pairs={{12,0},{4,8},{13,1},{5,9},{14,2},{6,10},{15,3},{7,11},{28,16},{20,... | collective-permute-start | bytes 393224 | tf_op jit(solution)/shard_map/ppermute | solution.py:256
  139.2 5.7 %collective-permute-start.51 = (bf16[64,1024]{1,0:T(8,128)(2,1)S(1)}, bf16[64,1024]{1,0:T(8,128)(2,1)S(1)}, u32[]{:S(2)}, u32[]{:S(2)}) collective-permute-start(bf16[64,1024]{1,0:T(8,128)(2,1)S(1)} %fusion.1), channel_id=1, source_target_pairs={{8,4},{0,12},{9,5},{1,13},{10,6},{2,14},{11,7},{3,15},{24,20},{16,... | collective-permute-start | bytes 393224 | tf_op jit(solution)/shard_map/ppermute | solution.py:256
  142.6 2.4 %copy-start.2 = (bf16[5,1024,64]{1,2,0:T(8,128)(2,1)}, bf16[5,1024,64]{1,2,0:T(8,128)(2,1)S(1)}, u32[]{:S(2)}) copy-start(bf16[5,1024,64]{1,2,0:T(8,128)(2,1)S(1)} %bitcast_dynamic-update-slice_fusion) | copy-start | bytes 1966084

commit v13 on v12

--- a/solution.py
+++ b/solution.py
@@ -60,7 +60,7 @@
     width = keep.shape[0]
     x = right[...].T
     x = jnp.concatenate(
-        [x[g * width : (g + 1) * width] for g in (s, STREAMS + s)], axis=0
+        [x[unit_place(s, h) * width : (unit_place(s, h) + 1) * width] for h in range(2)], axis=0
     )
     product[...] = times_transposed(x, block[...])
     own = pl.multiple_of(side[0] * width, width)
@@ -89,7 +89,7 @@
 def turn_kernel(width, side, sides, out, turned):
     turned[...] = sides[0].T
     for s in range(STREAMS):
-        own = pl.multiple_of((STREAMS * side[0] + s) * width, width)
+        own = pl.multiple_of(unit_place(s, side[0]) * width, width)
         out[0, s] = turned[pl.ds(own, width)]
 
 
@@ -114,6 +114,10 @@
 
 def narrow(value):
     return value.astype(jnp.bfloat16)
+
+
+def unit_place(s, h):
+    return STREAMS * h + (h if s == 0 else 1 - h)
 
 
 class Order:
@@ -227,7 +231,7 @@
             st = state[s]
             if exact and step == last_step:
                 own, other = st["own"], st["swap"]
-                stays = core == (s ^ (place >> 1))
+                stays = core == s
                 st["own"], st["swap"] = jnp.where(stays, other, own), jnp.where(stays, own, other)
             leaving = order.run(
                 lambda block, x: product(block, [x], kind=jnp.bfloat16), inverses[step], st["own"]
@@ -252,7 +256,7 @@
 
         def final_cross(s):
             st = state[s]
-            pairs = [(r ^ (n_row - 1), r) for r in range(n_row) if r % STREAMS == s]
+            pairs = [(r ^ 2, r) for r in range(n_row) if r in [unit_place(s, h) for h in range(2)]]
             st["flight"] = lax.ppermute(st["leaving"], "row", pairs)
 
         def solve(s, step):
@@ -326,9 +330,9 @@
         for step in range(steps_total):
             if exact and step == last_step:
                 final_cross(1)
-                even = (place & 1) == 0
-                found = jnp.where(even, state[0]["total"], state[1]["total"])
-                found = found + wide(jnp.where(even, state[0]["flight"], state[1]["flight"]))
+                first_gives = ((place ^ (place >> 1)) & 1) == 0
+                found = jnp.where(first_gives, state[0]["total"], state[1]["total"])
+                found = found + wide(jnp.where(first_gives, state[0]["flight"], state[1]["flight"]))
                 found = narrow(found)
                 outputs.append(found.T)
                 continue
@@ -340,7 +344,7 @@
             found = solved[step][0][0]
             for s in range(STREAMS):
                 for u in range(2):
-                    found = jnp.where(unit == STREAMS * (u ^ side) + s, solved[step][s][u], found)
+                    found = jnp.where(unit == unit_place(s, u ^ side), solved[step][s][u], found)
             if not exact:
                 slot = angles // n_row
                 found = lax.dynamic_slice_in_dim(found, (place * slot) % width, slot, 0)

time: 146 us -> 146 us (level)
  transfers between devices with their start and end apart: 52 -> 52, of which waited for: 29 -> 29; matrix products, arithmetic and copies ran while one was open for 9% -> 10% of each run, Pallas kernels for 21% -> 21%
where the time goes in v13:
time: 146 us; the launch traced here: 145 us
  waiting for transfers between devices  48.5 us (33%)
  starting transfers between devices  43.7 us (30%)
  Pallas kernels  32.5 us (22%)
  local copies, waits for them, and re-layouts  17 us (12%)
  other arithmetic  2.25 us (2%)
    ppermute x50, waiting for transfers between devices, trade(): return lax.ppermute(value, axis, [(i, i ^ step) for i in range(size)])  46.1 us
    ppermute x50, starting transfers between devices, trade(): return lax.ppermute(value, axis, [(i, i ^ step) for i in range(size)])  40 us
    pallas_call x38, Pallas kernels, product(): pl.pallas_call(functools.partial(product_kernel, len(units)), out_shape=j...  29.9 us
    squeeze x16, local copies, waits for them, and re-layouts, block(): self.last = lax.optimization_barrier(self.run(lambda v: v[index], blocks))  14.9 us
    ppermute x2, starting transfers between devices, final_cross(): st['flight'] = lax.ppermute(st['leaving'], 'row', pairs)  3.64 us
  transfers between devices with their start and end apart: 52, of which 29 were waited for; matrix products, arithmetic and copies ran while one was open for 10% of the time, Pallas kernels for 21%

profile of v13, /device:TPU:0, one launch (start us, length us, event | category | flops | bytes accessed | tf_op | source)
XLA Modules:
  0.0 144.9 jit_solution(10757653200866308057)
XLA Ops:
  0.0 1.8 %slice_bitcast_fusion.14.block = bf16[1024,1024]{1,0:T(8,128)(2,1)S(1)} fusion(bf16[5,1024,1024]{2,1,0:T(8,128)(2,1)} %param.4), kind=kLoop, calls=%fused_computation.14 | loop fusion | bytes 4194304 | tf_op jit(solution)/shard_map/squeeze | solution.py:135
  1.8 1.1 slice_bitcast_fusion.15.right
  2.9 0.8 shard_map.37
  3.7 3.1 %collective-permute-start.1 = (bf16[64,1024]{1,0:T(8,128)(2,1)S(1)}, bf16[64,1024]{1,0:T(8,128)(2,1)S(1)}, u32[]{:S(2)}, u32[]{:S(2)}) collective-permute-start(bf16[64,1024]{1,0:T(8,128)(2,1)S(1)} %get-tuple-element.222), channel_id=1, source_target_pairs={{0,4},{4,0},{8,12},{12,8},{1,5},{5,1},{9,13},{13,9},{2,6},{6,2},{1... | collective-permute-start | bytes 393224 | tf_op jit(solution)/shard_map/ppermute | solution.py:142
  6.8 0.8 shard_map.38
  7.8 1.7 %copy-done = bf16[5,1024,256]{2,1,0:T(8,128)(2,1)S(1)} copy-done((bf16[5,1024,256]{2,1,0:T(8,128)(2,1)S(1)}, bf16[5,1024,256]{2,1,0:T(8,128)(2,1)}, u32[]{:S(2)}) %copy-start) | copy-done | bytes 2621464
  9.5 0.9 shard_map.39
  10.7 3.0 %collective-permute-start.2 = (bf16[64,1024]{1,0:T(8,128)(2,1)S(1)}, bf16[64,1024]{1,0:T(8,128)(2,1)S(1)}, u32[]{:S(2)}, u32[]{:S(2)}) collective-permute-start(bf16[64,1024]{1,0:T(8,128)(2,1)S(1)} %get-tuple-element.453), channel_id=1, source_target_pairs={{0,8},{4,12},{8,0},{12,4},{1,9},{5,13},{9,1},{13,5},{2,10},{6,14},... | collective-permute-start | bytes 393224 | tf_op jit(solution)/shard_map/ppermute | solution.py:142
  13.7 1.8 %slice_bitcast_fusion.13.block = bf16[1024,1024]{1,0:T(8,128)(2,1)S(1)} fusion(bf16[10,1024,1024]{2,1,0:T(8,128)(2,1)} %param.3), kind=kLoop, calls=%fused_computation.13 | loop fusion | bytes 4194304 | tf_op jit(solution)/shard_map/squeeze | solution.py:135
  15.5 3.9 %collective-permute-done.2 = bf16[64,1024]{1,0:T(8,128)(2,1)S(1)} collective-permute-done((bf16[64,1024]{1,0:T(8,128)(2,1)S(1)}, bf16[64,1024]{1,0:T(8,128)(2,1)S(1)}, u32[]{:S(2)}, u32[]{:S(2)}) %collective-permute-start.2) | collective-permute-done | bytes 131104 | tf_op jit(solution)/shard_map/ppermute | solution.py:142
  19.4 0.8 collective-permute-start.4
  21.1 3.4 %collective-permute-start.3 = (bf16[64,1024]{1,0:T(8,128)(2,1)S(1)}, bf16[64,1024]{1,0:T(8,128)(2,1)S(1)}, u32[]{:S(2)}, u32[]{:S(2)}) collective-permute-start(bf16[64,1024]{1,0:T(8,128)(2,1)S(1)} %get-tuple-element.451), channel_id=1, source_target_pairs={{0,8},{4,12},{8,0},{12,4},{1,9},{5,13},{9,1},{13,5},{2,10},{6,14},... | collective-permute-start | bytes 393224 | tf_op jit(solution)/shard_map/ppermute | solution.py:142
  25.4 1.6 %collective-permute-start.7 = (bf16[64,1024]{1,0:T(8,128)(2,1)S(1)}, bf16[64,1024]{1,0:T(8,128)(2,1)S(1)}, u32[]{:S(2)}, u32[]{:S(2)}) collective-permute-start(bf16[64,1024]{1,0:T(8,128)(2,1)S(1)} %get-tuple-element.449), channel_id=1, source_target_pairs={{0,2},{1,3},{2,0},{3,1},{4,6},{5,7},{6,4},{7,5},{8,10},{9,11},{10,... | collective-permute-start | bytes 393224 | tf_op jit(solution)/shard_map/ppermute | solution.py:142
  26.9 1.9 %slice_bitcast_fusion.12.block = bf16[1024,1024]{1,0:T(8,128)(2,1)S(1)} fusion(bf16[10,1024,1024]{2,1,0:T(8,128)(2,1)} %param.3), kind=kLoop, calls=%fused_computation.12 | loop fusion | bytes 4194304 | tf_op jit(solution)/shard_map/squeeze | solution.py:135
  28.8 1.8 %slice_bitcast_fusion.11.block = bf16[1024,1024]{1,0:T(8,128)(2,1)S(1)} fusion(bf16[5,1024,1024]{2,1,0:T(8,128)(2,1)} %param.4), kind=kLoop, calls=%fused_computation.11 | loop fusion | bytes 4194304 | tf_op jit(solution)/shard_map/squeeze | solution.py:135
  30.5 0.9 collective-permute-done.3
  34.1 1.7 %collective-permute-start.11 = (bf16[64,1024]{1,0:T(8,128)(2,1)S(1)}, bf16[64,1024]{1,0:T(8,128)(2,1)S(1)}, u32[]{:S(2)}, u32[]{:S(2)}) collective-permute-start(bf16[64,1024]{1,0:T(8,128)(2,1)S(1)} %shard_map.43), channel_id=1, source_target_pairs={{0,4},{4,0},{8,12},{12,8},{1,5},{5,1},{9,13},{13,9},{2,6},{6,2},{1... | collective-permute-start | bytes 393224 | tf_op jit(solution)/shard_map/ppermute | solution.py:142
  35.8 1.2 collective-permute-done.6.refs_0_.refs_2_
  37.9 1.6 %collective-permute-start.9 = (bf16[64,1024]{1,0:T(8,128)(2,1)S(1)}, bf16[64,1024]{1,0:T(8,128)(2,1)S(1)}, u32[]{:S(2)}, u32[]{:S(2)}) collective-permute-start(bf16[64,1024]{1,0:T(8,128)(2,1)S(1)} %get-tuple-element.447), channel_id=1, source_target_pairs={{0,2},{1,3},{2,0},{3,1},{4,6},{5,7},{6,4},{7,5},{8,10},{9,11},{10,... | collective-permute-start | bytes 393224 | tf_op jit(solution)/shard_map/ppermute | solution.py:142
  39.6 0.9 shard_map.45
  41.4 2.6 %collective-permute-start.14 = (bf16[64,1024]{1,0:T(8,128)(2,1)S(1)}, bf16[64,1024]{1,0:T(8,128)(2,1)S(1)}, u32[]{:S(2)}, u32[]{:S(2)}) collective-permute-start(bf16[64,1024]{1,0:T(8,128)(2,1)S(1)} %get-tuple-element.445), channel_id=1, source_target_pairs={{0,8},{4,12},{8,0},{12,4},{1,9},{5,13},{9,1},{13,5},{2,10},{6,14},... | collective-permute-start | bytes 393224 | tf_op jit(solution)/shard_map/ppermute | solution.py:142
  46.4 3.3 %collective-permute-done.14 = bf16[64,1024]{1,0:T(8,128)(2,1)S(1)} collective-permute-done((bf16[64,1024]{1,0:T(8,128)(2,1)S(1)}, bf16[64,1024]{1,0:T(8,128)(2,1)S(1)}, u32[]{:S(2)}, u32[]{:S(2)}) %collective-permute-start.14) | collective-permute-done | bytes 131104 | tf_op jit(solution)/shard_map/ppermute | solution.py:142
  50.7 1.8 %collective-permute-done.13 = bf16[64,1024]{1,0:T(8,128)(2,1)S(1)} collective-permute-done((bf16[64,1024]{1,0:T(8,128)(2,1)S(1)}, bf16[64,1024]{1,0:T(8,128)(2,1)S(1)}, u32[]{:S(2)}, u32[]{:S(2)}) %collective-permute-start.13) | collective-permute-done | bytes 131104 | tf_op jit(solution)/shard_map/ppermute | solution.py:142
  52.5 1.5 %collective-permute-start.15 = (bf16[64,1024]{1,0:T(8,128)(2,1)S(1)}, bf16[64,1024]{1,0:T(8,128)(2,1)S(1)}, u32[]{:S(2)}, u32[]{:S(2)}) collective-permute-start(bf16[64,1024]{1,0:T(8,128)(2,1)S(1)} %get-tuple-element.443), channel_id=1, source_target_pairs={{0,8},{4,12},{8,0},{12,4},{1,9},{5,13},{9,1},{13,5},{2,10},{6,14},... | collective-permute-start | bytes 393224 | tf_op jit(solution)/shard_map/ppermute | solution.py:142
  54.0 1.2 collective-permute-done.16.refs_0_
  56.8 0.9 shard_map.51.refs_4_
  57.9 1.8 %slice_bitcast_fusion.7.block = bf16[1024,1024]{1,0:T(8,128)(2,1)S(1)} fusion(bf16[5,1024,1024]{2,1,0:T(8,128)(2,1)} %param.4), kind=kLoop, calls=%fused_computation.7 | loop fusion | bytes 4194304 | tf_op jit(solution)/shard_map/squeeze | solution.py:135
  59.7 2.0 %collective-permute-done.15 = bf16[64,1024]{1,0:T(8,128)(2,1)S(1)} collective-permute-done((bf16[64,1024]{1,0:T(8,128)(2,1)S(1)}, bf16[64,1024]{1,0:T(8,128)(2,1)S(1)}, u32[]{:S(2)}, u32[]{:S(2)}) %collective-permute-start.15) | collective-permute-done | bytes 131104 | tf_op jit(solution)/shard_map/ppermute | solution.py:142
  61.8 0.8 shard_map.52
  64.0 2.1 %collective-permute-start.23 = (bf16[64,1024]{1,0:T(8,128)(2,1)S(1)}, bf16[64,1024]{1,0:T(8,128)(2,1)S(1)}, u32[]{:S(2)}, u32[]{:S(2)}) collective-permute-start(bf16[64,1024]{1,0:T(8,128)(2,1)S(1)} %shard_map.53), channel_id=1, source_target_pairs={{0,4},{4,0},{8,12},{12,8},{1,5},{5,1},{9,13},{13,9},{2,6},{6,2},{1... | collective-permute-start | bytes 393224 | tf_op jit(solution)/shard_map/ppermute | solution.py:142
  66.1 1.0 collective-permute-done.18.refs_0_.refs_2_
  68.6 0.9 shard_map.55
  69.5 1.0 shard_map.56
  70.6 1.9 %collective-permute-start.26 = (bf16[64,1024]{1,0:T(8,128)(2,1)S(1)}, bf16[64,1024]{1,0:T(8,128)(2,1)S(1)}, u32[]{:S(2)}, u32[]{:S(2)}) collective-permute-start(bf16[64,1024]{1,0:T(8,128)(2,1)S(1)} %get-tuple-element.437), channel_id=1, source_target_pairs={{0,8},{4,12},{8,0},{12,4},{1,9},{5,13},{9,1},{13,5},{2,10},{6,14},... | collective-permute-start | bytes 393224 | tf_op jit(solution)/shard_map/ppermute | solution.py:142
  74.0 0.8 collective-permute-start.25
  75.6 3.2 %collective-permute-done.26 = bf16[64,1024]{1,0:T(8,128)(2,1)S(1)} collective-permute-done((bf16[64,1024]{1,0:T(8,128)(2,1)S(1)}, bf16[64,1024]{1,0:T(8,128)(2,1)S(1)}, u32[]{:S(2)}, u32[]{:S(2)}) %collective-permute-start.26) | collective-permute-done | bytes 131104 | tf_op jit(solution)/shard_map/ppermute | solution.py:142
  79.8 1.8 %collective-permute-done.25 = bf16[64,1024]{1,0:T(8,128)(2,1)S(1)} collective-permute-done((bf16[64,1024]{1,0:T(8,128)(2,1)S(1)}, bf16[64,1024]{1,0:T(8,128)(2,1)S(1)}, u32[]{:S(2)}, u32[]{:S(2)}) %collective-permute-start.25) | collective-permute-done | bytes 131104 | tf_op jit(solution)/shard_map/ppermute | solution.py:142
  81.6 1.3 collective-permute-start.27
  82.8 1.5 %collective-permute-done.28.refs_0_ = bf16[64,1024]{1,0:T(8,128)(2,1)S(1)} collective-permute-done((bf16[64,1024]{1,0:T(8,128)(2,1)S(1)}, bf16[64,1024]{1,0:T(8,128)(2,1)S(1)}, u32[]{:S(2)}, u32[]{:S(2)}) %collective-permute-start.28) | collective-permute-done | bytes 131104 | tf_op jit(solution)/shard_map/ppermute | solution.py:142
  85.1 1.3 collective-permute-start.31
  86.6 0.9 shard_map.61.refs_4_
  87.7 0.9 shard_map.62.refs_4_
  88.7 1.8 %slice_bitcast_fusion.2.block = bf16[1024,1024]{1,0:T(8,128)(2,1)S(1)} fusion(bf16[5,1024,1024]{2,1,0:T(8,128)(2,1)} %param.4), kind=kLoop, calls=%fused_computation.2 | loop fusion | bytes 4194304 | tf_op jit(solution)/shard_map/squeeze | solution.py:135
  93.1 2.1 %collective-permute-start.35 = (bf16[64,1024]{1,0:T(8,128)(2,1)S(1)}, bf16[64,1024]{1,0:T(8,128)(2,1)S(1)}, u32[]{:S(2)}, u32[]{:S(2)}) collective-permute-start(bf16[64,1024]{1,0:T(8,128)(2,1)S(1)} %shard_map.64), channel_id=1, source_target_pairs={{0,4},{4,0},{8,12},{12,8},{1,5},{5,1},{9,13},{13,9},{2,6},{6,2},{1... | collective-permute-start | bytes 393224 | tf_op jit(solution)/shard_map/ppermute | solution.py:142
  95.2 1.0 collective-permute-done.30.refs_0_.refs_2_
  97.0 0.8 collective-permute-start.33
  98.0 0.9 shard_map.66
  99.8 1.5 %collective-permute-start.38 = (bf16[64,1024]{1,0:T(8,128)(2,1)S(1)}, bf16[64,1024]{1,0:T(8,128)(2,1)S(1)}, u32[]{:S(2)}, u32[]{:S(2)}) collective-permute-start(bf16[64,1024]{1,0:T(8,128)(2,1)S(1)} %get-tuple-element.429), channel_id=1, source_target_pairs={{0,8},{4,12},{8,0},{12,4},{1,9},{5,13},{9,1},{13,5},{2,10},{6,14},... | collective-permute-start | bytes 393224 | tf_op jit(solution)/shard_map/ppermute | solution.py:142
  101.3 0.8 collective-permute-done.33
  104.3 3.6 %collective-permute-done.38 = bf16[64,1024]{1,0:T(8,128)(2,1)S(1)} collective-permute-done((bf16[64,1024]{1,0:T(8,128)(2,1)S(1)}, bf16[64,1024]{1,0:T(8,128)(2,1)S(1)}, u32[]{:S(2)}, u32[]{:S(2)}) %collective-permute-start.38) | collective-permute-done | bytes 131104 | tf_op jit(solution)/shard_map/ppermute | solution.py:142
  108.0 0.8 shard_map.70
  108.9 1.8 %collective-permute-done.37 = bf16[64,1024]{1,0:T(8,128)(2,1)S(1)} collective-permute-done((bf16[64,1024]{1,0:T(8,128)(2,1)S(1)}, bf16[64,1024]{1,0:T(8,128)(2,1)S(1)}, u32[]{:S(2)}, u32[]{:S(2)}) %collective-permute-start.37) | collective-permute-done | bytes 131104 | tf_op jit(solution)/shard_map/ppermute | solution.py:142
  111.3 2.1 %collective-permute-done.40.refs_0_ = bf16[64,1024]{1,0:T(8,128)(2,1)S(1)} collective-permute-done((bf16[64,1024]{1,0:T(8,128)(2,1)S(1)}, bf16[64,1024]{1,0:T(8,128)(2,1)S(1)}, u32[]{:S(2)}, u32[]{:S(2)}) %collective-permute-start.40) | collective-permute-done | bytes 131104 | tf_op jit(solution)/shard_map/ppermute | solution.py:142
  114.2 1.0 collective-permute-start.42
  115.3 1.8 %slice_bitcast_fusion.block = bf16[1024,1024]{1,0:T(8,128)(2,1)S(1)} fusion(bf16[5,1024,1024]{2,1,0:T(8,128)(2,1)} %param.4), kind=kLoop, calls=%fused_computation | loop fusion | bytes 4194304 | tf_op jit(solution)/shard_map/squeeze | solution.py:135
  117.0 2.2 %collective-permute-done.42 = bf16[64,1024]{1,0:T(8,128)(2,1)S(1)} collective-permute-done((bf16[64,1024]{1,0:T(8,128)(2,1)S(1)}, bf16[64,1024]{1,0:T(8,128)(2,1)S(1)}, u32[]{:S(2)}, u32[]{:S(2)}) %collective-permute-start.42) | collective-permute-done | bytes 131104 | tf_op jit(solution)/shard_map/ppermute | solution.py:142
  121.5 3.8 %collective-permute-done.43.refs_0_ = bf16[64,1024]{1,0:T(8,128)(2,1)S(1)} collective-permute-done((bf16[64,1024]{1,0:T(8,128)(2,1)S(1)}, bf16[64,1024]{1,0:T(8,128)(2,1)S(1)}, u32[]{:S(2)}, u32[]{:S(2)}) %collective-permute-start.43) | collective-permute-done | bytes 131104 | tf_op jit(solution)/shard_map/ppermute | solution.py:142
  125.3 1.0 shard_map.73
  128.7 2.6 %collective-permute-done.47 = bf16[64,1024]{1,0:T(8,128)(2,1)S(1)} collective-permute-done((bf16[64,1024]{1,0:T(8,128)(2,1)S(1)}, bf16[64,1024]{1,0:T(8,128)(2,1)S(1)}, u32[]{:S(2)}, u32[]{:S(2)}) %collective-permute-start.47) | collective-permute-done | bytes 131104 | tf_op jit(solution)/shard_map/ppermute | solution.py:142
  131.5 1.2 collective-permute-done.46
  134.0 1.3 collective-permute-start.50
  136.1 3.1 %collective-permute-done.49 = bf16[64,1024]{1,0:T(8,128)(2,1)S(1)} collective-permute-done((bf16[64,1024]{1,0:T(8,128)(2,1)S(1)}, bf16[64,1024]{1,0:T(8,128)(2,1)S(1)}, u32[]{:S(2)}, u32[]{:S(2)}) %collective-permute-start.49) | collective-permute-done | bytes 131104 | tf_op jit(solution)/shard_map/ppermute | solution.py:142
  139.3 2.3 %collective-permute-start.51 = (bf16[64,1024]{1,0:T(8,128)(2,1)S(1)}, bf16[64,1024]{1,0:T(8,128)(2,1)S(1)}, u32[]{:S(2)}, u32[]{:S(2)}) collective-permute-start(bf16[64,1024]{1,0:T(8,128)(2,1)S(1)} %fusion.1), channel_id=1, source_target_pairs={{12,4},{0,8},{13,5},{1,9},{14,6},{2,10},{15,7},{3,11},{28,20},{16,... | collective-permute-start | bytes 393224 | tf_op jit(solution)/shard_map/ppermute | solution.py:260
  142.1 2.0 %collective-permute-done.51 = bf16[64,1024]{1,0:T(8,128)(2,1)S(1)} collective-permute-done((bf16[64,1024]{1,0:T(8,128)(2,1)S(1)}, bf16[64,1024]{1,0:T(8,128)(2,1)S(1)}, u32[]{:S(2)}, u32[]{:S(2)}) %collective-permute-start.51) | collective-permute-done | bytes 131104 | tf_op jit(solution)/shard_map/ppermute | solution.py:260
  (148 shorter events, 35.4 us)
Async XLA Ops:
  3.7 7.0 %collective-permute-start.1 = (bf16[64,1024]{1,0:T(8,128)(2,1)S(1)}, bf16[64,1024]{1,0:T(8,128)(2,1)S(1)}, u32[]{:S(2)}, u32[]{:S(2)}) collective-permute-start(bf16[64,1024]{1,0:T(8,128)(2,1)S(1)} %get-tuple-element.222), channel_id=1, source_target_pairs={{0,4},{4,0},{8,12},{12,8},{1,5},{5,1},{9,13},{13,9},{2,6},{6,2},{1... | collective-permute-start | bytes 393224 | tf_op jit(solution)/shard_map/ppermute | solution.py:142
  7.6 13.4 %collective-permute-start = (bf16[64,1024]{1,0:T(8,128)(2,1)S(1)}, bf16[64,1024]{1,0:T(8,128)(2,1)S(1)}, u32[]{:S(2)}, u32[]{:S(2)}) collective-permute-start(bf16[64,1024]{1,0:T(8,128)(2,1)S(1)} %get-tuple-element.221), channel_id=1, source_target_pairs={{0,4},{4,0},{8,12},{12,8},{1,5},{5,1},{9,13},{13,9},{2,6},{6,2},{1... | collective-permute-start | bytes 393224 | tf_op jit(solution)/shard_map/ppermute | solution.py:142
  7.7 1.7 %copy-start = (bf16[5,1024,256]{2,1,0:T(8,128)(2,1)S(1)}, bf16[5,1024,256]{2,1,0:T(8,128)(2,1)}, u32[]{:S(2)}) copy-start(bf16[5,1024,256]{2,1,0:T(8,128)(2,1)} %sides) | copy-start | bytes 7864324
  10.7 8.7 %collective-permute-start.2 = (bf16[64,1024]{1,0:T(8,128)(2,1)S(1)}, bf16[64,1024]{1,0:T(8,128)(2,1)S(1)}, u32[]{:S(2)}, u32[]{:S(2)}) collective-permute-start(bf16[64,1024]{1,0:T(8,128)(2,1)S(1)} %get-tuple-element.453), channel_id=1, source_target_pairs={{0,8},{4,12},{8,0},{12,4},{1,9},{5,13},{9,1},{13,5},{2,10},{6,14},... | collective-permute-start | bytes 393224 | tf_op jit(solution)/shard_map/ppermute | solution.py:142
  19.4 5.1 %collective-permute-start.4 = (bf16[64,1024]{1,0:T(8,128)(2,1)S(1)}, bf16[64,1024]{1,0:T(8,128)(2,1)S(1)}, u32[]{:S(2)}, u32[]{:S(2)}) collective-permute-start(bf16[64,1024]{1,0:T(8,128)(2,1)S(1)} %add_convert_fusion.8.refs_0_.refs_1_), channel_id=1, source_target_pairs={{0,4},{4,0},{8,12},{12,8},{1,5},{5,1},{9,13},{13,9},{2,6},{6,2},{1... | collective-permute-start | bytes 393224 | tf_op jit(solution)/shard_map/ppermute | solution.py:142
  20.9 4.4 %collective-permute-start.5 = (bf16[64,1024]{1,0:T(8,128)(2,1)S(1)}, bf16[64,1024]{1,0:T(8,128)(2,1)S(1)}, u32[]{:S(2)}, u32[]{:S(2)}) collective-permute-start(bf16[64,1024]{1,0:T(8,128)(2,1)S(1)} %shard_map.40), channel_id=1, source_target_pairs={{0,1},{1,0},{2,3},{3,2},{4,5},{5,4},{6,7},{7,6},{8,9},{9,8},{10,11... | collective-permute-start | bytes 393224 | tf_op jit(solution)/shard_map/ppermute | solution.py:142
  21.0 18.4 %copy-start.1 = (bf16[10,1024,1024]{2,1,0:T(8,128)(2,1)S(1)}, bf16[10,1024,1024]{2,1,0:T(8,128)(2,1)}, u32[]{:S(2)}) copy-start(bf16[10,1024,1024]{2,1,0:T(8,128)(2,1)} %param.3) | copy-start | bytes 62914564
  21.1 10.4 %collective-permute-start.3 = (bf16[64,1024]{1,0:T(8,128)(2,1)S(1)}, bf16[64,1024]{1,0:T(8,128)(2,1)S(1)}, u32[]{:S(2)}, u32[]{:S(2)}) collective-permute-start(bf16[64,1024]{1,0:T(8,128)(2,1)S(1)} %get-tuple-element.451), channel_id=1, source_target_pairs={{0,8},{4,12},{8,0},{12,4},{1,9},{5,13},{9,1},{13,5},{2,10},{6,14},... | collective-permute-start | bytes 393224 | tf_op jit(solution)/shard_map/ppermute | solution.py:142
  25.4 7.4 %collective-permute-start.7 = (bf16[64,1024]{1,0:T(8,128)(2,1)S(1)}, bf16[64,1024]{1,0:T(8,128)(2,1)S(1)}, u32[]{:S(2)}, u32[]{:S(2)}) collective-permute-start(bf16[64,1024]{1,0:T(8,128)(2,1)S(1)} %get-tuple-element.449), channel_id=1, source_target_pairs={{0,2},{1,3},{2,0},{3,1},{4,6},{5,7},{6,4},{7,5},{8,10},{9,11},{10,... | collective-permute-start | bytes 393224 | tf_op jit(solution)/shard_map/ppermute | solution.py:142
  31.5 5.5 %collective-permute-start.6 = (bf16[64,1024]{1,0:T(8,128)(2,1)S(1)}, bf16[64,1024]{1,0:T(8,128)(2,1)S(1)}, u32[]{:S(2)}, u32[]{:S(2)}) collective-permute-start(bf16[64,1024]{1,0:T(8,128)(2,1)S(1)} %add_convert_fusion.7.refs_0_.refs_3_), channel_id=1, source_target_pairs={{0,4},{4,0},{8,12},{12,8},{1,5},{5,1},{9,13},{13,9},{2,6},{6,2},{1... | collective-permute-start | bytes 393224 | tf_op jit(solution)/shard_map/ppermute | solution.py:142
  32.7 5.1 %collective-permute-start.8 = (bf16[64,1024]{1,0:T(8,128)(2,1)S(1)}, bf16[64,1024]{1,0:T(8,128)(2,1)S(1)}, u32[]{:S(2)}, u32[]{:S(2)}) collective-permute-start(bf16[64,1024]{1,0:T(8,128)(2,1)S(1)} %shard_map.42), channel_id=1, source_target_pairs={{0,1},{1,0},{2,3},{3,2},{4,5},{5,4},{6,7},{7,6},{8,9},{9,8},{10,11... | collective-permute-start | bytes 393224 | tf_op jit(solution)/shard_map/ppermute | solution.py:142
  32.8 7.7 %collective-permute-start.10 = (bf16[64,1024]{1,0:T(8,128)(2,1)S(1)}, bf16[64,1024]{1,0:T(8,128)(2,1)S(1)}, u32[]{:S(2)}, u32[]{:S(2)}) collective-permute-start(bf16[64,1024]{1,0:T(8,128)(2,1)S(1)} %subtract_convert_fusion.7.refs_0_), channel_id=1, source_target_pairs={{0,1},{1,0},{2,3},{3,2},{4,5},{5,4},{6,7},{7,6},{8,9},{9,8},{10,11... | collective-permute-start | bytes 393224 | tf_op jit(solution)/shard_map/ppermute | solution.py:142
  34.1 7.2 %collective-permute-start.11 = (bf16[64,1024]{1,0:T(8,128)(2,1)S(1)}, bf16[64,1024]{1,0:T(8,128)(2,1)S(1)}, u32[]{:S(2)}, u32[]{:S(2)}) collective-permute-start(bf16[64,1024]{1,0:T(8,128)(2,1)S(1)} %shard_map.43), channel_id=1, source_target_pairs={{0,4},{4,0},{8,12},{12,8},{1,5},{5,1},{9,13},{13,9},{2,6},{6,2},{1... | collective-permute-start | bytes 393224 | tf_op jit(solution)/shard_map/ppermute | solution.py:142
  37.9 6.1 %collective-permute-start.9 = (bf16[64,1024]{1,0:T(8,128)(2,1)S(1)}, bf16[64,1024]{1,0:T(8,128)(2,1)S(1)}, u32[]{:S(2)}, u32[]{:S(2)}) collective-permute-start(bf16[64,1024]{1,0:T(8,128)(2,1)S(1)} %get-tuple-element.447), channel_id=1, source_target_pairs={{0,2},{1,3},{2,0},{3,1},{4,6},{5,7},{6,4},{7,5},{8,10},{9,11},{10,... | collective-permute-start | bytes 393224 | tf_op jit(solution)/shard_map/ppermute | solution.py:142
  41.4 8.3 %collective-permute-start.14 = (bf16[64,1024]{1,0:T(8,128)(2,1)S(1)}, bf16[64,1024]{1,0:T(8,128)(2,1)S(1)}, u32[]{:S(2)}, u32[]{:S(2)}) collective-permute-start(bf16[64,1024]{1,0:T(8,128)(2,1)S(1)} %get-tuple-element.445), channel_id=1, source_target_pairs={{0,8},{4,12},{8,0},{12,4},{1,9},{5,13},{9,1},{13,5},{2,10},{6,14},... | collective-permute-start | bytes 393224 | tf_op jit(solution)/shard_map/ppermute | solution.py:142
  44.0 1.6 %collective-permute-start.12 = (bf16[64,1024]{1,0:T(8,128)(2,1)S(1)}, bf16[64,1024]{1,0:T(8,128)(2,1)S(1)}, u32[]{:S(2)}, u32[]{:S(2)}) collective-permute-start(bf16[64,1024]{1,0:T(8,128)(2,1)S(1)} %subtract_convert_fusion.6.refs_0_), channel_id=1, source_target_pairs={{0,1},{1,0},{2,3},{3,2},{4,5},{5,4},{6,7},{7,6},{8,9},{9,8},{10,11... | collective-permute-start | bytes 393224 | tf_op jit(solution)/shard_map/ppermute | solution.py:142
  44.9 7.6 %collective-permute-start.13 = (bf16[64,1024]{1,0:T(8,128)(2,1)S(1)}, bf16[64,1024]{1,0:T(8,128)(2,1)S(1)}, u32[]{:S(2)}, u32[]{:S(2)}) collective-permute-start(bf16[64,1024]{1,0:T(8,128)(2,1)S(1)} %shard_map.47), channel_id=1, source_target_pairs={{0,4},{4,0},{8,12},{12,8},{1,5},{5,1},{9,13},{13,9},{2,6},{6,2},{1... | collective-permute-start | bytes 393224 | tf_op jit(solution)/shard_map/ppermute | solution.py:142
  49.7 5.5 %collective-permute-start.16 = (bf16[64,1024]{1,0:T(8,128)(2,1)S(1)}, bf16[64,1024]{1,0:T(8,128)(2,1)S(1)}, u32[]{:S(2)}, u32[]{:S(2)}) collective-permute-start(bf16[64,1024]{1,0:T(8,128)(2,1)S(1)} %add_convert_fusion.6.refs_0_.refs_1_), channel_id=1, source_target_pairs={{0,4},{4,0},{8,12},{12,8},{1,5},{5,1},{9,13},{13,9},{2,6},{6,2},{1... | collective-permute-start | bytes 393224 | tf_op jit(solution)/shard_map/ppermute | solution.py:142
  50.6 5.4 %collective-permute-start.17 = (bf16[64,1024]{1,0:T(8,128)(2,1)S(1)}, bf16[64,1024]{1,0:T(8,128)(2,1)S(1)}, u32[]{:S(2)}, u32[]{:S(2)}) collective-permute-start(bf16[64,1024]{1,0:T(8,128)(2,1)S(1)} %shard_map.49), channel_id=1, source_target_pairs={{0,1},{1,0},{2,3},{3,2},{4,5},{5,4},{6,7},{7,6},{8,9},{9,8},{10,11... | collective-permute-start | bytes 393224 | tf_op jit(solution)/shard_map/ppermute | solution.py:142
  52.5 9.2 %collective-permute-start.15 = (bf16[64,1024]{1,0:T(8,128)(2,1)S(1)}, bf16[64,1024]{1,0:T(8,128)(2,1)S(1)}, u32[]{:S(2)}, u32[]{:S(2)}) collective-permute-start(bf16[64,1024]{1,0:T(8,128)(2,1)S(1)} %get-tuple-element.443), channel_id=1, source_target_pairs={{0,8},{4,12},{8,0},{12,4},{1,9},{5,13},{9,1},{13,5},{2,10},{6,14},... | collective-permute-start | bytes 393224 | tf_op jit(solution)/shard_map/ppermute | solution.py:142
  56.1 6.6 %collective-permute-start.19 = (bf16[64,1024]{1,0:T(8,128)(2,1)S(1)}, bf16[64,1024]{1,0:T(8,128)(2,1)S(1)}, u32[]{:S(2)}, u32[]{:S(2)}) collective-permute-start(bf16[64,1024]{1,0:T(8,128)(2,1)S(1)} %get-tuple-element.441), channel_id=1, source_target_pairs={{0,2},{1,3},{2,0},{3,1},{4,6},{5,7},{6,4},{7,5},{8,10},{9,11},{10,... | collective-permute-start | bytes 393224 | tf_op jit(solution)/shard_map/ppermute | solution.py:142
  61.7 5.4 %collective-permute-start.18 = (bf16[64,1024]{1,0:T(8,128)(2,1)S(1)}, bf16[64,1024]{1,0:T(8,128)(2,1)S(1)}, u32[]{:S(2)}, u32[]{:S(2)}) collective-permute-start(bf16[64,1024]{1,0:T(8,128)(2,1)S(1)} %add_convert_fusion.5.refs_0_.refs_3_), channel_id=1, source_target_pairs={{0,4},{4,0},{8,12},{12,8},{1,5},{5,1},{9,13},{13,9},{2,6},{6,2},{1... | collective-permute-start | bytes 393224 | tf_op jit(solution)/shard_map/ppermute | solution.py:142
  62.6 5.3 %collective-permute-start.20 = (bf16[64,1024]{1,0:T(8,128)(2,1)S(1)}, bf16[64,1024]{1,0:T(8,128)(2,1)S(1)}, u32[]{:S(2)}, u32[]{:S(2)}) collective-permute-start(bf16[64,1024]{1,0:T(8,128)(2,1)S(1)} %shard_map.52), channel_id=1, source_target_pairs={{0,1},{1,0},{2,3},{3,2},{4,5},{5,4},{6,7},{7,6},{8,9},{9,8},{10,11... | collective-permute-start | bytes 393224 | tf_op jit(solution)/shard_map/ppermute | solution.py:142
  62.7 6.8 %collective-permute-start.22 = (bf16[64,1024]{1,0:T(8,128)(2,1)S(1)}, bf16[64,1024]{1,0:T(8,128)(2,1)S(1)}, u32[]{:S(2)}, u32[]{:S(2)}) collective-permute-start(bf16[64,1024]{1,0:T(8,128)(2,1)S(1)} %subtract_convert_fusion.5.refs_0_), channel_id=1, source_target_pairs={{0,1},{1,0},{2,3},{3,2},{4,5},{5,4},{6,7},{7,6},{8,9},{9,8},{10,11... | collective-permute-start | bytes 393224 | tf_op jit(solution)/shard_map/ppermute | solution.py:142
  64.0 6.5 %collective-permute-start.23 = (bf16[64,1024]{1,0:T(8,128)(2,1)S(1)}, bf16[64,1024]{1,0:T(8,128)(2,1)S(1)}, u32[]{:S(2)}, u32[]{:S(2)}) collective-permute-start(bf16[64,1024]{1,0:T(8,128)(2,1)S(1)} %shard_map.53), channel_id=1, source_target_pairs={{0,4},{4,0},{8,12},{12,8},{1,5},{5,1},{9,13},{13,9},{2,6},{6,2},{1... | collective-permute-start | bytes 393224 | tf_op jit(solution)/shard_map/ppermute | solution.py:142
  67.9 5.0 %collective-permute-start.21 = (bf16[64,1024]{1,0:T(8,128)(2,1)S(1)}, bf16[64,1024]{1,0:T(8,128)(2,1)S(1)}, u32[]{:S(2)}, u32[]{:S(2)}) collective-permute-start(bf16[64,1024]{1,0:T(8,128)(2,1)S(1)} %get-tuple-element.439), channel_id=1, source_target_pairs={{0,2},{1,3},{2,0},{3,1},{4,6},{5,7},{6,4},{7,5},{8,10},{9,11},{10,... | collective-permute-start | bytes 393224 | tf_op jit(solution)/shard_map/ppermute | solution.py:142
  70.6 8.2 %collective-permute-start.26 = (bf16[64,1024]{1,0:T(8,128)(2,1)S(1)}, bf16[64,1024]{1,0:T(8,128)(2,1)S(1)}, u32[]{:S(2)}, u32[]{:S(2)}) collective-permute-start(bf16[64,1024]{1,0:T(8,128)(2,1)S(1)} %get-tuple-element.437), channel_id=1, source_target_pairs={{0,8},{4,12},{8,0},{12,4},{1,9},{5,13},{9,1},{13,5},{2,10},{6,14},... | collective-permute-start | bytes 393224 | tf_op jit(solution)/shard_map/ppermute | solution.py:142
  73.0 1.8 %collective-permute-start.24 = (bf16[64,1024]{1,0:T(8,128)(2,1)S(1)}, bf16[64,1024]{1,0:T(8,128)(2,1)S(1)}, u32[]{:S(2)}, u32[]{:S(2)}) collective-permute-start(bf16[64,1024]{1,0:T(8,128)(2,1)S(1)} %subtract_convert_fusion.4.refs_0_), channel_id=1, source_target_pairs={{0,1},{1,0},{2,3},{3,2},{4,5},{5,4},{6,7},{7,6},{8,9},{9,8},{10,11... | collective-permute-start | bytes 393224 | tf_op jit(solution)/shard_map/ppermute | solution.py:142
  74.0 7.6 %collective-permute-start.25 = (bf16[64,1024]{1,0:T(8,128)(2,1)S(1)}, bf16[64,1024]{1,0:T(8,128)(2,1)S(1)}, u32[]{:S(2)}, u32[]{:S(2)}) collective-permute-start(bf16[64,1024]{1,0:T(8,128)(2,1)S(1)} %shard_map.57), channel_id=1, source_target_pairs={{0,4},{4,0},{8,12},{12,8},{1,5},{5,1},{9,13},{13,9},{2,6},{6,2},{1... | collective-permute-start | bytes 393224 | tf_op jit(solution)/shard_map/ppermute | solution.py:142
  78.8 5.5 %collective-permute-start.28 = (bf16[64,1024]{1,0:T(8,128)(2,1)S(1)}, bf16[64,1024]{1,0:T(8,128)(2,1)S(1)}, u32[]{:S(2)}, u32[]{:S(2)}) collective-permute-start(bf16[64,1024]{1,0:T(8,128)(2,1)S(1)} %add_convert_fusion.4.refs_0_.refs_1_), channel_id=1, source_target_pairs={{0,4},{4,0},{8,12},{12,8},{1,5},{5,1},{9,13},{13,9},{2,6},{6,2},{1... | collective-permute-start | bytes 393224 | tf_op jit(solution)/shard_map/ppermute | solution.py:142
  79.7 5.4 %collective-permute-start.29 = (bf16[64,1024]{1,0:T(8,128)(2,1)S(1)}, bf16[64,1024]{1,0:T(8,128)(2,1)S(1)}, u32[]{:S(2)}, u32[]{:S(2)}) collective-permute-start(bf16[64,1024]{1,0:T(8,128)(2,1)S(1)} %shard_map.59), channel_id=1, source_target_pairs={{0,1},{1,0},{2,3},{3,2},{4,5},{5,4},{6,7},{7,6},{8,9},{9,8},{10,11... | collective-permute-start | bytes 393224 | tf_op jit(solution)/shard_map/ppermute | solution.py:142
  81.6 9.2 %collective-permute-start.27 = (bf16[64,1024]{1,0:T(8,128)(2,1)S(1)}, bf16[64,1024]{1,0:T(8,128)(2,1)S(1)}, u32[]{:S(2)}, u32[]{:S(2)}) collective-permute-start(bf16[64,1024]{1,0:T(8,128)(2,1)S(1)} %get-tuple-element.435), channel_id=1, source_target_pairs={{0,8},{4,12},{8,0},{12,4},{1,9},{5,13},{9,1},{13,5},{2,10},{6,14},... | collective-permute-start | bytes 393224 | tf_op jit(solution)/shard_map/ppermute | solution.py:142
  85.1 6.6 %collective-permute-start.31 = (bf16[64,1024]{1,0:T(8,128)(2,1)S(1)}, bf16[64,1024]{1,0:T(8,128)(2,1)S(1)}, u32[]{:S(2)}, u32[]{:S(2)}) collective-permute-start(bf16[64,1024]{1,0:T(8,128)(2,1)S(1)} %get-tuple-element.433), channel_id=1, source_target_pairs={{0,2},{1,3},{2,0},{3,1},{4,6},{5,7},{6,4},{7,5},{8,10},{9,11},{10,... | collective-permute-start | bytes 393224 | tf_op jit(solution)/shard_map/ppermute | solution.py:142
  90.8 5.4 %collective-permute-start.30 = (bf16[64,1024]{1,0:T(8,128)(2,1)S(1)}, bf16[64,1024]{1,0:T(8,128)(2,1)S(1)}, u32[]{:S(2)}, u32[]{:S(2)}) collective-permute-start(bf16[64,1024]{1,0:T(8,128)(2,1)S(1)} %add_convert_fusion.3.refs_0_.refs_3_), channel_id=1, source_target_pairs={{0,4},{4,0},{8,12},{12,8},{1,5},{5,1},{9,13},{13,9},{2,6},{6,2},{1... | collective-permute-start | bytes 393224 | tf_op jit(solution)/shard_map/ppermute | solution.py:142
  91.7 5.3 %collective-permute-start.32 = (bf16[64,1024]{1,0:T(8,128)(2,1)S(1)}, bf16[64,1024]{1,0:T(8,128)(2,1)S(1)}, u32[]{:S(2)}, u32[]{:S(2)}) collective-permute-start(bf16[64,1024]{1,0:T(8,128)(2,1)S(1)} %shard_map.63), channel_id=1, source_target_pairs={{0,1},{1,0},{2,3},{3,2},{4,5},{5,4},{6,7},{7,6},{8,9},{9,8},{10,11... | collective-permute-start | bytes 393224 | tf_op jit(solution)/shard_map/ppermute | solution.py:142
  91.8 7.1 %collective-permute-start.34 = (bf16[64,1024]{1,0:T(8,128)(2,1)S(1)}, bf16[64,1024]{1,0:T(8,128)(2,1)S(1)}, u32[]{:S(2)}, u32[]{:S(2)}) collective-permute-start(bf16[64,1024]{1,0:T(8,128)(2,1)S(1)} %subtract_convert_fusion.3.refs_0_), channel_id=1, source_target_pairs={{0,1},{1,0},{2,3},{3,2},{4,5},{5,4},{6,7},{7,6},{8,9},{9,8},{10,11... | collective-permute-start | bytes 393224 | tf_op jit(solution)/shard_map/ppermute | solution.py:142
  93.1 6.6 %collective-permute-start.35 = (bf16[64,1024]{1,0:T(8,128)(2,1)S(1)}, bf16[64,1024]{1,0:T(8,128)(2,1)S(1)}, u32[]{:S(2)}, u32[]{:S(2)}) collective-permute-start(bf16[64,1024]{1,0:T(8,128)(2,1)S(1)} %shard_map.64), channel_id=1, source_target_pairs={{0,4},{4,0},{8,12},{12,8},{1,5},{5,1},{9,13},{13,9},{2,6},{6,2},{1... | collective-permute-start | bytes 393224 | tf_op jit(solution)/shard_map/ppermute | solution.py:142
  97.0 5.0 %collective-permute-start.33 = (bf16[64,1024]{1,0:T(8,128)(2,1)S(1)}, bf16[64,1024]{1,0:T(8,128)(2,1)S(1)}, u32[]{:S(2)}, u32[]{:S(2)}) collective-permute-start(bf16[64,1024]{1,0:T(8,128)(2,1)S(1)} %get-tuple-element.431), channel_id=1, source_target_pairs={{0,2},{1,3},{2,0},{3,1},{4,6},{5,7},{6,4},{7,5},{8,10},{9,11},{10,... | collective-permute-start | bytes 393224 | tf_op jit(solution)/shard_map/ppermute | solution.py:142
  99.8 8.1 %collective-permute-start.38 = (bf16[64,1024]{1,0:T(8,128)(2,1)S(1)}, bf16[64,1024]{1,0:T(8,128)(2,1)S(1)}, u32[]{:S(2)}, u32[]{:S(2)}) collective-permute-start(bf16[64,1024]{1,0:T(8,128)(2,1)S(1)} %get-tuple-element.429), channel_id=1, source_target_pairs={{0,8},{4,12},{8,0},{12,4},{1,9},{5,13},{9,1},{13,5},{2,10},{6,14},... | collective-permute-start | bytes 393224 | tf_op jit(solution)/shard_map/ppermute | solution.py:142
  102.1 1.4 collective-permute-start.36
  103.0 7.6 %collective-permute-start.37 = (bf16[64,1024]{1,0:T(8,128)(2,1)S(1)}, bf16[64,1024]{1,0:T(8,128)(2,1)S(1)}, u32[]{:S(2)}, u32[]{:S(2)}) collective-permute-start(bf16[64,1024]{1,0:T(8,128)(2,1)S(1)} %shard_map.68), channel_id=1, source_target_pairs={{0,4},{4,0},{8,12},{12,8},{1,5},{5,1},{9,13},{13,9},{2,6},{6,2},{1... | collective-permute-start | bytes 393224 | tf_op jit(solution)/shard_map/ppermute | solution.py:142
  107.9 5.5 %collective-permute-start.40 = (bf16[64,1024]{1,0:T(8,128)(2,1)S(1)}, bf16[64,1024]{1,0:T(8,128)(2,1)S(1)}, u32[]{:S(2)}, u32[]{:S(2)}) collective-permute-start(bf16[64,1024]{1,0:T(8,128)(2,1)S(1)} %add_convert_fusion.2.refs_0_), channel_id=1, source_target_pairs={{0,4},{4,0},{8,12},{12,8},{1,5},{5,1},{9,13},{13,9},{2,6},{6,2},{1... | collective-permute-start | bytes 393224 | tf_op jit(solution)/shard_map/ppermute | solution.py:142
  108.8 5.4 %collective-permute-start.41 = (bf16[64,1024]{1,0:T(8,128)(2,1)S(1)}, bf16[64,1024]{1,0:T(8,128)(2,1)S(1)}, u32[]{:S(2)}, u32[]{:S(2)}) collective-permute-start(bf16[64,1024]{1,0:T(8,128)(2,1)S(1)} %shard_map.70), channel_id=1, source_target_pairs={{0,1},{1,0},{2,3},{3,2},{4,5},{5,4},{6,7},{7,6},{8,9},{9,8},{10,11... | collective-permute-start | bytes 393224 | tf_op jit(solution)/shard_map/ppermute | solution.py:142
  110.7 9.2 %collective-permute-start.39 = (bf16[64,1024]{1,0:T(8,128)(2,1)S(1)}, bf16[64,1024]{1,0:T(8,128)(2,1)S(1)}, u32[]{:S(2)}, u32[]{:S(2)}) collective-permute-start(bf16[64,1024]{1,0:T(8,128)(2,1)S(1)} %get-tuple-element.427), channel_id=1, source_target_pairs={{0,8},{4,12},{8,0},{12,4},{1,9},{5,13},{9,1},{13,5},{2,10},{6,14},... | collective-permute-start | bytes 393224 | tf_op jit(solution)/shard_map/ppermute | solution.py:142
  114.2 5.0 %collective-permute-start.42 = (bf16[64,1024]{1,0:T(8,128)(2,1)S(1)}, bf16[64,1024]{1,0:T(8,128)(2,1)S(1)}, u32[]{:S(2)}, u32[]{:S(2)}) collective-permute-start(bf16[64,1024]{1,0:T(8,128)(2,1)S(1)} %get-tuple-element.425), channel_id=1, source_target_pairs={{0,2},{1,3},{2,0},{3,1},{4,6},{5,7},{6,4},{7,5},{8,10},{9,11},{10,... | collective-permute-start | bytes 393224 | tf_op jit(solution)/shard_map/ppermute | solution.py:142
  119.9 5.3 %collective-permute-start.43 = (bf16[64,1024]{1,0:T(8,128)(2,1)S(1)}, bf16[64,1024]{1,0:T(8,128)(2,1)S(1)}, u32[]{:S(2)}, u32[]{:S(2)}) collective-permute-start(bf16[64,1024]{1,0:T(8,128)(2,1)S(1)} %add_convert_fusion.1.refs_0_), channel_id=1, source_target_pairs={{0,4},{4,0},{8,12},{12,8},{1,5},{5,1},{9,13},{13,9},{2,6},{6,2},{1... | collective-permute-start | bytes 393224 | tf_op jit(solution)/shard_map/ppermute | solution.py:142
  120.8 5.5 %collective-permute-start.45 = (bf16[64,1024]{1,0:T(8,128)(2,1)S(1)}, bf16[64,1024]{1,0:T(8,128)(2,1)S(1)}, u32[]{:S(2)}, u32[]{:S(2)}) collective-permute-start(bf16[64,1024]{1,0:T(8,128)(2,1)S(1)} %shard_map.72), channel_id=1, source_target_pairs={{0,1},{1,0},{2,3},{3,2},{4,5},{5,4},{6,7},{7,6},{8,9},{9,8},{10,11... | collective-permute-start | bytes 393224 | tf_op jit(solution)/shard_map/ppermute | solution.py:142
  120.9 6.0 %collective-permute-start.44 = (bf16[64,1024]{1,0:T(8,128)(2,1)S(1)}, bf16[64,1024]{1,0:T(8,128)(2,1)S(1)}, u32[]{:S(2)}, u32[]{:S(2)}) collective-permute-start(bf16[64,1024]{1,0:T(8,128)(2,1)S(1)} %subtract_convert_fusion.1), channel_id=1, source_target_pairs={{0,1},{1,0},{2,3},{3,2},{4,5},{5,4},{6,7},{7,6},{8,9},{9,8},{10,11... | collective-permute-start | bytes 393224 | tf_op jit(solution)/shard_map/ppermute | solution.py:142
  126.3 5.0 %collective-permute-start.47 = (bf16[64,1024]{1,0:T(8,128)(2,1)S(1)}, bf16[64,1024]{1,0:T(8,128)(2,1)S(1)}, u32[]{:S(2)}, u32[]{:S(2)}) collective-permute-start(bf16[64,1024]{1,0:T(8,128)(2,1)S(1)} %get-tuple-element.423), channel_id=1, source_target_pairs={{0,2},{1,3},{2,0},{3,1},{4,6},{5,7},{6,4},{7,5},{8,10},{9,11},{10,... | collective-permute-start | bytes 393224 | tf_op jit(solution)/shard_map/ppermute | solution.py:142
  127.7 5.0 %collective-permute-start.46 = (bf16[64,1024]{1,0:T(8,128)(2,1)S(1)}, bf16[64,1024]{1,0:T(8,128)(2,1)S(1)}, u32[]{:S(2)}, u32[]{:S(2)}) collective-permute-start(bf16[64,1024]{1,0:T(8,128)(2,1)S(1)} %shard_map.74), channel_id=1, source_target_pairs={{0,4},{4,0},{8,12},{12,8},{1,5},{5,1},{9,13},{13,9},{2,6},{6,2},{1... | collective-permute-start | bytes 393224 | tf_op jit(solution)/shard_map/ppermute | solution.py:142
  131.4 1.4 collective-permute-start.48
  133.6 5.6 %collective-permute-start.49 = (bf16[64,1024]{1,0:T(8,128)(2,1)S(1)}, bf16[64,1024]{1,0:T(8,128)(2,1)S(1)}, u32[]{:S(2)}, u32[]{:S(2)}) collective-permute-start(bf16[64,1024]{1,0:T(8,128)(2,1)S(1)} %shard_map.76), channel_id=1, source_target_pairs={{0,4},{4,0},{8,12},{12,8},{1,5},{5,1},{9,13},{13,9},{2,6},{6,2},{1... | collective-permute-start | bytes 393224 | tf_op jit(solution)/shard_map/ppermute | solution.py:142
  134.0 8.1 %collective-permute-start.50 = (bf16[64,1024]{1,0:T(8,128)(2,1)S(1)}, bf16[64,1024]{1,0:T(8,128)(2,1)S(1)}, u32[]{:S(2)}, u32[]{:S(2)}) collective-permute-start(bf16[64,1024]{1,0:T(8,128)(2,1)S(1)} %fusion), channel_id=1, source_target_pairs={{8,0},{4,12},{9,1},{5,13},{10,2},{6,14},{11,3},{7,15},{24,16},{20,... | collective-permute-start | bytes 393224 | tf_op jit(solution)/shard_map/ppermute | solution.py:260
  139.3 4.9 %collective-permute-start.51 = (bf16[64,1024]{1,0:T(8,128)(2,1)S(1)}, bf16[64,1024]{1,0:T(8,128)(2,1)S(1)}, u32[]{:S(2)}, u32[]{:S(2)}) collective-permute-start(bf16[64,1024]{1,0:T(8,128)(2,1)S(1)} %fusion.1), channel_id=1, source_target_pairs={{12,4},{0,8},{13,5},{1,9},{14,6},{2,10},{15,7},{3,11},{28,20},{16,... | collective-permute-start | bytes 393224 | tf_op jit(solution)/shard_map/ppermute | solution.py:260
  141.7 2.4 %copy-start.2 = (bf16[5,1024,64]{1,2,0:T(8,128)(2,1)}, bf16[5,1024,64]{1,2,0:T(8,128)(2,1)S(1)}, u32[]{:S(2)}) copy-start(bf16[5,1024,64]{1,2,0:T(8,128)(2,1)S(1)} %bitcast_dynamic-update-slice_fusion) | copy-start | bytes 1966084

commit v14 on v13

--- a/solution.py
+++ b/solution.py
@@ -56,9 +56,9 @@
     )(block, *units, *rest)
 
 
-def first_kernel(s, side, right, block, keep, leave, product):
+def first_kernel(s, side, sides, block, keep, leave, product):
     width = keep.shape[0]
-    x = right[...].T
+    x = sides[0].T
     x = jnp.concatenate(
         [x[unit_place(s, h) * width : (unit_place(s, h) + 1) * width] for h in range(2)], axis=0
     )
@@ -69,9 +69,9 @@
     keep[...] = product[pl.ds(other, width)]
 
 
-def first_products(s, side, right, block):
+def first_products(s, side, sides, block):
     rows = block.shape[0]
-    width = right.shape[1] // UNITS
+    width = sides.shape[2] // UNITS
     return pl.pallas_call(
         functools.partial(first_kernel, s),
         out_shape=(
@@ -83,7 +83,7 @@
         scratch_shapes=[pltpu.VMEM((2 * width, rows), jnp.float32)],
         compiler_params=params(),
         cost_estimate=COST,
-    )(side, right, block)
+    )(side, sides, block)
 
 
 def turn_kernel(width, side, sides, out, turned):
@@ -271,10 +271,9 @@
             solved[step][s] = (trade(other, "row", 1), other)
 
         inverses[0] = order.block(inverse_blocks, 0)
-        right = order.block(right_sides, 0)
         def first(s):
             state[s]["total"], leaving = order.run(
-                lambda v, w: first_products(s, side_ref, v, w), right, inverses[0]
+                lambda v, w: first_products(s, side_ref, v, w), right_sides, inverses[0]
             )
             state[s]["flight"] = trade(leaving, "row", 1)
 

time: 146 us -> 150 us (1.027)
  waiting for transfers between devices: 48.5 us -> 51.8 us
    ppermute x50, waiting for transfers between devices: 46.1 us -> 49.4 us  [trade(): return lax.ppermute(value, axis, [(i, i ^ step) for i in range(size)])]
    squeeze x16 -> x15, local copies, waits for them, and re-layouts: 14.9 us -> 12.1 us  [block(): self.last = lax.optimization_barrier(self.run(lambda v: v[index], blocks))]
    ppermute x50, starting transfers between devices: 40 us -> 42.1 us  [trade(): return lax.ppermute(value, axis, [(i, i ^ step) for i in range(size)])]
  transfers between devices with their start and end apart: 52 -> 52, of which waited for: 29 -> 26; matrix products, arithmetic and copies ran while one was open for 10% -> 9% of each run, Pallas kernels for 21% -> 21%
where the time goes in v14:
time: 150 us
  waiting for transfers between devices  51.8 us (35%)
  starting transfers between devices  44.9 us (30%)
  Pallas kernels  32.5 us (22%)
  local copies, waits for them, and re-layouts  16.4 us (11%)
  other arithmetic  3.17 us (2%)
    ppermute x50, waiting for transfers between devices, trade(): return lax.ppermute(value, axis, [(i, i ^ step) for i in range(size)])  49.4 us
    ppermute x50, starting transfers between devices, trade(): return lax.ppermute(value, axis, [(i, i ^ step) for i in range(size)])  42.1 us
    pallas_call x38, Pallas kernels, product(): pl.pallas_call(functools.partial(product_kernel, len(units)), out_shape=j...  29.9 us
    squeeze x15, local copies, waits for them, and re-layouts, block(): self.last = lax.optimization_barrier(self.run(lambda v: v[index], blocks))  12.1 us
  transfers between devices with their start and end apart: 52, of which 26 were waited for; matrix products, arithmetic and copies ran while one was open for 9% of the time, Pallas kernels for 21%

profile of v14, /device:TPU:0, one launch (start us, length us, event | category | flops | bytes accessed | tf_op | source)
XLA Modules:
  0.0 149.7 jit_solution(12289429529893472626)
XLA Ops:
  0.0 3.2 %slice_bitcast_fusion.14.block = bf16[1024,1024]{1,0:T(8,128)(2,1)} fusion(bf16[5,1024,1024]{2,1,0:T(8,128)(2,1)} %param.4), kind=kLoop, calls=%fused_computation.14 | loop fusion | bytes 4194304 | tf_op jit(solution)/shard_map/squeeze | solution.py:135
  3.2 1.6 %copy-done.1 = bf16[1024,1024]{1,0:T(8,128)(2,1)S(1)} copy-done((bf16[1024,1024]{1,0:T(8,128)(2,1)S(1)}, bf16[1024,1024]{1,0:T(8,128)(2,1)}, u32[]{:S(2)}) %copy-start.1) | copy-done | bytes 2097176
  4.8 0.8 shard_map.37
  5.7 3.1 %collective-permute-start.1 = (bf16[64,1024]{1,0:T(8,128)(2,1)S(1)}, bf16[64,1024]{1,0:T(8,128)(2,1)}, u32[]{:S(2)}, u32[]{:S(2)}) collective-permute-start(bf16[64,1024]{1,0:T(8,128)(2,1)S(1)} %get-tuple-element.220), channel_id=1, source_target_pairs={{0,4},{4,0},{8,12},{12,8},{1,5},{5,1},{9,13},{13,9},{2,6},{6,2},{1... | collective-permute-start | bytes 393224 | tf_op jit(solution)/shard_map/ppermute | solution.py:142
  8.8 0.8 shard_map.38
  9.7 0.9 shard_map.39
  10.7 1.0 copy-done.2
  11.6 1.4 slice_bitcast_fusion.15
  13.0 0.9 fusion.19
  13.9 3.1 %collective-permute-start.2 = (bf16[64,1024]{1,0:T(8,128)(2,1)S(1)}, bf16[64,1024]{1,0:T(8,128)(2,1)S(1)}, u32[]{:S(2)}, u32[]{:S(2)}) collective-permute-start(bf16[64,1024]{1,0:T(8,128)(2,1)S(1)} %get-tuple-element.451), channel_id=1, source_target_pairs={{0,8},{4,12},{8,0},{12,4},{1,9},{5,13},{9,1},{13,5},{2,10},{6,14},... | collective-permute-start | bytes 393224 | tf_op jit(solution)/shard_map/ppermute | solution.py:142
  17.0 1.8 %slice_bitcast_fusion.13.block = bf16[1024,1024]{1,0:T(8,128)(2,1)S(1)} fusion(bf16[10,1024,1024]{2,1,0:T(8,128)(2,1)} %param.3), kind=kLoop, calls=%fused_computation.13 | loop fusion | bytes 4194304 | tf_op jit(solution)/shard_map/squeeze | solution.py:135
  18.7 4.0 %collective-permute-done.2 = bf16[64,1024]{1,0:T(8,128)(2,1)S(1)} collective-permute-done((bf16[64,1024]{1,0:T(8,128)(2,1)S(1)}, bf16[64,1024]{1,0:T(8,128)(2,1)S(1)}, u32[]{:S(2)}, u32[]{:S(2)}) %collective-permute-start.2) | collective-permute-done | bytes 131104 | tf_op jit(solution)/shard_map/ppermute | solution.py:142
  22.7 0.8 collective-permute-start.4
  24.4 3.5 %collective-permute-start.3 = (bf16[64,1024]{1,0:T(8,128)(2,1)S(1)}, bf16[64,1024]{1,0:T(8,128)(2,1)S(1)}, u32[]{:S(2)}, u32[]{:S(2)}) collective-permute-start(bf16[64,1024]{1,0:T(8,128)(2,1)S(1)} %get-tuple-element.449), channel_id=1, source_target_pairs={{0,8},{4,12},{8,0},{12,4},{1,9},{5,13},{9,1},{13,5},{2,10},{6,14},... | collective-permute-start | bytes 393224 | tf_op jit(solution)/shard_map/ppermute | solution.py:142
  28.7 1.6 %collective-permute-start.7 = (bf16[64,1024]{1,0:T(8,128)(2,1)S(1)}, bf16[64,1024]{1,0:T(8,128)(2,1)S(1)}, u32[]{:S(2)}, u32[]{:S(2)}) collective-permute-start(bf16[64,1024]{1,0:T(8,128)(2,1)S(1)} %get-tuple-element.447), channel_id=1, source_target_pairs={{0,2},{1,3},{2,0},{3,1},{4,6},{5,7},{6,4},{7,5},{8,10},{9,11},{10,... | collective-permute-start | bytes 393224 | tf_op jit(solution)/shard_map/ppermute | solution.py:142
  30.2 1.8 %slice_bitcast_fusion.12.block = bf16[1024,1024]{1,0:T(8,128)(2,1)S(1)} fusion(bf16[10,1024,1024]{2,1,0:T(8,128)(2,1)} %param.3), kind=kLoop, calls=%fused_computation.12 | loop fusion | bytes 4194304 | tf_op jit(solution)/shard_map/squeeze | solution.py:135
  32.0 1.9 %slice_bitcast_fusion.11.block = bf16[1024,1024]{1,0:T(8,128)(2,1)S(1)} fusion(bf16[5,1024,1024]{2,1,0:T(8,128)(2,1)} %param.4), kind=kLoop, calls=%fused_computation.11 | loop fusion | bytes 4194304 | tf_op jit(solution)/shard_map/squeeze | solution.py:135
  33.9 0.9 collective-permute-done.3
  37.1 2.1 %collective-permute-start.11 = (bf16[64,1024]{1,0:T(8,128)(2,1)S(1)}, bf16[64,1024]{1,0:T(8,128)(2,1)S(1)}, u32[]{:S(2)}, u32[]{:S(2)}) collective-permute-start(bf16[64,1024]{1,0:T(8,128)(2,1)S(1)} %shard_map.43), channel_id=1, source_target_pairs={{0,4},{4,0},{8,12},{12,8},{1,5},{5,1},{9,13},{13,9},{2,6},{6,2},{1... | collective-permute-start | bytes 393224 | tf_op jit(solution)/shard_map/ppermute | solution.py:142
  39.2 1.3 collective-permute-done.6.refs_0_.refs_2_
  41.3 1.5 %collective-permute-start.9 = (bf16[64,1024]{1,0:T(8,128)(2,1)S(1)}, bf16[64,1024]{1,0:T(8,128)(2,1)S(1)}, u32[]{:S(2)}, u32[]{:S(2)}) collective-permute-start(bf16[64,1024]{1,0:T(8,128)(2,1)S(1)} %get-tuple-element.445), channel_id=1, source_target_pairs={{0,2},{1,3},{2,0},{3,1},{4,6},{5,7},{6,4},{7,5},{8,10},{9,11},{10,... | collective-permute-start | bytes 393224 | tf_op jit(solution)/shard_map/ppermute | solution.py:142
  42.8 1.8 %slice_bitcast_fusion.10.block = bf16[1024,1024]{1,0:T(8,128)(2,1)S(1)} fusion(bf16[10,1024,1024]{2,1,0:T(8,128)(2,1)} %param.3), kind=kLoop, calls=%fused_computation.10 | loop fusion | bytes 4194304 | tf_op jit(solution)/shard_map/squeeze | solution.py:135
  44.6 0.9 shard_map.45
  46.4 1.8 %collective-permute-start.14 = (bf16[64,1024]{1,0:T(8,128)(2,1)S(1)}, bf16[64,1024]{1,0:T(8,128)(2,1)S(1)}, u32[]{:S(2)}, u32[]{:S(2)}) collective-permute-start(bf16[64,1024]{1,0:T(8,128)(2,1)S(1)} %get-tuple-element.443), channel_id=1, source_target_pairs={{0,8},{4,12},{8,0},{12,4},{1,9},{5,13},{9,1},{13,5},{2,10},{6,14},... | collective-permute-start | bytes 393224 | tf_op jit(solution)/shard_map/ppermute | solution.py:142
  49.2 2.1 %collective-permute-start.13 = (bf16[64,1024]{1,0:T(8,128)(2,1)S(1)}, bf16[64,1024]{1,0:T(8,128)(2,1)S(1)}, u32[]{:S(2)}, u32[]{:S(2)}) collective-permute-start(bf16[64,1024]{1,0:T(8,128)(2,1)S(1)} %shard_map.47), channel_id=1, source_target_pairs={{0,4},{4,0},{8,12},{12,8},{1,5},{5,1},{9,13},{13,9},{2,6},{6,2},{1... | collective-permute-start | bytes 393224 | tf_op jit(solution)/shard_map/ppermute | solution.py:142
  52.0 2.4 %collective-permute-done.14 = bf16[64,1024]{1,0:T(8,128)(2,1)S(1)} collective-permute-done((bf16[64,1024]{1,0:T(8,128)(2,1)S(1)}, bf16[64,1024]{1,0:T(8,128)(2,1)S(1)}, u32[]{:S(2)}, u32[]{:S(2)}) %collective-permute-start.14) | collective-permute-done | bytes 131104 | tf_op jit(solution)/shard_map/ppermute | solution.py:142
  55.4 1.8 %collective-permute-done.13 = bf16[64,1024]{1,0:T(8,128)(2,1)S(1)} collective-permute-done((bf16[64,1024]{1,0:T(8,128)(2,1)S(1)}, bf16[64,1024]{1,0:T(8,128)(2,1)S(1)}, u32[]{:S(2)}, u32[]{:S(2)}) %collective-permute-start.13) | collective-permute-done | bytes 131104 | tf_op jit(solution)/shard_map/ppermute | solution.py:142
  57.2 1.6 %collective-permute-start.15 = (bf16[64,1024]{1,0:T(8,128)(2,1)S(1)}, bf16[64,1024]{1,0:T(8,128)(2,1)S(1)}, u32[]{:S(2)}, u32[]{:S(2)}) collective-permute-start(bf16[64,1024]{1,0:T(8,128)(2,1)S(1)} %get-tuple-element.441), channel_id=1, source_target_pairs={{0,8},{4,12},{8,0},{12,4},{1,9},{5,13},{9,1},{13,5},{2,10},{6,14},... | collective-permute-start | bytes 393224 | tf_op jit(solution)/shard_map/ppermute | solution.py:142
  58.9 1.0 collective-permute-done.16.refs_0_
  60.6 0.9 collective-permute-start.19
  61.8 0.9 shard_map.51.refs_4_
  63.0 3.1 %collective-permute-done.15 = bf16[64,1024]{1,0:T(8,128)(2,1)S(1)} collective-permute-done((bf16[64,1024]{1,0:T(8,128)(2,1)S(1)}, bf16[64,1024]{1,0:T(8,128)(2,1)S(1)}, u32[]{:S(2)}, u32[]{:S(2)}) %collective-permute-start.15) | collective-permute-done | bytes 131104 | tf_op jit(solution)/shard_map/ppermute | solution.py:142
  68.5 2.1 %collective-permute-start.23 = (bf16[64,1024]{1,0:T(8,128)(2,1)S(1)}, bf16[64,1024]{1,0:T(8,128)(2,1)S(1)}, u32[]{:S(2)}, u32[]{:S(2)}) collective-permute-start(bf16[64,1024]{1,0:T(8,128)(2,1)S(1)} %shard_map.53), channel_id=1, source_target_pairs={{0,4},{4,0},{8,12},{12,8},{1,5},{5,1},{9,13},{13,9},{2,6},{6,2},{1... | collective-permute-start | bytes 393224 | tf_op jit(solution)/shard_map/ppermute | solution.py:142
  72.0 1.3 collective-permute-start.21
  73.5 0.9 shard_map.55
  74.4 0.9 shard_map.56
  75.4 1.1 collective-permute-start.26
  78.1 0.9 collective-permute-start.25
  79.7 3.5 %collective-permute-done.26 = bf16[64,1024]{1,0:T(8,128)(2,1)S(1)} collective-permute-done((bf16[64,1024]{1,0:T(8,128)(2,1)S(1)}, bf16[64,1024]{1,0:T(8,128)(2,1)S(1)}, u32[]{:S(2)}, u32[]{:S(2)}) %collective-permute-start.26) | collective-permute-done | bytes 131104 | tf_op jit(solution)/shard_map/ppermute | solution.py:142
  84.2 1.8 %collective-permute-done.25 = bf16[64,1024]{1,0:T(8,128)(2,1)S(1)} collective-permute-done((bf16[64,1024]{1,0:T(8,128)(2,1)S(1)}, bf16[64,1024]{1,0:T(8,128)(2,1)S(1)}, u32[]{:S(2)}, u32[]{:S(2)}) %collective-permute-start.25) | collective-permute-done | bytes 131104 | tf_op jit(solution)/shard_map/ppermute | solution.py:142
  86.1 0.9 collective-permute-start.27
  87.0 1.6 %collective-permute-done.28.refs_0_ = bf16[64,1024]{1,0:T(8,128)(2,1)S(1)} collective-permute-done((bf16[64,1024]{1,0:T(8,128)(2,1)S(1)}, bf16[64,1024]{1,0:T(8,128)(2,1)S(1)}, u32[]{:S(2)}, u32[]{:S(2)}) %collective-permute-start.28) | collective-permute-done | bytes 131104 | tf_op jit(solution)/shard_map/ppermute | solution.py:142
  89.4 1.2 collective-permute-start.31
  90.9 0.9 shard_map.61.refs_4_
  91.9 0.9 shard_map.62.refs_4_
  93.2 1.7 %collective-permute-done.27 = bf16[64,1024]{1,0:T(8,128)(2,1)S(1)} collective-permute-done((bf16[64,1024]{1,0:T(8,128)(2,1)S(1)}, bf16[64,1024]{1,0:T(8,128)(2,1)S(1)}, u32[]{:S(2)}, u32[]{:S(2)}) %collective-permute-start.27) | collective-permute-done | bytes 131104 | tf_op jit(solution)/shard_map/ppermute | solution.py:142
  97.2 2.1 %collective-permute-start.35 = (bf16[64,1024]{1,0:T(8,128)(2,1)S(1)}, bf16[64,1024]{1,0:T(8,128)(2,1)S(1)}, u32[]{:S(2)}, u32[]{:S(2)}) collective-permute-start(bf16[64,1024]{1,0:T(8,128)(2,1)S(1)} %shard_map.64), channel_id=1, source_target_pairs={{0,4},{4,0},{8,12},{12,8},{1,5},{5,1},{9,13},{13,9},{2,6},{6,2},{1... | collective-permute-start | bytes 393224 | tf_op jit(solution)/shard_map/ppermute | solution.py:142
  100.8 1.8 %collective-permute-start.33 = (bf16[64,1024]{1,0:T(8,128)(2,1)S(1)}, bf16[64,1024]{1,0:T(8,128)(2,1)S(1)}, u32[]{:S(2)}, u32[]{:S(2)}) collective-permute-start(bf16[64,1024]{1,0:T(8,128)(2,1)S(1)} %get-tuple-element.429), channel_id=1, source_target_pairs={{0,2},{1,3},{2,0},{3,1},{4,6},{5,7},{6,4},{7,5},{8,10},{9,11},{10,... | collective-permute-start | bytes 393224 | tf_op jit(solution)/shard_map/ppermute | solution.py:142
  102.8 0.9 shard_map.66
  104.5 0.9 collective-permute-start.38
  108.1 4.4 %collective-permute-done.38 = bf16[64,1024]{1,0:T(8,128)(2,1)S(1)} collective-permute-done((bf16[64,1024]{1,0:T(8,128)(2,1)S(1)}, bf16[64,1024]{1,0:T(8,128)(2,1)S(1)}, u32[]{:S(2)}, u32[]{:S(2)}) %collective-permute-start.38) | collective-permute-done | bytes 131104 | tf_op jit(solution)/shard_map/ppermute | solution.py:142
  113.4 1.8 %collective-permute-done.37 = bf16[64,1024]{1,0:T(8,128)(2,1)S(1)} collective-permute-done((bf16[64,1024]{1,0:T(8,128)(2,1)S(1)}, bf16[64,1024]{1,0:T(8,128)(2,1)S(1)}, u32[]{:S(2)}, u32[]{:S(2)}) %collective-permute-start.37) | collective-permute-done | bytes 131104 | tf_op jit(solution)/shard_map/ppermute | solution.py:142
  115.4 2.3 %collective-permute-done.40.refs_0_ = bf16[64,1024]{1,0:T(8,128)(2,1)S(1)} collective-permute-done((bf16[64,1024]{1,0:T(8,128)(2,1)S(1)}, bf16[64,1024]{1,0:T(8,128)(2,1)S(1)}, u32[]{:S(2)}, u32[]{:S(2)}) %collective-permute-start.40) | collective-permute-done | bytes 131104 | tf_op jit(solution)/shard_map/ppermute | solution.py:142
  118.6 1.2 collective-permute-start.42
  119.9 3.7 %collective-permute-done.42 = bf16[64,1024]{1,0:T(8,128)(2,1)S(1)} collective-permute-done((bf16[64,1024]{1,0:T(8,128)(2,1)S(1)}, bf16[64,1024]{1,0:T(8,128)(2,1)S(1)}, u32[]{:S(2)}, u32[]{:S(2)}) %collective-permute-start.42) | collective-permute-done | bytes 131104 | tf_op jit(solution)/shard_map/ppermute | solution.py:142
  125.6 3.5 %collective-permute-done.43.refs_0_ = bf16[64,1024]{1,0:T(8,128)(2,1)S(1)} collective-permute-done((bf16[64,1024]{1,0:T(8,128)(2,1)S(1)}, bf16[64,1024]{1,0:T(8,128)(2,1)S(1)}, u32[]{:S(2)}, u32[]{:S(2)}) %collective-permute-start.43) | collective-permute-done | bytes 131104 | tf_op jit(solution)/shard_map/ppermute | solution.py:142
  129.1 1.0 shard_map.73
  130.1 1.7 %collective-permute-start.47 = (bf16[64,1024]{1,0:T(8,128)(2,1)S(1)}, bf16[64,1024]{1,0:T(8,128)(2,1)S(1)}, u32[]{:S(2)}, u32[]{:S(2)}) collective-permute-start(bf16[64,1024]{1,0:T(8,128)(2,1)S(1)} %get-tuple-element.421), channel_id=1, source_target_pairs={{0,2},{1,3},{2,0},{3,1},{4,6},{5,7},{6,4},{7,5},{8,10},{9,11},{10,... | collective-permute-start | bytes 393224 | tf_op jit(solution)/shard_map/ppermute | solution.py:142
  133.7 1.4 collective-permute-done.47
  135.3 2.3 %collective-permute-done.46 = bf16[64,1024]{1,0:T(8,128)(2,1)S(1)} collective-permute-done((bf16[64,1024]{1,0:T(8,128)(2,1)S(1)}, bf16[64,1024]{1,0:T(8,128)(2,1)S(1)}, u32[]{:S(2)}, u32[]{:S(2)}) %collective-permute-start.46) | collective-permute-done | bytes 131104 | tf_op jit(solution)/shard_map/ppermute | solution.py:142
  138.9 1.3 collective-permute-start.50
  141.0 4.0 %collective-permute-done.49 = bf16[64,1024]{1,0:T(8,128)(2,1)S(1)} collective-permute-done((bf16[64,1024]{1,0:T(8,128)(2,1)S(1)}, bf16[64,1024]{1,0:T(8,128)(2,1)S(1)}, u32[]{:S(2)}, u32[]{:S(2)}) %collective-permute-start.49) | collective-permute-done | bytes 131104 | tf_op jit(solution)/shard_map/ppermute | solution.py:142
  144.9 1.5 %collective-permute-start.51 = (bf16[64,1024]{1,0:T(8,128)(2,1)S(1)}, bf16[64,1024]{1,0:T(8,128)(2,1)S(1)}, u32[]{:S(2)}, u32[]{:S(2)}) collective-permute-start(bf16[64,1024]{1,0:T(8,128)(2,1)S(1)} %fusion.1), channel_id=1, source_target_pairs={{12,4},{0,8},{13,5},{1,9},{14,6},{2,10},{15,7},{3,11},{28,20},{16,... | collective-permute-start | bytes 393224 | tf_op jit(solution)/shard_map/ppermute | solution.py:260
  146.7 2.3 %collective-permute-done.51 = bf16[64,1024]{1,0:T(8,128)(2,1)S(1)} collective-permute-done((bf16[64,1024]{1,0:T(8,128)(2,1)S(1)}, bf16[64,1024]{1,0:T(8,128)(2,1)S(1)}, u32[]{:S(2)}, u32[]{:S(2)}) %collective-permute-start.51) | collective-permute-done | bytes 131104 | tf_op jit(solution)/shard_map/ppermute | solution.py:260
  (167 shorter events, 34.8 us)
Async XLA Ops:
  0.0 3.2 %copy-start = (bf16[5,1024,256]{2,1,0:T(8,128)(2,1)S(1)}, bf16[5,1024,256]{2,1,0:T(8,128)(2,1)}, u32[]{:S(2)}) copy-start(bf16[5,1024,256]{2,1,0:T(8,128)(2,1)} %sides.2) | copy-start | bytes 7864324
  3.2 1.6 %copy-start.1 = (bf16[1024,1024]{1,0:T(8,128)(2,1)S(1)}, bf16[1024,1024]{1,0:T(8,128)(2,1)}, u32[]{:S(2)}) copy-start(bf16[1024,1024]{1,0:T(8,128)(2,1)} %slice_bitcast_fusion.14.block) | copy-start | bytes 6291460
  5.7 7.3 %collective-permute-start.1 = (bf16[64,1024]{1,0:T(8,128)(2,1)S(1)}, bf16[64,1024]{1,0:T(8,128)(2,1)}, u32[]{:S(2)}, u32[]{:S(2)}) collective-permute-start(bf16[64,1024]{1,0:T(8,128)(2,1)S(1)} %get-tuple-element.220), channel_id=1, source_target_pairs={{0,4},{4,0},{8,12},{12,8},{1,5},{5,1},{9,13},{13,9},{2,6},{6,2},{1... | collective-permute-start | bytes 393224 | tf_op jit(solution)/shard_map/ppermute | solution.py:142
  9.6 14.8 %collective-permute-start = (bf16[64,1024]{1,0:T(8,128)(2,1)S(1)}, bf16[64,1024]{1,0:T(8,128)(2,1)S(1)}, u32[]{:S(2)}, u32[]{:S(2)}) collective-permute-start(bf16[64,1024]{1,0:T(8,128)(2,1)S(1)} %get-tuple-element.219), channel_id=1, source_target_pairs={{0,4},{4,0},{8,12},{12,8},{1,5},{5,1},{9,13},{13,9},{2,6},{6,2},{1... | collective-permute-start | bytes 393224 | tf_op jit(solution)/shard_map/ppermute | solution.py:142
  10.6 1.0 copy-start.2
  13.9 8.8 %collective-permute-start.2 = (bf16[64,1024]{1,0:T(8,128)(2,1)S(1)}, bf16[64,1024]{1,0:T(8,128)(2,1)S(1)}, u32[]{:S(2)}, u32[]{:S(2)}) collective-permute-start(bf16[64,1024]{1,0:T(8,128)(2,1)S(1)} %get-tuple-element.451), channel_id=1, source_target_pairs={{0,8},{4,12},{8,0},{12,4},{1,9},{5,13},{9,1},{13,5},{2,10},{6,14},... | collective-permute-start | bytes 393224 | tf_op jit(solution)/shard_map/ppermute | solution.py:142
  22.7 5.1 %collective-permute-start.4 = (bf16[64,1024]{1,0:T(8,128)(2,1)S(1)}, bf16[64,1024]{1,0:T(8,128)(2,1)S(1)}, u32[]{:S(2)}, u32[]{:S(2)}) collective-permute-start(bf16[64,1024]{1,0:T(8,128)(2,1)S(1)} %add_convert_fusion.8.refs_0_.refs_1_), channel_id=1, source_target_pairs={{0,4},{4,0},{8,12},{12,8},{1,5},{5,1},{9,13},{13,9},{2,6},{6,2},{1... | collective-permute-start | bytes 393224 | tf_op jit(solution)/shard_map/ppermute | solution.py:142
  24.3 4.4 %collective-permute-start.5 = (bf16[64,1024]{1,0:T(8,128)(2,1)S(1)}, bf16[64,1024]{1,0:T(8,128)(2,1)S(1)}, u32[]{:S(2)}, u32[]{:S(2)}) collective-permute-start(bf16[64,1024]{1,0:T(8,128)(2,1)S(1)} %shard_map.40), channel_id=1, source_target_pairs={{0,1},{1,0},{2,3},{3,2},{4,5},{5,4},{6,7},{7,6},{8,9},{9,8},{10,11... | collective-permute-start | bytes 393224 | tf_op jit(solution)/shard_map/ppermute | solution.py:142
  24.4 10.4 %collective-permute-start.3 = (bf16[64,1024]{1,0:T(8,128)(2,1)S(1)}, bf16[64,1024]{1,0:T(8,128)(2,1)S(1)}, u32[]{:S(2)}, u32[]{:S(2)}) collective-permute-start(bf16[64,1024]{1,0:T(8,128)(2,1)S(1)} %get-tuple-element.449), channel_id=1, source_target_pairs={{0,8},{4,12},{8,0},{12,4},{1,9},{5,13},{9,1},{13,5},{2,10},{6,14},... | collective-permute-start | bytes 393224 | tf_op jit(solution)/shard_map/ppermute | solution.py:142
  28.7 7.1 %collective-permute-start.7 = (bf16[64,1024]{1,0:T(8,128)(2,1)S(1)}, bf16[64,1024]{1,0:T(8,128)(2,1)S(1)}, u32[]{:S(2)}, u32[]{:S(2)}) collective-permute-start(bf16[64,1024]{1,0:T(8,128)(2,1)S(1)} %get-tuple-element.447), channel_id=1, source_target_pairs={{0,2},{1,3},{2,0},{3,1},{4,6},{5,7},{6,4},{7,5},{8,10},{9,11},{10,... | collective-permute-start | bytes 393224 | tf_op jit(solution)/shard_map/ppermute | solution.py:142
  32.0 29.5 %slice-start = ((s8[20971520]{0:T(1024)(128)(4,1)}), s8[4194304]{0:T(1024)(128)(4,1)S(1)}, s32[]{:S(2)}) async-start(s8[20971520]{0:T(1024)(128)(4,1)} %bitcast.69), calls=%async_computation | async-start | bytes 8388608
  34.8 5.6 %collective-permute-start.6 = (bf16[64,1024]{1,0:T(8,128)(2,1)S(1)}, bf16[64,1024]{1,0:T(8,128)(2,1)S(1)}, u32[]{:S(2)}, u32[]{:S(2)}) collective-permute-start(bf16[64,1024]{1,0:T(8,128)(2,1)S(1)} %add_convert_fusion.7.refs_0_.refs_3_), channel_id=1, source_target_pairs={{0,4},{4,0},{8,12},{12,8},{1,5},{5,1},{9,13},{13,9},{2,6},{6,2},{1... | collective-permute-start | bytes 393224 | tf_op jit(solution)/shard_map/ppermute | solution.py:142
  35.7 5.5 %collective-permute-start.8 = (bf16[64,1024]{1,0:T(8,128)(2,1)S(1)}, bf16[64,1024]{1,0:T(8,128)(2,1)S(1)}, u32[]{:S(2)}, u32[]{:S(2)}) collective-permute-start(bf16[64,1024]{1,0:T(8,128)(2,1)S(1)} %shard_map.42), channel_id=1, source_target_pairs={{0,1},{1,0},{2,3},{3,2},{4,5},{5,4},{6,7},{7,6},{8,9},{9,8},{10,11... | collective-permute-start | bytes 393224 | tf_op jit(solution)/shard_map/ppermute | solution.py:142
  35.8 25.7 %slice-start.1 = ((s8[20971520]{0:T(1024)(128)(4,1)}), s8[4194304]{0:T(1024)(128)(4,1)S(1)}, s32[]{:S(2)}) async-start(s8[20971520]{0:T(1024)(128)(4,1)} %bitcast.69), calls=%async_computation.1 | async-start | bytes 8388608
  35.8 9.7 %collective-permute-start.10 = (bf16[64,1024]{1,0:T(8,128)(2,1)S(1)}, bf16[64,1024]{1,0:T(8,128)(2,1)S(1)}, u32[]{:S(2)}, u32[]{:S(2)}) collective-permute-start(bf16[64,1024]{1,0:T(8,128)(2,1)S(1)} %subtract_convert_fusion.7.refs_0_), channel_id=1, source_target_pairs={{0,1},{1,0},{2,3},{3,2},{4,5},{5,4},{6,7},{7,6},{8,9},{9,8},{10,11... | collective-permute-start | bytes 393224 | tf_op jit(solution)/shard_map/ppermute | solution.py:142
  37.1 9.2 %collective-permute-start.11 = (bf16[64,1024]{1,0:T(8,128)(2,1)S(1)}, bf16[64,1024]{1,0:T(8,128)(2,1)S(1)}, u32[]{:S(2)}, u32[]{:S(2)}) collective-permute-start(bf16[64,1024]{1,0:T(8,128)(2,1)S(1)} %shard_map.43), channel_id=1, source_target_pairs={{0,4},{4,0},{8,12},{12,8},{1,5},{5,1},{9,13},{13,9},{2,6},{6,2},{1... | collective-permute-start | bytes 393224 | tf_op jit(solution)/shard_map/ppermute | solution.py:142
  41.3 20.3 %slice-start.2 = ((s8[20971520]{0:T(1024)(128)(4,1)}), s8[4194304]{0:T(1024)(128)(4,1)S(1)}, s32[]{:S(2)}) async-start(s8[20971520]{0:T(1024)(128)(4,1)} %bitcast.69), calls=%async_computation.2 | async-start | bytes 8388608
  41.3 6.9 %collective-permute-start.9 = (bf16[64,1024]{1,0:T(8,128)(2,1)S(1)}, bf16[64,1024]{1,0:T(8,128)(2,1)S(1)}, u32[]{:S(2)}, u32[]{:S(2)}) collective-permute-start(bf16[64,1024]{1,0:T(8,128)(2,1)S(1)} %get-tuple-element.445), channel_id=1, source_target_pairs={{0,2},{1,3},{2,0},{3,1},{4,6},{5,7},{6,4},{7,5},{8,10},{9,11},{10,... | collective-permute-start | bytes 393224 | tf_op jit(solution)/shard_map/ppermute | solution.py:142
  45.5 16.0 %slice-start.3 = ((s8[20971520]{0:T(1024)(128)(4,1)}), s8[4194304]{0:T(1024)(128)(4,1)S(1)}, s32[]{:S(2)}) async-start(s8[20971520]{0:T(1024)(128)(4,1)} %bitcast.69), calls=%async_computation.3 | async-start | bytes 8388608
  46.4 8.0 %collective-permute-start.14 = (bf16[64,1024]{1,0:T(8,128)(2,1)S(1)}, bf16[64,1024]{1,0:T(8,128)(2,1)S(1)}, u32[]{:S(2)}, u32[]{:S(2)}) collective-permute-start(bf16[64,1024]{1,0:T(8,128)(2,1)S(1)} %get-tuple-element.443), channel_id=1, source_target_pairs={{0,8},{4,12},{8,0},{12,4},{1,9},{5,13},{9,1},{13,5},{2,10},{6,14},... | collective-permute-start | bytes 393224 | tf_op jit(solution)/shard_map/ppermute | solution.py:142
  48.2 3.0 %collective-permute-start.12 = (bf16[64,1024]{1,0:T(8,128)(2,1)S(1)}, bf16[64,1024]{1,0:T(8,128)(2,1)S(1)}, u32[]{:S(2)}, u32[]{:S(2)}) collective-permute-start(bf16[64,1024]{1,0:T(8,128)(2,1)S(1)} %subtract_convert_fusion.6.refs_0_), channel_id=1, source_target_pairs={{0,1},{1,0},{2,3},{3,2},{4,5},{5,4},{6,7},{7,6},{8,9},{9,8},{10,11... | collective-permute-start | bytes 393224 | tf_op jit(solution)/shard_map/ppermute | solution.py:142
  48.4 14.4 %slice-start.5 = ((s8[10485760]{0:T(1024)(128)(4,1)}), s8[4194304]{0:T(1024)(128)(4,1)S(1)}, s32[]{:S(2)}) async-start(s8[10485760]{0:T(1024)(128)(4,1)} %bitcast.71), calls=%async_computation.5 | async-start | bytes 8388608
  49.1 12.4 %slice-start.4 = ((s8[20971520]{0:T(1024)(128)(4,1)}), s8[4194304]{0:T(1024)(128)(4,1)S(1)}, s32[]{:S(2)}) async-start(s8[20971520]{0:T(1024)(128)(4,1)} %bitcast.69), calls=%async_computation.4 | async-start | bytes 8388608
  49.2 8.0 %collective-permute-start.13 = (bf16[64,1024]{1,0:T(8,128)(2,1)S(1)}, bf16[64,1024]{1,0:T(8,128)(2,1)S(1)}, u32[]{:S(2)}, u32[]{:S(2)}) collective-permute-start(bf16[64,1024]{1,0:T(8,128)(2,1)S(1)} %shard_map.47), channel_id=1, source_target_pairs={{0,4},{4,0},{8,12},{12,8},{1,5},{5,1},{9,13},{13,9},{2,6},{6,2},{1... | collective-permute-start | bytes 393224 | tf_op jit(solution)/shard_map/ppermute | solution.py:142
  54.4 5.4 %collective-permute-start.16 = (bf16[64,1024]{1,0:T(8,128)(2,1)S(1)}, bf16[64,1024]{1,0:T(8,128)(2,1)S(1)}, u32[]{:S(2)}, u32[]{:S(2)}) collective-permute-start(bf16[64,1024]{1,0:T(8,128)(2,1)S(1)} %add_convert_fusion.6.refs_0_.refs_1_), channel_id=1, source_target_pairs={{0,4},{4,0},{8,12},{12,8},{1,5},{5,1},{9,13},{13,9},{2,6},{6,2},{1... | collective-permute-start | bytes 393224 | tf_op jit(solution)/shard_map/ppermute | solution.py:142
  55.3 7.5 %slice-start.6 = ((s8[10485760]{0:T(1024)(128)(4,1)}), s8[4194304]{0:T(1024)(128)(4,1)S(1)}, s32[]{:S(2)}) async-start(s8[10485760]{0:T(1024)(128)(4,1)} %bitcast.71), calls=%async_computation.6 | async-start | bytes 8388608
  55.3 5.3 %collective-permute-start.17 = (bf16[64,1024]{1,0:T(8,128)(2,1)S(1)}, bf16[64,1024]{1,0:T(8,128)(2,1)S(1)}, u32[]{:S(2)}, u32[]{:S(2)}) collective-permute-start(bf16[64,1024]{1,0:T(8,128)(2,1)S(1)} %shard_map.49), channel_id=1, source_target_pairs={{0,1},{1,0},{2,3},{3,2},{4,5},{5,4},{6,7},{7,6},{8,9},{9,8},{10,11... | collective-permute-start | bytes 393224 | tf_op jit(solution)/shard_map/ppermute | solution.py:142
  57.2 8.9 %collective-permute-start.15 = (bf16[64,1024]{1,0:T(8,128)(2,1)S(1)}, bf16[64,1024]{1,0:T(8,128)(2,1)S(1)}, u32[]{:S(2)}, u32[]{:S(2)}) collective-permute-start(bf16[64,1024]{1,0:T(8,128)(2,1)S(1)} %get-tuple-element.441), channel_id=1, source_target_pairs={{0,8},{4,12},{8,0},{12,4},{1,9},{5,13},{9,1},{13,5},{2,10},{6,14},... | collective-permute-start | bytes 393224 | tf_op jit(solution)/shard_map/ppermute | solution.py:142
  60.6 2.2 %slice-start.7 = ((s8[10485760]{0:T(1024)(128)(4,1)}), s8[2097152]{0:T(1024)(128)(4,1)S(1)}, s32[]{:S(2)}) async-start(s8[10485760]{0:T(1024)(128)(4,1)} %bitcast.71), calls=%async_computation.7 | async-start | bytes 4194304
  60.6 6.5 %collective-permute-start.19 = (bf16[64,1024]{1,0:T(8,128)(2,1)S(1)}, bf16[64,1024]{1,0:T(8,128)(2,1)S(1)}, u32[]{:S(2)}, u32[]{:S(2)}) collective-permute-start(bf16[64,1024]{1,0:T(8,128)(2,1)S(1)} %get-tuple-element.439), channel_id=1, source_target_pairs={{0,2},{1,3},{2,0},{3,1},{4,6},{5,7},{6,4},{7,5},{8,10},{9,11},{10,... | collective-permute-start | bytes 393224 | tf_op jit(solution)/shard_map/ppermute | solution.py:142
  66.2 5.0 %collective-permute-start.18 = (bf16[64,1024]{1,0:T(8,128)(2,1)S(1)}, bf16[64,1024]{1,0:T(8,128)(2,1)S(1)}, u32[]{:S(2)}, u32[]{:S(2)}) collective-permute-start(bf16[64,1024]{1,0:T(8,128)(2,1)S(1)} %add_convert_fusion.5.refs_0_.refs_3_), channel_id=1, source_target_pairs={{0,4},{4,0},{8,12},{12,8},{1,5},{5,1},{9,13},{13,9},{2,6},{6,2},{1... | collective-permute-start | bytes 393224 | tf_op jit(solution)/shard_map/ppermute | solution.py:142
  67.0 5.0 %collective-permute-start.20 = (bf16[64,1024]{1,0:T(8,128)(2,1)S(1)}, bf16[64,1024]{1,0:T(8,128)(2,1)S(1)}, u32[]{:S(2)}, u32[]{:S(2)}) collective-permute-start(bf16[64,1024]{1,0:T(8,128)(2,1)S(1)} %shard_map.52), channel_id=1, source_target_pairs={{0,1},{1,0},{2,3},{3,2},{4,5},{5,4},{6,7},{7,6},{8,9},{9,8},{10,11... | collective-permute-start | bytes 393224 | tf_op jit(solution)/shard_map/ppermute | solution.py:142
  67.2 7.2 %collective-permute-start.22 = (bf16[64,1024]{1,0:T(8,128)(2,1)S(1)}, bf16[64,1024]{1,0:T(8,128)(2,1)S(1)}, u32[]{:S(2)}, u32[]{:S(2)}) collective-permute-start(bf16[64,1024]{1,0:T(8,128)(2,1)S(1)} %subtract_convert_fusion.5.refs_0_), channel_id=1, source_target_pairs={{0,1},{1,0},{2,3},{3,2},{4,5},{5,4},{6,7},{7,6},{8,9},{9,8},{10,11... | collective-permute-start | bytes 393224 | tf_op jit(solution)/shard_map/ppermute | solution.py:142
  68.5 6.9 %collective-permute-start.23 = (bf16[64,1024]{1,0:T(8,128)(2,1)S(1)}, bf16[64,1024]{1,0:T(8,128)(2,1)S(1)}, u32[]{:S(2)}, u32[]{:S(2)}) collective-permute-start(bf16[64,1024]{1,0:T(8,128)(2,1)S(1)} %shard_map.53), channel_id=1, source_target_pairs={{0,4},{4,0},{8,12},{12,8},{1,5},{5,1},{9,13},{13,9},{2,6},{6,2},{1... | collective-permute-start | bytes 393224 | tf_op jit(solution)/shard_map/ppermute | solution.py:142
  72.0 5.0 %collective-permute-start.21 = (bf16[64,1024]{1,0:T(8,128)(2,1)S(1)}, bf16[64,1024]{1,0:T(8,128)(2,1)S(1)}, u32[]{:S(2)}, u32[]{:S(2)}) collective-permute-start(bf16[64,1024]{1,0:T(8,128)(2,1)S(1)} %get-tuple-element.437), channel_id=1, source_target_pairs={{0,2},{1,3},{2,0},{3,1},{4,6},{5,7},{6,4},{7,5},{8,10},{9,11},{10,... | collective-permute-start | bytes 393224 | tf_op jit(solution)/shard_map/ppermute | solution.py:142
  75.4 7.9 %collective-permute-start.26 = (bf16[64,1024]{1,0:T(8,128)(2,1)S(1)}, bf16[64,1024]{1,0:T(8,128)(2,1)S(1)}, u32[]{:S(2)}, u32[]{:S(2)}) collective-permute-start(bf16[64,1024]{1,0:T(8,128)(2,1)S(1)} %get-tuple-element.435), channel_id=1, source_target_pairs={{0,8},{4,12},{8,0},{12,4},{1,9},{5,13},{9,1},{13,5},{2,10},{6,14},... | collective-permute-start | bytes 393224 | tf_op jit(solution)/shard_map/ppermute | solution.py:142
  77.1 1.8 %collective-permute-start.24 = (bf16[64,1024]{1,0:T(8,128)(2,1)S(1)}, bf16[64,1024]{1,0:T(8,128)(2,1)S(1)}, u32[]{:S(2)}, u32[]{:S(2)}) collective-permute-start(bf16[64,1024]{1,0:T(8,128)(2,1)S(1)} %subtract_convert_fusion.4.refs_0_), channel_id=1, source_target_pairs={{0,1},{1,0},{2,3},{3,2},{4,5},{5,4},{6,7},{7,6},{8,9},{9,8},{10,11... | collective-permute-start | bytes 393224 | tf_op jit(solution)/shard_map/ppermute | solution.py:142
  78.1 8.0 %collective-permute-start.25 = (bf16[64,1024]{1,0:T(8,128)(2,1)S(1)}, bf16[64,1024]{1,0:T(8,128)(2,1)S(1)}, u32[]{:S(2)}, u32[]{:S(2)}) collective-permute-start(bf16[64,1024]{1,0:T(8,128)(2,1)S(1)} %shard_map.57), channel_id=1, source_target_pairs={{0,4},{4,0},{8,12},{12,8},{1,5},{5,1},{9,13},{13,9},{2,6},{6,2},{1... | collective-permute-start | bytes 393224 | tf_op jit(solution)/shard_map/ppermute | solution.py:142
  83.3 5.3 %collective-permute-start.28 = (bf16[64,1024]{1,0:T(8,128)(2,1)S(1)}, bf16[64,1024]{1,0:T(8,128)(2,1)S(1)}, u32[]{:S(2)}, u32[]{:S(2)}) collective-permute-start(bf16[64,1024]{1,0:T(8,128)(2,1)S(1)} %add_convert_fusion.4.refs_0_.refs_1_), channel_id=1, source_target_pairs={{0,4},{4,0},{8,12},{12,8},{1,5},{5,1},{9,13},{13,9},{2,6},{6,2},{1... | collective-permute-start | bytes 393224 | tf_op jit(solution)/shard_map/ppermute | solution.py:142
  84.2 5.2 %collective-permute-start.29 = (bf16[64,1024]{1,0:T(8,128)(2,1)S(1)}, bf16[64,1024]{1,0:T(8,128)(2,1)S(1)}, u32[]{:S(2)}, u32[]{:S(2)}) collective-permute-start(bf16[64,1024]{1,0:T(8,128)(2,1)S(1)} %shard_map.59), channel_id=1, source_target_pairs={{0,1},{1,0},{2,3},{3,2},{4,5},{5,4},{6,7},{7,6},{8,9},{9,8},{10,11... | collective-permute-start | bytes 393224 | tf_op jit(solution)/shard_map/ppermute | solution.py:142
  86.1 8.8 %collective-permute-start.27 = (bf16[64,1024]{1,0:T(8,128)(2,1)S(1)}, bf16[64,1024]{1,0:T(8,128)(2,1)S(1)}, u32[]{:S(2)}, u32[]{:S(2)}) collective-permute-start(bf16[64,1024]{1,0:T(8,128)(2,1)S(1)} %get-tuple-element.433), channel_id=1, source_target_pairs={{0,8},{4,12},{8,0},{12,4},{1,9},{5,13},{9,1},{13,5},{2,10},{6,14},... | collective-permute-start | bytes 393224 | tf_op jit(solution)/shard_map/ppermute | solution.py:142
  89.4 6.4 %collective-permute-start.31 = (bf16[64,1024]{1,0:T(8,128)(2,1)S(1)}, bf16[64,1024]{1,0:T(8,128)(2,1)S(1)}, u32[]{:S(2)}, u32[]{:S(2)}) collective-permute-start(bf16[64,1024]{1,0:T(8,128)(2,1)S(1)} %get-tuple-element.431), channel_id=1, source_target_pairs={{0,2},{1,3},{2,0},{3,1},{4,6},{5,7},{6,4},{7,5},{8,10},{9,11},{10,... | collective-permute-start | bytes 393224 | tf_op jit(solution)/shard_map/ppermute | solution.py:142
  94.9 5.0 %collective-permute-start.30 = (bf16[64,1024]{1,0:T(8,128)(2,1)S(1)}, bf16[64,1024]{1,0:T(8,128)(2,1)S(1)}, u32[]{:S(2)}, u32[]{:S(2)}) collective-permute-start(bf16[64,1024]{1,0:T(8,128)(2,1)S(1)} %add_convert_fusion.3.refs_0_.refs_3_), channel_id=1, source_target_pairs={{0,4},{4,0},{8,12},{12,8},{1,5},{5,1},{9,13},{13,9},{2,6},{6,2},{1... | collective-permute-start | bytes 393224 | tf_op jit(solution)/shard_map/ppermute | solution.py:142
  95.8 5.0 %collective-permute-start.32 = (bf16[64,1024]{1,0:T(8,128)(2,1)S(1)}, bf16[64,1024]{1,0:T(8,128)(2,1)S(1)}, u32[]{:S(2)}, u32[]{:S(2)}) collective-permute-start(bf16[64,1024]{1,0:T(8,128)(2,1)S(1)} %shard_map.63), channel_id=1, source_target_pairs={{0,1},{1,0},{2,3},{3,2},{4,5},{5,4},{6,7},{7,6},{8,9},{9,8},{10,11... | collective-permute-start | bytes 393224 | tf_op jit(solution)/shard_map/ppermute | solution.py:142
  95.9 7.8 %collective-permute-start.34 = (bf16[64,1024]{1,0:T(8,128)(2,1)S(1)}, bf16[64,1024]{1,0:T(8,128)(2,1)S(1)}, u32[]{:S(2)}, u32[]{:S(2)}) collective-permute-start(bf16[64,1024]{1,0:T(8,128)(2,1)S(1)} %subtract_convert_fusion.3.refs_0_), channel_id=1, source_target_pairs={{0,1},{1,0},{2,3},{3,2},{4,5},{5,4},{6,7},{7,6},{8,9},{9,8},{10,11... | collective-permute-start | bytes 393224 | tf_op jit(solution)/shard_map/ppermute | solution.py:142
  97.2 7.2 %collective-permute-start.35 = (bf16[64,1024]{1,0:T(8,128)(2,1)S(1)}, bf16[64,1024]{1,0:T(8,128)(2,1)S(1)}, u32[]{:S(2)}, u32[]{:S(2)}) collective-permute-start(bf16[64,1024]{1,0:T(8,128)(2,1)S(1)} %shard_map.64), channel_id=1, source_target_pairs={{0,4},{4,0},{8,12},{12,8},{1,5},{5,1},{9,13},{13,9},{2,6},{6,2},{1... | collective-permute-start | bytes 393224 | tf_op jit(solution)/shard_map/ppermute | solution.py:142
  100.8 5.0 %collective-permute-start.33 = (bf16[64,1024]{1,0:T(8,128)(2,1)S(1)}, bf16[64,1024]{1,0:T(8,128)(2,1)S(1)}, u32[]{:S(2)}, u32[]{:S(2)}) collective-permute-start(bf16[64,1024]{1,0:T(8,128)(2,1)S(1)} %get-tuple-element.429), channel_id=1, source_target_pairs={{0,2},{1,3},{2,0},{3,1},{4,6},{5,7},{6,4},{7,5},{8,10},{9,11},{10,... | collective-permute-start | bytes 393224 | tf_op jit(solution)/shard_map/ppermute | solution.py:142
  104.5 8.0 %collective-permute-start.38 = (bf16[64,1024]{1,0:T(8,128)(2,1)S(1)}, bf16[64,1024]{1,0:T(8,128)(2,1)S(1)}, u32[]{:S(2)}, u32[]{:S(2)}) collective-permute-start(bf16[64,1024]{1,0:T(8,128)(2,1)S(1)} %get-tuple-element.427), channel_id=1, source_target_pairs={{0,8},{4,12},{8,0},{12,4},{1,9},{5,13},{9,1},{13,5},{2,10},{6,14},... | collective-permute-start | bytes 393224 | tf_op jit(solution)/shard_map/ppermute | solution.py:142
  105.8 1.5 collective-permute-start.36
  106.8 8.5 %collective-permute-start.37 = (bf16[64,1024]{1,0:T(8,128)(2,1)S(1)}, bf16[64,1024]{1,0:T(8,128)(2,1)S(1)}, u32[]{:S(2)}, u32[]{:S(2)}) collective-permute-start(bf16[64,1024]{1,0:T(8,128)(2,1)S(1)} %shard_map.68), channel_id=1, source_target_pairs={{0,4},{4,0},{8,12},{12,8},{1,5},{5,1},{9,13},{13,9},{2,6},{6,2},{1... | collective-permute-start | bytes 393224 | tf_op jit(solution)/shard_map/ppermute | solution.py:142
  112.5 5.3 %collective-permute-start.40 = (bf16[64,1024]{1,0:T(8,128)(2,1)S(1)}, bf16[64,1024]{1,0:T(8,128)(2,1)S(1)}, u32[]{:S(2)}, u32[]{:S(2)}) collective-permute-start(bf16[64,1024]{1,0:T(8,128)(2,1)S(1)} %add_convert_fusion.2.refs_0_), channel_id=1, source_target_pairs={{0,4},{4,0},{8,12},{12,8},{1,5},{5,1},{9,13},{13,9},{2,6},{6,2},{1... | collective-permute-start | bytes 393224 | tf_op jit(solution)/shard_map/ppermute | solution.py:142
  113.3 5.2 %collective-permute-start.41 = (bf16[64,1024]{1,0:T(8,128)(2,1)S(1)}, bf16[64,1024]{1,0:T(8,128)(2,1)S(1)}, u32[]{:S(2)}, u32[]{:S(2)}) collective-permute-start(bf16[64,1024]{1,0:T(8,128)(2,1)S(1)} %shard_map.70), channel_id=1, source_target_pairs={{0,1},{1,0},{2,3},{3,2},{4,5},{5,4},{6,7},{7,6},{8,9},{9,8},{10,11... | collective-permute-start | bytes 393224 | tf_op jit(solution)/shard_map/ppermute | solution.py:142
  115.3 8.7 %collective-permute-start.39 = (bf16[64,1024]{1,0:T(8,128)(2,1)S(1)}, bf16[64,1024]{1,0:T(8,128)(2,1)S(1)}, u32[]{:S(2)}, u32[]{:S(2)}) collective-permute-start(bf16[64,1024]{1,0:T(8,128)(2,1)S(1)} %get-tuple-element.425), channel_id=1, source_target_pairs={{0,8},{4,12},{8,0},{12,4},{1,9},{5,13},{9,1},{13,5},{2,10},{6,14},... | collective-permute-start | bytes 393224 | tf_op jit(solution)/shard_map/ppermute | solution.py:142
  118.6 5.0 %collective-permute-start.42 = (bf16[64,1024]{1,0:T(8,128)(2,1)S(1)}, bf16[64,1024]{1,0:T(8,128)(2,1)S(1)}, u32[]{:S(2)}, u32[]{:S(2)}) collective-permute-start(bf16[64,1024]{1,0:T(8,128)(2,1)S(1)} %get-tuple-element.423), channel_id=1, source_target_pairs={{0,2},{1,3},{2,0},{3,1},{4,6},{5,7},{6,4},{7,5},{8,10},{9,11},{10,... | collective-permute-start | bytes 393224 | tf_op jit(solution)/shard_map/ppermute | solution.py:142
  124.1 5.0 %collective-permute-start.43 = (bf16[64,1024]{1,0:T(8,128)(2,1)S(1)}, bf16[64,1024]{1,0:T(8,128)(2,1)S(1)}, u32[]{:S(2)}, u32[]{:S(2)}) collective-permute-start(bf16[64,1024]{1,0:T(8,128)(2,1)S(1)} %add_convert_fusion.1.refs_0_), channel_id=1, source_target_pairs={{0,4},{4,0},{8,12},{12,8},{1,5},{5,1},{9,13},{13,9},{2,6},{6,2},{1... | collective-permute-start | bytes 393224 | tf_op jit(solution)/shard_map/ppermute | solution.py:142
  124.9 5.2 %collective-permute-start.45 = (bf16[64,1024]{1,0:T(8,128)(2,1)S(1)}, bf16[64,1024]{1,0:T(8,128)(2,1)S(1)}, u32[]{:S(2)}, u32[]{:S(2)}) collective-permute-start(bf16[64,1024]{1,0:T(8,128)(2,1)S(1)} %shard_map.72), channel_id=1, source_target_pairs={{0,1},{1,0},{2,3},{3,2},{4,5},{5,4},{6,7},{7,6},{8,9},{9,8},{10,11... | collective-permute-start | bytes 393224 | tf_op jit(solution)/shard_map/ppermute | solution.py:142
  125.1 6.8 %collective-permute-start.44 = (bf16[64,1024]{1,0:T(8,128)(2,1)S(1)}, bf16[64,1024]{1,0:T(8,128)(2,1)S(1)}, u32[]{:S(2)}, u32[]{:S(2)}) collective-permute-start(bf16[64,1024]{1,0:T(8,128)(2,1)S(1)} %subtract_convert_fusion.1), channel_id=1, source_target_pairs={{0,1},{1,0},{2,3},{3,2},{4,5},{5,4},{6,7},{7,6},{8,9},{9,8},{10,11... | collective-permute-start | bytes 393224 | tf_op jit(solution)/shard_map/ppermute | solution.py:142
  130.1 5.0 %collective-permute-start.47 = (bf16[64,1024]{1,0:T(8,128)(2,1)S(1)}, bf16[64,1024]{1,0:T(8,128)(2,1)S(1)}, u32[]{:S(2)}, u32[]{:S(2)}) collective-permute-start(bf16[64,1024]{1,0:T(8,128)(2,1)S(1)} %get-tuple-element.421), channel_id=1, source_target_pairs={{0,2},{1,3},{2,0},{3,1},{4,6},{5,7},{6,4},{7,5},{8,10},{9,11},{10,... | collective-permute-start | bytes 393224 | tf_op jit(solution)/shard_map/ppermute | solution.py:142
  132.6 5.0 %collective-permute-start.46 = (bf16[64,1024]{1,0:T(8,128)(2,1)S(1)}, bf16[64,1024]{1,0:T(8,128)(2,1)S(1)}, u32[]{:S(2)}, u32[]{:S(2)}) collective-permute-start(bf16[64,1024]{1,0:T(8,128)(2,1)S(1)} %shard_map.74), channel_id=1, source_target_pairs={{0,4},{4,0},{8,12},{12,8},{1,5},{5,1},{9,13},{13,9},{2,6},{6,2},{1... | collective-permute-start | bytes 393224 | tf_op jit(solution)/shard_map/ppermute | solution.py:142
  135.2 2.5 %collective-permute-start.48 = (bf16[64,1024]{1,0:T(8,128)(2,1)S(1)}, bf16[64,1024]{1,0:T(8,128)(2,1)S(1)}, u32[]{:S(2)}, u32[]{:S(2)}) collective-permute-start(bf16[64,1024]{1,0:T(8,128)(2,1)S(1)} %subtract_convert_fusion), channel_id=1, source_target_pairs={{0,1},{1,0},{2,3},{3,2},{4,5},{5,4},{6,7},{7,6},{8,9},{9,8},{10,11... | collective-permute-start | bytes 393224 | tf_op jit(solution)/shard_map/ppermute | solution.py:142
  138.5 6.4 %collective-permute-start.49 = (bf16[64,1024]{1,0:T(8,128)(2,1)S(1)}, bf16[64,1024]{1,0:T(8,128)(2,1)S(1)}, u32[]{:S(2)}, u32[]{:S(2)}) collective-permute-start(bf16[64,1024]{1,0:T(8,128)(2,1)S(1)} %shard_map.76), channel_id=1, source_target_pairs={{0,4},{4,0},{8,12},{12,8},{1,5},{5,1},{9,13},{13,9},{2,6},{6,2},{1... | collective-permute-start | bytes 393224 | tf_op jit(solution)/shard_map/ppermute | solution.py:142
  138.9 7.8 %collective-permute-start.50 = (bf16[64,1024]{1,0:T(8,128)(2,1)S(1)}, bf16[64,1024]{1,0:T(8,128)(2,1)S(1)}, u32[]{:S(2)}, u32[]{:S(2)}) collective-permute-start(bf16[64,1024]{1,0:T(8,128)(2,1)S(1)} %fusion), channel_id=1, source_target_pairs={{8,0},{4,12},{9,1},{5,13},{10,2},{6,14},{11,3},{7,15},{24,16},{20,... | collective-permute-start | bytes 393224 | tf_op jit(solution)/shard_map/ppermute | solution.py:260
  144.9 4.0 %collective-permute-start.51 = (bf16[64,1024]{1,0:T(8,128)(2,1)S(1)}, bf16[64,1024]{1,0:T(8,128)(2,1)S(1)}, u32[]{:S(2)}, u32[]{:S(2)}) collective-permute-start(bf16[64,1024]{1,0:T(8,128)(2,1)S(1)} %fusion.1), channel_id=1, source_target_pairs={{12,4},{0,8},{13,5},{1,9},{14,6},{2,10},{15,7},{3,11},{28,20},{16,... | collective-permute-start | bytes 393224 | tf_op jit(solution)/shard_map/ppermute | solution.py:260
  146.6 2.4 %copy-start.3 = (bf16[5,1024,64]{1,2,0:T(8,128)(2,1)}, bf16[5,1024,64]{1,2,0:T(8,128)(2,1)S(1)}, u32[]{:S(2)}) copy-start(bf16[5,1024,64]{1,2,0:T(8,128)(2,1)S(1)} %bitcast_dynamic-update-slice_fusion) | copy-start | bytes 1966084

commit v15 on v13

--- a/solution.py
+++ b/solution.py
@@ -151,6 +151,7 @@
 
     def per_device(factor_blocks, inverse_blocks, right_sides):
         steps_total, group_rows, angles = right_sides.shape
+        col_rows = inverse_blocks.shape[1]
         last_step = steps_total - 1
         place = lax.axis_index("row")
         core = lax.axis_index("col") & 1
@@ -227,6 +228,15 @@
             st["own"] = order.run(work, base[step - 1, s], st["sum"], *arrived)
             st["swap"] = trade(st["own"], "col", 1)
 
+        def trade_sums(value, step, keep=lambda z: True):
+            pairs = []
+            for z in range(n_row):
+                for c in range(n_col):
+                    first_place = z - z % step
+                    if keep(z ^ step) and first_place * group_rows < (c + 1) * col_rows:
+                        pairs.append((z * n_col + c, (z ^ step) * n_col + c))
+            return lax.ppermute(value, ("row", "col"), pairs)
+
         def inverse_own(s, step):
             st = state[s]
             if exact and step == last_step:
@@ -236,7 +246,7 @@
             leaving = order.run(
                 lambda block, x: product(block, [x], kind=jnp.bfloat16), inverses[step], st["own"]
             )
-            st["flight"] = trade(leaving, "row", 1)
+            st["flight"] = trade_sums(leaving, 1)
 
         def inverse_other(s, step):
             st = state[s]
@@ -252,12 +262,12 @@
 
         def cross(s):
             st = state[s]
-            st["flight"] = trade(st["leaving"], "row", 2) if n_row > 2 else None
+            st["flight"] = trade_sums(st["leaving"], 2) if n_row > 2 else None
 
         def final_cross(s):
             st = state[s]
-            pairs = [(r ^ 2, r) for r in range(n_row) if r in [unit_place(s, h) for h in range(2)]]
-            st["flight"] = lax.ppermute(st["leaving"], "row", pairs)
+            places = [unit_place(s, h) for h in range(2)]
+            st["flight"] = trade_sums(st["leaving"], 2, lambda r: r in places)
 
         def solve(s, step):
             def work(value, *arrived):
@@ -276,7 +286,7 @@
             state[s]["total"], leaving = order.run(
                 lambda v, w: first_products(s, side_ref, v, w), right, inverses[0]
             )
-            state[s]["flight"] = trade(leaving, "row", 1)
+            state[s]["flight"] = trade_sums(leaving, 1)
 
         first(0)
         first(1)

time: 146 us -> 171 us (1.17)
  the two profiles are of different devices: /device:TPU:0 before, /device:TPU:18 now
where the time goes in v15:
time: 171 us; the launch traced here: 170 us
  starting transfers between devices  92.8 us (54%)
  Pallas kernels  32 us (19%)
  waiting for transfers between devices  24.2 us (14%)
  local copies, waits for them, and re-layouts  17.7 us (10%)
  other arithmetic  2.27 us (1%)
    ppermute x20, starting transfers between devices, trade_sums(): return lax.ppermute(value, ('row', 'col'), pairs)  63.8 us
    pallas_call x38, Pallas kernels, product(): pl.pallas_call(functools.partial(product_kernel, len(units)), out_shape=j...  29.4 us
    ppermute x32, starting transfers between devices, trade(): return lax.ppermute(value, axis, [(i, i ^ step) for i in range(size)])  29 us
    ppermute x20, waiting for transfers between devices, trade_sums(): return lax.ppermute(value, ('row', 'col'), pairs)  17.8 us
    squeeze x16, local copies, waits for them, and re-layouts, block(): self.last = lax.optimization_barrier(self.run(lambda v: v[index], blocks))  15.6 us
    ppermute x32, waiting for transfers between devices, trade(): return lax.ppermute(value, axis, [(i, i ^ step) for i in range(size)])  6.35 us
  transfers between devices with their start and end apart: 52, of which 13 were waited for; matrix products, arithmetic and copies ran while one was open for 9% of the time, Pallas kernels for 18%

profile of v15, /device:TPU:18, one launch (start us, length us, event | category | flops | bytes accessed | tf_op | source)
XLA Modules:
  0.0 170.3 jit_solution(3393694118080263788)
XLA Ops:
  0.0 1.8 %slice_bitcast_fusion.14.block = bf16[1024,1024]{1,0:T(8,128)(2,1)S(1)} fusion(bf16[5,1024,1024]{2,1,0:T(8,128)(2,1)} %param.4), kind=kLoop, calls=%fused_computation.14 | loop fusion | bytes 4194304 | tf_op jit(solution)/shard_map/squeeze | solution.py:135
  1.8 1.1 slice_bitcast_fusion.15.right
  2.9 0.8 shard_map.37
  3.7 3.5 %collective-permute-start.1 = (bf16[64,1024]{1,0:T(8,128)(2,1)S(1)}, bf16[64,1024]{1,0:T(8,128)(2,1)S(1)}, u32[]{:S(2)}, u32[]{:S(2)}) collective-permute-start(bf16[64,1024]{1,0:T(8,128)(2,1)S(1)} %get-tuple-element.222), channel_id=1, source_target_pairs={{0,4},{1,5},{2,6},{3,7},{5,1},{6,2},{7,3},{10,14},{11,15},{15,11},... | collective-permute-start | bytes 393224 | tf_op jit(solution)/shard_map/ppermute | solution.py:238
  7.2 0.9 shard_map.38
  8.1 1.3 collective-permute-start
  9.4 1.7 %copy-done = bf16[5,1024,256]{2,1,0:T(8,128)(2,1)S(1)} copy-done((bf16[5,1024,256]{2,1,0:T(8,128)(2,1)S(1)}, bf16[5,1024,256]{2,1,0:T(8,128)(2,1)}, u32[]{:S(2)}) %copy-start) | copy-done | bytes 2621464
  11.1 0.9 shard_map.39
  12.2 3.3 %collective-permute-start.2 = (bf16[64,1024]{1,0:T(8,128)(2,1)S(1)}, bf16[64,1024]{1,0:T(8,128)(2,1)S(1)}, u32[]{:S(2)}, u32[]{:S(2)}) collective-permute-start(bf16[64,1024]{1,0:T(8,128)(2,1)S(1)} %get-tuple-element.453), channel_id=1, source_target_pairs={{0,8},{1,9},{2,10},{3,11},{4,12},{5,13},{6,14},{7,15},{10,2},{11,3... | collective-permute-start | bytes 393224 | tf_op jit(solution)/shard_map/ppermute | solution.py:238
  15.5 1.8 %slice_bitcast_fusion.13.block = bf16[1024,1024]{1,0:T(8,128)(2,1)S(1)} fusion(bf16[10,1024,1024]{2,1,0:T(8,128)(2,1)} %param.3), kind=kLoop, calls=%fused_computation.13 | loop fusion | bytes 4194304 | tf_op jit(solution)/shard_map/squeeze | solution.py:135
  17.3 3.5 %collective-permute-done.2 = bf16[64,1024]{1,0:T(8,128)(2,1)S(1)} collective-permute-done((bf16[64,1024]{1,0:T(8,128)(2,1)S(1)}, bf16[64,1024]{1,0:T(8,128)(2,1)S(1)}, u32[]{:S(2)}, u32[]{:S(2)}) %collective-permute-start.2) | collective-permute-done | bytes 131104 | tf_op jit(solution)/shard_map/ppermute | solution.py:238
  20.9 3.0 %collective-permute-start.4 = (bf16[64,1024]{1,0:T(8,128)(2,1)S(1)}, bf16[64,1024]{1,0:T(8,128)(2,1)S(1)}, u32[]{:S(2)}, u32[]{:S(2)}) collective-permute-start(bf16[64,1024]{1,0:T(8,128)(2,1)S(1)} %add_convert_fusion.8.refs_0_.refs_1_), channel_id=1, source_target_pairs={{0,4},{4,0},{8,12},{12,8},{1,5},{5,1},{9,13},{13,9},{2,6},{6,2},{1... | collective-permute-start | bytes 393224 | tf_op jit(solution)/shard_map/ppermute | solution.py:142
  24.9 2.3 %collective-permute-start.3 = (bf16[64,1024]{1,0:T(8,128)(2,1)S(1)}, bf16[64,1024]{1,0:T(8,128)(2,1)S(1)}, u32[]{:S(2)}, u32[]{:S(2)}) collective-permute-start(bf16[64,1024]{1,0:T(8,128)(2,1)S(1)} %get-tuple-element.451), channel_id=1, source_target_pairs={{0,8},{1,9},{2,10},{3,11},{4,12},{5,13},{6,14},{7,15},{10,2},{11,3... | collective-permute-start | bytes 393224 | tf_op jit(solution)/shard_map/ppermute | solution.py:238
  27.2 0.8 collective-permute-done.4.refs_0_
  28.9 2.5 %slice_bitcast_fusion.12.block = bf16[1024,1024]{1,0:T(8,128)(2,1)S(1)} fusion(bf16[10,1024,1024]{2,1,0:T(8,128)(2,1)} %param.3), kind=kLoop, calls=%fused_computation.12 | loop fusion | bytes 4194304 | tf_op jit(solution)/shard_map/squeeze | solution.py:135
  31.4 1.8 %slice_bitcast_fusion.11.block = bf16[1024,1024]{1,0:T(8,128)(2,1)S(1)} fusion(bf16[5,1024,1024]{2,1,0:T(8,128)(2,1)} %param.4), kind=kLoop, calls=%fused_computation.11 | loop fusion | bytes 4194304 | tf_op jit(solution)/shard_map/squeeze | solution.py:135
  34.0 2.8 %collective-permute-start.6 = (bf16[64,1024]{1,0:T(8,128)(2,1)S(1)}, bf16[64,1024]{1,0:T(8,128)(2,1)S(1)}, u32[]{:S(2)}, u32[]{:S(2)}) collective-permute-start(bf16[64,1024]{1,0:T(8,128)(2,1)S(1)} %add_convert_fusion.7.refs_0_.refs_3_), channel_id=1, source_target_pairs={{0,4},{4,0},{8,12},{12,8},{1,5},{5,1},{9,13},{13,9},{2,6},{6,2},{1... | collective-permute-start | bytes 393224 | tf_op jit(solution)/shard_map/ppermute | solution.py:142
  38.9 1.9 %collective-permute-start.11 = (bf16[64,1024]{1,0:T(8,128)(2,1)S(1)}, bf16[64,1024]{1,0:T(8,128)(2,1)S(1)}, u32[]{:S(2)}, u32[]{:S(2)}) collective-permute-start(bf16[64,1024]{1,0:T(8,128)(2,1)S(1)} %shard_map.43), channel_id=1, source_target_pairs={{0,4},{1,5},{2,6},{3,7},{5,1},{6,2},{7,3},{10,14},{11,15},{15,11},... | collective-permute-start | bytes 393224 | tf_op jit(solution)/shard_map/ppermute | solution.py:238
  42.0 0.9 shard_map.45
  44.1 4.7 %collective-permute-start.14 = (bf16[64,1024]{1,0:T(8,128)(2,1)S(1)}, bf16[64,1024]{1,0:T(8,128)(2,1)S(1)}, u32[]{:S(2)}, u32[]{:S(2)}) collective-permute-start(bf16[64,1024]{1,0:T(8,128)(2,1)S(1)} %get-tuple-element.445), channel_id=1, source_target_pairs={{0,8},{1,9},{2,10},{3,11},{4,12},{5,13},{6,14},{7,15},{10,2},{11,3... | collective-permute-start | bytes 393224 | tf_op jit(solution)/shard_map/ppermute | solution.py:238
  49.7 3.7 %collective-permute-start.13 = (bf16[64,1024]{1,0:T(8,128)(2,1)S(1)}, bf16[64,1024]{1,0:T(8,128)(2,1)S(1)}, u32[]{:S(2)}, u32[]{:S(2)}) collective-permute-start(bf16[64,1024]{1,0:T(8,128)(2,1)S(1)} %shard_map.47), channel_id=1, source_target_pairs={{0,4},{1,5},{2,6},{3,7},{5,1},{6,2},{7,3},{10,14},{11,15},{15,11},... | collective-permute-start | bytes 393224 | tf_op jit(solution)/shard_map/ppermute | solution.py:238
  54.2 3.0 %collective-permute-start.16 = (bf16[64,1024]{1,0:T(8,128)(2,1)S(1)}, bf16[64,1024]{1,0:T(8,128)(2,1)S(1)}, u32[]{:S(2)}, u32[]{:S(2)}) collective-permute-start(bf16[64,1024]{1,0:T(8,128)(2,1)S(1)} %add_convert_fusion.6.refs_0_.refs_1_), channel_id=1, source_target_pairs={{0,4},{4,0},{8,12},{12,8},{1,5},{5,1},{9,13},{13,9},{2,6},{6,2},{1... | collective-permute-start | bytes 393224 | tf_op jit(solution)/shard_map/ppermute | solution.py:142
  57.2 0.8 shard_map.49
  58.1 4.0 %collective-permute-start.15 = (bf16[64,1024]{1,0:T(8,128)(2,1)S(1)}, bf16[64,1024]{1,0:T(8,128)(2,1)S(1)}, u32[]{:S(2)}, u32[]{:S(2)}) collective-permute-start(bf16[64,1024]{1,0:T(8,128)(2,1)S(1)} %get-tuple-element.443), channel_id=1, source_target_pairs={{0,8},{1,9},{2,10},{3,11},{4,12},{5,13},{6,14},{7,15},{10,2},{11,3... | collective-permute-start | bytes 393224 | tf_op jit(solution)/shard_map/ppermute | solution.py:238
  62.1 0.8 shard_map.50
  63.2 0.9 shard_map.51.refs_4_
  64.3 1.8 %slice_bitcast_fusion.7.block = bf16[1024,1024]{1,0:T(8,128)(2,1)S(1)} fusion(bf16[5,1024,1024]{2,1,0:T(8,128)(2,1)} %param.4), kind=kLoop, calls=%fused_computation.7 | loop fusion | bytes 4194304 | tf_op jit(solution)/shard_map/squeeze | solution.py:135
  66.1 1.5 collective-permute-done.15
  67.6 3.5 %collective-permute-start.18 = (bf16[64,1024]{1,0:T(8,128)(2,1)S(1)}, bf16[64,1024]{1,0:T(8,128)(2,1)S(1)}, u32[]{:S(2)}, u32[]{:S(2)}) collective-permute-start(bf16[64,1024]{1,0:T(8,128)(2,1)S(1)} %add_convert_fusion.5.refs_0_.refs_3_), channel_id=1, source_target_pairs={{0,4},{4,0},{8,12},{12,8},{1,5},{5,1},{9,13},{13,9},{2,6},{6,2},{1... | collective-permute-start | bytes 393224 | tf_op jit(solution)/shard_map/ppermute | solution.py:142
  71.1 0.8 shard_map.52
  73.3 2.1 %collective-permute-start.23 = (bf16[64,1024]{1,0:T(8,128)(2,1)S(1)}, bf16[64,1024]{1,0:T(8,128)(2,1)S(1)}, u32[]{:S(2)}, u32[]{:S(2)}) collective-permute-start(bf16[64,1024]{1,0:T(8,128)(2,1)S(1)} %shard_map.53), channel_id=1, source_target_pairs={{0,4},{1,5},{2,6},{3,7},{5,1},{6,2},{7,3},{10,14},{11,15},{15,11},... | collective-permute-start | bytes 393224 | tf_op jit(solution)/shard_map/ppermute | solution.py:238
  75.4 0.8 shard_map.54
  76.5 0.9 shard_map.55
  78.5 4.4 %collective-permute-start.26 = (bf16[64,1024]{1,0:T(8,128)(2,1)S(1)}, bf16[64,1024]{1,0:T(8,128)(2,1)S(1)}, u32[]{:S(2)}, u32[]{:S(2)}) collective-permute-start(bf16[64,1024]{1,0:T(8,128)(2,1)S(1)} %get-tuple-element.437), channel_id=1, source_target_pairs={{0,8},{1,9},{2,10},{3,11},{4,12},{5,13},{6,14},{7,15},{10,2},{11,3... | collective-permute-start | bytes 393224 | tf_op jit(solution)/shard_map/ppermute | solution.py:238
  83.9 3.6 %collective-permute-start.25 = (bf16[64,1024]{1,0:T(8,128)(2,1)S(1)}, bf16[64,1024]{1,0:T(8,128)(2,1)S(1)}, u32[]{:S(2)}, u32[]{:S(2)}) collective-permute-start(bf16[64,1024]{1,0:T(8,128)(2,1)S(1)} %shard_map.57), channel_id=1, source_target_pairs={{0,4},{1,5},{2,6},{3,7},{5,1},{6,2},{7,3},{10,14},{11,15},{15,11},... | collective-permute-start | bytes 393224 | tf_op jit(solution)/shard_map/ppermute | solution.py:238
  88.3 3.3 %collective-permute-start.28 = (bf16[64,1024]{1,0:T(8,128)(2,1)S(1)}, bf16[64,1024]{1,0:T(8,128)(2,1)S(1)}, u32[]{:S(2)}, u32[]{:S(2)}) collective-permute-start(bf16[64,1024]{1,0:T(8,128)(2,1)S(1)} %add_convert_fusion.4.refs_0_.refs_1_), channel_id=1, source_target_pairs={{0,4},{4,0},{8,12},{12,8},{1,5},{5,1},{9,13},{13,9},{2,6},{6,2},{1... | collective-permute-start | bytes 393224 | tf_op jit(solution)/shard_map/ppermute | solution.py:142
  91.7 0.8 shard_map.59
  92.6 3.6 %collective-permute-start.27 = (bf16[64,1024]{1,0:T(8,128)(2,1)S(1)}, bf16[64,1024]{1,0:T(8,128)(2,1)S(1)}, u32[]{:S(2)}, u32[]{:S(2)}) collective-permute-start(bf16[64,1024]{1,0:T(8,128)(2,1)S(1)} %get-tuple-element.435), channel_id=1, source_target_pairs={{0,8},{1,9},{2,10},{3,11},{4,12},{5,13},{6,14},{7,15},{10,2},{11,3... | collective-permute-start | bytes 393224 | tf_op jit(solution)/shard_map/ppermute | solution.py:238
  96.2 0.8 shard_map.60
  97.3 0.9 shard_map.61.refs_4_
  98.4 0.9 shard_map.62.refs_4_
  99.5 1.8 %slice_bitcast_fusion.2.block = bf16[1024,1024]{1,0:T(8,128)(2,1)S(1)} fusion(bf16[5,1024,1024]{2,1,0:T(8,128)(2,1)} %param.4), kind=kLoop, calls=%fused_computation.2 | loop fusion | bytes 4194304 | tf_op jit(solution)/shard_map/squeeze | solution.py:135
  102.0 3.5 %collective-permute-start.30 = (bf16[64,1024]{1,0:T(8,128)(2,1)S(1)}, bf16[64,1024]{1,0:T(8,128)(2,1)S(1)}, u32[]{:S(2)}, u32[]{:S(2)}) collective-permute-start(bf16[64,1024]{1,0:T(8,128)(2,1)S(1)} %add_convert_fusion.3.refs_0_.refs_3_), channel_id=1, source_target_pairs={{0,4},{4,0},{8,12},{12,8},{1,5},{5,1},{9,13},{13,9},{2,6},{6,2},{1... | collective-permute-start | bytes 393224 | tf_op jit(solution)/shard_map/ppermute | solution.py:142
  107.7 1.9 %collective-permute-start.35 = (bf16[64,1024]{1,0:T(8,128)(2,1)S(1)}, bf16[64,1024]{1,0:T(8,128)(2,1)S(1)}, u32[]{:S(2)}, u32[]{:S(2)}) collective-permute-start(bf16[64,1024]{1,0:T(8,128)(2,1)S(1)} %shard_map.64), channel_id=1, source_target_pairs={{0,4},{1,5},{2,6},{3,7},{5,1},{6,2},{7,3},{10,14},{11,15},{15,11},... | collective-permute-start | bytes 393224 | tf_op jit(solution)/shard_map/ppermute | solution.py:238
  109.6 0.8 shard_map.65
  110.7 0.9 shard_map.66
  112.9 4.4 %collective-permute-start.38 = (bf16[64,1024]{1,0:T(8,128)(2,1)S(1)}, bf16[64,1024]{1,0:T(8,128)(2,1)S(1)}, u32[]{:S(2)}, u32[]{:S(2)}) collective-permute-start(bf16[64,1024]{1,0:T(8,128)(2,1)S(1)} %get-tuple-element.429), channel_id=1, source_target_pairs={{0,8},{1,9},{2,10},{3,11},{4,12},{5,13},{6,14},{7,15},{10,2},{11,3... | collective-permute-start | bytes 393224 | tf_op jit(solution)/shard_map/ppermute | solution.py:238
  118.2 3.6 %collective-permute-start.37 = (bf16[64,1024]{1,0:T(8,128)(2,1)S(1)}, bf16[64,1024]{1,0:T(8,128)(2,1)S(1)}, u32[]{:S(2)}, u32[]{:S(2)}) collective-permute-start(bf16[64,1024]{1,0:T(8,128)(2,1)S(1)} %shard_map.68), channel_id=1, source_target_pairs={{0,4},{1,5},{2,6},{3,7},{5,1},{6,2},{7,3},{10,14},{11,15},{15,11},... | collective-permute-start | bytes 393224 | tf_op jit(solution)/shard_map/ppermute | solution.py:238
  122.7 3.3 %collective-permute-start.40 = (bf16[64,1024]{1,0:T(8,128)(2,1)S(1)}, bf16[64,1024]{1,0:T(8,128)(2,1)S(1)}, u32[]{:S(2)}, u32[]{:S(2)}) collective-permute-start(bf16[64,1024]{1,0:T(8,128)(2,1)S(1)} %add_convert_fusion.2.refs_0_), channel_id=1, source_target_pairs={{0,4},{4,0},{8,12},{12,8},{1,5},{5,1},{9,13},{13,9},{2,6},{6,2},{1... | collective-permute-start | bytes 393224 | tf_op jit(solution)/shard_map/ppermute | solution.py:142
  126.9 3.9 %collective-permute-start.39 = (bf16[64,1024]{1,0:T(8,128)(2,1)S(1)}, bf16[64,1024]{1,0:T(8,128)(2,1)S(1)}, u32[]{:S(2)}, u32[]{:S(2)}) collective-permute-start(bf16[64,1024]{1,0:T(8,128)(2,1)S(1)} %get-tuple-element.427), channel_id=1, source_target_pairs={{0,8},{1,9},{2,10},{3,11},{4,12},{5,13},{6,14},{7,15},{10,2},{11,3... | collective-permute-start | bytes 393224 | tf_op jit(solution)/shard_map/ppermute | solution.py:238
  130.8 0.8 shard_map.71
  131.7 1.8 %slice_bitcast_fusion.block = bf16[1024,1024]{1,0:T(8,128)(2,1)S(1)} fusion(bf16[5,1024,1024]{2,1,0:T(8,128)(2,1)} %param.4), kind=kLoop, calls=%fused_computation | loop fusion | bytes 4194304 | tf_op jit(solution)/shard_map/squeeze | solution.py:135
  133.5 3.4 %collective-permute-done.42 = bf16[64,1024]{1,0:T(8,128)(2,1)S(1)} collective-permute-done((bf16[64,1024]{1,0:T(8,128)(2,1)S(1)}, bf16[64,1024]{1,0:T(8,128)(2,1)S(1)}, u32[]{:S(2)}, u32[]{:S(2)}) %collective-permute-start.42) | collective-permute-done | bytes 131104 | tf_op jit(solution)/shard_map/ppermute | solution.py:142
  137.0 2.8 %collective-permute-start.43 = (bf16[64,1024]{1,0:T(8,128)(2,1)S(1)}, bf16[64,1024]{1,0:T(8,128)(2,1)S(1)}, u32[]{:S(2)}, u32[]{:S(2)}) collective-permute-start(bf16[64,1024]{1,0:T(8,128)(2,1)S(1)} %add_convert_fusion.1.refs_0_), channel_id=1, source_target_pairs={{0,4},{4,0},{8,12},{12,8},{1,5},{5,1},{9,13},{13,9},{2,6},{6,2},{1... | collective-permute-start | bytes 393224 | tf_op jit(solution)/shard_map/ppermute | solution.py:142
  139.9 0.8 shard_map.72
  141.3 2.1 %collective-permute-done.43.refs_0_ = bf16[64,1024]{1,0:T(8,128)(2,1)S(1)} collective-permute-done((bf16[64,1024]{1,0:T(8,128)(2,1)S(1)}, bf16[64,1024]{1,0:T(8,128)(2,1)S(1)}, u32[]{:S(2)}, u32[]{:S(2)}) %collective-permute-start.43) | collective-permute-done | bytes 131104 | tf_op jit(solution)/shard_map/ppermute | solution.py:142
  143.4 0.8 shard_map.73
  145.1 3.7 %collective-permute-start.46 = (bf16[64,1024]{1,0:T(8,128)(2,1)S(1)}, bf16[64,1024]{1,0:T(8,128)(2,1)S(1)}, u32[]{:S(2)}, u32[]{:S(2)}) collective-permute-start(bf16[64,1024]{1,0:T(8,128)(2,1)S(1)} %shard_map.74), channel_id=1, source_target_pairs={{0,4},{1,5},{2,6},{3,7},{5,1},{6,2},{7,3},{10,14},{11,15},{15,11},... | collective-permute-start | bytes 393224 | tf_op jit(solution)/shard_map/ppermute | solution.py:238
  149.7 1.6 collective-permute-done.46
  152.1 4.4 %collective-permute-start.49 = (bf16[64,1024]{1,0:T(8,128)(2,1)S(1)}, bf16[64,1024]{1,0:T(8,128)(2,1)S(1)}, u32[]{:S(2)}, u32[]{:S(2)}) collective-permute-start(bf16[64,1024]{1,0:T(8,128)(2,1)S(1)} %shard_map.76), channel_id=1, source_target_pairs={{0,4},{1,5},{2,6},{3,7},{5,1},{6,2},{7,3},{10,14},{11,15},{15,11},... | collective-permute-start | bytes 393224 | tf_op jit(solution)/shard_map/ppermute | solution.py:238
  156.5 2.2 %collective-permute-start.50 = (bf16[64,1024]{1,0:T(8,128)(2,1)S(1)}, bf16[64,1024]{1,0:T(8,128)(2,1)S(1)}, u32[]{:S(2)}, u32[]{:S(2)}) collective-permute-start(bf16[64,1024]{1,0:T(8,128)(2,1)S(1)} %fusion), channel_id=1, source_target_pairs={{4,12},{5,13},{6,14},{7,15},{10,2},{11,3},{20,28},{21,29},{22,30},... | collective-permute-start | bytes 393224 | tf_op jit(solution)/shard_map/ppermute | solution.py:238
  159.5 2.2 %collective-permute-done.49 = bf16[64,1024]{1,0:T(8,128)(2,1)S(1)} collective-permute-done((bf16[64,1024]{1,0:T(8,128)(2,1)S(1)}, bf16[64,1024]{1,0:T(8,128)(2,1)S(1)}, u32[]{:S(2)}, u32[]{:S(2)}) %collective-permute-start.49) | collective-permute-done | bytes 131104 | tf_op jit(solution)/shard_map/ppermute | solution.py:238
  161.8 1.3 collective-permute-start.51
  163.2 6.4 %collective-permute-done.51 = bf16[64,1024]{1,0:T(8,128)(2,1)S(1)} collective-permute-done((bf16[64,1024]{1,0:T(8,128)(2,1)S(1)}, bf16[64,1024]{1,0:T(8,128)(2,1)S(1)}, u32[]{:S(2)}, u32[]{:S(2)}) %collective-permute-start.51) | collective-permute-done | bytes 131104 | tf_op jit(solution)/shard_map/ppermute | solution.py:238
  (148 shorter events, 27.0 us)
Async XLA Ops:
  3.7 8.5 %collective-permute-start.1 = (bf16[64,1024]{1,0:T(8,128)(2,1)S(1)}, bf16[64,1024]{1,0:T(8,128)(2,1)S(1)}, u32[]{:S(2)}, u32[]{:S(2)}) collective-permute-start(bf16[64,1024]{1,0:T(8,128)(2,1)S(1)} %get-tuple-element.222), channel_id=1, source_target_pairs={{0,4},{1,5},{2,6},{3,7},{5,1},{6,2},{7,3},{10,14},{11,15},{15,11},... | collective-permute-start | bytes 393224 | tf_op jit(solution)/shard_map/ppermute | solution.py:238
  8.1 16.8 %collective-permute-start = (bf16[64,1024]{1,0:T(8,128)(2,1)S(1)}, bf16[64,1024]{1,0:T(8,128)(2,1)S(1)}, u32[]{:S(2)}, u32[]{:S(2)}) collective-permute-start(bf16[64,1024]{1,0:T(8,128)(2,1)S(1)} %get-tuple-element.221), channel_id=1, source_target_pairs={{0,4},{1,5},{2,6},{3,7},{5,1},{6,2},{7,3},{10,14},{11,15},{15,11},... | collective-permute-start | bytes 393224 | tf_op jit(solution)/shard_map/ppermute | solution.py:238
  9.4 1.7 %copy-start = (bf16[5,1024,256]{2,1,0:T(8,128)(2,1)S(1)}, bf16[5,1024,256]{2,1,0:T(8,128)(2,1)}, u32[]{:S(2)}) copy-start(bf16[5,1024,256]{2,1,0:T(8,128)(2,1)} %sides) | copy-start | bytes 7864324
  12.2 8.6 %collective-permute-start.2 = (bf16[64,1024]{1,0:T(8,128)(2,1)S(1)}, bf16[64,1024]{1,0:T(8,128)(2,1)S(1)}, u32[]{:S(2)}, u32[]{:S(2)}) collective-permute-start(bf16[64,1024]{1,0:T(8,128)(2,1)S(1)} %get-tuple-element.453), channel_id=1, source_target_pairs={{0,8},{1,9},{2,10},{3,11},{4,12},{5,13},{6,14},{7,15},{10,2},{11,3... | collective-permute-start | bytes 393224 | tf_op jit(solution)/shard_map/ppermute | solution.py:238
  20.9 7.1 %collective-permute-start.4 = (bf16[64,1024]{1,0:T(8,128)(2,1)S(1)}, bf16[64,1024]{1,0:T(8,128)(2,1)S(1)}, u32[]{:S(2)}, u32[]{:S(2)}) collective-permute-start(bf16[64,1024]{1,0:T(8,128)(2,1)S(1)} %add_convert_fusion.8.refs_0_.refs_1_), channel_id=1, source_target_pairs={{0,4},{4,0},{8,12},{12,8},{1,5},{5,1},{9,13},{13,9},{2,6},{6,2},{1... | collective-permute-start | bytes 393224 | tf_op jit(solution)/shard_map/ppermute | solution.py:142
  24.6 4.1 %collective-permute-start.5 = (bf16[64,1024]{1,0:T(8,128)(2,1)S(1)}, bf16[64,1024]{1,0:T(8,128)(2,1)S(1)}, u32[]{:S(2)}, u32[]{:S(2)}) collective-permute-start(bf16[64,1024]{1,0:T(8,128)(2,1)S(1)} %shard_map.40), channel_id=1, source_target_pairs={{0,1},{1,0},{2,3},{3,2},{4,5},{5,4},{6,7},{7,6},{8,9},{9,8},{10,11... | collective-permute-start | bytes 393224 | tf_op jit(solution)/shard_map/ppermute | solution.py:142
  24.9 16.9 %copy-start.1 = (bf16[10,1024,1024]{2,1,0:T(8,128)(2,1)S(1)}, bf16[10,1024,1024]{2,1,0:T(8,128)(2,1)}, u32[]{:S(2)}) copy-start(bf16[10,1024,1024]{2,1,0:T(8,128)(2,1)} %param.3) | copy-start | bytes 62914564
  24.9 9.0 %collective-permute-start.3 = (bf16[64,1024]{1,0:T(8,128)(2,1)S(1)}, bf16[64,1024]{1,0:T(8,128)(2,1)S(1)}, u32[]{:S(2)}, u32[]{:S(2)}) collective-permute-start(bf16[64,1024]{1,0:T(8,128)(2,1)S(1)} %get-tuple-element.451), channel_id=1, source_target_pairs={{0,8},{1,9},{2,10},{3,11},{4,12},{5,13},{6,14},{7,15},{10,2},{11,3... | collective-permute-start | bytes 393224 | tf_op jit(solution)/shard_map/ppermute | solution.py:238
  28.8 8.8 %collective-permute-start.7 = (bf16[64,1024]{1,0:T(8,128)(2,1)S(1)}, bf16[64,1024]{1,0:T(8,128)(2,1)S(1)}, u32[]{:S(2)}, u32[]{:S(2)}) collective-permute-start(bf16[64,1024]{1,0:T(8,128)(2,1)S(1)} %get-tuple-element.449), channel_id=1, source_target_pairs={{0,2},{1,3},{2,0},{3,1},{4,6},{5,7},{6,4},{7,5},{8,10},{9,11},{10,... | collective-permute-start | bytes 393224 | tf_op jit(solution)/shard_map/ppermute | solution.py:142
  34.0 6.9 %collective-permute-start.6 = (bf16[64,1024]{1,0:T(8,128)(2,1)S(1)}, bf16[64,1024]{1,0:T(8,128)(2,1)S(1)}, u32[]{:S(2)}, u32[]{:S(2)}) collective-permute-start(bf16[64,1024]{1,0:T(8,128)(2,1)S(1)} %add_convert_fusion.7.refs_0_.refs_3_), channel_id=1, source_target_pairs={{0,4},{4,0},{8,12},{12,8},{1,5},{5,1},{9,13},{13,9},{2,6},{6,2},{1... | collective-permute-start | bytes 393224 | tf_op jit(solution)/shard_map/ppermute | solution.py:142
  37.5 4.2 %collective-permute-start.8 = (bf16[64,1024]{1,0:T(8,128)(2,1)S(1)}, bf16[64,1024]{1,0:T(8,128)(2,1)S(1)}, u32[]{:S(2)}, u32[]{:S(2)}) collective-permute-start(bf16[64,1024]{1,0:T(8,128)(2,1)S(1)} %shard_map.42), channel_id=1, source_target_pairs={{0,1},{1,0},{2,3},{3,2},{4,5},{5,4},{6,7},{7,6},{8,9},{9,8},{10,11... | collective-permute-start | bytes 393224 | tf_op jit(solution)/shard_map/ppermute | solution.py:142
  37.6 5.3 %collective-permute-start.10 = (bf16[64,1024]{1,0:T(8,128)(2,1)S(1)}, bf16[64,1024]{1,0:T(8,128)(2,1)S(1)}, u32[]{:S(2)}, u32[]{:S(2)}) collective-permute-start(bf16[64,1024]{1,0:T(8,128)(2,1)S(1)} %subtract_convert_fusion.7.refs_0_), channel_id=1, source_target_pairs={{0,1},{1,0},{2,3},{3,2},{4,5},{5,4},{6,7},{7,6},{8,9},{9,8},{10,11... | collective-permute-start | bytes 393224 | tf_op jit(solution)/shard_map/ppermute | solution.py:142
  38.9 5.1 %collective-permute-start.11 = (bf16[64,1024]{1,0:T(8,128)(2,1)S(1)}, bf16[64,1024]{1,0:T(8,128)(2,1)S(1)}, u32[]{:S(2)}, u32[]{:S(2)}) collective-permute-start(bf16[64,1024]{1,0:T(8,128)(2,1)S(1)} %shard_map.43), channel_id=1, source_target_pairs={{0,4},{1,5},{2,6},{3,7},{5,1},{6,2},{7,3},{10,14},{11,15},{15,11},... | collective-permute-start | bytes 393224 | tf_op jit(solution)/shard_map/ppermute | solution.py:238
  41.7 7.1 %collective-permute-start.9 = (bf16[64,1024]{1,0:T(8,128)(2,1)S(1)}, bf16[64,1024]{1,0:T(8,128)(2,1)S(1)}, u32[]{:S(2)}, u32[]{:S(2)}) collective-permute-start(bf16[64,1024]{1,0:T(8,128)(2,1)S(1)} %get-tuple-element.447), channel_id=1, source_target_pairs={{0,2},{1,3},{2,0},{3,1},{4,6},{5,7},{6,4},{7,5},{8,10},{9,11},{10,... | collective-permute-start | bytes 393224 | tf_op jit(solution)/shard_map/ppermute | solution.py:142
  44.1 10.1 %collective-permute-start.14 = (bf16[64,1024]{1,0:T(8,128)(2,1)S(1)}, bf16[64,1024]{1,0:T(8,128)(2,1)S(1)}, u32[]{:S(2)}, u32[]{:S(2)}) collective-permute-start(bf16[64,1024]{1,0:T(8,128)(2,1)S(1)} %get-tuple-element.445), channel_id=1, source_target_pairs={{0,8},{1,9},{2,10},{3,11},{4,12},{5,13},{6,14},{7,15},{10,2},{11,3... | collective-permute-start | bytes 393224 | tf_op jit(solution)/shard_map/ppermute | solution.py:238
  48.8 4.6 %collective-permute-start.12 = (bf16[64,1024]{1,0:T(8,128)(2,1)S(1)}, bf16[64,1024]{1,0:T(8,128)(2,1)S(1)}, u32[]{:S(2)}, u32[]{:S(2)}) collective-permute-start(bf16[64,1024]{1,0:T(8,128)(2,1)S(1)} %subtract_convert_fusion.6.refs_0_), channel_id=1, source_target_pairs={{0,1},{1,0},{2,3},{3,2},{4,5},{5,4},{6,7},{7,6},{8,9},{9,8},{10,11... | collective-permute-start | bytes 393224 | tf_op jit(solution)/shard_map/ppermute | solution.py:142
  49.7 8.3 %collective-permute-start.13 = (bf16[64,1024]{1,0:T(8,128)(2,1)S(1)}, bf16[64,1024]{1,0:T(8,128)(2,1)S(1)}, u32[]{:S(2)}, u32[]{:S(2)}) collective-permute-start(bf16[64,1024]{1,0:T(8,128)(2,1)S(1)} %shard_map.47), channel_id=1, source_target_pairs={{0,4},{1,5},{2,6},{3,7},{5,1},{6,2},{7,3},{10,14},{11,15},{15,11},... | collective-permute-start | bytes 393224 | tf_op jit(solution)/shard_map/ppermute | solution.py:238
  54.2 7.9 %collective-permute-start.16 = (bf16[64,1024]{1,0:T(8,128)(2,1)S(1)}, bf16[64,1024]{1,0:T(8,128)(2,1)S(1)}, u32[]{:S(2)}, u32[]{:S(2)}) collective-permute-start(bf16[64,1024]{1,0:T(8,128)(2,1)S(1)} %add_convert_fusion.6.refs_0_.refs_1_), channel_id=1, source_target_pairs={{0,4},{4,0},{8,12},{12,8},{1,5},{5,1},{9,13},{13,9},{2,6},{6,2},{1... | collective-permute-start | bytes 393224 | tf_op jit(solution)/shard_map/ppermute | solution.py:142
  58.0 4.9 %collective-permute-start.17 = (bf16[64,1024]{1,0:T(8,128)(2,1)S(1)}, bf16[64,1024]{1,0:T(8,128)(2,1)S(1)}, u32[]{:S(2)}, u32[]{:S(2)}) collective-permute-start(bf16[64,1024]{1,0:T(8,128)(2,1)S(1)} %shard_map.49), channel_id=1, source_target_pairs={{0,1},{1,0},{2,3},{3,2},{4,5},{5,4},{6,7},{7,6},{8,9},{9,8},{10,11... | collective-permute-start | bytes 393224 | tf_op jit(solution)/shard_map/ppermute | solution.py:142
  58.1 9.5 %collective-permute-start.15 = (bf16[64,1024]{1,0:T(8,128)(2,1)S(1)}, bf16[64,1024]{1,0:T(8,128)(2,1)S(1)}, u32[]{:S(2)}, u32[]{:S(2)}) collective-permute-start(bf16[64,1024]{1,0:T(8,128)(2,1)S(1)} %get-tuple-element.443), channel_id=1, source_target_pairs={{0,8},{1,9},{2,10},{3,11},{4,12},{5,13},{6,14},{7,15},{10,2},{11,3... | collective-permute-start | bytes 393224 | tf_op jit(solution)/shard_map/ppermute | solution.py:238
  63.0 9.0 %collective-permute-start.19 = (bf16[64,1024]{1,0:T(8,128)(2,1)S(1)}, bf16[64,1024]{1,0:T(8,128)(2,1)S(1)}, u32[]{:S(2)}, u32[]{:S(2)}) collective-permute-start(bf16[64,1024]{1,0:T(8,128)(2,1)S(1)} %get-tuple-element.441), channel_id=1, source_target_pairs={{0,2},{1,3},{2,0},{3,1},{4,6},{5,7},{6,4},{7,5},{8,10},{9,11},{10,... | collective-permute-start | bytes 393224 | tf_op jit(solution)/shard_map/ppermute | solution.py:142
  67.6 7.8 %collective-permute-start.18 = (bf16[64,1024]{1,0:T(8,128)(2,1)S(1)}, bf16[64,1024]{1,0:T(8,128)(2,1)S(1)}, u32[]{:S(2)}, u32[]{:S(2)}) collective-permute-start(bf16[64,1024]{1,0:T(8,128)(2,1)S(1)} %add_convert_fusion.5.refs_0_.refs_3_), channel_id=1, source_target_pairs={{0,4},{4,0},{8,12},{12,8},{1,5},{5,1},{9,13},{13,9},{2,6},{6,2},{1... | collective-permute-start | bytes 393224 | tf_op jit(solution)/shard_map/ppermute | solution.py:142
  71.9 4.3 %collective-permute-start.20 = (bf16[64,1024]{1,0:T(8,128)(2,1)S(1)}, bf16[64,1024]{1,0:T(8,128)(2,1)S(1)}, u32[]{:S(2)}, u32[]{:S(2)}) collective-permute-start(bf16[64,1024]{1,0:T(8,128)(2,1)S(1)} %shard_map.52), channel_id=1, source_target_pairs={{0,1},{1,0},{2,3},{3,2},{4,5},{5,4},{6,7},{7,6},{8,9},{9,8},{10,11... | collective-permute-start | bytes 393224 | tf_op jit(solution)/shard_map/ppermute | solution.py:142
  72.0 5.4 %collective-permute-start.22 = (bf16[64,1024]{1,0:T(8,128)(2,1)S(1)}, bf16[64,1024]{1,0:T(8,128)(2,1)S(1)}, u32[]{:S(2)}, u32[]{:S(2)}) collective-permute-start(bf16[64,1024]{1,0:T(8,128)(2,1)S(1)} %subtract_convert_fusion.5.refs_0_), channel_id=1, source_target_pairs={{0,1},{1,0},{2,3},{3,2},{4,5},{5,4},{6,7},{7,6},{8,9},{9,8},{10,11... | collective-permute-start | bytes 393224 | tf_op jit(solution)/shard_map/ppermute | solution.py:142
  73.3 5.1 %collective-permute-start.23 = (bf16[64,1024]{1,0:T(8,128)(2,1)S(1)}, bf16[64,1024]{1,0:T(8,128)(2,1)S(1)}, u32[]{:S(2)}, u32[]{:S(2)}) collective-permute-start(bf16[64,1024]{1,0:T(8,128)(2,1)S(1)} %shard_map.53), channel_id=1, source_target_pairs={{0,4},{1,5},{2,6},{3,7},{5,1},{6,2},{7,3},{10,14},{11,15},{15,11},... | collective-permute-start | bytes 393224 | tf_op jit(solution)/shard_map/ppermute | solution.py:238
  76.2 6.6 %collective-permute-start.21 = (bf16[64,1024]{1,0:T(8,128)(2,1)S(1)}, bf16[64,1024]{1,0:T(8,128)(2,1)S(1)}, u32[]{:S(2)}, u32[]{:S(2)}) collective-permute-start(bf16[64,1024]{1,0:T(8,128)(2,1)S(1)} %get-tuple-element.439), channel_id=1, source_target_pairs={{0,2},{1,3},{2,0},{3,1},{4,6},{5,7},{6,4},{7,5},{8,10},{9,11},{10,... | collective-permute-start | bytes 393224 | tf_op jit(solution)/shard_map/ppermute | solution.py:142
  78.5 9.8 %collective-permute-start.26 = (bf16[64,1024]{1,0:T(8,128)(2,1)S(1)}, bf16[64,1024]{1,0:T(8,128)(2,1)S(1)}, u32[]{:S(2)}, u32[]{:S(2)}) collective-permute-start(bf16[64,1024]{1,0:T(8,128)(2,1)S(1)} %get-tuple-element.437), channel_id=1, source_target_pairs={{0,8},{1,9},{2,10},{3,11},{4,12},{5,13},{6,14},{7,15},{10,2},{11,3... | collective-permute-start | bytes 393224 | tf_op jit(solution)/shard_map/ppermute | solution.py:238
  82.9 4.6 %collective-permute-start.24 = (bf16[64,1024]{1,0:T(8,128)(2,1)S(1)}, bf16[64,1024]{1,0:T(8,128)(2,1)S(1)}, u32[]{:S(2)}, u32[]{:S(2)}) collective-permute-start(bf16[64,1024]{1,0:T(8,128)(2,1)S(1)} %subtract_convert_fusion.4.refs_0_), channel_id=1, source_target_pairs={{0,1},{1,0},{2,3},{3,2},{4,5},{5,4},{6,7},{7,6},{8,9},{9,8},{10,11... | collective-permute-start | bytes 393224 | tf_op jit(solution)/shard_map/ppermute | solution.py:142
  83.9 8.7 %collective-permute-start.25 = (bf16[64,1024]{1,0:T(8,128)(2,1)S(1)}, bf16[64,1024]{1,0:T(8,128)(2,1)S(1)}, u32[]{:S(2)}, u32[]{:S(2)}) collective-permute-start(bf16[64,1024]{1,0:T(8,128)(2,1)S(1)} %shard_map.57), channel_id=1, source_target_pairs={{0,4},{1,5},{2,6},{3,7},{5,1},{6,2},{7,3},{10,14},{11,15},{15,11},... | collective-permute-start | bytes 393224 | tf_op jit(solution)/shard_map/ppermute | solution.py:238
  88.3 7.9 %collective-permute-start.28 = (bf16[64,1024]{1,0:T(8,128)(2,1)S(1)}, bf16[64,1024]{1,0:T(8,128)(2,1)S(1)}, u32[]{:S(2)}, u32[]{:S(2)}) collective-permute-start(bf16[64,1024]{1,0:T(8,128)(2,1)S(1)} %add_convert_fusion.4.refs_0_.refs_1_), channel_id=1, source_target_pairs={{0,4},{4,0},{8,12},{12,8},{1,5},{5,1},{9,13},{13,9},{2,6},{6,2},{1... | collective-permute-start | bytes 393224 | tf_op jit(solution)/shard_map/ppermute | solution.py:142
  92.4 4.6 %collective-permute-start.29 = (bf16[64,1024]{1,0:T(8,128)(2,1)S(1)}, bf16[64,1024]{1,0:T(8,128)(2,1)S(1)}, u32[]{:S(2)}, u32[]{:S(2)}) collective-permute-start(bf16[64,1024]{1,0:T(8,128)(2,1)S(1)} %shard_map.59), channel_id=1, source_target_pairs={{0,1},{1,0},{2,3},{3,2},{4,5},{5,4},{6,7},{7,6},{8,9},{9,8},{10,11... | collective-permute-start | bytes 393224 | tf_op jit(solution)/shard_map/ppermute | solution.py:142
  92.6 9.4 %collective-permute-start.27 = (bf16[64,1024]{1,0:T(8,128)(2,1)S(1)}, bf16[64,1024]{1,0:T(8,128)(2,1)S(1)}, u32[]{:S(2)}, u32[]{:S(2)}) collective-permute-start(bf16[64,1024]{1,0:T(8,128)(2,1)S(1)} %get-tuple-element.435), channel_id=1, source_target_pairs={{0,8},{1,9},{2,10},{3,11},{4,12},{5,13},{6,14},{7,15},{10,2},{11,3... | collective-permute-start | bytes 393224 | tf_op jit(solution)/shard_map/ppermute | solution.py:238
  97.0 9.3 %collective-permute-start.31 = (bf16[64,1024]{1,0:T(8,128)(2,1)S(1)}, bf16[64,1024]{1,0:T(8,128)(2,1)S(1)}, u32[]{:S(2)}, u32[]{:S(2)}) collective-permute-start(bf16[64,1024]{1,0:T(8,128)(2,1)S(1)} %get-tuple-element.433), channel_id=1, source_target_pairs={{0,2},{1,3},{2,0},{3,1},{4,6},{5,7},{6,4},{7,5},{8,10},{9,11},{10,... | collective-permute-start | bytes 393224 | tf_op jit(solution)/shard_map/ppermute | solution.py:142
  102.0 7.6 %collective-permute-start.30 = (bf16[64,1024]{1,0:T(8,128)(2,1)S(1)}, bf16[64,1024]{1,0:T(8,128)(2,1)S(1)}, u32[]{:S(2)}, u32[]{:S(2)}) collective-permute-start(bf16[64,1024]{1,0:T(8,128)(2,1)S(1)} %add_convert_fusion.3.refs_0_.refs_3_), channel_id=1, source_target_pairs={{0,4},{4,0},{8,12},{12,8},{1,5},{5,1},{9,13},{13,9},{2,6},{6,2},{1... | collective-permute-start | bytes 393224 | tf_op jit(solution)/shard_map/ppermute | solution.py:142
  106.2 4.2 %collective-permute-start.32 = (bf16[64,1024]{1,0:T(8,128)(2,1)S(1)}, bf16[64,1024]{1,0:T(8,128)(2,1)S(1)}, u32[]{:S(2)}, u32[]{:S(2)}) collective-permute-start(bf16[64,1024]{1,0:T(8,128)(2,1)S(1)} %shard_map.63), channel_id=1, source_target_pairs={{0,1},{1,0},{2,3},{3,2},{4,5},{5,4},{6,7},{7,6},{8,9},{9,8},{10,11... | collective-permute-start | bytes 393224 | tf_op jit(solution)/shard_map/ppermute | solution.py:142
  106.4 5.2 %collective-permute-start.34 = (bf16[64,1024]{1,0:T(8,128)(2,1)S(1)}, bf16[64,1024]{1,0:T(8,128)(2,1)S(1)}, u32[]{:S(2)}, u32[]{:S(2)}) collective-permute-start(bf16[64,1024]{1,0:T(8,128)(2,1)S(1)} %subtract_convert_fusion.3.refs_0_), channel_id=1, source_target_pairs={{0,1},{1,0},{2,3},{3,2},{4,5},{5,4},{6,7},{7,6},{8,9},{9,8},{10,11... | collective-permute-start | bytes 393224 | tf_op jit(solution)/shard_map/ppermute | solution.py:142
  107.7 5.1 %collective-permute-start.35 = (bf16[64,1024]{1,0:T(8,128)(2,1)S(1)}, bf16[64,1024]{1,0:T(8,128)(2,1)S(1)}, u32[]{:S(2)}, u32[]{:S(2)}) collective-permute-start(bf16[64,1024]{1,0:T(8,128)(2,1)S(1)} %shard_map.64), channel_id=1, source_target_pairs={{0,4},{1,5},{2,6},{3,7},{5,1},{6,2},{7,3},{10,14},{11,15},{15,11},... | collective-permute-start | bytes 393224 | tf_op jit(solution)/shard_map/ppermute | solution.py:238
  110.5 6.8 %collective-permute-start.33 = (bf16[64,1024]{1,0:T(8,128)(2,1)S(1)}, bf16[64,1024]{1,0:T(8,128)(2,1)S(1)}, u32[]{:S(2)}, u32[]{:S(2)}) collective-permute-start(bf16[64,1024]{1,0:T(8,128)(2,1)S(1)} %get-tuple-element.431), channel_id=1, source_target_pairs={{0,2},{1,3},{2,0},{3,1},{4,6},{5,7},{6,4},{7,5},{8,10},{9,11},{10,... | collective-permute-start | bytes 393224 | tf_op jit(solution)/shard_map/ppermute | solution.py:142
  112.9 9.8 %collective-permute-start.38 = (bf16[64,1024]{1,0:T(8,128)(2,1)S(1)}, bf16[64,1024]{1,0:T(8,128)(2,1)S(1)}, u32[]{:S(2)}, u32[]{:S(2)}) collective-permute-start(bf16[64,1024]{1,0:T(8,128)(2,1)S(1)} %get-tuple-element.429), channel_id=1, source_target_pairs={{0,8},{1,9},{2,10},{3,11},{4,12},{5,13},{6,14},{7,15},{10,2},{11,3... | collective-permute-start | bytes 393224 | tf_op jit(solution)/shard_map/ppermute | solution.py:238
  117.3 4.6 %collective-permute-start.36 = (bf16[64,1024]{1,0:T(8,128)(2,1)S(1)}, bf16[64,1024]{1,0:T(8,128)(2,1)S(1)}, u32[]{:S(2)}, u32[]{:S(2)}) collective-permute-start(bf16[64,1024]{1,0:T(8,128)(2,1)S(1)} %subtract_convert_fusion.2.refs_0_), channel_id=1, source_target_pairs={{0,1},{1,0},{2,3},{3,2},{4,5},{5,4},{6,7},{7,6},{8,9},{9,8},{10,11... | collective-permute-start | bytes 393224 | tf_op jit(solution)/shard_map/ppermute | solution.py:142
  118.2 8.6 %collective-permute-start.37 = (bf16[64,1024]{1,0:T(8,128)(2,1)S(1)}, bf16[64,1024]{1,0:T(8,128)(2,1)S(1)}, u32[]{:S(2)}, u32[]{:S(2)}) collective-permute-start(bf16[64,1024]{1,0:T(8,128)(2,1)S(1)} %shard_map.68), channel_id=1, source_target_pairs={{0,4},{1,5},{2,6},{3,7},{5,1},{6,2},{7,3},{10,14},{11,15},{15,11},... | collective-permute-start | bytes 393224 | tf_op jit(solution)/shard_map/ppermute | solution.py:238
  122.7 8.1 %collective-permute-start.40 = (bf16[64,1024]{1,0:T(8,128)(2,1)S(1)}, bf16[64,1024]{1,0:T(8,128)(2,1)S(1)}, u32[]{:S(2)}, u32[]{:S(2)}) collective-permute-start(bf16[64,1024]{1,0:T(8,128)(2,1)S(1)} %add_convert_fusion.2.refs_0_), channel_id=1, source_target_pairs={{0,4},{4,0},{8,12},{12,8},{1,5},{5,1},{9,13},{13,9},{2,6},{6,2},{1... | collective-permute-start | bytes 393224 | tf_op jit(solution)/shard_map/ppermute | solution.py:142
  126.8 4.8 %collective-permute-start.41 = (bf16[64,1024]{1,0:T(8,128)(2,1)S(1)}, bf16[64,1024]{1,0:T(8,128)(2,1)S(1)}, u32[]{:S(2)}, u32[]{:S(2)}) collective-permute-start(bf16[64,1024]{1,0:T(8,128)(2,1)S(1)} %shard_map.70), channel_id=1, source_target_pairs={{0,1},{1,0},{2,3},{3,2},{4,5},{5,4},{6,7},{7,6},{8,9},{9,8},{10,11... | collective-permute-start | bytes 393224 | tf_op jit(solution)/shard_map/ppermute | solution.py:142
  126.9 10.1 %collective-permute-start.39 = (bf16[64,1024]{1,0:T(8,128)(2,1)S(1)}, bf16[64,1024]{1,0:T(8,128)(2,1)S(1)}, u32[]{:S(2)}, u32[]{:S(2)}) collective-permute-start(bf16[64,1024]{1,0:T(8,128)(2,1)S(1)} %get-tuple-element.427), channel_id=1, source_target_pairs={{0,8},{1,9},{2,10},{3,11},{4,12},{5,13},{6,14},{7,15},{10,2},{11,3... | collective-permute-start | bytes 393224 | tf_op jit(solution)/shard_map/ppermute | solution.py:238
  131.7 5.3 %collective-permute-start.42 = (bf16[64,1024]{1,0:T(8,128)(2,1)S(1)}, bf16[64,1024]{1,0:T(8,128)(2,1)S(1)}, u32[]{:S(2)}, u32[]{:S(2)}) collective-permute-start(bf16[64,1024]{1,0:T(8,128)(2,1)S(1)} %get-tuple-element.425), channel_id=1, source_target_pairs={{0,2},{1,3},{2,0},{3,1},{4,6},{5,7},{6,4},{7,5},{8,10},{9,11},{10,... | collective-permute-start | bytes 393224 | tf_op jit(solution)/shard_map/ppermute | solution.py:142
  137.0 6.4 %collective-permute-start.43 = (bf16[64,1024]{1,0:T(8,128)(2,1)S(1)}, bf16[64,1024]{1,0:T(8,128)(2,1)S(1)}, u32[]{:S(2)}, u32[]{:S(2)}) collective-permute-start(bf16[64,1024]{1,0:T(8,128)(2,1)S(1)} %add_convert_fusion.1.refs_0_), channel_id=1, source_target_pairs={{0,4},{4,0},{8,12},{12,8},{1,5},{5,1},{9,13},{13,9},{2,6},{6,2},{1... | collective-permute-start | bytes 393224 | tf_op jit(solution)/shard_map/ppermute | solution.py:142
  140.6 3.6 %collective-permute-start.45 = (bf16[64,1024]{1,0:T(8,128)(2,1)S(1)}, bf16[64,1024]{1,0:T(8,128)(2,1)S(1)}, u32[]{:S(2)}, u32[]{:S(2)}) collective-permute-start(bf16[64,1024]{1,0:T(8,128)(2,1)S(1)} %shard_map.72), channel_id=1, source_target_pairs={{0,1},{1,0},{2,3},{3,2},{4,5},{5,4},{6,7},{7,6},{8,9},{9,8},{10,11... | collective-permute-start | bytes 393224 | tf_op jit(solution)/shard_map/ppermute | solution.py:142
  140.8 3.5 %collective-permute-start.44 = (bf16[64,1024]{1,0:T(8,128)(2,1)S(1)}, bf16[64,1024]{1,0:T(8,128)(2,1)S(1)}, u32[]{:S(2)}, u32[]{:S(2)}) collective-permute-start(bf16[64,1024]{1,0:T(8,128)(2,1)S(1)} %subtract_convert_fusion.1), channel_id=1, source_target_pairs={{0,1},{1,0},{2,3},{3,2},{4,5},{5,4},{6,7},{7,6},{8,9},{9,8},{10,11... | collective-permute-start | bytes 393224 | tf_op jit(solution)/shard_map/ppermute | solution.py:142
  144.2 5.3 %collective-permute-start.47 = (bf16[64,1024]{1,0:T(8,128)(2,1)S(1)}, bf16[64,1024]{1,0:T(8,128)(2,1)S(1)}, u32[]{:S(2)}, u32[]{:S(2)}) collective-permute-start(bf16[64,1024]{1,0:T(8,128)(2,1)S(1)} %get-tuple-element.423), channel_id=1, source_target_pairs={{0,2},{1,3},{2,0},{3,1},{4,6},{5,7},{6,4},{7,5},{8,10},{9,11},{10,... | collective-permute-start | bytes 393224 | tf_op jit(solution)/shard_map/ppermute | solution.py:142
  145.1 6.2 %collective-permute-start.46 = (bf16[64,1024]{1,0:T(8,128)(2,1)S(1)}, bf16[64,1024]{1,0:T(8,128)(2,1)S(1)}, u32[]{:S(2)}, u32[]{:S(2)}) collective-permute-start(bf16[64,1024]{1,0:T(8,128)(2,1)S(1)} %shard_map.74), channel_id=1, source_target_pairs={{0,4},{1,5},{2,6},{3,7},{5,1},{6,2},{7,3},{10,14},{11,15},{15,11},... | collective-permute-start | bytes 393224 | tf_op jit(solution)/shard_map/ppermute | solution.py:238
  149.6 1.7 collective-permute-start.48
  152.1 9.7 %collective-permute-start.49 = (bf16[64,1024]{1,0:T(8,128)(2,1)S(1)}, bf16[64,1024]{1,0:T(8,128)(2,1)S(1)}, u32[]{:S(2)}, u32[]{:S(2)}) collective-permute-start(bf16[64,1024]{1,0:T(8,128)(2,1)S(1)} %shard_map.76), channel_id=1, source_target_pairs={{0,4},{1,5},{2,6},{3,7},{5,1},{6,2},{7,3},{10,14},{11,15},{15,11},... | collective-permute-start | bytes 393224 | tf_op jit(solution)/shard_map/ppermute | solution.py:238
  156.5 6.7 %collective-permute-start.50 = (bf16[64,1024]{1,0:T(8,128)(2,1)S(1)}, bf16[64,1024]{1,0:T(8,128)(2,1)S(1)}, u32[]{:S(2)}, u32[]{:S(2)}) collective-permute-start(bf16[64,1024]{1,0:T(8,128)(2,1)S(1)} %fusion), channel_id=1, source_target_pairs={{4,12},{5,13},{6,14},{7,15},{10,2},{11,3},{20,28},{21,29},{22,30},... | collective-permute-start | bytes 393224 | tf_op jit(solution)/shard_map/ppermute | solution.py:238
  161.8 7.8 %collective-permute-start.51 = (bf16[64,1024]{1,0:T(8,128)(2,1)S(1)}, bf16[64,1024]{1,0:T(8,128)(2,1)S(1)}, u32[]{:S(2)}, u32[]{:S(2)}) collective-permute-start(bf16[64,1024]{1,0:T(8,128)(2,1)S(1)} %fusion.1), channel_id=1, source_target_pairs={{0,8},{1,9},{2,10},{3,11},{14,6},{15,7},{16,24},{17,25},{18,26},{1... | collective-permute-start | bytes 393224 | tf_op jit(solution)/shard_map/ppermute | solution.py:238
  163.2 6.4 %copy-start.2 = (bf16[5,1024,64]{1,2,0:T(8,128)(2,1)}, bf16[5,1024,64]{1,2,0:T(8,128)(2,1)S(1)}, u32[]{:S(2)}) copy-start(bf16[5,1024,64]{1,2,0:T(8,128)(2,1)S(1)} %bitcast_dynamic-update-slice_fusion) | copy-start | bytes 1966084

commit v16 on v13

--- a/solution.py
+++ b/solution.py
@@ -285,6 +285,7 @@
         pair_sum(0)
         cross(0)
         load_factor(1)
+        load_inverse(1)
 
         for step in range(1, steps_total):
             final = exact and step == last_step
@@ -296,7 +297,8 @@
             chip_sum(0)
             older(step + 1, range(step - 1))
             load_factor(step + 1)
-            load_inverse(step)
+            if step > 1:
+                load_inverse(step)
             if final:
                 residual(0, step)
                 solve(1, step - 1)

time: 146 us -> 146 us (level)
  waiting for transfers between devices: 48.5 us -> 56.3 us
  local copies, waits for them, and re-layouts: 17 us -> 12.8 us
  starting transfers between devices: 43.7 us -> 40.3 us
    ppermute x50, waiting for transfers between devices: 46.1 us -> 53.9 us  [trade(): return lax.ppermute(value, axis, [(i, i ^ step) for i in range(size)])]
    squeeze x16, local copies, waits for them, and re-layouts: 14.9 us -> 10.2 us  [block(): self.last = lax.optimization_barrier(self.run(lambda v: v[index], blocks))]
    ppermute x50, starting transfers between devices: 40 us -> 36.4 us  [trade(): return lax.ppermute(value, axis, [(i, i ^ step) for i in range(size)])]
  transfers between devices with their start and end apart: 52 -> 52, of which waited for: 29 -> 29; matrix products, arithmetic and copies ran while one was open for 10% -> 6% of each run, Pallas kernels for 21% -> 21%
where the time goes in v16:
time: 146 us; the launch traced here: 145 us
  waiting for transfers between devices  56.3 us (39%)
  starting transfers between devices  40.3 us (28%)
  Pallas kernels  32.5 us (22%)
  local copies, waits for them, and re-layouts  12.8 us (9%)
  other arithmetic  2.28 us (2%)
    ppermute x50, waiting for transfers between devices, trade(): return lax.ppermute(value, axis, [(i, i ^ step) for i in range(size)])  53.9 us
    ppermute x50, starting transfers between devices, trade(): return lax.ppermute(value, axis, [(i, i ^ step) for i in range(size)])  36.4 us
    pallas_call x38, Pallas kernels, product(): pl.pallas_call(functools.partial(product_kernel, len(units)), out_shape=j...  29.9 us
    squeeze x16, local copies, waits for them, and re-layouts, block(): self.last = lax.optimization_barrier(self.run(lambda v: v[index], blocks))  10.2 us
    ppermute x2, starting transfers between devices, final_cross(): st['flight'] = lax.ppermute(st['leaving'], 'row', pairs)  3.97 us
  transfers between devices with their start and end apart: 52, of which 29 were waited for; matrix products, arithmetic and copies ran while one was open for 6% of the time, Pallas kernels for 21%

profile of v16, /device:TPU:0, one launch (start us, length us, event | category | flops | bytes accessed | tf_op | source)
XLA Modules:
  0.0 145.2 jit_solution(16741846966229102249)
XLA Ops:
  0.0 1.8 %slice_bitcast_fusion.14.block = bf16[1024,1024]{1,0:T(8,128)(2,1)S(1)} fusion(bf16[5,1024,1024]{2,1,0:T(8,128)(2,1)} %param.4), kind=kLoop, calls=%fused_computation.14 | loop fusion | bytes 4194304 | tf_op jit(solution)/shard_map/squeeze | solution.py:135
  1.8 1.1 slice_bitcast_fusion.15.right
  2.9 0.8 shard_map.37
  3.7 3.1 %collective-permute-start.1 = (bf16[64,1024]{1,0:T(8,128)(2,1)S(1)}, bf16[64,1024]{1,0:T(8,128)(2,1)S(1)}, u32[]{:S(2)}, u32[]{:S(2)}) collective-permute-start(bf16[64,1024]{1,0:T(8,128)(2,1)S(1)} %get-tuple-element.222), channel_id=1, source_target_pairs={{0,4},{4,0},{8,12},{12,8},{1,5},{5,1},{9,13},{13,9},{2,6},{6,2},{1... | collective-permute-start | bytes 393224 | tf_op jit(solution)/shard_map/ppermute | solution.py:142
  6.8 0.8 shard_map.38
  7.8 1.7 %copy-done = bf16[5,1024,256]{2,1,0:T(8,128)(2,1)S(1)} copy-done((bf16[5,1024,256]{2,1,0:T(8,128)(2,1)S(1)}, bf16[5,1024,256]{2,1,0:T(8,128)(2,1)}, u32[]{:S(2)}) %copy-start) | copy-done | bytes 2621464
  9.5 0.9 shard_map.39
  10.7 3.0 %collective-permute-start.2 = (bf16[64,1024]{1,0:T(8,128)(2,1)S(1)}, bf16[64,1024]{1,0:T(8,128)(2,1)S(1)}, u32[]{:S(2)}, u32[]{:S(2)}) collective-permute-start(bf16[64,1024]{1,0:T(8,128)(2,1)S(1)} %get-tuple-element.453), channel_id=1, source_target_pairs={{0,8},{4,12},{8,0},{12,4},{1,9},{5,13},{9,1},{13,5},{2,10},{6,14},... | collective-permute-start | bytes 393224 | tf_op jit(solution)/shard_map/ppermute | solution.py:142
  13.7 1.8 %slice_bitcast_fusion.13.block = bf16[1024,1024]{1,0:T(8,128)(2,1)S(1)} fusion(bf16[10,1024,1024]{2,1,0:T(8,128)(2,1)} %param.3), kind=kLoop, calls=%fused_computation.13 | loop fusion | bytes 4194304 | tf_op jit(solution)/shard_map/squeeze | solution.py:135
  15.5 1.9 %slice_bitcast_fusion.12.block = bf16[1024,1024]{1,0:T(8,128)(2,1)S(1)} fusion(bf16[5,1024,1024]{2,1,0:T(8,128)(2,1)} %param.4), kind=kLoop, calls=%fused_computation.12 | loop fusion | bytes 4194304 | tf_op jit(solution)/shard_map/squeeze | solution.py:135
  17.4 2.0 %collective-permute-done.2 = bf16[64,1024]{1,0:T(8,128)(2,1)S(1)} collective-permute-done((bf16[64,1024]{1,0:T(8,128)(2,1)S(1)}, bf16[64,1024]{1,0:T(8,128)(2,1)S(1)}, u32[]{:S(2)}, u32[]{:S(2)}) %collective-permute-start.2) | collective-permute-done | bytes 131104 | tf_op jit(solution)/shard_map/ppermute | solution.py:142
  19.4 0.8 collective-permute-start.4
  21.1 3.4 %collective-permute-start.3 = (bf16[64,1024]{1,0:T(8,128)(2,1)S(1)}, bf16[64,1024]{1,0:T(8,128)(2,1)S(1)}, u32[]{:S(2)}, u32[]{:S(2)}) collective-permute-start(bf16[64,1024]{1,0:T(8,128)(2,1)S(1)} %get-tuple-element.451), channel_id=1, source_target_pairs={{0,8},{4,12},{8,0},{12,4},{1,9},{5,13},{9,1},{13,5},{2,10},{6,14},... | collective-permute-start | bytes 393224 | tf_op jit(solution)/shard_map/ppermute | solution.py:142
  25.3 1.6 %collective-permute-start.7 = (bf16[64,1024]{1,0:T(8,128)(2,1)S(1)}, bf16[64,1024]{1,0:T(8,128)(2,1)S(1)}, u32[]{:S(2)}, u32[]{:S(2)}) collective-permute-start(bf16[64,1024]{1,0:T(8,128)(2,1)S(1)} %get-tuple-element.449), channel_id=1, source_target_pairs={{0,2},{1,3},{2,0},{3,1},{4,6},{5,7},{6,4},{7,5},{8,10},{9,11},{10,... | collective-permute-start | bytes 393224 | tf_op jit(solution)/shard_map/ppermute | solution.py:142
  26.9 1.8 %slice_bitcast_fusion.11.block = bf16[1024,1024]{1,0:T(8,128)(2,1)S(1)} fusion(bf16[10,1024,1024]{2,1,0:T(8,128)(2,1)} %param.3), kind=kLoop, calls=%fused_computation.11 | loop fusion | bytes 4194304 | tf_op jit(solution)/shard_map/squeeze | solution.py:135
  28.7 2.8 %collective-permute-done.3 = bf16[64,1024]{1,0:T(8,128)(2,1)S(1)} collective-permute-done((bf16[64,1024]{1,0:T(8,128)(2,1)S(1)}, bf16[64,1024]{1,0:T(8,128)(2,1)S(1)}, u32[]{:S(2)}, u32[]{:S(2)}) %collective-permute-start.3) | collective-permute-done | bytes 131104 | tf_op jit(solution)/shard_map/ppermute | solution.py:142
  33.8 2.1 %collective-permute-start.11 = (bf16[64,1024]{1,0:T(8,128)(2,1)S(1)}, bf16[64,1024]{1,0:T(8,128)(2,1)S(1)}, u32[]{:S(2)}, u32[]{:S(2)}) collective-permute-start(bf16[64,1024]{1,0:T(8,128)(2,1)S(1)} %shard_map.43), channel_id=1, source_target_pairs={{0,4},{4,0},{8,12},{12,8},{1,5},{5,1},{9,13},{13,9},{2,6},{6,2},{1... | collective-permute-start | bytes 393224 | tf_op jit(solution)/shard_map/ppermute | solution.py:142
  35.8 1.3 collective-permute-done.6.refs_0_.refs_2_
  37.9 1.5 %collective-permute-start.9 = (bf16[64,1024]{1,0:T(8,128)(2,1)S(1)}, bf16[64,1024]{1,0:T(8,128)(2,1)S(1)}, u32[]{:S(2)}, u32[]{:S(2)}) collective-permute-start(bf16[64,1024]{1,0:T(8,128)(2,1)S(1)} %get-tuple-element.447), channel_id=1, source_target_pairs={{0,2},{1,3},{2,0},{3,1},{4,6},{5,7},{6,4},{7,5},{8,10},{9,11},{10,... | collective-permute-start | bytes 393224 | tf_op jit(solution)/shard_map/ppermute | solution.py:142
  39.6 0.9 shard_map.45
  42.2 0.8 collective-permute-done.9
  43.9 0.9 collective-permute-start.13
  45.6 3.8 %collective-permute-done.14 = bf16[64,1024]{1,0:T(8,128)(2,1)S(1)} collective-permute-done((bf16[64,1024]{1,0:T(8,128)(2,1)S(1)}, bf16[64,1024]{1,0:T(8,128)(2,1)S(1)}, u32[]{:S(2)}, u32[]{:S(2)}) %collective-permute-start.14) | collective-permute-done | bytes 131104 | tf_op jit(solution)/shard_map/ppermute | solution.py:142
  50.3 1.8 %collective-permute-done.13 = bf16[64,1024]{1,0:T(8,128)(2,1)S(1)} collective-permute-done((bf16[64,1024]{1,0:T(8,128)(2,1)S(1)}, bf16[64,1024]{1,0:T(8,128)(2,1)S(1)}, u32[]{:S(2)}, u32[]{:S(2)}) %collective-permute-start.13) | collective-permute-done | bytes 131104 | tf_op jit(solution)/shard_map/ppermute | solution.py:142
  52.1 0.8 collective-permute-start.15
  52.9 1.9 %collective-permute-done.16.refs_0_ = bf16[64,1024]{1,0:T(8,128)(2,1)S(1)} collective-permute-done((bf16[64,1024]{1,0:T(8,128)(2,1)S(1)}, bf16[64,1024]{1,0:T(8,128)(2,1)S(1)}, u32[]{:S(2)}, u32[]{:S(2)}) %collective-permute-start.16) | collective-permute-done | bytes 131104 | tf_op jit(solution)/shard_map/ppermute | solution.py:142
  55.7 0.9 collective-permute-start.19
  56.8 0.9 shard_map.51.refs_4_
  58.6 2.7 %collective-permute-done.15 = bf16[64,1024]{1,0:T(8,128)(2,1)S(1)} collective-permute-done((bf16[64,1024]{1,0:T(8,128)(2,1)S(1)}, bf16[64,1024]{1,0:T(8,128)(2,1)S(1)}, u32[]{:S(2)}, u32[]{:S(2)}) %collective-permute-start.15) | collective-permute-done | bytes 131104 | tf_op jit(solution)/shard_map/ppermute | solution.py:142
  63.7 2.1 %collective-permute-start.23 = (bf16[64,1024]{1,0:T(8,128)(2,1)S(1)}, bf16[64,1024]{1,0:T(8,128)(2,1)S(1)}, u32[]{:S(2)}, u32[]{:S(2)}) collective-permute-start(bf16[64,1024]{1,0:T(8,128)(2,1)S(1)} %shard_map.53), channel_id=1, source_target_pairs={{0,4},{4,0},{8,12},{12,8},{1,5},{5,1},{9,13},{13,9},{2,6},{6,2},{1... | collective-permute-start | bytes 393224 | tf_op jit(solution)/shard_map/ppermute | solution.py:142
  65.7 1.0 collective-permute-done.18.refs_0_.refs_2_
  67.6 1.0 collective-permute-start.21
  68.7 0.9 shard_map.55
  69.6 1.0 shard_map.56
  70.7 1.1 collective-permute-start.26
  71.7 0.9 collective-permute-done.21
  73.6 0.9 collective-permute-start.25
  75.3 3.3 %collective-permute-done.26 = bf16[64,1024]{1,0:T(8,128)(2,1)S(1)} collective-permute-done((bf16[64,1024]{1,0:T(8,128)(2,1)S(1)}, bf16[64,1024]{1,0:T(8,128)(2,1)S(1)}, u32[]{:S(2)}, u32[]{:S(2)}) %collective-permute-start.26) | collective-permute-done | bytes 131104 | tf_op jit(solution)/shard_map/ppermute | solution.py:142
  79.6 1.8 %collective-permute-done.25 = bf16[64,1024]{1,0:T(8,128)(2,1)S(1)} collective-permute-done((bf16[64,1024]{1,0:T(8,128)(2,1)S(1)}, bf16[64,1024]{1,0:T(8,128)(2,1)S(1)}, u32[]{:S(2)}, u32[]{:S(2)}) %collective-permute-start.25) | collective-permute-done | bytes 131104 | tf_op jit(solution)/shard_map/ppermute | solution.py:142
  81.4 0.9 collective-permute-start.27
  82.3 1.8 %collective-permute-done.28.refs_0_ = bf16[64,1024]{1,0:T(8,128)(2,1)S(1)} collective-permute-done((bf16[64,1024]{1,0:T(8,128)(2,1)S(1)}, bf16[64,1024]{1,0:T(8,128)(2,1)S(1)}, u32[]{:S(2)}, u32[]{:S(2)}) %collective-permute-start.28) | collective-permute-done | bytes 131104 | tf_op jit(solution)/shard_map/ppermute | solution.py:142
  84.9 1.2 collective-permute-start.31
  86.3 0.9 shard_map.61.refs_4_
  87.4 0.9 shard_map.62.refs_4_
  88.7 1.9 %collective-permute-done.27 = bf16[64,1024]{1,0:T(8,128)(2,1)S(1)} collective-permute-done((bf16[64,1024]{1,0:T(8,128)(2,1)S(1)}, bf16[64,1024]{1,0:T(8,128)(2,1)S(1)}, u32[]{:S(2)}, u32[]{:S(2)}) %collective-permute-start.27) | collective-permute-done | bytes 131104 | tf_op jit(solution)/shard_map/ppermute | solution.py:142
  92.9 2.1 %collective-permute-start.35 = (bf16[64,1024]{1,0:T(8,128)(2,1)S(1)}, bf16[64,1024]{1,0:T(8,128)(2,1)S(1)}, u32[]{:S(2)}, u32[]{:S(2)}) collective-permute-start(bf16[64,1024]{1,0:T(8,128)(2,1)S(1)} %shard_map.64), channel_id=1, source_target_pairs={{0,4},{4,0},{8,12},{12,8},{1,5},{5,1},{9,13},{13,9},{2,6},{6,2},{1... | collective-permute-start | bytes 393224 | tf_op jit(solution)/shard_map/ppermute | solution.py:142
  95.0 1.0 collective-permute-done.30.refs_0_.refs_2_
  96.8 1.2 collective-permute-start.33
  98.2 0.9 shard_map.66
  100.2 1.7 %collective-permute-done.33 = bf16[64,1024]{1,0:T(8,128)(2,1)S(1)} collective-permute-done((bf16[64,1024]{1,0:T(8,128)(2,1)S(1)}, bf16[64,1024]{1,0:T(8,128)(2,1)S(1)}, u32[]{:S(2)}, u32[]{:S(2)}) %collective-permute-start.33) | collective-permute-done | bytes 131104 | tf_op jit(solution)/shard_map/ppermute | solution.py:142
  104.1 3.8 %collective-permute-done.38 = bf16[64,1024]{1,0:T(8,128)(2,1)S(1)} collective-permute-done((bf16[64,1024]{1,0:T(8,128)(2,1)S(1)}, bf16[64,1024]{1,0:T(8,128)(2,1)S(1)}, u32[]{:S(2)}, u32[]{:S(2)}) %collective-permute-start.38) | collective-permute-done | bytes 131104 | tf_op jit(solution)/shard_map/ppermute | solution.py:142
  108.9 1.8 %collective-permute-done.37 = bf16[64,1024]{1,0:T(8,128)(2,1)S(1)} collective-permute-done((bf16[64,1024]{1,0:T(8,128)(2,1)S(1)}, bf16[64,1024]{1,0:T(8,128)(2,1)S(1)}, u32[]{:S(2)}, u32[]{:S(2)}) %collective-permute-start.37) | collective-permute-done | bytes 131104 | tf_op jit(solution)/shard_map/ppermute | solution.py:142
  110.9 2.5 %collective-permute-done.40.refs_0_ = bf16[64,1024]{1,0:T(8,128)(2,1)S(1)} collective-permute-done((bf16[64,1024]{1,0:T(8,128)(2,1)S(1)}, bf16[64,1024]{1,0:T(8,128)(2,1)S(1)}, u32[]{:S(2)}, u32[]{:S(2)}) %collective-permute-start.40) | collective-permute-done | bytes 131104 | tf_op jit(solution)/shard_map/ppermute | solution.py:142
  114.2 1.0 collective-permute-start.42
  115.4 3.9 %collective-permute-done.42 = bf16[64,1024]{1,0:T(8,128)(2,1)S(1)} collective-permute-done((bf16[64,1024]{1,0:T(8,128)(2,1)S(1)}, bf16[64,1024]{1,0:T(8,128)(2,1)S(1)}, u32[]{:S(2)}, u32[]{:S(2)}) %collective-permute-start.42) | collective-permute-done | bytes 131104 | tf_op jit(solution)/shard_map/ppermute | solution.py:142
  121.5 3.8 %collective-permute-done.43.refs_0_ = bf16[64,1024]{1,0:T(8,128)(2,1)S(1)} collective-permute-done((bf16[64,1024]{1,0:T(8,128)(2,1)S(1)}, bf16[64,1024]{1,0:T(8,128)(2,1)S(1)}, u32[]{:S(2)}, u32[]{:S(2)}) %collective-permute-start.43) | collective-permute-done | bytes 131104 | tf_op jit(solution)/shard_map/ppermute | solution.py:142
  125.3 1.0 shard_map.73
  126.3 1.0 collective-permute-start.47
  129.2 2.2 %collective-permute-done.47 = bf16[64,1024]{1,0:T(8,128)(2,1)S(1)} collective-permute-done((bf16[64,1024]{1,0:T(8,128)(2,1)S(1)}, bf16[64,1024]{1,0:T(8,128)(2,1)S(1)}, u32[]{:S(2)}, u32[]{:S(2)}) %collective-permute-start.47) | collective-permute-done | bytes 131104 | tf_op jit(solution)/shard_map/ppermute | solution.py:142
  131.5 1.6 %collective-permute-done.46 = bf16[64,1024]{1,0:T(8,128)(2,1)S(1)} collective-permute-done((bf16[64,1024]{1,0:T(8,128)(2,1)S(1)}, bf16[64,1024]{1,0:T(8,128)(2,1)S(1)}, u32[]{:S(2)}, u32[]{:S(2)}) %collective-permute-start.46) | collective-permute-done | bytes 131104 | tf_op jit(solution)/shard_map/ppermute | solution.py:142
  134.4 1.3 collective-permute-start.50
  136.4 2.8 %collective-permute-done.49 = bf16[64,1024]{1,0:T(8,128)(2,1)S(1)} collective-permute-done((bf16[64,1024]{1,0:T(8,128)(2,1)S(1)}, bf16[64,1024]{1,0:T(8,128)(2,1)S(1)}, u32[]{:S(2)}, u32[]{:S(2)}) %collective-permute-start.49) | collective-permute-done | bytes 131104 | tf_op jit(solution)/shard_map/ppermute | solution.py:142
  139.3 2.7 %collective-permute-start.51 = (bf16[64,1024]{1,0:T(8,128)(2,1)S(1)}, bf16[64,1024]{1,0:T(8,128)(2,1)S(1)}, u32[]{:S(2)}, u32[]{:S(2)}) collective-permute-start(bf16[64,1024]{1,0:T(8,128)(2,1)S(1)} %fusion.1), channel_id=1, source_target_pairs={{12,4},{0,8},{13,5},{1,9},{14,6},{2,10},{15,7},{3,11},{28,20},{16,... | collective-permute-start | bytes 393224 | tf_op jit(solution)/shard_map/ppermute | solution.py:260
  142.1 2.3 %collective-permute-done.51 = bf16[64,1024]{1,0:T(8,128)(2,1)S(1)} collective-permute-done((bf16[64,1024]{1,0:T(8,128)(2,1)S(1)}, bf16[64,1024]{1,0:T(8,128)(2,1)S(1)}, u32[]{:S(2)}, u32[]{:S(2)}) %collective-permute-start.51) | collective-permute-done | bytes 131104 | tf_op jit(solution)/shard_map/ppermute | solution.py:260
  (155 shorter events, 34.6 us)
Async XLA Ops:
  3.7 7.0 %collective-permute-start.1 = (bf16[64,1024]{1,0:T(8,128)(2,1)S(1)}, bf16[64,1024]{1,0:T(8,128)(2,1)S(1)}, u32[]{:S(2)}, u32[]{:S(2)}) collective-permute-start(bf16[64,1024]{1,0:T(8,128)(2,1)S(1)} %get-tuple-element.222), channel_id=1, source_target_pairs={{0,4},{4,0},{8,12},{12,8},{1,5},{5,1},{9,13},{13,9},{2,6},{6,2},{1... | collective-permute-start | bytes 393224 | tf_op jit(solution)/shard_map/ppermute | solution.py:142
  7.6 13.4 %collective-permute-start = (bf16[64,1024]{1,0:T(8,128)(2,1)S(1)}, bf16[64,1024]{1,0:T(8,128)(2,1)S(1)}, u32[]{:S(2)}, u32[]{:S(2)}) collective-permute-start(bf16[64,1024]{1,0:T(8,128)(2,1)S(1)} %get-tuple-element.221), channel_id=1, source_target_pairs={{0,4},{4,0},{8,12},{12,8},{1,5},{5,1},{9,13},{13,9},{2,6},{6,2},{1... | collective-permute-start | bytes 393224 | tf_op jit(solution)/shard_map/ppermute | solution.py:142
  7.7 1.7 %copy-start = (bf16[5,1024,256]{2,1,0:T(8,128)(2,1)S(1)}, bf16[5,1024,256]{2,1,0:T(8,128)(2,1)}, u32[]{:S(2)}) copy-start(bf16[5,1024,256]{2,1,0:T(8,128)(2,1)} %sides) | copy-start | bytes 7864324
  10.7 8.7 %collective-permute-start.2 = (bf16[64,1024]{1,0:T(8,128)(2,1)S(1)}, bf16[64,1024]{1,0:T(8,128)(2,1)S(1)}, u32[]{:S(2)}, u32[]{:S(2)}) collective-permute-start(bf16[64,1024]{1,0:T(8,128)(2,1)S(1)} %get-tuple-element.453), channel_id=1, source_target_pairs={{0,8},{4,12},{8,0},{12,4},{1,9},{5,13},{9,1},{13,5},{2,10},{6,14},... | collective-permute-start | bytes 393224 | tf_op jit(solution)/shard_map/ppermute | solution.py:142
  15.5 23.9 %copy-start.1 = (bf16[10,1024,1024]{2,1,0:T(8,128)(2,1)S(1)}, bf16[10,1024,1024]{2,1,0:T(8,128)(2,1)}, u32[]{:S(2)}) copy-start(bf16[10,1024,1024]{2,1,0:T(8,128)(2,1)} %param.3) | copy-start | bytes 62914564
  19.4 5.1 %collective-permute-start.4 = (bf16[64,1024]{1,0:T(8,128)(2,1)S(1)}, bf16[64,1024]{1,0:T(8,128)(2,1)S(1)}, u32[]{:S(2)}, u32[]{:S(2)}) collective-permute-start(bf16[64,1024]{1,0:T(8,128)(2,1)S(1)} %add_convert_fusion.8.refs_0_.refs_1_), channel_id=1, source_target_pairs={{0,4},{4,0},{8,12},{12,8},{1,5},{5,1},{9,13},{13,9},{2,6},{6,2},{1... | collective-permute-start | bytes 393224 | tf_op jit(solution)/shard_map/ppermute | solution.py:142
  20.9 4.3 %collective-permute-start.5 = (bf16[64,1024]{1,0:T(8,128)(2,1)S(1)}, bf16[64,1024]{1,0:T(8,128)(2,1)S(1)}, u32[]{:S(2)}, u32[]{:S(2)}) collective-permute-start(bf16[64,1024]{1,0:T(8,128)(2,1)S(1)} %shard_map.40), channel_id=1, source_target_pairs={{0,1},{1,0},{2,3},{3,2},{4,5},{5,4},{6,7},{7,6},{8,9},{9,8},{10,11... | collective-permute-start | bytes 393224 | tf_op jit(solution)/shard_map/ppermute | solution.py:142
  21.1 10.4 %collective-permute-start.3 = (bf16[64,1024]{1,0:T(8,128)(2,1)S(1)}, bf16[64,1024]{1,0:T(8,128)(2,1)S(1)}, u32[]{:S(2)}, u32[]{:S(2)}) collective-permute-start(bf16[64,1024]{1,0:T(8,128)(2,1)S(1)} %get-tuple-element.451), channel_id=1, source_target_pairs={{0,8},{4,12},{8,0},{12,4},{1,9},{5,13},{9,1},{13,5},{2,10},{6,14},... | collective-permute-start | bytes 393224 | tf_op jit(solution)/shard_map/ppermute | solution.py:142
  25.3 7.1 %collective-permute-start.7 = (bf16[64,1024]{1,0:T(8,128)(2,1)S(1)}, bf16[64,1024]{1,0:T(8,128)(2,1)S(1)}, u32[]{:S(2)}, u32[]{:S(2)}) collective-permute-start(bf16[64,1024]{1,0:T(8,128)(2,1)S(1)} %get-tuple-element.449), channel_id=1, source_target_pairs={{0,2},{1,3},{2,0},{3,1},{4,6},{5,7},{6,4},{7,5},{8,10},{9,11},{10,... | collective-permute-start | bytes 393224 | tf_op jit(solution)/shard_map/ppermute | solution.py:142
  31.5 5.6 %collective-permute-start.6 = (bf16[64,1024]{1,0:T(8,128)(2,1)S(1)}, bf16[64,1024]{1,0:T(8,128)(2,1)S(1)}, u32[]{:S(2)}, u32[]{:S(2)}) collective-permute-start(bf16[64,1024]{1,0:T(8,128)(2,1)S(1)} %add_convert_fusion.7.refs_0_.refs_3_), channel_id=1, source_target_pairs={{0,4},{4,0},{8,12},{12,8},{1,5},{5,1},{9,13},{13,9},{2,6},{6,2},{1... | collective-permute-start | bytes 393224 | tf_op jit(solution)/shard_map/ppermute | solution.py:142
  32.3 5.6 %collective-permute-start.8 = (bf16[64,1024]{1,0:T(8,128)(2,1)S(1)}, bf16[64,1024]{1,0:T(8,128)(2,1)S(1)}, u32[]{:S(2)}, u32[]{:S(2)}) collective-permute-start(bf16[64,1024]{1,0:T(8,128)(2,1)S(1)} %shard_map.42), channel_id=1, source_target_pairs={{0,1},{1,0},{2,3},{3,2},{4,5},{5,4},{6,7},{7,6},{8,9},{9,8},{10,11... | collective-permute-start | bytes 393224 | tf_op jit(solution)/shard_map/ppermute | solution.py:142
  32.5 8.1 %collective-permute-start.10 = (bf16[64,1024]{1,0:T(8,128)(2,1)S(1)}, bf16[64,1024]{1,0:T(8,128)(2,1)S(1)}, u32[]{:S(2)}, u32[]{:S(2)}) collective-permute-start(bf16[64,1024]{1,0:T(8,128)(2,1)S(1)} %subtract_convert_fusion.7.refs_0_), channel_id=1, source_target_pairs={{0,1},{1,0},{2,3},{3,2},{4,5},{5,4},{6,7},{7,6},{8,9},{9,8},{10,11... | collective-permute-start | bytes 393224 | tf_op jit(solution)/shard_map/ppermute | solution.py:142
  33.8 7.6 %collective-permute-start.11 = (bf16[64,1024]{1,0:T(8,128)(2,1)S(1)}, bf16[64,1024]{1,0:T(8,128)(2,1)S(1)}, u32[]{:S(2)}, u32[]{:S(2)}) collective-permute-start(bf16[64,1024]{1,0:T(8,128)(2,1)S(1)} %shard_map.43), channel_id=1, source_target_pairs={{0,4},{4,0},{8,12},{12,8},{1,5},{5,1},{9,13},{13,9},{2,6},{6,2},{1... | collective-permute-start | bytes 393224 | tf_op jit(solution)/shard_map/ppermute | solution.py:142
  37.9 5.0 %collective-permute-start.9 = (bf16[64,1024]{1,0:T(8,128)(2,1)S(1)}, bf16[64,1024]{1,0:T(8,128)(2,1)S(1)}, u32[]{:S(2)}, u32[]{:S(2)}) collective-permute-start(bf16[64,1024]{1,0:T(8,128)(2,1)S(1)} %get-tuple-element.447), channel_id=1, source_target_pairs={{0,2},{1,3},{2,0},{3,1},{4,6},{5,7},{6,4},{7,5},{8,10},{9,11},{10,... | collective-permute-start | bytes 393224 | tf_op jit(solution)/shard_map/ppermute | solution.py:142
  41.4 8.0 %collective-permute-start.14 = (bf16[64,1024]{1,0:T(8,128)(2,1)S(1)}, bf16[64,1024]{1,0:T(8,128)(2,1)S(1)}, u32[]{:S(2)}, u32[]{:S(2)}) collective-permute-start(bf16[64,1024]{1,0:T(8,128)(2,1)S(1)} %get-tuple-element.445), channel_id=1, source_target_pairs={{0,8},{4,12},{8,0},{12,4},{1,9},{5,13},{9,1},{13,5},{2,10},{6,14},... | collective-permute-start | bytes 393224 | tf_op jit(solution)/shard_map/ppermute | solution.py:142
  43.0 1.8 %collective-permute-start.12 = (bf16[64,1024]{1,0:T(8,128)(2,1)S(1)}, bf16[64,1024]{1,0:T(8,128)(2,1)S(1)}, u32[]{:S(2)}, u32[]{:S(2)}) collective-permute-start(bf16[64,1024]{1,0:T(8,128)(2,1)S(1)} %subtract_convert_fusion.6.refs_0_), channel_id=1, source_target_pairs={{0,1},{1,0},{2,3},{3,2},{4,5},{5,4},{6,7},{7,6},{8,9},{9,8},{10,11... | collective-permute-start | bytes 393224 | tf_op jit(solution)/shard_map/ppermute | solution.py:142
  43.9 8.2 %collective-permute-start.13 = (bf16[64,1024]{1,0:T(8,128)(2,1)S(1)}, bf16[64,1024]{1,0:T(8,128)(2,1)S(1)}, u32[]{:S(2)}, u32[]{:S(2)}) collective-permute-start(bf16[64,1024]{1,0:T(8,128)(2,1)S(1)} %shard_map.47), channel_id=1, source_target_pairs={{0,4},{4,0},{8,12},{12,8},{1,5},{5,1},{9,13},{13,9},{2,6},{6,2},{1... | collective-permute-start | bytes 393224 | tf_op jit(solution)/shard_map/ppermute | solution.py:142
  44.8 13.1 %slice-start = ((s8[10485760]{0:T(1024)(128)(4,1)}), s8[4194304]{0:T(1024)(128)(4,1)S(1)}, s32[]{:S(2)}) async-start(s8[10485760]{0:T(1024)(128)(4,1)} %bitcast.71), calls=%async_computation | async-start | bytes 8388608
  49.4 5.5 %collective-permute-start.16 = (bf16[64,1024]{1,0:T(8,128)(2,1)S(1)}, bf16[64,1024]{1,0:T(8,128)(2,1)S(1)}, u32[]{:S(2)}, u32[]{:S(2)}) collective-permute-start(bf16[64,1024]{1,0:T(8,128)(2,1)S(1)} %add_convert_fusion.6.refs_0_.refs_1_), channel_id=1, source_target_pairs={{0,4},{4,0},{8,12},{12,8},{1,5},{5,1},{9,13},{13,9},{2,6},{6,2},{1... | collective-permute-start | bytes 393224 | tf_op jit(solution)/shard_map/ppermute | solution.py:142
  50.2 5.4 %collective-permute-start.17 = (bf16[64,1024]{1,0:T(8,128)(2,1)S(1)}, bf16[64,1024]{1,0:T(8,128)(2,1)S(1)}, u32[]{:S(2)}, u32[]{:S(2)}) collective-permute-start(bf16[64,1024]{1,0:T(8,128)(2,1)S(1)} %shard_map.49), channel_id=1, source_target_pairs={{0,1},{1,0},{2,3},{3,2},{4,5},{5,4},{6,7},{7,6},{8,9},{9,8},{10,11... | collective-permute-start | bytes 393224 | tf_op jit(solution)/shard_map/ppermute | solution.py:142
  52.1 9.2 %collective-permute-start.15 = (bf16[64,1024]{1,0:T(8,128)(2,1)S(1)}, bf16[64,1024]{1,0:T(8,128)(2,1)S(1)}, u32[]{:S(2)}, u32[]{:S(2)}) collective-permute-start(bf16[64,1024]{1,0:T(8,128)(2,1)S(1)} %get-tuple-element.443), channel_id=1, source_target_pairs={{0,8},{4,12},{8,0},{12,4},{1,9},{5,13},{9,1},{13,5},{2,10},{6,14},... | collective-permute-start | bytes 393224 | tf_op jit(solution)/shard_map/ppermute | solution.py:142
  54.9 3.0 %slice-start.1 = ((s8[10485760]{0:T(1024)(128)(4,1)}), s8[4194304]{0:T(1024)(128)(4,1)S(1)}, s32[]{:S(2)}) async-start(s8[10485760]{0:T(1024)(128)(4,1)} %bitcast.71), calls=%async_computation.1 | async-start | bytes 8388608
  55.7 6.6 %collective-permute-start.19 = (bf16[64,1024]{1,0:T(8,128)(2,1)S(1)}, bf16[64,1024]{1,0:T(8,128)(2,1)S(1)}, u32[]{:S(2)}, u32[]{:S(2)}) collective-permute-start(bf16[64,1024]{1,0:T(8,128)(2,1)S(1)} %get-tuple-element.441), channel_id=1, source_target_pairs={{0,2},{1,3},{2,0},{3,1},{4,6},{5,7},{6,4},{7,5},{8,10},{9,11},{10,... | collective-permute-start | bytes 393224 | tf_op jit(solution)/shard_map/ppermute | solution.py:142
  56.8 1.7 %slice-start.2 = ((s8[10485760]{0:T(1024)(128)(4,1)}), s8[2097152]{0:T(1024)(128)(4,1)S(1)}, s32[]{:S(2)}) async-start(s8[10485760]{0:T(1024)(128)(4,1)} %bitcast.71), calls=%async_computation.2 | async-start | bytes 4194304
  61.4 5.4 %collective-permute-start.18 = (bf16[64,1024]{1,0:T(8,128)(2,1)S(1)}, bf16[64,1024]{1,0:T(8,128)(2,1)S(1)}, u32[]{:S(2)}, u32[]{:S(2)}) collective-permute-start(bf16[64,1024]{1,0:T(8,128)(2,1)S(1)} %add_convert_fusion.5.refs_0_.refs_3_), channel_id=1, source_target_pairs={{0,4},{4,0},{8,12},{12,8},{1,5},{5,1},{9,13},{13,9},{2,6},{6,2},{1... | collective-permute-start | bytes 393224 | tf_op jit(solution)/shard_map/ppermute | solution.py:142
  62.2 5.3 %collective-permute-start.20 = (bf16[64,1024]{1,0:T(8,128)(2,1)S(1)}, bf16[64,1024]{1,0:T(8,128)(2,1)S(1)}, u32[]{:S(2)}, u32[]{:S(2)}) collective-permute-start(bf16[64,1024]{1,0:T(8,128)(2,1)S(1)} %shard_map.52), channel_id=1, source_target_pairs={{0,1},{1,0},{2,3},{3,2},{4,5},{5,4},{6,7},{7,6},{8,9},{9,8},{10,11... | collective-permute-start | bytes 393224 | tf_op jit(solution)/shard_map/ppermute | solution.py:142
  62.4 7.2 %collective-permute-start.22 = (bf16[64,1024]{1,0:T(8,128)(2,1)S(1)}, bf16[64,1024]{1,0:T(8,128)(2,1)S(1)}, u32[]{:S(2)}, u32[]{:S(2)}) collective-permute-start(bf16[64,1024]{1,0:T(8,128)(2,1)S(1)} %subtract_convert_fusion.5.refs_0_), channel_id=1, source_target_pairs={{0,1},{1,0},{2,3},{3,2},{4,5},{5,4},{6,7},{7,6},{8,9},{9,8},{10,11... | collective-permute-start | bytes 393224 | tf_op jit(solution)/shard_map/ppermute | solution.py:142
  63.7 6.9 %collective-permute-start.23 = (bf16[64,1024]{1,0:T(8,128)(2,1)S(1)}, bf16[64,1024]{1,0:T(8,128)(2,1)S(1)}, u32[]{:S(2)}, u32[]{:S(2)}) collective-permute-start(bf16[64,1024]{1,0:T(8,128)(2,1)S(1)} %shard_map.53), channel_id=1, source_target_pairs={{0,4},{4,0},{8,12},{12,8},{1,5},{5,1},{9,13},{13,9},{2,6},{6,2},{1... | collective-permute-start | bytes 393224 | tf_op jit(solution)/shard_map/ppermute | solution.py:142
  67.6 5.0 %collective-permute-start.21 = (bf16[64,1024]{1,0:T(8,128)(2,1)S(1)}, bf16[64,1024]{1,0:T(8,128)(2,1)S(1)}, u32[]{:S(2)}, u32[]{:S(2)}) collective-permute-start(bf16[64,1024]{1,0:T(8,128)(2,1)S(1)} %get-tuple-element.439), channel_id=1, source_target_pairs={{0,2},{1,3},{2,0},{3,1},{4,6},{5,7},{6,4},{7,5},{8,10},{9,11},{10,... | collective-permute-start | bytes 393224 | tf_op jit(solution)/shard_map/ppermute | solution.py:142
  70.7 8.0 %collective-permute-start.26 = (bf16[64,1024]{1,0:T(8,128)(2,1)S(1)}, bf16[64,1024]{1,0:T(8,128)(2,1)S(1)}, u32[]{:S(2)}, u32[]{:S(2)}) collective-permute-start(bf16[64,1024]{1,0:T(8,128)(2,1)S(1)} %get-tuple-element.437), channel_id=1, source_target_pairs={{0,8},{4,12},{8,0},{12,4},{1,9},{5,13},{9,1},{13,5},{2,10},{6,14},... | collective-permute-start | bytes 393224 | tf_op jit(solution)/shard_map/ppermute | solution.py:142
  72.7 1.9 %collective-permute-start.24 = (bf16[64,1024]{1,0:T(8,128)(2,1)S(1)}, bf16[64,1024]{1,0:T(8,128)(2,1)S(1)}, u32[]{:S(2)}, u32[]{:S(2)}) collective-permute-start(bf16[64,1024]{1,0:T(8,128)(2,1)S(1)} %subtract_convert_fusion.4.refs_0_), channel_id=1, source_target_pairs={{0,1},{1,0},{2,3},{3,2},{4,5},{5,4},{6,7},{7,6},{8,9},{9,8},{10,11... | collective-permute-start | bytes 393224 | tf_op jit(solution)/shard_map/ppermute | solution.py:142
  73.6 7.7 %collective-permute-start.25 = (bf16[64,1024]{1,0:T(8,128)(2,1)S(1)}, bf16[64,1024]{1,0:T(8,128)(2,1)S(1)}, u32[]{:S(2)}, u32[]{:S(2)}) collective-permute-start(bf16[64,1024]{1,0:T(8,128)(2,1)S(1)} %shard_map.57), channel_id=1, source_target_pairs={{0,4},{4,0},{8,12},{12,8},{1,5},{5,1},{9,13},{13,9},{2,6},{6,2},{1... | collective-permute-start | bytes 393224 | tf_op jit(solution)/shard_map/ppermute | solution.py:142
  78.6 5.5 %collective-permute-start.28 = (bf16[64,1024]{1,0:T(8,128)(2,1)S(1)}, bf16[64,1024]{1,0:T(8,128)(2,1)S(1)}, u32[]{:S(2)}, u32[]{:S(2)}) collective-permute-start(bf16[64,1024]{1,0:T(8,128)(2,1)S(1)} %add_convert_fusion.4.refs_0_.refs_1_), channel_id=1, source_target_pairs={{0,4},{4,0},{8,12},{12,8},{1,5},{5,1},{9,13},{13,9},{2,6},{6,2},{1... | collective-permute-start | bytes 393224 | tf_op jit(solution)/shard_map/ppermute | solution.py:142
  79.5 5.4 %collective-permute-start.29 = (bf16[64,1024]{1,0:T(8,128)(2,1)S(1)}, bf16[64,1024]{1,0:T(8,128)(2,1)S(1)}, u32[]{:S(2)}, u32[]{:S(2)}) collective-permute-start(bf16[64,1024]{1,0:T(8,128)(2,1)S(1)} %shard_map.59), channel_id=1, source_target_pairs={{0,1},{1,0},{2,3},{3,2},{4,5},{5,4},{6,7},{7,6},{8,9},{9,8},{10,11... | collective-permute-start | bytes 393224 | tf_op jit(solution)/shard_map/ppermute | solution.py:142
  81.4 9.2 %collective-permute-start.27 = (bf16[64,1024]{1,0:T(8,128)(2,1)S(1)}, bf16[64,1024]{1,0:T(8,128)(2,1)S(1)}, u32[]{:S(2)}, u32[]{:S(2)}) collective-permute-start(bf16[64,1024]{1,0:T(8,128)(2,1)S(1)} %get-tuple-element.435), channel_id=1, source_target_pairs={{0,8},{4,12},{8,0},{12,4},{1,9},{5,13},{9,1},{13,5},{2,10},{6,14},... | collective-permute-start | bytes 393224 | tf_op jit(solution)/shard_map/ppermute | solution.py:142
  84.9 6.6 %collective-permute-start.31 = (bf16[64,1024]{1,0:T(8,128)(2,1)S(1)}, bf16[64,1024]{1,0:T(8,128)(2,1)S(1)}, u32[]{:S(2)}, u32[]{:S(2)}) collective-permute-start(bf16[64,1024]{1,0:T(8,128)(2,1)S(1)} %get-tuple-element.433), channel_id=1, source_target_pairs={{0,2},{1,3},{2,0},{3,1},{4,6},{5,7},{6,4},{7,5},{8,10},{9,11},{10,... | collective-permute-start | bytes 393224 | tf_op jit(solution)/shard_map/ppermute | solution.py:142
  90.6 5.4 %collective-permute-start.30 = (bf16[64,1024]{1,0:T(8,128)(2,1)S(1)}, bf16[64,1024]{1,0:T(8,128)(2,1)S(1)}, u32[]{:S(2)}, u32[]{:S(2)}) collective-permute-start(bf16[64,1024]{1,0:T(8,128)(2,1)S(1)} %add_convert_fusion.3.refs_0_.refs_3_), channel_id=1, source_target_pairs={{0,4},{4,0},{8,12},{12,8},{1,5},{5,1},{9,13},{13,9},{2,6},{6,2},{1... | collective-permute-start | bytes 393224 | tf_op jit(solution)/shard_map/ppermute | solution.py:142
  91.5 5.3 %collective-permute-start.32 = (bf16[64,1024]{1,0:T(8,128)(2,1)S(1)}, bf16[64,1024]{1,0:T(8,128)(2,1)S(1)}, u32[]{:S(2)}, u32[]{:S(2)}) collective-permute-start(bf16[64,1024]{1,0:T(8,128)(2,1)S(1)} %shard_map.63), channel_id=1, source_target_pairs={{0,1},{1,0},{2,3},{3,2},{4,5},{5,4},{6,7},{7,6},{8,9},{9,8},{10,11... | collective-permute-start | bytes 393224 | tf_op jit(solution)/shard_map/ppermute | solution.py:142
  91.6 7.5 %collective-permute-start.34 = (bf16[64,1024]{1,0:T(8,128)(2,1)S(1)}, bf16[64,1024]{1,0:T(8,128)(2,1)S(1)}, u32[]{:S(2)}, u32[]{:S(2)}) collective-permute-start(bf16[64,1024]{1,0:T(8,128)(2,1)S(1)} %subtract_convert_fusion.3.refs_0_), channel_id=1, source_target_pairs={{0,1},{1,0},{2,3},{3,2},{4,5},{5,4},{6,7},{7,6},{8,9},{9,8},{10,11... | collective-permute-start | bytes 393224 | tf_op jit(solution)/shard_map/ppermute | solution.py:142
  92.9 7.0 %collective-permute-start.35 = (bf16[64,1024]{1,0:T(8,128)(2,1)S(1)}, bf16[64,1024]{1,0:T(8,128)(2,1)S(1)}, u32[]{:S(2)}, u32[]{:S(2)}) collective-permute-start(bf16[64,1024]{1,0:T(8,128)(2,1)S(1)} %shard_map.64), channel_id=1, source_target_pairs={{0,4},{4,0},{8,12},{12,8},{1,5},{5,1},{9,13},{13,9},{2,6},{6,2},{1... | collective-permute-start | bytes 393224 | tf_op jit(solution)/shard_map/ppermute | solution.py:142
  96.8 5.0 %collective-permute-start.33 = (bf16[64,1024]{1,0:T(8,128)(2,1)S(1)}, bf16[64,1024]{1,0:T(8,128)(2,1)S(1)}, u32[]{:S(2)}, u32[]{:S(2)}) collective-permute-start(bf16[64,1024]{1,0:T(8,128)(2,1)S(1)} %get-tuple-element.431), channel_id=1, source_target_pairs={{0,2},{1,3},{2,0},{3,1},{4,6},{5,7},{6,4},{7,5},{8,10},{9,11},{10,... | collective-permute-start | bytes 393224 | tf_op jit(solution)/shard_map/ppermute | solution.py:142
  99.9 8.0 %collective-permute-start.38 = (bf16[64,1024]{1,0:T(8,128)(2,1)S(1)}, bf16[64,1024]{1,0:T(8,128)(2,1)S(1)}, u32[]{:S(2)}, u32[]{:S(2)}) collective-permute-start(bf16[64,1024]{1,0:T(8,128)(2,1)S(1)} %get-tuple-element.429), channel_id=1, source_target_pairs={{0,8},{4,12},{8,0},{12,4},{1,9},{5,13},{9,1},{13,5},{2,10},{6,14},... | collective-permute-start | bytes 393224 | tf_op jit(solution)/shard_map/ppermute | solution.py:142
  101.9 1.4 collective-permute-start.36
  102.8 7.8 %collective-permute-start.37 = (bf16[64,1024]{1,0:T(8,128)(2,1)S(1)}, bf16[64,1024]{1,0:T(8,128)(2,1)S(1)}, u32[]{:S(2)}, u32[]{:S(2)}) collective-permute-start(bf16[64,1024]{1,0:T(8,128)(2,1)S(1)} %shard_map.68), channel_id=1, source_target_pairs={{0,4},{4,0},{8,12},{12,8},{1,5},{5,1},{9,13},{13,9},{2,6},{6,2},{1... | collective-permute-start | bytes 393224 | tf_op jit(solution)/shard_map/ppermute | solution.py:142
  107.9 5.5 %collective-permute-start.40 = (bf16[64,1024]{1,0:T(8,128)(2,1)S(1)}, bf16[64,1024]{1,0:T(8,128)(2,1)S(1)}, u32[]{:S(2)}, u32[]{:S(2)}) collective-permute-start(bf16[64,1024]{1,0:T(8,128)(2,1)S(1)} %add_convert_fusion.2.refs_0_), channel_id=1, source_target_pairs={{0,4},{4,0},{8,12},{12,8},{1,5},{5,1},{9,13},{13,9},{2,6},{6,2},{1... | collective-permute-start | bytes 393224 | tf_op jit(solution)/shard_map/ppermute | solution.py:142
  108.8 5.4 %collective-permute-start.41 = (bf16[64,1024]{1,0:T(8,128)(2,1)S(1)}, bf16[64,1024]{1,0:T(8,128)(2,1)S(1)}, u32[]{:S(2)}, u32[]{:S(2)}) collective-permute-start(bf16[64,1024]{1,0:T(8,128)(2,1)S(1)} %shard_map.70), channel_id=1, source_target_pairs={{0,1},{1,0},{2,3},{3,2},{4,5},{5,4},{6,7},{7,6},{8,9},{9,8},{10,11... | collective-permute-start | bytes 393224 | tf_op jit(solution)/shard_map/ppermute | solution.py:142
  110.7 9.2 %collective-permute-start.39 = (bf16[64,1024]{1,0:T(8,128)(2,1)S(1)}, bf16[64,1024]{1,0:T(8,128)(2,1)S(1)}, u32[]{:S(2)}, u32[]{:S(2)}) collective-permute-start(bf16[64,1024]{1,0:T(8,128)(2,1)S(1)} %get-tuple-element.427), channel_id=1, source_target_pairs={{0,8},{4,12},{8,0},{12,4},{1,9},{5,13},{9,1},{13,5},{2,10},{6,14},... | collective-permute-start | bytes 393224 | tf_op jit(solution)/shard_map/ppermute | solution.py:142
  114.2 5.0 %collective-permute-start.42 = (bf16[64,1024]{1,0:T(8,128)(2,1)S(1)}, bf16[64,1024]{1,0:T(8,128)(2,1)S(1)}, u32[]{:S(2)}, u32[]{:S(2)}) collective-permute-start(bf16[64,1024]{1,0:T(8,128)(2,1)S(1)} %get-tuple-element.425), channel_id=1, source_target_pairs={{0,2},{1,3},{2,0},{3,1},{4,6},{5,7},{6,4},{7,5},{8,10},{9,11},{10,... | collective-permute-start | bytes 393224 | tf_op jit(solution)/shard_map/ppermute | solution.py:142
  119.9 5.4 %collective-permute-start.43 = (bf16[64,1024]{1,0:T(8,128)(2,1)S(1)}, bf16[64,1024]{1,0:T(8,128)(2,1)S(1)}, u32[]{:S(2)}, u32[]{:S(2)}) collective-permute-start(bf16[64,1024]{1,0:T(8,128)(2,1)S(1)} %add_convert_fusion.1.refs_0_), channel_id=1, source_target_pairs={{0,4},{4,0},{8,12},{12,8},{1,5},{5,1},{9,13},{13,9},{2,6},{6,2},{1... | collective-permute-start | bytes 393224 | tf_op jit(solution)/shard_map/ppermute | solution.py:142
  120.8 5.5 %collective-permute-start.45 = (bf16[64,1024]{1,0:T(8,128)(2,1)S(1)}, bf16[64,1024]{1,0:T(8,128)(2,1)S(1)}, u32[]{:S(2)}, u32[]{:S(2)}) collective-permute-start(bf16[64,1024]{1,0:T(8,128)(2,1)S(1)} %shard_map.72), channel_id=1, source_target_pairs={{0,1},{1,0},{2,3},{3,2},{4,5},{5,4},{6,7},{7,6},{8,9},{9,8},{10,11... | collective-permute-start | bytes 393224 | tf_op jit(solution)/shard_map/ppermute | solution.py:142
  120.9 6.4 %collective-permute-start.44 = (bf16[64,1024]{1,0:T(8,128)(2,1)S(1)}, bf16[64,1024]{1,0:T(8,128)(2,1)S(1)}, u32[]{:S(2)}, u32[]{:S(2)}) collective-permute-start(bf16[64,1024]{1,0:T(8,128)(2,1)S(1)} %subtract_convert_fusion.1), channel_id=1, source_target_pairs={{0,1},{1,0},{2,3},{3,2},{4,5},{5,4},{6,7},{7,6},{8,9},{9,8},{10,11... | collective-permute-start | bytes 393224 | tf_op jit(solution)/shard_map/ppermute | solution.py:142
  126.3 5.0 %collective-permute-start.47 = (bf16[64,1024]{1,0:T(8,128)(2,1)S(1)}, bf16[64,1024]{1,0:T(8,128)(2,1)S(1)}, u32[]{:S(2)}, u32[]{:S(2)}) collective-permute-start(bf16[64,1024]{1,0:T(8,128)(2,1)S(1)} %get-tuple-element.423), channel_id=1, source_target_pairs={{0,2},{1,3},{2,0},{3,1},{4,6},{5,7},{6,4},{7,5},{8,10},{9,11},{10,... | collective-permute-start | bytes 393224 | tf_op jit(solution)/shard_map/ppermute | solution.py:142
  128.1 5.0 %collective-permute-start.46 = (bf16[64,1024]{1,0:T(8,128)(2,1)S(1)}, bf16[64,1024]{1,0:T(8,128)(2,1)S(1)}, u32[]{:S(2)}, u32[]{:S(2)}) collective-permute-start(bf16[64,1024]{1,0:T(8,128)(2,1)S(1)} %shard_map.74), channel_id=1, source_target_pairs={{0,4},{4,0},{8,12},{12,8},{1,5},{5,1},{9,13},{13,9},{2,6},{6,2},{1... | collective-permute-start | bytes 393224 | tf_op jit(solution)/shard_map/ppermute | solution.py:142
  131.4 1.7 %collective-permute-start.48 = (bf16[64,1024]{1,0:T(8,128)(2,1)S(1)}, bf16[64,1024]{1,0:T(8,128)(2,1)S(1)}, u32[]{:S(2)}, u32[]{:S(2)}) collective-permute-start(bf16[64,1024]{1,0:T(8,128)(2,1)S(1)} %subtract_convert_fusion), channel_id=1, source_target_pairs={{0,1},{1,0},{2,3},{3,2},{4,5},{5,4},{6,7},{7,6},{8,9},{9,8},{10,11... | collective-permute-start | bytes 393224 | tf_op jit(solution)/shard_map/ppermute | solution.py:142
  134.0 5.3 %collective-permute-start.49 = (bf16[64,1024]{1,0:T(8,128)(2,1)S(1)}, bf16[64,1024]{1,0:T(8,128)(2,1)S(1)}, u32[]{:S(2)}, u32[]{:S(2)}) collective-permute-start(bf16[64,1024]{1,0:T(8,128)(2,1)S(1)} %shard_map.76), channel_id=1, source_target_pairs={{0,4},{4,0},{8,12},{12,8},{1,5},{5,1},{9,13},{13,9},{2,6},{6,2},{1... | collective-permute-start | bytes 393224 | tf_op jit(solution)/shard_map/ppermute | solution.py:142
  134.4 7.8 %collective-permute-start.50 = (bf16[64,1024]{1,0:T(8,128)(2,1)S(1)}, bf16[64,1024]{1,0:T(8,128)(2,1)S(1)}, u32[]{:S(2)}, u32[]{:S(2)}) collective-permute-start(bf16[64,1024]{1,0:T(8,128)(2,1)S(1)} %fusion), channel_id=1, source_target_pairs={{8,0},{4,12},{9,1},{5,13},{10,2},{6,14},{11,3},{7,15},{24,16},{20,... | collective-permute-start | bytes 393224 | tf_op jit(solution)/shard_map/ppermute | solution.py:260
  139.3 5.2 %collective-permute-start.51 = (bf16[64,1024]{1,0:T(8,128)(2,1)S(1)}, bf16[64,1024]{1,0:T(8,128)(2,1)S(1)}, u32[]{:S(2)}, u32[]{:S(2)}) collective-permute-start(bf16[64,1024]{1,0:T(8,128)(2,1)S(1)} %fusion.1), channel_id=1, source_target_pairs={{12,4},{0,8},{13,5},{1,9},{14,6},{2,10},{15,7},{3,11},{28,20},{16,... | collective-permute-start | bytes 393224 | tf_op jit(solution)/shard_map/ppermute | solution.py:260
  142.0 2.4 %copy-start.2 = (bf16[5,1024,64]{1,2,0:T(8,128)(2,1)}, bf16[5,1024,64]{1,2,0:T(8,128)(2,1)S(1)}, u32[]{:S(2)}) copy-start(bf16[5,1024,64]{1,2,0:T(8,128)(2,1)S(1)} %bitcast_dynamic-update-slice_fusion) | copy-start | bytes 1966084
